TPU v7x, 32 devices: a whole 2x2x4 slice. The times are simulated.
32 devices in a mesh: section: 2 (over x), expert: 16 (over z, y, core).
Axes of the slice: x: 2, y: 2, z: 4, core: 2. Of those that a mesh axis runs over, the one named last changes fastest.
Arguments:
- rows: bfloat16 [2, 512, 3584], P('section', 'expert'), may hold values from -6 to 6
- route_ids: int32 [2, 512, 2], P('section', 'expert'), may hold values from 0 to 7, all different within a row; in each aligned block of 32 rows (0 to 31, 32 to 63, ..., all dimensions but the last counted through in order) at most 16 rows name the same one
- route_weights: float32 [2, 512, 2], P('section', 'expert'), may hold values from 0.1 to 1
- w_gate_up: bfloat16 [2, 3584, 16384], P('section', None, 'expert'), may hold values from -0.09375 to 0.09375
- w_down: bfloat16 [2, 8192, 3584], P('section', 'expert'), may hold values from -0.1875 to 0.1875
Outputs:
- next_rows: bfloat16 [2, 512, 3584], P('section', 'expert')
Inputs may be any that keep to these rules, and one draw needn't show every extreme that they name: `route_ids`: within each section, the 32 rows of one device name any one expert at most 16 times, a bound that some block reaches; the choices of one token differ.
All inputs are finite; a program needn't handle non-finite values.
Results may differ from a plain program's by a relative error of at most 0.0065.
Values may be sent and summed in bfloat16 or wider, within the bound.
No kernel may reach another device: no remote copies, remote signals or barrier semaphores. Data moves between devices by JAX's collectives and lax.ppermute only.
A program may use at most 64 MiB of HBM per device.

v0:
```python
import jax
import jax.numpy as jnp
from jax import lax
from jax.sharding import PartitionSpec as P


def passed_along(shard, axis, by):
    length = lax.axis_size(axis)
    return lax.ppermute(shard, axis, [(i, (i + by) % length) for i in range(length)])


def per_device(rows, route_ids, route_weights, w_gate_up, w_down):
    devices = lax.axis_size("expert")
    experts = devices // 2
    tokens = rows[0]
    tok_count, width = tokens.shape
    top_count = route_ids.shape[2]
    choices_flat = route_ids[0].reshape(-1)
    capacity = max(2, 2 * tok_count * top_count // experts)
    onehot = (choices_flat[:, None] == jnp.arange(experts, dtype=jnp.int32)[None, :]).astype(
        jnp.int32
    )
    before = jnp.cumsum(onehot, axis=0) - onehot
    slot = jnp.sum(before * onehot, axis=1)
    place = slot * experts + choices_flat
    slot_total = experts * capacity
    picker = (place[None, :] == jnp.arange(slot_total, dtype=jnp.int32)[:, None]).astype(
        jnp.bfloat16
    )
    token_pairs = jnp.repeat(tokens, top_count, axis=0)
    packed = jnp.dot(picker, token_pairs, preferred_element_type=jnp.float32).astype(jnp.bfloat16)
    w_in = w_gate_up[0]
    w_out = w_down[0]
    hidden = w_out.shape[0]
    outgoing = jnp.broadcast_to(
        packed.reshape(capacity, experts, 1, width), (capacity, experts, 2, width)
    )
    outgoing = outgoing.reshape(capacity, devices, width)
    block = lax.all_to_all(outgoing, "expert", split_axis=1, concat_axis=1, tiled=True)
    flat = block.reshape(-1, width)
    both = jnp.dot(flat, w_in, preferred_element_type=jnp.float32)
    active = (jax.nn.silu(both[:, :hidden]) * both[:, hidden:]).astype(jnp.bfloat16)
    result = jnp.dot(active, w_out, preferred_element_type=jnp.float32)
    partial_out = result.reshape(block.shape[0], block.shape[1], width).astype(jnp.bfloat16)
    returned = lax.all_to_all(partial_out, "expert", split_axis=1, concat_axis=1, tiled=True)
    returned = returned.reshape(capacity, experts, 2, width).astype(jnp.float32)
    expert_out = jnp.sum(returned, axis=2).astype(jnp.bfloat16).reshape(slot_total, width)
    pair_out = expert_out[place].astype(jnp.float32) * route_weights[0].reshape(-1)[:, None]
    layer_out = jnp.sum(pair_out.reshape(tok_count, top_count, width), axis=1).astype(jnp.bfloat16)
    handed = passed_along(layer_out, "section", 1)
    return handed[None]


def solution(mesh):
    in_specs = (
        P("section", "expert", None),
        P("section", "expert", None),
        P("section", "expert", None),
        P("section", None, "expert"),
        P("section", "expert", None),
    )
    out_specs = P("section", "expert", None)
    return jax.shard_map(
        per_device, mesh=mesh, in_specs=in_specs, out_specs=out_specs, check_vma=False
    )
```

profile of v0, /device:TPU:12, one launch (start us, length us, event | category | flops | bytes accessed | tf_op | source)
XLA Modules:
  0.0 120.1 jit_solution(12550948492186748329)
XLA Ops:
  0.0 0.8 copy.23
  0.8 0.1 eq.28
  1.0 0.2 select_reduce_fusion
  1.2 1.2 broadcast_in_dim.8
  2.4 0.2 reshape.66
  2.6 0.4 fusion.2
  3.0 0.3 copy.24
  3.3 0.2 broadcast_in_dim.19
  3.4 47.6 %all_to_all.10 = bf16[16,16,3584]{2,0,1:T(8,128)(2,1)S(1)} all-to-all(bf16[16,16,3584]{2,0,1:T(8,128)(2,1)S(1)} %bitcast.30), channel_id=1, replica_groups=mesh['section'=2,'expert'=16] {'expert'}, dimensions={1} | all-to-all | bytes 3670016 | tf_op jit(solution)/shard_map/all_to_all | solution.py:39
  51.0 1.0 copy.25
  52.1 5.4 %fusion = f32[256,1024]{1,0:T(8,128)S(1)} fusion(bf16[256,3584]{1,0:T(8,128)(2,1)S(1)} %bitcast.31, bf16[1,3584,1024]{2,1,0:T(8,128)(2,1)} %param.8), kind=kOutput, calls=%fused_computation.1 | convolution fusion | flops 1879048192 | bytes 10223616 | tf_op jit(solution)/shard_map/dot_general | solution.py:41
  57.5 0.2 fusion.4
  57.7 1.1 convolution_convert_fusion
  58.8 2.3 %copy.26 = bf16[16,16,3584]{2,0,1:T(8,128)(2,1)} copy(bf16[16,16,3584]{2,1,0:T(8,128)(2,1)S(1)} %convolution_convert_fusion) | data formatting | bytes 3670016 | tf_op jit(solution)/shard_map/convert_element_type | solution.py:44
  61.1 5.4 %all-to-all-start.1 = ((bf16[16,16,3584]{2,0,1:T(8,128)(2,1)}), bf16[16,16,3584]{2,0,1:T(8,128)(2,1)S(1)}, u32[]{:S(2)}, u32[]{:S(2)}) async-start(bf16[16,16,3584]{2,0,1:T(8,128)(2,1)} %copy.26), calls=%async_computation.1 | async-start | bytes 3670016 | tf_op jit(solution)/shard_map/all_to_all | solution.py:45
  66.6 41.4 %all-to-all-done.1 = bf16[16,16,3584]{2,0,1:T(8,128)(2,1)S(1)} async-done(((bf16[16,16,3584]{2,0,1:T(8,128)(2,1)}), bf16[16,16,3584]{2,0,1:T(8,128)(2,1)S(1)}, u32[]{:S(2)}, u32[]{:S(2)}) %all-to-all-start.1) | async-done | bytes 1835040 | tf_op jit(solution)/shard_map/all_to_all | solution.py:45
  108.1 0.3 bitcast_reduce_fusion
  108.4 0.5 copy.31
  108.9 0.8 gather_fusion
  109.7 0.6 reshape.71
  110.3 1.2 %multiply_reduce_fusion = bf16[32,3584]{1,0:T(8,128)(2,1)S(1)} fusion(f32[32,2,3584]{2,1,0:T(2,128)S(1)} %reshape.71, f32[32,2]{1,0:T(8,128)S(1)} %copy.29), kind=kLoop, calls=%fused_computation.9 | loop fusion | flops 344064 | bytes 1147136 | tf_op jit(solution)/shard_map/reduce_sum | solution.py:49
  111.6 1.6 %collective-permute-start = (bf16[32,3584]{1,0:T(8,128)(2,1)S(1)}, bf16[32,3584]{1,0:T(8,128)(2,1)S(1)}, u32[]{:S(2)}, u32[]{:S(2)}) collective-permute-start(bf16[32,3584]{1,0:T(8,128)(2,1)S(1)} %multiply_reduce_fusion), channel_id=1, source_target_pairs={{0,16},{16,0},{1,17},{17,1},{2,18},{18,2},{3,19},{19,3},{4,20},{20... | collective-permute-start | bytes 688136 | tf_op jit(solution)/shard_map/ppermute | solution.py:9
  113.1 6.3 %collective-permute-done = bf16[32,3584]{1,0:T(8,128)(2,1)S(1)} collective-permute-done((bf16[32,3584]{1,0:T(8,128)(2,1)S(1)}, bf16[32,3584]{1,0:T(8,128)(2,1)S(1)}, u32[]{:S(2)}, u32[]{:S(2)}) %collective-permute-start) | collective-permute-done | bytes 229408 | tf_op jit(solution)/shard_map/ppermute | solution.py:9
  119.4 0.7 copy.33
  (11 shorter events, 0.4 us)
Async XLA Ops:
  52.0 5.6 %copy-start.1 = (bf16[1,512,3584]{2,1,0:T(8,128)(2,1)S(1)}, bf16[1,512,3584]{2,1,0:T(8,128)(2,1)}, u32[]{:S(2)}) copy-start(bf16[1,512,3584]{2,1,0:T(8,128)(2,1)} %param.9) | copy-start | bytes 11010052
  61.1 5.5 %copy-start = (f32[1,32,2]{1,2,0:T(2,128)S(1)}, f32[1,32,2]{1,2,0:T(2,128)}, u32[]{:S(2)}) copy-start(f32[1,32,2]{1,2,0:T(2,128)} %param.7) | copy-start | bytes 772
  61.1 47.0 %all-to-all-start.1 = ((bf16[16,16,3584]{2,0,1:T(8,128)(2,1)}), bf16[16,16,3584]{2,0,1:T(8,128)(2,1)S(1)}, u32[]{:S(2)}, u32[]{:S(2)}) async-start(bf16[16,16,3584]{2,0,1:T(8,128)(2,1)} %copy.26), calls=%async_computation.1 | async-start | bytes 3670016 | tf_op jit(solution)/shard_map/all_to_all | solution.py:45
  111.6 7.9 %collective-permute-start = (bf16[32,3584]{1,0:T(8,128)(2,1)S(1)}, bf16[32,3584]{1,0:T(8,128)(2,1)S(1)}, u32[]{:S(2)}, u32[]{:S(2)}) collective-permute-start(bf16[32,3584]{1,0:T(8,128)(2,1)S(1)} %multiply_reduce_fusion), channel_id=1, source_target_pairs={{0,16},{16,0},{1,17},{17,1},{2,18},{18,2},{3,19},{19,3},{4,20},{20... | collective-permute-start | bytes 688136 | tf_op jit(solution)/shard_map/ppermute | solution.py:9
where the time goes:
time: 120 us
  waiting for transfers between devices  47.8 us (40%)
  blocking collectives  47.6 us (40%)
  local copies, waits for them, and re-layouts  8.73 us (7%)
  matrix products  6.93 us (6%)
  starting transfers between devices  6.91 us (6%)
  other arithmetic  2.08 us (2%)
    all_to_all x1, blocking collectives, per_device(): lax.all_to_all(outgoing, 'expert', split_axis=1, concat_axis=1, tiled=True)  47.6 us
    all_to_all x1, waiting for transfers between devices, per_device(): lax.all_to_all(partial_out, 'expert', split_axis=1, concat_axis=1, tiled=...  41.4 us
    ppermute x1, waiting for transfers between devices, passed_along(): lax.ppermute(shard, axis, [(i, (i + by) % length) for i in range(length)])  6.32 us
    dot_general x1, matrix products, per_device(): both = jnp.dot(flat, w_in, preferred_element_type=jnp.float32)  5.43 us
    all_to_all x1, starting transfers between devices, per_device(): lax.all_to_all(partial_out, 'expert', split_axis=1, concat_axis=1, tiled=...  5.36 us
  transfers between devices with their start and end apart: 2, of which 2 were waited for; matrix products, arithmetic and copies ran while one was open for 0% of the time, Pallas kernels for 0%

commit v1 on v0

--- a/solution.py
+++ b/solution.py
@@ -9,7 +9,7 @@
     return lax.ppermute(shard, axis, [(i, (i + by) % length) for i in range(length)])
 
 
-def per_device(rows, route_ids, route_weights, w_gate_up, w_down):
+def by_slots(rows, route_ids, route_weights, w_gate_up, w_down):
     devices = lax.axis_size("expert")
     experts = devices // 2
     tokens = rows[0]
@@ -47,8 +47,36 @@
     expert_out = jnp.sum(returned, axis=2).astype(jnp.bfloat16).reshape(slot_total, width)
     pair_out = expert_out[place].astype(jnp.float32) * route_weights[0].reshape(-1)[:, None]
     layer_out = jnp.sum(pair_out.reshape(tok_count, top_count, width), axis=1).astype(jnp.bfloat16)
-    handed = passed_along(layer_out, "section", 1)
-    return handed[None]
+    return passed_along(layer_out, "section", 1)[None]
+
+
+def by_gather(rows, route_ids, route_weights, w_gate_up, w_down):
+    devices = lax.axis_size("expert")
+    experts = devices // 2
+    mine = lax.axis_index("expert") // 2
+    tokens = rows[0]
+    w_in = w_gate_up[0]
+    w_out = w_down[0]
+    hidden = w_out.shape[0]
+    chosen = route_ids[0][:, :, None] == jnp.arange(experts, dtype=jnp.int32)
+    scale = jnp.sum(jnp.where(chosen, route_weights[0][:, :, None], 0.0), axis=1)
+    every_scale = lax.all_gather(scale, "expert", axis=0, tiled=True)
+    own_scale = lax.dynamic_index_in_dim(every_scale, mine, axis=1, keepdims=True)
+    every = lax.all_gather(tokens, "expert", axis=0, tiled=True)
+    both = jnp.dot(every, w_in, preferred_element_type=jnp.float32)
+    active = (jax.nn.silu(both[:, :hidden]) * both[:, hidden:]).astype(jnp.bfloat16)
+    result = jnp.dot(active, w_out, preferred_element_type=jnp.float32)
+    part = (result * own_scale).astype(jnp.bfloat16)
+    layer_out = lax.psum_scatter(part, "expert", scatter_dimension=0, tiled=True)
+    return passed_along(layer_out, "section", 1)[None]
+
+
+def per_device(rows, route_ids, route_weights, w_gate_up, w_down):
+    experts = lax.axis_size("expert") // 2
+    tok_count = rows.shape[1]
+    capacity = max(2, 2 * tok_count * route_ids.shape[2] // experts)
+    plan = by_gather if tok_count <= 2 * capacity else by_slots
+    return plan(rows, route_ids, route_weights, w_gate_up, w_down)
 
 
 def solution(mesh):

time: 120 us -> 153 us (1.27)
  the two profiles are of different devices: /device:TPU:12 before, /device:TPU:0 now
where the time goes in v1:
time: 153 us
  waiting for transfers between devices  102 us (67%)
  blocking collectives  23.3 us (15%)
  between operations  13.5 us (9%)
  matrix products  11.3 us (7%)
    reduce_scatter x1, waiting for transfers between devices, by_gather(): lax.psum_scatter(part, 'expert', scatter_dimension=0, tiled=True)  67.9 us
    all_gather x1, waiting for transfers between devices, by_gather(): every = lax.all_gather(tokens, 'expert', axis=0, tiled=True)  28.5 us
    all_gather x1, blocking collectives, by_gather(): every_scale = lax.all_gather(scale, 'expert', axis=0, tiled=True)  23.3 us
    dot_general x1, matrix products, by_gather(): both = jnp.dot(every, w_in, preferred_element_type=jnp.float32)  7.43 us
    ppermute x1, waiting for transfers between devices, passed_along(): lax.ppermute(shard, axis, [(i, (i + by) % length) for i in range(length)])  4.81 us
    dot_general x1, matrix products, by_gather(): result = jnp.dot(active, w_out, preferred_element_type=jnp.float32)  3.91 us
  transfers between devices with their start and end apart: 3, of which 3 were waited for; matrix products, arithmetic and copies ran while one was open for 1% of the time, Pallas kernels for 0%

profile of v1, /device:TPU:0, one launch (start us, length us, event | category | flops | bytes accessed | tf_op | source)
XLA Modules:
  0.0 153.0 jit_solution(5675496327789734420)
XLA Ops:
  6.5 0.0 all-gather.4.cloned.1.call-start
  6.5 0.7 all-gather.4.cloned.1.call-update
  7.3 0.0 reduce-scatter.2.cloned.1.call-start
  7.3 0.7 select_reduce_fusion
  8.0 23.3 %all-gather.1 = f32[16,32,8]{1,2,0:T(8,128)S(1)} all-gather(f32[1,32,8]{1,2,0:T(8,128)S(1)} %bitcast.17), channel_id=1, replica_groups=mesh['section'=2,'expert'=16] {'expert'}, dimensions={0}, use_global_device_ids=true | all-gather | bytes 17408 | tf_op jit(solution)/shard_map/all_gather | solution.py:63
  31.3 0.1 reshape.4
  31.5 28.5 %all-gather.4.cloned.1.call-done = bf16[1,512,3584]{2,1,0:T(8,128)(2,1)} async-done(((bf16[1,32,3584]{2,1,0:T(8,128)(2,1)}), bf16[1,512,3584]{2,1,0:T(8,128)(2,1)}) %all-gather.4.cloned.1.call-update) | async-done | bytes 3670032 | tf_op jit(solution)/shard_map/all_gather | solution.py:65
  60.0 0.0 copy-start
  60.0 7.4 %fusion = f32[512,1024]{1,0:T(8,128)S(1)} fusion(bf16[1,3584,1024]{2,1,0:T(8,128)(2,1)} %param.8, bf16[1,512,3584]{2,1,0:T(8,128)(2,1)} %all-gather.4.cloned.1.call-done), kind=kOutput, calls=%fused_computation | convolution fusion | flops 3758096384 | bytes 13107200 | tf_op jit(solution)/shard_map/dot_general | solution.py:66
  67.4 0.0 copy-done
  67.4 3.9 %multiply_convert_fusion = bf16[512,3584]{1,0:T(8,128)(2,1)} fusion(bf16[1,512,3584]{2,1,0:T(8,128)(2,1)S(1)} %copy-done, f32[512]{0:T(512)S(1)} %bitcast.18, f32[512,1024]{1,0:T(8,128)S(1)} %fusion), kind=kOutput, calls=%fused_computation.2 | convolution fusion | flops 1884291072 | bytes 9439232 | tf_op jit(solution)/shard_map/dot_general | solution.py:68
  71.3 0.0 reduce-scatter.2.cloned.1.call-update
  71.4 67.9 %reduce-scatter.2.cloned.1.call-done = bf16[32,3584]{1,0:T(8,128)(2,1)} async-done(((bf16[512,3584]{1,0:T(8,128)(2,1)}), bf16[32,3584]{1,0:T(8,128)(2,1)}) %reduce-scatter.2.cloned.1.call-update) | async-done | bytes 229392 | tf_op jit(solution)/shard_map/reduce_scatter | solution.py:70
  139.2 1.5 collective-permute-start
  140.7 4.8 %collective-permute-done = bf16[32,3584]{1,0:T(8,128)(2,1)S(1)} collective-permute-done((bf16[32,3584]{1,0:T(8,128)(2,1)}, bf16[32,3584]{1,0:T(8,128)(2,1)S(1)}, u32[]{:S(2)}, u32[]{:S(2)}) %collective-permute-start) | collective-permute-done | bytes 229408 | tf_op jit(solution)/shard_map/ppermute | solution.py:9
  145.5 0.7 copy.17
  (2 shorter events, 0.0 us)
Async XLA Ops:
  6.5 53.4 %all-gather.4.cloned.1.call-start = ((), (), s32[]{:S(2)}) async-start(), calls=%async_computation.2 | async-start | bytes 3899392 | tf_op jit(solution)/shard_map/all_gather | solution.py:65
  7.3 132.0 %reduce-scatter.2.cloned.1.call-start = ((), (), s32[]{:S(2)}) async-start(), calls=%async_computation.1 | async-start | bytes 3899392 | tf_op jit(solution)/shard_map/reduce_scatter | solution.py:70
  60.0 7.4 %copy-start = (bf16[1,512,3584]{2,1,0:T(8,128)(2,1)S(1)}, bf16[1,512,3584]{2,1,0:T(8,128)(2,1)}, u32[]{:S(2)}) copy-start(bf16[1,512,3584]{2,1,0:T(8,128)(2,1)} %param.9) | copy-start | bytes 11010052
  139.2 6.3 %collective-permute-start = (bf16[32,3584]{1,0:T(8,128)(2,1)}, bf16[32,3584]{1,0:T(8,128)(2,1)S(1)}, u32[]{:S(2)}, u32[]{:S(2)}) collective-permute-start(bf16[32,3584]{1,0:T(8,128)(2,1)} %reduce-scatter.2.cloned.1.call-done), channel_id=1, source_target_pairs={{0,16},{16,0},{1,17},{17,1},{2,18},{18,2},{3,19},{19,3},{4,20},{20... | collective-permute-start | bytes 688136 | tf_op jit(solution)/shard_map/ppermute | solution.py:9
Sparse Core Ops, SparseCore 0:
  9.6 50.2 all-gather.3
  71.5 67.6 reduce-scatter.1

commit v2 on v0

--- a/solution.py
+++ b/solution.py
@@ -1,6 +1,8 @@
 import jax
 import jax.numpy as jnp
 from jax import lax
+from jax.experimental import pallas as pl
+from jax.experimental.pallas import tpu as pltpu
 from jax.sharding import PartitionSpec as P
 
 
@@ -9,7 +11,7 @@
     return lax.ppermute(shard, axis, [(i, (i + by) % length) for i in range(length)])
 
 
-def per_device(rows, route_ids, route_weights, w_gate_up, w_down):
+def by_slots(rows, route_ids, route_weights, w_gate_up, w_down):
     devices = lax.axis_size("expert")
     experts = devices // 2
     tokens = rows[0]
@@ -47,8 +49,146 @@
     expert_out = jnp.sum(returned, axis=2).astype(jnp.bfloat16).reshape(slot_total, width)
     pair_out = expert_out[place].astype(jnp.float32) * route_weights[0].reshape(-1)[:, None]
     layer_out = jnp.sum(pair_out.reshape(tok_count, top_count, width), axis=1).astype(jnp.bfloat16)
-    handed = passed_along(layer_out, "section", 1)
-    return handed[None]
+    return passed_along(layer_out, "section", 1)[None]
+
+
+def pack_kernel(chip, ids, weights, tokens, *outs):
+    blocks, mixing = outs[:-1], outs[-1]
+    experts = len(blocks)
+    capacity, _ = blocks[0].shape
+    top_count, tok_count = ids.shape
+    away = ids[...] ^ chip[0]
+    partner = lax.broadcasted_iota(jnp.int32, (experts, tok_count), 0)
+    named = jnp.zeros((experts, tok_count), jnp.float32)
+    scale = jnp.zeros((experts, tok_count), jnp.float32)
+    for k in range(top_count):
+        hit = away[k : k + 1, :] == partner
+        named = named + jnp.where(hit, 1.0, 0.0)
+        scale = scale + jnp.where(hit, weights[k : k + 1, :], 0.0)
+    square = (tok_count, tok_count)
+    earlier = lax.broadcasted_iota(jnp.int32, square, 0) < lax.broadcasted_iota(jnp.int32, square, 1)
+    rank = jnp.dot(
+        named.astype(jnp.bfloat16),
+        jnp.where(earlier, 1.0, 0.0).astype(jnp.bfloat16),
+        preferred_element_type=jnp.float32,
+    )
+    rank = jnp.where(named > 0.5, rank, -1.0)
+    slot = lax.broadcasted_iota(jnp.int32, (capacity, tok_count), 0).astype(jnp.float32)
+    picks, scales = [], []
+    for r in range(experts):
+        hit = rank[r : r + 1, :] == slot
+        picks.append(jnp.where(hit, 1.0, 0.0))
+        scales.append(jnp.where(hit, scale[r : r + 1, :], 0.0))
+    pick = jnp.concatenate(picks, axis=0).astype(jnp.bfloat16)
+    packed = jnp.dot(pick, tokens[...], preferred_element_type=jnp.float32).astype(jnp.bfloat16)
+    for r in range(experts):
+        blocks[r][...] = packed[r * capacity : (r + 1) * capacity]
+    left = jnp.concatenate(scales, axis=0)
+    slots = experts * capacity
+    same = lax.broadcasted_iota(jnp.int32, (slots, slots), 0) == lax.broadcasted_iota(
+        jnp.int32, (slots, slots), 1
+    )
+    unit = jnp.where(same, 1.0, 0.0).astype(jnp.bfloat16)
+    for part in range(3):
+        piece = left.astype(jnp.bfloat16)
+        left = left - piece.astype(jnp.float32)
+        turned = lax.dot_general(
+            piece, unit, (((0,), (0,)), ((), ())), preferred_element_type=jnp.float32
+        )
+        mixing[part * tok_count : (part + 1) * tok_count, :] = turned.astype(jnp.bfloat16)
+
+
+def pack(chip, ids, weights, tokens, experts, capacity):
+    tok_count, width = tokens.shape
+    vmem = pl.BlockSpec(memory_space=pltpu.VMEM)
+    return pl.pallas_call(
+        pack_kernel,
+        out_shape=[jax.ShapeDtypeStruct((capacity, width), jnp.bfloat16)] * experts
+        + [jax.ShapeDtypeStruct((3 * tok_count, experts * capacity), jnp.bfloat16)],
+        in_specs=[pl.BlockSpec(memory_space=pltpu.SMEM), vmem, vmem, vmem],
+        out_specs=[vmem] * (experts + 1),
+        compiler_params=pltpu.CompilerParams(vmem_limit_bytes=12 << 20),
+        name="pack",
+    )(chip, ids, weights, tokens)
+
+
+def combine_kernel(mixing, *refs):
+    blocks, out = refs[:-1], refs[-1]
+    tok_count = out.shape[0]
+    slots = jnp.concatenate([block[...] for block in blocks], axis=0)
+    mixed = jnp.dot(mixing[...], slots, preferred_element_type=jnp.float32)
+    total = mixed[2 * tok_count :] + mixed[tok_count : 2 * tok_count] + mixed[:tok_count]
+    out[...] = total.astype(out.dtype)
+
+
+def combine(mixing, blocks):
+    tok_count = mixing.shape[0] // 3
+    vmem = pl.BlockSpec(memory_space=pltpu.VMEM)
+    return pl.pallas_call(
+        combine_kernel,
+        out_shape=jax.ShapeDtypeStruct((tok_count, blocks[0].shape[1]), jnp.bfloat16),
+        in_specs=[vmem] * (1 + len(blocks)),
+        out_specs=vmem,
+        compiler_params=pltpu.CompilerParams(vmem_limit_bytes=12 << 20),
+        name="combine",
+    )(mixing, *blocks)
+
+
+def sent(shard, sections, experts, section_step, chip_xor):
+    pairs = []
+    for s in range(sections):
+        for e in range(experts):
+            for core in range(2):
+                target = ((s + section_step) % sections) * experts + (e ^ chip_xor)
+                pairs.append(((s * experts + e) * 2 + core, target * 2 + core))
+    return lax.ppermute(shard, ("section", "expert"), pairs)
+
+
+def by_direct(rows, route_ids, route_weights, w_gate_up, w_down):
+    sections = lax.axis_size("section")
+    devices = lax.axis_size("expert")
+    experts = devices // 2
+    tokens = rows[0]
+    tok_count, width = tokens.shape
+    top_count = route_ids.shape[2]
+    capacity = max(2, 2 * tok_count * top_count // experts)
+    chip = lax.axis_index("expert") // 2
+    swap = [(i, i ^ 1) for i in range(devices)]
+    halves = [(w_gate_up[0], w_down[0])]
+    halves.append(tuple(lax.ppermute(w, "expert", swap) for w in halves[0]))
+    hidden = w_down.shape[1]
+    packed = pack(
+        chip.reshape(1).astype(jnp.int32), route_ids[0].T, route_weights[0].T, tokens, experts, capacity
+    )
+    blocks, mixing = packed[:-1], packed[-1]
+    half = experts // 2
+    first = [r for r in range(experts) if (r & half) and not (r & (half // 2))]
+    second = [r for r in range(experts) if (r & half) and (r & (half // 2))]
+    near = [r for r in range(half)]
+    groups = [first + near[: half // 2], second + near[half // 2 :]]
+    arrived = {0: blocks[0]}
+    for r in first + second + near[half // 2 :] + near[1 : half // 2]:
+        arrived[r] = sent(blocks[r], sections, experts, 0, r)
+    mixing = sent(mixing, sections, experts, 1, 0)
+    back = {}
+    for group in groups:
+        held = jnp.concatenate([arrived[r] for r in group], axis=0)
+        total = jnp.zeros((held.shape[0], width), jnp.float32)
+        for w_in, w_out in halves:
+            both = jnp.dot(held, w_in, preferred_element_type=jnp.float32)
+            active = (jax.nn.silu(both[:, :hidden]) * both[:, hidden:]).astype(jnp.bfloat16)
+            total = total + jnp.dot(active, w_out, preferred_element_type=jnp.float32)
+        total = total.astype(jnp.bfloat16)
+        for at, r in enumerate(group):
+            piece = total[at * capacity : (at + 1) * capacity]
+            back[r] = sent(piece, sections, experts, 1, r)
+    return combine(mixing, [back[r] for r in range(experts)])[None]
+
+
+def per_device(rows, route_ids, route_weights, w_gate_up, w_down):
+    experts = lax.axis_size("expert") // 2
+    plan = by_direct if experts in (4, 8) else by_slots
+    return plan(rows, route_ids, route_weights, w_gate_up, w_down)
 
 
 def solution(mesh):

time: 120 us -> 77.1 us (0.64)
  the two profiles are of different devices: /device:TPU:12 before, /device:TPU:0 now
where the time goes in v2:
time: 77.1 us; the launch traced here: 76.9 us
  starting transfers between devices  28 us (36%)
  waiting for transfers between devices  26.8 us (35%)
  matrix products  17.9 us (23%)
  local copies, waits for them, and re-layouts  2.45 us (3%)
  Pallas kernels  1.53 us (2%)
    ppermute x16, starting transfers between devices, sent(): return lax.ppermute(shard, ('section', 'expert'), pairs)  27.5 us
    ppermute x16, waiting for transfers between devices, sent(): return lax.ppermute(shard, ('section', 'expert'), pairs)  26.8 us
    dot_general x4, matrix products, by_direct(): both = jnp.dot(held, w_in, preferred_element_type=jnp.float32)  14.9 us
    dot_general x4, matrix products, by_direct(): total = total + jnp.dot(active, w_out, preferred_element_type=jnp.float32)  2.96 us
    unnamed x18, local copies, waits for them, and re-layouts  2.37 us
  transfers between devices with their start and end apart: 18, of which 6 were waited for; matrix products, arithmetic and copies ran while one was open for 23% of the time, Pallas kernels for 1%

profile of v2, /device:TPU:0, one launch (start us, length us, event | category | flops | bytes accessed | tf_op | source)
XLA Modules:
  0.0 76.9 jit_solution(5727015707807213723)
XLA Ops:
  0.5 0.9 %copy-done = bf16[1,32,3584]{2,1,0:T(8,128)(2,1)S(1)} copy-done((bf16[1,32,3584]{2,1,0:T(8,128)(2,1)S(1)}, bf16[1,32,3584]{2,1,0:T(8,128)(2,1)}, u32[]{:S(2)}) %copy-start) | copy-done | bytes 229400
  3.3 3.7 %collective-permute-start.1 = (bf16[16,3584]{1,0:T(8,128)(2,1)S(1)}, bf16[16,3584]{1,0:T(8,128)(2,1)S(1)}, u32[]{:S(2)}, u32[]{:S(2)}) collective-permute-start(bf16[16,3584]{1,0:T(8,128)(2,1)S(1)} %get-tuple-element.15), channel_id=1, source_target_pairs={{0,8},{1,9},{2,10},{3,11},{4,12},{5,13},{6,14},{7,15},{8,0},{9,1},... | collective-permute-start | bytes 344072 | tf_op jit(solution)/shard_map/ppermute | solution.py:144
  6.9 1.3 %collective-permute-start.8 = (bf16[16,3584]{1,0:T(8,128)(2,1)S(1)}, bf16[16,3584]{1,0:T(8,128)(2,1)S(1)}, u32[]{:S(2)}, u32[]{:S(2)}) collective-permute-start(bf16[16,3584]{1,0:T(8,128)(2,1)S(1)} %get-tuple-element.19), channel_id=1, source_target_pairs={{0,12},{1,13},{2,14},{3,15},{4,8},{5,9},{6,10},{7,11},{8,4},{9,5},... | collective-permute-start | bytes 344072 | tf_op jit(solution)/shard_map/ppermute | solution.py:144
  8.3 3.4 %collective-permute-start.9 = (bf16[16,3584]{1,0:T(8,128)(2,1)S(1)}, bf16[16,3584]{1,0:T(8,128)(2,1)S(1)}, u32[]{:S(2)}, u32[]{:S(2)}) collective-permute-start(bf16[16,3584]{1,0:T(8,128)(2,1)S(1)} %get-tuple-element.20), channel_id=1, source_target_pairs={{0,14},{1,15},{2,12},{3,13},{4,10},{5,11},{6,8},{7,9},{8,6},{9,7},... | collective-permute-start | bytes 344072 | tf_op jit(solution)/shard_map/ppermute | solution.py:144
  11.7 6.6 %collective-permute-done.1 = bf16[16,3584]{1,0:T(8,128)(2,1)S(1)} collective-permute-done((bf16[16,3584]{1,0:T(8,128)(2,1)S(1)}, bf16[16,3584]{1,0:T(8,128)(2,1)S(1)}, u32[]{:S(2)}, u32[]{:S(2)}) %collective-permute-start.1) | collective-permute-done | bytes 114720 | tf_op jit(solution)/shard_map/ppermute | solution.py:144
  19.1 9.9 %collective-permute-done.2 = bf16[16,3584]{1,0:T(8,128)(2,1)S(1)} collective-permute-done((bf16[16,3584]{1,0:T(8,128)(2,1)S(1)}, bf16[16,3584]{1,0:T(8,128)(2,1)S(1)}, u32[]{:S(2)}, u32[]{:S(2)}) %collective-permute-start.2) | collective-permute-done | bytes 114720 | tf_op jit(solution)/shard_map/ppermute | solution.py:144
  30.4 1.6 %collective-permute-start = (bf16[96,128]{1,0:T(8,128)(2,1)S(1)}, bf16[96,128]{1,0:T(8,128)(2,1)S(1)}, u32[]{:S(2)}, u32[]{:S(2)}) collective-permute-start(bf16[96,128]{1,0:T(8,128)(2,1)S(1)} %get-tuple-element.14), channel_id=1, source_target_pairs={{0,16},{1,17},{2,18},{3,19},{4,20},{5,21},{6,22},{7,23},{8,24},{9,... | collective-permute-start | bytes 73736 | tf_op jit(solution)/shard_map/ppermute | solution.py:144
  32.0 2.8 %collective-permute-done.11 = bf16[16,3584]{1,0:T(8,128)(2,1)S(1)} collective-permute-done((bf16[16,3584]{1,0:T(8,128)(2,1)S(1)}, bf16[16,3584]{1,0:T(8,128)(2,1)S(1)}, u32[]{:S(2)}, u32[]{:S(2)}) %collective-permute-start.11) | collective-permute-done | bytes 114720 | tf_op jit(solution)/shard_map/ppermute | solution.py:144
  34.8 4.6 %fusion.18 = f32[64,1024]{1,0:T(8,128)S(1)} fusion(bf16[64,3584]{1,0:T(8,128)(2,1)S(1)} %constant_dynamic-update-slice_fusion.4, bf16[1,3584,1024]{2,1,0:T(8,128)(2,1)} %param.8), kind=kOutput, calls=%fused_computation.28 | convolution fusion | flops 469762048 | bytes 8060928 | tf_op jit(solution)/shard_map/dot_general | solution.py:178
  40.2 1.4 %fusion.20 = f32[64,1024]{1,0:T(8,128)S(1)} fusion(bf16[64,3584]{1,0:T(8,128)(2,1)S(1)} %constant_dynamic-update-slice_fusion, bf16[1,3584,1024]{2,1,0:T(8,128)(2,1)S(1)} %bitcast.32), kind=kOutput, calls=%fused_computation.30 | convolution fusion | flops 469762048 | bytes 8060928 | tf_op jit(solution)/shard_map/dot_general | solution.py:178
  42.4 4.5 %fusion.29 = f32[64,1024]{1,0:T(8,128)S(1)} fusion(bf16[64,3584]{1,0:T(8,128)(2,1)S(1)} %constant_dynamic-update-slice_fusion.4, bf16[3584,1024]{1,0:T(8,128)(2,1)} %collective-permute-done.4), kind=kOutput, calls=%fused_computation.39 | convolution fusion | flops 469762048 | bytes 8060928 | tf_op jit(solution)/shard_map/dot_general | solution.py:178
  46.9 0.7 fusion.1
  47.6 1.0 %collective-permute-start.12 = (bf16[16,3584]{1,0:T(8,128)(2,1)S(1)}, bf16[16,3584]{1,0:T(8,128)(2,1)S(1)}, u32[]{:S(2)}, u32[]{:S(2)}) collective-permute-start(bf16[16,3584]{1,0:T(8,128)(2,1)S(1)} %get-tuple-element.26), channel_id=1, source_target_pairs={{0,20},{1,21},{2,22},{3,23},{4,16},{5,17},{6,18},{7,19},{8,28},{9,... | collective-permute-start | bytes 344072 | tf_op jit(solution)/shard_map/ppermute | solution.py:144
  48.7 2.1 %collective-permute-start.13 = (bf16[16,3584]{1,0:T(8,128)(2,1)S(1)}, bf16[16,3584]{1,0:T(8,128)(2,1)S(1)}, u32[]{:S(2)}, u32[]{:S(2)}) collective-permute-start(bf16[16,3584]{1,0:T(8,128)(2,1)S(1)} %get-tuple-element.25), channel_id=1, source_target_pairs={{0,22},{1,23},{2,20},{3,21},{4,18},{5,19},{6,16},{7,17},{8,30},{9,... | collective-permute-start | bytes 344072 | tf_op jit(solution)/shard_map/ppermute | solution.py:144
  50.7 4.6 %collective-permute-start.16 = (bf16[16,3584]{1,0:T(8,128)(2,1)S(1)}, bf16[16,3584]{1,0:T(8,128)(2,1)S(1)}, u32[]{:S(2)}, u32[]{:S(2)}) collective-permute-start(bf16[16,3584]{1,0:T(8,128)(2,1)S(1)} %get-tuple-element.24), channel_id=1, source_target_pairs={{0,28},{1,29},{2,30},{3,31},{4,24},{5,25},{6,26},{7,27},{8,20},{9,... | collective-permute-start | bytes 344072 | tf_op jit(solution)/shard_map/ppermute | solution.py:144
  55.4 1.0 %collective-permute-start.17 = (bf16[16,3584]{1,0:T(8,128)(2,1)S(1)}, bf16[16,3584]{1,0:T(8,128)(2,1)S(1)}, u32[]{:S(2)}, u32[]{:S(2)}) collective-permute-start(bf16[16,3584]{1,0:T(8,128)(2,1)S(1)} %get-tuple-element.23), channel_id=1, source_target_pairs={{0,30},{1,31},{2,28},{3,29},{4,26},{5,27},{6,24},{7,25},{8,22},{9,... | collective-permute-start | bytes 344072 | tf_op jit(solution)/shard_map/ppermute | solution.py:144
  56.3 4.5 %fusion.28 = f32[64,1024]{1,0:T(8,128)S(1)} fusion(bf16[64,3584]{1,0:T(8,128)(2,1)S(1)} %constant_dynamic-update-slice_fusion, bf16[3584,1024]{1,0:T(8,128)(2,1)} %collective-permute-done.4), kind=kOutput, calls=%fused_computation.38 | convolution fusion | flops 469762048 | bytes 8060928 | tf_op jit(solution)/shard_map/dot_general | solution.py:178
  62.3 3.2 %collective-permute-start.15 = (bf16[16,3584]{1,0:T(8,128)(2,1)S(1)}, bf16[16,3584]{1,0:T(8,128)(2,1)S(1)}, u32[]{:S(2)}, u32[]{:S(2)}) collective-permute-start(bf16[16,3584]{1,0:T(8,128)(2,1)S(1)} %get-tuple-element.27), channel_id=1, source_target_pairs={{0,26},{1,27},{2,24},{3,25},{4,30},{5,31},{6,28},{7,29},{8,18},{9,... | collective-permute-start | bytes 344072 | tf_op jit(solution)/shard_map/ppermute | solution.py:144
  65.5 1.4 %collective-permute-start.6 = (bf16[16,3584]{1,0:T(8,128)(2,1)S(1)}, bf16[16,3584]{1,0:T(8,128)(2,1)S(1)}, u32[]{:S(2)}, u32[]{:S(2)}) collective-permute-start(bf16[16,3584]{1,0:T(8,128)(2,1)S(1)} %get-tuple-element.30), channel_id=1, source_target_pairs={{0,16},{1,17},{2,18},{3,19},{4,20},{5,21},{6,22},{7,23},{8,24},{9,... | collective-permute-start | bytes 344072 | tf_op jit(solution)/shard_map/ppermute | solution.py:144
  66.9 1.5 %collective-permute-start.7 = (bf16[16,3584]{1,0:T(8,128)(2,1)S(1)}, bf16[16,3584]{1,0:T(8,128)(2,1)S(1)}, u32[]{:S(2)}, u32[]{:S(2)}) collective-permute-start(bf16[16,3584]{1,0:T(8,128)(2,1)S(1)} %get-tuple-element.29), channel_id=1, source_target_pairs={{0,18},{1,19},{2,16},{3,17},{4,22},{5,23},{6,20},{7,21},{8,26},{9,... | collective-permute-start | bytes 344072 | tf_op jit(solution)/shard_map/ppermute | solution.py:144
  68.4 4.9 %collective-permute-done.14.refs_4_ = bf16[16,3584]{1,0:T(8,128)(2,1)S(1)} collective-permute-done((bf16[16,3584]{1,0:T(8,128)(2,1)S(1)}, bf16[16,3584]{1,0:T(8,128)(2,1)S(1)}, u32[]{:S(2)}, u32[]{:S(2)}) %collective-permute-start.14) | collective-permute-done | bytes 114720 | tf_op jit(solution)/shard_map/ppermute | solution.py:144
  73.3 1.4 %collective-permute-done.15.refs_5_ = bf16[16,3584]{1,0:T(8,128)(2,1)S(1)} collective-permute-done((bf16[16,3584]{1,0:T(8,128)(2,1)S(1)}, bf16[16,3584]{1,0:T(8,128)(2,1)S(1)}, u32[]{:S(2)}, u32[]{:S(2)}) %collective-permute-start.15) | collective-permute-done | bytes 114720 | tf_op jit(solution)/shard_map/ppermute | solution.py:144
  74.7 1.1 %collective-permute-done.7.refs_1_ = bf16[16,3584]{1,0:T(8,128)(2,1)S(1)} collective-permute-done((bf16[16,3584]{1,0:T(8,128)(2,1)S(1)}, bf16[16,3584]{1,0:T(8,128)(2,1)S(1)}, u32[]{:S(2)}, u32[]{:S(2)}) %collective-permute-start.7) | collective-permute-done | bytes 114720 | tf_op jit(solution)/shard_map/ppermute | solution.py:144
  75.9 1.0 %combine.1 = bf16[32,3584]{1,0:T(8,128)(2,1)} custom-call(bf16[96,128]{1,0:T(8,128)(2,1)S(1)} %collective-permute-done.mixing, bf16[16,3584]{1,0:T(8,128)(2,1)S(1)} %collective-permute-done.6.refs_0_, bf16[16,3584]{1,0:T(8,128)(2,1)S(1)} %collective-permute-done.7.refs_1_, bf16[16,3584]{1,0:T(8,128)(2,1)S(1)} %collective-permute-done.12.refs_2_, ...), custom_call_target="tpu_custom_call" | custom-call | tf_op jit(solution)/shard_map/combine/pallas_call | solution.py:127
  (45 shorter events, 7.5 us)
Async XLA Ops:
  0.0 42.4 %collective-permute-start.4 = (bf16[3584,1024]{1,0:T(8,128)(2,1)}, bf16[3584,1024]{1,0:T(8,128)(2,1)}, u32[]{:S(2)}, u32[]{:S(2)}) collective-permute-start(bf16[3584,1024]{1,0:T(8,128)(2,1)} %bitcast.30), channel_id=1, source_target_pairs={{0,1},{1,0},{2,3},{3,2},{4,5},{5,4},{6,7},{7,6},{8,9},{9,8},{10,11... | collective-permute-start | bytes 22020104 | tf_op jit(solution)/shard_map/ppermute | solution.py:158
  0.5 0.9 %copy-start = (bf16[1,32,3584]{2,1,0:T(8,128)(2,1)S(1)}, bf16[1,32,3584]{2,1,0:T(8,128)(2,1)}, u32[]{:S(2)}) copy-start(bf16[1,32,3584]{2,1,0:T(8,128)(2,1)} %param.5) | copy-start | bytes 688132
  1.4 0.7 copy-start.1
  2.1 0.7 copy-start.2
  2.8 36.7 %copy-start.3 = (bf16[1,512,3584]{2,1,0:T(8,128)(2,1)S(1)}, bf16[1,512,3584]{2,1,0:T(8,128)(2,1)}, u32[]{:S(2)}) copy-start(bf16[1,512,3584]{2,1,0:T(8,128)(2,1)} %param.9) | copy-start | bytes 11010052
  3.3 37.0 %slice-start = ((s8[7340032]{0:T(1024)(128)(4,1)}), s8[4194304]{0:T(1024)(128)(4,1)S(1)}, s32[]{:S(2)}) async-start(s8[7340032]{0:T(1024)(128)(4,1)} %bitcast.31), calls=%async_computation | async-start | bytes 8388608
  3.3 15.1 %collective-permute-start.1 = (bf16[16,3584]{1,0:T(8,128)(2,1)S(1)}, bf16[16,3584]{1,0:T(8,128)(2,1)S(1)}, u32[]{:S(2)}, u32[]{:S(2)}) collective-permute-start(bf16[16,3584]{1,0:T(8,128)(2,1)S(1)} %get-tuple-element.15), channel_id=1, source_target_pairs={{0,8},{1,9},{2,10},{3,11},{4,12},{5,13},{6,14},{7,15},{8,0},{9,1},... | collective-permute-start | bytes 344072 | tf_op jit(solution)/shard_map/ppermute | solution.py:144
  6.9 22.8 %collective-permute-start.8 = (bf16[16,3584]{1,0:T(8,128)(2,1)S(1)}, bf16[16,3584]{1,0:T(8,128)(2,1)S(1)}, u32[]{:S(2)}, u32[]{:S(2)}) collective-permute-start(bf16[16,3584]{1,0:T(8,128)(2,1)S(1)} %get-tuple-element.19), channel_id=1, source_target_pairs={{0,12},{1,13},{2,14},{3,15},{4,8},{5,9},{6,10},{7,11},{8,4},{9,5},... | collective-permute-start | bytes 344072 | tf_op jit(solution)/shard_map/ppermute | solution.py:144
  8.3 21.6 %collective-permute-start.9 = (bf16[16,3584]{1,0:T(8,128)(2,1)S(1)}, bf16[16,3584]{1,0:T(8,128)(2,1)S(1)}, u32[]{:S(2)}, u32[]{:S(2)}) collective-permute-start(bf16[16,3584]{1,0:T(8,128)(2,1)S(1)} %get-tuple-element.20), channel_id=1, source_target_pairs={{0,14},{1,15},{2,12},{3,13},{4,10},{5,11},{6,8},{7,9},{8,6},{9,7},... | collective-permute-start | bytes 344072 | tf_op jit(solution)/shard_map/ppermute | solution.py:144
  11.7 18.7 %collective-permute-start.10 = (bf16[16,3584]{1,0:T(8,128)(2,1)S(1)}, bf16[16,3584]{1,0:T(8,128)(2,1)S(1)}, u32[]{:S(2)}, u32[]{:S(2)}) collective-permute-start(bf16[16,3584]{1,0:T(8,128)(2,1)S(1)} %get-tuple-element.21), channel_id=1, source_target_pairs={{0,4},{1,5},{2,6},{3,7},{4,0},{5,1},{6,2},{7,3},{8,12},{9,13},{10,... | collective-permute-start | bytes 344072 | tf_op jit(solution)/shard_map/ppermute | solution.py:144
  18.4 10.7 %collective-permute-start.2 = (bf16[16,3584]{1,0:T(8,128)(2,1)S(1)}, bf16[16,3584]{1,0:T(8,128)(2,1)S(1)}, u32[]{:S(2)}, u32[]{:S(2)}) collective-permute-start(bf16[16,3584]{1,0:T(8,128)(2,1)S(1)} %get-tuple-element.16), channel_id=1, source_target_pairs={{0,10},{1,11},{2,8},{3,9},{4,14},{5,15},{6,12},{7,13},{8,2},{9,3},... | collective-permute-start | bytes 344072 | tf_op jit(solution)/shard_map/ppermute | solution.py:144
  29.0 5.8 %collective-permute-start.11 = (bf16[16,3584]{1,0:T(8,128)(2,1)S(1)}, bf16[16,3584]{1,0:T(8,128)(2,1)S(1)}, u32[]{:S(2)}, u32[]{:S(2)}) collective-permute-start(bf16[16,3584]{1,0:T(8,128)(2,1)S(1)} %get-tuple-element.22), channel_id=1, source_target_pairs={{0,6},{1,7},{2,4},{3,5},{4,2},{5,3},{6,0},{7,1},{8,14},{9,15},{10,... | collective-permute-start | bytes 344072 | tf_op jit(solution)/shard_map/ppermute | solution.py:144
  29.7 17.1 %collective-permute-start.5 = (bf16[512,3584]{1,0:T(8,128)(2,1)}, bf16[512,3584]{1,0:T(8,128)(2,1)S(1)}, u32[]{:S(2)}, u32[]{:S(2)}) collective-permute-start(bf16[512,3584]{1,0:T(8,128)(2,1)} %bitcast.33), channel_id=1, source_target_pairs={{0,1},{1,0},{2,3},{3,2},{4,5},{5,4},{6,7},{7,6},{8,9},{9,8},{10,11... | collective-permute-start | bytes 11010056 | tf_op jit(solution)/shard_map/ppermute | solution.py:158
  29.8 10.3 %collective-permute-start.3 = (bf16[16,3584]{1,0:T(8,128)(2,1)S(1)}, bf16[16,3584]{1,0:T(8,128)(2,1)S(1)}, u32[]{:S(2)}, u32[]{:S(2)}) collective-permute-start(bf16[16,3584]{1,0:T(8,128)(2,1)S(1)} %get-tuple-element.18), channel_id=1, source_target_pairs={{0,2},{1,3},{2,0},{3,1},{4,6},{5,7},{6,4},{7,5},{8,10},{9,11},{10,... | collective-permute-start | bytes 344072 | tf_op jit(solution)/shard_map/ppermute | solution.py:144
  30.4 31.1 %collective-permute-start = (bf16[96,128]{1,0:T(8,128)(2,1)S(1)}, bf16[96,128]{1,0:T(8,128)(2,1)S(1)}, u32[]{:S(2)}, u32[]{:S(2)}) collective-permute-start(bf16[96,128]{1,0:T(8,128)(2,1)S(1)} %get-tuple-element.14), channel_id=1, source_target_pairs={{0,16},{1,17},{2,18},{3,19},{4,20},{5,21},{6,22},{7,23},{8,24},{9,... | collective-permute-start | bytes 73736 | tf_op jit(solution)/shard_map/ppermute | solution.py:144
  34.8 5.4 %slice-start.1 = ((s8[7340032]{0:T(1024)(128)(4,1)}), s8[3145728]{0:T(1024)(128)(4,1)S(1)}, s32[]{:S(2)}) async-start(s8[7340032]{0:T(1024)(128)(4,1)} %bitcast.31), calls=%async_computation.1 | async-start | bytes 6291456
  47.6 14.7 %collective-permute-start.12 = (bf16[16,3584]{1,0:T(8,128)(2,1)S(1)}, bf16[16,3584]{1,0:T(8,128)(2,1)S(1)}, u32[]{:S(2)}, u32[]{:S(2)}) collective-permute-start(bf16[16,3584]{1,0:T(8,128)(2,1)S(1)} %get-tuple-element.26), channel_id=1, source_target_pairs={{0,20},{1,21},{2,22},{3,23},{4,16},{5,17},{6,18},{7,19},{8,28},{9,... | collective-permute-start | bytes 344072 | tf_op jit(solution)/shard_map/ppermute | solution.py:144
  48.7 16.9 %collective-permute-start.13 = (bf16[16,3584]{1,0:T(8,128)(2,1)S(1)}, bf16[16,3584]{1,0:T(8,128)(2,1)S(1)}, u32[]{:S(2)}, u32[]{:S(2)}) collective-permute-start(bf16[16,3584]{1,0:T(8,128)(2,1)S(1)} %get-tuple-element.25), channel_id=1, source_target_pairs={{0,22},{1,23},{2,20},{3,21},{4,18},{5,19},{6,16},{7,17},{8,30},{9,... | collective-permute-start | bytes 344072 | tf_op jit(solution)/shard_map/ppermute | solution.py:144
  50.7 16.1 %collective-permute-start.16 = (bf16[16,3584]{1,0:T(8,128)(2,1)S(1)}, bf16[16,3584]{1,0:T(8,128)(2,1)S(1)}, u32[]{:S(2)}, u32[]{:S(2)}) collective-permute-start(bf16[16,3584]{1,0:T(8,128)(2,1)S(1)} %get-tuple-element.24), channel_id=1, source_target_pairs={{0,28},{1,29},{2,30},{3,31},{4,24},{5,25},{6,26},{7,27},{8,20},{9,... | collective-permute-start | bytes 344072 | tf_op jit(solution)/shard_map/ppermute | solution.py:144
  55.4 13.1 %collective-permute-start.17 = (bf16[16,3584]{1,0:T(8,128)(2,1)S(1)}, bf16[16,3584]{1,0:T(8,128)(2,1)S(1)}, u32[]{:S(2)}, u32[]{:S(2)}) collective-permute-start(bf16[16,3584]{1,0:T(8,128)(2,1)S(1)} %get-tuple-element.23), channel_id=1, source_target_pairs={{0,30},{1,31},{2,28},{3,29},{4,26},{5,27},{6,24},{7,25},{8,22},{9,... | collective-permute-start | bytes 344072 | tf_op jit(solution)/shard_map/ppermute | solution.py:144
  61.6 11.7 %collective-permute-start.14 = (bf16[16,3584]{1,0:T(8,128)(2,1)S(1)}, bf16[16,3584]{1,0:T(8,128)(2,1)S(1)}, u32[]{:S(2)}, u32[]{:S(2)}) collective-permute-start(bf16[16,3584]{1,0:T(8,128)(2,1)S(1)} %get-tuple-element.28), channel_id=1, source_target_pairs={{0,24},{1,25},{2,26},{3,27},{4,28},{5,29},{6,30},{7,31},{8,16},{9,... | collective-permute-start | bytes 344072 | tf_op jit(solution)/shard_map/ppermute | solution.py:144
  62.3 12.4 %collective-permute-start.15 = (bf16[16,3584]{1,0:T(8,128)(2,1)S(1)}, bf16[16,3584]{1,0:T(8,128)(2,1)S(1)}, u32[]{:S(2)}, u32[]{:S(2)}) collective-permute-start(bf16[16,3584]{1,0:T(8,128)(2,1)S(1)} %get-tuple-element.27), channel_id=1, source_target_pairs={{0,26},{1,27},{2,24},{3,25},{4,30},{5,31},{6,28},{7,29},{8,18},{9,... | collective-permute-start | bytes 344072 | tf_op jit(solution)/shard_map/ppermute | solution.py:144
  65.5 9.2 %collective-permute-start.6 = (bf16[16,3584]{1,0:T(8,128)(2,1)S(1)}, bf16[16,3584]{1,0:T(8,128)(2,1)S(1)}, u32[]{:S(2)}, u32[]{:S(2)}) collective-permute-start(bf16[16,3584]{1,0:T(8,128)(2,1)S(1)} %get-tuple-element.30), channel_id=1, source_target_pairs={{0,16},{1,17},{2,18},{3,19},{4,20},{5,21},{6,22},{7,23},{8,24},{9,... | collective-permute-start | bytes 344072 | tf_op jit(solution)/shard_map/ppermute | solution.py:144
  66.9 9.0 %collective-permute-start.7 = (bf16[16,3584]{1,0:T(8,128)(2,1)S(1)}, bf16[16,3584]{1,0:T(8,128)(2,1)S(1)}, u32[]{:S(2)}, u32[]{:S(2)}) collective-permute-start(bf16[16,3584]{1,0:T(8,128)(2,1)S(1)} %get-tuple-element.29), channel_id=1, source_target_pairs={{0,18},{1,19},{2,16},{3,17},{4,22},{5,23},{6,20},{7,21},{8,26},{9,... | collective-permute-start | bytes 344072 | tf_op jit(solution)/shard_map/ppermute | solution.py:144

commit v3 on v0

--- a/solution.py
+++ b/solution.py
@@ -1,6 +1,8 @@
 import jax
 import jax.numpy as jnp
 from jax import lax
+from jax.experimental import pallas as pl
+from jax.experimental.pallas import tpu as pltpu
 from jax.sharding import PartitionSpec as P
 
 
@@ -9,7 +11,7 @@
     return lax.ppermute(shard, axis, [(i, (i + by) % length) for i in range(length)])
 
 
-def per_device(rows, route_ids, route_weights, w_gate_up, w_down):
+def by_slots(rows, route_ids, route_weights, w_gate_up, w_down):
     devices = lax.axis_size("expert")
     experts = devices // 2
     tokens = rows[0]
@@ -47,8 +49,272 @@
     expert_out = jnp.sum(returned, axis=2).astype(jnp.bfloat16).reshape(slot_total, width)
     pair_out = expert_out[place].astype(jnp.float32) * route_weights[0].reshape(-1)[:, None]
     layer_out = jnp.sum(pair_out.reshape(tok_count, top_count, width), axis=1).astype(jnp.bfloat16)
-    handed = passed_along(layer_out, "section", 1)
-    return handed[None]
+    return passed_along(layer_out, "section", 1)[None]
+
+
+RING = (0, 1, 3, 2)
+
+
+def on_ring(place):
+    return place ^ (place >> 1)
+
+
+def chosen_rows(codes, source, chip, capacity):
+    tok_count = codes.shape[0]
+    lane = lax.broadcasted_iota(jnp.int32, codes.shape, 1)
+    wanted = [
+        jnp.sum(jnp.where(lane == expert, codes, 0.0), axis=1, keepdims=True)
+        for expert in (chip, chip ^ 1)
+    ]
+    slot = lax.broadcasted_iota(jnp.int32, (tok_count, 2 * capacity), 1)
+    code = jnp.where(slot < capacity, slot + 1, slot + 1 - capacity).astype(jnp.float32)
+    hit = jnp.where(slot < capacity, wanted[0], wanted[1]) == code
+    pick = jnp.where(hit, 1.0, 0.0).astype(jnp.bfloat16)
+    rows = lax.dot_general(
+        pick, source, (((0,), (0,)), ((), ())), preferred_element_type=jnp.float32
+    )
+    return rows.astype(jnp.bfloat16)
+
+
+def prepare_kernel(chip, ids_in, weights_in, rows_in, block, own, other, mixing, ids, weights, sems):
+    tok_count, width = rows_in.shape
+    top_count = ids.shape[0]
+    capacity = own.shape[0]
+    experts = mixing.shape[1] // capacity
+    copies = [
+        pltpu.make_async_copy(ids_in, ids, sems.at[0]),
+        pltpu.make_async_copy(weights_in, weights, sems.at[1]),
+        pltpu.make_async_copy(rows_in, block.at[:, pl.ds(0, width)], sems.at[2]),
+    ]
+    for copy in copies:
+        copy.start()
+    copies[0].wait()
+    copies[1].wait()
+    here = chip[0]
+    expert = lax.broadcasted_iota(jnp.int32, (experts, tok_count), 0)
+    square = (tok_count, tok_count)
+    earlier = lax.broadcasted_iota(jnp.int32, square, 0) < lax.broadcasted_iota(jnp.int32, square, 1)
+    named = jnp.zeros((experts, tok_count), jnp.float32)
+    for k in range(top_count):
+        named = named + jnp.where(ids[k : k + 1, :] == expert, 1.0, 0.0)
+    rank = jnp.dot(
+        named.astype(jnp.bfloat16),
+        jnp.where(earlier, 1.0, 0.0).astype(jnp.bfloat16),
+        preferred_element_type=jnp.float32,
+    )
+    code = jnp.where(named > 0.5, rank + 1.0, 0.0)
+    lanes = block.shape[1] - width
+    unit = jnp.where(
+        lax.broadcasted_iota(jnp.int32, (experts, lanes), 0)
+        == lax.broadcasted_iota(jnp.int32, (experts, lanes), 1),
+        1.0,
+        0.0,
+    ).astype(jnp.bfloat16)
+    codes = lax.dot_general(
+        code.astype(jnp.bfloat16), unit, (((0,), (0,)), ((), ())), preferred_element_type=jnp.float32
+    )
+    block[:, width:] = codes.astype(jnp.bfloat16)
+    slot = lax.broadcasted_iota(jnp.int32, (capacity, tok_count), 0).astype(jnp.float32)
+    scales = []
+    for at in range(experts):
+        plane = on_ring((on_ring(here >> 1) + (at >> 1)) & 3)
+        which = (plane << 1) | ((here & 1) ^ (at & 1))
+        scale = jnp.zeros((1, tok_count), jnp.float32)
+        for k in range(top_count):
+            scale = scale + jnp.where(ids[k : k + 1, :] == which, weights[k : k + 1, :], 0.0)
+        place = jnp.sum(jnp.where(expert == which, code, 0.0), axis=0, keepdims=True) - 1.0
+        scales.append(jnp.where(place == slot, scale, 0.0))
+    left = jnp.concatenate(scales, axis=0)
+    slots = experts * capacity
+    unit = jnp.where(
+        lax.broadcasted_iota(jnp.int32, (slots, slots), 0)
+        == lax.broadcasted_iota(jnp.int32, (slots, slots), 1),
+        1.0,
+        0.0,
+    ).astype(jnp.bfloat16)
+    for part in range(3):
+        piece = left.astype(jnp.bfloat16)
+        left = left - piece.astype(jnp.float32)
+        turned = lax.dot_general(
+            piece, unit, (((0,), (0,)), ((), ())), preferred_element_type=jnp.float32
+        )
+        mixing[part * tok_count : (part + 1) * tok_count, :] = turned.astype(jnp.bfloat16)
+    copies[2].wait()
+    rows = chosen_rows(codes, block[:, :width], here, capacity)
+    own[...] = rows[:capacity]
+    other[...] = rows[capacity:]
+
+
+def prepare(chip, ids, weights, tokens, experts, capacity, lanes):
+    tok_count, width = tokens.shape
+    vmem = pl.BlockSpec(memory_space=pltpu.VMEM)
+    anywhere = pl.BlockSpec(memory_space=pl.ANY)
+    half = jax.ShapeDtypeStruct((capacity, width), jnp.bfloat16)
+    return pl.pallas_call(
+        prepare_kernel,
+        out_shape=[
+            jax.ShapeDtypeStruct((tok_count, width + lanes), jnp.bfloat16),
+            half,
+            half,
+            jax.ShapeDtypeStruct((3 * tok_count, experts * capacity), jnp.bfloat16),
+        ],
+        in_specs=[pl.BlockSpec(memory_space=pltpu.SMEM), anywhere, anywhere, anywhere],
+        out_specs=[vmem] * 4,
+        scratch_shapes=[
+            pltpu.VMEM(ids.shape, ids.dtype),
+            pltpu.VMEM(weights.shape, weights.dtype),
+            pltpu.SemaphoreType.DMA((3,)),
+        ],
+        compiler_params=pltpu.CompilerParams(vmem_limit_bytes=60 << 20),
+        name="prepare",
+    )(chip, ids, weights, tokens)
+
+
+def choose_kernel(chip, block, own, other):
+    capacity, width = own.shape
+    codes = block[:, width:].astype(jnp.float32)
+    rows = chosen_rows(codes, block[:, :width], chip[0], capacity)
+    own[...] = rows[:capacity]
+    other[...] = rows[capacity:]
+
+
+def choose(chip, block, capacity, width):
+    vmem = pl.BlockSpec(memory_space=pltpu.VMEM)
+    half = jax.ShapeDtypeStruct((capacity, width), jnp.bfloat16)
+    return pl.pallas_call(
+        choose_kernel,
+        out_shape=[half, half],
+        in_specs=[pl.BlockSpec(memory_space=pltpu.SMEM), vmem],
+        out_specs=[vmem] * 2,
+        compiler_params=pltpu.CompilerParams(vmem_limit_bytes=12 << 20),
+        name="choose",
+    )(chip, block)
+
+
+def load_kernel(source, target, sem):
+    copy = pltpu.make_async_copy(source, target, sem)
+    copy.start()
+    copy.wait()
+
+
+def loaded(weights):
+    return pl.pallas_call(
+        load_kernel,
+        out_shape=pltpu.VMEM(weights.shape, weights.dtype),
+        in_specs=[pl.BlockSpec(memory_space=pltpu.HBM)],
+        out_specs=pl.BlockSpec(memory_space=pltpu.VMEM),
+        scratch_shapes=[pltpu.SemaphoreType.DMA],
+        compiler_params=pltpu.CompilerParams(vmem_limit_bytes=9 << 20),
+        cost_estimate=pl.CostEstimate(
+            flops=0, bytes_accessed=2 * weights.size * weights.dtype.itemsize, transcendentals=0
+        ),
+        name="loaded",
+    )(weights)
+
+
+def combine_kernel(mixing, *refs):
+    blocks, out = refs[:-1], refs[-1]
+    tok_count = out.shape[0]
+    slots = jnp.concatenate([block[...] for block in blocks], axis=0)
+    mixed = jnp.dot(mixing[...], slots, preferred_element_type=jnp.float32)
+    total = mixed[2 * tok_count :] + mixed[tok_count : 2 * tok_count] + mixed[:tok_count]
+    out[...] = total.astype(out.dtype)
+
+
+def combine(mixing, blocks):
+    tok_count = mixing.shape[0] // 3
+    vmem = pl.BlockSpec(memory_space=pltpu.VMEM)
+    return pl.pallas_call(
+        combine_kernel,
+        out_shape=jax.ShapeDtypeStruct((tok_count, blocks[0].shape[1]), jnp.bfloat16),
+        in_specs=[vmem] * (1 + len(blocks)),
+        out_specs=vmem,
+        compiler_params=pltpu.CompilerParams(vmem_limit_bytes=12 << 20),
+        name="combine",
+    )(mixing, *blocks)
+
+
+def sent(shard, sections, section_step, ring_step, flip):
+    planes = len(RING)
+    pairs = []
+    for s in range(sections):
+        for z in range(planes):
+            for y in range(2):
+                for core in range(2):
+                    plane = RING[(RING.index(z) + ring_step) % planes]
+                    target = (((s + section_step) % sections) * planes + plane) * 2 + (y ^ flip)
+                    pairs.append((((s * planes + z) * 2 + y) * 2 + core, target * 2 + core))
+    return lax.ppermute(shard, ("section", "expert"), pairs)
+
+
+def after(value, other):
+    return lax.optimization_barrier((value, other))[0]
+
+
+def by_ring(rows, route_ids, route_weights, w_gate_up, w_down):
+    sections = lax.axis_size("section")
+    devices = lax.axis_size("expert")
+    experts = devices // 2
+    planes = len(RING)
+    tokens = rows[0]
+    tok_count, width = tokens.shape
+    top_count = route_ids.shape[2]
+    capacity = max(2, 2 * tok_count * top_count // experts)
+    chip = (lax.axis_index("expert") // 2).reshape(1).astype(jnp.int32)
+    swap = [(i, i ^ 1) for i in range(devices)]
+    w_in, w_out = w_gate_up[0], w_down[0]
+    hidden = w_out.shape[0]
+    far_in = lax.ppermute(w_in, "expert", swap)
+    far_out = lax.ppermute(w_out, "expert", swap)
+    block, own, other, mixing = prepare(
+        chip, route_ids[0].T, route_weights[0].T, tokens, experts, capacity, 128
+    )
+    held = [(own, sent(other, sections, 0, 0, 1))]
+    near = (loaded(after(w_in, mixing)), loaded(after(w_out, mixing)))
+    mixing = sent(mixing, sections, 1, 0, 0)
+
+    def start(group):
+        slots = jnp.concatenate([part for step in group for part in held[step]], axis=0)
+        return slots, one_half(slots, *near)
+
+    def finish(group, slots, total):
+        total = (total + one_half(slots, *far)).astype(jnp.bfloat16)
+        pieces = total.reshape(-1, capacity, width)
+        back = [
+            sent(pieces[2 * at + flip], sections, 1, -step, flip)
+            for at, step in enumerate(group)
+            for flip in range(2)
+        ]
+        return total, back
+
+    def one_half(slots, first, second):
+        both = jnp.dot(slots, first, preferred_element_type=jnp.float32)
+        active = (jax.nn.silu(both[:, :hidden]) * both[:, hidden:]).astype(jnp.bfloat16)
+        return jnp.dot(active, second, preferred_element_type=jnp.float32)
+
+    block = sent(block, sections, 0, 1, 0)
+    own, other = choose(chip, block, capacity, width)
+    held.append((own, sent(other, sections, 0, 0, 1)))
+    slots, total = start((0, 1))
+    block = sent(block, sections, 0, 1, 0)
+    own, other = choose(chip, block, capacity, width)
+    held.append((own, sent(other, sections, 0, 0, 1)))
+    far = (loaded(after(far_in, own)), loaded(after(far_out, own)))
+    block = sent(block, sections, 0, 1, 0)
+    total, back = finish((0, 1), slots, total)
+    own, other = choose(chip, after(block, total), capacity, width)
+    held[2] = after(held[2], own)
+    held.append((own, sent(other, sections, 0, 0, 1)))
+    total, more = finish((2,), *start((2,)))
+    held[3], back = lax.optimization_barrier((held[3], back))
+    back = back + more + finish((3,), *start((3,)))[1]
+    return combine(mixing, back)[None]
+
+
+def per_device(rows, route_ids, route_weights, w_gate_up, w_down):
+    experts = lax.axis_size("expert") // 2
+    plan = by_ring if experts == 2 * len(RING) else by_slots
+    return plan(rows, route_ids, route_weights, w_gate_up, w_down)
 
 
 def solution(mesh):

time: 120 us -> 66.5 us (0.55)
  the two profiles are of different devices: /device:TPU:12 before, /device:TPU:0 now
where the time goes in v3:
time: 66.5 us; the launch traced here: 66.2 us
  starting transfers between devices  26.3 us (40%)
  matrix products  12.6 us (19%)
  waiting for transfers between devices  11.5 us (17%)
  Pallas kernels  9.95 us (15%)
  local copies, waits for them, and re-layouts  5.67 us (9%)
    ppermute x16, starting transfers between devices, sent(): return lax.ppermute(shard, ('section', 'expert'), pairs)  25.8 us
    ppermute x16, waiting for transfers between devices, sent(): return lax.ppermute(shard, ('section', 'expert'), pairs)  11.5 us
    dot_general x6, matrix products, one_half(): both = jnp.dot(slots, first, preferred_element_type=jnp.float32)  8.23 us
    pallas_call x4, Pallas kernels, loaded(): pl.pallas_call(load_kernel, out_shape=pltpu.VMEM(weights.shape, weights.d...  5.89 us
    unnamed x11, local copies, waits for them, and re-layouts  5.56 us
    dot_general x6, matrix products, one_half(): return jnp.dot(active, second, preferred_element_type=jnp.float32)  4.34 us
    pallas_call x1, Pallas kernels, prepare(): pl.pallas_call(prepare_kernel, out_shape=[jax.ShapeDtypeStruct((tok_count...  2.07 us
  transfers between devices with their start and end apart: 18, of which 5 were waited for; matrix products, arithmetic and copies ran while one was open for 16% of the time, Pallas kernels for 13%

profile of v3, /device:TPU:0, one launch (start us, length us, event | category | flops | bytes accessed | tf_op | source)
XLA Modules:
  0.0 66.2 jit_solution(11607395181265147238)
XLA Ops:
  0.5 2.1 %prepare.1 = (bf16[32,3712]{1,0:T(8,128)(2,1)}, bf16[16,3584]{1,0:T(8,128)(2,1)}, bf16[16,3584]{1,0:T(8,128)(2,1)}, bf16[96,128]{1,0:T(8,128)(2,1)}) custom-call(s32[1]{0:T(128)} %bitcast.chip, s32[2,32]{1,0:T(2,128)} %bitcast.34, f32[2,32]{1,0:T(2,128)} %bitcast.35, bf16[32,3584]{1,0:T(8,128)(2,1)} %bitcast.33), custom_call_target="tpu_custom_call" | custom-call | tf_op jit(solution)/shard_map/prepare/pallas_call | solution.py:153
  2.6 3.1 %collective-permute-start.1 = (bf16[32,3712]{1,0:T(8,128)(2,1)}, bf16[32,3712]{1,0:T(8,128)(2,1)S(1)}, u32[]{:S(2)}, u32[]{:S(2)}) collective-permute-start(bf16[32,3712]{1,0:T(8,128)(2,1)} %get-tuple-element.29), channel_id=1, source_target_pairs={{0,4},{1,5},{2,6},{3,7},{4,12},{5,13},{6,14},{7,15},{8,0},{9,1},{1... | collective-permute-start | bytes 712712 | tf_op jit(solution)/shard_map/ppermute | solution.py:247
  5.7 1.5 %collective-permute-start.4 = (bf16[16,3584]{1,0:T(8,128)(2,1)}, bf16[16,3584]{1,0:T(8,128)(2,1)S(1)}, u32[]{:S(2)}, u32[]{:S(2)}) collective-permute-start(bf16[16,3584]{1,0:T(8,128)(2,1)} %get-tuple-element.31), channel_id=1, source_target_pairs={{0,2},{1,3},{2,0},{3,1},{4,6},{5,7},{6,4},{7,5},{8,10},{9,11},{10,... | collective-permute-start | bytes 344072 | tf_op jit(solution)/shard_map/ppermute | solution.py:247
  8.1 3.1 %copy-done = bf16[1,3584,1024]{2,1,0:T(8,128)(2,1)S(1)} copy-done((bf16[1,3584,1024]{2,1,0:T(8,128)(2,1)S(1)}, bf16[1,3584,1024]{2,1,0:T(8,128)(2,1)}, u32[]{:S(2)}) %copy-start) | copy-done | bytes 7340056
  11.7 1.5 %copy-done.1 = bf16[1,512,3584]{2,1,0:T(8,128)(2,1)S(1)} copy-done((bf16[1,512,3584]{2,1,0:T(8,128)(2,1)S(1)}, bf16[1,512,3584]{2,1,0:T(8,128)(2,1)}, u32[]{:S(2)}) %copy-start.1) | copy-done | bytes 3670040
  14.8 2.3 %collective-permute-start.2 = (bf16[32,3712]{1,0:T(8,128)(2,1)S(1)}, bf16[32,3712]{1,0:T(8,128)(2,1)S(1)}, u32[]{:S(2)}, u32[]{:S(2)}) collective-permute-start(bf16[32,3712]{1,0:T(8,128)(2,1)S(1)} %collective-permute-done.1.block), channel_id=1, source_target_pairs={{0,4},{1,5},{2,6},{3,7},{4,12},{5,13},{6,14},{7,15},{8,0},{9,1},{1... | collective-permute-start | bytes 712712 | tf_op jit(solution)/shard_map/ppermute | solution.py:247
  17.1 1.6 %collective-permute-done.5 = bf16[16,3584]{1,0:T(8,128)(2,1)S(1)} collective-permute-done((bf16[16,3584]{1,0:T(8,128)(2,1)S(1)}, bf16[16,3584]{1,0:T(8,128)(2,1)S(1)}, u32[]{:S(2)}, u32[]{:S(2)}) %collective-permute-start.5) | collective-permute-done | bytes 114720 | tf_op jit(solution)/shard_map/ppermute | solution.py:247
  18.7 1.4 %fusion.33 = f32[64,1024]{1,0:T(8,128)S(1)} fusion(bf16[64,3584]{1,0:T(8,128)(2,1)S(1)} %constant_dynamic-update-slice_fusion, bf16[3584,1024]{1,0:T(8,128)(2,1)S(1)} %loaded.4), kind=kOutput, calls=%fused_computation.44 | convolution fusion | flops 469762048 | bytes 8060928 | tf_op jit(solution)/shard_map/dot_general | solution.py:291
  20.8 1.5 %collective-permute-done.2.block = bf16[32,3712]{1,0:T(8,128)(2,1)S(1)} collective-permute-done((bf16[32,3712]{1,0:T(8,128)(2,1)S(1)}, bf16[32,3712]{1,0:T(8,128)(2,1)S(1)}, u32[]{:S(2)}, u32[]{:S(2)}) %collective-permute-start.2) | collective-permute-done | bytes 237600 | tf_op jit(solution)/shard_map/ppermute | solution.py:247
  22.6 1.5 %collective-permute-start.13 = (bf16[16,3584]{1,0:T(8,128)(2,1)S(1)}, bf16[16,3584]{1,0:T(8,128)(2,1)S(1)}, u32[]{:S(2)}, u32[]{:S(2)}) collective-permute-start(bf16[16,3584]{1,0:T(8,128)(2,1)S(1)} %get-tuple-element.46), channel_id=1, source_target_pairs={{0,2},{1,3},{2,0},{3,1},{4,6},{5,7},{6,4},{7,5},{8,10},{9,11},{10,... | collective-permute-start | bytes 344072 | tf_op jit(solution)/shard_map/ppermute | solution.py:247
  24.1 1.7 %collective-permute-start.3 = (bf16[32,3712]{1,0:T(8,128)(2,1)S(1)}, bf16[32,3712]{1,0:T(8,128)(2,1)S(1)}, u32[]{:S(2)}, u32[]{:S(2)}) collective-permute-start(bf16[32,3712]{1,0:T(8,128)(2,1)S(1)} %collective-permute-done.2.block), channel_id=1, source_target_pairs={{0,4},{1,5},{2,6},{3,7},{4,12},{5,13},{6,14},{7,15},{8,0},{9,1},{1... | collective-permute-start | bytes 712712 | tf_op jit(solution)/shard_map/ppermute | solution.py:247
  25.8 2.0 %loaded.7 = bf16[512,3584]{1,0:T(8,128)(2,1)S(1)} custom-call(bf16[512,3584]{1,0:T(8,128)(2,1)} %collective-permute-done.7.source), custom_call_target="tpu_custom_call" | custom-call | bytes 7340032 | tf_op jit(solution)/shard_map/loaded/pallas_call | solution.py:201
  27.9 3.1 %loaded.6 = bf16[3584,1024]{1,0:T(8,128)(2,1)S(1)} custom-call(bf16[3584,1024]{1,0:T(8,128)(2,1)} %collective-permute-done.6.source), custom_call_target="tpu_custom_call" | custom-call | bytes 14680064 | tf_op jit(solution)/shard_map/loaded/pallas_call | solution.py:201
  31.0 1.4 %fusion.34 = f32[64,1024]{1,0:T(8,128)S(1)} fusion(bf16[64,3584]{1,0:T(8,128)(2,1)S(1)} %constant_dynamic-update-slice_fusion, bf16[3584,1024]{1,0:T(8,128)(2,1)S(1)} %loaded.6), kind=kOutput, calls=%fused_computation.45 | convolution fusion | flops 469762048 | bytes 8060928 | tf_op jit(solution)/shard_map/dot_general | solution.py:291
  34.9 1.4 %fusion.35 = f32[32,1024]{1,0:T(8,128)S(1)} fusion(bf16[32,3584]{1,0:T(8,128)(2,1)S(1)} %constant_dynamic-update-slice_fusion.4, bf16[3584,1024]{1,0:T(8,128)(2,1)S(1)} %loaded.4), kind=kOutput, calls=%fused_computation.46 | convolution fusion | flops 234881024 | bytes 7700480 | tf_op jit(solution)/shard_map/dot_general | solution.py:291
  36.3 1.4 %collective-permute-start.10 = (bf16[16,3584]{1,0:T(8,128)(2,1)S(1)}, bf16[16,3584]{1,0:T(8,128)(2,1)S(1)}, u32[]{:S(2)}, u32[]{:S(2)}) collective-permute-start(bf16[16,3584]{1,0:T(8,128)(2,1)S(1)} %get-tuple-element.53), channel_id=1, source_target_pairs={{0,18},{1,19},{2,16},{3,17},{4,22},{5,23},{6,20},{7,21},{8,26},{9,... | collective-permute-start | bytes 344072 | tf_op jit(solution)/shard_map/ppermute | solution.py:247
  39.0 2.1 %collective-permute-start.12 = (bf16[16,3584]{1,0:T(8,128)(2,1)S(1)}, bf16[16,3584]{1,0:T(8,128)(2,1)S(1)}, u32[]{:S(2)}, u32[]{:S(2)}) collective-permute-start(bf16[16,3584]{1,0:T(8,128)(2,1)S(1)} %get-tuple-element.51), channel_id=1, source_target_pairs={{0,26},{1,27},{2,24},{3,25},{4,18},{5,19},{6,16},{7,17},{8,30},{9,... | collective-permute-start | bytes 344072 | tf_op jit(solution)/shard_map/ppermute | solution.py:247
  41.7 1.5 %collective-permute-start.8 = (bf16[16,3584]{1,0:T(8,128)(2,1)S(1)}, bf16[16,3584]{1,0:T(8,128)(2,1)S(1)}, u32[]{:S(2)}, u32[]{:S(2)}) collective-permute-start(bf16[16,3584]{1,0:T(8,128)(2,1)S(1)} %get-tuple-element.41), channel_id=1, source_target_pairs={{0,2},{1,3},{2,0},{3,1},{4,6},{5,7},{6,4},{7,5},{8,10},{9,11},{10,... | collective-permute-start | bytes 344072 | tf_op jit(solution)/shard_map/ppermute | solution.py:247
  44.7 2.7 %collective-permute-done.10.refs_1_ = bf16[16,3584]{1,0:T(8,128)(2,1)S(1)} collective-permute-done((bf16[16,3584]{1,0:T(8,128)(2,1)S(1)}, bf16[16,3584]{1,0:T(8,128)(2,1)S(1)}, u32[]{:S(2)}, u32[]{:S(2)}) %collective-permute-start.10) | collective-permute-done | bytes 114720 | tf_op jit(solution)/shard_map/ppermute | solution.py:247
  47.5 2.8 %collective-permute-start.15 = (bf16[16,3584]{1,0:T(8,128)(2,1)S(1)}, bf16[16,3584]{1,0:T(8,128)(2,1)S(1)}, u32[]{:S(2)}, u32[]{:S(2)}) collective-permute-start(bf16[16,3584]{1,0:T(8,128)(2,1)S(1)} %get-tuple-element.57), channel_id=1, source_target_pairs={{0,30},{1,31},{2,28},{3,29},{4,26},{5,27},{6,24},{7,25},{8,22},{9,... | collective-permute-start | bytes 344072 | tf_op jit(solution)/shard_map/ppermute | solution.py:247
  51.7 1.4 %fusion.37 = f32[32,1024]{1,0:T(8,128)S(1)} fusion(bf16[32,3584]{1,0:T(8,128)(2,1)S(1)} %constant_dynamic-update-slice_fusion.6, bf16[3584,1024]{1,0:T(8,128)(2,1)S(1)} %loaded.4), kind=kOutput, calls=%fused_computation.48 | convolution fusion | flops 234881024 | bytes 7700480 | tf_op jit(solution)/shard_map/dot_general | solution.py:291
  54.5 2.9 %collective-permute-start.16 = (bf16[16,3584]{1,0:T(8,128)(2,1)S(1)}, bf16[16,3584]{1,0:T(8,128)(2,1)S(1)}, u32[]{:S(2)}, u32[]{:S(2)}) collective-permute-start(bf16[16,3584]{1,0:T(8,128)(2,1)S(1)} %get-tuple-element.56), channel_id=1, source_target_pairs={{0,20},{1,21},{2,22},{3,23},{4,28},{5,29},{6,30},{7,31},{8,16},{9,... | collective-permute-start | bytes 344072 | tf_op jit(solution)/shard_map/ppermute | solution.py:247
  59.5 2.9 %collective-permute-done.mixing = bf16[96,128]{1,0:T(8,128)(2,1)S(1)} collective-permute-done((bf16[96,128]{1,0:T(8,128)(2,1)S(1)}, bf16[96,128]{1,0:T(8,128)(2,1)S(1)}, u32[]{:S(2)}, u32[]{:S(2)}) %collective-permute-start) | collective-permute-done | bytes 24608 | tf_op jit(solution)/shard_map/ppermute | solution.py:247
  62.4 2.8 %collective-permute-done.17.refs_7_ = bf16[16,3584]{1,0:T(8,128)(2,1)S(1)} collective-permute-done((bf16[16,3584]{1,0:T(8,128)(2,1)S(1)}, bf16[16,3584]{1,0:T(8,128)(2,1)S(1)}, u32[]{:S(2)}, u32[]{:S(2)}) %collective-permute-start.17) | collective-permute-done | bytes 114720 | tf_op jit(solution)/shard_map/ppermute | solution.py:247
  (50 shorter events, 16.4 us)
Async XLA Ops:
  0.0 27.9 %collective-permute-start.6 = (bf16[3584,1024]{1,0:T(8,128)(2,1)}, bf16[3584,1024]{1,0:T(8,128)(2,1)}, u32[]{:S(2)}, u32[]{:S(2)}) collective-permute-start(bf16[3584,1024]{1,0:T(8,128)(2,1)} %bitcast.29), channel_id=1, source_target_pairs={{0,1},{1,0},{2,3},{3,2},{4,5},{5,4},{6,7},{7,6},{8,9},{9,8},{10,11... | collective-permute-start | bytes 22020104 | tf_op jit(solution)/shard_map/ppermute | solution.py:267
  0.5 25.4 %collective-permute-start.7 = (bf16[512,3584]{1,0:T(8,128)(2,1)}, bf16[512,3584]{1,0:T(8,128)(2,1)}, u32[]{:S(2)}, u32[]{:S(2)}) collective-permute-start(bf16[512,3584]{1,0:T(8,128)(2,1)} %bitcast.31), channel_id=1, source_target_pairs={{0,1},{1,0},{2,3},{3,2},{4,5},{5,4},{6,7},{7,6},{8,9},{9,8},{10,11... | collective-permute-start | bytes 11010056 | tf_op jit(solution)/shard_map/ppermute | solution.py:268
  2.6 10.9 %collective-permute-start.1 = (bf16[32,3712]{1,0:T(8,128)(2,1)}, bf16[32,3712]{1,0:T(8,128)(2,1)S(1)}, u32[]{:S(2)}, u32[]{:S(2)}) collective-permute-start(bf16[32,3712]{1,0:T(8,128)(2,1)} %get-tuple-element.29), channel_id=1, source_target_pairs={{0,4},{1,5},{2,6},{3,7},{4,12},{5,13},{6,14},{7,15},{8,0},{9,1},{1... | collective-permute-start | bytes 712712 | tf_op jit(solution)/shard_map/ppermute | solution.py:247
  5.7 7.8 %collective-permute-start.4 = (bf16[16,3584]{1,0:T(8,128)(2,1)}, bf16[16,3584]{1,0:T(8,128)(2,1)S(1)}, u32[]{:S(2)}, u32[]{:S(2)}) collective-permute-start(bf16[16,3584]{1,0:T(8,128)(2,1)} %get-tuple-element.31), channel_id=1, source_target_pairs={{0,2},{1,3},{2,0},{3,1},{4,6},{5,7},{6,4},{7,5},{8,10},{9,11},{10,... | collective-permute-start | bytes 344072 | tf_op jit(solution)/shard_map/ppermute | solution.py:247
  8.1 3.1 %copy-start = (bf16[1,3584,1024]{2,1,0:T(8,128)(2,1)S(1)}, bf16[1,3584,1024]{2,1,0:T(8,128)(2,1)}, u32[]{:S(2)}) copy-start(bf16[1,3584,1024]{2,1,0:T(8,128)(2,1)} %param.8) | copy-start | bytes 22020100
  11.2 2.0 %copy-start.1 = (bf16[1,512,3584]{2,1,0:T(8,128)(2,1)S(1)}, bf16[1,512,3584]{2,1,0:T(8,128)(2,1)}, u32[]{:S(2)}) copy-start(bf16[1,512,3584]{2,1,0:T(8,128)(2,1)} %param.9) | copy-start | bytes 11010052
  13.8 4.9 %collective-permute-start.5 = (bf16[16,3584]{1,0:T(8,128)(2,1)S(1)}, bf16[16,3584]{1,0:T(8,128)(2,1)S(1)}, u32[]{:S(2)}, u32[]{:S(2)}) collective-permute-start(bf16[16,3584]{1,0:T(8,128)(2,1)S(1)} %get-tuple-element.33), channel_id=1, source_target_pairs={{0,2},{1,3},{2,0},{3,1},{4,6},{5,7},{6,4},{7,5},{8,10},{9,11},{10,... | collective-permute-start | bytes 344072 | tf_op jit(solution)/shard_map/ppermute | solution.py:247
  14.8 7.5 %collective-permute-start.2 = (bf16[32,3712]{1,0:T(8,128)(2,1)S(1)}, bf16[32,3712]{1,0:T(8,128)(2,1)S(1)}, u32[]{:S(2)}, u32[]{:S(2)}) collective-permute-start(bf16[32,3712]{1,0:T(8,128)(2,1)S(1)} %collective-permute-done.1.block), channel_id=1, source_target_pairs={{0,4},{1,5},{2,6},{3,7},{4,12},{5,13},{6,14},{7,15},{8,0},{9,1},{1... | collective-permute-start | bytes 712712 | tf_op jit(solution)/shard_map/ppermute | solution.py:247
  22.6 10.9 %collective-permute-start.13 = (bf16[16,3584]{1,0:T(8,128)(2,1)S(1)}, bf16[16,3584]{1,0:T(8,128)(2,1)S(1)}, u32[]{:S(2)}, u32[]{:S(2)}) collective-permute-start(bf16[16,3584]{1,0:T(8,128)(2,1)S(1)} %get-tuple-element.46), channel_id=1, source_target_pairs={{0,2},{1,3},{2,0},{3,1},{4,6},{5,7},{6,4},{7,5},{8,10},{9,11},{10,... | collective-permute-start | bytes 344072 | tf_op jit(solution)/shard_map/ppermute | solution.py:247
  24.1 9.0 %collective-permute-start.3 = (bf16[32,3712]{1,0:T(8,128)(2,1)S(1)}, bf16[32,3712]{1,0:T(8,128)(2,1)S(1)}, u32[]{:S(2)}, u32[]{:S(2)}) collective-permute-start(bf16[32,3712]{1,0:T(8,128)(2,1)S(1)} %collective-permute-done.2.block), channel_id=1, source_target_pairs={{0,4},{1,5},{2,6},{3,7},{4,12},{5,13},{6,14},{7,15},{8,0},{9,1},{1... | collective-permute-start | bytes 712712 | tf_op jit(solution)/shard_map/ppermute | solution.py:247
  36.3 11.0 %collective-permute-start.10 = (bf16[16,3584]{1,0:T(8,128)(2,1)S(1)}, bf16[16,3584]{1,0:T(8,128)(2,1)S(1)}, u32[]{:S(2)}, u32[]{:S(2)}) collective-permute-start(bf16[16,3584]{1,0:T(8,128)(2,1)S(1)} %get-tuple-element.53), channel_id=1, source_target_pairs={{0,18},{1,19},{2,16},{3,17},{4,22},{5,23},{6,20},{7,21},{8,26},{9,... | collective-permute-start | bytes 344072 | tf_op jit(solution)/shard_map/ppermute | solution.py:247
  37.7 9.8 %collective-permute-start.11 = (bf16[16,3584]{1,0:T(8,128)(2,1)S(1)}, bf16[16,3584]{1,0:T(8,128)(2,1)S(1)}, u32[]{:S(2)}, u32[]{:S(2)}) collective-permute-start(bf16[16,3584]{1,0:T(8,128)(2,1)S(1)} %get-tuple-element.52), channel_id=1, source_target_pairs={{0,24},{1,25},{2,26},{3,27},{4,16},{5,17},{6,18},{7,19},{8,28},{9,... | collective-permute-start | bytes 344072 | tf_op jit(solution)/shard_map/ppermute | solution.py:247
  39.0 11.2 %collective-permute-start.12 = (bf16[16,3584]{1,0:T(8,128)(2,1)S(1)}, bf16[16,3584]{1,0:T(8,128)(2,1)S(1)}, u32[]{:S(2)}, u32[]{:S(2)}) collective-permute-start(bf16[16,3584]{1,0:T(8,128)(2,1)S(1)} %get-tuple-element.51), channel_id=1, source_target_pairs={{0,26},{1,27},{2,24},{3,25},{4,18},{5,19},{6,16},{7,17},{8,30},{9,... | collective-permute-start | bytes 344072 | tf_op jit(solution)/shard_map/ppermute | solution.py:247
  41.1 9.1 %collective-permute-start.9 = (bf16[16,3584]{1,0:T(8,128)(2,1)S(1)}, bf16[16,3584]{1,0:T(8,128)(2,1)S(1)}, u32[]{:S(2)}, u32[]{:S(2)}) collective-permute-start(bf16[16,3584]{1,0:T(8,128)(2,1)S(1)} %get-tuple-element.54), channel_id=1, source_target_pairs={{0,16},{1,17},{2,18},{3,19},{4,20},{5,21},{6,22},{7,23},{8,24},{9,... | collective-permute-start | bytes 344072 | tf_op jit(solution)/shard_map/ppermute | solution.py:247
  41.7 8.6 %collective-permute-start.8 = (bf16[16,3584]{1,0:T(8,128)(2,1)S(1)}, bf16[16,3584]{1,0:T(8,128)(2,1)S(1)}, u32[]{:S(2)}, u32[]{:S(2)}) collective-permute-start(bf16[16,3584]{1,0:T(8,128)(2,1)S(1)} %get-tuple-element.41), channel_id=1, source_target_pairs={{0,2},{1,3},{2,0},{3,1},{4,6},{5,7},{6,4},{7,5},{8,10},{9,11},{10,... | collective-permute-start | bytes 344072 | tf_op jit(solution)/shard_map/ppermute | solution.py:247
  47.3 15.0 %collective-permute-start.14 = (bf16[16,3584]{1,0:T(8,128)(2,1)S(1)}, bf16[16,3584]{1,0:T(8,128)(2,1)S(1)}, u32[]{:S(2)}, u32[]{:S(2)}) collective-permute-start(bf16[16,3584]{1,0:T(8,128)(2,1)S(1)} %get-tuple-element.58), channel_id=1, source_target_pairs={{0,28},{1,29},{2,30},{3,31},{4,24},{5,25},{6,26},{7,27},{8,20},{9,... | collective-permute-start | bytes 344072 | tf_op jit(solution)/shard_map/ppermute | solution.py:247
  47.5 14.9 %collective-permute-start.15 = (bf16[16,3584]{1,0:T(8,128)(2,1)S(1)}, bf16[16,3584]{1,0:T(8,128)(2,1)S(1)}, u32[]{:S(2)}, u32[]{:S(2)}) collective-permute-start(bf16[16,3584]{1,0:T(8,128)(2,1)S(1)} %get-tuple-element.57), channel_id=1, source_target_pairs={{0,30},{1,31},{2,28},{3,29},{4,26},{5,27},{6,24},{7,25},{8,22},{9,... | collective-permute-start | bytes 344072 | tf_op jit(solution)/shard_map/ppermute | solution.py:247
  51.7 6.9 %copy-start.2 = (bf16[96,128]{1,0:T(8,128)(2,1)S(1)}, bf16[96,128]{1,0:T(8,128)(2,1)}, u32[]{:S(2)}) copy-start(bf16[96,128]{1,0:T(8,128)(2,1)} %get-tuple-element.28) | copy-start | bytes 73732
  54.5 7.9 %collective-permute-start.16 = (bf16[16,3584]{1,0:T(8,128)(2,1)S(1)}, bf16[16,3584]{1,0:T(8,128)(2,1)S(1)}, u32[]{:S(2)}, u32[]{:S(2)}) collective-permute-start(bf16[16,3584]{1,0:T(8,128)(2,1)S(1)} %get-tuple-element.56), channel_id=1, source_target_pairs={{0,20},{1,21},{2,22},{3,23},{4,28},{5,29},{6,30},{7,31},{8,16},{9,... | collective-permute-start | bytes 344072 | tf_op jit(solution)/shard_map/ppermute | solution.py:247
  57.4 7.8 %collective-permute-start.17 = (bf16[16,3584]{1,0:T(8,128)(2,1)S(1)}, bf16[16,3584]{1,0:T(8,128)(2,1)S(1)}, u32[]{:S(2)}, u32[]{:S(2)}) collective-permute-start(bf16[16,3584]{1,0:T(8,128)(2,1)S(1)} %get-tuple-element.55), channel_id=1, source_target_pairs={{0,22},{1,23},{2,20},{3,21},{4,30},{5,31},{6,28},{7,29},{8,18},{9,... | collective-permute-start | bytes 344072 | tf_op jit(solution)/shard_map/ppermute | solution.py:247
  58.5 3.8 %collective-permute-start = (bf16[96,128]{1,0:T(8,128)(2,1)S(1)}, bf16[96,128]{1,0:T(8,128)(2,1)S(1)}, u32[]{:S(2)}, u32[]{:S(2)}) collective-permute-start(bf16[96,128]{1,0:T(8,128)(2,1)S(1)} %copy-done.2), channel_id=1, source_target_pairs={{0,16},{1,17},{2,18},{3,19},{4,20},{5,21},{6,22},{7,23},{8,24},{9,... | collective-permute-start | bytes 73736 | tf_op jit(solution)/shard_map/ppermute | solution.py:247

commit v4 on v0

--- a/solution.py
+++ b/solution.py
@@ -1,6 +1,10 @@
+import functools
+
 import jax
 import jax.numpy as jnp
 from jax import lax
+from jax.experimental import pallas as pl
+from jax.experimental.pallas import tpu as pltpu
 from jax.sharding import PartitionSpec as P
 
 
@@ -9,7 +13,7 @@
     return lax.ppermute(shard, axis, [(i, (i + by) % length) for i in range(length)])
 
 
-def per_device(rows, route_ids, route_weights, w_gate_up, w_down):
+def by_slots(rows, route_ids, route_weights, w_gate_up, w_down):
     devices = lax.axis_size("expert")
     experts = devices // 2
     tokens = rows[0]
@@ -47,8 +51,376 @@
     expert_out = jnp.sum(returned, axis=2).astype(jnp.bfloat16).reshape(slot_total, width)
     pair_out = expert_out[place].astype(jnp.float32) * route_weights[0].reshape(-1)[:, None]
     layer_out = jnp.sum(pair_out.reshape(tok_count, top_count, width), axis=1).astype(jnp.bfloat16)
-    handed = passed_along(layer_out, "section", 1)
-    return handed[None]
+    return passed_along(layer_out, "section", 1)[None]
+
+
+RING = (0, 1, 3, 2)
+LANES = 128
+TOKEN_LANE = 64
+
+
+def on_ring(place):
+    return place ^ (place >> 1)
+
+
+def chip_at(chip, steps, flip):
+    return (on_ring((on_ring(chip >> 1) + steps) & 3) << 1) | ((chip & 1) ^ flip)
+
+
+def iota(shape, axis):
+    return lax.broadcasted_iota(jnp.int32, shape, axis)
+
+
+def ones_where(condition):
+    return jnp.where(condition, 1.0, 0.0).astype(jnp.bfloat16)
+
+
+def across(left, right):
+    return lax.dot_general(left, right, (((0,), (0,)), ((), ())), preferred_element_type=jnp.float32)
+
+
+def local_call(kernel, name, out_shape, in_specs, operands, scratch=(), limit=12, flops=0, moved=0):
+    vmem = pl.BlockSpec(memory_space=pltpu.VMEM)
+    return pl.pallas_call(
+        kernel,
+        out_shape=out_shape,
+        in_specs=[vmem if spec is None else pl.BlockSpec(memory_space=spec) for spec in in_specs],
+        out_specs=jax.tree.map(lambda _: vmem, out_shape),
+        scratch_shapes=list(scratch),
+        compiler_params=pltpu.CompilerParams(vmem_limit_bytes=limit << 20),
+        cost_estimate=pl.CostEstimate(flops=flops, bytes_accessed=moved, transcendentals=0),
+        name=name,
+    )(*operands)
+
+
+def prepare_kernel(ids_in, weights_in, rows_in, block, ids, weights, sems):
+    tok_count, width = rows_in.shape
+    top_count = ids.shape[0]
+    experts = 2 * len(RING)
+    copies = [
+        pltpu.make_async_copy(ids_in, ids, sems.at[0]),
+        pltpu.make_async_copy(weights_in, weights, sems.at[1]),
+        pltpu.make_async_copy(rows_in, block.at[:, pl.ds(0, width)], sems.at[2]),
+    ]
+    for copy in copies:
+        copy.start()
+    square = (tok_count, tok_count)
+    earlier = ones_where(iota(square, 0) < iota(square, 1))
+    expert = iota((experts, tok_count), 0)
+    unit = ones_where(iota((4 * experts, LANES), 0) == iota((4 * experts, LANES), 1))
+    token = ones_where(iota((tok_count, LANES), 0) + TOKEN_LANE == iota((tok_count, LANES), 1))
+    copies[0].wait()
+    copies[1].wait()
+    named = jnp.zeros((experts, tok_count), jnp.float32)
+    scale = jnp.zeros((experts, tok_count), jnp.float32)
+    for k in range(top_count):
+        hit = ids[k : k + 1, :] == expert
+        named = named + jnp.where(hit, 1.0, 0.0)
+        scale = scale + jnp.where(hit, weights[k : k + 1, :], 0.0)
+    rank = jnp.dot(named.astype(jnp.bfloat16), earlier, preferred_element_type=jnp.float32)
+    notes = [jnp.where(named > 0.5, rank + 1.0, 0.0)]
+    for _ in range(3):
+        piece = scale.astype(jnp.bfloat16).astype(jnp.float32)
+        scale = scale - piece
+        notes.append(piece)
+    notes = across(jnp.concatenate(notes, axis=0).astype(jnp.bfloat16), unit)
+    block[:, width:] = notes.astype(jnp.bfloat16) + token
+    copies[2].wait()
+
+
+def prepare(ids, weights, tokens):
+    tok_count, width = tokens.shape
+    return local_call(
+        prepare_kernel,
+        "prepare",
+        jax.ShapeDtypeStruct((tok_count, width + LANES), jnp.bfloat16),
+        [pl.ANY] * 3,
+        (ids, weights, tokens),
+        [
+            pltpu.VMEM(ids.shape, ids.dtype),
+            pltpu.VMEM(weights.shape, weights.dtype),
+            pltpu.SemaphoreType.DMA((3,)),
+        ],
+        limit=60,
+    )
+
+
+def choose_kernel(places, capacity, chip, block, *refs):
+    refs = list(refs)
+    first = refs.pop(0) if refs[-1].shape[0] == 2 * capacity else None
+    tok_count = block.shape[0]
+    notes = block[:, -LANES:].astype(jnp.float32)
+    lane = iota(notes.shape, 1)
+    slot = iota((tok_count, len(places) * capacity), 1)
+    code = jnp.zeros(slot.shape, jnp.float32)
+    order = jnp.zeros(slot.shape, jnp.int32)
+    for at, (steps, flip) in enumerate(places):
+        wanted = chip_at(chip[0], steps, flip)
+        column = jnp.sum(jnp.where(lane == wanted, notes, 0.0), axis=1, keepdims=True)
+        code = jnp.where(slot >= at * capacity, column, code)
+        order = jnp.where(slot >= at * capacity, slot + 1 - at * capacity, order)
+    rows = across(ones_where(code == order.astype(jnp.float32)), block[...]).astype(jnp.bfloat16)
+    for at in range(len(places)):
+        piece = rows[at * capacity : (at + 1) * capacity]
+        if first is not None and at == len(places) - 1:
+            refs[at][:capacity] = first[...]
+            refs[at][capacity:] = piece
+        else:
+            refs[at][...] = piece
+
+
+def choose(chip, block, capacity, places, first=None):
+    out_shape = [jax.ShapeDtypeStruct((capacity, block.shape[1]), jnp.bfloat16) for _ in places]
+    operands = (chip, block)
+    if first is not None:
+        out_shape[-1] = jax.ShapeDtypeStruct((2 * capacity, block.shape[1]), jnp.bfloat16)
+        operands = operands + (first,)
+    return local_call(
+        functools.partial(choose_kernel, places, capacity),
+        "choose",
+        out_shape,
+        [pltpu.SMEM] + [None] * (len(operands) - 1),
+        operands,
+    )
+
+
+def load_kernel(source, target, sem):
+    copy = pltpu.make_async_copy(source, target, sem)
+    copy.start()
+    copy.wait()
+
+
+def loaded(weights):
+    return local_call(
+        load_kernel,
+        "loaded",
+        pltpu.VMEM(weights.shape, weights.dtype),
+        [pl.ANY],
+        (weights,),
+        [pltpu.SemaphoreType.DMA],
+        limit=9,
+        moved=2 * weights.size * weights.dtype.itemsize,
+    )
+
+
+def gated(both):
+    hidden = both.shape[1] // 2
+    gate = both[:, :hidden]
+    return (gate / (1.0 + jnp.exp(-gate)) * both[:, hidden:]).astype(jnp.bfloat16)
+
+
+def near_kernel(*refs):
+    pieces, (first, second, slots, total) = refs[:-4], refs[-4:]
+    start = 0
+    for piece in pieces:
+        slots[start : start + piece.shape[0]] = piece[...]
+        start += piece.shape[0]
+    width = total.shape[1]
+    both = jnp.dot(slots[:, :width], first[...], preferred_element_type=jnp.float32)
+    total[...] = jnp.dot(gated(both), second[...], preferred_element_type=jnp.float32)
+
+
+def near_pass(pieces, weights):
+    count = sum(piece.shape[0] for piece in pieces)
+    full = pieces[0].shape[1]
+    width = full - LANES
+    return local_call(
+        near_kernel,
+        "near_pass",
+        [
+            jax.ShapeDtypeStruct((count, full), jnp.bfloat16),
+            jax.ShapeDtypeStruct((count, width), jnp.float32),
+        ],
+        [None] * (len(pieces) + 2),
+        (*pieces, *weights),
+        moved=2 * sum(w.size for w in weights),
+    )
+
+
+def write_pieces(chip, slots, total, outs):
+    width = total.shape[1]
+    experts = 2 * len(RING)
+    notes = slots[:, width:].astype(jnp.float32)
+    lane = iota(notes.shape, 1)
+    mine = (lane >= experts) & (lane < 4 * experts) & ((lane & (experts - 1)) == chip[0])
+    scale = jnp.sum(jnp.where(mine, notes, 0.0), axis=1, keepdims=True)
+    start = 0
+    for out in outs:
+        stop = start + out.shape[0]
+        out[:, :width] = (total[start:stop] * scale[start:stop]).astype(jnp.bfloat16)
+        out[:, width:] = slots[start:stop, width:]
+        start = stop
+
+
+def far_kernel(parts, chip, slots, total, first_in, second_in, *refs):
+    outs, (first, second, both, sems) = refs[:-4], refs[-4:]
+    width = total.shape[1]
+    step = width // parts
+    hidden = second.shape[0]
+    copies = []
+    for at in range(parts):
+        place = pl.ds(at * step, step)
+        copies.append(pltpu.make_async_copy(first_in.at[place], first.at[place], sems.at[at]))
+    for at in range(2):
+        place = pl.ds(at * (hidden // 2), hidden // 2)
+        copies.append(
+            pltpu.make_async_copy(second_in.at[place], second.at[place], sems.at[parts + at])
+        )
+    for copy in copies:
+        copy.start()
+    for at in range(parts):
+        copies[at].wait()
+        place = slice(at * step, (at + 1) * step)
+        term = jnp.dot(slots[:, place], first[place], preferred_element_type=jnp.float32)
+        both[...] = term if at == 0 else both[...] + term
+    active = gated(both[...])
+    for at in range(2):
+        copies[parts + at].wait()
+        place = slice(at * (hidden // 2), (at + 1) * (hidden // 2))
+        total[...] += jnp.dot(active[:, place], second[place], preferred_element_type=jnp.float32)
+    write_pieces(chip, slots, total, outs)
+
+
+def far_body(parts, chip, slots, total_in, first_in, second_in, *refs):
+    outs, (first, second, both, total, sems) = refs[:-5], refs[-5:]
+    total[...] = total_in[...]
+    far_kernel(parts, chip, slots, total, first_in, second_in, *outs, first, second, both, sems)
+
+
+def far_pass(chip, slots, total, weights, capacity):
+    count, full = slots.shape
+    hidden = weights[1].shape[0]
+    parts = 7
+    piece = jax.ShapeDtypeStruct((capacity, full), jnp.bfloat16)
+    outs = local_call(
+        functools.partial(far_body, parts),
+        "far_pass",
+        [piece] * (count // capacity) + [pltpu.VMEM(w.shape, w.dtype) for w in weights],
+        [pltpu.SMEM, None, None, pl.ANY, pl.ANY],
+        (chip, slots, total, *weights),
+        [
+            pltpu.VMEM((count, 2 * hidden), jnp.float32),
+            pltpu.VMEM(total.shape, jnp.float32),
+            pltpu.SemaphoreType.DMA((parts + 2,)),
+        ],
+        limit=20,
+        moved=2 * sum(w.size for w in weights),
+    )
+    return outs[:-2], outs[-2:]
+
+
+def last_kernel(chip, *refs):
+    pieces, weights, outs, (slots, total) = refs[:2], refs[2:6], refs[6:-2], refs[-2:]
+    start = 0
+    for piece in pieces:
+        slots[start : start + piece.shape[0]] = piece[...]
+        start += piece.shape[0]
+    width = total.shape[1]
+    for half in range(2):
+        first, second = weights[2 * half : 2 * half + 2]
+        both = jnp.dot(slots[:, :width], first[...], preferred_element_type=jnp.float32)
+        term = jnp.dot(gated(both), second[...], preferred_element_type=jnp.float32)
+        total[...] = term if half == 0 else total[...] + term
+    write_pieces(chip, slots, total, outs)
+
+
+def last_pass(chip, pieces, near, far):
+    capacity, full = pieces[0].shape
+    count = capacity * len(pieces)
+    return local_call(
+        last_kernel,
+        "last_pass",
+        [jax.ShapeDtypeStruct((capacity, full), jnp.bfloat16)] * len(pieces),
+        [pltpu.SMEM] + [None] * (len(pieces) + 4),
+        (chip, *pieces, *near, *far),
+        [pltpu.VMEM((count, full), jnp.bfloat16), pltpu.VMEM((count, full - LANES), jnp.float32)],
+        moved=2 * sum(w.size for w in (*near, *far)),
+    )
+
+
+def combine_kernel(*refs):
+    blocks, out, slots = refs[:-2], refs[-2], refs[-1]
+    tok_count, width = out.shape
+    start = 0
+    for block in blocks:
+        slots[start : start + block.shape[0]] = block[...]
+        start += block.shape[0]
+    token = slots[:, width:]
+    part = width // 7
+    for at in range(7):
+        place = slice(at * part, (at + 1) * part)
+        mixed = across(token, slots[:, place])
+        out[:, place] = mixed[TOKEN_LANE : TOKEN_LANE + tok_count].astype(out.dtype)
+
+
+def combine(blocks, tok_count):
+    capacity, full = blocks[0].shape
+    return local_call(
+        combine_kernel,
+        "combine",
+        jax.ShapeDtypeStruct((tok_count, full - LANES), jnp.bfloat16),
+        [None] * len(blocks),
+        tuple(blocks),
+        [pltpu.VMEM((capacity * len(blocks), full), jnp.bfloat16)],
+    )
+
+
+def sent(shard, sections, section_step, ring_step, flip):
+    planes = len(RING)
+    pairs = []
+    for s in range(sections):
+        for z in range(planes):
+            for y in range(2):
+                for core in range(2):
+                    plane = RING[(RING.index(z) + ring_step) % planes]
+                    target = (((s + section_step) % sections) * planes + plane) * 2 + (y ^ flip)
+                    pairs.append((((s * planes + z) * 2 + y) * 2 + core, target * 2 + core))
+    return lax.ppermute(shard, ("section", "expert"), pairs)
+
+
+def after(value, other):
+    return lax.optimization_barrier((value, other))[0]
+
+
+def by_ring(rows, route_ids, route_weights, w_gate_up, w_down):
+    sections = lax.axis_size("section")
+    devices = lax.axis_size("expert")
+    experts = devices // 2
+    tokens = rows[0]
+    tok_count = tokens.shape[0]
+    top_count = route_ids.shape[2]
+    capacity = max(2, 2 * tok_count * top_count // experts)
+    chip = (lax.axis_index("expert") // 2).reshape(1).astype(jnp.int32)
+    swap = [(i, i ^ 1) for i in range(devices)]
+    w_in, w_out = w_gate_up[0], w_down[0]
+    far = (lax.ppermute(w_in, "expert", swap), lax.ppermute(w_out, "expert", swap))
+    block = prepare(route_ids[0].T, route_weights[0].T, tokens)
+    block1 = sent(block, sections, 0, 1, 0)
+    own0, other0, back0, back1 = choose(chip, block, capacity, ((0, 0), (0, 1), (3, 0), (3, 1)))
+    own3 = sent(back0, sections, 0, 3, 0)
+    other3 = sent(back1, sections, 0, 3, 1)
+    near = (loaded(after(w_in, back1)), loaded(after(w_out, back1)))
+    block2 = sent(after(block1, near), sections, 0, 1, 0)
+    own1, other = choose(chip, block1, capacity, ((0, 0), (0, 1)), other0)
+    other01 = sent(after(other, (own3, other3)), sections, 0, 0, 1)
+    own2, other = choose(chip, block2, capacity, ((0, 0), (0, 1)))
+    other2 = sent(other, sections, 0, 0, 1)
+    slots, total = near_pass((own1, own3, other3, own0, other01), near)
+    pieces, far = far_pass(chip, slots, total, far, capacity)
+    places = ((1, 0), (3, 0), (3, 1), (0, 0), (0, 1), (1, 1))
+    back = [
+        sent(piece, sections, 1, -steps, flip) for piece, (steps, flip) in zip(pieces, places)
+    ]
+    pieces = last_pass(chip, (own2, other2), near, far)
+    back += [sent(piece, sections, 1, -2, flip) for flip, piece in enumerate(pieces)]
+    return combine(back, tok_count)[None]
+
+
+def per_device(rows, route_ids, route_weights, w_gate_up, w_down):
+    experts = lax.axis_size("expert") // 2
+    fits = experts == 2 * len(RING) and rows.shape[1] <= LANES - TOKEN_LANE
+    plan = by_ring if fits else by_slots
+    return plan(rows, route_ids, route_weights, w_gate_up, w_down)
 
 
 def solution(mesh):

time: 120 us -> 61.5 us (0.51)
  the two profiles are of different devices: /device:TPU:12 before, /device:TPU:0 now
where the time goes in v4:
time: 61.5 us; the launch traced here: 61.3 us
  starting transfers between devices  32.6 us (53%)
  Pallas kernels  15.4 us (25%)
  waiting for transfers between devices  10.2 us (17%)
  local copies, waits for them, and re-layouts  3.02 us (5%)
    ppermute x14, starting transfers between devices, sent(): return lax.ppermute(shard, ('section', 'expert'), pairs)  32.1 us
    pallas_call x10, Pallas kernels, local_call(): pl.pallas_call(kernel, out_shape=out_shape, in_specs=[vmem if spec is Non...  15.4 us
    ppermute x14, waiting for transfers between devices, sent(): return lax.ppermute(shard, ('section', 'expert'), pairs)  10.2 us
    unnamed x6, local copies, waits for them, and re-layouts  3.02 us
  transfers between devices with their start and end apart: 16, of which 5 were waited for; matrix products, arithmetic and copies ran while one was open for 0% of the time, Pallas kernels for 23%

profile of v4, /device:TPU:0, one launch (start us, length us, event | category | flops | bytes accessed | tf_op | source)
XLA Modules:
  0.0 61.3 jit_solution(14992137268119375113)
XLA Ops:
  0.5 1.7 %prepare.1.block = bf16[32,3712]{1,0:T(8,128)(2,1)} custom-call(s32[2,32]{1,0:T(2,128)} %bitcast.16, f32[2,32]{1,0:T(2,128)} %bitcast.17, bf16[32,3584]{1,0:T(8,128)(2,1)} %bitcast.15), custom_call_target="tpu_custom_call" | custom-call | tf_op jit(solution)/shard_map/prepare/pallas_call | solution.py:84
  2.2 3.1 %collective-permute-start = (bf16[32,3712]{1,0:T(8,128)(2,1)}, bf16[32,3712]{1,0:T(8,128)(2,1)S(1)}, u32[]{:S(2)}, u32[]{:S(2)}) collective-permute-start(bf16[32,3712]{1,0:T(8,128)(2,1)} %prepare.1.block), channel_id=1, source_target_pairs={{0,4},{1,5},{2,6},{3,7},{4,12},{5,13},{6,14},{7,15},{8,0},{9,1},{1... | collective-permute-start | bytes 712712 | tf_op jit(solution)/shard_map/ppermute | solution.py:378
  5.3 1.0 %copy-done.2 = bf16[32,3712]{1,0:T(8,128)(2,1)S(1)} copy-done((bf16[32,3712]{1,0:T(8,128)(2,1)S(1)}, bf16[32,3712]{1,0:T(8,128)(2,1)}, u32[]{:S(2)}) %copy-start.2) | copy-done | bytes 237592
  6.7 1.1 %collective-permute-start.1 = (bf16[16,3712]{1,0:T(8,128)(2,1)S(1)}, bf16[16,3712]{1,0:T(8,128)(2,1)S(1)}, u32[]{:S(2)}, u32[]{:S(2)}) collective-permute-start(bf16[16,3712]{1,0:T(8,128)(2,1)S(1)} %get-tuple-element.31), channel_id=1, source_target_pairs={{0,8},{1,9},{2,10},{3,11},{4,0},{5,1},{6,2},{7,3},{8,12},{9,13},{1... | collective-permute-start | bytes 356360 | tf_op jit(solution)/shard_map/ppermute | solution.py:378
  7.8 3.0 %collective-permute-start.2 = (bf16[16,3712]{1,0:T(8,128)(2,1)S(1)}, bf16[16,3712]{1,0:T(8,128)(2,1)S(1)}, u32[]{:S(2)}, u32[]{:S(2)}) collective-permute-start(bf16[16,3712]{1,0:T(8,128)(2,1)S(1)} %get-tuple-element.32), channel_id=1, source_target_pairs={{0,10},{1,11},{2,8},{3,9},{4,2},{5,3},{6,0},{7,1},{8,14},{9,15},{1... | collective-permute-start | bytes 356360 | tf_op jit(solution)/shard_map/ppermute | solution.py:378
  10.8 2.0 %copy-done.1 = bf16[1,512,3584]{2,1,0:T(8,128)(2,1)S(1)} copy-done((bf16[1,512,3584]{2,1,0:T(8,128)(2,1)S(1)}, bf16[1,512,3584]{2,1,0:T(8,128)(2,1)}, u32[]{:S(2)}) %copy-start.1) | copy-done | bytes 3670040
  13.6 5.0 %collective-permute-start.12 = (bf16[32,3712]{1,0:T(8,128)(2,1)S(1)}, bf16[32,3712]{1,0:T(8,128)(2,1)S(1)}, u32[]{:S(2)}, u32[]{:S(2)}) collective-permute-start(bf16[32,3712]{1,0:T(8,128)(2,1)S(1)} %collective-permute-done.block), channel_id=1, source_target_pairs={{0,4},{1,5},{2,6},{3,7},{4,12},{5,13},{6,14},{7,15},{8,0},{9,1},{1... | collective-permute-start | bytes 712712 | tf_op jit(solution)/shard_map/ppermute | solution.py:378
  18.9 1.6 %collective-permute-start.3 = (bf16[32,3712]{1,0:T(8,128)(2,1)S(1)}, bf16[32,3712]{1,0:T(8,128)(2,1)S(1)}, u32[]{:S(2)}, u32[]{:S(2)}) collective-permute-start(bf16[32,3712]{1,0:T(8,128)(2,1)S(1)} %get-tuple-element.35), channel_id=1, source_target_pairs={{0,2},{1,3},{2,0},{3,1},{4,6},{5,7},{6,4},{7,5},{8,10},{9,11},{10,... | collective-permute-start | bytes 712712 | tf_op jit(solution)/shard_map/ppermute | solution.py:378
  20.5 3.3 %collective-permute-done.12.block = bf16[32,3712]{1,0:T(8,128)(2,1)S(1)} collective-permute-done((bf16[32,3712]{1,0:T(8,128)(2,1)S(1)}, bf16[32,3712]{1,0:T(8,128)(2,1)S(1)}, u32[]{:S(2)}, u32[]{:S(2)}) %collective-permute-start.12) | collective-permute-done | bytes 237600 | tf_op jit(solution)/shard_map/ppermute | solution.py:378
  24.2 1.6 %collective-permute-start.13 = (bf16[16,3712]{1,0:T(8,128)(2,1)S(1)}, bf16[16,3712]{1,0:T(8,128)(2,1)S(1)}, u32[]{:S(2)}, u32[]{:S(2)}) collective-permute-start(bf16[16,3712]{1,0:T(8,128)(2,1)S(1)} %get-tuple-element.48), channel_id=1, source_target_pairs={{0,2},{1,3},{2,0},{3,1},{4,6},{5,7},{6,4},{7,5},{8,10},{9,11},{10,... | collective-permute-start | bytes 356360 | tf_op jit(solution)/shard_map/ppermute | solution.py:378
  26.4 2.0 %near_pass.1 = (bf16[96,3712]{1,0:T(8,128)(2,1)S(1)}, f32[96,3584]{1,0:T(8,128)S(1)}) custom-call(bf16[16,3712]{1,0:T(8,128)(2,1)S(1)} %get-tuple-element.30.refs_0_, bf16[16,3712]{1,0:T(8,128)(2,1)S(1)} %collective-permute-done.1.refs_1_, bf16[16,3712]{1,0:T(8,128)(2,1)S(1)} %collective-permute-done.2.refs_2_, ...), custom_call_target="tpu_custom_call" | custom-call | bytes 11010048 | tf_op jit(solution)/shard_map/near_pass/pallas_call | solution.py:84
  28.4 4.7 %far_pass.1 = (bf16[16,3712]{1,0:T(8,128)(2,1)S(1)}, bf16[16,3712]{1,0:T(8,128)(2,1)S(1)}, bf16[16,3712]{1,0:T(8,128)(2,1)S(1)}, bf16[16,3712]{1,0:T(8,128)(2,1)...) custom-call(s32[1]{0:T(128)} %bitcast.chip, ...), custom_call_target="tpu_custom_call" | custom-call | bytes 11010048 | tf_op jit(solution)/shard_map/far_pass/pallas_call | solution.py:84
  33.1 2.6 %collective-permute-start.6 = (bf16[16,3712]{1,0:T(8,128)(2,1)S(1)}, bf16[16,3712]{1,0:T(8,128)(2,1)S(1)}, u32[]{:S(2)}, u32[]{:S(2)}) collective-permute-start(bf16[16,3712]{1,0:T(8,128)(2,1)S(1)} %get-tuple-element.40), channel_id=1, source_target_pairs={{0,24},{1,25},{2,26},{3,27},{4,16},{5,17},{6,18},{7,19},{8,28},{9,... | collective-permute-start | bytes 356360 | tf_op jit(solution)/shard_map/ppermute | solution.py:378
  35.8 1.7 %collective-permute-start.7 = (bf16[16,3712]{1,0:T(8,128)(2,1)S(1)}, bf16[16,3712]{1,0:T(8,128)(2,1)S(1)}, u32[]{:S(2)}, u32[]{:S(2)}) collective-permute-start(bf16[16,3712]{1,0:T(8,128)(2,1)S(1)} %get-tuple-element.41), channel_id=1, source_target_pairs={{0,20},{1,21},{2,22},{3,23},{4,28},{5,29},{6,30},{7,31},{8,16},{9,... | collective-permute-start | bytes 356360 | tf_op jit(solution)/shard_map/ppermute | solution.py:378
  37.4 4.7 %collective-permute-start.8 = (bf16[16,3712]{1,0:T(8,128)(2,1)S(1)}, bf16[16,3712]{1,0:T(8,128)(2,1)S(1)}, u32[]{:S(2)}, u32[]{:S(2)}) collective-permute-start(bf16[16,3712]{1,0:T(8,128)(2,1)S(1)} %get-tuple-element.42), channel_id=1, source_target_pairs={{0,22},{1,23},{2,20},{3,21},{4,30},{5,31},{6,28},{7,29},{8,18},{9,... | collective-permute-start | bytes 356360 | tf_op jit(solution)/shard_map/ppermute | solution.py:378
  42.7 1.4 %collective-permute-start.10 = (bf16[16,3712]{1,0:T(8,128)(2,1)S(1)}, bf16[16,3712]{1,0:T(8,128)(2,1)S(1)}, u32[]{:S(2)}, u32[]{:S(2)}) collective-permute-start(bf16[16,3712]{1,0:T(8,128)(2,1)S(1)} %get-tuple-element.44), channel_id=1, source_target_pairs={{0,18},{1,19},{2,16},{3,17},{4,22},{5,23},{6,20},{7,21},{8,26},{9,... | collective-permute-start | bytes 356360 | tf_op jit(solution)/shard_map/ppermute | solution.py:378
  44.1 4.0 %last_pass.1 = (bf16[16,3712]{1,0:T(8,128)(2,1)S(1)}, bf16[16,3712]{1,0:T(8,128)(2,1)S(1)}) custom-call(s32[1]{0:T(128)} %bitcast.chip, bf16[16,3712]{1,0:T(8,128)(2,1)S(1)} %get-tuple-element.47.refs_0_, bf16[16,3712]{1,0:T(8,128)(2,1)S(1)} %collective-permute-done.13.refs_1_, bf16[3584,1024]{1,0:T(8,128)(2,1)S(1)} %loaded.2.refs_5_.refs_2_, ...), custom_call_target="tpu_custom_call" | custom-call | bytes 22020096 | tf_op jit(solution)/shard_map/last_pass/pallas_call | solution.py:84
  48.2 1.1 %collective-permute-start.11 = (bf16[16,3712]{1,0:T(8,128)(2,1)S(1)}, bf16[16,3712]{1,0:T(8,128)(2,1)S(1)}, u32[]{:S(2)}, u32[]{:S(2)}) collective-permute-start(bf16[16,3712]{1,0:T(8,128)(2,1)S(1)} %get-tuple-element.45), channel_id=1, source_target_pairs={{0,26},{1,27},{2,24},{3,25},{4,18},{5,19},{6,16},{7,17},{8,30},{9,... | collective-permute-start | bytes 356360 | tf_op jit(solution)/shard_map/ppermute | solution.py:378
  49.2 2.4 %collective-permute-start.14 = (bf16[16,3712]{1,0:T(8,128)(2,1)S(1)}, bf16[16,3712]{1,0:T(8,128)(2,1)S(1)}, u32[]{:S(2)}, u32[]{:S(2)}) collective-permute-start(bf16[16,3712]{1,0:T(8,128)(2,1)S(1)} %get-tuple-element.51), channel_id=1, source_target_pairs={{0,28},{1,29},{2,30},{3,31},{4,24},{5,25},{6,26},{7,27},{8,20},{9,... | collective-permute-start | bytes 356360 | tf_op jit(solution)/shard_map/ppermute | solution.py:378
  51.6 2.3 %collective-permute-start.15 = (bf16[16,3712]{1,0:T(8,128)(2,1)S(1)}, bf16[16,3712]{1,0:T(8,128)(2,1)S(1)}, u32[]{:S(2)}, u32[]{:S(2)}) collective-permute-start(bf16[16,3712]{1,0:T(8,128)(2,1)S(1)} %get-tuple-element.52), channel_id=1, source_target_pairs={{0,30},{1,31},{2,28},{3,29},{4,26},{5,27},{6,24},{7,25},{8,22},{9,... | collective-permute-start | bytes 356360 | tf_op jit(solution)/shard_map/ppermute | solution.py:378
  54.0 2.1 %collective-permute-done.11.refs_5_ = bf16[16,3712]{1,0:T(8,128)(2,1)S(1)} collective-permute-done((bf16[16,3712]{1,0:T(8,128)(2,1)S(1)}, bf16[16,3712]{1,0:T(8,128)(2,1)S(1)}, u32[]{:S(2)}, u32[]{:S(2)}) %collective-permute-start.11) | collective-permute-done | bytes 118816 | tf_op jit(solution)/shard_map/ppermute | solution.py:378
  56.1 1.1 %collective-permute-done.14.refs_6_ = bf16[16,3712]{1,0:T(8,128)(2,1)S(1)} collective-permute-done((bf16[16,3712]{1,0:T(8,128)(2,1)S(1)}, bf16[16,3712]{1,0:T(8,128)(2,1)S(1)}, u32[]{:S(2)}, u32[]{:S(2)}) %collective-permute-start.14) | collective-permute-done | bytes 118816 | tf_op jit(solution)/shard_map/ppermute | solution.py:378
  57.2 3.0 %collective-permute-done.15.refs_7_ = bf16[16,3712]{1,0:T(8,128)(2,1)S(1)} collective-permute-done((bf16[16,3712]{1,0:T(8,128)(2,1)S(1)}, bf16[16,3712]{1,0:T(8,128)(2,1)S(1)}, u32[]{:S(2)}, u32[]{:S(2)}) %collective-permute-start.15) | collective-permute-done | bytes 118816 | tf_op jit(solution)/shard_map/ppermute | solution.py:378
  60.2 1.1 %combine.1 = bf16[32,3584]{1,0:T(8,128)(2,1)} custom-call(bf16[16,3712]{1,0:T(8,128)(2,1)S(1)} %collective-permute-done.6.refs_0_, bf16[16,3712]{1,0:T(8,128)(2,1)S(1)} %collective-permute-done.7.refs_1_, bf16[16,3712]{1,0:T(8,128)(2,1)S(1)} %collective-permute-done.8.refs_2_, bf16[16,3712]{1,0:T(8,128)(2,1)S(1)} %collective-permute-done.9.refs_3_, ...), custom_call_target="tpu_custom_call" | custom-call | tf_op jit(solution)/shard_map/combine/pallas_call | solution.py:84
  (24 shorter events, 3.5 us)
Async XLA Ops:
  0.0 28.4 %collective-permute-start.4 = (bf16[3584,1024]{1,0:T(8,128)(2,1)}, bf16[3584,1024]{1,0:T(8,128)(2,1)}, u32[]{:S(2)}, u32[]{:S(2)}) collective-permute-start(bf16[3584,1024]{1,0:T(8,128)(2,1)} %bitcast.11), channel_id=1, source_target_pairs={{0,1},{1,0},{2,3},{3,2},{4,5},{5,4},{6,7},{7,6},{8,9},{9,8},{10,11... | collective-permute-start | bytes 22020104 | tf_op jit(solution)/shard_map/ppermute | solution.py:396
  0.5 27.9 %collective-permute-start.5 = (bf16[512,3584]{1,0:T(8,128)(2,1)}, bf16[512,3584]{1,0:T(8,128)(2,1)}, u32[]{:S(2)}, u32[]{:S(2)}) collective-permute-start(bf16[512,3584]{1,0:T(8,128)(2,1)} %bitcast.13), channel_id=1, source_target_pairs={{0,1},{1,0},{2,3},{3,2},{4,5},{5,4},{6,7},{7,6},{8,9},{9,8},{10,11... | collective-permute-start | bytes 11010056 | tf_op jit(solution)/shard_map/ppermute | solution.py:396
  2.2 11.3 %collective-permute-start = (bf16[32,3712]{1,0:T(8,128)(2,1)}, bf16[32,3712]{1,0:T(8,128)(2,1)S(1)}, u32[]{:S(2)}, u32[]{:S(2)}) collective-permute-start(bf16[32,3712]{1,0:T(8,128)(2,1)} %prepare.1.block), channel_id=1, source_target_pairs={{0,4},{1,5},{2,6},{3,7},{4,12},{5,13},{6,14},{7,15},{8,0},{9,1},{1... | collective-permute-start | bytes 712712 | tf_op jit(solution)/shard_map/ppermute | solution.py:378
  5.3 1.0 %copy-start.2 = (bf16[32,3712]{1,0:T(8,128)(2,1)S(1)}, bf16[32,3712]{1,0:T(8,128)(2,1)}, u32[]{:S(2)}) copy-start(bf16[32,3712]{1,0:T(8,128)(2,1)} %prepare.1.block) | copy-start | bytes 712708
  6.7 12.2 %collective-permute-start.1 = (bf16[16,3712]{1,0:T(8,128)(2,1)S(1)}, bf16[16,3712]{1,0:T(8,128)(2,1)S(1)}, u32[]{:S(2)}, u32[]{:S(2)}) collective-permute-start(bf16[16,3712]{1,0:T(8,128)(2,1)S(1)} %get-tuple-element.31), channel_id=1, source_target_pairs={{0,8},{1,9},{2,10},{3,11},{4,0},{5,1},{6,2},{7,3},{8,12},{9,13},{1... | collective-permute-start | bytes 356360 | tf_op jit(solution)/shard_map/ppermute | solution.py:378
  7.8 5.3 %copy-start = (bf16[1,3584,1024]{2,1,0:T(8,128)(2,1)S(1)}, bf16[1,3584,1024]{2,1,0:T(8,128)(2,1)}, u32[]{:S(2)}) copy-start(bf16[1,3584,1024]{2,1,0:T(8,128)(2,1)} %param.8) | copy-start | bytes 22020100
  7.8 11.2 %collective-permute-start.2 = (bf16[16,3712]{1,0:T(8,128)(2,1)S(1)}, bf16[16,3712]{1,0:T(8,128)(2,1)S(1)}, u32[]{:S(2)}, u32[]{:S(2)}) collective-permute-start(bf16[16,3712]{1,0:T(8,128)(2,1)S(1)} %get-tuple-element.32), channel_id=1, source_target_pairs={{0,10},{1,11},{2,8},{3,9},{4,2},{5,3},{6,0},{7,1},{8,14},{9,15},{1... | collective-permute-start | bytes 356360 | tf_op jit(solution)/shard_map/ppermute | solution.py:378
  10.8 2.0 %copy-start.1 = (bf16[1,512,3584]{2,1,0:T(8,128)(2,1)S(1)}, bf16[1,512,3584]{2,1,0:T(8,128)(2,1)}, u32[]{:S(2)}) copy-start(bf16[1,512,3584]{2,1,0:T(8,128)(2,1)} %param.9) | copy-start | bytes 11010052
  13.6 10.3 %collective-permute-start.12 = (bf16[32,3712]{1,0:T(8,128)(2,1)S(1)}, bf16[32,3712]{1,0:T(8,128)(2,1)S(1)}, u32[]{:S(2)}, u32[]{:S(2)}) collective-permute-start(bf16[32,3712]{1,0:T(8,128)(2,1)S(1)} %collective-permute-done.block), channel_id=1, source_target_pairs={{0,4},{1,5},{2,6},{3,7},{4,12},{5,13},{6,14},{7,15},{8,0},{9,1},{1... | collective-permute-start | bytes 712712 | tf_op jit(solution)/shard_map/ppermute | solution.py:378
  18.9 7.5 %collective-permute-start.3 = (bf16[32,3712]{1,0:T(8,128)(2,1)S(1)}, bf16[32,3712]{1,0:T(8,128)(2,1)S(1)}, u32[]{:S(2)}, u32[]{:S(2)}) collective-permute-start(bf16[32,3712]{1,0:T(8,128)(2,1)S(1)} %get-tuple-element.35), channel_id=1, source_target_pairs={{0,2},{1,3},{2,0},{3,1},{4,6},{5,7},{6,4},{7,5},{8,10},{9,11},{10,... | collective-permute-start | bytes 712712 | tf_op jit(solution)/shard_map/ppermute | solution.py:378
  24.2 18.5 %collective-permute-start.13 = (bf16[16,3712]{1,0:T(8,128)(2,1)S(1)}, bf16[16,3712]{1,0:T(8,128)(2,1)S(1)}, u32[]{:S(2)}, u32[]{:S(2)}) collective-permute-start(bf16[16,3712]{1,0:T(8,128)(2,1)S(1)} %get-tuple-element.48), channel_id=1, source_target_pairs={{0,2},{1,3},{2,0},{3,1},{4,6},{5,7},{6,4},{7,5},{8,10},{9,11},{10,... | collective-permute-start | bytes 356360 | tf_op jit(solution)/shard_map/ppermute | solution.py:378
  33.1 15.0 %collective-permute-start.6 = (bf16[16,3712]{1,0:T(8,128)(2,1)S(1)}, bf16[16,3712]{1,0:T(8,128)(2,1)S(1)}, u32[]{:S(2)}, u32[]{:S(2)}) collective-permute-start(bf16[16,3712]{1,0:T(8,128)(2,1)S(1)} %get-tuple-element.40), channel_id=1, source_target_pairs={{0,24},{1,25},{2,26},{3,27},{4,16},{5,17},{6,18},{7,19},{8,28},{9,... | collective-permute-start | bytes 356360 | tf_op jit(solution)/shard_map/ppermute | solution.py:378
  35.8 13.5 %collective-permute-start.7 = (bf16[16,3712]{1,0:T(8,128)(2,1)S(1)}, bf16[16,3712]{1,0:T(8,128)(2,1)S(1)}, u32[]{:S(2)}, u32[]{:S(2)}) collective-permute-start(bf16[16,3712]{1,0:T(8,128)(2,1)S(1)} %get-tuple-element.41), channel_id=1, source_target_pairs={{0,20},{1,21},{2,22},{3,23},{4,28},{5,29},{6,30},{7,31},{8,16},{9,... | collective-permute-start | bytes 356360 | tf_op jit(solution)/shard_map/ppermute | solution.py:378
  37.4 14.2 %collective-permute-start.8 = (bf16[16,3712]{1,0:T(8,128)(2,1)S(1)}, bf16[16,3712]{1,0:T(8,128)(2,1)S(1)}, u32[]{:S(2)}, u32[]{:S(2)}) collective-permute-start(bf16[16,3712]{1,0:T(8,128)(2,1)S(1)} %get-tuple-element.42), channel_id=1, source_target_pairs={{0,22},{1,23},{2,20},{3,21},{4,30},{5,31},{6,28},{7,29},{8,18},{9,... | collective-permute-start | bytes 356360 | tf_op jit(solution)/shard_map/ppermute | solution.py:378
  42.1 11.8 %collective-permute-start.9 = (bf16[16,3712]{1,0:T(8,128)(2,1)S(1)}, bf16[16,3712]{1,0:T(8,128)(2,1)S(1)}, u32[]{:S(2)}, u32[]{:S(2)}) collective-permute-start(bf16[16,3712]{1,0:T(8,128)(2,1)S(1)} %get-tuple-element.43), channel_id=1, source_target_pairs={{0,16},{1,17},{2,18},{3,19},{4,20},{5,21},{6,22},{7,23},{8,24},{9,... | collective-permute-start | bytes 356360 | tf_op jit(solution)/shard_map/ppermute | solution.py:378
  42.7 11.3 %collective-permute-start.10 = (bf16[16,3712]{1,0:T(8,128)(2,1)S(1)}, bf16[16,3712]{1,0:T(8,128)(2,1)S(1)}, u32[]{:S(2)}, u32[]{:S(2)}) collective-permute-start(bf16[16,3712]{1,0:T(8,128)(2,1)S(1)} %get-tuple-element.44), channel_id=1, source_target_pairs={{0,18},{1,19},{2,16},{3,17},{4,22},{5,23},{6,20},{7,21},{8,26},{9,... | collective-permute-start | bytes 356360 | tf_op jit(solution)/shard_map/ppermute | solution.py:378
  48.2 7.9 %collective-permute-start.11 = (bf16[16,3712]{1,0:T(8,128)(2,1)S(1)}, bf16[16,3712]{1,0:T(8,128)(2,1)S(1)}, u32[]{:S(2)}, u32[]{:S(2)}) collective-permute-start(bf16[16,3712]{1,0:T(8,128)(2,1)S(1)} %get-tuple-element.45), channel_id=1, source_target_pairs={{0,26},{1,27},{2,24},{3,25},{4,18},{5,19},{6,16},{7,17},{8,30},{9,... | collective-permute-start | bytes 356360 | tf_op jit(solution)/shard_map/ppermute | solution.py:378
  49.2 8.0 %collective-permute-start.14 = (bf16[16,3712]{1,0:T(8,128)(2,1)S(1)}, bf16[16,3712]{1,0:T(8,128)(2,1)S(1)}, u32[]{:S(2)}, u32[]{:S(2)}) collective-permute-start(bf16[16,3712]{1,0:T(8,128)(2,1)S(1)} %get-tuple-element.51), channel_id=1, source_target_pairs={{0,28},{1,29},{2,30},{3,31},{4,24},{5,25},{6,26},{7,27},{8,20},{9,... | collective-permute-start | bytes 356360 | tf_op jit(solution)/shard_map/ppermute | solution.py:378
  51.6 8.5 %collective-permute-start.15 = (bf16[16,3712]{1,0:T(8,128)(2,1)S(1)}, bf16[16,3712]{1,0:T(8,128)(2,1)S(1)}, u32[]{:S(2)}, u32[]{:S(2)}) collective-permute-start(bf16[16,3712]{1,0:T(8,128)(2,1)S(1)} %get-tuple-element.52), channel_id=1, source_target_pairs={{0,30},{1,31},{2,28},{3,29},{4,26},{5,27},{6,24},{7,25},{8,22},{9,... | collective-permute-start | bytes 356360 | tf_op jit(solution)/shard_map/ppermute | solution.py:378

commit v5 on v4

--- a/solution.py
+++ b/solution.py
@@ -133,7 +133,7 @@
     return local_call(
         prepare_kernel,
         "prepare",
-        jax.ShapeDtypeStruct((tok_count, width + LANES), jnp.bfloat16),
+        pltpu.VMEM((tok_count, width + LANES), jnp.bfloat16),
         [pl.ANY] * 3,
         (ids, weights, tokens),
         [
@@ -209,34 +209,6 @@
     return (gate / (1.0 + jnp.exp(-gate)) * both[:, hidden:]).astype(jnp.bfloat16)
 
 
-def near_kernel(*refs):
-    pieces, (first, second, slots, total) = refs[:-4], refs[-4:]
-    start = 0
-    for piece in pieces:
-        slots[start : start + piece.shape[0]] = piece[...]
-        start += piece.shape[0]
-    width = total.shape[1]
-    both = jnp.dot(slots[:, :width], first[...], preferred_element_type=jnp.float32)
-    total[...] = jnp.dot(gated(both), second[...], preferred_element_type=jnp.float32)
-
-
-def near_pass(pieces, weights):
-    count = sum(piece.shape[0] for piece in pieces)
-    full = pieces[0].shape[1]
-    width = full - LANES
-    return local_call(
-        near_kernel,
-        "near_pass",
-        [
-            jax.ShapeDtypeStruct((count, full), jnp.bfloat16),
-            jax.ShapeDtypeStruct((count, width), jnp.float32),
-        ],
-        [None] * (len(pieces) + 2),
-        (*pieces, *weights),
-        moved=2 * sum(w.size for w in weights),
-    )
-
-
 def write_pieces(chip, slots, total, outs):
     width = total.shape[1]
     experts = 2 * len(RING)
@@ -252,65 +224,9 @@
         start = stop
 
 
-def far_kernel(parts, chip, slots, total, first_in, second_in, *refs):
-    outs, (first, second, both, sems) = refs[:-4], refs[-4:]
-    width = total.shape[1]
-    step = width // parts
-    hidden = second.shape[0]
-    copies = []
-    for at in range(parts):
-        place = pl.ds(at * step, step)
-        copies.append(pltpu.make_async_copy(first_in.at[place], first.at[place], sems.at[at]))
-    for at in range(2):
-        place = pl.ds(at * (hidden // 2), hidden // 2)
-        copies.append(
-            pltpu.make_async_copy(second_in.at[place], second.at[place], sems.at[parts + at])
-        )
-    for copy in copies:
-        copy.start()
-    for at in range(parts):
-        copies[at].wait()
-        place = slice(at * step, (at + 1) * step)
-        term = jnp.dot(slots[:, place], first[place], preferred_element_type=jnp.float32)
-        both[...] = term if at == 0 else both[...] + term
-    active = gated(both[...])
-    for at in range(2):
-        copies[parts + at].wait()
-        place = slice(at * (hidden // 2), (at + 1) * (hidden // 2))
-        total[...] += jnp.dot(active[:, place], second[place], preferred_element_type=jnp.float32)
-    write_pieces(chip, slots, total, outs)
-
-
-def far_body(parts, chip, slots, total_in, first_in, second_in, *refs):
-    outs, (first, second, both, total, sems) = refs[:-5], refs[-5:]
-    total[...] = total_in[...]
-    far_kernel(parts, chip, slots, total, first_in, second_in, *outs, first, second, both, sems)
-
-
-def far_pass(chip, slots, total, weights, capacity):
-    count, full = slots.shape
-    hidden = weights[1].shape[0]
-    parts = 7
-    piece = jax.ShapeDtypeStruct((capacity, full), jnp.bfloat16)
-    outs = local_call(
-        functools.partial(far_body, parts),
-        "far_pass",
-        [piece] * (count // capacity) + [pltpu.VMEM(w.shape, w.dtype) for w in weights],
-        [pltpu.SMEM, None, None, pl.ANY, pl.ANY],
-        (chip, slots, total, *weights),
-        [
-            pltpu.VMEM((count, 2 * hidden), jnp.float32),
-            pltpu.VMEM(total.shape, jnp.float32),
-            pltpu.SemaphoreType.DMA((parts + 2,)),
-        ],
-        limit=20,
-        moved=2 * sum(w.size for w in weights),
-    )
-    return outs[:-2], outs[-2:]
-
-
-def last_kernel(chip, *refs):
-    pieces, weights, outs, (slots, total) = refs[:2], refs[2:6], refs[6:-2], refs[-2:]
+def expert_kernel(chip, *refs):
+    outs, (slots, total) = refs[-10:-2], refs[-2:]
+    pieces, weights = refs[:-14], refs[-14:-10]
     start = 0
     for piece in pieces:
         slots[start : start + piece.shape[0]] = piece[...]
@@ -324,13 +240,13 @@
     write_pieces(chip, slots, total, outs)
 
 
-def last_pass(chip, pieces, near, far):
-    capacity, full = pieces[0].shape
-    count = capacity * len(pieces)
-    return local_call(
-        last_kernel,
-        "last_pass",
-        [jax.ShapeDtypeStruct((capacity, full), jnp.bfloat16)] * len(pieces),
+def expert_pass(chip, pieces, near, far, capacity):
+    full = pieces[0].shape[1]
+    count = capacity * 2 * len(RING)
+    return local_call(
+        expert_kernel,
+        "expert_pass",
+        [jax.ShapeDtypeStruct((capacity, full), jnp.bfloat16)] * (2 * len(RING)),
         [pltpu.SMEM] + [None] * (len(pieces) + 4),
         (chip, *pieces, *near, *far),
         [pltpu.VMEM((count, full), jnp.bfloat16), pltpu.VMEM((count, full - LANES), jnp.float32)],
@@ -393,26 +309,27 @@
     chip = (lax.axis_index("expert") // 2).reshape(1).astype(jnp.int32)
     swap = [(i, i ^ 1) for i in range(devices)]
     w_in, w_out = w_gate_up[0], w_down[0]
-    far = (lax.ppermute(w_in, "expert", swap), lax.ppermute(w_out, "expert", swap))
+    far_out = lax.ppermute(w_out, "expert", swap)
+    far_in = lax.ppermute(w_in, "expert", swap)
     block = prepare(route_ids[0].T, route_weights[0].T, tokens)
     block1 = sent(block, sections, 0, 1, 0)
     own0, other0, back0, back1 = choose(chip, block, capacity, ((0, 0), (0, 1), (3, 0), (3, 1)))
     own3 = sent(back0, sections, 0, 3, 0)
     other3 = sent(back1, sections, 0, 3, 1)
     near = (loaded(after(w_in, back1)), loaded(after(w_out, back1)))
-    block2 = sent(after(block1, near), sections, 0, 1, 0)
-    own1, other = choose(chip, block1, capacity, ((0, 0), (0, 1)), other0)
-    other01 = sent(after(other, (own3, other3)), sections, 0, 0, 1)
-    own2, other = choose(chip, block2, capacity, ((0, 0), (0, 1)))
-    other2 = sent(other, sections, 0, 0, 1)
-    slots, total = near_pass((own1, own3, other3, own0, other01), near)
-    pieces, far = far_pass(chip, slots, total, far, capacity)
-    places = ((1, 0), (3, 0), (3, 1), (0, 0), (0, 1), (1, 1))
+    far_out = loaded(after(far_out, near))
+    block1 = after(block1, far_out)
+    own1, on0, on1, other = choose(chip, block1, capacity, ((0, 0), (1, 0), (1, 1), (0, 1)), other0)
+    own2 = sent(on0, sections, 0, 1, 0)
+    other2 = sent(on1, sections, 0, 1, 1)
+    other01 = sent(other, sections, 0, 0, 1)
+    far = (loaded(after(far_in, (own3, other3, other))), far_out)
+    places = ((2, 0), (2, 1), (1, 0), (3, 0), (3, 1), (0, 0), (0, 1), (1, 1))
+    pieces = (own2, other2, own1, own3, other3, own0, other01)
+    pieces = expert_pass(chip, pieces, near, far, capacity)
     back = [
         sent(piece, sections, 1, -steps, flip) for piece, (steps, flip) in zip(pieces, places)
     ]
-    pieces = last_pass(chip, (own2, other2), near, far)
-    back += [sent(piece, sections, 1, -2, flip) for flip, piece in enumerate(pieces)]
     return combine(back, tok_count)[None]
 
 

time: 61.5 us -> 67.3 us (1.094); the launches traced: 61.3 us -> 66.2 us
  waiting for transfers between devices: 10.2 us -> 17.1 us
  Pallas kernels: 15.4 us -> 12.2 us
  starting transfers between devices: 32.6 us -> 34.2 us
    ppermute x2, waiting for transfers between devices: 0.01 us -> 7.81 us  [the longest x1 7.81 us: by_ring(): far_out = lax.ppermute(w_out, 'expert', swap)]
    pallas_call x10 -> x9, Pallas kernels: 15.4 us -> 12.2 us  [local_call(): pl.pallas_call(kernel, out_shape=out_shape, in_specs=[vmem if spec is Non...]
    ppermute x14, starting transfers between devices: 32.1 us -> 33.7 us  [sent(): return lax.ppermute(shard, ('section', 'expert'), pairs)]
    ppermute x14, waiting for transfers between devices: 10.2 us -> 9.25 us  [sent(): return lax.ppermute(shard, ('section', 'expert'), pairs)]
    unnamed x6 -> x4, local copies, waits for them, and re-layouts: 3.02 us -> 2.61 us
  transfers between devices with their start and end apart: 16 -> 16, of which waited for: 5 -> 6; matrix products, arithmetic and copies ran while one was open for 0% -> 0% of each run, Pallas kernels for 23% -> 12%
where the time goes in v5:
time: 67.3 us; the launch traced here: 66.2 us
  starting transfers between devices  34.2 us (51%)
  waiting for transfers between devices  17.1 us (25%)
  Pallas kernels  12.2 us (18%)
  local copies, waits for them, and re-layouts  2.61 us (4%)
    ppermute x14, starting transfers between devices, sent(): return lax.ppermute(shard, ('section', 'expert'), pairs)  33.7 us
    pallas_call x9, Pallas kernels, local_call(): pl.pallas_call(kernel, out_shape=out_shape, in_specs=[vmem if spec is Non...  12.2 us
    ppermute x14, waiting for transfers between devices, sent(): return lax.ppermute(shard, ('section', 'expert'), pairs)  9.25 us
    ppermute x1, waiting for transfers between devices, by_ring(): far_out = lax.ppermute(w_out, 'expert', swap)  7.81 us
    unnamed x4, local copies, waits for them, and re-layouts  2.61 us
  transfers between devices with their start and end apart: 16, of which 6 were waited for; matrix products, arithmetic and copies ran while one was open for 0% of the time, Pallas kernels for 12%

profile of v5, /device:TPU:0, one launch (start us, length us, event | category | flops | bytes accessed | tf_op | source)
XLA Modules:
  0.0 66.2 jit_solution(765700445834699945)
XLA Ops:
  0.5 1.0 %prepare.1.block = bf16[32,3712]{1,0:T(8,128)(2,1)S(1)} custom-call(s32[2,32]{1,0:T(2,128)} %bitcast.16, f32[2,32]{1,0:T(2,128)} %bitcast.17, bf16[32,3584]{1,0:T(8,128)(2,1)} %bitcast.15), custom_call_target="tpu_custom_call" | custom-call | tf_op jit(solution)/shard_map/prepare/pallas_call | solution.py:84
  1.5 3.1 %collective-permute-start = (bf16[32,3712]{1,0:T(8,128)(2,1)S(1)}, bf16[32,3712]{1,0:T(8,128)(2,1)S(1)}, u32[]{:S(2)}, u32[]{:S(2)}) collective-permute-start(bf16[32,3712]{1,0:T(8,128)(2,1)S(1)} %prepare.1.block), channel_id=1, source_target_pairs={{0,4},{1,5},{2,6},{3,7},{4,12},{5,13},{6,14},{7,15},{8,0},{9,1},{1... | collective-permute-start | bytes 712712 | tf_op jit(solution)/shard_map/ppermute | solution.py:294
  5.0 1.1 %collective-permute-start.4 = (bf16[16,3712]{1,0:T(8,128)(2,1)S(1)}, bf16[16,3712]{1,0:T(8,128)(2,1)S(1)}, u32[]{:S(2)}, u32[]{:S(2)}) collective-permute-start(bf16[16,3712]{1,0:T(8,128)(2,1)S(1)} %get-tuple-element.35), channel_id=1, source_target_pairs={{0,8},{1,9},{2,10},{3,11},{4,0},{5,1},{6,2},{7,3},{8,12},{9,13},{1... | collective-permute-start | bytes 356360 | tf_op jit(solution)/shard_map/ppermute | solution.py:294
  6.1 2.6 %copy-done.1 = bf16[1,512,3584]{2,1,0:T(8,128)(2,1)S(1)} copy-done((bf16[1,512,3584]{2,1,0:T(8,128)(2,1)S(1)}, bf16[1,512,3584]{2,1,0:T(8,128)(2,1)}, u32[]{:S(2)}) %copy-start.1) | copy-done | bytes 3670040
  9.5 7.8 %collective-permute-done.1.source = bf16[512,3584]{1,0:T(8,128)(2,1)} collective-permute-done((bf16[512,3584]{1,0:T(8,128)(2,1)}, bf16[512,3584]{1,0:T(8,128)(2,1)}, u32[]{:S(2)}, u32[]{:S(2)}) %collective-permute-start.1) | collective-permute-done | bytes 3670048 | tf_op jit(solution)/shard_map/ppermute | solution.py:312
  17.3 2.0 %loaded.6.refs_10_ = bf16[512,3584]{1,0:T(8,128)(2,1)S(1)} custom-call(bf16[512,3584]{1,0:T(8,128)(2,1)} %collective-permute-done.1.source), custom_call_target="tpu_custom_call" | custom-call | bytes 7340032 | tf_op jit(solution)/shard_map/loaded/pallas_call | solution.py:84
  19.8 2.9 %collective-permute-start.6 = (bf16[32,3712]{1,0:T(8,128)(2,1)S(1)}, bf16[32,3712]{1,0:T(8,128)(2,1)S(1)}, u32[]{:S(2)}, u32[]{:S(2)}) collective-permute-start(bf16[32,3712]{1,0:T(8,128)(2,1)S(1)} %get-tuple-element.37), channel_id=1, source_target_pairs={{0,2},{1,3},{2,0},{3,1},{4,6},{5,7},{6,4},{7,5},{8,10},{9,11},{10,... | collective-permute-start | bytes 712712 | tf_op jit(solution)/shard_map/ppermute | solution.py:294
  22.8 2.5 %collective-permute-start.5 = (bf16[16,3712]{1,0:T(8,128)(2,1)S(1)}, bf16[16,3712]{1,0:T(8,128)(2,1)S(1)}, u32[]{:S(2)}, u32[]{:S(2)}) collective-permute-start(bf16[16,3712]{1,0:T(8,128)(2,1)S(1)} %get-tuple-element.26), channel_id=1, source_target_pairs={{0,10},{1,11},{2,8},{3,9},{4,2},{5,3},{6,0},{7,1},{8,14},{9,15},{1... | collective-permute-start | bytes 356360 | tf_op jit(solution)/shard_map/ppermute | solution.py:294
  25.3 2.9 %collective-permute-start.3 = (bf16[16,3712]{1,0:T(8,128)(2,1)S(1)}, bf16[16,3712]{1,0:T(8,128)(2,1)S(1)}, u32[]{:S(2)}, u32[]{:S(2)}) collective-permute-start(bf16[16,3712]{1,0:T(8,128)(2,1)S(1)} %get-tuple-element.33), channel_id=1, source_target_pairs={{0,6},{1,7},{2,4},{3,5},{4,14},{5,15},{6,12},{7,13},{8,2},{9,3},{1... | collective-permute-start | bytes 356360 | tf_op jit(solution)/shard_map/ppermute | solution.py:294
  28.9 3.1 %loaded.7.refs_9_ = bf16[3584,1024]{1,0:T(8,128)(2,1)S(1)} custom-call(bf16[3584,1024]{1,0:T(8,128)(2,1)} %collective-permute-done.7.source), custom_call_target="tpu_custom_call" | custom-call | bytes 14680064 | tf_op jit(solution)/shard_map/loaded/pallas_call | solution.py:84
  32.0 0.8 %collective-permute-done.2.refs_0_ = bf16[16,3712]{1,0:T(8,128)(2,1)S(1)} collective-permute-done((bf16[16,3712]{1,0:T(8,128)(2,1)S(1)}, bf16[16,3712]{1,0:T(8,128)(2,1)S(1)}, u32[]{:S(2)}, u32[]{:S(2)}) %collective-permute-start.2) | collective-permute-done | bytes 118816 | tf_op jit(solution)/shard_map/ppermute | solution.py:294
  32.8 2.9 %collective-permute-done.3.refs_1_ = bf16[16,3712]{1,0:T(8,128)(2,1)S(1)} collective-permute-done((bf16[16,3712]{1,0:T(8,128)(2,1)S(1)}, bf16[16,3712]{1,0:T(8,128)(2,1)S(1)}, u32[]{:S(2)}, u32[]{:S(2)}) %collective-permute-start.3) | collective-permute-done | bytes 118816 | tf_op jit(solution)/shard_map/ppermute | solution.py:294
  35.7 3.4 %expert_pass.1 = (bf16[16,3712]{1,0:T(8,128)(2,1)S(1)}, bf16[16,3712]{1,0:T(8,128)(2,1)S(1)}, bf16[16,3712]{1,0:T(8,128)(2,1)S(1)}, bf16[16,3712]{1,0:T(8,128)(2...) custom-call(s32[1]{0:T(128)} %bitcast.chip, ...), custom_call_target="tpu_custom_call" | custom-call | bytes 22020096 | tf_op jit(solution)/shard_map/expert_pass/pallas_call | solution.py:84
  39.1 3.4 %collective-permute-start.8 = (bf16[16,3712]{1,0:T(8,128)(2,1)S(1)}, bf16[16,3712]{1,0:T(8,128)(2,1)S(1)}, u32[]{:S(2)}, u32[]{:S(2)}) collective-permute-start(bf16[16,3712]{1,0:T(8,128)(2,1)S(1)} %get-tuple-element.39), channel_id=1, source_target_pairs={{0,28},{1,29},{2,30},{3,31},{4,24},{5,25},{6,26},{7,27},{8,20},{9,... | collective-permute-start | bytes 356360 | tf_op jit(solution)/shard_map/ppermute | solution.py:294
  42.5 1.3 %collective-permute-start.9 = (bf16[16,3712]{1,0:T(8,128)(2,1)S(1)}, bf16[16,3712]{1,0:T(8,128)(2,1)S(1)}, u32[]{:S(2)}, u32[]{:S(2)}) collective-permute-start(bf16[16,3712]{1,0:T(8,128)(2,1)S(1)} %get-tuple-element.40), channel_id=1, source_target_pairs={{0,30},{1,31},{2,28},{3,29},{4,26},{5,27},{6,24},{7,25},{8,22},{9,... | collective-permute-start | bytes 356360 | tf_op jit(solution)/shard_map/ppermute | solution.py:294
  43.8 1.2 %collective-permute-start.10 = (bf16[16,3712]{1,0:T(8,128)(2,1)S(1)}, bf16[16,3712]{1,0:T(8,128)(2,1)S(1)}, u32[]{:S(2)}, u32[]{:S(2)}) collective-permute-start(bf16[16,3712]{1,0:T(8,128)(2,1)S(1)} %get-tuple-element.41), channel_id=1, source_target_pairs={{0,24},{1,25},{2,26},{3,27},{4,16},{5,17},{6,18},{7,19},{8,28},{9,... | collective-permute-start | bytes 356360 | tf_op jit(solution)/shard_map/ppermute | solution.py:294
  45.0 1.8 %collective-permute-start.11 = (bf16[16,3712]{1,0:T(8,128)(2,1)S(1)}, bf16[16,3712]{1,0:T(8,128)(2,1)S(1)}, u32[]{:S(2)}, u32[]{:S(2)}) collective-permute-start(bf16[16,3712]{1,0:T(8,128)(2,1)S(1)} %get-tuple-element.42), channel_id=1, source_target_pairs={{0,20},{1,21},{2,22},{3,23},{4,28},{5,29},{6,30},{7,31},{8,16},{9,... | collective-permute-start | bytes 356360 | tf_op jit(solution)/shard_map/ppermute | solution.py:294
  46.8 1.9 %collective-permute-start.12 = (bf16[16,3712]{1,0:T(8,128)(2,1)S(1)}, bf16[16,3712]{1,0:T(8,128)(2,1)S(1)}, u32[]{:S(2)}, u32[]{:S(2)}) collective-permute-start(bf16[16,3712]{1,0:T(8,128)(2,1)S(1)} %get-tuple-element.43), channel_id=1, source_target_pairs={{0,22},{1,23},{2,20},{3,21},{4,30},{5,31},{6,28},{7,29},{8,18},{9,... | collective-permute-start | bytes 356360 | tf_op jit(solution)/shard_map/ppermute | solution.py:294
  48.7 1.5 %collective-permute-start.13 = (bf16[16,3712]{1,0:T(8,128)(2,1)S(1)}, bf16[16,3712]{1,0:T(8,128)(2,1)S(1)}, u32[]{:S(2)}, u32[]{:S(2)}) collective-permute-start(bf16[16,3712]{1,0:T(8,128)(2,1)S(1)} %get-tuple-element.44), channel_id=1, source_target_pairs={{0,16},{1,17},{2,18},{3,19},{4,20},{5,21},{6,22},{7,23},{8,24},{9,... | collective-permute-start | bytes 356360 | tf_op jit(solution)/shard_map/ppermute | solution.py:294
  50.2 2.2 %collective-permute-done.9.refs_1_ = bf16[16,3712]{1,0:T(8,128)(2,1)S(1)} collective-permute-done((bf16[16,3712]{1,0:T(8,128)(2,1)S(1)}, bf16[16,3712]{1,0:T(8,128)(2,1)S(1)}, u32[]{:S(2)}, u32[]{:S(2)}) %collective-permute-start.9) | collective-permute-done | bytes 118816 | tf_op jit(solution)/shard_map/ppermute | solution.py:294
  52.4 1.1 %collective-permute-start.14 = (bf16[16,3712]{1,0:T(8,128)(2,1)S(1)}, bf16[16,3712]{1,0:T(8,128)(2,1)S(1)}, u32[]{:S(2)}, u32[]{:S(2)}) collective-permute-start(bf16[16,3712]{1,0:T(8,128)(2,1)S(1)} %get-tuple-element.45), channel_id=1, source_target_pairs={{0,18},{1,19},{2,16},{3,17},{4,22},{5,23},{6,20},{7,21},{8,26},{9,... | collective-permute-start | bytes 356360 | tf_op jit(solution)/shard_map/ppermute | solution.py:294
  53.5 9.0 %collective-permute-start.15 = (bf16[16,3712]{1,0:T(8,128)(2,1)S(1)}, bf16[16,3712]{1,0:T(8,128)(2,1)S(1)}, u32[]{:S(2)}, u32[]{:S(2)}) collective-permute-start(bf16[16,3712]{1,0:T(8,128)(2,1)S(1)} %get-tuple-element.46), channel_id=1, source_target_pairs={{0,26},{1,27},{2,24},{3,25},{4,18},{5,19},{6,16},{7,17},{8,30},{9,... | collective-permute-start | bytes 356360 | tf_op jit(solution)/shard_map/ppermute | solution.py:294
  62.5 2.6 %collective-permute-done.14.refs_6_ = bf16[16,3712]{1,0:T(8,128)(2,1)S(1)} collective-permute-done((bf16[16,3712]{1,0:T(8,128)(2,1)S(1)}, bf16[16,3712]{1,0:T(8,128)(2,1)S(1)}, u32[]{:S(2)}, u32[]{:S(2)}) %collective-permute-start.14) | collective-permute-done | bytes 118816 | tf_op jit(solution)/shard_map/ppermute | solution.py:294
  65.1 1.1 %combine.1 = bf16[32,3584]{1,0:T(8,128)(2,1)} custom-call(bf16[16,3712]{1,0:T(8,128)(2,1)S(1)} %collective-permute-done.8.refs_0_, bf16[16,3712]{1,0:T(8,128)(2,1)S(1)} %collective-permute-done.9.refs_1_, bf16[16,3712]{1,0:T(8,128)(2,1)S(1)} %collective-permute-done.10.refs_2_, bf16[16,3712]{1,0:T(8,128)(2,1)S(1)} %collective-permute-done.11.refs_3_, ...), custom_call_target="tpu_custom_call" | custom-call | tf_op jit(solution)/shard_map/combine/pallas_call | solution.py:84
  (21 shorter events, 2.9 us)
Async XLA Ops:
  0.0 28.9 %collective-permute-start.7 = (bf16[3584,1024]{1,0:T(8,128)(2,1)}, bf16[3584,1024]{1,0:T(8,128)(2,1)}, u32[]{:S(2)}, u32[]{:S(2)}) collective-permute-start(bf16[3584,1024]{1,0:T(8,128)(2,1)} %bitcast.11), channel_id=1, source_target_pairs={{0,1},{1,0},{2,3},{3,2},{4,5},{5,4},{6,7},{7,6},{8,9},{9,8},{10,11... | collective-permute-start | bytes 22020104 | tf_op jit(solution)/shard_map/ppermute | solution.py:313
  0.5 16.9 %collective-permute-start.1 = (bf16[512,3584]{1,0:T(8,128)(2,1)}, bf16[512,3584]{1,0:T(8,128)(2,1)}, u32[]{:S(2)}, u32[]{:S(2)}) collective-permute-start(bf16[512,3584]{1,0:T(8,128)(2,1)} %bitcast.13), channel_id=1, source_target_pairs={{0,1},{1,0},{2,3},{3,2},{4,5},{5,4},{6,7},{7,6},{8,9},{9,8},{10,11... | collective-permute-start | bytes 11010056 | tf_op jit(solution)/shard_map/ppermute | solution.py:312
  1.5 17.9 %collective-permute-start = (bf16[32,3712]{1,0:T(8,128)(2,1)S(1)}, bf16[32,3712]{1,0:T(8,128)(2,1)S(1)}, u32[]{:S(2)}, u32[]{:S(2)}) collective-permute-start(bf16[32,3712]{1,0:T(8,128)(2,1)S(1)} %prepare.1.block), channel_id=1, source_target_pairs={{0,4},{1,5},{2,6},{3,7},{4,12},{5,13},{6,14},{7,15},{8,0},{9,1},{1... | collective-permute-start | bytes 712712 | tf_op jit(solution)/shard_map/ppermute | solution.py:294
  4.6 4.4 %copy-start = (bf16[1,3584,1024]{2,1,0:T(8,128)(2,1)S(1)}, bf16[1,3584,1024]{2,1,0:T(8,128)(2,1)}, u32[]{:S(2)}) copy-start(bf16[1,3584,1024]{2,1,0:T(8,128)(2,1)} %param.8) | copy-start | bytes 22020100
  5.0 20.3 %collective-permute-start.4 = (bf16[16,3712]{1,0:T(8,128)(2,1)S(1)}, bf16[16,3712]{1,0:T(8,128)(2,1)S(1)}, u32[]{:S(2)}, u32[]{:S(2)}) collective-permute-start(bf16[16,3712]{1,0:T(8,128)(2,1)S(1)} %get-tuple-element.35), channel_id=1, source_target_pairs={{0,8},{1,9},{2,10},{3,11},{4,0},{5,1},{6,2},{7,3},{8,12},{9,13},{1... | collective-permute-start | bytes 356360 | tf_op jit(solution)/shard_map/ppermute | solution.py:294
  6.1 2.6 %copy-start.1 = (bf16[1,512,3584]{2,1,0:T(8,128)(2,1)S(1)}, bf16[1,512,3584]{2,1,0:T(8,128)(2,1)}, u32[]{:S(2)}) copy-start(bf16[1,512,3584]{2,1,0:T(8,128)(2,1)} %param.9) | copy-start | bytes 11010052
  19.8 15.9 %collective-permute-start.6 = (bf16[32,3712]{1,0:T(8,128)(2,1)S(1)}, bf16[32,3712]{1,0:T(8,128)(2,1)S(1)}, u32[]{:S(2)}, u32[]{:S(2)}) collective-permute-start(bf16[32,3712]{1,0:T(8,128)(2,1)S(1)} %get-tuple-element.37), channel_id=1, source_target_pairs={{0,2},{1,3},{2,0},{3,1},{4,6},{5,7},{6,4},{7,5},{8,10},{9,11},{10,... | collective-permute-start | bytes 712712 | tf_op jit(solution)/shard_map/ppermute | solution.py:294
  22.8 6.2 %collective-permute-start.5 = (bf16[16,3712]{1,0:T(8,128)(2,1)S(1)}, bf16[16,3712]{1,0:T(8,128)(2,1)S(1)}, u32[]{:S(2)}, u32[]{:S(2)}) collective-permute-start(bf16[16,3712]{1,0:T(8,128)(2,1)S(1)} %get-tuple-element.26), channel_id=1, source_target_pairs={{0,10},{1,11},{2,8},{3,9},{4,2},{5,3},{6,0},{7,1},{8,14},{9,15},{1... | collective-permute-start | bytes 356360 | tf_op jit(solution)/shard_map/ppermute | solution.py:294
  25.3 7.5 %collective-permute-start.2 = (bf16[16,3712]{1,0:T(8,128)(2,1)S(1)}, bf16[16,3712]{1,0:T(8,128)(2,1)S(1)}, u32[]{:S(2)}, u32[]{:S(2)}) collective-permute-start(bf16[16,3712]{1,0:T(8,128)(2,1)S(1)} %get-tuple-element.32), channel_id=1, source_target_pairs={{0,4},{1,5},{2,6},{3,7},{4,12},{5,13},{6,14},{7,15},{8,0},{9,1},{1... | collective-permute-start | bytes 356360 | tf_op jit(solution)/shard_map/ppermute | solution.py:294
  25.3 10.4 %collective-permute-start.3 = (bf16[16,3712]{1,0:T(8,128)(2,1)S(1)}, bf16[16,3712]{1,0:T(8,128)(2,1)S(1)}, u32[]{:S(2)}, u32[]{:S(2)}) collective-permute-start(bf16[16,3712]{1,0:T(8,128)(2,1)S(1)} %get-tuple-element.33), channel_id=1, source_target_pairs={{0,6},{1,7},{2,4},{3,5},{4,14},{5,15},{6,12},{7,13},{8,2},{9,3},{1... | collective-permute-start | bytes 356360 | tf_op jit(solution)/shard_map/ppermute | solution.py:294
  39.1 9.6 %collective-permute-start.8 = (bf16[16,3712]{1,0:T(8,128)(2,1)S(1)}, bf16[16,3712]{1,0:T(8,128)(2,1)S(1)}, u32[]{:S(2)}, u32[]{:S(2)}) collective-permute-start(bf16[16,3712]{1,0:T(8,128)(2,1)S(1)} %get-tuple-element.39), channel_id=1, source_target_pairs={{0,28},{1,29},{2,30},{3,31},{4,24},{5,25},{6,26},{7,27},{8,20},{9,... | collective-permute-start | bytes 356360 | tf_op jit(solution)/shard_map/ppermute | solution.py:294
  42.5 9.8 %collective-permute-start.9 = (bf16[16,3712]{1,0:T(8,128)(2,1)S(1)}, bf16[16,3712]{1,0:T(8,128)(2,1)S(1)}, u32[]{:S(2)}, u32[]{:S(2)}) collective-permute-start(bf16[16,3712]{1,0:T(8,128)(2,1)S(1)} %get-tuple-element.40), channel_id=1, source_target_pairs={{0,30},{1,31},{2,28},{3,29},{4,26},{5,27},{6,24},{7,25},{8,22},{9,... | collective-permute-start | bytes 356360 | tf_op jit(solution)/shard_map/ppermute | solution.py:294
  43.8 9.7 %collective-permute-start.10 = (bf16[16,3712]{1,0:T(8,128)(2,1)S(1)}, bf16[16,3712]{1,0:T(8,128)(2,1)S(1)}, u32[]{:S(2)}, u32[]{:S(2)}) collective-permute-start(bf16[16,3712]{1,0:T(8,128)(2,1)S(1)} %get-tuple-element.41), channel_id=1, source_target_pairs={{0,24},{1,25},{2,26},{3,27},{4,16},{5,17},{6,18},{7,19},{8,28},{9,... | collective-permute-start | bytes 356360 | tf_op jit(solution)/shard_map/ppermute | solution.py:294
  45.0 17.5 %collective-permute-start.11 = (bf16[16,3712]{1,0:T(8,128)(2,1)S(1)}, bf16[16,3712]{1,0:T(8,128)(2,1)S(1)}, u32[]{:S(2)}, u32[]{:S(2)}) collective-permute-start(bf16[16,3712]{1,0:T(8,128)(2,1)S(1)} %get-tuple-element.42), channel_id=1, source_target_pairs={{0,20},{1,21},{2,22},{3,23},{4,28},{5,29},{6,30},{7,31},{8,16},{9,... | collective-permute-start | bytes 356360 | tf_op jit(solution)/shard_map/ppermute | solution.py:294
  46.8 15.7 %collective-permute-start.12 = (bf16[16,3712]{1,0:T(8,128)(2,1)S(1)}, bf16[16,3712]{1,0:T(8,128)(2,1)S(1)}, u32[]{:S(2)}, u32[]{:S(2)}) collective-permute-start(bf16[16,3712]{1,0:T(8,128)(2,1)S(1)} %get-tuple-element.43), channel_id=1, source_target_pairs={{0,22},{1,23},{2,20},{3,21},{4,30},{5,31},{6,28},{7,29},{8,18},{9,... | collective-permute-start | bytes 356360 | tf_op jit(solution)/shard_map/ppermute | solution.py:294
  48.7 13.8 %collective-permute-start.13 = (bf16[16,3712]{1,0:T(8,128)(2,1)S(1)}, bf16[16,3712]{1,0:T(8,128)(2,1)S(1)}, u32[]{:S(2)}, u32[]{:S(2)}) collective-permute-start(bf16[16,3712]{1,0:T(8,128)(2,1)S(1)} %get-tuple-element.44), channel_id=1, source_target_pairs={{0,16},{1,17},{2,18},{3,19},{4,20},{5,21},{6,22},{7,23},{8,24},{9,... | collective-permute-start | bytes 356360 | tf_op jit(solution)/shard_map/ppermute | solution.py:294
  52.4 12.7 %collective-permute-start.14 = (bf16[16,3712]{1,0:T(8,128)(2,1)S(1)}, bf16[16,3712]{1,0:T(8,128)(2,1)S(1)}, u32[]{:S(2)}, u32[]{:S(2)}) collective-permute-start(bf16[16,3712]{1,0:T(8,128)(2,1)S(1)} %get-tuple-element.45), channel_id=1, source_target_pairs={{0,18},{1,19},{2,16},{3,17},{4,22},{5,23},{6,20},{7,21},{8,26},{9,... | collective-permute-start | bytes 356360 | tf_op jit(solution)/shard_map/ppermute | solution.py:294
  53.5 11.6 %collective-permute-start.15 = (bf16[16,3712]{1,0:T(8,128)(2,1)S(1)}, bf16[16,3712]{1,0:T(8,128)(2,1)S(1)}, u32[]{:S(2)}, u32[]{:S(2)}) collective-permute-start(bf16[16,3712]{1,0:T(8,128)(2,1)S(1)} %get-tuple-element.46), channel_id=1, source_target_pairs={{0,26},{1,27},{2,24},{3,25},{4,18},{5,19},{6,16},{7,17},{8,30},{9,... | collective-permute-start | bytes 356360 | tf_op jit(solution)/shard_map/ppermute | solution.py:294

commit v6 on v0

--- a/solution.py
+++ b/solution.py
@@ -1,6 +1,10 @@
+import functools
+
 import jax
 import jax.numpy as jnp
 from jax import lax
+from jax.experimental import pallas as pl
+from jax.experimental.pallas import tpu as pltpu
 from jax.sharding import PartitionSpec as P
 
 
@@ -9,7 +13,7 @@
     return lax.ppermute(shard, axis, [(i, (i + by) % length) for i in range(length)])
 
 
-def per_device(rows, route_ids, route_weights, w_gate_up, w_down):
+def by_slots(rows, route_ids, route_weights, w_gate_up, w_down):
     devices = lax.axis_size("expert")
     experts = devices // 2
     tokens = rows[0]
@@ -47,8 +51,238 @@
     expert_out = jnp.sum(returned, axis=2).astype(jnp.bfloat16).reshape(slot_total, width)
     pair_out = expert_out[place].astype(jnp.float32) * route_weights[0].reshape(-1)[:, None]
     layer_out = jnp.sum(pair_out.reshape(tok_count, top_count, width), axis=1).astype(jnp.bfloat16)
-    handed = passed_along(layer_out, "section", 1)
-    return handed[None]
+    return passed_along(layer_out, "section", 1)[None]
+
+
+LANES = 128
+TOKEN_LANE = 64
+
+
+def iota(shape, axis):
+    return lax.broadcasted_iota(jnp.int32, shape, axis)
+
+
+def ones_where(condition):
+    return jnp.where(condition, 1.0, 0.0).astype(jnp.bfloat16)
+
+
+def across(left, right):
+    return lax.dot_general(left, right, (((0,), (0,)), ((), ())), preferred_element_type=jnp.float32)
+
+
+def local_call(kernel, name, out_shape, in_specs, operands, scratch=(), limit=12, flops=0, moved=0):
+    vmem = pl.BlockSpec(memory_space=pltpu.VMEM)
+    return pl.pallas_call(
+        kernel,
+        out_shape=out_shape,
+        in_specs=[vmem if spec is None else pl.BlockSpec(memory_space=spec) for spec in in_specs],
+        out_specs=jax.tree.map(lambda _: vmem, out_shape),
+        scratch_shapes=list(scratch),
+        compiler_params=pltpu.CompilerParams(vmem_limit_bytes=limit << 20),
+        cost_estimate=pl.CostEstimate(flops=flops, bytes_accessed=moved, transcendentals=0),
+        name=name,
+    )(*operands)
+
+
+def pack_kernel(experts, ids_in, weights_in, rows_in, packed, ids, weights, block, sems):
+    tok_count, width = rows_in.shape
+    top_count = ids.shape[0]
+    capacity = packed.shape[0] // experts
+    copies = [
+        pltpu.make_async_copy(ids_in, ids, sems.at[0]),
+        pltpu.make_async_copy(weights_in, weights, sems.at[1]),
+        pltpu.make_async_copy(rows_in, block.at[:, pl.ds(0, width)], sems.at[2]),
+    ]
+    for copy in copies:
+        copy.start()
+    square = (tok_count, tok_count)
+    earlier = ones_where(iota(square, 0) < iota(square, 1))
+    expert = iota((experts, tok_count), 0)
+    unit = ones_where(iota((4 * experts, LANES), 0) == iota((4 * experts, LANES), 1))
+    token = ones_where(iota((tok_count, LANES), 0) + TOKEN_LANE == iota((tok_count, LANES), 1))
+    slot = iota((capacity, tok_count), 0).astype(jnp.float32)
+    copies[0].wait()
+    copies[1].wait()
+    named = jnp.zeros((experts, tok_count), jnp.float32)
+    scale = jnp.zeros((experts, tok_count), jnp.float32)
+    for k in range(top_count):
+        hit = ids[k : k + 1, :] == expert
+        named = named + jnp.where(hit, 1.0, 0.0)
+        scale = scale + jnp.where(hit, weights[k : k + 1, :], 0.0)
+    rank = jnp.dot(named.astype(jnp.bfloat16), earlier, preferred_element_type=jnp.float32)
+    rank = jnp.where(named > 0.5, rank, -1.0)
+    pick = [jnp.where(rank[e : e + 1, :] == slot, 1.0, 0.0) for e in range(experts)]
+    pick = jnp.concatenate(pick, axis=0).astype(jnp.bfloat16)
+    notes = [jnp.zeros_like(scale)]
+    for _ in range(3):
+        piece = scale.astype(jnp.bfloat16).astype(jnp.float32)
+        scale = scale - piece
+        notes.append(piece)
+    notes = across(jnp.concatenate(notes, axis=0).astype(jnp.bfloat16), unit)
+    block[:, width:] = notes.astype(jnp.bfloat16) + token
+    copies[2].wait()
+    rows = jnp.dot(pick, block[...], preferred_element_type=jnp.float32)
+    packed[...] = rows.astype(jnp.bfloat16)
+
+
+def pack(ids, weights, tokens, experts, capacity):
+    tok_count, width = tokens.shape
+    return local_call(
+        functools.partial(pack_kernel, experts),
+        "pack",
+        pltpu.VMEM((experts * capacity, width + LANES), jnp.bfloat16),
+        [pl.ANY] * 3,
+        tuple(pltpu.with_memory_space_constraint(x, pltpu.HBM) for x in (ids, weights, tokens)),
+        [
+            pltpu.VMEM(ids.shape, ids.dtype),
+            pltpu.VMEM(weights.shape, weights.dtype),
+            pltpu.VMEM((tok_count, width + LANES), jnp.bfloat16),
+            pltpu.SemaphoreType.DMA((3,)),
+        ],
+        limit=8,
+    )
+
+
+def gated(both):
+    hidden = both.shape[1] // 2
+    gate = both[:, :hidden]
+    return (gate / (1.0 + jnp.exp(-gate)) * both[:, hidden:]).astype(jnp.bfloat16)
+
+
+def expert_kernel(sections, slots, far_in, far_out, near_in, near_out, *refs):
+    apart, (close, total, w_in, w_out, sems) = refs[:-5], refs[-5:]
+    copies = [
+        pltpu.make_async_copy(near_in, w_in, sems.at[0]),
+        pltpu.make_async_copy(near_out, w_out, sems.at[1]),
+    ]
+    for copy in copies:
+        copy.start()
+    chip, section = lax.axis_index("expert") >> 1, lax.axis_index("section")
+    width = total.shape[1]
+    half = len(apart)
+    experts = 2 * half
+    capacity = slots.shape[0] // experts
+    both = jnp.dot(slots[:, :width], far_in[...], preferred_element_type=jnp.float32)
+    total[...] = jnp.dot(gated(both), far_out[...], preferred_element_type=jnp.float32)
+    copies[0].wait()
+    both = jnp.dot(slots[:, :width], w_in[...], preferred_element_type=jnp.float32)
+    copies[1].wait()
+    total[...] += jnp.dot(gated(both), w_out[...], preferred_element_type=jnp.float32)
+    notes = slots[:, width:].astype(jnp.float32)
+    lane = iota(notes.shape, 1)
+    mine = (lane >= experts) & (lane < 4 * experts) & ((lane & (experts - 1)) == chip)
+    total[...] = total[...] * jnp.sum(jnp.where(mine, notes, 0.0), axis=1, keepdims=True)
+
+    def rows_of(source, count):
+        return pl.ds(pl.multiple_of(source * capacity, capacity), count * capacity)
+
+    for r, out in enumerate(apart):
+        rows = rows_of(chip ^ (half + r), 1)
+        out[:, :width] = total[rows, :].astype(jnp.bfloat16)
+        out[:, width:] = slots[rows, width:]
+    close[...] = jnp.zeros(close.shape, close.dtype)
+    rows = rows_of(chip & half, half)
+    target = jnp.where(section == sections - 1, 0, section + 1) * half
+    to = rows_of(target, half)
+    close[to, :width] = total[rows, :].astype(jnp.bfloat16)
+    close[to, width:] = slots[rows, width:]
+
+
+def expert_pass(slots, far, near, capacity, experts, sections):
+    count, full = slots.shape
+    half = experts // 2
+    piece = jax.ShapeDtypeStruct((capacity, full), jnp.bfloat16)
+    close = jax.ShapeDtypeStruct((sections * half * capacity, full), jnp.bfloat16)
+    outs = local_call(
+        functools.partial(expert_kernel, sections),
+        "expert_pass",
+        [piece] * half + [close],
+        [None] * 3 + [pl.ANY] * 2,
+        (slots, *far, *(pltpu.with_memory_space_constraint(w, pltpu.HBM) for w in near)),
+        [
+            pltpu.VMEM((count, full - LANES), jnp.float32),
+            *(pltpu.VMEM(w.shape, w.dtype) for w in near),
+            pltpu.SemaphoreType.DMA((2,)),
+        ],
+        limit=40,
+        moved=2 * sum(w.size for w in (*far, *near)),
+    )
+    return outs[:-1], outs[-1]
+
+
+def combine_kernel(*refs):
+    blocks, out, slots = refs[:-2], refs[-2], refs[-1]
+    tok_count, width = out.shape
+    start = 0
+    for block in blocks:
+        slots[start : start + block.shape[0]] = block[...]
+        start += block.shape[0]
+    token = slots[:, width:]
+    part = width // 7
+    for at in range(7):
+        place = slice(at * part, (at + 1) * part)
+        mixed = across(token, slots[:, place])[TOKEN_LANE : TOKEN_LANE + tok_count]
+        out[:, place] = mixed.astype(out.dtype)
+
+
+def combine(blocks, tok_count):
+    full = blocks[0].shape[1]
+    count = sum(block.shape[0] for block in blocks)
+    return local_call(
+        combine_kernel,
+        "combine",
+        jax.ShapeDtypeStruct((tok_count, full - LANES), jnp.bfloat16),
+        [None] * len(blocks),
+        tuple(blocks),
+        [pltpu.VMEM((count, full), jnp.bfloat16)],
+    )
+
+
+def by_chips(rows, route_ids, route_weights, w_gate_up, w_down):
+    sections = lax.axis_size("section")
+    devices = lax.axis_size("expert")
+    experts = devices // 2
+    half = experts // 2
+    tokens = rows[0]
+    tok_count = tokens.shape[0]
+    top_count = route_ids.shape[2]
+    capacity = max(2, 2 * tok_count * top_count // experts)
+    swap = [(i, i ^ 1) for i in range(devices)]
+    w_in, w_out = w_gate_up[0], w_down[0]
+    far = [lax.ppermute(w, "expert", swap) for w in (w_out, w_in)]
+    packed = pack(route_ids[0].T, route_weights[0].T, tokens, experts, capacity)
+    groups = [[2 * e + core for e in range(experts)] for core in range(2)]
+    slots = lax.all_to_all(packed, "expert", 0, 0, axis_index_groups=groups, tiled=True)
+    pieces, close = expert_pass(
+        slots, (far[1], far[0]), (w_in, w_out), capacity, experts, sections
+    )
+    axes = ("section", "expert")
+    back = []
+    for r, piece in enumerate(pieces):
+        pairs = [
+            (
+                (s * experts + e) * 2 + core,
+                ((s + 1) % sections * experts + (e ^ (half + r))) * 2 + core,
+            )
+            for s in range(sections)
+            for e in range(experts)
+            for core in range(2)
+        ]
+        back.append(lax.ppermute(piece, axes, pairs))
+    groups = [
+        [(s * experts + e) * 2 + core for s in range(sections) for e in range(at, at + half)]
+        for at in (0, half)
+        for core in range(2)
+    ]
+    back.append(lax.all_to_all(close, axes, 0, 0, axis_index_groups=groups, tiled=True))
+    return combine(back, tok_count)[None]
+
+
+def per_device(rows, route_ids, route_weights, w_gate_up, w_down):
+    experts = lax.axis_size("expert") // 2
+    fits = experts in (4, 8) and rows.shape[1] <= LANES - TOKEN_LANE
+    plan = by_chips if fits else by_slots
+    return plan(rows, route_ids, route_weights, w_gate_up, w_down)
 
 
 def solution(mesh):

time: 120 us -> 70.7 us (0.59)
  the two profiles are of different devices: /device:TPU:12 before, /device:TPU:0 now
where the time goes in v6:
time: 70.7 us; the launch traced here: 70.5 us
  blocking collectives  31.1 us (44%)
  waiting for transfers between devices  15.6 us (22%)
  starting transfers between devices  13.6 us (19%)
  Pallas kernels  10.2 us (14%)
    all_to_all x1, blocking collectives, by_chips(): lax.all_to_all(packed, 'expert', 0, 0, axis_index_groups=groups, tiled=True)  31.1 us
    ppermute x4, waiting for transfers between devices, by_chips(): back.append(lax.ppermute(piece, axes, pairs))  15.6 us
    pallas_call x3, Pallas kernels, local_call(): pl.pallas_call(kernel, out_shape=out_shape, in_specs=[vmem if spec is Non...  10.2 us
    ppermute x4, starting transfers between devices, by_chips(): back.append(lax.ppermute(piece, axes, pairs))  9.51 us
    all_to_all x1, starting transfers between devices, by_chips(): lax.all_to_all(close, axes, 0, 0, axis_index_groups=groups, tiled=True)  3.57 us
  transfers between devices with their start and end apart: 7, of which 4 were waited for; matrix products, arithmetic and copies ran while one was open for 0% of the time, Pallas kernels for 2%

profile of v6, /device:TPU:0, one launch (start us, length us, event | category | flops | bytes accessed | tf_op | source)
XLA Modules:
  0.0 70.5 jit_solution(13663443053934261196)
XLA Ops:
  0.0 0.5 collective-permute-start
  0.5 0.1 collective-permute-start.1
  0.5 1.4 %pack.1 = bf16[128,3712]{1,0:T(8,128)(2,1)S(1)} custom-call(s32[2,32]{1,0:T(2,128)} %bitcast.22, f32[2,32]{1,0:T(2,128)} %bitcast.23, bf16[32,3584]{1,0:T(8,128)(2,1)} %bitcast.21), custom_call_target="tpu_custom_call" | custom-call | tf_op jit(solution)/shard_map/pack/pallas_call | solution.py:75
  1.9 31.1 %all_to_all.22 = bf16[8,16,3712]{2,1,0:T(8,128)(2,1)S(1)} all-to-all(bf16[8,16,3712]{2,1,0:T(8,128)(2,1)S(1)} %bitcast.15), channel_id=1, replica_groups={{0,2,4,6,8,10,12,14},{1,3,5,7,9,11,13,15},{16,18,20,22,24,26,28,30},{17..., dimensions={0} | all-to-all | bytes 1900544 | tf_op jit(solution)/shard_map/all_to_all | solution.py:255
  33.0 0.0 collective-permute-done.1.far_out
  33.0 0.0 collective-permute-done.far_in
  33.0 7.7 %expert_pass.1 = (bf16[16,3712]{1,0:T(8,128)(2,1)S(1)}, bf16[16,3712]{1,0:T(8,128)(2,1)S(1)}, bf16[16,3712]{1,0:T(8,128)(2,1)S(1)}, bf16[16,3712]{1,0:T(8,128)(2,1)S(1)}, bf16[128,3712]{1,0:T(8,128)(2,1)}) custom-call(bf16[128,3712]{1,0:T(8,128)(2,1)S(1)} %bitcast.16, bf16[3584,1024]{1,0:T(8,128)(2,1)S(1)} %collective-permute-done.far_in, ...), custom_call_target="tpu_custom_call" | custom-call | bytes 22020096 | tf_op jit(solution)/shard_map/expert_pass/pallas_call | solution.py:75
  40.7 3.6 %all-to-all-start.1 = ((bf16[8,16,3712]{2,1,0:T(8,128)(2,1)}), bf16[8,16,3712]{2,1,0:T(8,128)(2,1)S(1)}, u32[]{:S(2)}, u32[]{:S(2)}) async-start(bf16[8,16,3712]{2,1,0:T(8,128)(2,1)} %bitcast.9), calls=%async_computation.1 | async-start | bytes 1900544 | tf_op jit(solution)/shard_map/all_to_all | solution.py:277
  44.2 2.8 %collective-permute-start.2 = (bf16[16,3712]{1,0:T(8,128)(2,1)S(1)}, bf16[16,3712]{1,0:T(8,128)(2,1)S(1)}, u32[]{:S(2)}, u32[]{:S(2)}) collective-permute-start(bf16[16,3712]{1,0:T(8,128)(2,1)S(1)} %get-tuple-element.10), channel_id=1, source_target_pairs={{0,24},{1,25},{2,26},{3,27},{4,28},{5,29},{6,30},{7,31},{8,16},{9,... | collective-permute-start | bytes 356360 | tf_op jit(solution)/shard_map/ppermute | solution.py:271
  47.0 2.4 %collective-permute-start.3 = (bf16[16,3712]{1,0:T(8,128)(2,1)S(1)}, bf16[16,3712]{1,0:T(8,128)(2,1)S(1)}, u32[]{:S(2)}, u32[]{:S(2)}) collective-permute-start(bf16[16,3712]{1,0:T(8,128)(2,1)S(1)} %get-tuple-element.11), channel_id=1, source_target_pairs={{0,26},{1,27},{2,24},{3,25},{4,30},{5,31},{6,28},{7,29},{8,18},{9,... | collective-permute-start | bytes 356360 | tf_op jit(solution)/shard_map/ppermute | solution.py:271
  49.4 3.2 %collective-permute-start.4 = (bf16[16,3712]{1,0:T(8,128)(2,1)S(1)}, bf16[16,3712]{1,0:T(8,128)(2,1)S(1)}, u32[]{:S(2)}, u32[]{:S(2)}) collective-permute-start(bf16[16,3712]{1,0:T(8,128)(2,1)S(1)} %get-tuple-element.12), channel_id=1, source_target_pairs={{0,28},{1,29},{2,30},{3,31},{4,24},{5,25},{6,26},{7,27},{8,20},{9,... | collective-permute-start | bytes 356360 | tf_op jit(solution)/shard_map/ppermute | solution.py:271
  52.7 1.1 %collective-permute-start.5 = (bf16[16,3712]{1,0:T(8,128)(2,1)S(1)}, bf16[16,3712]{1,0:T(8,128)(2,1)S(1)}, u32[]{:S(2)}, u32[]{:S(2)}) collective-permute-start(bf16[16,3712]{1,0:T(8,128)(2,1)S(1)} %get-tuple-element.13), channel_id=1, source_target_pairs={{0,30},{1,31},{2,28},{3,29},{4,26},{5,27},{6,24},{7,25},{8,22},{9,... | collective-permute-start | bytes 356360 | tf_op jit(solution)/shard_map/ppermute | solution.py:271
  53.8 5.3 %collective-permute-done.2.refs_0_ = bf16[16,3712]{1,0:T(8,128)(2,1)S(1)} collective-permute-done((bf16[16,3712]{1,0:T(8,128)(2,1)S(1)}, bf16[16,3712]{1,0:T(8,128)(2,1)S(1)}, u32[]{:S(2)}, u32[]{:S(2)}) %collective-permute-start.2) | collective-permute-done | bytes 118816 | tf_op jit(solution)/shard_map/ppermute | solution.py:271
  59.0 2.5 %collective-permute-done.3.refs_1_ = bf16[16,3712]{1,0:T(8,128)(2,1)S(1)} collective-permute-done((bf16[16,3712]{1,0:T(8,128)(2,1)S(1)}, bf16[16,3712]{1,0:T(8,128)(2,1)S(1)}, u32[]{:S(2)}, u32[]{:S(2)}) %collective-permute-start.3) | collective-permute-done | bytes 118816 | tf_op jit(solution)/shard_map/ppermute | solution.py:271
  61.6 5.7 %collective-permute-done.4.refs_2_ = bf16[16,3712]{1,0:T(8,128)(2,1)S(1)} collective-permute-done((bf16[16,3712]{1,0:T(8,128)(2,1)S(1)}, bf16[16,3712]{1,0:T(8,128)(2,1)S(1)}, u32[]{:S(2)}, u32[]{:S(2)}) %collective-permute-start.4) | collective-permute-done | bytes 118816 | tf_op jit(solution)/shard_map/ppermute | solution.py:271
  67.3 2.0 %collective-permute-done.5.refs_3_ = bf16[16,3712]{1,0:T(8,128)(2,1)S(1)} collective-permute-done((bf16[16,3712]{1,0:T(8,128)(2,1)S(1)}, bf16[16,3712]{1,0:T(8,128)(2,1)S(1)}, u32[]{:S(2)}, u32[]{:S(2)}) %collective-permute-start.5) | collective-permute-done | bytes 118816 | tf_op jit(solution)/shard_map/ppermute | solution.py:271
  69.3 0.0 all-to-all-done.1
  69.3 1.1 %combine.1 = bf16[32,3584]{1,0:T(8,128)(2,1)} custom-call(bf16[16,3712]{1,0:T(8,128)(2,1)S(1)} %collective-permute-done.2.refs_0_, bf16[16,3712]{1,0:T(8,128)(2,1)S(1)} %collective-permute-done.3.refs_1_, bf16[16,3712]{1,0:T(8,128)(2,1)S(1)} %collective-permute-done.4.refs_2_, bf16[16,3712]{1,0:T(8,128)(2,1)S(1)} %collective-permute-done.5.refs_3_, ...), custom_call_target="tpu_custom_call" | custom-call | tf_op jit(solution)/shard_map/combine/pallas_call | solution.py:75
Async XLA Ops:
  0.0 33.0 %collective-permute-start = (bf16[3584,1024]{1,0:T(8,128)(2,1)}, bf16[3584,1024]{1,0:T(8,128)(2,1)S(1)}, u32[]{:S(2)}, u32[]{:S(2)}) collective-permute-start(bf16[3584,1024]{1,0:T(8,128)(2,1)} %bitcast.17), channel_id=1, source_target_pairs={{0,1},{1,0},{2,3},{3,2},{4,5},{5,4},{6,7},{7,6},{8,9},{9,8},{10,11... | collective-permute-start | bytes 22020104 | tf_op jit(solution)/shard_map/ppermute | solution.py:252
  0.5 32.5 %collective-permute-start.1 = (bf16[512,3584]{1,0:T(8,128)(2,1)}, bf16[512,3584]{1,0:T(8,128)(2,1)S(1)}, u32[]{:S(2)}, u32[]{:S(2)}) collective-permute-start(bf16[512,3584]{1,0:T(8,128)(2,1)} %bitcast.19), channel_id=1, source_target_pairs={{0,1},{1,0},{2,3},{3,2},{4,5},{5,4},{6,7},{7,6},{8,9},{9,8},{10,11... | collective-permute-start | bytes 11010056 | tf_op jit(solution)/shard_map/ppermute | solution.py:252
  40.7 28.7 %all-to-all-start.1 = ((bf16[8,16,3712]{2,1,0:T(8,128)(2,1)}), bf16[8,16,3712]{2,1,0:T(8,128)(2,1)S(1)}, u32[]{:S(2)}, u32[]{:S(2)}) async-start(bf16[8,16,3712]{2,1,0:T(8,128)(2,1)} %bitcast.9), calls=%async_computation.1 | async-start | bytes 1900544 | tf_op jit(solution)/shard_map/all_to_all | solution.py:277
  44.2 14.8 %collective-permute-start.2 = (bf16[16,3712]{1,0:T(8,128)(2,1)S(1)}, bf16[16,3712]{1,0:T(8,128)(2,1)S(1)}, u32[]{:S(2)}, u32[]{:S(2)}) collective-permute-start(bf16[16,3712]{1,0:T(8,128)(2,1)S(1)} %get-tuple-element.10), channel_id=1, source_target_pairs={{0,24},{1,25},{2,26},{3,27},{4,28},{5,29},{6,30},{7,31},{8,16},{9,... | collective-permute-start | bytes 356360 | tf_op jit(solution)/shard_map/ppermute | solution.py:271
  47.0 14.5 %collective-permute-start.3 = (bf16[16,3712]{1,0:T(8,128)(2,1)S(1)}, bf16[16,3712]{1,0:T(8,128)(2,1)S(1)}, u32[]{:S(2)}, u32[]{:S(2)}) collective-permute-start(bf16[16,3712]{1,0:T(8,128)(2,1)S(1)} %get-tuple-element.11), channel_id=1, source_target_pairs={{0,26},{1,27},{2,24},{3,25},{4,30},{5,31},{6,28},{7,29},{8,18},{9,... | collective-permute-start | bytes 356360 | tf_op jit(solution)/shard_map/ppermute | solution.py:271
  49.4 17.9 %collective-permute-start.4 = (bf16[16,3712]{1,0:T(8,128)(2,1)S(1)}, bf16[16,3712]{1,0:T(8,128)(2,1)S(1)}, u32[]{:S(2)}, u32[]{:S(2)}) collective-permute-start(bf16[16,3712]{1,0:T(8,128)(2,1)S(1)} %get-tuple-element.12), channel_id=1, source_target_pairs={{0,28},{1,29},{2,30},{3,31},{4,24},{5,25},{6,26},{7,27},{8,20},{9,... | collective-permute-start | bytes 356360 | tf_op jit(solution)/shard_map/ppermute | solution.py:271
  52.7 16.7 %collective-permute-start.5 = (bf16[16,3712]{1,0:T(8,128)(2,1)S(1)}, bf16[16,3712]{1,0:T(8,128)(2,1)S(1)}, u32[]{:S(2)}, u32[]{:S(2)}) collective-permute-start(bf16[16,3712]{1,0:T(8,128)(2,1)S(1)} %get-tuple-element.13), channel_id=1, source_target_pairs={{0,30},{1,31},{2,28},{3,29},{4,26},{5,27},{6,24},{7,25},{8,22},{9,... | collective-permute-start | bytes 356360 | tf_op jit(solution)/shard_map/ppermute | solution.py:271

commit v7 on v5

--- a/solution.py
+++ b/solution.py
@@ -135,17 +135,18 @@
         "prepare",
         pltpu.VMEM((tok_count, width + LANES), jnp.bfloat16),
         [pl.ANY] * 3,
-        (ids, weights, tokens),
+        tuple(pltpu.with_memory_space_constraint(x, pltpu.HBM) for x in (ids, weights, tokens)),
         [
             pltpu.VMEM(ids.shape, ids.dtype),
             pltpu.VMEM(weights.shape, weights.dtype),
             pltpu.SemaphoreType.DMA((3,)),
         ],
-        limit=60,
-    )
-
-
-def choose_kernel(places, capacity, chip, block, *refs):
+        limit=8,
+    )
+
+
+def choose_kernel(places, capacity, block, *refs):
+    chip = lax.axis_index("expert") >> 1
     refs = list(refs)
     first = refs.pop(0) if refs[-1].shape[0] == 2 * capacity else None
     tok_count = block.shape[0]
@@ -155,7 +156,7 @@
     code = jnp.zeros(slot.shape, jnp.float32)
     order = jnp.zeros(slot.shape, jnp.int32)
     for at, (steps, flip) in enumerate(places):
-        wanted = chip_at(chip[0], steps, flip)
+        wanted = chip_at(chip, steps, flip)
         column = jnp.sum(jnp.where(lane == wanted, notes, 0.0), axis=1, keepdims=True)
         code = jnp.where(slot >= at * capacity, column, code)
         order = jnp.where(slot >= at * capacity, slot + 1 - at * capacity, order)
@@ -169,9 +170,9 @@
             refs[at][...] = piece
 
 
-def choose(chip, block, capacity, places, first=None):
+def choose(block, capacity, places, first=None):
     out_shape = [jax.ShapeDtypeStruct((capacity, block.shape[1]), jnp.bfloat16) for _ in places]
-    operands = (chip, block)
+    operands = (block,)
     if first is not None:
         out_shape[-1] = jax.ShapeDtypeStruct((2 * capacity, block.shape[1]), jnp.bfloat16)
         operands = operands + (first,)
@@ -179,7 +180,7 @@
         functools.partial(choose_kernel, places, capacity),
         "choose",
         out_shape,
-        [pltpu.SMEM] + [None] * (len(operands) - 1),
+        [None] * len(operands),
         operands,
     )
 
@@ -209,12 +210,13 @@
     return (gate / (1.0 + jnp.exp(-gate)) * both[:, hidden:]).astype(jnp.bfloat16)
 
 
-def write_pieces(chip, slots, total, outs):
+def write_pieces(slots, total, outs):
+    chip = lax.axis_index("expert") >> 1
     width = total.shape[1]
     experts = 2 * len(RING)
     notes = slots[:, width:].astype(jnp.float32)
     lane = iota(notes.shape, 1)
-    mine = (lane >= experts) & (lane < 4 * experts) & ((lane & (experts - 1)) == chip[0])
+    mine = (lane >= experts) & (lane < 4 * experts) & ((lane & (experts - 1)) == chip)
     scale = jnp.sum(jnp.where(mine, notes, 0.0), axis=1, keepdims=True)
     start = 0
     for out in outs:
@@ -224,7 +226,7 @@
         start = stop
 
 
-def expert_kernel(chip, *refs):
+def expert_kernel(*refs):
     outs, (slots, total) = refs[-10:-2], refs[-2:]
     pieces, weights = refs[:-14], refs[-14:-10]
     start = 0
@@ -237,19 +239,20 @@
         both = jnp.dot(slots[:, :width], first[...], preferred_element_type=jnp.float32)
         term = jnp.dot(gated(both), second[...], preferred_element_type=jnp.float32)
         total[...] = term if half == 0 else total[...] + term
-    write_pieces(chip, slots, total, outs)
-
-
-def expert_pass(chip, pieces, near, far, capacity):
+    write_pieces(slots, total, outs)
+
+
+def expert_pass(pieces, near, far, capacity):
     full = pieces[0].shape[1]
     count = capacity * 2 * len(RING)
     return local_call(
         expert_kernel,
         "expert_pass",
         [jax.ShapeDtypeStruct((capacity, full), jnp.bfloat16)] * (2 * len(RING)),
-        [pltpu.SMEM] + [None] * (len(pieces) + 4),
-        (chip, *pieces, *near, *far),
+        [None] * (len(pieces) + 4),
+        (*pieces, *near, *far),
         [pltpu.VMEM((count, full), jnp.bfloat16), pltpu.VMEM((count, full - LANES), jnp.float32)],
+        limit=24,
         moved=2 * sum(w.size for w in (*near, *far)),
     )
 
@@ -306,27 +309,24 @@
     tok_count = tokens.shape[0]
     top_count = route_ids.shape[2]
     capacity = max(2, 2 * tok_count * top_count // experts)
-    chip = (lax.axis_index("expert") // 2).reshape(1).astype(jnp.int32)
     swap = [(i, i ^ 1) for i in range(devices)]
     w_in, w_out = w_gate_up[0], w_down[0]
     far_out = lax.ppermute(w_out, "expert", swap)
     far_in = lax.ppermute(w_in, "expert", swap)
     block = prepare(route_ids[0].T, route_weights[0].T, tokens)
     block1 = sent(block, sections, 0, 1, 0)
-    own0, other0, back0, back1 = choose(chip, block, capacity, ((0, 0), (0, 1), (3, 0), (3, 1)))
+    own0, other0, back0, back1 = choose(block, capacity, ((0, 0), (0, 1), (3, 0), (3, 1)))
     own3 = sent(back0, sections, 0, 3, 0)
     other3 = sent(back1, sections, 0, 3, 1)
     near = (loaded(after(w_in, back1)), loaded(after(w_out, back1)))
-    far_out = loaded(after(far_out, near))
-    block1 = after(block1, far_out)
-    own1, on0, on1, other = choose(chip, block1, capacity, ((0, 0), (1, 0), (1, 1), (0, 1)), other0)
+    block1 = after(block1, near)
+    own1, on0, on1, other = choose(block1, capacity, ((0, 0), (1, 0), (1, 1), (0, 1)), other0)
     own2 = sent(on0, sections, 0, 1, 0)
     other2 = sent(on1, sections, 0, 1, 1)
     other01 = sent(other, sections, 0, 0, 1)
-    far = (loaded(after(far_in, (own3, other3, other))), far_out)
-    places = ((2, 0), (2, 1), (1, 0), (3, 0), (3, 1), (0, 0), (0, 1), (1, 1))
-    pieces = (own2, other2, own1, own3, other3, own0, other01)
-    pieces = expert_pass(chip, pieces, near, far, capacity)
+    places = ((0, 0), (2, 0), (2, 1), (0, 1), (1, 1), (1, 0), (3, 0), (3, 1))
+    pieces = (own0, own2, other2, other01, own1, own3, other3)
+    pieces = expert_pass(pieces, near, (far_in, far_out), capacity)
     back = [
         sent(piece, sections, 1, -steps, flip) for piece, (steps, flip) in zip(pieces, places)
     ]

time: 67.3 us -> 58.6 us (0.87)
  waiting for transfers between devices: 17.1 us -> 7.83 us
  starting transfers between devices: 34.2 us -> 40.8 us
  Pallas kernels: 12.2 us -> 7.28 us
    ppermute x1, waiting for transfers between devices: 7.81 us -> 0.01 us  [by_ring(): far_out = lax.ppermute(w_out, 'expert', swap)]
    ppermute x14, starting transfers between devices: 33.7 us -> 40.2 us  [sent(): return lax.ppermute(shard, ('section', 'expert'), pairs)]
    pallas_call x9 -> x7, Pallas kernels: 12.2 us -> 7.28 us  [local_call(): pl.pallas_call(kernel, out_shape=out_shape, in_specs=[vmem if spec is Non...]
    ppermute x14, waiting for transfers between devices: 9.25 us -> 7.82 us  [sent(): return lax.ppermute(shard, ('section', 'expert'), pairs)]
  transfers between devices with their start and end apart: 16 -> 16, of which waited for: 6 -> 4; matrix products, arithmetic and copies ran while one was open for 0% -> 0% of each run, Pallas kernels for 12% -> 5%
where the time goes in v7:
time: 58.6 us; the launch traced here: 58 us
  starting transfers between devices  40.8 us (70%)
  waiting for transfers between devices  7.83 us (13%)
  Pallas kernels  7.28 us (12%)
  local copies, waits for them, and re-layouts  2.04 us (3%)
    ppermute x14, starting transfers between devices, sent(): return lax.ppermute(shard, ('section', 'expert'), pairs)  40.2 us
    ppermute x14, waiting for transfers between devices, sent(): return lax.ppermute(shard, ('section', 'expert'), pairs)  7.82 us
    pallas_call x7, Pallas kernels, local_call(): pl.pallas_call(kernel, out_shape=out_shape, in_specs=[vmem if spec is Non...  7.28 us
    unnamed x4, local copies, waits for them, and re-layouts  2.04 us
  transfers between devices with their start and end apart: 16, of which 4 were waited for; matrix products, arithmetic and copies ran while one was open for 0% of the time, Pallas kernels for 5%

profile of v7, /device:TPU:0, one launch (start us, length us, event | category | flops | bytes accessed | tf_op | source)
XLA Modules:
  0.0 58.0 jit_solution(15564647448127446080)
XLA Ops:
  0.0 0.5 collective-permute-start.6
  0.5 1.2 %prepare.1.block = bf16[32,3712]{1,0:T(8,128)(2,1)S(1)} custom-call(s32[2,32]{1,0:T(2,128)} %bitcast.15, f32[2,32]{1,0:T(2,128)} %bitcast.16, bf16[32,3584]{1,0:T(8,128)(2,1)} %bitcast.14), custom_call_target="tpu_custom_call" | custom-call | tf_op jit(solution)/shard_map/prepare/pallas_call | solution.py:84
  1.8 3.1 %collective-permute-start = (bf16[32,3712]{1,0:T(8,128)(2,1)S(1)}, bf16[32,3712]{1,0:T(8,128)(2,1)S(1)}, u32[]{:S(2)}, u32[]{:S(2)}) collective-permute-start(bf16[32,3712]{1,0:T(8,128)(2,1)S(1)} %prepare.1.block), channel_id=1, source_target_pairs={{0,4},{1,5},{2,6},{3,7},{4,12},{5,13},{6,14},{7,15},{8,0},{9,1},{1... | collective-permute-start | bytes 712712 | tf_op jit(solution)/shard_map/ppermute | solution.py:297
  5.2 1.1 %collective-permute-start.4 = (bf16[16,3712]{1,0:T(8,128)(2,1)S(1)}, bf16[16,3712]{1,0:T(8,128)(2,1)S(1)}, u32[]{:S(2)}, u32[]{:S(2)}) collective-permute-start(bf16[16,3712]{1,0:T(8,128)(2,1)S(1)} %get-tuple-element.34), channel_id=1, source_target_pairs={{0,8},{1,9},{2,10},{3,11},{4,0},{5,1},{6,2},{7,3},{8,12},{9,13},{1... | collective-permute-start | bytes 356360 | tf_op jit(solution)/shard_map/ppermute | solution.py:297
  6.3 3.0 %collective-permute-start.5 = (bf16[16,3712]{1,0:T(8,128)(2,1)S(1)}, bf16[16,3712]{1,0:T(8,128)(2,1)S(1)}, u32[]{:S(2)}, u32[]{:S(2)}) collective-permute-start(bf16[16,3712]{1,0:T(8,128)(2,1)S(1)} %get-tuple-element.25), channel_id=1, source_target_pairs={{0,10},{1,11},{2,8},{3,9},{4,2},{5,3},{6,0},{7,1},{8,14},{9,15},{1... | collective-permute-start | bytes 356360 | tf_op jit(solution)/shard_map/ppermute | solution.py:297
  9.3 2.0 %copy-done.1 = bf16[1,512,3584]{2,1,0:T(8,128)(2,1)S(1)} copy-done((bf16[1,512,3584]{2,1,0:T(8,128)(2,1)S(1)}, bf16[1,512,3584]{2,1,0:T(8,128)(2,1)}, u32[]{:S(2)}) %copy-start.1) | copy-done | bytes 3670040
  11.6 0.5 loaded.2.refs_7_
  12.5 1.6 %collective-permute-start.3 = (bf16[32,3712]{1,0:T(8,128)(2,1)S(1)}, bf16[32,3712]{1,0:T(8,128)(2,1)S(1)}, u32[]{:S(2)}, u32[]{:S(2)}) collective-permute-start(bf16[32,3712]{1,0:T(8,128)(2,1)S(1)} %get-tuple-element.32), channel_id=1, source_target_pairs={{0,2},{1,3},{2,0},{3,1},{4,6},{5,7},{6,4},{7,5},{8,10},{9,11},{10,... | collective-permute-start | bytes 712712 | tf_op jit(solution)/shard_map/ppermute | solution.py:297
  14.1 0.5 collective-permute-done.4.refs_5_
  14.6 5.4 %collective-permute-start.1 = (bf16[16,3712]{1,0:T(8,128)(2,1)S(1)}, bf16[16,3712]{1,0:T(8,128)(2,1)S(1)}, u32[]{:S(2)}, u32[]{:S(2)}) collective-permute-start(bf16[16,3712]{1,0:T(8,128)(2,1)S(1)} %get-tuple-element.30), channel_id=1, source_target_pairs={{0,4},{1,5},{2,6},{3,7},{4,12},{5,13},{6,14},{7,15},{8,0},{9,1},{1... | collective-permute-start | bytes 356360 | tf_op jit(solution)/shard_map/ppermute | solution.py:297
  19.9 3.3 %collective-permute-start.2 = (bf16[16,3712]{1,0:T(8,128)(2,1)S(1)}, bf16[16,3712]{1,0:T(8,128)(2,1)S(1)}, u32[]{:S(2)}, u32[]{:S(2)}) collective-permute-start(bf16[16,3712]{1,0:T(8,128)(2,1)S(1)} %get-tuple-element.31), channel_id=1, source_target_pairs={{0,6},{1,7},{2,4},{3,5},{4,14},{5,15},{6,12},{7,13},{8,2},{9,3},{1... | collective-permute-start | bytes 356360 | tf_op jit(solution)/shard_map/ppermute | solution.py:297
  23.3 3.3 %collective-permute-done.2.refs_2_ = bf16[16,3712]{1,0:T(8,128)(2,1)S(1)} collective-permute-done((bf16[16,3712]{1,0:T(8,128)(2,1)S(1)}, bf16[16,3712]{1,0:T(8,128)(2,1)S(1)}, u32[]{:S(2)}, u32[]{:S(2)}) %collective-permute-start.2) | collective-permute-done | bytes 118816 | tf_op jit(solution)/shard_map/ppermute | solution.py:297
  26.6 3.3 %expert_pass.1 = (bf16[16,3712]{1,0:T(8,128)(2,1)S(1)}, bf16[16,3712]{1,0:T(8,128)(2,1)S(1)}, bf16[16,3712]{1,0:T(8,128)(2,1)S(1)}, bf16[16,3712]{1,0:T(8,128)(2...) custom-call(bf16[16,3712]{1,0:T(8,128)(2,1)S(1)} %get-tuple-element., ...), custom_call_target="tpu_custom_call" | custom-call | bytes 22020096 | tf_op jit(solution)/shard_map/expert_pass/pallas_call | solution.py:84
  29.9 1.5 %collective-permute-start.8 = (bf16[16,3712]{1,0:T(8,128)(2,1)S(1)}, bf16[16,3712]{1,0:T(8,128)(2,1)S(1)}, u32[]{:S(2)}, u32[]{:S(2)}) collective-permute-start(bf16[16,3712]{1,0:T(8,128)(2,1)S(1)} %get-tuple-element.35), channel_id=1, source_target_pairs={{0,16},{1,17},{2,18},{3,19},{4,20},{5,21},{6,22},{7,23},{8,24},{9,... | collective-permute-start | bytes 356360 | tf_op jit(solution)/shard_map/ppermute | solution.py:297
  31.5 4.2 %collective-permute-start.9 = (bf16[16,3712]{1,0:T(8,128)(2,1)S(1)}, bf16[16,3712]{1,0:T(8,128)(2,1)S(1)}, u32[]{:S(2)}, u32[]{:S(2)}) collective-permute-start(bf16[16,3712]{1,0:T(8,128)(2,1)S(1)} %get-tuple-element.36), channel_id=1, source_target_pairs={{0,28},{1,29},{2,30},{3,31},{4,24},{5,25},{6,26},{7,27},{8,20},{9,... | collective-permute-start | bytes 356360 | tf_op jit(solution)/shard_map/ppermute | solution.py:297
  35.7 1.0 %collective-permute-start.10 = (bf16[16,3712]{1,0:T(8,128)(2,1)S(1)}, bf16[16,3712]{1,0:T(8,128)(2,1)S(1)}, u32[]{:S(2)}, u32[]{:S(2)}) collective-permute-start(bf16[16,3712]{1,0:T(8,128)(2,1)S(1)} %get-tuple-element.37), channel_id=1, source_target_pairs={{0,30},{1,31},{2,28},{3,29},{4,26},{5,27},{6,24},{7,25},{8,22},{9,... | collective-permute-start | bytes 356360 | tf_op jit(solution)/shard_map/ppermute | solution.py:297
  36.6 1.5 %collective-permute-start.11 = (bf16[16,3712]{1,0:T(8,128)(2,1)S(1)}, bf16[16,3712]{1,0:T(8,128)(2,1)S(1)}, u32[]{:S(2)}, u32[]{:S(2)}) collective-permute-start(bf16[16,3712]{1,0:T(8,128)(2,1)S(1)} %get-tuple-element.38), channel_id=1, source_target_pairs={{0,18},{1,19},{2,16},{3,17},{4,22},{5,23},{6,20},{7,21},{8,26},{9,... | collective-permute-start | bytes 356360 | tf_op jit(solution)/shard_map/ppermute | solution.py:297
  38.1 1.3 %collective-permute-start.12 = (bf16[16,3712]{1,0:T(8,128)(2,1)S(1)}, bf16[16,3712]{1,0:T(8,128)(2,1)S(1)}, u32[]{:S(2)}, u32[]{:S(2)}) collective-permute-start(bf16[16,3712]{1,0:T(8,128)(2,1)S(1)} %get-tuple-element.39), channel_id=1, source_target_pairs={{0,26},{1,27},{2,24},{3,25},{4,18},{5,19},{6,16},{7,17},{8,30},{9,... | collective-permute-start | bytes 356360 | tf_op jit(solution)/shard_map/ppermute | solution.py:297
  39.4 4.9 %collective-permute-start.13 = (bf16[16,3712]{1,0:T(8,128)(2,1)S(1)}, bf16[16,3712]{1,0:T(8,128)(2,1)S(1)}, u32[]{:S(2)}, u32[]{:S(2)}) collective-permute-start(bf16[16,3712]{1,0:T(8,128)(2,1)S(1)} %get-tuple-element.40), channel_id=1, source_target_pairs={{0,24},{1,25},{2,26},{3,27},{4,16},{5,17},{6,18},{7,19},{8,28},{9,... | collective-permute-start | bytes 356360 | tf_op jit(solution)/shard_map/ppermute | solution.py:297
  44.3 3.3 %collective-permute-start.14 = (bf16[16,3712]{1,0:T(8,128)(2,1)S(1)}, bf16[16,3712]{1,0:T(8,128)(2,1)S(1)}, u32[]{:S(2)}, u32[]{:S(2)}) collective-permute-start(bf16[16,3712]{1,0:T(8,128)(2,1)S(1)} %get-tuple-element.41), channel_id=1, source_target_pairs={{0,20},{1,21},{2,22},{3,23},{4,28},{5,29},{6,30},{7,31},{8,16},{9,... | collective-permute-start | bytes 356360 | tf_op jit(solution)/shard_map/ppermute | solution.py:297
  47.6 5.2 %collective-permute-start.15 = (bf16[16,3712]{1,0:T(8,128)(2,1)S(1)}, bf16[16,3712]{1,0:T(8,128)(2,1)S(1)}, u32[]{:S(2)}, u32[]{:S(2)}) collective-permute-start(bf16[16,3712]{1,0:T(8,128)(2,1)S(1)} %get-tuple-element.42), channel_id=1, source_target_pairs={{0,22},{1,23},{2,20},{3,21},{4,30},{5,31},{6,28},{7,29},{8,18},{9,... | collective-permute-start | bytes 356360 | tf_op jit(solution)/shard_map/ppermute | solution.py:297
  52.8 2.0 %collective-permute-done.14.refs_6_ = bf16[16,3712]{1,0:T(8,128)(2,1)S(1)} collective-permute-done((bf16[16,3712]{1,0:T(8,128)(2,1)S(1)}, bf16[16,3712]{1,0:T(8,128)(2,1)S(1)}, u32[]{:S(2)}, u32[]{:S(2)}) %collective-permute-start.14) | collective-permute-done | bytes 118816 | tf_op jit(solution)/shard_map/ppermute | solution.py:297
  54.9 2.0 %collective-permute-done.15.refs_7_ = bf16[16,3712]{1,0:T(8,128)(2,1)S(1)} collective-permute-done((bf16[16,3712]{1,0:T(8,128)(2,1)S(1)}, bf16[16,3712]{1,0:T(8,128)(2,1)S(1)}, u32[]{:S(2)}, u32[]{:S(2)}) %collective-permute-start.15) | collective-permute-done | bytes 118816 | tf_op jit(solution)/shard_map/ppermute | solution.py:297
  56.9 1.1 %combine.1 = bf16[32,3584]{1,0:T(8,128)(2,1)} custom-call(bf16[16,3712]{1,0:T(8,128)(2,1)S(1)} %collective-permute-done.8.refs_0_, bf16[16,3712]{1,0:T(8,128)(2,1)S(1)} %collective-permute-done.9.refs_1_, bf16[16,3712]{1,0:T(8,128)(2,1)S(1)} %collective-permute-done.10.refs_2_, bf16[16,3712]{1,0:T(8,128)(2,1)S(1)} %collective-permute-done.11.refs_3_, ...), custom_call_target="tpu_custom_call" | custom-call | tf_op jit(solution)/shard_map/combine/pallas_call | solution.py:84
  (19 shorter events, 1.2 us)
Async XLA Ops:
  0.0 11.6 %copy-start = (bf16[1,3584,1024]{2,1,0:T(8,128)(2,1)S(1)}, bf16[1,3584,1024]{2,1,0:T(8,128)(2,1)}, u32[]{:S(2)}) copy-start(bf16[1,3584,1024]{2,1,0:T(8,128)(2,1)} %param.8) | copy-start | bytes 22020100
  0.0 26.6 %collective-permute-start.6 = (bf16[3584,1024]{1,0:T(8,128)(2,1)}, bf16[3584,1024]{1,0:T(8,128)(2,1)S(1)}, u32[]{:S(2)}, u32[]{:S(2)}) collective-permute-start(bf16[3584,1024]{1,0:T(8,128)(2,1)} %bitcast.10), channel_id=1, source_target_pairs={{0,1},{1,0},{2,3},{3,2},{4,5},{5,4},{6,7},{7,6},{8,9},{9,8},{10,11... | collective-permute-start | bytes 22020104 | tf_op jit(solution)/shard_map/ppermute | solution.py:315
  0.5 26.1 %collective-permute-start.7 = (bf16[512,3584]{1,0:T(8,128)(2,1)}, bf16[512,3584]{1,0:T(8,128)(2,1)S(1)}, u32[]{:S(2)}, u32[]{:S(2)}) collective-permute-start(bf16[512,3584]{1,0:T(8,128)(2,1)} %bitcast.12), channel_id=1, source_target_pairs={{0,1},{1,0},{2,3},{3,2},{4,5},{5,4},{6,7},{7,6},{8,9},{9,8},{10,11... | collective-permute-start | bytes 11010056 | tf_op jit(solution)/shard_map/ppermute | solution.py:314
  1.8 10.3 %collective-permute-start = (bf16[32,3712]{1,0:T(8,128)(2,1)S(1)}, bf16[32,3712]{1,0:T(8,128)(2,1)S(1)}, u32[]{:S(2)}, u32[]{:S(2)}) collective-permute-start(bf16[32,3712]{1,0:T(8,128)(2,1)S(1)} %prepare.1.block), channel_id=1, source_target_pairs={{0,4},{1,5},{2,6},{3,7},{4,12},{5,13},{6,14},{7,15},{8,0},{9,1},{1... | collective-permute-start | bytes 712712 | tf_op jit(solution)/shard_map/ppermute | solution.py:297
  5.2 9.3 %collective-permute-start.4 = (bf16[16,3712]{1,0:T(8,128)(2,1)S(1)}, bf16[16,3712]{1,0:T(8,128)(2,1)S(1)}, u32[]{:S(2)}, u32[]{:S(2)}) collective-permute-start(bf16[16,3712]{1,0:T(8,128)(2,1)S(1)} %get-tuple-element.34), channel_id=1, source_target_pairs={{0,8},{1,9},{2,10},{3,11},{4,0},{5,1},{6,2},{7,3},{8,12},{9,13},{1... | collective-permute-start | bytes 356360 | tf_op jit(solution)/shard_map/ppermute | solution.py:297
  6.3 13.6 %collective-permute-start.5 = (bf16[16,3712]{1,0:T(8,128)(2,1)S(1)}, bf16[16,3712]{1,0:T(8,128)(2,1)S(1)}, u32[]{:S(2)}, u32[]{:S(2)}) collective-permute-start(bf16[16,3712]{1,0:T(8,128)(2,1)S(1)} %get-tuple-element.25), channel_id=1, source_target_pairs={{0,10},{1,11},{2,8},{3,9},{4,2},{5,3},{6,0},{7,1},{8,14},{9,15},{1... | collective-permute-start | bytes 356360 | tf_op jit(solution)/shard_map/ppermute | solution.py:297
  9.3 2.0 %copy-start.1 = (bf16[1,512,3584]{2,1,0:T(8,128)(2,1)S(1)}, bf16[1,512,3584]{2,1,0:T(8,128)(2,1)}, u32[]{:S(2)}) copy-start(bf16[1,512,3584]{2,1,0:T(8,128)(2,1)} %param.9) | copy-start | bytes 11010052
  12.5 14.0 %collective-permute-start.3 = (bf16[32,3712]{1,0:T(8,128)(2,1)S(1)}, bf16[32,3712]{1,0:T(8,128)(2,1)S(1)}, u32[]{:S(2)}, u32[]{:S(2)}) collective-permute-start(bf16[32,3712]{1,0:T(8,128)(2,1)S(1)} %get-tuple-element.32), channel_id=1, source_target_pairs={{0,2},{1,3},{2,0},{3,1},{4,6},{5,7},{6,4},{7,5},{8,10},{9,11},{10,... | collective-permute-start | bytes 712712 | tf_op jit(solution)/shard_map/ppermute | solution.py:297
  14.6 8.7 %collective-permute-start.1 = (bf16[16,3712]{1,0:T(8,128)(2,1)S(1)}, bf16[16,3712]{1,0:T(8,128)(2,1)S(1)}, u32[]{:S(2)}, u32[]{:S(2)}) collective-permute-start(bf16[16,3712]{1,0:T(8,128)(2,1)S(1)} %get-tuple-element.30), channel_id=1, source_target_pairs={{0,4},{1,5},{2,6},{3,7},{4,12},{5,13},{6,14},{7,15},{8,0},{9,1},{1... | collective-permute-start | bytes 356360 | tf_op jit(solution)/shard_map/ppermute | solution.py:297
  19.9 6.6 %collective-permute-start.2 = (bf16[16,3712]{1,0:T(8,128)(2,1)S(1)}, bf16[16,3712]{1,0:T(8,128)(2,1)S(1)}, u32[]{:S(2)}, u32[]{:S(2)}) collective-permute-start(bf16[16,3712]{1,0:T(8,128)(2,1)S(1)} %get-tuple-element.31), channel_id=1, source_target_pairs={{0,6},{1,7},{2,4},{3,5},{4,14},{5,15},{6,12},{7,13},{8,2},{9,3},{1... | collective-permute-start | bytes 356360 | tf_op jit(solution)/shard_map/ppermute | solution.py:297
  29.9 9.5 %collective-permute-start.8 = (bf16[16,3712]{1,0:T(8,128)(2,1)S(1)}, bf16[16,3712]{1,0:T(8,128)(2,1)S(1)}, u32[]{:S(2)}, u32[]{:S(2)}) collective-permute-start(bf16[16,3712]{1,0:T(8,128)(2,1)S(1)} %get-tuple-element.35), channel_id=1, source_target_pairs={{0,16},{1,17},{2,18},{3,19},{4,20},{5,21},{6,22},{7,23},{8,24},{9,... | collective-permute-start | bytes 356360 | tf_op jit(solution)/shard_map/ppermute | solution.py:297
  31.5 12.8 %collective-permute-start.9 = (bf16[16,3712]{1,0:T(8,128)(2,1)S(1)}, bf16[16,3712]{1,0:T(8,128)(2,1)S(1)}, u32[]{:S(2)}, u32[]{:S(2)}) collective-permute-start(bf16[16,3712]{1,0:T(8,128)(2,1)S(1)} %get-tuple-element.36), channel_id=1, source_target_pairs={{0,28},{1,29},{2,30},{3,31},{4,24},{5,25},{6,26},{7,27},{8,20},{9,... | collective-permute-start | bytes 356360 | tf_op jit(solution)/shard_map/ppermute | solution.py:297
  35.7 11.9 %collective-permute-start.10 = (bf16[16,3712]{1,0:T(8,128)(2,1)S(1)}, bf16[16,3712]{1,0:T(8,128)(2,1)S(1)}, u32[]{:S(2)}, u32[]{:S(2)}) collective-permute-start(bf16[16,3712]{1,0:T(8,128)(2,1)S(1)} %get-tuple-element.37), channel_id=1, source_target_pairs={{0,30},{1,31},{2,28},{3,29},{4,26},{5,27},{6,24},{7,25},{8,22},{9,... | collective-permute-start | bytes 356360 | tf_op jit(solution)/shard_map/ppermute | solution.py:297
  36.6 16.2 %collective-permute-start.11 = (bf16[16,3712]{1,0:T(8,128)(2,1)S(1)}, bf16[16,3712]{1,0:T(8,128)(2,1)S(1)}, u32[]{:S(2)}, u32[]{:S(2)}) collective-permute-start(bf16[16,3712]{1,0:T(8,128)(2,1)S(1)} %get-tuple-element.38), channel_id=1, source_target_pairs={{0,18},{1,19},{2,16},{3,17},{4,22},{5,23},{6,20},{7,21},{8,26},{9,... | collective-permute-start | bytes 356360 | tf_op jit(solution)/shard_map/ppermute | solution.py:297
  38.1 14.7 %collective-permute-start.12 = (bf16[16,3712]{1,0:T(8,128)(2,1)S(1)}, bf16[16,3712]{1,0:T(8,128)(2,1)S(1)}, u32[]{:S(2)}, u32[]{:S(2)}) collective-permute-start(bf16[16,3712]{1,0:T(8,128)(2,1)S(1)} %get-tuple-element.39), channel_id=1, source_target_pairs={{0,26},{1,27},{2,24},{3,25},{4,18},{5,19},{6,16},{7,17},{8,30},{9,... | collective-permute-start | bytes 356360 | tf_op jit(solution)/shard_map/ppermute | solution.py:297
  39.4 13.4 %collective-permute-start.13 = (bf16[16,3712]{1,0:T(8,128)(2,1)S(1)}, bf16[16,3712]{1,0:T(8,128)(2,1)S(1)}, u32[]{:S(2)}, u32[]{:S(2)}) collective-permute-start(bf16[16,3712]{1,0:T(8,128)(2,1)S(1)} %get-tuple-element.40), channel_id=1, source_target_pairs={{0,24},{1,25},{2,26},{3,27},{4,16},{5,17},{6,18},{7,19},{8,28},{9,... | collective-permute-start | bytes 356360 | tf_op jit(solution)/shard_map/ppermute | solution.py:297
  44.3 10.6 %collective-permute-start.14 = (bf16[16,3712]{1,0:T(8,128)(2,1)S(1)}, bf16[16,3712]{1,0:T(8,128)(2,1)S(1)}, u32[]{:S(2)}, u32[]{:S(2)}) collective-permute-start(bf16[16,3712]{1,0:T(8,128)(2,1)S(1)} %get-tuple-element.41), channel_id=1, source_target_pairs={{0,20},{1,21},{2,22},{3,23},{4,28},{5,29},{6,30},{7,31},{8,16},{9,... | collective-permute-start | bytes 356360 | tf_op jit(solution)/shard_map/ppermute | solution.py:297
  47.6 9.3 %collective-permute-start.15 = (bf16[16,3712]{1,0:T(8,128)(2,1)S(1)}, bf16[16,3712]{1,0:T(8,128)(2,1)S(1)}, u32[]{:S(2)}, u32[]{:S(2)}) collective-permute-start(bf16[16,3712]{1,0:T(8,128)(2,1)S(1)} %get-tuple-element.42), channel_id=1, source_target_pairs={{0,22},{1,23},{2,20},{3,21},{4,30},{5,31},{6,28},{7,29},{8,18},{9,... | collective-permute-start | bytes 356360 | tf_op jit(solution)/shard_map/ppermute | solution.py:297

commit v8 on v7

--- a/solution.py
+++ b/solution.py
@@ -257,8 +257,8 @@
     )
 
 
-def combine_kernel(*refs):
-    blocks, out, slots = refs[:-2], refs[-2], refs[-1]
+def combine_kernel(count, *refs):
+    blocks, more, (out, slots) = refs[:count], refs[count:-2], refs[-2:]
     tok_count, width = out.shape
     start = 0
     for block in blocks:
@@ -268,18 +268,20 @@
     part = width // 7
     for at in range(7):
         place = slice(at * part, (at + 1) * part)
-        mixed = across(token, slots[:, place])
-        out[:, place] = mixed[TOKEN_LANE : TOKEN_LANE + tok_count].astype(out.dtype)
-
-
-def combine(blocks, tok_count):
+        mixed = across(token, slots[:, place])[TOKEN_LANE : TOKEN_LANE + tok_count]
+        for other in more:
+            mixed = mixed + other[:, place].astype(jnp.float32)
+        out[:, place] = mixed.astype(out.dtype)
+
+
+def combine(blocks, tok_count, *more):
     capacity, full = blocks[0].shape
     return local_call(
-        combine_kernel,
+        functools.partial(combine_kernel, len(blocks)),
         "combine",
         jax.ShapeDtypeStruct((tok_count, full - LANES), jnp.bfloat16),
-        [None] * len(blocks),
-        tuple(blocks),
+        [None] * (len(blocks) + len(more)),
+        (*blocks, *more),
         [pltpu.VMEM((capacity * len(blocks), full), jnp.bfloat16)],
     )
 
@@ -316,21 +318,26 @@
     block = prepare(route_ids[0].T, route_weights[0].T, tokens)
     block1 = sent(block, sections, 0, 1, 0)
     own0, other0, back0, back1 = choose(block, capacity, ((0, 0), (0, 1), (3, 0), (3, 1)))
+    near = (loaded(after(w_in, block)), loaded(after(w_out, block)))
+    back0, back1 = after((back0, back1), near)
     own3 = sent(back0, sections, 0, 3, 0)
     other3 = sent(back1, sections, 0, 3, 1)
-    near = (loaded(after(w_in, back1)), loaded(after(w_out, back1)))
     block1 = after(block1, near)
     own1, on0, on1, other = choose(block1, capacity, ((0, 0), (1, 0), (1, 1), (0, 1)), other0)
     own2 = sent(on0, sections, 0, 1, 0)
     other2 = sent(on1, sections, 0, 1, 1)
     other01 = sent(other, sections, 0, 0, 1)
-    places = ((0, 0), (2, 0), (2, 1), (0, 1), (1, 1), (1, 0), (3, 0), (3, 1))
-    pieces = (own0, own2, other2, other01, own1, own3, other3)
-    pieces = expert_pass(pieces, near, (far_in, far_out), capacity)
-    back = [
-        sent(piece, sections, 1, -steps, flip) for piece, (steps, flip) in zip(pieces, places)
-    ]
-    return combine(back, tok_count)[None]
+    slots = (own0, own1, own3, other3, other01, own2, other2)
+    places = ((0, 0), (1, 0), (3, 0), (3, 1), (0, 1), (1, 1), (2, 0), (2, 1))
+    pieces = dict(zip(places, expert_pass(slots, near, (far_in, far_out), capacity)))
+    here, straight = [pieces[0, 0]], []
+    for steps, flip in ((1, 0), (1, 1), (3, 0), (3, 1), (0, 1)):
+        here.append(sent(pieces[steps, flip], sections, 0, -steps, flip))
+    for flip in range(2):
+        straight.append(sent(pieces[2, flip], sections, 1, -2, flip))
+    here = after(here, straight[0])
+    most = sent(combine(here, tok_count), sections, 1, 0, 0)
+    return combine(straight, tok_count, most)[None]
 
 
 def per_device(rows, route_ids, route_weights, w_gate_up, w_down):

time: 58.6 us -> 59.6 us (1.017)
  waiting for transfers between devices: 7.83 us -> 14.6 us
  starting transfers between devices: 40.8 us -> 35 us
    ppermute x14, waiting for transfers between devices: 7.82 us -> 14.6 us  [sent(): return lax.ppermute(shard, ('section', 'expert'), pairs)]
    ppermute x14, starting transfers between devices: 40.2 us -> 34.5 us  [sent(): return lax.ppermute(shard, ('section', 'expert'), pairs)]
    pallas_call x7 -> x8, Pallas kernels: 7.28 us -> 7.68 us  [local_call(): pl.pallas_call(kernel, out_shape=out_shape, in_specs=[vmem if spec is Non...]
  transfers between devices with their start and end apart: 16 -> 16, of which waited for: 4 -> 7; matrix products, arithmetic and copies ran while one was open for 0% -> 0% of each run, Pallas kernels for 5% -> 5%
where the time goes in v8:
time: 59.6 us; the launch traced here: 59.4 us
  starting transfers between devices  35 us (59%)
  waiting for transfers between devices  14.6 us (24%)
  Pallas kernels  7.68 us (13%)
  local copies, waits for them, and re-layouts  2.04 us (3%)
    ppermute x14, starting transfers between devices, sent(): return lax.ppermute(shard, ('section', 'expert'), pairs)  34.5 us
    ppermute x14, waiting for transfers between devices, sent(): return lax.ppermute(shard, ('section', 'expert'), pairs)  14.6 us
    pallas_call x8, Pallas kernels, local_call(): pl.pallas_call(kernel, out_shape=out_shape, in_specs=[vmem if spec is Non...  7.68 us
    unnamed x4, local copies, waits for them, and re-layouts  2.04 us
  transfers between devices with their start and end apart: 16, of which 7 were waited for; matrix products, arithmetic and copies ran while one was open for 0% of the time, Pallas kernels for 5%

profile of v8, /device:TPU:0, one launch (start us, length us, event | category | flops | bytes accessed | tf_op | source)
XLA Modules:
  0.0 59.4 jit_solution(18309307016642002273)
XLA Ops:
  0.0 0.5 collective-permute-start.6
  0.5 1.2 %prepare.1.block = bf16[32,3712]{1,0:T(8,128)(2,1)S(1)} custom-call(s32[2,32]{1,0:T(2,128)} %bitcast.15, f32[2,32]{1,0:T(2,128)} %bitcast.16, bf16[32,3584]{1,0:T(8,128)(2,1)} %bitcast.14), custom_call_target="tpu_custom_call" | custom-call | tf_op jit(solution)/shard_map/prepare/pallas_call | solution.py:84
  1.8 3.1 %collective-permute-start = (bf16[32,3712]{1,0:T(8,128)(2,1)S(1)}, bf16[32,3712]{1,0:T(8,128)(2,1)S(1)}, u32[]{:S(2)}, u32[]{:S(2)}) collective-permute-start(bf16[32,3712]{1,0:T(8,128)(2,1)S(1)} %prepare.1.block), channel_id=1, source_target_pairs={{0,4},{1,5},{2,6},{3,7},{4,12},{5,13},{6,14},{7,15},{8,0},{9,1},{1... | collective-permute-start | bytes 712712 | tf_op jit(solution)/shard_map/ppermute | solution.py:299
  5.3 2.0 %copy-done.1 = bf16[1,512,3584]{2,1,0:T(8,128)(2,1)S(1)} copy-done((bf16[1,512,3584]{2,1,0:T(8,128)(2,1)S(1)}, bf16[1,512,3584]{2,1,0:T(8,128)(2,1)}, u32[]{:S(2)}) %copy-start.1) | copy-done | bytes 3670040
  7.6 0.5 loaded.2.refs_7_
  8.1 1.1 %collective-permute-start.1 = (bf16[16,3712]{1,0:T(8,128)(2,1)S(1)}, bf16[16,3712]{1,0:T(8,128)(2,1)S(1)}, u32[]{:S(2)}, u32[]{:S(2)}) collective-permute-start(bf16[16,3712]{1,0:T(8,128)(2,1)S(1)} %get-tuple-element.40), channel_id=1, source_target_pairs={{0,8},{1,9},{2,10},{3,11},{4,0},{5,1},{6,2},{7,3},{8,12},{9,13},{1... | collective-permute-start | bytes 356360 | tf_op jit(solution)/shard_map/ppermute | solution.py:299
  9.2 3.0 %collective-permute-start.2 = (bf16[16,3712]{1,0:T(8,128)(2,1)S(1)}, bf16[16,3712]{1,0:T(8,128)(2,1)S(1)}, u32[]{:S(2)}, u32[]{:S(2)}) collective-permute-start(bf16[16,3712]{1,0:T(8,128)(2,1)S(1)} %get-tuple-element.41), channel_id=1, source_target_pairs={{0,10},{1,11},{2,8},{3,9},{4,2},{5,3},{6,0},{7,1},{8,14},{9,15},{1... | collective-permute-start | bytes 356360 | tf_op jit(solution)/shard_map/ppermute | solution.py:299
  12.5 1.5 %collective-permute-start.3 = (bf16[32,3712]{1,0:T(8,128)(2,1)S(1)}, bf16[32,3712]{1,0:T(8,128)(2,1)S(1)}, u32[]{:S(2)}, u32[]{:S(2)}) collective-permute-start(bf16[32,3712]{1,0:T(8,128)(2,1)S(1)} %get-tuple-element.42), channel_id=1, source_target_pairs={{0,2},{1,3},{2,0},{3,1},{4,6},{5,7},{6,4},{7,5},{8,10},{9,11},{10,... | collective-permute-start | bytes 712712 | tf_op jit(solution)/shard_map/ppermute | solution.py:299
  14.1 0.7 %collective-permute-done.1.refs_2_ = bf16[16,3712]{1,0:T(8,128)(2,1)S(1)} collective-permute-done((bf16[16,3712]{1,0:T(8,128)(2,1)S(1)}, bf16[16,3712]{1,0:T(8,128)(2,1)S(1)}, u32[]{:S(2)}, u32[]{:S(2)}) %collective-permute-start.1) | collective-permute-done | bytes 118816 | tf_op jit(solution)/shard_map/ppermute | solution.py:299
  14.8 5.1 %collective-permute-start.4 = (bf16[16,3712]{1,0:T(8,128)(2,1)S(1)}, bf16[16,3712]{1,0:T(8,128)(2,1)S(1)}, u32[]{:S(2)}, u32[]{:S(2)}) collective-permute-start(bf16[16,3712]{1,0:T(8,128)(2,1)S(1)} %get-tuple-element.43), channel_id=1, source_target_pairs={{0,4},{1,5},{2,6},{3,7},{4,12},{5,13},{6,14},{7,15},{8,0},{9,1},{1... | collective-permute-start | bytes 356360 | tf_op jit(solution)/shard_map/ppermute | solution.py:299
  19.9 3.3 %collective-permute-start.5 = (bf16[16,3712]{1,0:T(8,128)(2,1)S(1)}, bf16[16,3712]{1,0:T(8,128)(2,1)S(1)}, u32[]{:S(2)}, u32[]{:S(2)}) collective-permute-start(bf16[16,3712]{1,0:T(8,128)(2,1)S(1)} %get-tuple-element.44), channel_id=1, source_target_pairs={{0,6},{1,7},{2,4},{3,5},{4,14},{5,15},{6,12},{7,13},{8,2},{9,3},{1... | collective-permute-start | bytes 356360 | tf_op jit(solution)/shard_map/ppermute | solution.py:299
  23.2 3.3 %collective-permute-done.5.refs_6_ = bf16[16,3712]{1,0:T(8,128)(2,1)S(1)} collective-permute-done((bf16[16,3712]{1,0:T(8,128)(2,1)S(1)}, bf16[16,3712]{1,0:T(8,128)(2,1)S(1)}, u32[]{:S(2)}, u32[]{:S(2)}) %collective-permute-start.5) | collective-permute-done | bytes 118816 | tf_op jit(solution)/shard_map/ppermute | solution.py:299
  26.5 3.3 %expert_pass.1 = (bf16[16,3712]{1,0:T(8,128)(2,1)S(1)}, bf16[16,3712]{1,0:T(8,128)(2,1)S(1)}, bf16[16,3712]{1,0:T(8,128)(2,1)S(1)}, bf16[16,3712]{1,0:T(8,128)(2...) custom-call(bf16[16,3712]{1,0:T(8,128)(2,1)S(1)} %get-tuple-element., ...), custom_call_target="tpu_custom_call" | custom-call | bytes 22020096 | tf_op jit(solution)/shard_map/expert_pass/pallas_call | solution.py:84
  29.9 5.2 %collective-permute-start.8 = (bf16[16,3712]{1,0:T(8,128)(2,1)S(1)}, bf16[16,3712]{1,0:T(8,128)(2,1)S(1)}, u32[]{:S(2)}, u32[]{:S(2)}) collective-permute-start(bf16[16,3712]{1,0:T(8,128)(2,1)S(1)} %get-tuple-element.45), channel_id=1, source_target_pairs={{0,28},{1,29},{2,30},{3,31},{4,24},{5,25},{6,26},{7,27},{8,20},{9,... | collective-permute-start | bytes 356360 | tf_op jit(solution)/shard_map/ppermute | solution.py:299
  35.0 0.7 %collective-permute-start.11 = (bf16[16,3712]{1,0:T(8,128)(2,1)S(1)}, bf16[16,3712]{1,0:T(8,128)(2,1)S(1)}, u32[]{:S(2)}, u32[]{:S(2)}) collective-permute-start(bf16[16,3712]{1,0:T(8,128)(2,1)S(1)} %get-tuple-element.49), channel_id=1, source_target_pairs={{0,10},{1,11},{2,8},{3,9},{4,2},{5,3},{6,0},{7,1},{8,14},{9,15},{1... | collective-permute-start | bytes 356360 | tf_op jit(solution)/shard_map/ppermute | solution.py:299
  35.7 2.3 %collective-permute-start.12 = (bf16[16,3712]{1,0:T(8,128)(2,1)S(1)}, bf16[16,3712]{1,0:T(8,128)(2,1)S(1)}, u32[]{:S(2)}, u32[]{:S(2)}) collective-permute-start(bf16[16,3712]{1,0:T(8,128)(2,1)S(1)} %get-tuple-element.50), channel_id=1, source_target_pairs={{0,4},{1,5},{2,6},{3,7},{4,12},{5,13},{6,14},{7,15},{8,0},{9,1},{1... | collective-permute-start | bytes 356360 | tf_op jit(solution)/shard_map/ppermute | solution.py:299
  38.0 2.9 %collective-permute-start.13 = (bf16[16,3712]{1,0:T(8,128)(2,1)S(1)}, bf16[16,3712]{1,0:T(8,128)(2,1)S(1)}, u32[]{:S(2)}, u32[]{:S(2)}) collective-permute-start(bf16[16,3712]{1,0:T(8,128)(2,1)S(1)} %get-tuple-element.51), channel_id=1, source_target_pairs={{0,6},{1,7},{2,4},{3,5},{4,14},{5,15},{6,12},{7,13},{8,2},{9,3},{1... | collective-permute-start | bytes 356360 | tf_op jit(solution)/shard_map/ppermute | solution.py:299
  40.9 1.5 %collective-permute-start.14 = (bf16[16,3712]{1,0:T(8,128)(2,1)S(1)}, bf16[16,3712]{1,0:T(8,128)(2,1)S(1)}, u32[]{:S(2)}, u32[]{:S(2)}) collective-permute-start(bf16[16,3712]{1,0:T(8,128)(2,1)S(1)} %get-tuple-element.52), channel_id=1, source_target_pairs={{0,2},{1,3},{2,0},{3,1},{4,6},{5,7},{6,4},{7,5},{8,10},{9,11},{10,... | collective-permute-start | bytes 356360 | tf_op jit(solution)/shard_map/ppermute | solution.py:299
  42.8 3.6 %collective-permute-done.12.refs_3_ = bf16[16,3712]{1,0:T(8,128)(2,1)S(1)} collective-permute-done((bf16[16,3712]{1,0:T(8,128)(2,1)S(1)}, bf16[16,3712]{1,0:T(8,128)(2,1)S(1)}, u32[]{:S(2)}, u32[]{:S(2)}) %collective-permute-start.12) | collective-permute-done | bytes 118816 | tf_op jit(solution)/shard_map/ppermute | solution.py:299
  46.4 1.9 %collective-permute-done.13.refs_4_ = bf16[16,3712]{1,0:T(8,128)(2,1)S(1)} collective-permute-done((bf16[16,3712]{1,0:T(8,128)(2,1)S(1)}, bf16[16,3712]{1,0:T(8,128)(2,1)S(1)}, u32[]{:S(2)}, u32[]{:S(2)}) %collective-permute-start.13) | collective-permute-done | bytes 118816 | tf_op jit(solution)/shard_map/ppermute | solution.py:299
  48.8 0.6 %collective-permute-start.15 = (bf16[32,3584]{1,0:T(8,128)(2,1)S(1)}, bf16[32,3584]{1,0:T(8,128)(2,1)S(1)}, u32[]{:S(2)}, u32[]{:S(2)}) collective-permute-start(bf16[32,3584]{1,0:T(8,128)(2,1)S(1)} %combine.2), channel_id=1, source_target_pairs={{0,16},{1,17},{2,18},{3,19},{4,20},{5,21},{6,22},{7,23},{8,24},{9,... | collective-permute-start | bytes 688136 | tf_op jit(solution)/shard_map/ppermute | solution.py:299
  49.4 4.3 %collective-permute-start.9 = (bf16[16,3712]{1,0:T(8,128)(2,1)S(1)}, bf16[16,3712]{1,0:T(8,128)(2,1)S(1)}, u32[]{:S(2)}, u32[]{:S(2)}) collective-permute-start(bf16[16,3712]{1,0:T(8,128)(2,1)S(1)} %get-tuple-element.46), channel_id=1, source_target_pairs={{0,30},{1,31},{2,28},{3,29},{4,26},{5,27},{6,24},{7,25},{8,22},{9,... | collective-permute-start | bytes 356360 | tf_op jit(solution)/shard_map/ppermute | solution.py:299
  53.7 4.2 %collective-permute-done.9.refs_1_ = bf16[16,3712]{1,0:T(8,128)(2,1)S(1)} collective-permute-done((bf16[16,3712]{1,0:T(8,128)(2,1)S(1)}, bf16[16,3712]{1,0:T(8,128)(2,1)S(1)}, u32[]{:S(2)}, u32[]{:S(2)}) %collective-permute-start.9) | collective-permute-done | bytes 118816 | tf_op jit(solution)/shard_map/ppermute | solution.py:299
  58.3 1.1 %combine.3 = bf16[32,3584]{1,0:T(8,128)(2,1)} custom-call(bf16[16,3712]{1,0:T(8,128)(2,1)S(1)} %collective-permute-done.8.refs_0_, bf16[16,3712]{1,0:T(8,128)(2,1)S(1)} %collective-permute-done.9.refs_1_, bf16[32,3584]{1,0:T(8,128)(2,1)S(1)} %collective-permute-done.15.refs_2_), custom_call_target="tpu_custom_call" | custom-call | tf_op jit(solution)/shard_map/combine/pallas_call | solution.py:84
  (20 shorter events, 2.3 us)
Async XLA Ops:
  0.0 7.6 %copy-start = (bf16[1,3584,1024]{2,1,0:T(8,128)(2,1)S(1)}, bf16[1,3584,1024]{2,1,0:T(8,128)(2,1)}, u32[]{:S(2)}) copy-start(bf16[1,3584,1024]{2,1,0:T(8,128)(2,1)} %param.8) | copy-start | bytes 22020100
  0.0 26.5 %collective-permute-start.6 = (bf16[3584,1024]{1,0:T(8,128)(2,1)}, bf16[3584,1024]{1,0:T(8,128)(2,1)S(1)}, u32[]{:S(2)}, u32[]{:S(2)}) collective-permute-start(bf16[3584,1024]{1,0:T(8,128)(2,1)} %bitcast.10), channel_id=1, source_target_pairs={{0,1},{1,0},{2,3},{3,2},{4,5},{5,4},{6,7},{7,6},{8,9},{9,8},{10,11... | collective-permute-start | bytes 22020104 | tf_op jit(solution)/shard_map/ppermute | solution.py:317
  0.5 26.1 %collective-permute-start.7 = (bf16[512,3584]{1,0:T(8,128)(2,1)}, bf16[512,3584]{1,0:T(8,128)(2,1)S(1)}, u32[]{:S(2)}, u32[]{:S(2)}) collective-permute-start(bf16[512,3584]{1,0:T(8,128)(2,1)} %bitcast.12), channel_id=1, source_target_pairs={{0,1},{1,0},{2,3},{3,2},{4,5},{5,4},{6,7},{7,6},{8,9},{9,8},{10,11... | collective-permute-start | bytes 11010056 | tf_op jit(solution)/shard_map/ppermute | solution.py:316
  1.8 10.4 %collective-permute-start = (bf16[32,3712]{1,0:T(8,128)(2,1)S(1)}, bf16[32,3712]{1,0:T(8,128)(2,1)S(1)}, u32[]{:S(2)}, u32[]{:S(2)}) collective-permute-start(bf16[32,3712]{1,0:T(8,128)(2,1)S(1)} %prepare.1.block), channel_id=1, source_target_pairs={{0,4},{1,5},{2,6},{3,7},{4,12},{5,13},{6,14},{7,15},{8,0},{9,1},{1... | collective-permute-start | bytes 712712 | tf_op jit(solution)/shard_map/ppermute | solution.py:299
  5.2 2.0 %copy-start.1 = (bf16[1,512,3584]{2,1,0:T(8,128)(2,1)S(1)}, bf16[1,512,3584]{2,1,0:T(8,128)(2,1)}, u32[]{:S(2)}) copy-start(bf16[1,512,3584]{2,1,0:T(8,128)(2,1)} %param.9) | copy-start | bytes 11010052
  8.1 6.7 %collective-permute-start.1 = (bf16[16,3712]{1,0:T(8,128)(2,1)S(1)}, bf16[16,3712]{1,0:T(8,128)(2,1)S(1)}, u32[]{:S(2)}, u32[]{:S(2)}) collective-permute-start(bf16[16,3712]{1,0:T(8,128)(2,1)S(1)} %get-tuple-element.40), channel_id=1, source_target_pairs={{0,8},{1,9},{2,10},{3,11},{4,0},{5,1},{6,2},{7,3},{8,12},{9,13},{1... | collective-permute-start | bytes 356360 | tf_op jit(solution)/shard_map/ppermute | solution.py:299
  9.2 10.7 %collective-permute-start.2 = (bf16[16,3712]{1,0:T(8,128)(2,1)S(1)}, bf16[16,3712]{1,0:T(8,128)(2,1)S(1)}, u32[]{:S(2)}, u32[]{:S(2)}) collective-permute-start(bf16[16,3712]{1,0:T(8,128)(2,1)S(1)} %get-tuple-element.41), channel_id=1, source_target_pairs={{0,10},{1,11},{2,8},{3,9},{4,2},{5,3},{6,0},{7,1},{8,14},{9,15},{1... | collective-permute-start | bytes 356360 | tf_op jit(solution)/shard_map/ppermute | solution.py:299
  12.5 14.0 %collective-permute-start.3 = (bf16[32,3712]{1,0:T(8,128)(2,1)S(1)}, bf16[32,3712]{1,0:T(8,128)(2,1)S(1)}, u32[]{:S(2)}, u32[]{:S(2)}) collective-permute-start(bf16[32,3712]{1,0:T(8,128)(2,1)S(1)} %get-tuple-element.42), channel_id=1, source_target_pairs={{0,2},{1,3},{2,0},{3,1},{4,6},{5,7},{6,4},{7,5},{8,10},{9,11},{10,... | collective-permute-start | bytes 712712 | tf_op jit(solution)/shard_map/ppermute | solution.py:299
  14.8 8.4 %collective-permute-start.4 = (bf16[16,3712]{1,0:T(8,128)(2,1)S(1)}, bf16[16,3712]{1,0:T(8,128)(2,1)S(1)}, u32[]{:S(2)}, u32[]{:S(2)}) collective-permute-start(bf16[16,3712]{1,0:T(8,128)(2,1)S(1)} %get-tuple-element.43), channel_id=1, source_target_pairs={{0,4},{1,5},{2,6},{3,7},{4,12},{5,13},{6,14},{7,15},{8,0},{9,1},{1... | collective-permute-start | bytes 356360 | tf_op jit(solution)/shard_map/ppermute | solution.py:299
  19.9 6.6 %collective-permute-start.5 = (bf16[16,3712]{1,0:T(8,128)(2,1)S(1)}, bf16[16,3712]{1,0:T(8,128)(2,1)S(1)}, u32[]{:S(2)}, u32[]{:S(2)}) collective-permute-start(bf16[16,3712]{1,0:T(8,128)(2,1)S(1)} %get-tuple-element.44), channel_id=1, source_target_pairs={{0,6},{1,7},{2,4},{3,5},{4,14},{5,15},{6,12},{7,13},{8,2},{9,3},{1... | collective-permute-start | bytes 356360 | tf_op jit(solution)/shard_map/ppermute | solution.py:299
  29.9 11.0 %collective-permute-start.8 = (bf16[16,3712]{1,0:T(8,128)(2,1)S(1)}, bf16[16,3712]{1,0:T(8,128)(2,1)S(1)}, u32[]{:S(2)}, u32[]{:S(2)}) collective-permute-start(bf16[16,3712]{1,0:T(8,128)(2,1)S(1)} %get-tuple-element.45), channel_id=1, source_target_pairs={{0,28},{1,29},{2,30},{3,31},{4,24},{5,25},{6,26},{7,27},{8,20},{9,... | collective-permute-start | bytes 356360 | tf_op jit(solution)/shard_map/ppermute | solution.py:299
  35.0 7.4 %collective-permute-start.10 = (bf16[16,3712]{1,0:T(8,128)(2,1)S(1)}, bf16[16,3712]{1,0:T(8,128)(2,1)S(1)}, u32[]{:S(2)}, u32[]{:S(2)}) collective-permute-start(bf16[16,3712]{1,0:T(8,128)(2,1)S(1)} %get-tuple-element.48), channel_id=1, source_target_pairs={{0,8},{1,9},{2,10},{3,11},{4,0},{5,1},{6,2},{7,3},{8,12},{9,13},{1... | collective-permute-start | bytes 356360 | tf_op jit(solution)/shard_map/ppermute | solution.py:299
  35.0 7.7 %collective-permute-start.11 = (bf16[16,3712]{1,0:T(8,128)(2,1)S(1)}, bf16[16,3712]{1,0:T(8,128)(2,1)S(1)}, u32[]{:S(2)}, u32[]{:S(2)}) collective-permute-start(bf16[16,3712]{1,0:T(8,128)(2,1)S(1)} %get-tuple-element.49), channel_id=1, source_target_pairs={{0,10},{1,11},{2,8},{3,9},{4,2},{5,3},{6,0},{7,1},{8,14},{9,15},{1... | collective-permute-start | bytes 356360 | tf_op jit(solution)/shard_map/ppermute | solution.py:299
  35.7 10.7 %collective-permute-start.12 = (bf16[16,3712]{1,0:T(8,128)(2,1)S(1)}, bf16[16,3712]{1,0:T(8,128)(2,1)S(1)}, u32[]{:S(2)}, u32[]{:S(2)}) collective-permute-start(bf16[16,3712]{1,0:T(8,128)(2,1)S(1)} %get-tuple-element.50), channel_id=1, source_target_pairs={{0,4},{1,5},{2,6},{3,7},{4,12},{5,13},{6,14},{7,15},{8,0},{9,1},{1... | collective-permute-start | bytes 356360 | tf_op jit(solution)/shard_map/ppermute | solution.py:299
  38.0 10.3 %collective-permute-start.13 = (bf16[16,3712]{1,0:T(8,128)(2,1)S(1)}, bf16[16,3712]{1,0:T(8,128)(2,1)S(1)}, u32[]{:S(2)}, u32[]{:S(2)}) collective-permute-start(bf16[16,3712]{1,0:T(8,128)(2,1)S(1)} %get-tuple-element.51), channel_id=1, source_target_pairs={{0,6},{1,7},{2,4},{3,5},{4,14},{5,15},{6,12},{7,13},{8,2},{9,3},{1... | collective-permute-start | bytes 356360 | tf_op jit(solution)/shard_map/ppermute | solution.py:299
  40.9 7.5 %collective-permute-start.14 = (bf16[16,3712]{1,0:T(8,128)(2,1)S(1)}, bf16[16,3712]{1,0:T(8,128)(2,1)S(1)}, u32[]{:S(2)}, u32[]{:S(2)}) collective-permute-start(bf16[16,3712]{1,0:T(8,128)(2,1)S(1)} %get-tuple-element.52), channel_id=1, source_target_pairs={{0,2},{1,3},{2,0},{3,1},{4,6},{5,7},{6,4},{7,5},{8,10},{9,11},{10,... | collective-permute-start | bytes 356360 | tf_op jit(solution)/shard_map/ppermute | solution.py:299
  48.8 9.5 %collective-permute-start.15 = (bf16[32,3584]{1,0:T(8,128)(2,1)S(1)}, bf16[32,3584]{1,0:T(8,128)(2,1)S(1)}, u32[]{:S(2)}, u32[]{:S(2)}) collective-permute-start(bf16[32,3584]{1,0:T(8,128)(2,1)S(1)} %combine.2), channel_id=1, source_target_pairs={{0,16},{1,17},{2,18},{3,19},{4,20},{5,21},{6,22},{7,23},{8,24},{9,... | collective-permute-start | bytes 688136 | tf_op jit(solution)/shard_map/ppermute | solution.py:299
  49.4 8.5 %collective-permute-start.9 = (bf16[16,3712]{1,0:T(8,128)(2,1)S(1)}, bf16[16,3712]{1,0:T(8,128)(2,1)S(1)}, u32[]{:S(2)}, u32[]{:S(2)}) collective-permute-start(bf16[16,3712]{1,0:T(8,128)(2,1)S(1)} %get-tuple-element.46), channel_id=1, source_target_pairs={{0,30},{1,31},{2,28},{3,29},{4,26},{5,27},{6,24},{7,25},{8,22},{9,... | collective-permute-start | bytes 356360 | tf_op jit(solution)/shard_map/ppermute | solution.py:299

commit v9 on v7

--- a/solution.py
+++ b/solution.py
@@ -147,8 +147,6 @@
 
 def choose_kernel(places, capacity, block, *refs):
     chip = lax.axis_index("expert") >> 1
-    refs = list(refs)
-    first = refs.pop(0) if refs[-1].shape[0] == 2 * capacity else None
     tok_count = block.shape[0]
     notes = block[:, -LANES:].astype(jnp.float32)
     lane = iota(notes.shape, 1)
@@ -162,26 +160,16 @@
         order = jnp.where(slot >= at * capacity, slot + 1 - at * capacity, order)
     rows = across(ones_where(code == order.astype(jnp.float32)), block[...]).astype(jnp.bfloat16)
     for at in range(len(places)):
-        piece = rows[at * capacity : (at + 1) * capacity]
-        if first is not None and at == len(places) - 1:
-            refs[at][:capacity] = first[...]
-            refs[at][capacity:] = piece
-        else:
-            refs[at][...] = piece
-
-
-def choose(block, capacity, places, first=None):
-    out_shape = [jax.ShapeDtypeStruct((capacity, block.shape[1]), jnp.bfloat16) for _ in places]
-    operands = (block,)
-    if first is not None:
-        out_shape[-1] = jax.ShapeDtypeStruct((2 * capacity, block.shape[1]), jnp.bfloat16)
-        operands = operands + (first,)
+        refs[at][...] = rows[at * capacity : (at + 1) * capacity]
+
+
+def choose(block, capacity, places):
     return local_call(
         functools.partial(choose_kernel, places, capacity),
         "choose",
-        out_shape,
-        [None] * len(operands),
-        operands,
+        [jax.ShapeDtypeStruct((capacity, block.shape[1]), jnp.bfloat16) for _ in places],
+        [None],
+        (block,),
     )
 
 
@@ -226,34 +214,53 @@
         start = stop
 
 
-def expert_kernel(*refs):
-    outs, (slots, total) = refs[-10:-2], refs[-2:]
-    pieces, weights = refs[:-14], refs[-14:-10]
+def near_kernel(*refs):
+    pieces, (first, second, slots, total) = refs[:-4], refs[-4:]
     start = 0
     for piece in pieces:
         slots[start : start + piece.shape[0]] = piece[...]
         start += piece.shape[0]
     width = total.shape[1]
-    for half in range(2):
-        first, second = weights[2 * half : 2 * half + 2]
-        both = jnp.dot(slots[:, :width], first[...], preferred_element_type=jnp.float32)
-        term = jnp.dot(gated(both), second[...], preferred_element_type=jnp.float32)
-        total[...] = term if half == 0 else total[...] + term
+    both = jnp.dot(slots[:, :width], first[...], preferred_element_type=jnp.float32)
+    total[...] = jnp.dot(gated(both), second[...], preferred_element_type=jnp.float32)
+
+
+def near_pass(pieces, weights):
+    count = sum(piece.shape[0] for piece in pieces)
+    full = pieces[0].shape[1]
+    return local_call(
+        near_kernel,
+        "near_pass",
+        [
+            jax.ShapeDtypeStruct((count, full), jnp.bfloat16),
+            jax.ShapeDtypeStruct((count, full - LANES), jnp.float32),
+        ],
+        [None] * (len(pieces) + 2),
+        (*pieces, *weights),
+        moved=2 * sum(w.size for w in weights),
+    )
+
+
+def far_kernel(slots, before, first, second, *refs):
+    outs, total = refs[:-1], refs[-1]
+    width = total.shape[1]
+    both = jnp.dot(slots[:, :width], first[...], preferred_element_type=jnp.float32)
+    term = jnp.dot(gated(both), second[...], preferred_element_type=jnp.float32)
+    total[...] = before[...] + term
     write_pieces(slots, total, outs)
 
 
-def expert_pass(pieces, near, far, capacity):
-    full = pieces[0].shape[1]
-    count = capacity * 2 * len(RING)
-    return local_call(
-        expert_kernel,
-        "expert_pass",
-        [jax.ShapeDtypeStruct((capacity, full), jnp.bfloat16)] * (2 * len(RING)),
-        [None] * (len(pieces) + 4),
-        (*pieces, *near, *far),
-        [pltpu.VMEM((count, full), jnp.bfloat16), pltpu.VMEM((count, full - LANES), jnp.float32)],
+def far_pass(slots, total, weights, capacity):
+    count, full = slots.shape
+    return local_call(
+        far_kernel,
+        "far_pass",
+        [jax.ShapeDtypeStruct((capacity, full), jnp.bfloat16)] * (count // capacity),
+        [None] * 4,
+        (slots, total, *weights),
+        [pltpu.VMEM(total.shape, jnp.float32)],
         limit=24,
-        moved=2 * sum(w.size for w in (*near, *far)),
+        moved=2 * sum(w.size for w in weights),
     )
 
 
@@ -315,18 +322,21 @@
     far_in = lax.ppermute(w_in, "expert", swap)
     block = prepare(route_ids[0].T, route_weights[0].T, tokens)
     block1 = sent(block, sections, 0, 1, 0)
-    own0, other0, back0, back1 = choose(block, capacity, ((0, 0), (0, 1), (3, 0), (3, 1)))
+    own0, other, back0, back1 = choose(block, capacity, ((0, 0), (0, 1), (3, 0), (3, 1)))
+    other0 = sent(other, sections, 0, 0, 1)
+    near = (loaded(after(w_in, own0)), loaded(after(w_out, own0)))
+    block1 = after(block1, (near, other0))
+    own1, other, on0, on1 = choose(block1, capacity, ((0, 0), (0, 1), (1, 0), (1, 1)))
+    other1 = sent(other, sections, 0, 0, 1)
+    own2 = sent(on0, sections, 0, 1, 0)
+    other2 = sent(on1, sections, 0, 1, 1)
+    back0, back1 = after((back0, back1), other1)
     own3 = sent(back0, sections, 0, 3, 0)
     other3 = sent(back1, sections, 0, 3, 1)
-    near = (loaded(after(w_in, back1)), loaded(after(w_out, back1)))
-    block1 = after(block1, near)
-    own1, on0, on1, other = choose(block1, capacity, ((0, 0), (1, 0), (1, 1), (0, 1)), other0)
-    own2 = sent(on0, sections, 0, 1, 0)
-    other2 = sent(on1, sections, 0, 1, 1)
-    other01 = sent(other, sections, 0, 0, 1)
-    places = ((0, 0), (2, 0), (2, 1), (0, 1), (1, 1), (1, 0), (3, 0), (3, 1))
-    pieces = (own0, own2, other2, other01, own1, own3, other3)
-    pieces = expert_pass(pieces, near, (far_in, far_out), capacity)
+    pieces = (own0, other0, own1, own2, other2, other1, own3, other3)
+    places = ((0, 0), (0, 1), (1, 0), (2, 0), (2, 1), (1, 1), (3, 0), (3, 1))
+    slots, total = near_pass(pieces, near)
+    pieces = far_pass(slots, total, (far_in, far_out), capacity)
     back = [
         sent(piece, sections, 1, -steps, flip) for piece, (steps, flip) in zip(pieces, places)
     ]

time: 58.6 us -> 60.7 us (1.036)
  starting transfers between devices: 40.8 us -> 36.7 us
  waiting for transfers between devices: 7.83 us -> 11.9 us
  local copies, waits for them, and re-layouts: 2.04 us -> 4.62 us
    ppermute x14 -> x15, starting transfers between devices: 40.2 us -> 36.2 us  [sent(): return lax.ppermute(shard, ('section', 'expert'), pairs)]
    ppermute x14 -> x15, waiting for transfers between devices: 7.82 us -> 11.9 us  [sent(): return lax.ppermute(shard, ('section', 'expert'), pairs)]
    unnamed x4, local copies, waits for them, and re-layouts: 2.04 us -> 4.62 us
    pallas_call x7 -> x8, Pallas kernels: 7.28 us -> 7.19 us  [local_call(): pl.pallas_call(kernel, out_shape=out_shape, in_specs=[vmem if spec is Non...]
  transfers between devices with their start and end apart: 16 -> 17, of which waited for: 4 -> 6; matrix products, arithmetic and copies ran while one was open for 0% -> 0% of each run, Pallas kernels for 5% -> 7%
where the time goes in v9:
time: 60.7 us; the launch traced here: 60.5 us
  starting transfers between devices  36.7 us (60%)
  waiting for transfers between devices  11.9 us (20%)
  Pallas kernels  7.19 us (12%)
  local copies, waits for them, and re-layouts  4.62 us (8%)
    ppermute x15, starting transfers between devices, sent(): return lax.ppermute(shard, ('section', 'expert'), pairs)  36.2 us
    ppermute x15, waiting for transfers between devices, sent(): return lax.ppermute(shard, ('section', 'expert'), pairs)  11.9 us
    pallas_call x8, Pallas kernels, local_call(): pl.pallas_call(kernel, out_shape=out_shape, in_specs=[vmem if spec is Non...  7.19 us
    unnamed x4, local copies, waits for them, and re-layouts  4.62 us
  transfers between devices with their start and end apart: 17, of which 6 were waited for; matrix products, arithmetic and copies ran while one was open for 0% of the time, Pallas kernels for 7%

profile of v9, /device:TPU:0, one launch (start us, length us, event | category | flops | bytes accessed | tf_op | source)
XLA Modules:
  0.0 60.5 jit_solution(15371524872419190745)
XLA Ops:
  1.5 3.1 %collective-permute-start.1 = (bf16[32,3712]{1,0:T(8,128)(2,1)S(1)}, bf16[32,3712]{1,0:T(8,128)(2,1)S(1)}, u32[]{:S(2)}, u32[]{:S(2)}) collective-permute-start(bf16[32,3712]{1,0:T(8,128)(2,1)S(1)} %prepare.1.block), channel_id=1, source_target_pairs={{0,4},{1,5},{2,6},{3,7},{4,12},{5,13},{6,14},{7,15},{8,0},{9,1},{1... | collective-permute-start | bytes 712712 | tf_op jit(solution)/shard_map/ppermute | solution.py:304
  5.0 1.6 %collective-permute-start = (bf16[16,3712]{1,0:T(8,128)(2,1)S(1)}, bf16[16,3712]{1,0:T(8,128)(2,1)S(1)}, u32[]{:S(2)}, u32[]{:S(2)}) collective-permute-start(bf16[16,3712]{1,0:T(8,128)(2,1)S(1)} %get-tuple-element.29), channel_id=1, source_target_pairs={{0,2},{1,3},{2,0},{3,1},{4,6},{5,7},{6,4},{7,5},{8,10},{9,11},{10,... | collective-permute-start | bytes 356360 | tf_op jit(solution)/shard_map/ppermute | solution.py:304
  6.6 3.1 %copy-done = bf16[1,3584,1024]{2,1,0:T(8,128)(2,1)S(1)} copy-done((bf16[1,3584,1024]{2,1,0:T(8,128)(2,1)S(1)}, bf16[1,3584,1024]{2,1,0:T(8,128)(2,1)}, u32[]{:S(2)}) %copy-start) | copy-done | bytes 7340056
  10.2 1.5 %copy-done.1 = bf16[1,512,3584]{2,1,0:T(8,128)(2,1)S(1)} copy-done((bf16[1,512,3584]{2,1,0:T(8,128)(2,1)S(1)}, bf16[1,512,3584]{2,1,0:T(8,128)(2,1)}, u32[]{:S(2)}) %copy-start.1) | copy-done | bytes 3670040
  12.4 1.2 %collective-permute-start.4 = (bf16[16,3712]{1,0:T(8,128)(2,1)S(1)}, bf16[16,3712]{1,0:T(8,128)(2,1)S(1)}, u32[]{:S(2)}, u32[]{:S(2)}) collective-permute-start(bf16[16,3712]{1,0:T(8,128)(2,1)S(1)} %get-tuple-element.36), channel_id=1, source_target_pairs={{0,2},{1,3},{2,0},{3,1},{4,6},{5,7},{6,4},{7,5},{8,10},{9,11},{10,... | collective-permute-start | bytes 356360 | tf_op jit(solution)/shard_map/ppermute | solution.py:304
  13.6 2.0 %collective-permute-start.2 = (bf16[16,3712]{1,0:T(8,128)(2,1)S(1)}, bf16[16,3712]{1,0:T(8,128)(2,1)S(1)}, u32[]{:S(2)}, u32[]{:S(2)}) collective-permute-start(bf16[16,3712]{1,0:T(8,128)(2,1)S(1)} %get-tuple-element.34), channel_id=1, source_target_pairs={{0,4},{1,5},{2,6},{3,7},{4,12},{5,13},{6,14},{7,15},{8,0},{9,1},{1... | collective-permute-start | bytes 356360 | tf_op jit(solution)/shard_map/ppermute | solution.py:304
  15.6 2.1 %collective-permute-start.3 = (bf16[16,3712]{1,0:T(8,128)(2,1)S(1)}, bf16[16,3712]{1,0:T(8,128)(2,1)S(1)}, u32[]{:S(2)}, u32[]{:S(2)}) collective-permute-start(bf16[16,3712]{1,0:T(8,128)(2,1)S(1)} %get-tuple-element.35), channel_id=1, source_target_pairs={{0,6},{1,7},{2,4},{3,5},{4,14},{5,15},{6,12},{7,13},{8,2},{9,3},{1... | collective-permute-start | bytes 356360 | tf_op jit(solution)/shard_map/ppermute | solution.py:304
  17.7 1.7 %collective-permute-start.5 = (bf16[16,3712]{1,0:T(8,128)(2,1)S(1)}, bf16[16,3712]{1,0:T(8,128)(2,1)S(1)}, u32[]{:S(2)}, u32[]{:S(2)}) collective-permute-start(bf16[16,3712]{1,0:T(8,128)(2,1)S(1)} %get-tuple-element.39), channel_id=1, source_target_pairs={{0,8},{1,9},{2,10},{3,11},{4,0},{5,1},{6,2},{7,3},{8,12},{9,13},{1... | collective-permute-start | bytes 356360 | tf_op jit(solution)/shard_map/ppermute | solution.py:304
  19.9 2.2 %collective-permute-start.6 = (bf16[16,3712]{1,0:T(8,128)(2,1)S(1)}, bf16[16,3712]{1,0:T(8,128)(2,1)S(1)}, u32[]{:S(2)}, u32[]{:S(2)}) collective-permute-start(bf16[16,3712]{1,0:T(8,128)(2,1)S(1)} %get-tuple-element.40), channel_id=1, source_target_pairs={{0,10},{1,11},{2,8},{3,9},{4,2},{5,3},{6,0},{7,1},{8,14},{9,15},{1... | collective-permute-start | bytes 356360 | tf_op jit(solution)/shard_map/ppermute | solution.py:304
  22.1 4.1 %collective-permute-done.3.refs_4_ = bf16[16,3712]{1,0:T(8,128)(2,1)S(1)} collective-permute-done((bf16[16,3712]{1,0:T(8,128)(2,1)S(1)}, bf16[16,3712]{1,0:T(8,128)(2,1)S(1)}, u32[]{:S(2)}, u32[]{:S(2)}) %collective-permute-start.3) | collective-permute-done | bytes 118816 | tf_op jit(solution)/shard_map/ppermute | solution.py:304
  26.2 1.2 %collective-permute-done.6.refs_7_ = bf16[16,3712]{1,0:T(8,128)(2,1)S(1)} collective-permute-done((bf16[16,3712]{1,0:T(8,128)(2,1)S(1)}, bf16[16,3712]{1,0:T(8,128)(2,1)S(1)}, u32[]{:S(2)}, u32[]{:S(2)}) %collective-permute-start.6) | collective-permute-done | bytes 118816 | tf_op jit(solution)/shard_map/ppermute | solution.py:304
  27.3 1.8 %near_pass.1 = (bf16[128,3712]{1,0:T(8,128)(2,1)S(1)}, f32[128,3584]{1,0:T(8,128)S(1)}) custom-call(bf16[16,3712]{1,0:T(8,128)(2,1)S(1)} %get-tuple-element.28.refs_0_, bf16[16,3712]{1,0:T(8,128)(2,1)S(1)} %collective-permute-done.refs_1_, bf16[16,3712]{1,0:T(8,128)(2,1)S(1)} %get-tuple-element.33.refs_2_, ...), custom_call_target="tpu_custom_call" | custom-call | bytes 11010048 | tf_op jit(solution)/shard_map/near_pass/pallas_call | solution.py:84
  29.1 1.7 %far_pass.1 = (bf16[16,3712]{1,0:T(8,128)(2,1)S(1)}, bf16[16,3712]{1,0:T(8,128)(2,1)S(1)}, bf16[16,3712]{1,0:T(8,128)(2,1)S(1)}, bf16[16,3712]{1,0:T(8,128)(2,1)...) custom-call(bf16[128,3712]{1,0:T(8,128)(2,1)S(1)} %get-tuple-element, ...), custom_call_target="tpu_custom_call" | custom-call | bytes 11010048 | tf_op jit(solution)/shard_map/far_pass/pallas_call | solution.py:84
  30.9 2.1 %collective-permute-start.10 = (bf16[16,3712]{1,0:T(8,128)(2,1)S(1)}, bf16[16,3712]{1,0:T(8,128)(2,1)S(1)}, u32[]{:S(2)}, u32[]{:S(2)}) collective-permute-start(bf16[16,3712]{1,0:T(8,128)(2,1)S(1)} %get-tuple-element.44), channel_id=1, source_target_pairs={{0,18},{1,19},{2,16},{3,17},{4,22},{5,23},{6,20},{7,21},{8,26},{9,... | collective-permute-start | bytes 356360 | tf_op jit(solution)/shard_map/ppermute | solution.py:304
  33.0 1.8 %collective-permute-start.11 = (bf16[16,3712]{1,0:T(8,128)(2,1)S(1)}, bf16[16,3712]{1,0:T(8,128)(2,1)S(1)}, u32[]{:S(2)}, u32[]{:S(2)}) collective-permute-start(bf16[16,3712]{1,0:T(8,128)(2,1)S(1)} %get-tuple-element.45), channel_id=1, source_target_pairs={{0,24},{1,25},{2,26},{3,27},{4,16},{5,17},{6,18},{7,19},{8,28},{9,... | collective-permute-start | bytes 356360 | tf_op jit(solution)/shard_map/ppermute | solution.py:304
  34.8 2.9 %collective-permute-start.12 = (bf16[16,3712]{1,0:T(8,128)(2,1)S(1)}, bf16[16,3712]{1,0:T(8,128)(2,1)S(1)}, u32[]{:S(2)}, u32[]{:S(2)}) collective-permute-start(bf16[16,3712]{1,0:T(8,128)(2,1)S(1)} %get-tuple-element.46), channel_id=1, source_target_pairs={{0,28},{1,29},{2,30},{3,31},{4,24},{5,25},{6,26},{7,27},{8,20},{9,... | collective-permute-start | bytes 356360 | tf_op jit(solution)/shard_map/ppermute | solution.py:304
  37.6 2.7 %collective-permute-start.13 = (bf16[16,3712]{1,0:T(8,128)(2,1)S(1)}, bf16[16,3712]{1,0:T(8,128)(2,1)S(1)}, u32[]{:S(2)}, u32[]{:S(2)}) collective-permute-start(bf16[16,3712]{1,0:T(8,128)(2,1)S(1)} %get-tuple-element.47), channel_id=1, source_target_pairs={{0,30},{1,31},{2,28},{3,29},{4,26},{5,27},{6,24},{7,25},{8,22},{9,... | collective-permute-start | bytes 356360 | tf_op jit(solution)/shard_map/ppermute | solution.py:304
  41.1 2.2 %collective-permute-start.15 = (bf16[16,3712]{1,0:T(8,128)(2,1)S(1)}, bf16[16,3712]{1,0:T(8,128)(2,1)S(1)}, u32[]{:S(2)}, u32[]{:S(2)}) collective-permute-start(bf16[16,3712]{1,0:T(8,128)(2,1)S(1)} %get-tuple-element.49), channel_id=1, source_target_pairs={{0,20},{1,21},{2,22},{3,23},{4,28},{5,29},{6,30},{7,31},{8,16},{9,... | collective-permute-start | bytes 356360 | tf_op jit(solution)/shard_map/ppermute | solution.py:304
  43.3 2.0 %collective-permute-start.16 = (bf16[16,3712]{1,0:T(8,128)(2,1)S(1)}, bf16[16,3712]{1,0:T(8,128)(2,1)S(1)}, u32[]{:S(2)}, u32[]{:S(2)}) collective-permute-start(bf16[16,3712]{1,0:T(8,128)(2,1)S(1)} %get-tuple-element.50), channel_id=1, source_target_pairs={{0,22},{1,23},{2,20},{3,21},{4,30},{5,31},{6,28},{7,29},{8,18},{9,... | collective-permute-start | bytes 356360 | tf_op jit(solution)/shard_map/ppermute | solution.py:304
  45.3 7.9 %collective-permute-start.9 = (bf16[16,3712]{1,0:T(8,128)(2,1)S(1)}, bf16[16,3712]{1,0:T(8,128)(2,1)S(1)}, u32[]{:S(2)}, u32[]{:S(2)}) collective-permute-start(bf16[16,3712]{1,0:T(8,128)(2,1)S(1)} %get-tuple-element.43), channel_id=1, source_target_pairs={{0,16},{1,17},{2,18},{3,19},{4,20},{5,21},{6,22},{7,23},{8,24},{9,... | collective-permute-start | bytes 356360 | tf_op jit(solution)/shard_map/ppermute | solution.py:304
  53.2 3.4 %collective-permute-done.15.refs_6_ = bf16[16,3712]{1,0:T(8,128)(2,1)S(1)} collective-permute-done((bf16[16,3712]{1,0:T(8,128)(2,1)S(1)}, bf16[16,3712]{1,0:T(8,128)(2,1)S(1)}, u32[]{:S(2)}, u32[]{:S(2)}) %collective-permute-start.15) | collective-permute-done | bytes 118816 | tf_op jit(solution)/shard_map/ppermute | solution.py:304
  56.6 1.3 %collective-permute-done.16.refs_7_ = bf16[16,3712]{1,0:T(8,128)(2,1)S(1)} collective-permute-done((bf16[16,3712]{1,0:T(8,128)(2,1)S(1)}, bf16[16,3712]{1,0:T(8,128)(2,1)S(1)}, u32[]{:S(2)}, u32[]{:S(2)}) %collective-permute-start.16) | collective-permute-done | bytes 118816 | tf_op jit(solution)/shard_map/ppermute | solution.py:304
  57.9 1.4 %collective-permute-done.9.refs_0_ = bf16[16,3712]{1,0:T(8,128)(2,1)S(1)} collective-permute-done((bf16[16,3712]{1,0:T(8,128)(2,1)S(1)}, bf16[16,3712]{1,0:T(8,128)(2,1)S(1)}, u32[]{:S(2)}, u32[]{:S(2)}) %collective-permute-start.9) | collective-permute-done | bytes 118816 | tf_op jit(solution)/shard_map/ppermute | solution.py:304
  59.3 1.1 %combine.1 = bf16[32,3584]{1,0:T(8,128)(2,1)} custom-call(bf16[16,3712]{1,0:T(8,128)(2,1)S(1)} %collective-permute-done.9.refs_0_, bf16[16,3712]{1,0:T(8,128)(2,1)S(1)} %collective-permute-done.10.refs_1_, bf16[16,3712]{1,0:T(8,128)(2,1)S(1)} %collective-permute-done.11.refs_2_, bf16[16,3712]{1,0:T(8,128)(2,1)S(1)} %collective-permute-done.12.refs_3_, ...), custom_call_target="tpu_custom_call" | custom-call | tf_op jit(solution)/shard_map/combine/pallas_call | solution.py:84
  (22 shorter events, 4.3 us)
Async XLA Ops:
  0.0 29.1 %collective-permute-start.7 = (bf16[3584,1024]{1,0:T(8,128)(2,1)}, bf16[3584,1024]{1,0:T(8,128)(2,1)S(1)}, u32[]{:S(2)}, u32[]{:S(2)}) collective-permute-start(bf16[3584,1024]{1,0:T(8,128)(2,1)} %bitcast.10), channel_id=1, source_target_pairs={{0,1},{1,0},{2,3},{3,2},{4,5},{5,4},{6,7},{7,6},{8,9},{9,8},{10,11... | collective-permute-start | bytes 22020104 | tf_op jit(solution)/shard_map/ppermute | solution.py:322
  0.5 28.6 %collective-permute-start.8 = (bf16[512,3584]{1,0:T(8,128)(2,1)}, bf16[512,3584]{1,0:T(8,128)(2,1)S(1)}, u32[]{:S(2)}, u32[]{:S(2)}) collective-permute-start(bf16[512,3584]{1,0:T(8,128)(2,1)} %bitcast.12), channel_id=1, source_target_pairs={{0,1},{1,0},{2,3},{3,2},{4,5},{5,4},{6,7},{7,6},{8,9},{9,8},{10,11... | collective-permute-start | bytes 11010056 | tf_op jit(solution)/shard_map/ppermute | solution.py:321
  1.5 10.5 %collective-permute-start.1 = (bf16[32,3712]{1,0:T(8,128)(2,1)S(1)}, bf16[32,3712]{1,0:T(8,128)(2,1)S(1)}, u32[]{:S(2)}, u32[]{:S(2)}) collective-permute-start(bf16[32,3712]{1,0:T(8,128)(2,1)S(1)} %prepare.1.block), channel_id=1, source_target_pairs={{0,4},{1,5},{2,6},{3,7},{4,12},{5,13},{6,14},{7,15},{8,0},{9,1},{1... | collective-permute-start | bytes 712712 | tf_op jit(solution)/shard_map/ppermute | solution.py:304
  5.0 7.0 %collective-permute-start = (bf16[16,3712]{1,0:T(8,128)(2,1)S(1)}, bf16[16,3712]{1,0:T(8,128)(2,1)S(1)}, u32[]{:S(2)}, u32[]{:S(2)}) collective-permute-start(bf16[16,3712]{1,0:T(8,128)(2,1)S(1)} %get-tuple-element.29), channel_id=1, source_target_pairs={{0,2},{1,3},{2,0},{3,1},{4,6},{5,7},{6,4},{7,5},{8,10},{9,11},{10,... | collective-permute-start | bytes 356360 | tf_op jit(solution)/shard_map/ppermute | solution.py:304
  6.6 3.1 %copy-start = (bf16[1,3584,1024]{2,1,0:T(8,128)(2,1)S(1)}, bf16[1,3584,1024]{2,1,0:T(8,128)(2,1)}, u32[]{:S(2)}) copy-start(bf16[1,3584,1024]{2,1,0:T(8,128)(2,1)} %param.8) | copy-start | bytes 22020100
  9.7 2.0 %copy-start.1 = (bf16[1,512,3584]{2,1,0:T(8,128)(2,1)S(1)}, bf16[1,512,3584]{2,1,0:T(8,128)(2,1)}, u32[]{:S(2)}) copy-start(bf16[1,512,3584]{2,1,0:T(8,128)(2,1)} %param.9) | copy-start | bytes 11010052
  12.4 5.3 %collective-permute-start.4 = (bf16[16,3712]{1,0:T(8,128)(2,1)S(1)}, bf16[16,3712]{1,0:T(8,128)(2,1)S(1)}, u32[]{:S(2)}, u32[]{:S(2)}) collective-permute-start(bf16[16,3712]{1,0:T(8,128)(2,1)S(1)} %get-tuple-element.36), channel_id=1, source_target_pairs={{0,2},{1,3},{2,0},{3,1},{4,6},{5,7},{6,4},{7,5},{8,10},{9,11},{10,... | collective-permute-start | bytes 356360 | tf_op jit(solution)/shard_map/ppermute | solution.py:304
  13.6 6.3 %collective-permute-start.2 = (bf16[16,3712]{1,0:T(8,128)(2,1)S(1)}, bf16[16,3712]{1,0:T(8,128)(2,1)S(1)}, u32[]{:S(2)}, u32[]{:S(2)}) collective-permute-start(bf16[16,3712]{1,0:T(8,128)(2,1)S(1)} %get-tuple-element.34), channel_id=1, source_target_pairs={{0,4},{1,5},{2,6},{3,7},{4,12},{5,13},{6,14},{7,15},{8,0},{9,1},{1... | collective-permute-start | bytes 356360 | tf_op jit(solution)/shard_map/ppermute | solution.py:304
  15.6 10.6 %collective-permute-start.3 = (bf16[16,3712]{1,0:T(8,128)(2,1)S(1)}, bf16[16,3712]{1,0:T(8,128)(2,1)S(1)}, u32[]{:S(2)}, u32[]{:S(2)}) collective-permute-start(bf16[16,3712]{1,0:T(8,128)(2,1)S(1)} %get-tuple-element.35), channel_id=1, source_target_pairs={{0,6},{1,7},{2,4},{3,5},{4,14},{5,15},{6,12},{7,13},{8,2},{9,3},{1... | collective-permute-start | bytes 356360 | tf_op jit(solution)/shard_map/ppermute | solution.py:304
  17.7 8.4 %collective-permute-start.5 = (bf16[16,3712]{1,0:T(8,128)(2,1)S(1)}, bf16[16,3712]{1,0:T(8,128)(2,1)S(1)}, u32[]{:S(2)}, u32[]{:S(2)}) collective-permute-start(bf16[16,3712]{1,0:T(8,128)(2,1)S(1)} %get-tuple-element.39), channel_id=1, source_target_pairs={{0,8},{1,9},{2,10},{3,11},{4,0},{5,1},{6,2},{7,3},{8,12},{9,13},{1... | collective-permute-start | bytes 356360 | tf_op jit(solution)/shard_map/ppermute | solution.py:304
  19.9 7.5 %collective-permute-start.6 = (bf16[16,3712]{1,0:T(8,128)(2,1)S(1)}, bf16[16,3712]{1,0:T(8,128)(2,1)S(1)}, u32[]{:S(2)}, u32[]{:S(2)}) collective-permute-start(bf16[16,3712]{1,0:T(8,128)(2,1)S(1)} %get-tuple-element.40), channel_id=1, source_target_pairs={{0,10},{1,11},{2,8},{3,9},{4,2},{5,3},{6,0},{7,1},{8,14},{9,15},{1... | collective-permute-start | bytes 356360 | tf_op jit(solution)/shard_map/ppermute | solution.py:304
  30.9 10.2 %collective-permute-start.10 = (bf16[16,3712]{1,0:T(8,128)(2,1)S(1)}, bf16[16,3712]{1,0:T(8,128)(2,1)S(1)}, u32[]{:S(2)}, u32[]{:S(2)}) collective-permute-start(bf16[16,3712]{1,0:T(8,128)(2,1)S(1)} %get-tuple-element.44), channel_id=1, source_target_pairs={{0,18},{1,19},{2,16},{3,17},{4,22},{5,23},{6,20},{7,21},{8,26},{9,... | collective-permute-start | bytes 356360 | tf_op jit(solution)/shard_map/ppermute | solution.py:304
  33.0 10.3 %collective-permute-start.11 = (bf16[16,3712]{1,0:T(8,128)(2,1)S(1)}, bf16[16,3712]{1,0:T(8,128)(2,1)S(1)}, u32[]{:S(2)}, u32[]{:S(2)}) collective-permute-start(bf16[16,3712]{1,0:T(8,128)(2,1)S(1)} %get-tuple-element.45), channel_id=1, source_target_pairs={{0,24},{1,25},{2,26},{3,27},{4,16},{5,17},{6,18},{7,19},{8,28},{9,... | collective-permute-start | bytes 356360 | tf_op jit(solution)/shard_map/ppermute | solution.py:304
  34.8 10.5 %collective-permute-start.12 = (bf16[16,3712]{1,0:T(8,128)(2,1)S(1)}, bf16[16,3712]{1,0:T(8,128)(2,1)S(1)}, u32[]{:S(2)}, u32[]{:S(2)}) collective-permute-start(bf16[16,3712]{1,0:T(8,128)(2,1)S(1)} %get-tuple-element.46), channel_id=1, source_target_pairs={{0,28},{1,29},{2,30},{3,31},{4,24},{5,25},{6,26},{7,27},{8,20},{9,... | collective-permute-start | bytes 356360 | tf_op jit(solution)/shard_map/ppermute | solution.py:304
  37.6 15.5 %collective-permute-start.13 = (bf16[16,3712]{1,0:T(8,128)(2,1)S(1)}, bf16[16,3712]{1,0:T(8,128)(2,1)S(1)}, u32[]{:S(2)}, u32[]{:S(2)}) collective-permute-start(bf16[16,3712]{1,0:T(8,128)(2,1)S(1)} %get-tuple-element.47), channel_id=1, source_target_pairs={{0,30},{1,31},{2,28},{3,29},{4,26},{5,27},{6,24},{7,25},{8,22},{9,... | collective-permute-start | bytes 356360 | tf_op jit(solution)/shard_map/ppermute | solution.py:304
  40.3 12.8 %collective-permute-start.14 = (bf16[16,3712]{1,0:T(8,128)(2,1)S(1)}, bf16[16,3712]{1,0:T(8,128)(2,1)S(1)}, u32[]{:S(2)}, u32[]{:S(2)}) collective-permute-start(bf16[16,3712]{1,0:T(8,128)(2,1)S(1)} %get-tuple-element.48), channel_id=1, source_target_pairs={{0,26},{1,27},{2,24},{3,25},{4,18},{5,19},{6,16},{7,17},{8,30},{9,... | collective-permute-start | bytes 356360 | tf_op jit(solution)/shard_map/ppermute | solution.py:304
  41.1 15.5 %collective-permute-start.15 = (bf16[16,3712]{1,0:T(8,128)(2,1)S(1)}, bf16[16,3712]{1,0:T(8,128)(2,1)S(1)}, u32[]{:S(2)}, u32[]{:S(2)}) collective-permute-start(bf16[16,3712]{1,0:T(8,128)(2,1)S(1)} %get-tuple-element.49), channel_id=1, source_target_pairs={{0,20},{1,21},{2,22},{3,23},{4,28},{5,29},{6,30},{7,31},{8,16},{9,... | collective-permute-start | bytes 356360 | tf_op jit(solution)/shard_map/ppermute | solution.py:304
  43.3 14.6 %collective-permute-start.16 = (bf16[16,3712]{1,0:T(8,128)(2,1)S(1)}, bf16[16,3712]{1,0:T(8,128)(2,1)S(1)}, u32[]{:S(2)}, u32[]{:S(2)}) collective-permute-start(bf16[16,3712]{1,0:T(8,128)(2,1)S(1)} %get-tuple-element.50), channel_id=1, source_target_pairs={{0,22},{1,23},{2,20},{3,21},{4,30},{5,31},{6,28},{7,29},{8,18},{9,... | collective-permute-start | bytes 356360 | tf_op jit(solution)/shard_map/ppermute | solution.py:304
  45.3 14.0 %collective-permute-start.9 = (bf16[16,3712]{1,0:T(8,128)(2,1)S(1)}, bf16[16,3712]{1,0:T(8,128)(2,1)S(1)}, u32[]{:S(2)}, u32[]{:S(2)}) collective-permute-start(bf16[16,3712]{1,0:T(8,128)(2,1)S(1)} %get-tuple-element.43), channel_id=1, source_target_pairs={{0,16},{1,17},{2,18},{3,19},{4,20},{5,21},{6,22},{7,23},{8,24},{9,... | collective-permute-start | bytes 356360 | tf_op jit(solution)/shard_map/ppermute | solution.py:304

commit v10 on v9

--- a/solution.py
+++ b/solution.py
@@ -264,8 +264,8 @@
     )
 
 
-def combine_kernel(*refs):
-    blocks, out, slots = refs[:-2], refs[-2], refs[-1]
+def combine_kernel(count, *refs):
+    blocks, more, (out, slots) = refs[:count], refs[count:-2], refs[-2:]
     tok_count, width = out.shape
     start = 0
     for block in blocks:
@@ -275,18 +275,20 @@
     part = width // 7
     for at in range(7):
         place = slice(at * part, (at + 1) * part)
-        mixed = across(token, slots[:, place])
-        out[:, place] = mixed[TOKEN_LANE : TOKEN_LANE + tok_count].astype(out.dtype)
-
-
-def combine(blocks, tok_count):
+        mixed = across(token, slots[:, place])[TOKEN_LANE : TOKEN_LANE + tok_count]
+        for other in more:
+            mixed = mixed + other[:, place].astype(jnp.float32)
+        out[:, place] = mixed.astype(out.dtype)
+
+
+def combine(blocks, tok_count, *more):
     capacity, full = blocks[0].shape
     return local_call(
-        combine_kernel,
+        functools.partial(combine_kernel, len(blocks)),
         "combine",
         jax.ShapeDtypeStruct((tok_count, full - LANES), jnp.bfloat16),
-        [None] * len(blocks),
-        tuple(blocks),
+        [None] * (len(blocks) + len(more)),
+        (*blocks, *more),
         [pltpu.VMEM((capacity * len(blocks), full), jnp.bfloat16)],
     )
 
@@ -337,10 +339,18 @@
     places = ((0, 0), (0, 1), (1, 0), (2, 0), (2, 1), (1, 1), (3, 0), (3, 1))
     slots, total = near_pass(pieces, near)
     pieces = far_pass(slots, total, (far_in, far_out), capacity)
-    back = [
-        sent(piece, sections, 1, -steps, flip) for piece, (steps, flip) in zip(pieces, places)
+    piece = dict(zip(places, pieces))
+    merged = [
+        piece[3, 0],
+        sent(piece[2, 0], sections, 0, 1, 0),
+        sent(piece[2, 1], sections, 0, 1, 1),
+        sent(piece[3, 1], sections, 0, 0, 1),
     ]
-    return combine(back, tok_count)[None]
+    straight = [sent(piece[0, flip], sections, 1, 0, flip) for flip in range(2)]
+    merged, straight = lax.optimization_barrier((merged, straight))
+    straight += [sent(piece[1, flip], sections, 1, -1, flip) for flip in range(2)]
+    merged = sent(combine(merged, tok_count), sections, 1, 1, 0)
+    return combine(straight, tok_count, merged)[None]
 
 
 def per_device(rows, route_ids, route_weights, w_gate_up, w_down):

time: 60.7 us -> 56.6 us (0.932)
  starting transfers between devices: 36.7 us -> 26.7 us
  waiting for transfers between devices: 11.9 us -> 17.3 us
    ppermute x15, starting transfers between devices: 36.2 us -> 26.2 us  [sent(): return lax.ppermute(shard, ('section', 'expert'), pairs)]
    ppermute x15, waiting for transfers between devices: 11.9 us -> 17.3 us  [sent(): return lax.ppermute(shard, ('section', 'expert'), pairs)]
    pallas_call x8 -> x9, Pallas kernels: 7.19 us -> 7.6 us  [local_call(): pl.pallas_call(kernel, out_shape=out_shape, in_specs=[vmem if spec is Non...]
  transfers between devices with their start and end apart: 17 -> 17, of which waited for: 6 -> 9; matrix products, arithmetic and copies ran while one was open for 0% -> 0% of each run, Pallas kernels for 7% -> 8%
where the time goes in v10:
time: 56.6 us; the launch traced here: 56.4 us
  starting transfers between devices  26.7 us (47%)
  waiting for transfers between devices  17.3 us (31%)
  Pallas kernels  7.6 us (13%)
  local copies, waits for them, and re-layouts  4.62 us (8%)
    ppermute x15, starting transfers between devices, sent(): return lax.ppermute(shard, ('section', 'expert'), pairs)  26.2 us
    ppermute x15, waiting for transfers between devices, sent(): return lax.ppermute(shard, ('section', 'expert'), pairs)  17.3 us
    pallas_call x9, Pallas kernels, local_call(): pl.pallas_call(kernel, out_shape=out_shape, in_specs=[vmem if spec is Non...  7.6 us
    unnamed x4, local copies, waits for them, and re-layouts  4.62 us
  transfers between devices with their start and end apart: 17, of which 9 were waited for; matrix products, arithmetic and copies ran while one was open for 0% of the time, Pallas kernels for 8%

profile of v10, /device:TPU:0, one launch (start us, length us, event | category | flops | bytes accessed | tf_op | source)
XLA Modules:
  0.0 56.4 jit_solution(14209145761347893701)
XLA Ops:
  1.5 3.1 %collective-permute-start.1 = (bf16[32,3712]{1,0:T(8,128)(2,1)S(1)}, bf16[32,3712]{1,0:T(8,128)(2,1)S(1)}, u32[]{:S(2)}, u32[]{:S(2)}) collective-permute-start(bf16[32,3712]{1,0:T(8,128)(2,1)S(1)} %prepare.1.block), channel_id=1, source_target_pairs={{0,4},{1,5},{2,6},{3,7},{4,12},{5,13},{6,14},{7,15},{8,0},{9,1},{1... | collective-permute-start | bytes 712712 | tf_op jit(solution)/shard_map/ppermute | solution.py:306
  5.0 1.6 %collective-permute-start = (bf16[16,3712]{1,0:T(8,128)(2,1)S(1)}, bf16[16,3712]{1,0:T(8,128)(2,1)S(1)}, u32[]{:S(2)}, u32[]{:S(2)}) collective-permute-start(bf16[16,3712]{1,0:T(8,128)(2,1)S(1)} %get-tuple-element.35), channel_id=1, source_target_pairs={{0,2},{1,3},{2,0},{3,1},{4,6},{5,7},{6,4},{7,5},{8,10},{9,11},{10,... | collective-permute-start | bytes 356360 | tf_op jit(solution)/shard_map/ppermute | solution.py:306
  6.6 3.1 %copy-done = bf16[1,3584,1024]{2,1,0:T(8,128)(2,1)S(1)} copy-done((bf16[1,3584,1024]{2,1,0:T(8,128)(2,1)S(1)}, bf16[1,3584,1024]{2,1,0:T(8,128)(2,1)}, u32[]{:S(2)}) %copy-start) | copy-done | bytes 7340056
  10.2 1.5 %copy-done.1 = bf16[1,512,3584]{2,1,0:T(8,128)(2,1)S(1)} copy-done((bf16[1,512,3584]{2,1,0:T(8,128)(2,1)S(1)}, bf16[1,512,3584]{2,1,0:T(8,128)(2,1)}, u32[]{:S(2)}) %copy-start.1) | copy-done | bytes 3670040
  12.4 1.2 %collective-permute-start.4 = (bf16[16,3712]{1,0:T(8,128)(2,1)S(1)}, bf16[16,3712]{1,0:T(8,128)(2,1)S(1)}, u32[]{:S(2)}, u32[]{:S(2)}) collective-permute-start(bf16[16,3712]{1,0:T(8,128)(2,1)S(1)} %get-tuple-element.42), channel_id=1, source_target_pairs={{0,2},{1,3},{2,0},{3,1},{4,6},{5,7},{6,4},{7,5},{8,10},{9,11},{10,... | collective-permute-start | bytes 356360 | tf_op jit(solution)/shard_map/ppermute | solution.py:306
  13.6 2.0 %collective-permute-start.2 = (bf16[16,3712]{1,0:T(8,128)(2,1)S(1)}, bf16[16,3712]{1,0:T(8,128)(2,1)S(1)}, u32[]{:S(2)}, u32[]{:S(2)}) collective-permute-start(bf16[16,3712]{1,0:T(8,128)(2,1)S(1)} %get-tuple-element.40), channel_id=1, source_target_pairs={{0,4},{1,5},{2,6},{3,7},{4,12},{5,13},{6,14},{7,15},{8,0},{9,1},{1... | collective-permute-start | bytes 356360 | tf_op jit(solution)/shard_map/ppermute | solution.py:306
  15.6 2.1 %collective-permute-start.3 = (bf16[16,3712]{1,0:T(8,128)(2,1)S(1)}, bf16[16,3712]{1,0:T(8,128)(2,1)S(1)}, u32[]{:S(2)}, u32[]{:S(2)}) collective-permute-start(bf16[16,3712]{1,0:T(8,128)(2,1)S(1)} %get-tuple-element.41), channel_id=1, source_target_pairs={{0,6},{1,7},{2,4},{3,5},{4,14},{5,15},{6,12},{7,13},{8,2},{9,3},{1... | collective-permute-start | bytes 356360 | tf_op jit(solution)/shard_map/ppermute | solution.py:306
  17.7 1.7 %collective-permute-start.5 = (bf16[16,3712]{1,0:T(8,128)(2,1)S(1)}, bf16[16,3712]{1,0:T(8,128)(2,1)S(1)}, u32[]{:S(2)}, u32[]{:S(2)}) collective-permute-start(bf16[16,3712]{1,0:T(8,128)(2,1)S(1)} %get-tuple-element.45), channel_id=1, source_target_pairs={{0,8},{1,9},{2,10},{3,11},{4,0},{5,1},{6,2},{7,3},{8,12},{9,13},{1... | collective-permute-start | bytes 356360 | tf_op jit(solution)/shard_map/ppermute | solution.py:306
  19.9 2.2 %collective-permute-start.6 = (bf16[16,3712]{1,0:T(8,128)(2,1)S(1)}, bf16[16,3712]{1,0:T(8,128)(2,1)S(1)}, u32[]{:S(2)}, u32[]{:S(2)}) collective-permute-start(bf16[16,3712]{1,0:T(8,128)(2,1)S(1)} %get-tuple-element.46), channel_id=1, source_target_pairs={{0,10},{1,11},{2,8},{3,9},{4,2},{5,3},{6,0},{7,1},{8,14},{9,15},{1... | collective-permute-start | bytes 356360 | tf_op jit(solution)/shard_map/ppermute | solution.py:306
  22.1 4.1 %collective-permute-done.3.refs_4_ = bf16[16,3712]{1,0:T(8,128)(2,1)S(1)} collective-permute-done((bf16[16,3712]{1,0:T(8,128)(2,1)S(1)}, bf16[16,3712]{1,0:T(8,128)(2,1)S(1)}, u32[]{:S(2)}, u32[]{:S(2)}) %collective-permute-start.3) | collective-permute-done | bytes 118816 | tf_op jit(solution)/shard_map/ppermute | solution.py:306
  26.2 1.2 %collective-permute-done.6.refs_7_ = bf16[16,3712]{1,0:T(8,128)(2,1)S(1)} collective-permute-done((bf16[16,3712]{1,0:T(8,128)(2,1)S(1)}, bf16[16,3712]{1,0:T(8,128)(2,1)S(1)}, u32[]{:S(2)}, u32[]{:S(2)}) %collective-permute-start.6) | collective-permute-done | bytes 118816 | tf_op jit(solution)/shard_map/ppermute | solution.py:306
  27.3 1.8 %near_pass.1 = (bf16[128,3712]{1,0:T(8,128)(2,1)S(1)}, f32[128,3584]{1,0:T(8,128)S(1)}) custom-call(bf16[16,3712]{1,0:T(8,128)(2,1)S(1)} %get-tuple-element.34.refs_0_, bf16[16,3712]{1,0:T(8,128)(2,1)S(1)} %collective-permute-done.refs_1_, bf16[16,3712]{1,0:T(8,128)(2,1)S(1)} %get-tuple-element.39.refs_2_, ...), custom_call_target="tpu_custom_call" | custom-call | bytes 11010048 | tf_op jit(solution)/shard_map/near_pass/pallas_call | solution.py:84
  29.1 1.7 %far_pass.1 = (bf16[16,3712]{1,0:T(8,128)(2,1)S(1)}, bf16[16,3712]{1,0:T(8,128)(2,1)S(1)}, bf16[16,3712]{1,0:T(8,128)(2,1)S(1)}, bf16[16,3712]{1,0:T(8,128)(2,1)...) custom-call(bf16[128,3712]{1,0:T(8,128)(2,1)S(1)} %get-tuple-element, ...), custom_call_target="tpu_custom_call" | custom-call | bytes 11010048 | tf_op jit(solution)/shard_map/far_pass/pallas_call | solution.py:84
  30.9 2.0 %collective-permute-start.10 = (bf16[16,3712]{1,0:T(8,128)(2,1)S(1)}, bf16[16,3712]{1,0:T(8,128)(2,1)S(1)}, u32[]{:S(2)}, u32[]{:S(2)}) collective-permute-start(bf16[16,3712]{1,0:T(8,128)(2,1)S(1)} %get-tuple-element.51), channel_id=1, source_target_pairs={{0,6},{1,7},{2,4},{3,5},{4,14},{5,15},{6,12},{7,13},{8,2},{9,3},{1... | collective-permute-start | bytes 356360 | tf_op jit(solution)/shard_map/ppermute | solution.py:306
  33.4 1.5 %collective-permute-start.12 = (bf16[16,3712]{1,0:T(8,128)(2,1)S(1)}, bf16[16,3712]{1,0:T(8,128)(2,1)S(1)}, u32[]{:S(2)}, u32[]{:S(2)}) collective-permute-start(bf16[16,3712]{1,0:T(8,128)(2,1)S(1)} %get-tuple-element.53), channel_id=1, source_target_pairs={{0,16},{1,17},{2,18},{3,19},{4,20},{5,21},{6,22},{7,23},{8,24},{9,... | collective-permute-start | bytes 356360 | tf_op jit(solution)/shard_map/ppermute | solution.py:306
  34.8 1.5 %collective-permute-start.13 = (bf16[16,3712]{1,0:T(8,128)(2,1)S(1)}, bf16[16,3712]{1,0:T(8,128)(2,1)S(1)}, u32[]{:S(2)}, u32[]{:S(2)}) collective-permute-start(bf16[16,3712]{1,0:T(8,128)(2,1)S(1)} %get-tuple-element.54), channel_id=1, source_target_pairs={{0,18},{1,19},{2,16},{3,17},{4,22},{5,23},{6,20},{7,21},{8,26},{9,... | collective-permute-start | bytes 356360 | tf_op jit(solution)/shard_map/ppermute | solution.py:306
  36.3 2.0 %collective-permute-start.9 = (bf16[16,3712]{1,0:T(8,128)(2,1)S(1)}, bf16[16,3712]{1,0:T(8,128)(2,1)S(1)}, u32[]{:S(2)}, u32[]{:S(2)}) collective-permute-start(bf16[16,3712]{1,0:T(8,128)(2,1)S(1)} %get-tuple-element.50), channel_id=1, source_target_pairs={{0,4},{1,5},{2,6},{3,7},{4,12},{5,13},{6,14},{7,15},{8,0},{9,1},{1... | collective-permute-start | bytes 356360 | tf_op jit(solution)/shard_map/ppermute | solution.py:306
  38.7 2.4 %collective-permute-done.11.refs_3_ = bf16[16,3712]{1,0:T(8,128)(2,1)S(1)} collective-permute-done((bf16[16,3712]{1,0:T(8,128)(2,1)S(1)}, bf16[16,3712]{1,0:T(8,128)(2,1)S(1)}, u32[]{:S(2)}, u32[]{:S(2)}) %collective-permute-start.11) | collective-permute-done | bytes 118816 | tf_op jit(solution)/shard_map/ppermute | solution.py:306
  42.5 2.1 %collective-permute-start.16 = (bf16[32,3584]{1,0:T(8,128)(2,1)S(1)}, bf16[32,3584]{1,0:T(8,128)(2,1)S(1)}, u32[]{:S(2)}, u32[]{:S(2)}) collective-permute-start(bf16[32,3584]{1,0:T(8,128)(2,1)S(1)} %combine.2), channel_id=1, source_target_pairs={{0,20},{1,21},{2,22},{3,23},{4,28},{5,29},{6,30},{7,31},{8,16},{9,... | collective-permute-start | bytes 688136 | tf_op jit(solution)/shard_map/ppermute | solution.py:306
  44.6 1.8 %collective-permute-start.14 = (bf16[16,3712]{1,0:T(8,128)(2,1)S(1)}, bf16[16,3712]{1,0:T(8,128)(2,1)S(1)}, u32[]{:S(2)}, u32[]{:S(2)}) collective-permute-start(bf16[16,3712]{1,0:T(8,128)(2,1)S(1)} %get-tuple-element.57), channel_id=1, source_target_pairs={{0,24},{1,25},{2,26},{3,27},{4,16},{5,17},{6,18},{7,19},{8,28},{9,... | collective-permute-start | bytes 356360 | tf_op jit(solution)/shard_map/ppermute | solution.py:306
  47.4 4.7 %collective-permute-done.14.refs_2_ = bf16[16,3712]{1,0:T(8,128)(2,1)S(1)} collective-permute-done((bf16[16,3712]{1,0:T(8,128)(2,1)S(1)}, bf16[16,3712]{1,0:T(8,128)(2,1)S(1)}, u32[]{:S(2)}, u32[]{:S(2)}) %collective-permute-start.14) | collective-permute-done | bytes 118816 | tf_op jit(solution)/shard_map/ppermute | solution.py:306
  52.1 1.6 %collective-permute-done.15.refs_3_ = bf16[16,3712]{1,0:T(8,128)(2,1)S(1)} collective-permute-done((bf16[16,3712]{1,0:T(8,128)(2,1)S(1)}, bf16[16,3712]{1,0:T(8,128)(2,1)S(1)}, u32[]{:S(2)}, u32[]{:S(2)}) %collective-permute-start.15) | collective-permute-done | bytes 118816 | tf_op jit(solution)/shard_map/ppermute | solution.py:306
  53.8 1.5 %collective-permute-done.16.refs_4_ = bf16[32,3584]{1,0:T(8,128)(2,1)S(1)} collective-permute-done((bf16[32,3584]{1,0:T(8,128)(2,1)S(1)}, bf16[32,3584]{1,0:T(8,128)(2,1)S(1)}, u32[]{:S(2)}, u32[]{:S(2)}) %collective-permute-start.16) | collective-permute-done | bytes 229408 | tf_op jit(solution)/shard_map/ppermute | solution.py:306
  55.3 1.1 %combine.3 = bf16[32,3584]{1,0:T(8,128)(2,1)} custom-call(bf16[16,3712]{1,0:T(8,128)(2,1)S(1)} %collective-permute-done.12.refs_0_, bf16[16,3712]{1,0:T(8,128)(2,1)S(1)} %collective-permute-done.13.refs_1_, bf16[16,3712]{1,0:T(8,128)(2,1)S(1)} %collective-permute-done.14.refs_2_, bf16[16,3712]{1,0:T(8,128)(2,1)S(1)} %collective-permute-done.15.refs_3_, ...), custom_call_target="tpu_custom_call" | custom-call | tf_op jit(solution)/shard_map/combine/pallas_call | solution.py:84
  (23 shorter events, 6.8 us)
Async XLA Ops:
  0.0 29.1 %collective-permute-start.7 = (bf16[3584,1024]{1,0:T(8,128)(2,1)}, bf16[3584,1024]{1,0:T(8,128)(2,1)S(1)}, u32[]{:S(2)}, u32[]{:S(2)}) collective-permute-start(bf16[3584,1024]{1,0:T(8,128)(2,1)} %bitcast.10), channel_id=1, source_target_pairs={{0,1},{1,0},{2,3},{3,2},{4,5},{5,4},{6,7},{7,6},{8,9},{9,8},{10,11... | collective-permute-start | bytes 22020104 | tf_op jit(solution)/shard_map/ppermute | solution.py:324
  0.5 28.6 %collective-permute-start.8 = (bf16[512,3584]{1,0:T(8,128)(2,1)}, bf16[512,3584]{1,0:T(8,128)(2,1)S(1)}, u32[]{:S(2)}, u32[]{:S(2)}) collective-permute-start(bf16[512,3584]{1,0:T(8,128)(2,1)} %bitcast.12), channel_id=1, source_target_pairs={{0,1},{1,0},{2,3},{3,2},{4,5},{5,4},{6,7},{7,6},{8,9},{9,8},{10,11... | collective-permute-start | bytes 11010056 | tf_op jit(solution)/shard_map/ppermute | solution.py:323
  1.5 10.5 %collective-permute-start.1 = (bf16[32,3712]{1,0:T(8,128)(2,1)S(1)}, bf16[32,3712]{1,0:T(8,128)(2,1)S(1)}, u32[]{:S(2)}, u32[]{:S(2)}) collective-permute-start(bf16[32,3712]{1,0:T(8,128)(2,1)S(1)} %prepare.1.block), channel_id=1, source_target_pairs={{0,4},{1,5},{2,6},{3,7},{4,12},{5,13},{6,14},{7,15},{8,0},{9,1},{1... | collective-permute-start | bytes 712712 | tf_op jit(solution)/shard_map/ppermute | solution.py:306
  5.0 7.0 %collective-permute-start = (bf16[16,3712]{1,0:T(8,128)(2,1)S(1)}, bf16[16,3712]{1,0:T(8,128)(2,1)S(1)}, u32[]{:S(2)}, u32[]{:S(2)}) collective-permute-start(bf16[16,3712]{1,0:T(8,128)(2,1)S(1)} %get-tuple-element.35), channel_id=1, source_target_pairs={{0,2},{1,3},{2,0},{3,1},{4,6},{5,7},{6,4},{7,5},{8,10},{9,11},{10,... | collective-permute-start | bytes 356360 | tf_op jit(solution)/shard_map/ppermute | solution.py:306
  6.6 3.1 %copy-start = (bf16[1,3584,1024]{2,1,0:T(8,128)(2,1)S(1)}, bf16[1,3584,1024]{2,1,0:T(8,128)(2,1)}, u32[]{:S(2)}) copy-start(bf16[1,3584,1024]{2,1,0:T(8,128)(2,1)} %param.8) | copy-start | bytes 22020100
  9.7 2.0 %copy-start.1 = (bf16[1,512,3584]{2,1,0:T(8,128)(2,1)S(1)}, bf16[1,512,3584]{2,1,0:T(8,128)(2,1)}, u32[]{:S(2)}) copy-start(bf16[1,512,3584]{2,1,0:T(8,128)(2,1)} %param.9) | copy-start | bytes 11010052
  12.4 5.3 %collective-permute-start.4 = (bf16[16,3712]{1,0:T(8,128)(2,1)S(1)}, bf16[16,3712]{1,0:T(8,128)(2,1)S(1)}, u32[]{:S(2)}, u32[]{:S(2)}) collective-permute-start(bf16[16,3712]{1,0:T(8,128)(2,1)S(1)} %get-tuple-element.42), channel_id=1, source_target_pairs={{0,2},{1,3},{2,0},{3,1},{4,6},{5,7},{6,4},{7,5},{8,10},{9,11},{10,... | collective-permute-start | bytes 356360 | tf_op jit(solution)/shard_map/ppermute | solution.py:306
  13.6 6.3 %collective-permute-start.2 = (bf16[16,3712]{1,0:T(8,128)(2,1)S(1)}, bf16[16,3712]{1,0:T(8,128)(2,1)S(1)}, u32[]{:S(2)}, u32[]{:S(2)}) collective-permute-start(bf16[16,3712]{1,0:T(8,128)(2,1)S(1)} %get-tuple-element.40), channel_id=1, source_target_pairs={{0,4},{1,5},{2,6},{3,7},{4,12},{5,13},{6,14},{7,15},{8,0},{9,1},{1... | collective-permute-start | bytes 356360 | tf_op jit(solution)/shard_map/ppermute | solution.py:306
  15.6 10.6 %collective-permute-start.3 = (bf16[16,3712]{1,0:T(8,128)(2,1)S(1)}, bf16[16,3712]{1,0:T(8,128)(2,1)S(1)}, u32[]{:S(2)}, u32[]{:S(2)}) collective-permute-start(bf16[16,3712]{1,0:T(8,128)(2,1)S(1)} %get-tuple-element.41), channel_id=1, source_target_pairs={{0,6},{1,7},{2,4},{3,5},{4,14},{5,15},{6,12},{7,13},{8,2},{9,3},{1... | collective-permute-start | bytes 356360 | tf_op jit(solution)/shard_map/ppermute | solution.py:306
  17.7 8.4 %collective-permute-start.5 = (bf16[16,3712]{1,0:T(8,128)(2,1)S(1)}, bf16[16,3712]{1,0:T(8,128)(2,1)S(1)}, u32[]{:S(2)}, u32[]{:S(2)}) collective-permute-start(bf16[16,3712]{1,0:T(8,128)(2,1)S(1)} %get-tuple-element.45), channel_id=1, source_target_pairs={{0,8},{1,9},{2,10},{3,11},{4,0},{5,1},{6,2},{7,3},{8,12},{9,13},{1... | collective-permute-start | bytes 356360 | tf_op jit(solution)/shard_map/ppermute | solution.py:306
  19.9 7.5 %collective-permute-start.6 = (bf16[16,3712]{1,0:T(8,128)(2,1)S(1)}, bf16[16,3712]{1,0:T(8,128)(2,1)S(1)}, u32[]{:S(2)}, u32[]{:S(2)}) collective-permute-start(bf16[16,3712]{1,0:T(8,128)(2,1)S(1)} %get-tuple-element.46), channel_id=1, source_target_pairs={{0,10},{1,11},{2,8},{3,9},{4,2},{5,3},{6,0},{7,1},{8,14},{9,15},{1... | collective-permute-start | bytes 356360 | tf_op jit(solution)/shard_map/ppermute | solution.py:306
  30.9 7.8 %collective-permute-start.10 = (bf16[16,3712]{1,0:T(8,128)(2,1)S(1)}, bf16[16,3712]{1,0:T(8,128)(2,1)S(1)}, u32[]{:S(2)}, u32[]{:S(2)}) collective-permute-start(bf16[16,3712]{1,0:T(8,128)(2,1)S(1)} %get-tuple-element.51), channel_id=1, source_target_pairs={{0,6},{1,7},{2,4},{3,5},{4,14},{5,15},{6,12},{7,13},{8,2},{9,3},{1... | collective-permute-start | bytes 356360 | tf_op jit(solution)/shard_map/ppermute | solution.py:306
  32.8 8.3 %collective-permute-start.11 = (bf16[16,3712]{1,0:T(8,128)(2,1)S(1)}, bf16[16,3712]{1,0:T(8,128)(2,1)S(1)}, u32[]{:S(2)}, u32[]{:S(2)}) collective-permute-start(bf16[16,3712]{1,0:T(8,128)(2,1)S(1)} %get-tuple-element.52), channel_id=1, source_target_pairs={{0,2},{1,3},{2,0},{3,1},{4,6},{5,7},{6,4},{7,5},{8,10},{9,11},{10,... | collective-permute-start | bytes 356360 | tf_op jit(solution)/shard_map/ppermute | solution.py:306
  33.4 7.8 %collective-permute-start.12 = (bf16[16,3712]{1,0:T(8,128)(2,1)S(1)}, bf16[16,3712]{1,0:T(8,128)(2,1)S(1)}, u32[]{:S(2)}, u32[]{:S(2)}) collective-permute-start(bf16[16,3712]{1,0:T(8,128)(2,1)S(1)} %get-tuple-element.53), channel_id=1, source_target_pairs={{0,16},{1,17},{2,18},{3,19},{4,20},{5,21},{6,22},{7,23},{8,24},{9,... | collective-permute-start | bytes 356360 | tf_op jit(solution)/shard_map/ppermute | solution.py:306
  34.8 6.3 %collective-permute-start.13 = (bf16[16,3712]{1,0:T(8,128)(2,1)S(1)}, bf16[16,3712]{1,0:T(8,128)(2,1)S(1)}, u32[]{:S(2)}, u32[]{:S(2)}) collective-permute-start(bf16[16,3712]{1,0:T(8,128)(2,1)S(1)} %get-tuple-element.54), channel_id=1, source_target_pairs={{0,18},{1,19},{2,16},{3,17},{4,22},{5,23},{6,20},{7,21},{8,26},{9,... | collective-permute-start | bytes 356360 | tf_op jit(solution)/shard_map/ppermute | solution.py:306
  36.3 5.7 %collective-permute-start.9 = (bf16[16,3712]{1,0:T(8,128)(2,1)S(1)}, bf16[16,3712]{1,0:T(8,128)(2,1)S(1)}, u32[]{:S(2)}, u32[]{:S(2)}) collective-permute-start(bf16[16,3712]{1,0:T(8,128)(2,1)S(1)} %get-tuple-element.50), channel_id=1, source_target_pairs={{0,4},{1,5},{2,6},{3,7},{4,12},{5,13},{6,14},{7,15},{8,0},{9,1},{1... | collective-permute-start | bytes 356360 | tf_op jit(solution)/shard_map/ppermute | solution.py:306
  42.5 12.8 %collective-permute-start.16 = (bf16[32,3584]{1,0:T(8,128)(2,1)S(1)}, bf16[32,3584]{1,0:T(8,128)(2,1)S(1)}, u32[]{:S(2)}, u32[]{:S(2)}) collective-permute-start(bf16[32,3584]{1,0:T(8,128)(2,1)S(1)} %combine.2), channel_id=1, source_target_pairs={{0,20},{1,21},{2,22},{3,23},{4,28},{5,29},{6,30},{7,31},{8,16},{9,... | collective-permute-start | bytes 688136 | tf_op jit(solution)/shard_map/ppermute | solution.py:306
  44.6 7.5 %collective-permute-start.14 = (bf16[16,3712]{1,0:T(8,128)(2,1)S(1)}, bf16[16,3712]{1,0:T(8,128)(2,1)S(1)}, u32[]{:S(2)}, u32[]{:S(2)}) collective-permute-start(bf16[16,3712]{1,0:T(8,128)(2,1)S(1)} %get-tuple-element.57), channel_id=1, source_target_pairs={{0,24},{1,25},{2,26},{3,27},{4,16},{5,17},{6,18},{7,19},{8,28},{9,... | collective-permute-start | bytes 356360 | tf_op jit(solution)/shard_map/ppermute | solution.py:306
  46.4 7.4 %collective-permute-start.15 = (bf16[16,3712]{1,0:T(8,128)(2,1)S(1)}, bf16[16,3712]{1,0:T(8,128)(2,1)S(1)}, u32[]{:S(2)}, u32[]{:S(2)}) collective-permute-start(bf16[16,3712]{1,0:T(8,128)(2,1)S(1)} %get-tuple-element.58), channel_id=1, source_target_pairs={{0,26},{1,27},{2,24},{3,25},{4,18},{5,19},{6,16},{7,17},{8,30},{9,... | collective-permute-start | bytes 356360 | tf_op jit(solution)/shard_map/ppermute | solution.py:306

commit v11 on v10

--- a/solution.py
+++ b/solution.py
@@ -329,26 +329,26 @@
     near = (loaded(after(w_in, own0)), loaded(after(w_out, own0)))
     block1 = after(block1, (near, other0))
     own1, other, on0, on1 = choose(block1, capacity, ((0, 0), (0, 1), (1, 0), (1, 1)))
-    other1 = sent(other, sections, 0, 0, 1)
     own2 = sent(on0, sections, 0, 1, 0)
     other2 = sent(on1, sections, 0, 1, 1)
-    back0, back1 = after((back0, back1), other1)
-    own3 = sent(back0, sections, 0, 3, 0)
-    other3 = sent(back1, sections, 0, 3, 1)
+    own3 = sent(after(back0, own1), sections, 0, 3, 0)
+    other1 = sent(after(other, own2), sections, 0, 0, 1)
+    other3 = sent(after(back1, other2), sections, 0, 3, 1)
     pieces = (own0, other0, own1, own2, other2, other1, own3, other3)
     places = ((0, 0), (0, 1), (1, 0), (2, 0), (2, 1), (1, 1), (3, 0), (3, 1))
     slots, total = near_pass(pieces, near)
     pieces = far_pass(slots, total, (far_in, far_out), capacity)
     piece = dict(zip(places, pieces))
+    straight = [sent(piece[1, 0], sections, 1, -1, 0)]
     merged = [
         piece[3, 0],
         sent(piece[2, 0], sections, 0, 1, 0),
         sent(piece[2, 1], sections, 0, 1, 1),
         sent(piece[3, 1], sections, 0, 0, 1),
     ]
-    straight = [sent(piece[0, flip], sections, 1, 0, flip) for flip in range(2)]
+    straight.append(sent(piece[1, 1], sections, 1, -1, 1))
     merged, straight = lax.optimization_barrier((merged, straight))
-    straight += [sent(piece[1, flip], sections, 1, -1, flip) for flip in range(2)]
+    straight += [sent(piece[0, flip], sections, 1, 0, flip) for flip in range(2)]
     merged = sent(combine(merged, tok_count), sections, 1, 1, 0)
     return combine(straight, tok_count, merged)[None]
 

time: 56.6 us -> 61.2 us (1.081)
  waiting for transfers between devices: 17.3 us -> 23.6 us
  starting transfers between devices: 26.7 us -> 25.1 us
    ppermute x15, waiting for transfers between devices: 17.3 us -> 23.6 us  [sent(): return lax.ppermute(shard, ('section', 'expert'), pairs)]
    ppermute x15, starting transfers between devices: 26.2 us -> 24.6 us  [sent(): return lax.ppermute(shard, ('section', 'expert'), pairs)]
  transfers between devices with their start and end apart: 17 -> 17, of which waited for: 9 -> 11; matrix products, arithmetic and copies ran while one was open for 0% -> 0% of each run, Pallas kernels for 8% -> 7%
where the time goes in v11:
time: 61.2 us; the launch traced here: 61 us
  starting transfers between devices  25.1 us (41%)
  waiting for transfers between devices  23.6 us (39%)
  Pallas kernels  7.58 us (12%)
  local copies, waits for them, and re-layouts  4.62 us (8%)
    ppermute x15, starting transfers between devices, sent(): return lax.ppermute(shard, ('section', 'expert'), pairs)  24.6 us
    ppermute x15, waiting for transfers between devices, sent(): return lax.ppermute(shard, ('section', 'expert'), pairs)  23.6 us
    pallas_call x9, Pallas kernels, local_call(): pl.pallas_call(kernel, out_shape=out_shape, in_specs=[vmem if spec is Non...  7.58 us
    unnamed x4, local copies, waits for them, and re-layouts  4.62 us
  transfers between devices with their start and end apart: 17, of which 11 were waited for; matrix products, arithmetic and copies ran while one was open for 0% of the time, Pallas kernels for 7%

profile of v11, /device:TPU:0, one launch (start us, length us, event | category | flops | bytes accessed | tf_op | source)
XLA Modules:
  0.0 61.0 jit_solution(3722965024950000222)
XLA Ops:
  0.5 1.0 %prepare.1.block = bf16[32,3712]{1,0:T(8,128)(2,1)S(1)} custom-call(s32[2,32]{1,0:T(2,128)} %bitcast.15, f32[2,32]{1,0:T(2,128)} %bitcast.16, bf16[32,3584]{1,0:T(8,128)(2,1)} %bitcast.14), custom_call_target="tpu_custom_call" | custom-call | tf_op jit(solution)/shard_map/prepare/pallas_call | solution.py:84
  1.5 3.1 %collective-permute-start.1 = (bf16[32,3712]{1,0:T(8,128)(2,1)S(1)}, bf16[32,3712]{1,0:T(8,128)(2,1)S(1)}, u32[]{:S(2)}, u32[]{:S(2)}) collective-permute-start(bf16[32,3712]{1,0:T(8,128)(2,1)S(1)} %prepare.1.block), channel_id=1, source_target_pairs={{0,4},{1,5},{2,6},{3,7},{4,12},{5,13},{6,14},{7,15},{8,0},{9,1},{1... | collective-permute-start | bytes 712712 | tf_op jit(solution)/shard_map/ppermute | solution.py:306
  5.0 1.6 %collective-permute-start = (bf16[16,3712]{1,0:T(8,128)(2,1)S(1)}, bf16[16,3712]{1,0:T(8,128)(2,1)S(1)}, u32[]{:S(2)}, u32[]{:S(2)}) collective-permute-start(bf16[16,3712]{1,0:T(8,128)(2,1)S(1)} %get-tuple-element.36), channel_id=1, source_target_pairs={{0,2},{1,3},{2,0},{3,1},{4,6},{5,7},{6,4},{7,5},{8,10},{9,11},{10,... | collective-permute-start | bytes 356360 | tf_op jit(solution)/shard_map/ppermute | solution.py:306
  6.6 3.1 %copy-done = bf16[1,3584,1024]{2,1,0:T(8,128)(2,1)S(1)} copy-done((bf16[1,3584,1024]{2,1,0:T(8,128)(2,1)S(1)}, bf16[1,3584,1024]{2,1,0:T(8,128)(2,1)}, u32[]{:S(2)}) %copy-start) | copy-done | bytes 7340056
  10.2 1.5 %copy-done.1 = bf16[1,512,3584]{2,1,0:T(8,128)(2,1)S(1)} copy-done((bf16[1,512,3584]{2,1,0:T(8,128)(2,1)S(1)}, bf16[1,512,3584]{2,1,0:T(8,128)(2,1)}, u32[]{:S(2)}) %copy-start.1) | copy-done | bytes 3670040
  12.4 2.6 %collective-permute-start.2 = (bf16[16,3712]{1,0:T(8,128)(2,1)S(1)}, bf16[16,3712]{1,0:T(8,128)(2,1)S(1)}, u32[]{:S(2)}, u32[]{:S(2)}) collective-permute-start(bf16[16,3712]{1,0:T(8,128)(2,1)S(1)} %get-tuple-element.41), channel_id=1, source_target_pairs={{0,4},{1,5},{2,6},{3,7},{4,12},{5,13},{6,14},{7,15},{8,0},{9,1},{1... | collective-permute-start | bytes 356360 | tf_op jit(solution)/shard_map/ppermute | solution.py:306
  15.1 2.1 %collective-permute-start.3 = (bf16[16,3712]{1,0:T(8,128)(2,1)S(1)}, bf16[16,3712]{1,0:T(8,128)(2,1)S(1)}, u32[]{:S(2)}, u32[]{:S(2)}) collective-permute-start(bf16[16,3712]{1,0:T(8,128)(2,1)S(1)} %get-tuple-element.42), channel_id=1, source_target_pairs={{0,6},{1,7},{2,4},{3,5},{4,14},{5,15},{6,12},{7,13},{8,2},{9,3},{1... | collective-permute-start | bytes 356360 | tf_op jit(solution)/shard_map/ppermute | solution.py:306
  17.2 0.7 %collective-permute-start.5 = (bf16[16,3712]{1,0:T(8,128)(2,1)S(1)}, bf16[16,3712]{1,0:T(8,128)(2,1)S(1)}, u32[]{:S(2)}, u32[]{:S(2)}) collective-permute-start(bf16[16,3712]{1,0:T(8,128)(2,1)S(1)} %get-tuple-element.46), channel_id=1, source_target_pairs={{0,8},{1,9},{2,10},{3,11},{4,0},{5,1},{6,2},{7,3},{8,12},{9,13},{1... | collective-permute-start | bytes 356360 | tf_op jit(solution)/shard_map/ppermute | solution.py:306
  17.9 0.9 %collective-permute-done.2.refs_3_ = bf16[16,3712]{1,0:T(8,128)(2,1)S(1)} collective-permute-done((bf16[16,3712]{1,0:T(8,128)(2,1)S(1)}, bf16[16,3712]{1,0:T(8,128)(2,1)S(1)}, u32[]{:S(2)}, u32[]{:S(2)}) %collective-permute-start.2) | collective-permute-done | bytes 118816 | tf_op jit(solution)/shard_map/ppermute | solution.py:306
  19.5 3.3 %collective-permute-done.3.refs_4_ = bf16[16,3712]{1,0:T(8,128)(2,1)S(1)} collective-permute-done((bf16[16,3712]{1,0:T(8,128)(2,1)S(1)}, bf16[16,3712]{1,0:T(8,128)(2,1)S(1)}, u32[]{:S(2)}, u32[]{:S(2)}) %collective-permute-start.3) | collective-permute-done | bytes 118816 | tf_op jit(solution)/shard_map/ppermute | solution.py:306
  24.2 4.3 %collective-permute-done.6.refs_7_ = bf16[16,3712]{1,0:T(8,128)(2,1)S(1)} collective-permute-done((bf16[16,3712]{1,0:T(8,128)(2,1)S(1)}, bf16[16,3712]{1,0:T(8,128)(2,1)S(1)}, u32[]{:S(2)}, u32[]{:S(2)}) %collective-permute-start.6) | collective-permute-done | bytes 118816 | tf_op jit(solution)/shard_map/ppermute | solution.py:306
  28.6 1.7 %near_pass.1 = (bf16[128,3712]{1,0:T(8,128)(2,1)S(1)}, f32[128,3584]{1,0:T(8,128)S(1)}) custom-call(bf16[16,3712]{1,0:T(8,128)(2,1)S(1)} %get-tuple-element.35.refs_0_, bf16[16,3712]{1,0:T(8,128)(2,1)S(1)} %collective-permute-done.refs_1_, bf16[16,3712]{1,0:T(8,128)(2,1)S(1)} %get-tuple-element.40.refs_2_, ...), custom_call_target="tpu_custom_call" | custom-call | bytes 11010048 | tf_op jit(solution)/shard_map/near_pass/pallas_call | solution.py:84
  30.4 1.7 %far_pass.1 = (bf16[16,3712]{1,0:T(8,128)(2,1)S(1)}, bf16[16,3712]{1,0:T(8,128)(2,1)S(1)}, bf16[16,3712]{1,0:T(8,128)(2,1)S(1)}, bf16[16,3712]{1,0:T(8,128)(2,1)...) custom-call(bf16[128,3712]{1,0:T(8,128)(2,1)S(1)} %get-tuple-element, ...), custom_call_target="tpu_custom_call" | custom-call | bytes 11010048 | tf_op jit(solution)/shard_map/far_pass/pallas_call | solution.py:84
  32.1 4.0 %collective-permute-start.10 = (bf16[16,3712]{1,0:T(8,128)(2,1)S(1)}, bf16[16,3712]{1,0:T(8,128)(2,1)S(1)}, u32[]{:S(2)}, u32[]{:S(2)}) collective-permute-start(bf16[16,3712]{1,0:T(8,128)(2,1)S(1)} %get-tuple-element.53), channel_id=1, source_target_pairs={{0,6},{1,7},{2,4},{3,5},{4,14},{5,15},{6,12},{7,13},{8,2},{9,3},{1... | collective-permute-start | bytes 356360 | tf_op jit(solution)/shard_map/ppermute | solution.py:306
  36.1 1.3 %collective-permute-start.12 = (bf16[16,3712]{1,0:T(8,128)(2,1)S(1)}, bf16[16,3712]{1,0:T(8,128)(2,1)S(1)}, u32[]{:S(2)}, u32[]{:S(2)}) collective-permute-start(bf16[16,3712]{1,0:T(8,128)(2,1)S(1)} %get-tuple-element.55), channel_id=1, source_target_pairs={{0,24},{1,25},{2,26},{3,27},{4,16},{5,17},{6,18},{7,19},{8,28},{9,... | collective-permute-start | bytes 356360 | tf_op jit(solution)/shard_map/ppermute | solution.py:306
  37.4 3.2 %collective-permute-start.13 = (bf16[16,3712]{1,0:T(8,128)(2,1)S(1)}, bf16[16,3712]{1,0:T(8,128)(2,1)S(1)}, u32[]{:S(2)}, u32[]{:S(2)}) collective-permute-start(bf16[16,3712]{1,0:T(8,128)(2,1)S(1)} %get-tuple-element.56), channel_id=1, source_target_pairs={{0,26},{1,27},{2,24},{3,25},{4,18},{5,19},{6,16},{7,17},{8,30},{9,... | collective-permute-start | bytes 356360 | tf_op jit(solution)/shard_map/ppermute | solution.py:306
  40.6 1.1 %collective-permute-done.10.refs_2_ = bf16[16,3712]{1,0:T(8,128)(2,1)S(1)} collective-permute-done((bf16[16,3712]{1,0:T(8,128)(2,1)S(1)}, bf16[16,3712]{1,0:T(8,128)(2,1)S(1)}, u32[]{:S(2)}, u32[]{:S(2)}) %collective-permute-start.10) | collective-permute-done | bytes 118816 | tf_op jit(solution)/shard_map/ppermute | solution.py:306
  41.7 1.7 %collective-permute-done.12.refs_0_ = bf16[16,3712]{1,0:T(8,128)(2,1)S(1)} collective-permute-done((bf16[16,3712]{1,0:T(8,128)(2,1)S(1)}, bf16[16,3712]{1,0:T(8,128)(2,1)S(1)}, u32[]{:S(2)}, u32[]{:S(2)}) %collective-permute-start.12) | collective-permute-done | bytes 118816 | tf_op jit(solution)/shard_map/ppermute | solution.py:306
  43.4 1.3 %collective-permute-done.13.refs_1_ = bf16[16,3712]{1,0:T(8,128)(2,1)S(1)} collective-permute-done((bf16[16,3712]{1,0:T(8,128)(2,1)S(1)}, bf16[16,3712]{1,0:T(8,128)(2,1)S(1)}, u32[]{:S(2)}, u32[]{:S(2)}) %collective-permute-start.13) | collective-permute-done | bytes 118816 | tf_op jit(solution)/shard_map/ppermute | solution.py:306
  44.8 4.3 %collective-permute-done.9.refs_1_ = bf16[16,3712]{1,0:T(8,128)(2,1)S(1)} collective-permute-done((bf16[16,3712]{1,0:T(8,128)(2,1)S(1)}, bf16[16,3712]{1,0:T(8,128)(2,1)S(1)}, u32[]{:S(2)}, u32[]{:S(2)}) %collective-permute-start.9) | collective-permute-done | bytes 118816 | tf_op jit(solution)/shard_map/ppermute | solution.py:306
  50.4 3.8 %collective-permute-start.15 = (bf16[16,3712]{1,0:T(8,128)(2,1)S(1)}, bf16[16,3712]{1,0:T(8,128)(2,1)S(1)}, u32[]{:S(2)}, u32[]{:S(2)}) collective-permute-start(bf16[16,3712]{1,0:T(8,128)(2,1)S(1)} %get-tuple-element.60), channel_id=1, source_target_pairs={{0,18},{1,19},{2,16},{3,17},{4,22},{5,23},{6,20},{7,21},{8,26},{9,... | collective-permute-start | bytes 356360 | tf_op jit(solution)/shard_map/ppermute | solution.py:306
  54.1 3.5 %collective-permute-done.14.refs_2_ = bf16[16,3712]{1,0:T(8,128)(2,1)S(1)} collective-permute-done((bf16[16,3712]{1,0:T(8,128)(2,1)S(1)}, bf16[16,3712]{1,0:T(8,128)(2,1)S(1)}, u32[]{:S(2)}, u32[]{:S(2)}) %collective-permute-start.14) | collective-permute-done | bytes 118816 | tf_op jit(solution)/shard_map/ppermute | solution.py:306
  57.6 2.4 %collective-permute-done.15.refs_3_ = bf16[16,3712]{1,0:T(8,128)(2,1)S(1)} collective-permute-done((bf16[16,3712]{1,0:T(8,128)(2,1)S(1)}, bf16[16,3712]{1,0:T(8,128)(2,1)S(1)}, u32[]{:S(2)}, u32[]{:S(2)}) %collective-permute-start.15) | collective-permute-done | bytes 118816 | tf_op jit(solution)/shard_map/ppermute | solution.py:306
  59.9 1.1 %combine.3 = bf16[32,3584]{1,0:T(8,128)(2,1)} custom-call(bf16[16,3712]{1,0:T(8,128)(2,1)S(1)} %collective-permute-done.12.refs_0_, bf16[16,3712]{1,0:T(8,128)(2,1)S(1)} %collective-permute-done.13.refs_1_, bf16[16,3712]{1,0:T(8,128)(2,1)S(1)} %collective-permute-done.14.refs_2_, bf16[16,3712]{1,0:T(8,128)(2,1)S(1)} %collective-permute-done.15.refs_3_, ...), custom_call_target="tpu_custom_call" | custom-call | tf_op jit(solution)/shard_map/combine/pallas_call | solution.py:84
  (23 shorter events, 5.4 us)
Async XLA Ops:
  0.0 30.3 %collective-permute-start.7 = (bf16[3584,1024]{1,0:T(8,128)(2,1)}, bf16[3584,1024]{1,0:T(8,128)(2,1)S(1)}, u32[]{:S(2)}, u32[]{:S(2)}) collective-permute-start(bf16[3584,1024]{1,0:T(8,128)(2,1)} %bitcast.10), channel_id=1, source_target_pairs={{0,1},{1,0},{2,3},{3,2},{4,5},{5,4},{6,7},{7,6},{8,9},{9,8},{10,11... | collective-permute-start | bytes 22020104 | tf_op jit(solution)/shard_map/ppermute | solution.py:324
  0.5 29.9 %collective-permute-start.8 = (bf16[512,3584]{1,0:T(8,128)(2,1)}, bf16[512,3584]{1,0:T(8,128)(2,1)S(1)}, u32[]{:S(2)}, u32[]{:S(2)}) collective-permute-start(bf16[512,3584]{1,0:T(8,128)(2,1)} %bitcast.12), channel_id=1, source_target_pairs={{0,1},{1,0},{2,3},{3,2},{4,5},{5,4},{6,7},{7,6},{8,9},{9,8},{10,11... | collective-permute-start | bytes 11010056 | tf_op jit(solution)/shard_map/ppermute | solution.py:323
  1.5 10.5 %collective-permute-start.1 = (bf16[32,3712]{1,0:T(8,128)(2,1)S(1)}, bf16[32,3712]{1,0:T(8,128)(2,1)S(1)}, u32[]{:S(2)}, u32[]{:S(2)}) collective-permute-start(bf16[32,3712]{1,0:T(8,128)(2,1)S(1)} %prepare.1.block), channel_id=1, source_target_pairs={{0,4},{1,5},{2,6},{3,7},{4,12},{5,13},{6,14},{7,15},{8,0},{9,1},{1... | collective-permute-start | bytes 712712 | tf_op jit(solution)/shard_map/ppermute | solution.py:306
  5.0 7.0 %collective-permute-start = (bf16[16,3712]{1,0:T(8,128)(2,1)S(1)}, bf16[16,3712]{1,0:T(8,128)(2,1)S(1)}, u32[]{:S(2)}, u32[]{:S(2)}) collective-permute-start(bf16[16,3712]{1,0:T(8,128)(2,1)S(1)} %get-tuple-element.36), channel_id=1, source_target_pairs={{0,2},{1,3},{2,0},{3,1},{4,6},{5,7},{6,4},{7,5},{8,10},{9,11},{10,... | collective-permute-start | bytes 356360 | tf_op jit(solution)/shard_map/ppermute | solution.py:306
  6.6 3.1 %copy-start = (bf16[1,3584,1024]{2,1,0:T(8,128)(2,1)S(1)}, bf16[1,3584,1024]{2,1,0:T(8,128)(2,1)}, u32[]{:S(2)}) copy-start(bf16[1,3584,1024]{2,1,0:T(8,128)(2,1)} %param.8) | copy-start | bytes 22020100
  9.7 2.0 %copy-start.1 = (bf16[1,512,3584]{2,1,0:T(8,128)(2,1)S(1)}, bf16[1,512,3584]{2,1,0:T(8,128)(2,1)}, u32[]{:S(2)}) copy-start(bf16[1,512,3584]{2,1,0:T(8,128)(2,1)} %param.9) | copy-start | bytes 11010052
  12.4 6.4 %collective-permute-start.2 = (bf16[16,3712]{1,0:T(8,128)(2,1)S(1)}, bf16[16,3712]{1,0:T(8,128)(2,1)S(1)}, u32[]{:S(2)}, u32[]{:S(2)}) collective-permute-start(bf16[16,3712]{1,0:T(8,128)(2,1)S(1)} %get-tuple-element.41), channel_id=1, source_target_pairs={{0,4},{1,5},{2,6},{3,7},{4,12},{5,13},{6,14},{7,15},{8,0},{9,1},{1... | collective-permute-start | bytes 356360 | tf_op jit(solution)/shard_map/ppermute | solution.py:306
  15.1 7.8 %collective-permute-start.3 = (bf16[16,3712]{1,0:T(8,128)(2,1)S(1)}, bf16[16,3712]{1,0:T(8,128)(2,1)S(1)}, u32[]{:S(2)}, u32[]{:S(2)}) collective-permute-start(bf16[16,3712]{1,0:T(8,128)(2,1)S(1)} %get-tuple-element.42), channel_id=1, source_target_pairs={{0,6},{1,7},{2,4},{3,5},{4,14},{5,15},{6,12},{7,13},{8,2},{9,3},{1... | collective-permute-start | bytes 356360 | tf_op jit(solution)/shard_map/ppermute | solution.py:306
  17.2 6.5 %collective-permute-start.5 = (bf16[16,3712]{1,0:T(8,128)(2,1)S(1)}, bf16[16,3712]{1,0:T(8,128)(2,1)S(1)}, u32[]{:S(2)}, u32[]{:S(2)}) collective-permute-start(bf16[16,3712]{1,0:T(8,128)(2,1)S(1)} %get-tuple-element.46), channel_id=1, source_target_pairs={{0,8},{1,9},{2,10},{3,11},{4,0},{5,1},{6,2},{7,3},{8,12},{9,13},{1... | collective-permute-start | bytes 356360 | tf_op jit(solution)/shard_map/ppermute | solution.py:306
  18.9 5.4 %collective-permute-start.4 = (bf16[16,3712]{1,0:T(8,128)(2,1)S(1)}, bf16[16,3712]{1,0:T(8,128)(2,1)S(1)}, u32[]{:S(2)}, u32[]{:S(2)}) collective-permute-start(bf16[16,3712]{1,0:T(8,128)(2,1)S(1)} %get-tuple-element.44), channel_id=1, source_target_pairs={{0,2},{1,3},{2,0},{3,1},{4,6},{5,7},{6,4},{7,5},{8,10},{9,11},{10,... | collective-permute-start | bytes 356360 | tf_op jit(solution)/shard_map/ppermute | solution.py:306
  22.9 5.7 %collective-permute-start.6 = (bf16[16,3712]{1,0:T(8,128)(2,1)S(1)}, bf16[16,3712]{1,0:T(8,128)(2,1)S(1)}, u32[]{:S(2)}, u32[]{:S(2)}) collective-permute-start(bf16[16,3712]{1,0:T(8,128)(2,1)S(1)} %get-tuple-element.48), channel_id=1, source_target_pairs={{0,10},{1,11},{2,8},{3,9},{4,2},{5,3},{6,0},{7,1},{8,14},{9,15},{1... | collective-permute-start | bytes 356360 | tf_op jit(solution)/shard_map/ppermute | solution.py:306
  32.1 9.6 %collective-permute-start.10 = (bf16[16,3712]{1,0:T(8,128)(2,1)S(1)}, bf16[16,3712]{1,0:T(8,128)(2,1)S(1)}, u32[]{:S(2)}, u32[]{:S(2)}) collective-permute-start(bf16[16,3712]{1,0:T(8,128)(2,1)S(1)} %get-tuple-element.53), channel_id=1, source_target_pairs={{0,6},{1,7},{2,4},{3,5},{4,14},{5,15},{6,12},{7,13},{8,2},{9,3},{1... | collective-permute-start | bytes 356360 | tf_op jit(solution)/shard_map/ppermute | solution.py:306
  36.1 5.6 %collective-permute-start.11 = (bf16[16,3712]{1,0:T(8,128)(2,1)S(1)}, bf16[16,3712]{1,0:T(8,128)(2,1)S(1)}, u32[]{:S(2)}, u32[]{:S(2)}) collective-permute-start(bf16[16,3712]{1,0:T(8,128)(2,1)S(1)} %get-tuple-element.54), channel_id=1, source_target_pairs={{0,2},{1,3},{2,0},{3,1},{4,6},{5,7},{6,4},{7,5},{8,10},{9,11},{10,... | collective-permute-start | bytes 356360 | tf_op jit(solution)/shard_map/ppermute | solution.py:306
  36.1 7.3 %collective-permute-start.12 = (bf16[16,3712]{1,0:T(8,128)(2,1)S(1)}, bf16[16,3712]{1,0:T(8,128)(2,1)S(1)}, u32[]{:S(2)}, u32[]{:S(2)}) collective-permute-start(bf16[16,3712]{1,0:T(8,128)(2,1)S(1)} %get-tuple-element.55), channel_id=1, source_target_pairs={{0,24},{1,25},{2,26},{3,27},{4,16},{5,17},{6,18},{7,19},{8,28},{9,... | collective-permute-start | bytes 356360 | tf_op jit(solution)/shard_map/ppermute | solution.py:306
  37.4 7.3 %collective-permute-start.13 = (bf16[16,3712]{1,0:T(8,128)(2,1)S(1)}, bf16[16,3712]{1,0:T(8,128)(2,1)S(1)}, u32[]{:S(2)}, u32[]{:S(2)}) collective-permute-start(bf16[16,3712]{1,0:T(8,128)(2,1)S(1)} %get-tuple-element.56), channel_id=1, source_target_pairs={{0,26},{1,27},{2,24},{3,25},{4,18},{5,19},{6,16},{7,17},{8,30},{9,... | collective-permute-start | bytes 356360 | tf_op jit(solution)/shard_map/ppermute | solution.py:306
  40.6 8.5 %collective-permute-start.9 = (bf16[16,3712]{1,0:T(8,128)(2,1)S(1)}, bf16[16,3712]{1,0:T(8,128)(2,1)S(1)}, u32[]{:S(2)}, u32[]{:S(2)}) collective-permute-start(bf16[16,3712]{1,0:T(8,128)(2,1)S(1)} %get-tuple-element.52), channel_id=1, source_target_pairs={{0,4},{1,5},{2,6},{3,7},{4,12},{5,13},{6,14},{7,15},{8,0},{9,1},{1... | collective-permute-start | bytes 356360 | tf_op jit(solution)/shard_map/ppermute | solution.py:306
  49.6 10.4 %collective-permute-start.16 = (bf16[32,3584]{1,0:T(8,128)(2,1)S(1)}, bf16[32,3584]{1,0:T(8,128)(2,1)S(1)}, u32[]{:S(2)}, u32[]{:S(2)}) collective-permute-start(bf16[32,3584]{1,0:T(8,128)(2,1)S(1)} %combine.2), channel_id=1, source_target_pairs={{0,20},{1,21},{2,22},{3,23},{4,28},{5,29},{6,30},{7,31},{8,16},{9,... | collective-permute-start | bytes 688136 | tf_op jit(solution)/shard_map/ppermute | solution.py:306
  50.3 7.3 %collective-permute-start.14 = (bf16[16,3712]{1,0:T(8,128)(2,1)S(1)}, bf16[16,3712]{1,0:T(8,128)(2,1)S(1)}, u32[]{:S(2)}, u32[]{:S(2)}) collective-permute-start(bf16[16,3712]{1,0:T(8,128)(2,1)S(1)} %get-tuple-element.59), channel_id=1, source_target_pairs={{0,16},{1,17},{2,18},{3,19},{4,20},{5,21},{6,22},{7,23},{8,24},{9,... | collective-permute-start | bytes 356360 | tf_op jit(solution)/shard_map/ppermute | solution.py:306
  50.4 9.6 %collective-permute-start.15 = (bf16[16,3712]{1,0:T(8,128)(2,1)S(1)}, bf16[16,3712]{1,0:T(8,128)(2,1)S(1)}, u32[]{:S(2)}, u32[]{:S(2)}) collective-permute-start(bf16[16,3712]{1,0:T(8,128)(2,1)S(1)} %get-tuple-element.60), channel_id=1, source_target_pairs={{0,18},{1,19},{2,16},{3,17},{4,22},{5,23},{6,20},{7,21},{8,26},{9,... | collective-permute-start | bytes 356360 | tf_op jit(solution)/shard_map/ppermute | solution.py:306

commit v12 on v10

--- a/solution.py
+++ b/solution.py
@@ -264,31 +264,74 @@
     )
 
 
+PARTS = 7
+
+
 def combine_kernel(count, *refs):
-    blocks, more, (out, slots) = refs[:count], refs[count:-2], refs[-2:]
+    blocks, more, (out, slots, mixed, sems) = refs[:count], refs[count:-4], refs[-4:]
     tok_count, width = out.shape
     start = 0
     for block in blocks:
         slots[start : start + block.shape[0]] = block[...]
         start += block.shape[0]
     token = slots[:, width:]
-    part = width // 7
-    for at in range(7):
-        place = slice(at * part, (at + 1) * part)
-        mixed = across(token, slots[:, place])[TOKEN_LANE : TOKEN_LANE + tok_count]
+    part = width // PARTS
+    copies = []
+    for at in range(PARTS):
+        place = pl.ds(at * part, part)
+        total = across(token, slots[:, place])[TOKEN_LANE : TOKEN_LANE + tok_count]
         for other in more:
-            mixed = mixed + other[:, place].astype(jnp.float32)
-        out[:, place] = mixed.astype(out.dtype)
+            total = total + other[:, place].astype(jnp.float32)
+        mixed[:, place] = total.astype(out.dtype)
+        copies.append(
+            pltpu.make_async_copy(mixed.at[:, place], out.at[:, place], sems.at[at])
+        )
+        copies[-1].start()
+    for copy in copies:
+        copy.wait()
 
 
 def combine(blocks, tok_count, *more):
     capacity, full = blocks[0].shape
-    return local_call(
+    shape = (tok_count, full - LANES)
+    return pl.pallas_call(
         functools.partial(combine_kernel, len(blocks)),
-        "combine",
+        out_shape=jax.ShapeDtypeStruct(shape, jnp.bfloat16),
+        in_specs=[pl.BlockSpec(memory_space=pltpu.VMEM)] * (len(blocks) + len(more)),
+        out_specs=pl.BlockSpec(memory_space=pl.ANY),
+        scratch_shapes=[
+            pltpu.VMEM((capacity * len(blocks), full), jnp.bfloat16),
+            pltpu.VMEM(shape, jnp.bfloat16),
+            pltpu.SemaphoreType.DMA((PARTS,)),
+        ],
+        compiler_params=pltpu.CompilerParams(vmem_limit_bytes=12 << 20),
+        name="combine",
+    )(*blocks, *more)
+
+
+def merge_kernel(*refs):
+    blocks, (out, slots) = refs[:-2], refs[-2:]
+    tok_count, width = out.shape
+    start = 0
+    for block in blocks:
+        slots[start : start + block.shape[0]] = block[...]
+        start += block.shape[0]
+    token = slots[:, width:]
+    part = width // PARTS
+    for at in range(PARTS):
+        place = pl.ds(at * part, part)
+        total = across(token, slots[:, place])[TOKEN_LANE : TOKEN_LANE + tok_count]
+        out[:, place] = total.astype(out.dtype)
+
+
+def merge(blocks, tok_count):
+    capacity, full = blocks[0].shape
+    return local_call(
+        merge_kernel,
+        "merge",
         jax.ShapeDtypeStruct((tok_count, full - LANES), jnp.bfloat16),
-        [None] * (len(blocks) + len(more)),
-        (*blocks, *more),
+        [None] * len(blocks),
+        tuple(blocks),
         [pltpu.VMEM((capacity * len(blocks), full), jnp.bfloat16)],
     )
 
@@ -340,16 +383,18 @@
     slots, total = near_pass(pieces, near)
     pieces = far_pass(slots, total, (far_in, far_out), capacity)
     piece = dict(zip(places, pieces))
+    straight = [sent(piece[0, 0], sections, 1, 0, 0)]
     merged = [
         piece[3, 0],
         sent(piece[2, 0], sections, 0, 1, 0),
         sent(piece[2, 1], sections, 0, 1, 1),
         sent(piece[3, 1], sections, 0, 0, 1),
     ]
-    straight = [sent(piece[0, flip], sections, 1, 0, flip) for flip in range(2)]
-    merged, straight = lax.optimization_barrier((merged, straight))
+    straight.append(sent(piece[0, 1], sections, 1, 0, 1))
+    first, *merged, last = lax.optimization_barrier([straight[0], *merged, straight[1]])
+    straight = [first, last]
     straight += [sent(piece[1, flip], sections, 1, -1, flip) for flip in range(2)]
-    merged = sent(combine(merged, tok_count), sections, 1, 1, 0)
+    merged = sent(merge(merged, tok_count), sections, 1, 1, 0)
     return combine(straight, tok_count, merged)[None]
 
 

time: 56.6 us -> 59.2 us (1.046)
  waiting for transfers between devices: 17.3 us -> 20.2 us
    ppermute x15, waiting for transfers between devices: 17.3 us -> 20.2 us  [sent(): return lax.ppermute(shard, ('section', 'expert'), pairs)]
    pallas_call x9 -> x8, Pallas kernels: 7.6 us -> 6.5 us  [local_call(): pl.pallas_call(kernel, out_shape=out_shape, in_specs=[vmem if spec is Non...]
    pallas_call x0 -> x1, Pallas kernels: none -> 1.1 us  [combine(): pl.pallas_call(functools.partial(combine_kernel, len(blocks)), out_shape=...]
  transfers between devices with their start and end apart: 17 -> 17, of which waited for: 9 -> 8; matrix products, arithmetic and copies ran while one was open for 0% -> 0% of each run, Pallas kernels for 8% -> 7%
where the time goes in v12:
time: 59.2 us; the launch traced here: 59 us
  starting transfers between devices  26.5 us (45%)
  waiting for transfers between devices  20.2 us (34%)
  Pallas kernels  7.6 us (13%)
  local copies, waits for them, and re-layouts  4.62 us (8%)
    ppermute x15, starting transfers between devices, sent(): return lax.ppermute(shard, ('section', 'expert'), pairs)  26 us
    ppermute x15, waiting for transfers between devices, sent(): return lax.ppermute(shard, ('section', 'expert'), pairs)  20.2 us
    pallas_call x8, Pallas kernels, local_call(): pl.pallas_call(kernel, out_shape=out_shape, in_specs=[vmem if spec is Non...  6.5 us
    unnamed x4, local copies, waits for them, and re-layouts  4.62 us
  transfers between devices with their start and end apart: 17, of which 8 were waited for; matrix products, arithmetic and copies ran while one was open for 0% of the time, Pallas kernels for 7%

profile of v12, /device:TPU:0, one launch (start us, length us, event | category | flops | bytes accessed | tf_op | source)
XLA Modules:
  0.0 59.0 jit_solution(14069351178577201242)
XLA Ops:
  1.5 3.1 %collective-permute-start.1 = (bf16[32,3712]{1,0:T(8,128)(2,1)S(1)}, bf16[32,3712]{1,0:T(8,128)(2,1)S(1)}, u32[]{:S(2)}, u32[]{:S(2)}) collective-permute-start(bf16[32,3712]{1,0:T(8,128)(2,1)S(1)} %prepare.1.block), channel_id=1, source_target_pairs={{0,4},{1,5},{2,6},{3,7},{4,12},{5,13},{6,14},{7,15},{8,0},{9,1},{1... | collective-permute-start | bytes 712712 | tf_op jit(solution)/shard_map/ppermute | solution.py:349
  5.0 1.6 %collective-permute-start = (bf16[16,3712]{1,0:T(8,128)(2,1)S(1)}, bf16[16,3712]{1,0:T(8,128)(2,1)S(1)}, u32[]{:S(2)}, u32[]{:S(2)}) collective-permute-start(bf16[16,3712]{1,0:T(8,128)(2,1)S(1)} %get-tuple-element.35), channel_id=1, source_target_pairs={{0,2},{1,3},{2,0},{3,1},{4,6},{5,7},{6,4},{7,5},{8,10},{9,11},{10,... | collective-permute-start | bytes 356360 | tf_op jit(solution)/shard_map/ppermute | solution.py:349
  6.6 3.1 %copy-done = bf16[1,3584,1024]{2,1,0:T(8,128)(2,1)S(1)} copy-done((bf16[1,3584,1024]{2,1,0:T(8,128)(2,1)S(1)}, bf16[1,3584,1024]{2,1,0:T(8,128)(2,1)}, u32[]{:S(2)}) %copy-start) | copy-done | bytes 7340056
  10.2 1.5 %copy-done.1 = bf16[1,512,3584]{2,1,0:T(8,128)(2,1)S(1)} copy-done((bf16[1,512,3584]{2,1,0:T(8,128)(2,1)S(1)}, bf16[1,512,3584]{2,1,0:T(8,128)(2,1)}, u32[]{:S(2)}) %copy-start.1) | copy-done | bytes 3670040
  12.4 1.2 %collective-permute-start.4 = (bf16[16,3712]{1,0:T(8,128)(2,1)S(1)}, bf16[16,3712]{1,0:T(8,128)(2,1)S(1)}, u32[]{:S(2)}, u32[]{:S(2)}) collective-permute-start(bf16[16,3712]{1,0:T(8,128)(2,1)S(1)} %get-tuple-element.42), channel_id=1, source_target_pairs={{0,2},{1,3},{2,0},{3,1},{4,6},{5,7},{6,4},{7,5},{8,10},{9,11},{10,... | collective-permute-start | bytes 356360 | tf_op jit(solution)/shard_map/ppermute | solution.py:349
  13.6 2.0 %collective-permute-start.2 = (bf16[16,3712]{1,0:T(8,128)(2,1)S(1)}, bf16[16,3712]{1,0:T(8,128)(2,1)S(1)}, u32[]{:S(2)}, u32[]{:S(2)}) collective-permute-start(bf16[16,3712]{1,0:T(8,128)(2,1)S(1)} %get-tuple-element.40), channel_id=1, source_target_pairs={{0,4},{1,5},{2,6},{3,7},{4,12},{5,13},{6,14},{7,15},{8,0},{9,1},{1... | collective-permute-start | bytes 356360 | tf_op jit(solution)/shard_map/ppermute | solution.py:349
  15.6 2.1 %collective-permute-start.3 = (bf16[16,3712]{1,0:T(8,128)(2,1)S(1)}, bf16[16,3712]{1,0:T(8,128)(2,1)S(1)}, u32[]{:S(2)}, u32[]{:S(2)}) collective-permute-start(bf16[16,3712]{1,0:T(8,128)(2,1)S(1)} %get-tuple-element.41), channel_id=1, source_target_pairs={{0,6},{1,7},{2,4},{3,5},{4,14},{5,15},{6,12},{7,13},{8,2},{9,3},{1... | collective-permute-start | bytes 356360 | tf_op jit(solution)/shard_map/ppermute | solution.py:349
  17.7 1.7 %collective-permute-start.5 = (bf16[16,3712]{1,0:T(8,128)(2,1)S(1)}, bf16[16,3712]{1,0:T(8,128)(2,1)S(1)}, u32[]{:S(2)}, u32[]{:S(2)}) collective-permute-start(bf16[16,3712]{1,0:T(8,128)(2,1)S(1)} %get-tuple-element.45), channel_id=1, source_target_pairs={{0,8},{1,9},{2,10},{3,11},{4,0},{5,1},{6,2},{7,3},{8,12},{9,13},{1... | collective-permute-start | bytes 356360 | tf_op jit(solution)/shard_map/ppermute | solution.py:349
  19.9 2.2 %collective-permute-start.6 = (bf16[16,3712]{1,0:T(8,128)(2,1)S(1)}, bf16[16,3712]{1,0:T(8,128)(2,1)S(1)}, u32[]{:S(2)}, u32[]{:S(2)}) collective-permute-start(bf16[16,3712]{1,0:T(8,128)(2,1)S(1)} %get-tuple-element.46), channel_id=1, source_target_pairs={{0,10},{1,11},{2,8},{3,9},{4,2},{5,3},{6,0},{7,1},{8,14},{9,15},{1... | collective-permute-start | bytes 356360 | tf_op jit(solution)/shard_map/ppermute | solution.py:349
  22.1 4.1 %collective-permute-done.3.refs_4_ = bf16[16,3712]{1,0:T(8,128)(2,1)S(1)} collective-permute-done((bf16[16,3712]{1,0:T(8,128)(2,1)S(1)}, bf16[16,3712]{1,0:T(8,128)(2,1)S(1)}, u32[]{:S(2)}, u32[]{:S(2)}) %collective-permute-start.3) | collective-permute-done | bytes 118816 | tf_op jit(solution)/shard_map/ppermute | solution.py:349
  26.2 1.2 %collective-permute-done.6.refs_7_ = bf16[16,3712]{1,0:T(8,128)(2,1)S(1)} collective-permute-done((bf16[16,3712]{1,0:T(8,128)(2,1)S(1)}, bf16[16,3712]{1,0:T(8,128)(2,1)S(1)}, u32[]{:S(2)}, u32[]{:S(2)}) %collective-permute-start.6) | collective-permute-done | bytes 118816 | tf_op jit(solution)/shard_map/ppermute | solution.py:349
  27.3 1.8 %near_pass.1 = (bf16[128,3712]{1,0:T(8,128)(2,1)S(1)}, f32[128,3584]{1,0:T(8,128)S(1)}) custom-call(bf16[16,3712]{1,0:T(8,128)(2,1)S(1)} %get-tuple-element.34.refs_0_, bf16[16,3712]{1,0:T(8,128)(2,1)S(1)} %collective-permute-done.refs_1_, bf16[16,3712]{1,0:T(8,128)(2,1)S(1)} %get-tuple-element.39.refs_2_, ...), custom_call_target="tpu_custom_call" | custom-call | bytes 11010048 | tf_op jit(solution)/shard_map/near_pass/pallas_call | solution.py:84
  29.1 1.7 %far_pass.1 = (bf16[16,3712]{1,0:T(8,128)(2,1)S(1)}, bf16[16,3712]{1,0:T(8,128)(2,1)S(1)}, bf16[16,3712]{1,0:T(8,128)(2,1)S(1)}, bf16[16,3712]{1,0:T(8,128)(2,1)...) custom-call(bf16[128,3712]{1,0:T(8,128)(2,1)S(1)} %get-tuple-element, ...), custom_call_target="tpu_custom_call" | custom-call | bytes 11010048 | tf_op jit(solution)/shard_map/far_pass/pallas_call | solution.py:84
  30.9 1.0 %collective-permute-start.10 = (bf16[16,3712]{1,0:T(8,128)(2,1)S(1)}, bf16[16,3712]{1,0:T(8,128)(2,1)S(1)}, u32[]{:S(2)}, u32[]{:S(2)}) collective-permute-start(bf16[16,3712]{1,0:T(8,128)(2,1)S(1)} %get-tuple-element.51), channel_id=1, source_target_pairs={{0,4},{1,5},{2,6},{3,7},{4,12},{5,13},{6,14},{7,15},{8,0},{9,1},{1... | collective-permute-start | bytes 356360 | tf_op jit(solution)/shard_map/ppermute | solution.py:349
  31.9 2.9 %collective-permute-start.11 = (bf16[16,3712]{1,0:T(8,128)(2,1)S(1)}, bf16[16,3712]{1,0:T(8,128)(2,1)S(1)}, u32[]{:S(2)}, u32[]{:S(2)}) collective-permute-start(bf16[16,3712]{1,0:T(8,128)(2,1)S(1)} %get-tuple-element.52), channel_id=1, source_target_pairs={{0,6},{1,7},{2,4},{3,5},{4,14},{5,15},{6,12},{7,13},{8,2},{9,3},{1... | collective-permute-start | bytes 356360 | tf_op jit(solution)/shard_map/ppermute | solution.py:349
  35.3 2.5 %collective-permute-start.13 = (bf16[16,3712]{1,0:T(8,128)(2,1)S(1)}, bf16[16,3712]{1,0:T(8,128)(2,1)S(1)}, u32[]{:S(2)}, u32[]{:S(2)}) collective-permute-start(bf16[16,3712]{1,0:T(8,128)(2,1)S(1)} %get-tuple-element.54), channel_id=1, source_target_pairs={{0,18},{1,19},{2,16},{3,17},{4,22},{5,23},{6,20},{7,21},{8,26},{9,... | collective-permute-start | bytes 356360 | tf_op jit(solution)/shard_map/ppermute | solution.py:349
  38.3 2.0 %collective-permute-done.11.refs_2_ = bf16[16,3712]{1,0:T(8,128)(2,1)S(1)} collective-permute-done((bf16[16,3712]{1,0:T(8,128)(2,1)S(1)}, bf16[16,3712]{1,0:T(8,128)(2,1)S(1)}, u32[]{:S(2)}, u32[]{:S(2)}) %collective-permute-start.11) | collective-permute-done | bytes 118816 | tf_op jit(solution)/shard_map/ppermute | solution.py:349
  40.3 3.2 %collective-permute-done.12.refs_3_ = bf16[16,3712]{1,0:T(8,128)(2,1)S(1)} collective-permute-done((bf16[16,3712]{1,0:T(8,128)(2,1)S(1)}, bf16[16,3712]{1,0:T(8,128)(2,1)S(1)}, u32[]{:S(2)}, u32[]{:S(2)}) %collective-permute-start.12) | collective-permute-done | bytes 118816 | tf_op jit(solution)/shard_map/ppermute | solution.py:349
  43.9 1.1 %collective-permute-start.16 = (bf16[32,3584]{1,0:T(8,128)(2,1)S(1)}, bf16[32,3584]{1,0:T(8,128)(2,1)S(1)}, u32[]{:S(2)}, u32[]{:S(2)}) collective-permute-start(bf16[32,3584]{1,0:T(8,128)(2,1)S(1)} %merge.1), channel_id=1, source_target_pairs={{0,20},{1,21},{2,22},{3,23},{4,28},{5,29},{6,30},{7,31},{8,16},{9,... | collective-permute-start | bytes 688136 | tf_op jit(solution)/shard_map/ppermute | solution.py:349
  45.1 2.7 %collective-permute-start.14 = (bf16[16,3712]{1,0:T(8,128)(2,1)S(1)}, bf16[16,3712]{1,0:T(8,128)(2,1)S(1)}, u32[]{:S(2)}, u32[]{:S(2)}) collective-permute-start(bf16[16,3712]{1,0:T(8,128)(2,1)S(1)} %get-tuple-element.57), channel_id=1, source_target_pairs={{0,24},{1,25},{2,26},{3,27},{4,16},{5,17},{6,18},{7,19},{8,28},{9,... | collective-permute-start | bytes 356360 | tf_op jit(solution)/shard_map/ppermute | solution.py:349
  48.6 5.7 %collective-permute-done.14.refs_2_ = bf16[16,3712]{1,0:T(8,128)(2,1)S(1)} collective-permute-done((bf16[16,3712]{1,0:T(8,128)(2,1)S(1)}, bf16[16,3712]{1,0:T(8,128)(2,1)S(1)}, u32[]{:S(2)}, u32[]{:S(2)}) %collective-permute-start.14) | collective-permute-done | bytes 118816 | tf_op jit(solution)/shard_map/ppermute | solution.py:349
  54.3 2.6 %collective-permute-done.15.refs_3_ = bf16[16,3712]{1,0:T(8,128)(2,1)S(1)} collective-permute-done((bf16[16,3712]{1,0:T(8,128)(2,1)S(1)}, bf16[16,3712]{1,0:T(8,128)(2,1)S(1)}, u32[]{:S(2)}, u32[]{:S(2)}) %collective-permute-start.15) | collective-permute-done | bytes 118816 | tf_op jit(solution)/shard_map/ppermute | solution.py:349
  56.9 1.0 %collective-permute-done.16.refs_4_ = bf16[32,3584]{1,0:T(8,128)(2,1)S(1)} collective-permute-done((bf16[32,3584]{1,0:T(8,128)(2,1)S(1)}, bf16[32,3584]{1,0:T(8,128)(2,1)S(1)}, u32[]{:S(2)}, u32[]{:S(2)}) %collective-permute-start.16) | collective-permute-done | bytes 229408 | tf_op jit(solution)/shard_map/ppermute | solution.py:349
  57.9 1.1 %combine.1 = bf16[32,3584]{1,0:T(8,128)(2,1)} custom-call(bf16[16,3712]{1,0:T(8,128)(2,1)S(1)} %collective-permute-done.9.refs_0_, bf16[16,3712]{1,0:T(8,128)(2,1)S(1)} %collective-permute-done.13.refs_1_, bf16[16,3712]{1,0:T(8,128)(2,1)S(1)} %collective-permute-done.14.refs_2_, bf16[16,3712]{1,0:T(8,128)(2,1)S(1)} %collective-permute-done.15.refs_3_, ...), custom_call_target="tpu_custom_call" | custom-call | tf_op jit(solution)/shard_map/combine/pallas_call | solution.py:297
  (23 shorter events, 5.7 us)
Async XLA Ops:
  0.0 29.1 %collective-permute-start.7 = (bf16[3584,1024]{1,0:T(8,128)(2,1)}, bf16[3584,1024]{1,0:T(8,128)(2,1)S(1)}, u32[]{:S(2)}, u32[]{:S(2)}) collective-permute-start(bf16[3584,1024]{1,0:T(8,128)(2,1)} %bitcast.10), channel_id=1, source_target_pairs={{0,1},{1,0},{2,3},{3,2},{4,5},{5,4},{6,7},{7,6},{8,9},{9,8},{10,11... | collective-permute-start | bytes 22020104 | tf_op jit(solution)/shard_map/ppermute | solution.py:367
  0.5 28.6 %collective-permute-start.8 = (bf16[512,3584]{1,0:T(8,128)(2,1)}, bf16[512,3584]{1,0:T(8,128)(2,1)S(1)}, u32[]{:S(2)}, u32[]{:S(2)}) collective-permute-start(bf16[512,3584]{1,0:T(8,128)(2,1)} %bitcast.12), channel_id=1, source_target_pairs={{0,1},{1,0},{2,3},{3,2},{4,5},{5,4},{6,7},{7,6},{8,9},{9,8},{10,11... | collective-permute-start | bytes 11010056 | tf_op jit(solution)/shard_map/ppermute | solution.py:366
  1.5 10.5 %collective-permute-start.1 = (bf16[32,3712]{1,0:T(8,128)(2,1)S(1)}, bf16[32,3712]{1,0:T(8,128)(2,1)S(1)}, u32[]{:S(2)}, u32[]{:S(2)}) collective-permute-start(bf16[32,3712]{1,0:T(8,128)(2,1)S(1)} %prepare.1.block), channel_id=1, source_target_pairs={{0,4},{1,5},{2,6},{3,7},{4,12},{5,13},{6,14},{7,15},{8,0},{9,1},{1... | collective-permute-start | bytes 712712 | tf_op jit(solution)/shard_map/ppermute | solution.py:349
  5.0 7.0 %collective-permute-start = (bf16[16,3712]{1,0:T(8,128)(2,1)S(1)}, bf16[16,3712]{1,0:T(8,128)(2,1)S(1)}, u32[]{:S(2)}, u32[]{:S(2)}) collective-permute-start(bf16[16,3712]{1,0:T(8,128)(2,1)S(1)} %get-tuple-element.35), channel_id=1, source_target_pairs={{0,2},{1,3},{2,0},{3,1},{4,6},{5,7},{6,4},{7,5},{8,10},{9,11},{10,... | collective-permute-start | bytes 356360 | tf_op jit(solution)/shard_map/ppermute | solution.py:349
  6.6 3.1 %copy-start = (bf16[1,3584,1024]{2,1,0:T(8,128)(2,1)S(1)}, bf16[1,3584,1024]{2,1,0:T(8,128)(2,1)}, u32[]{:S(2)}) copy-start(bf16[1,3584,1024]{2,1,0:T(8,128)(2,1)} %param.8) | copy-start | bytes 22020100
  9.7 2.0 %copy-start.1 = (bf16[1,512,3584]{2,1,0:T(8,128)(2,1)S(1)}, bf16[1,512,3584]{2,1,0:T(8,128)(2,1)}, u32[]{:S(2)}) copy-start(bf16[1,512,3584]{2,1,0:T(8,128)(2,1)} %param.9) | copy-start | bytes 11010052
  12.4 5.3 %collective-permute-start.4 = (bf16[16,3712]{1,0:T(8,128)(2,1)S(1)}, bf16[16,3712]{1,0:T(8,128)(2,1)S(1)}, u32[]{:S(2)}, u32[]{:S(2)}) collective-permute-start(bf16[16,3712]{1,0:T(8,128)(2,1)S(1)} %get-tuple-element.42), channel_id=1, source_target_pairs={{0,2},{1,3},{2,0},{3,1},{4,6},{5,7},{6,4},{7,5},{8,10},{9,11},{10,... | collective-permute-start | bytes 356360 | tf_op jit(solution)/shard_map/ppermute | solution.py:349
  13.6 6.3 %collective-permute-start.2 = (bf16[16,3712]{1,0:T(8,128)(2,1)S(1)}, bf16[16,3712]{1,0:T(8,128)(2,1)S(1)}, u32[]{:S(2)}, u32[]{:S(2)}) collective-permute-start(bf16[16,3712]{1,0:T(8,128)(2,1)S(1)} %get-tuple-element.40), channel_id=1, source_target_pairs={{0,4},{1,5},{2,6},{3,7},{4,12},{5,13},{6,14},{7,15},{8,0},{9,1},{1... | collective-permute-start | bytes 356360 | tf_op jit(solution)/shard_map/ppermute | solution.py:349
  15.6 10.6 %collective-permute-start.3 = (bf16[16,3712]{1,0:T(8,128)(2,1)S(1)}, bf16[16,3712]{1,0:T(8,128)(2,1)S(1)}, u32[]{:S(2)}, u32[]{:S(2)}) collective-permute-start(bf16[16,3712]{1,0:T(8,128)(2,1)S(1)} %get-tuple-element.41), channel_id=1, source_target_pairs={{0,6},{1,7},{2,4},{3,5},{4,14},{5,15},{6,12},{7,13},{8,2},{9,3},{1... | collective-permute-start | bytes 356360 | tf_op jit(solution)/shard_map/ppermute | solution.py:349
  17.7 8.4 %collective-permute-start.5 = (bf16[16,3712]{1,0:T(8,128)(2,1)S(1)}, bf16[16,3712]{1,0:T(8,128)(2,1)S(1)}, u32[]{:S(2)}, u32[]{:S(2)}) collective-permute-start(bf16[16,3712]{1,0:T(8,128)(2,1)S(1)} %get-tuple-element.45), channel_id=1, source_target_pairs={{0,8},{1,9},{2,10},{3,11},{4,0},{5,1},{6,2},{7,3},{8,12},{9,13},{1... | collective-permute-start | bytes 356360 | tf_op jit(solution)/shard_map/ppermute | solution.py:349
  19.9 7.5 %collective-permute-start.6 = (bf16[16,3712]{1,0:T(8,128)(2,1)S(1)}, bf16[16,3712]{1,0:T(8,128)(2,1)S(1)}, u32[]{:S(2)}, u32[]{:S(2)}) collective-permute-start(bf16[16,3712]{1,0:T(8,128)(2,1)S(1)} %get-tuple-element.46), channel_id=1, source_target_pairs={{0,10},{1,11},{2,8},{3,9},{4,2},{5,3},{6,0},{7,1},{8,14},{9,15},{1... | collective-permute-start | bytes 356360 | tf_op jit(solution)/shard_map/ppermute | solution.py:349
  30.9 7.5 %collective-permute-start.10 = (bf16[16,3712]{1,0:T(8,128)(2,1)S(1)}, bf16[16,3712]{1,0:T(8,128)(2,1)S(1)}, u32[]{:S(2)}, u32[]{:S(2)}) collective-permute-start(bf16[16,3712]{1,0:T(8,128)(2,1)S(1)} %get-tuple-element.51), channel_id=1, source_target_pairs={{0,4},{1,5},{2,6},{3,7},{4,12},{5,13},{6,14},{7,15},{8,0},{9,1},{1... | collective-permute-start | bytes 356360 | tf_op jit(solution)/shard_map/ppermute | solution.py:349
  31.9 8.4 %collective-permute-start.11 = (bf16[16,3712]{1,0:T(8,128)(2,1)S(1)}, bf16[16,3712]{1,0:T(8,128)(2,1)S(1)}, u32[]{:S(2)}, u32[]{:S(2)}) collective-permute-start(bf16[16,3712]{1,0:T(8,128)(2,1)S(1)} %get-tuple-element.52), channel_id=1, source_target_pairs={{0,6},{1,7},{2,4},{3,5},{4,14},{5,15},{6,12},{7,13},{8,2},{9,3},{1... | collective-permute-start | bytes 356360 | tf_op jit(solution)/shard_map/ppermute | solution.py:349
  34.8 8.7 %collective-permute-start.12 = (bf16[16,3712]{1,0:T(8,128)(2,1)S(1)}, bf16[16,3712]{1,0:T(8,128)(2,1)S(1)}, u32[]{:S(2)}, u32[]{:S(2)}) collective-permute-start(bf16[16,3712]{1,0:T(8,128)(2,1)S(1)} %get-tuple-element.53), channel_id=1, source_target_pairs={{0,2},{1,3},{2,0},{3,1},{4,6},{5,7},{6,4},{7,5},{8,10},{9,11},{10,... | collective-permute-start | bytes 356360 | tf_op jit(solution)/shard_map/ppermute | solution.py:349
  35.3 8.2 %collective-permute-start.13 = (bf16[16,3712]{1,0:T(8,128)(2,1)S(1)}, bf16[16,3712]{1,0:T(8,128)(2,1)S(1)}, u32[]{:S(2)}, u32[]{:S(2)}) collective-permute-start(bf16[16,3712]{1,0:T(8,128)(2,1)S(1)} %get-tuple-element.54), channel_id=1, source_target_pairs={{0,18},{1,19},{2,16},{3,17},{4,22},{5,23},{6,20},{7,21},{8,26},{9,... | collective-permute-start | bytes 356360 | tf_op jit(solution)/shard_map/ppermute | solution.py:349
  37.8 5.7 %collective-permute-start.9 = (bf16[16,3712]{1,0:T(8,128)(2,1)S(1)}, bf16[16,3712]{1,0:T(8,128)(2,1)S(1)}, u32[]{:S(2)}, u32[]{:S(2)}) collective-permute-start(bf16[16,3712]{1,0:T(8,128)(2,1)S(1)} %get-tuple-element.49), channel_id=1, source_target_pairs={{0,16},{1,17},{2,18},{3,19},{4,20},{5,21},{6,22},{7,23},{8,24},{9,... | collective-permute-start | bytes 356360 | tf_op jit(solution)/shard_map/ppermute | solution.py:349
  43.9 14.0 %collective-permute-start.16 = (bf16[32,3584]{1,0:T(8,128)(2,1)S(1)}, bf16[32,3584]{1,0:T(8,128)(2,1)S(1)}, u32[]{:S(2)}, u32[]{:S(2)}) collective-permute-start(bf16[32,3584]{1,0:T(8,128)(2,1)S(1)} %merge.1), channel_id=1, source_target_pairs={{0,20},{1,21},{2,22},{3,23},{4,28},{5,29},{6,30},{7,31},{8,16},{9,... | collective-permute-start | bytes 688136 | tf_op jit(solution)/shard_map/ppermute | solution.py:349
  45.1 9.2 %collective-permute-start.14 = (bf16[16,3712]{1,0:T(8,128)(2,1)S(1)}, bf16[16,3712]{1,0:T(8,128)(2,1)S(1)}, u32[]{:S(2)}, u32[]{:S(2)}) collective-permute-start(bf16[16,3712]{1,0:T(8,128)(2,1)S(1)} %get-tuple-element.57), channel_id=1, source_target_pairs={{0,24},{1,25},{2,26},{3,27},{4,16},{5,17},{6,18},{7,19},{8,28},{9,... | collective-permute-start | bytes 356360 | tf_op jit(solution)/shard_map/ppermute | solution.py:349
  47.8 9.1 %collective-permute-start.15 = (bf16[16,3712]{1,0:T(8,128)(2,1)S(1)}, bf16[16,3712]{1,0:T(8,128)(2,1)S(1)}, u32[]{:S(2)}, u32[]{:S(2)}) collective-permute-start(bf16[16,3712]{1,0:T(8,128)(2,1)S(1)} %get-tuple-element.58), channel_id=1, source_target_pairs={{0,26},{1,27},{2,24},{3,25},{4,18},{5,19},{6,16},{7,17},{8,30},{9,... | collective-permute-start | bytes 356360 | tf_op jit(solution)/shard_map/ppermute | solution.py:349

commit v13 on v10

--- a/solution.py
+++ b/solution.py
@@ -340,15 +340,17 @@
     slots, total = near_pass(pieces, near)
     pieces = far_pass(slots, total, (far_in, far_out), capacity)
     piece = dict(zip(places, pieces))
-    merged = [
-        piece[3, 0],
-        sent(piece[2, 0], sections, 0, 1, 0),
+    straight = {at: sent(piece[at, 0], sections, 1, -at, 0) for at in range(2)}
+    first = [
+        straight[1],
         sent(piece[2, 1], sections, 0, 1, 1),
         sent(piece[3, 1], sections, 0, 0, 1),
+        sent(piece[2, 0], sections, 0, 1, 0),
+        straight[0],
     ]
-    straight = [sent(piece[0, flip], sections, 1, 0, flip) for flip in range(2)]
-    merged, straight = lax.optimization_barrier((merged, straight))
-    straight += [sent(piece[1, flip], sections, 1, -1, flip) for flip in range(2)]
+    one, *merged, zero = lax.optimization_barrier(first)
+    merged.append(piece[3, 0])
+    straight = [one, zero] + [sent(piece[at, 1], sections, 1, -at, 1) for at in range(2)]
     merged = sent(combine(merged, tok_count), sections, 1, 1, 0)
     return combine(straight, tok_count, merged)[None]
 

time: 56.6 us -> 57.7 us (1.019)
  waiting for transfers between devices: 17.3 us -> 18 us
    ppermute x15, waiting for transfers between devices: 17.3 us -> 18 us  [sent(): return lax.ppermute(shard, ('section', 'expert'), pairs)]
where the time goes in v13:
time: 57.7 us; the launch traced here: 57.5 us
  starting transfers between devices  27.1 us (47%)
  waiting for transfers between devices  18 us (31%)
  Pallas kernels  7.61 us (13%)
  local copies, waits for them, and re-layouts  4.62 us (8%)
    ppermute x15, starting transfers between devices, sent(): return lax.ppermute(shard, ('section', 'expert'), pairs)  26.6 us
    ppermute x15, waiting for transfers between devices, sent(): return lax.ppermute(shard, ('section', 'expert'), pairs)  18 us
    pallas_call x9, Pallas kernels, local_call(): pl.pallas_call(kernel, out_shape=out_shape, in_specs=[vmem if spec is Non...  7.61 us
    unnamed x4, local copies, waits for them, and re-layouts  4.62 us
  transfers between devices with their start and end apart: 17, of which 9 were waited for; matrix products, arithmetic and copies ran while one was open for 0% of the time, Pallas kernels for 8%

profile of v13, /device:TPU:0, one launch (start us, length us, event | category | flops | bytes accessed | tf_op | source)
XLA Modules:
  0.0 57.5 jit_solution(2545218759914160182)
XLA Ops:
  1.5 3.1 %collective-permute-start.1 = (bf16[32,3712]{1,0:T(8,128)(2,1)S(1)}, bf16[32,3712]{1,0:T(8,128)(2,1)S(1)}, u32[]{:S(2)}, u32[]{:S(2)}) collective-permute-start(bf16[32,3712]{1,0:T(8,128)(2,1)S(1)} %prepare.1.block), channel_id=1, source_target_pairs={{0,4},{1,5},{2,6},{3,7},{4,12},{5,13},{6,14},{7,15},{8,0},{9,1},{1... | collective-permute-start | bytes 712712 | tf_op jit(solution)/shard_map/ppermute | solution.py:306
  5.0 1.6 %collective-permute-start = (bf16[16,3712]{1,0:T(8,128)(2,1)S(1)}, bf16[16,3712]{1,0:T(8,128)(2,1)S(1)}, u32[]{:S(2)}, u32[]{:S(2)}) collective-permute-start(bf16[16,3712]{1,0:T(8,128)(2,1)S(1)} %get-tuple-element.34), channel_id=1, source_target_pairs={{0,2},{1,3},{2,0},{3,1},{4,6},{5,7},{6,4},{7,5},{8,10},{9,11},{10,... | collective-permute-start | bytes 356360 | tf_op jit(solution)/shard_map/ppermute | solution.py:306
  6.6 3.1 %copy-done = bf16[1,3584,1024]{2,1,0:T(8,128)(2,1)S(1)} copy-done((bf16[1,3584,1024]{2,1,0:T(8,128)(2,1)S(1)}, bf16[1,3584,1024]{2,1,0:T(8,128)(2,1)}, u32[]{:S(2)}) %copy-start) | copy-done | bytes 7340056
  10.2 1.5 %copy-done.1 = bf16[1,512,3584]{2,1,0:T(8,128)(2,1)S(1)} copy-done((bf16[1,512,3584]{2,1,0:T(8,128)(2,1)S(1)}, bf16[1,512,3584]{2,1,0:T(8,128)(2,1)}, u32[]{:S(2)}) %copy-start.1) | copy-done | bytes 3670040
  12.4 1.2 %collective-permute-start.4 = (bf16[16,3712]{1,0:T(8,128)(2,1)S(1)}, bf16[16,3712]{1,0:T(8,128)(2,1)S(1)}, u32[]{:S(2)}, u32[]{:S(2)}) collective-permute-start(bf16[16,3712]{1,0:T(8,128)(2,1)S(1)} %get-tuple-element.41), channel_id=1, source_target_pairs={{0,2},{1,3},{2,0},{3,1},{4,6},{5,7},{6,4},{7,5},{8,10},{9,11},{10,... | collective-permute-start | bytes 356360 | tf_op jit(solution)/shard_map/ppermute | solution.py:306
  13.6 2.0 %collective-permute-start.2 = (bf16[16,3712]{1,0:T(8,128)(2,1)S(1)}, bf16[16,3712]{1,0:T(8,128)(2,1)S(1)}, u32[]{:S(2)}, u32[]{:S(2)}) collective-permute-start(bf16[16,3712]{1,0:T(8,128)(2,1)S(1)} %get-tuple-element.39), channel_id=1, source_target_pairs={{0,4},{1,5},{2,6},{3,7},{4,12},{5,13},{6,14},{7,15},{8,0},{9,1},{1... | collective-permute-start | bytes 356360 | tf_op jit(solution)/shard_map/ppermute | solution.py:306
  15.6 2.1 %collective-permute-start.3 = (bf16[16,3712]{1,0:T(8,128)(2,1)S(1)}, bf16[16,3712]{1,0:T(8,128)(2,1)S(1)}, u32[]{:S(2)}, u32[]{:S(2)}) collective-permute-start(bf16[16,3712]{1,0:T(8,128)(2,1)S(1)} %get-tuple-element.40), channel_id=1, source_target_pairs={{0,6},{1,7},{2,4},{3,5},{4,14},{5,15},{6,12},{7,13},{8,2},{9,3},{1... | collective-permute-start | bytes 356360 | tf_op jit(solution)/shard_map/ppermute | solution.py:306
  17.7 1.7 %collective-permute-start.5 = (bf16[16,3712]{1,0:T(8,128)(2,1)S(1)}, bf16[16,3712]{1,0:T(8,128)(2,1)S(1)}, u32[]{:S(2)}, u32[]{:S(2)}) collective-permute-start(bf16[16,3712]{1,0:T(8,128)(2,1)S(1)} %get-tuple-element.44), channel_id=1, source_target_pairs={{0,8},{1,9},{2,10},{3,11},{4,0},{5,1},{6,2},{7,3},{8,12},{9,13},{1... | collective-permute-start | bytes 356360 | tf_op jit(solution)/shard_map/ppermute | solution.py:306
  19.9 2.2 %collective-permute-start.6 = (bf16[16,3712]{1,0:T(8,128)(2,1)S(1)}, bf16[16,3712]{1,0:T(8,128)(2,1)S(1)}, u32[]{:S(2)}, u32[]{:S(2)}) collective-permute-start(bf16[16,3712]{1,0:T(8,128)(2,1)S(1)} %get-tuple-element.45), channel_id=1, source_target_pairs={{0,10},{1,11},{2,8},{3,9},{4,2},{5,3},{6,0},{7,1},{8,14},{9,15},{1... | collective-permute-start | bytes 356360 | tf_op jit(solution)/shard_map/ppermute | solution.py:306
  22.1 4.1 %collective-permute-done.3.refs_4_ = bf16[16,3712]{1,0:T(8,128)(2,1)S(1)} collective-permute-done((bf16[16,3712]{1,0:T(8,128)(2,1)S(1)}, bf16[16,3712]{1,0:T(8,128)(2,1)S(1)}, u32[]{:S(2)}, u32[]{:S(2)}) %collective-permute-start.3) | collective-permute-done | bytes 118816 | tf_op jit(solution)/shard_map/ppermute | solution.py:306
  26.2 1.2 %collective-permute-done.6.refs_7_ = bf16[16,3712]{1,0:T(8,128)(2,1)S(1)} collective-permute-done((bf16[16,3712]{1,0:T(8,128)(2,1)S(1)}, bf16[16,3712]{1,0:T(8,128)(2,1)S(1)}, u32[]{:S(2)}, u32[]{:S(2)}) %collective-permute-start.6) | collective-permute-done | bytes 118816 | tf_op jit(solution)/shard_map/ppermute | solution.py:306
  27.3 1.8 %near_pass.1 = (bf16[128,3712]{1,0:T(8,128)(2,1)S(1)}, f32[128,3584]{1,0:T(8,128)S(1)}) custom-call(bf16[16,3712]{1,0:T(8,128)(2,1)S(1)} %get-tuple-element.33.refs_0_, bf16[16,3712]{1,0:T(8,128)(2,1)S(1)} %collective-permute-done.refs_1_, bf16[16,3712]{1,0:T(8,128)(2,1)S(1)} %get-tuple-element.38.refs_2_, ...), custom_call_target="tpu_custom_call" | custom-call | bytes 11010048 | tf_op jit(solution)/shard_map/near_pass/pallas_call | solution.py:84
  29.1 1.7 %far_pass.1 = (bf16[16,3712]{1,0:T(8,128)(2,1)S(1)}, bf16[16,3712]{1,0:T(8,128)(2,1)S(1)}, bf16[16,3712]{1,0:T(8,128)(2,1)S(1)}, bf16[16,3712]{1,0:T(8,128)(2,1)...) custom-call(bf16[128,3712]{1,0:T(8,128)(2,1)S(1)} %get-tuple-element, ...), custom_call_target="tpu_custom_call" | custom-call | bytes 11010048 | tf_op jit(solution)/shard_map/far_pass/pallas_call | solution.py:84
  30.9 2.0 %collective-permute-start.10 = (bf16[16,3712]{1,0:T(8,128)(2,1)S(1)}, bf16[16,3712]{1,0:T(8,128)(2,1)S(1)}, u32[]{:S(2)}, u32[]{:S(2)}) collective-permute-start(bf16[16,3712]{1,0:T(8,128)(2,1)S(1)} %get-tuple-element.49), channel_id=1, source_target_pairs={{0,6},{1,7},{2,4},{3,5},{4,14},{5,15},{6,12},{7,13},{8,2},{9,3},{1... | collective-permute-start | bytes 356360 | tf_op jit(solution)/shard_map/ppermute | solution.py:306
  33.4 2.0 %collective-permute-start.12 = (bf16[16,3712]{1,0:T(8,128)(2,1)S(1)}, bf16[16,3712]{1,0:T(8,128)(2,1)S(1)}, u32[]{:S(2)}, u32[]{:S(2)}) collective-permute-start(bf16[16,3712]{1,0:T(8,128)(2,1)S(1)} %get-tuple-element.51), channel_id=1, source_target_pairs={{0,4},{1,5},{2,6},{3,7},{4,12},{5,13},{6,14},{7,15},{8,0},{9,1},{1... | collective-permute-start | bytes 356360 | tf_op jit(solution)/shard_map/ppermute | solution.py:306
  35.3 1.5 %collective-permute-start.13 = (bf16[16,3712]{1,0:T(8,128)(2,1)S(1)}, bf16[16,3712]{1,0:T(8,128)(2,1)S(1)}, u32[]{:S(2)}, u32[]{:S(2)}) collective-permute-start(bf16[16,3712]{1,0:T(8,128)(2,1)S(1)} %get-tuple-element.52), channel_id=1, source_target_pairs={{0,16},{1,17},{2,18},{3,19},{4,20},{5,21},{6,22},{7,23},{8,24},{9,... | collective-permute-start | bytes 356360 | tf_op jit(solution)/shard_map/ppermute | solution.py:306
  38.9 1.5 %collective-permute-done.12.refs_2_ = bf16[16,3712]{1,0:T(8,128)(2,1)S(1)} collective-permute-done((bf16[16,3712]{1,0:T(8,128)(2,1)S(1)}, bf16[16,3712]{1,0:T(8,128)(2,1)S(1)}, u32[]{:S(2)}, u32[]{:S(2)}) %collective-permute-start.12) | collective-permute-done | bytes 118816 | tf_op jit(solution)/shard_map/ppermute | solution.py:306
  40.4 1.2 %collective-permute-done.13.refs_1_ = bf16[16,3712]{1,0:T(8,128)(2,1)S(1)} collective-permute-done((bf16[16,3712]{1,0:T(8,128)(2,1)S(1)}, bf16[16,3712]{1,0:T(8,128)(2,1)S(1)}, u32[]{:S(2)}, u32[]{:S(2)}) %collective-permute-start.13) | collective-permute-done | bytes 118816 | tf_op jit(solution)/shard_map/ppermute | solution.py:306
  41.6 1.4 %collective-permute-done.9.refs_0_ = bf16[16,3712]{1,0:T(8,128)(2,1)S(1)} collective-permute-done((bf16[16,3712]{1,0:T(8,128)(2,1)S(1)}, bf16[16,3712]{1,0:T(8,128)(2,1)S(1)}, u32[]{:S(2)}, u32[]{:S(2)}) %collective-permute-start.9) | collective-permute-done | bytes 118816 | tf_op jit(solution)/shard_map/ppermute | solution.py:306
  43.5 1.9 %collective-permute-start.16 = (bf16[32,3584]{1,0:T(8,128)(2,1)S(1)}, bf16[32,3584]{1,0:T(8,128)(2,1)S(1)}, u32[]{:S(2)}, u32[]{:S(2)}) collective-permute-start(bf16[32,3584]{1,0:T(8,128)(2,1)S(1)} %combine.2), channel_id=1, source_target_pairs={{0,20},{1,21},{2,22},{3,23},{4,28},{5,29},{6,30},{7,31},{8,16},{9,... | collective-permute-start | bytes 688136 | tf_op jit(solution)/shard_map/ppermute | solution.py:306
  45.3 1.5 %collective-permute-start.14 = (bf16[16,3712]{1,0:T(8,128)(2,1)S(1)}, bf16[16,3712]{1,0:T(8,128)(2,1)S(1)}, u32[]{:S(2)}, u32[]{:S(2)}) collective-permute-start(bf16[16,3712]{1,0:T(8,128)(2,1)S(1)} %get-tuple-element.55), channel_id=1, source_target_pairs={{0,18},{1,19},{2,16},{3,17},{4,22},{5,23},{6,20},{7,21},{8,26},{9,... | collective-permute-start | bytes 356360 | tf_op jit(solution)/shard_map/ppermute | solution.py:306
  46.8 2.4 %collective-permute-start.15 = (bf16[16,3712]{1,0:T(8,128)(2,1)S(1)}, bf16[16,3712]{1,0:T(8,128)(2,1)S(1)}, u32[]{:S(2)}, u32[]{:S(2)}) collective-permute-start(bf16[16,3712]{1,0:T(8,128)(2,1)S(1)} %get-tuple-element.56), channel_id=1, source_target_pairs={{0,26},{1,27},{2,24},{3,25},{4,18},{5,19},{6,16},{7,17},{8,30},{9,... | collective-permute-start | bytes 356360 | tf_op jit(solution)/shard_map/ppermute | solution.py:306
  49.3 7.1 %collective-permute-done.14.refs_2_ = bf16[16,3712]{1,0:T(8,128)(2,1)S(1)} collective-permute-done((bf16[16,3712]{1,0:T(8,128)(2,1)S(1)}, bf16[16,3712]{1,0:T(8,128)(2,1)S(1)}, u32[]{:S(2)}, u32[]{:S(2)}) %collective-permute-start.14) | collective-permute-done | bytes 118816 | tf_op jit(solution)/shard_map/ppermute | solution.py:306
  56.4 1.1 %combine.3 = bf16[32,3584]{1,0:T(8,128)(2,1)} custom-call(bf16[16,3712]{1,0:T(8,128)(2,1)S(1)} %collective-permute-done.9.refs_0_, bf16[16,3712]{1,0:T(8,128)(2,1)S(1)} %collective-permute-done.13.refs_1_, bf16[16,3712]{1,0:T(8,128)(2,1)S(1)} %collective-permute-done.14.refs_2_, bf16[16,3712]{1,0:T(8,128)(2,1)S(1)} %collective-permute-done.15.refs_3_, ...), custom_call_target="tpu_custom_call" | custom-call | tf_op jit(solution)/shard_map/combine/pallas_call | solution.py:84
  (23 shorter events, 6.6 us)
Async XLA Ops:
  0.0 29.1 %collective-permute-start.7 = (bf16[3584,1024]{1,0:T(8,128)(2,1)}, bf16[3584,1024]{1,0:T(8,128)(2,1)S(1)}, u32[]{:S(2)}, u32[]{:S(2)}) collective-permute-start(bf16[3584,1024]{1,0:T(8,128)(2,1)} %bitcast.10), channel_id=1, source_target_pairs={{0,1},{1,0},{2,3},{3,2},{4,5},{5,4},{6,7},{7,6},{8,9},{9,8},{10,11... | collective-permute-start | bytes 22020104 | tf_op jit(solution)/shard_map/ppermute | solution.py:324
  0.5 28.6 %collective-permute-start.8 = (bf16[512,3584]{1,0:T(8,128)(2,1)}, bf16[512,3584]{1,0:T(8,128)(2,1)S(1)}, u32[]{:S(2)}, u32[]{:S(2)}) collective-permute-start(bf16[512,3584]{1,0:T(8,128)(2,1)} %bitcast.12), channel_id=1, source_target_pairs={{0,1},{1,0},{2,3},{3,2},{4,5},{5,4},{6,7},{7,6},{8,9},{9,8},{10,11... | collective-permute-start | bytes 11010056 | tf_op jit(solution)/shard_map/ppermute | solution.py:323
  1.5 10.5 %collective-permute-start.1 = (bf16[32,3712]{1,0:T(8,128)(2,1)S(1)}, bf16[32,3712]{1,0:T(8,128)(2,1)S(1)}, u32[]{:S(2)}, u32[]{:S(2)}) collective-permute-start(bf16[32,3712]{1,0:T(8,128)(2,1)S(1)} %prepare.1.block), channel_id=1, source_target_pairs={{0,4},{1,5},{2,6},{3,7},{4,12},{5,13},{6,14},{7,15},{8,0},{9,1},{1... | collective-permute-start | bytes 712712 | tf_op jit(solution)/shard_map/ppermute | solution.py:306
  5.0 7.0 %collective-permute-start = (bf16[16,3712]{1,0:T(8,128)(2,1)S(1)}, bf16[16,3712]{1,0:T(8,128)(2,1)S(1)}, u32[]{:S(2)}, u32[]{:S(2)}) collective-permute-start(bf16[16,3712]{1,0:T(8,128)(2,1)S(1)} %get-tuple-element.34), channel_id=1, source_target_pairs={{0,2},{1,3},{2,0},{3,1},{4,6},{5,7},{6,4},{7,5},{8,10},{9,11},{10,... | collective-permute-start | bytes 356360 | tf_op jit(solution)/shard_map/ppermute | solution.py:306
  6.6 3.1 %copy-start = (bf16[1,3584,1024]{2,1,0:T(8,128)(2,1)S(1)}, bf16[1,3584,1024]{2,1,0:T(8,128)(2,1)}, u32[]{:S(2)}) copy-start(bf16[1,3584,1024]{2,1,0:T(8,128)(2,1)} %param.8) | copy-start | bytes 22020100
  9.7 2.0 %copy-start.1 = (bf16[1,512,3584]{2,1,0:T(8,128)(2,1)S(1)}, bf16[1,512,3584]{2,1,0:T(8,128)(2,1)}, u32[]{:S(2)}) copy-start(bf16[1,512,3584]{2,1,0:T(8,128)(2,1)} %param.9) | copy-start | bytes 11010052
  12.4 5.3 %collective-permute-start.4 = (bf16[16,3712]{1,0:T(8,128)(2,1)S(1)}, bf16[16,3712]{1,0:T(8,128)(2,1)S(1)}, u32[]{:S(2)}, u32[]{:S(2)}) collective-permute-start(bf16[16,3712]{1,0:T(8,128)(2,1)S(1)} %get-tuple-element.41), channel_id=1, source_target_pairs={{0,2},{1,3},{2,0},{3,1},{4,6},{5,7},{6,4},{7,5},{8,10},{9,11},{10,... | collective-permute-start | bytes 356360 | tf_op jit(solution)/shard_map/ppermute | solution.py:306
  13.6 6.3 %collective-permute-start.2 = (bf16[16,3712]{1,0:T(8,128)(2,1)S(1)}, bf16[16,3712]{1,0:T(8,128)(2,1)S(1)}, u32[]{:S(2)}, u32[]{:S(2)}) collective-permute-start(bf16[16,3712]{1,0:T(8,128)(2,1)S(1)} %get-tuple-element.39), channel_id=1, source_target_pairs={{0,4},{1,5},{2,6},{3,7},{4,12},{5,13},{6,14},{7,15},{8,0},{9,1},{1... | collective-permute-start | bytes 356360 | tf_op jit(solution)/shard_map/ppermute | solution.py:306
  15.6 10.6 %collective-permute-start.3 = (bf16[16,3712]{1,0:T(8,128)(2,1)S(1)}, bf16[16,3712]{1,0:T(8,128)(2,1)S(1)}, u32[]{:S(2)}, u32[]{:S(2)}) collective-permute-start(bf16[16,3712]{1,0:T(8,128)(2,1)S(1)} %get-tuple-element.40), channel_id=1, source_target_pairs={{0,6},{1,7},{2,4},{3,5},{4,14},{5,15},{6,12},{7,13},{8,2},{9,3},{1... | collective-permute-start | bytes 356360 | tf_op jit(solution)/shard_map/ppermute | solution.py:306
  17.7 8.4 %collective-permute-start.5 = (bf16[16,3712]{1,0:T(8,128)(2,1)S(1)}, bf16[16,3712]{1,0:T(8,128)(2,1)S(1)}, u32[]{:S(2)}, u32[]{:S(2)}) collective-permute-start(bf16[16,3712]{1,0:T(8,128)(2,1)S(1)} %get-tuple-element.44), channel_id=1, source_target_pairs={{0,8},{1,9},{2,10},{3,11},{4,0},{5,1},{6,2},{7,3},{8,12},{9,13},{1... | collective-permute-start | bytes 356360 | tf_op jit(solution)/shard_map/ppermute | solution.py:306
  19.9 7.5 %collective-permute-start.6 = (bf16[16,3712]{1,0:T(8,128)(2,1)S(1)}, bf16[16,3712]{1,0:T(8,128)(2,1)S(1)}, u32[]{:S(2)}, u32[]{:S(2)}) collective-permute-start(bf16[16,3712]{1,0:T(8,128)(2,1)S(1)} %get-tuple-element.45), channel_id=1, source_target_pairs={{0,10},{1,11},{2,8},{3,9},{4,2},{5,3},{6,0},{7,1},{8,14},{9,15},{1... | collective-permute-start | bytes 356360 | tf_op jit(solution)/shard_map/ppermute | solution.py:306
  30.9 7.8 %collective-permute-start.10 = (bf16[16,3712]{1,0:T(8,128)(2,1)S(1)}, bf16[16,3712]{1,0:T(8,128)(2,1)S(1)}, u32[]{:S(2)}, u32[]{:S(2)}) collective-permute-start(bf16[16,3712]{1,0:T(8,128)(2,1)S(1)} %get-tuple-element.49), channel_id=1, source_target_pairs={{0,6},{1,7},{2,4},{3,5},{4,14},{5,15},{6,12},{7,13},{8,2},{9,3},{1... | collective-permute-start | bytes 356360 | tf_op jit(solution)/shard_map/ppermute | solution.py:306
  32.8 6.1 %collective-permute-start.11 = (bf16[16,3712]{1,0:T(8,128)(2,1)S(1)}, bf16[16,3712]{1,0:T(8,128)(2,1)S(1)}, u32[]{:S(2)}, u32[]{:S(2)}) collective-permute-start(bf16[16,3712]{1,0:T(8,128)(2,1)S(1)} %get-tuple-element.50), channel_id=1, source_target_pairs={{0,2},{1,3},{2,0},{3,1},{4,6},{5,7},{6,4},{7,5},{8,10},{9,11},{10,... | collective-permute-start | bytes 356360 | tf_op jit(solution)/shard_map/ppermute | solution.py:306
  33.4 7.0 %collective-permute-start.12 = (bf16[16,3712]{1,0:T(8,128)(2,1)S(1)}, bf16[16,3712]{1,0:T(8,128)(2,1)S(1)}, u32[]{:S(2)}, u32[]{:S(2)}) collective-permute-start(bf16[16,3712]{1,0:T(8,128)(2,1)S(1)} %get-tuple-element.51), channel_id=1, source_target_pairs={{0,4},{1,5},{2,6},{3,7},{4,12},{5,13},{6,14},{7,15},{8,0},{9,1},{1... | collective-permute-start | bytes 356360 | tf_op jit(solution)/shard_map/ppermute | solution.py:306
  35.3 6.3 %collective-permute-start.13 = (bf16[16,3712]{1,0:T(8,128)(2,1)S(1)}, bf16[16,3712]{1,0:T(8,128)(2,1)S(1)}, u32[]{:S(2)}, u32[]{:S(2)}) collective-permute-start(bf16[16,3712]{1,0:T(8,128)(2,1)S(1)} %get-tuple-element.52), channel_id=1, source_target_pairs={{0,16},{1,17},{2,18},{3,19},{4,20},{5,21},{6,22},{7,23},{8,24},{9,... | collective-permute-start | bytes 356360 | tf_op jit(solution)/shard_map/ppermute | solution.py:306
  36.8 6.2 %collective-permute-start.9 = (bf16[16,3712]{1,0:T(8,128)(2,1)S(1)}, bf16[16,3712]{1,0:T(8,128)(2,1)S(1)}, u32[]{:S(2)}, u32[]{:S(2)}) collective-permute-start(bf16[16,3712]{1,0:T(8,128)(2,1)S(1)} %get-tuple-element.48), channel_id=1, source_target_pairs={{0,24},{1,25},{2,26},{3,27},{4,16},{5,17},{6,18},{7,19},{8,28},{9,... | collective-permute-start | bytes 356360 | tf_op jit(solution)/shard_map/ppermute | solution.py:306
  43.5 12.9 %collective-permute-start.16 = (bf16[32,3584]{1,0:T(8,128)(2,1)S(1)}, bf16[32,3584]{1,0:T(8,128)(2,1)S(1)}, u32[]{:S(2)}, u32[]{:S(2)}) collective-permute-start(bf16[32,3584]{1,0:T(8,128)(2,1)S(1)} %combine.2), channel_id=1, source_target_pairs={{0,20},{1,21},{2,22},{3,23},{4,28},{5,29},{6,30},{7,31},{8,16},{9,... | collective-permute-start | bytes 688136 | tf_op jit(solution)/shard_map/ppermute | solution.py:306
  45.3 11.0 %collective-permute-start.14 = (bf16[16,3712]{1,0:T(8,128)(2,1)S(1)}, bf16[16,3712]{1,0:T(8,128)(2,1)S(1)}, u32[]{:S(2)}, u32[]{:S(2)}) collective-permute-start(bf16[16,3712]{1,0:T(8,128)(2,1)S(1)} %get-tuple-element.55), channel_id=1, source_target_pairs={{0,18},{1,19},{2,16},{3,17},{4,22},{5,23},{6,20},{7,21},{8,26},{9,... | collective-permute-start | bytes 356360 | tf_op jit(solution)/shard_map/ppermute | solution.py:306
  46.8 9.5 %collective-permute-start.15 = (bf16[16,3712]{1,0:T(8,128)(2,1)S(1)}, bf16[16,3712]{1,0:T(8,128)(2,1)S(1)}, u32[]{:S(2)}, u32[]{:S(2)}) collective-permute-start(bf16[16,3712]{1,0:T(8,128)(2,1)S(1)} %get-tuple-element.56), channel_id=1, source_target_pairs={{0,26},{1,27},{2,24},{3,25},{4,18},{5,19},{6,16},{7,17},{8,30},{9,... | collective-permute-start | bytes 356360 | tf_op jit(solution)/shard_map/ppermute | solution.py:306

commit v14 on v13

--- a/solution.py
+++ b/solution.py
@@ -340,17 +340,17 @@
     slots, total = near_pass(pieces, near)
     pieces = far_pass(slots, total, (far_in, far_out), capacity)
     piece = dict(zip(places, pieces))
-    straight = {at: sent(piece[at, 0], sections, 1, -at, 0) for at in range(2)}
     first = [
-        straight[1],
+        sent(piece[1, 0], sections, 1, -1, 0),
         sent(piece[2, 1], sections, 0, 1, 1),
         sent(piece[3, 1], sections, 0, 0, 1),
         sent(piece[2, 0], sections, 0, 1, 0),
-        straight[0],
+        sent(piece[0, 0], sections, 1, 0, 0),
+        sent(piece[0, 1], sections, 1, 0, 1),
     ]
-    one, *merged, zero = lax.optimization_barrier(first)
-    merged.append(piece[3, 0])
-    straight = [one, zero] + [sent(piece[at, 1], sections, 1, -at, 1) for at in range(2)]
+    one, two, three, four, *straight = lax.optimization_barrier(first)
+    merged = [piece[3, 0], two, three, four]
+    straight += [one, sent(piece[1, 1], sections, 1, -1, 1)]
     merged = sent(combine(merged, tok_count), sections, 1, 1, 0)
     return combine(straight, tok_count, merged)[None]
 

time: 57.7 us -> 56.8 us (0.984)
  waiting for transfers between devices: 18 us -> 14.2 us
  starting transfers between devices: 27.1 us -> 30 us
    ppermute x15, waiting for transfers between devices: 18 us -> 14.2 us  [sent(): return lax.ppermute(shard, ('section', 'expert'), pairs)]
    ppermute x15, starting transfers between devices: 26.6 us -> 29.5 us  [sent(): return lax.ppermute(shard, ('section', 'expert'), pairs)]
  transfers between devices with their start and end apart: 17 -> 17, of which waited for: 9 -> 8; matrix products, arithmetic and copies ran while one was open for 0% -> 0% of each run, Pallas kernels for 8% -> 8%
where the time goes in v14:
time: 56.8 us; the launch traced here: 56.6 us
  starting transfers between devices  30 us (53%)
  waiting for transfers between devices  14.2 us (25%)
  Pallas kernels  7.61 us (13%)
  local copies, waits for them, and re-layouts  4.62 us (8%)
    ppermute x15, starting transfers between devices, sent(): return lax.ppermute(shard, ('section', 'expert'), pairs)  29.5 us
    ppermute x15, waiting for transfers between devices, sent(): return lax.ppermute(shard, ('section', 'expert'), pairs)  14.2 us
    pallas_call x9, Pallas kernels, local_call(): pl.pallas_call(kernel, out_shape=out_shape, in_specs=[vmem if spec is Non...  7.61 us
    unnamed x4, local copies, waits for them, and re-layouts  4.62 us
  transfers between devices with their start and end apart: 17, of which 8 were waited for; matrix products, arithmetic and copies ran while one was open for 0% of the time, Pallas kernels for 8%

profile of v14, /device:TPU:0, one launch (start us, length us, event | category | flops | bytes accessed | tf_op | source)
XLA Modules:
  0.0 56.6 jit_solution(8356107564774458204)
XLA Ops:
  0.5 1.0 %prepare.1.block = bf16[32,3712]{1,0:T(8,128)(2,1)S(1)} custom-call(s32[2,32]{1,0:T(2,128)} %bitcast.15, f32[2,32]{1,0:T(2,128)} %bitcast.16, bf16[32,3584]{1,0:T(8,128)(2,1)} %bitcast.14), custom_call_target="tpu_custom_call" | custom-call | tf_op jit(solution)/shard_map/prepare/pallas_call | solution.py:84
  1.5 3.1 %collective-permute-start.1 = (bf16[32,3712]{1,0:T(8,128)(2,1)S(1)}, bf16[32,3712]{1,0:T(8,128)(2,1)S(1)}, u32[]{:S(2)}, u32[]{:S(2)}) collective-permute-start(bf16[32,3712]{1,0:T(8,128)(2,1)S(1)} %prepare.1.block), channel_id=1, source_target_pairs={{0,4},{1,5},{2,6},{3,7},{4,12},{5,13},{6,14},{7,15},{8,0},{9,1},{1... | collective-permute-start | bytes 712712 | tf_op jit(solution)/shard_map/ppermute | solution.py:306
  5.0 1.6 %collective-permute-start = (bf16[16,3712]{1,0:T(8,128)(2,1)S(1)}, bf16[16,3712]{1,0:T(8,128)(2,1)S(1)}, u32[]{:S(2)}, u32[]{:S(2)}) collective-permute-start(bf16[16,3712]{1,0:T(8,128)(2,1)S(1)} %get-tuple-element.35), channel_id=1, source_target_pairs={{0,2},{1,3},{2,0},{3,1},{4,6},{5,7},{6,4},{7,5},{8,10},{9,11},{10,... | collective-permute-start | bytes 356360 | tf_op jit(solution)/shard_map/ppermute | solution.py:306
  6.6 3.1 %copy-done = bf16[1,3584,1024]{2,1,0:T(8,128)(2,1)S(1)} copy-done((bf16[1,3584,1024]{2,1,0:T(8,128)(2,1)S(1)}, bf16[1,3584,1024]{2,1,0:T(8,128)(2,1)}, u32[]{:S(2)}) %copy-start) | copy-done | bytes 7340056
  10.2 1.5 %copy-done.1 = bf16[1,512,3584]{2,1,0:T(8,128)(2,1)S(1)} copy-done((bf16[1,512,3584]{2,1,0:T(8,128)(2,1)S(1)}, bf16[1,512,3584]{2,1,0:T(8,128)(2,1)}, u32[]{:S(2)}) %copy-start.1) | copy-done | bytes 3670040
  12.4 1.2 %collective-permute-start.4 = (bf16[16,3712]{1,0:T(8,128)(2,1)S(1)}, bf16[16,3712]{1,0:T(8,128)(2,1)S(1)}, u32[]{:S(2)}, u32[]{:S(2)}) collective-permute-start(bf16[16,3712]{1,0:T(8,128)(2,1)S(1)} %get-tuple-element.42), channel_id=1, source_target_pairs={{0,2},{1,3},{2,0},{3,1},{4,6},{5,7},{6,4},{7,5},{8,10},{9,11},{10,... | collective-permute-start | bytes 356360 | tf_op jit(solution)/shard_map/ppermute | solution.py:306
  13.6 2.0 %collective-permute-start.2 = (bf16[16,3712]{1,0:T(8,128)(2,1)S(1)}, bf16[16,3712]{1,0:T(8,128)(2,1)S(1)}, u32[]{:S(2)}, u32[]{:S(2)}) collective-permute-start(bf16[16,3712]{1,0:T(8,128)(2,1)S(1)} %get-tuple-element.40), channel_id=1, source_target_pairs={{0,4},{1,5},{2,6},{3,7},{4,12},{5,13},{6,14},{7,15},{8,0},{9,1},{1... | collective-permute-start | bytes 356360 | tf_op jit(solution)/shard_map/ppermute | solution.py:306
  15.6 2.1 %collective-permute-start.3 = (bf16[16,3712]{1,0:T(8,128)(2,1)S(1)}, bf16[16,3712]{1,0:T(8,128)(2,1)S(1)}, u32[]{:S(2)}, u32[]{:S(2)}) collective-permute-start(bf16[16,3712]{1,0:T(8,128)(2,1)S(1)} %get-tuple-element.41), channel_id=1, source_target_pairs={{0,6},{1,7},{2,4},{3,5},{4,14},{5,15},{6,12},{7,13},{8,2},{9,3},{1... | collective-permute-start | bytes 356360 | tf_op jit(solution)/shard_map/ppermute | solution.py:306
  17.7 1.7 %collective-permute-start.5 = (bf16[16,3712]{1,0:T(8,128)(2,1)S(1)}, bf16[16,3712]{1,0:T(8,128)(2,1)S(1)}, u32[]{:S(2)}, u32[]{:S(2)}) collective-permute-start(bf16[16,3712]{1,0:T(8,128)(2,1)S(1)} %get-tuple-element.45), channel_id=1, source_target_pairs={{0,8},{1,9},{2,10},{3,11},{4,0},{5,1},{6,2},{7,3},{8,12},{9,13},{1... | collective-permute-start | bytes 356360 | tf_op jit(solution)/shard_map/ppermute | solution.py:306
  19.9 2.2 %collective-permute-start.6 = (bf16[16,3712]{1,0:T(8,128)(2,1)S(1)}, bf16[16,3712]{1,0:T(8,128)(2,1)S(1)}, u32[]{:S(2)}, u32[]{:S(2)}) collective-permute-start(bf16[16,3712]{1,0:T(8,128)(2,1)S(1)} %get-tuple-element.46), channel_id=1, source_target_pairs={{0,10},{1,11},{2,8},{3,9},{4,2},{5,3},{6,0},{7,1},{8,14},{9,15},{1... | collective-permute-start | bytes 356360 | tf_op jit(solution)/shard_map/ppermute | solution.py:306
  22.1 4.1 %collective-permute-done.3.refs_4_ = bf16[16,3712]{1,0:T(8,128)(2,1)S(1)} collective-permute-done((bf16[16,3712]{1,0:T(8,128)(2,1)S(1)}, bf16[16,3712]{1,0:T(8,128)(2,1)S(1)}, u32[]{:S(2)}, u32[]{:S(2)}) %collective-permute-start.3) | collective-permute-done | bytes 118816 | tf_op jit(solution)/shard_map/ppermute | solution.py:306
  26.2 1.2 %collective-permute-done.6.refs_7_ = bf16[16,3712]{1,0:T(8,128)(2,1)S(1)} collective-permute-done((bf16[16,3712]{1,0:T(8,128)(2,1)S(1)}, bf16[16,3712]{1,0:T(8,128)(2,1)S(1)}, u32[]{:S(2)}, u32[]{:S(2)}) %collective-permute-start.6) | collective-permute-done | bytes 118816 | tf_op jit(solution)/shard_map/ppermute | solution.py:306
  27.3 1.8 %near_pass.1 = (bf16[128,3712]{1,0:T(8,128)(2,1)S(1)}, f32[128,3584]{1,0:T(8,128)S(1)}) custom-call(bf16[16,3712]{1,0:T(8,128)(2,1)S(1)} %get-tuple-element.34.refs_0_, bf16[16,3712]{1,0:T(8,128)(2,1)S(1)} %collective-permute-done.refs_1_, bf16[16,3712]{1,0:T(8,128)(2,1)S(1)} %get-tuple-element.39.refs_2_, ...), custom_call_target="tpu_custom_call" | custom-call | bytes 11010048 | tf_op jit(solution)/shard_map/near_pass/pallas_call | solution.py:84
  29.1 1.7 %far_pass.1 = (bf16[16,3712]{1,0:T(8,128)(2,1)S(1)}, bf16[16,3712]{1,0:T(8,128)(2,1)S(1)}, bf16[16,3712]{1,0:T(8,128)(2,1)S(1)}, bf16[16,3712]{1,0:T(8,128)(2,1)...) custom-call(bf16[128,3712]{1,0:T(8,128)(2,1)S(1)} %get-tuple-element, ...), custom_call_target="tpu_custom_call" | custom-call | bytes 11010048 | tf_op jit(solution)/shard_map/far_pass/pallas_call | solution.py:84
  30.9 2.0 %collective-permute-start.10 = (bf16[16,3712]{1,0:T(8,128)(2,1)S(1)}, bf16[16,3712]{1,0:T(8,128)(2,1)S(1)}, u32[]{:S(2)}, u32[]{:S(2)}) collective-permute-start(bf16[16,3712]{1,0:T(8,128)(2,1)S(1)} %get-tuple-element.50), channel_id=1, source_target_pairs={{0,6},{1,7},{2,4},{3,5},{4,14},{5,15},{6,12},{7,13},{8,2},{9,3},{1... | collective-permute-start | bytes 356360 | tf_op jit(solution)/shard_map/ppermute | solution.py:306
  33.4 2.0 %collective-permute-start.12 = (bf16[16,3712]{1,0:T(8,128)(2,1)S(1)}, bf16[16,3712]{1,0:T(8,128)(2,1)S(1)}, u32[]{:S(2)}, u32[]{:S(2)}) collective-permute-start(bf16[16,3712]{1,0:T(8,128)(2,1)S(1)} %get-tuple-element.52), channel_id=1, source_target_pairs={{0,4},{1,5},{2,6},{3,7},{4,12},{5,13},{6,14},{7,15},{8,0},{9,1},{1... | collective-permute-start | bytes 356360 | tf_op jit(solution)/shard_map/ppermute | solution.py:306
  35.3 1.5 %collective-permute-start.13 = (bf16[16,3712]{1,0:T(8,128)(2,1)S(1)}, bf16[16,3712]{1,0:T(8,128)(2,1)S(1)}, u32[]{:S(2)}, u32[]{:S(2)}) collective-permute-start(bf16[16,3712]{1,0:T(8,128)(2,1)S(1)} %get-tuple-element.53), channel_id=1, source_target_pairs={{0,16},{1,17},{2,18},{3,19},{4,20},{5,21},{6,22},{7,23},{8,24},{9,... | collective-permute-start | bytes 356360 | tf_op jit(solution)/shard_map/ppermute | solution.py:306
  36.8 1.5 %collective-permute-start.14 = (bf16[16,3712]{1,0:T(8,128)(2,1)S(1)}, bf16[16,3712]{1,0:T(8,128)(2,1)S(1)}, u32[]{:S(2)}, u32[]{:S(2)}) collective-permute-start(bf16[16,3712]{1,0:T(8,128)(2,1)S(1)} %get-tuple-element.54), channel_id=1, source_target_pairs={{0,18},{1,19},{2,16},{3,17},{4,22},{5,23},{6,20},{7,21},{8,26},{9,... | collective-permute-start | bytes 356360 | tf_op jit(solution)/shard_map/ppermute | solution.py:306
  38.7 2.9 %collective-permute-start.9 = (bf16[16,3712]{1,0:T(8,128)(2,1)S(1)}, bf16[16,3712]{1,0:T(8,128)(2,1)S(1)}, u32[]{:S(2)}, u32[]{:S(2)}) collective-permute-start(bf16[16,3712]{1,0:T(8,128)(2,1)S(1)} %get-tuple-element.49), channel_id=1, source_target_pairs={{0,24},{1,25},{2,26},{3,27},{4,16},{5,17},{6,18},{7,19},{8,28},{9,... | collective-permute-start | bytes 356360 | tf_op jit(solution)/shard_map/ppermute | solution.py:306
  42.4 1.3 %collective-permute-done.14.refs_1_ = bf16[16,3712]{1,0:T(8,128)(2,1)S(1)} collective-permute-done((bf16[16,3712]{1,0:T(8,128)(2,1)S(1)}, bf16[16,3712]{1,0:T(8,128)(2,1)S(1)}, u32[]{:S(2)}, u32[]{:S(2)}) %collective-permute-start.14) | collective-permute-done | bytes 118816 | tf_op jit(solution)/shard_map/ppermute | solution.py:306
  45.0 1.9 %collective-permute-start.16 = (bf16[32,3584]{1,0:T(8,128)(2,1)S(1)}, bf16[32,3584]{1,0:T(8,128)(2,1)S(1)}, u32[]{:S(2)}, u32[]{:S(2)}) collective-permute-start(bf16[32,3584]{1,0:T(8,128)(2,1)S(1)} %combine.2), channel_id=1, source_target_pairs={{0,20},{1,21},{2,22},{3,23},{4,28},{5,29},{6,30},{7,31},{8,16},{9,... | collective-permute-start | bytes 688136 | tf_op jit(solution)/shard_map/ppermute | solution.py:306
  46.8 3.3 %collective-permute-start.15 = (bf16[16,3712]{1,0:T(8,128)(2,1)S(1)}, bf16[16,3712]{1,0:T(8,128)(2,1)S(1)}, u32[]{:S(2)}, u32[]{:S(2)}) collective-permute-start(bf16[16,3712]{1,0:T(8,128)(2,1)S(1)} %get-tuple-element.58), channel_id=1, source_target_pairs={{0,26},{1,27},{2,24},{3,25},{4,18},{5,19},{6,16},{7,17},{8,30},{9,... | collective-permute-start | bytes 356360 | tf_op jit(solution)/shard_map/ppermute | solution.py:306
  50.2 5.3 %collective-permute-done.15.refs_3_ = bf16[16,3712]{1,0:T(8,128)(2,1)S(1)} collective-permute-done((bf16[16,3712]{1,0:T(8,128)(2,1)S(1)}, bf16[16,3712]{1,0:T(8,128)(2,1)S(1)}, u32[]{:S(2)}, u32[]{:S(2)}) %collective-permute-start.15) | collective-permute-done | bytes 118816 | tf_op jit(solution)/shard_map/ppermute | solution.py:306
  55.4 1.1 %combine.3 = bf16[32,3584]{1,0:T(8,128)(2,1)} custom-call(bf16[16,3712]{1,0:T(8,128)(2,1)S(1)} %collective-permute-done.13.refs_0_, bf16[16,3712]{1,0:T(8,128)(2,1)S(1)} %collective-permute-done.14.refs_1_, bf16[16,3712]{1,0:T(8,128)(2,1)S(1)} %collective-permute-done.9.refs_2_, bf16[16,3712]{1,0:T(8,128)(2,1)S(1)} %collective-permute-done.15.refs_3_, ...), custom_call_target="tpu_custom_call" | custom-call | tf_op jit(solution)/shard_map/combine/pallas_call | solution.py:84
  (23 shorter events, 5.4 us)
Async XLA Ops:
  0.0 29.1 %collective-permute-start.7 = (bf16[3584,1024]{1,0:T(8,128)(2,1)}, bf16[3584,1024]{1,0:T(8,128)(2,1)S(1)}, u32[]{:S(2)}, u32[]{:S(2)}) collective-permute-start(bf16[3584,1024]{1,0:T(8,128)(2,1)} %bitcast.10), channel_id=1, source_target_pairs={{0,1},{1,0},{2,3},{3,2},{4,5},{5,4},{6,7},{7,6},{8,9},{9,8},{10,11... | collective-permute-start | bytes 22020104 | tf_op jit(solution)/shard_map/ppermute | solution.py:324
  0.5 28.6 %collective-permute-start.8 = (bf16[512,3584]{1,0:T(8,128)(2,1)}, bf16[512,3584]{1,0:T(8,128)(2,1)S(1)}, u32[]{:S(2)}, u32[]{:S(2)}) collective-permute-start(bf16[512,3584]{1,0:T(8,128)(2,1)} %bitcast.12), channel_id=1, source_target_pairs={{0,1},{1,0},{2,3},{3,2},{4,5},{5,4},{6,7},{7,6},{8,9},{9,8},{10,11... | collective-permute-start | bytes 11010056 | tf_op jit(solution)/shard_map/ppermute | solution.py:323
  1.5 10.5 %collective-permute-start.1 = (bf16[32,3712]{1,0:T(8,128)(2,1)S(1)}, bf16[32,3712]{1,0:T(8,128)(2,1)S(1)}, u32[]{:S(2)}, u32[]{:S(2)}) collective-permute-start(bf16[32,3712]{1,0:T(8,128)(2,1)S(1)} %prepare.1.block), channel_id=1, source_target_pairs={{0,4},{1,5},{2,6},{3,7},{4,12},{5,13},{6,14},{7,15},{8,0},{9,1},{1... | collective-permute-start | bytes 712712 | tf_op jit(solution)/shard_map/ppermute | solution.py:306
  5.0 7.0 %collective-permute-start = (bf16[16,3712]{1,0:T(8,128)(2,1)S(1)}, bf16[16,3712]{1,0:T(8,128)(2,1)S(1)}, u32[]{:S(2)}, u32[]{:S(2)}) collective-permute-start(bf16[16,3712]{1,0:T(8,128)(2,1)S(1)} %get-tuple-element.35), channel_id=1, source_target_pairs={{0,2},{1,3},{2,0},{3,1},{4,6},{5,7},{6,4},{7,5},{8,10},{9,11},{10,... | collective-permute-start | bytes 356360 | tf_op jit(solution)/shard_map/ppermute | solution.py:306
  6.6 3.1 %copy-start = (bf16[1,3584,1024]{2,1,0:T(8,128)(2,1)S(1)}, bf16[1,3584,1024]{2,1,0:T(8,128)(2,1)}, u32[]{:S(2)}) copy-start(bf16[1,3584,1024]{2,1,0:T(8,128)(2,1)} %param.8) | copy-start | bytes 22020100
  9.7 2.0 %copy-start.1 = (bf16[1,512,3584]{2,1,0:T(8,128)(2,1)S(1)}, bf16[1,512,3584]{2,1,0:T(8,128)(2,1)}, u32[]{:S(2)}) copy-start(bf16[1,512,3584]{2,1,0:T(8,128)(2,1)} %param.9) | copy-start | bytes 11010052
  12.4 5.3 %collective-permute-start.4 = (bf16[16,3712]{1,0:T(8,128)(2,1)S(1)}, bf16[16,3712]{1,0:T(8,128)(2,1)S(1)}, u32[]{:S(2)}, u32[]{:S(2)}) collective-permute-start(bf16[16,3712]{1,0:T(8,128)(2,1)S(1)} %get-tuple-element.42), channel_id=1, source_target_pairs={{0,2},{1,3},{2,0},{3,1},{4,6},{5,7},{6,4},{7,5},{8,10},{9,11},{10,... | collective-permute-start | bytes 356360 | tf_op jit(solution)/shard_map/ppermute | solution.py:306
  13.6 6.3 %collective-permute-start.2 = (bf16[16,3712]{1,0:T(8,128)(2,1)S(1)}, bf16[16,3712]{1,0:T(8,128)(2,1)S(1)}, u32[]{:S(2)}, u32[]{:S(2)}) collective-permute-start(bf16[16,3712]{1,0:T(8,128)(2,1)S(1)} %get-tuple-element.40), channel_id=1, source_target_pairs={{0,4},{1,5},{2,6},{3,7},{4,12},{5,13},{6,14},{7,15},{8,0},{9,1},{1... | collective-permute-start | bytes 356360 | tf_op jit(solution)/shard_map/ppermute | solution.py:306
  15.6 10.6 %collective-permute-start.3 = (bf16[16,3712]{1,0:T(8,128)(2,1)S(1)}, bf16[16,3712]{1,0:T(8,128)(2,1)S(1)}, u32[]{:S(2)}, u32[]{:S(2)}) collective-permute-start(bf16[16,3712]{1,0:T(8,128)(2,1)S(1)} %get-tuple-element.41), channel_id=1, source_target_pairs={{0,6},{1,7},{2,4},{3,5},{4,14},{5,15},{6,12},{7,13},{8,2},{9,3},{1... | collective-permute-start | bytes 356360 | tf_op jit(solution)/shard_map/ppermute | solution.py:306
  17.7 8.4 %collective-permute-start.5 = (bf16[16,3712]{1,0:T(8,128)(2,1)S(1)}, bf16[16,3712]{1,0:T(8,128)(2,1)S(1)}, u32[]{:S(2)}, u32[]{:S(2)}) collective-permute-start(bf16[16,3712]{1,0:T(8,128)(2,1)S(1)} %get-tuple-element.45), channel_id=1, source_target_pairs={{0,8},{1,9},{2,10},{3,11},{4,0},{5,1},{6,2},{7,3},{8,12},{9,13},{1... | collective-permute-start | bytes 356360 | tf_op jit(solution)/shard_map/ppermute | solution.py:306
  19.9 7.5 %collective-permute-start.6 = (bf16[16,3712]{1,0:T(8,128)(2,1)S(1)}, bf16[16,3712]{1,0:T(8,128)(2,1)S(1)}, u32[]{:S(2)}, u32[]{:S(2)}) collective-permute-start(bf16[16,3712]{1,0:T(8,128)(2,1)S(1)} %get-tuple-element.46), channel_id=1, source_target_pairs={{0,10},{1,11},{2,8},{3,9},{4,2},{5,3},{6,0},{7,1},{8,14},{9,15},{1... | collective-permute-start | bytes 356360 | tf_op jit(solution)/shard_map/ppermute | solution.py:306
  30.9 7.8 %collective-permute-start.10 = (bf16[16,3712]{1,0:T(8,128)(2,1)S(1)}, bf16[16,3712]{1,0:T(8,128)(2,1)S(1)}, u32[]{:S(2)}, u32[]{:S(2)}) collective-permute-start(bf16[16,3712]{1,0:T(8,128)(2,1)S(1)} %get-tuple-element.50), channel_id=1, source_target_pairs={{0,6},{1,7},{2,4},{3,5},{4,14},{5,15},{6,12},{7,13},{8,2},{9,3},{1... | collective-permute-start | bytes 356360 | tf_op jit(solution)/shard_map/ppermute | solution.py:306
  32.8 8.8 %collective-permute-start.11 = (bf16[16,3712]{1,0:T(8,128)(2,1)S(1)}, bf16[16,3712]{1,0:T(8,128)(2,1)S(1)}, u32[]{:S(2)}, u32[]{:S(2)}) collective-permute-start(bf16[16,3712]{1,0:T(8,128)(2,1)S(1)} %get-tuple-element.51), channel_id=1, source_target_pairs={{0,2},{1,3},{2,0},{3,1},{4,6},{5,7},{6,4},{7,5},{8,10},{9,11},{10,... | collective-permute-start | bytes 356360 | tf_op jit(solution)/shard_map/ppermute | solution.py:306
  33.4 8.3 %collective-permute-start.12 = (bf16[16,3712]{1,0:T(8,128)(2,1)S(1)}, bf16[16,3712]{1,0:T(8,128)(2,1)S(1)}, u32[]{:S(2)}, u32[]{:S(2)}) collective-permute-start(bf16[16,3712]{1,0:T(8,128)(2,1)S(1)} %get-tuple-element.52), channel_id=1, source_target_pairs={{0,4},{1,5},{2,6},{3,7},{4,12},{5,13},{6,14},{7,15},{8,0},{9,1},{1... | collective-permute-start | bytes 356360 | tf_op jit(solution)/shard_map/ppermute | solution.py:306
  35.3 7.1 %collective-permute-start.13 = (bf16[16,3712]{1,0:T(8,128)(2,1)S(1)}, bf16[16,3712]{1,0:T(8,128)(2,1)S(1)}, u32[]{:S(2)}, u32[]{:S(2)}) collective-permute-start(bf16[16,3712]{1,0:T(8,128)(2,1)S(1)} %get-tuple-element.53), channel_id=1, source_target_pairs={{0,16},{1,17},{2,18},{3,19},{4,20},{5,21},{6,22},{7,23},{8,24},{9,... | collective-permute-start | bytes 356360 | tf_op jit(solution)/shard_map/ppermute | solution.py:306
  36.8 7.0 %collective-permute-start.14 = (bf16[16,3712]{1,0:T(8,128)(2,1)S(1)}, bf16[16,3712]{1,0:T(8,128)(2,1)S(1)}, u32[]{:S(2)}, u32[]{:S(2)}) collective-permute-start(bf16[16,3712]{1,0:T(8,128)(2,1)S(1)} %get-tuple-element.54), channel_id=1, source_target_pairs={{0,18},{1,19},{2,16},{3,17},{4,22},{5,23},{6,20},{7,21},{8,26},{9,... | collective-permute-start | bytes 356360 | tf_op jit(solution)/shard_map/ppermute | solution.py:306
  38.7 5.8 %collective-permute-start.9 = (bf16[16,3712]{1,0:T(8,128)(2,1)S(1)}, bf16[16,3712]{1,0:T(8,128)(2,1)S(1)}, u32[]{:S(2)}, u32[]{:S(2)}) collective-permute-start(bf16[16,3712]{1,0:T(8,128)(2,1)S(1)} %get-tuple-element.49), channel_id=1, source_target_pairs={{0,24},{1,25},{2,26},{3,27},{4,16},{5,17},{6,18},{7,19},{8,28},{9,... | collective-permute-start | bytes 356360 | tf_op jit(solution)/shard_map/ppermute | solution.py:306
  45.0 10.5 %collective-permute-start.16 = (bf16[32,3584]{1,0:T(8,128)(2,1)S(1)}, bf16[32,3584]{1,0:T(8,128)(2,1)S(1)}, u32[]{:S(2)}, u32[]{:S(2)}) collective-permute-start(bf16[32,3584]{1,0:T(8,128)(2,1)S(1)} %combine.2), channel_id=1, source_target_pairs={{0,20},{1,21},{2,22},{3,23},{4,28},{5,29},{6,30},{7,31},{8,16},{9,... | collective-permute-start | bytes 688136 | tf_op jit(solution)/shard_map/ppermute | solution.py:306
  46.8 8.6 %collective-permute-start.15 = (bf16[16,3712]{1,0:T(8,128)(2,1)S(1)}, bf16[16,3712]{1,0:T(8,128)(2,1)S(1)}, u32[]{:S(2)}, u32[]{:S(2)}) collective-permute-start(bf16[16,3712]{1,0:T(8,128)(2,1)S(1)} %get-tuple-element.58), channel_id=1, source_target_pairs={{0,26},{1,27},{2,24},{3,25},{4,18},{5,19},{6,16},{7,17},{8,30},{9,... | collective-permute-start | bytes 356360 | tf_op jit(solution)/shard_map/ppermute | solution.py:306

commit v15 on v10

--- a/solution.py
+++ b/solution.py
@@ -340,17 +340,18 @@
     slots, total = near_pass(pieces, near)
     pieces = far_pass(slots, total, (far_in, far_out), capacity)
     piece = dict(zip(places, pieces))
-    merged = [
-        piece[3, 0],
-        sent(piece[2, 0], sections, 0, 1, 0),
-        sent(piece[2, 1], sections, 0, 1, 1),
-        sent(piece[3, 1], sections, 0, 0, 1),
+    blocks = [
+        sent(piece[2, 1], sections, 0, 0, 1),
+        sent(piece[1, 0], sections, 0, 1, 0),
+        sent(piece[1, 1], sections, 0, 1, 1),
+        piece[2, 0],
     ]
+    total = sent(combine(blocks, tok_count), sections, 0, 1, 0)
+    side = sent(piece[3, 1], sections, 0, 0, 1)
     straight = [sent(piece[0, flip], sections, 1, 0, flip) for flip in range(2)]
-    merged, straight = lax.optimization_barrier((merged, straight))
-    straight += [sent(piece[1, flip], sections, 1, -1, flip) for flip in range(2)]
-    merged = sent(combine(merged, tok_count), sections, 1, 1, 0)
-    return combine(straight, tok_count, merged)[None]
+    total, side, straight = lax.optimization_barrier((total, side, straight))
+    total = sent(combine([side, piece[3, 0]], tok_count, total), sections, 1, 1, 0)
+    return combine(straight, tok_count, total)[None]
 
 
 def per_device(rows, route_ids, route_weights, w_gate_up, w_down):

time: 56.6 us -> 59.7 us (1.055)
  waiting for transfers between devices: 17.3 us -> 22.2 us
  starting transfers between devices: 26.7 us -> 24.6 us
    ppermute x15, waiting for transfers between devices: 17.3 us -> 22.2 us  [sent(): return lax.ppermute(shard, ('section', 'expert'), pairs)]
    ppermute x15, starting transfers between devices: 26.2 us -> 24 us  [sent(): return lax.ppermute(shard, ('section', 'expert'), pairs)]
    pallas_call x9 -> x10, Pallas kernels: 7.6 us -> 8.02 us  [local_call(): pl.pallas_call(kernel, out_shape=out_shape, in_specs=[vmem if spec is Non...]
  transfers between devices with their start and end apart: 17 -> 17, of which waited for: 9 -> 10; matrix products, arithmetic and copies ran while one was open for 0% -> 0% of each run, Pallas kernels for 8% -> 7%
where the time goes in v15:
time: 59.7 us; the launch traced here: 59.5 us
  starting transfers between devices  24.6 us (41%)
  waiting for transfers between devices  22.2 us (37%)
  Pallas kernels  8.02 us (13%)
  local copies, waits for them, and re-layouts  4.62 us (8%)
    ppermute x15, starting transfers between devices, sent(): return lax.ppermute(shard, ('section', 'expert'), pairs)  24 us
    ppermute x15, waiting for transfers between devices, sent(): return lax.ppermute(shard, ('section', 'expert'), pairs)  22.2 us
    pallas_call x10, Pallas kernels, local_call(): pl.pallas_call(kernel, out_shape=out_shape, in_specs=[vmem if spec is Non...  8.02 us
    unnamed x4, local copies, waits for them, and re-layouts  4.62 us
  transfers between devices with their start and end apart: 17, of which 10 were waited for; matrix products, arithmetic and copies ran while one was open for 0% of the time, Pallas kernels for 7%

profile of v15, /device:TPU:0, one launch (start us, length us, event | category | flops | bytes accessed | tf_op | source)
XLA Modules:
  0.0 59.5 jit_solution(15904576127911280465)
XLA Ops:
  1.5 3.1 %collective-permute-start.1 = (bf16[32,3712]{1,0:T(8,128)(2,1)S(1)}, bf16[32,3712]{1,0:T(8,128)(2,1)S(1)}, u32[]{:S(2)}, u32[]{:S(2)}) collective-permute-start(bf16[32,3712]{1,0:T(8,128)(2,1)S(1)} %prepare.1.block), channel_id=1, source_target_pairs={{0,4},{1,5},{2,6},{3,7},{4,12},{5,13},{6,14},{7,15},{8,0},{9,1},{1... | collective-permute-start | bytes 712712 | tf_op jit(solution)/shard_map/ppermute | solution.py:306
  5.0 1.6 %collective-permute-start = (bf16[16,3712]{1,0:T(8,128)(2,1)S(1)}, bf16[16,3712]{1,0:T(8,128)(2,1)S(1)}, u32[]{:S(2)}, u32[]{:S(2)}) collective-permute-start(bf16[16,3712]{1,0:T(8,128)(2,1)S(1)} %get-tuple-element.33), channel_id=1, source_target_pairs={{0,2},{1,3},{2,0},{3,1},{4,6},{5,7},{6,4},{7,5},{8,10},{9,11},{10,... | collective-permute-start | bytes 356360 | tf_op jit(solution)/shard_map/ppermute | solution.py:306
  6.6 3.1 %copy-done = bf16[1,3584,1024]{2,1,0:T(8,128)(2,1)S(1)} copy-done((bf16[1,3584,1024]{2,1,0:T(8,128)(2,1)S(1)}, bf16[1,3584,1024]{2,1,0:T(8,128)(2,1)}, u32[]{:S(2)}) %copy-start) | copy-done | bytes 7340056
  10.2 1.5 %copy-done.1 = bf16[1,512,3584]{2,1,0:T(8,128)(2,1)S(1)} copy-done((bf16[1,512,3584]{2,1,0:T(8,128)(2,1)S(1)}, bf16[1,512,3584]{2,1,0:T(8,128)(2,1)}, u32[]{:S(2)}) %copy-start.1) | copy-done | bytes 3670040
  12.4 1.2 %collective-permute-start.4 = (bf16[16,3712]{1,0:T(8,128)(2,1)S(1)}, bf16[16,3712]{1,0:T(8,128)(2,1)S(1)}, u32[]{:S(2)}, u32[]{:S(2)}) collective-permute-start(bf16[16,3712]{1,0:T(8,128)(2,1)S(1)} %get-tuple-element.40), channel_id=1, source_target_pairs={{0,2},{1,3},{2,0},{3,1},{4,6},{5,7},{6,4},{7,5},{8,10},{9,11},{10,... | collective-permute-start | bytes 356360 | tf_op jit(solution)/shard_map/ppermute | solution.py:306
  13.6 2.0 %collective-permute-start.2 = (bf16[16,3712]{1,0:T(8,128)(2,1)S(1)}, bf16[16,3712]{1,0:T(8,128)(2,1)S(1)}, u32[]{:S(2)}, u32[]{:S(2)}) collective-permute-start(bf16[16,3712]{1,0:T(8,128)(2,1)S(1)} %get-tuple-element.38), channel_id=1, source_target_pairs={{0,4},{1,5},{2,6},{3,7},{4,12},{5,13},{6,14},{7,15},{8,0},{9,1},{1... | collective-permute-start | bytes 356360 | tf_op jit(solution)/shard_map/ppermute | solution.py:306
  15.6 2.1 %collective-permute-start.3 = (bf16[16,3712]{1,0:T(8,128)(2,1)S(1)}, bf16[16,3712]{1,0:T(8,128)(2,1)S(1)}, u32[]{:S(2)}, u32[]{:S(2)}) collective-permute-start(bf16[16,3712]{1,0:T(8,128)(2,1)S(1)} %get-tuple-element.39), channel_id=1, source_target_pairs={{0,6},{1,7},{2,4},{3,5},{4,14},{5,15},{6,12},{7,13},{8,2},{9,3},{1... | collective-permute-start | bytes 356360 | tf_op jit(solution)/shard_map/ppermute | solution.py:306
  17.7 1.7 %collective-permute-start.5 = (bf16[16,3712]{1,0:T(8,128)(2,1)S(1)}, bf16[16,3712]{1,0:T(8,128)(2,1)S(1)}, u32[]{:S(2)}, u32[]{:S(2)}) collective-permute-start(bf16[16,3712]{1,0:T(8,128)(2,1)S(1)} %get-tuple-element.43), channel_id=1, source_target_pairs={{0,8},{1,9},{2,10},{3,11},{4,0},{5,1},{6,2},{7,3},{8,12},{9,13},{1... | collective-permute-start | bytes 356360 | tf_op jit(solution)/shard_map/ppermute | solution.py:306
  19.9 2.2 %collective-permute-start.6 = (bf16[16,3712]{1,0:T(8,128)(2,1)S(1)}, bf16[16,3712]{1,0:T(8,128)(2,1)S(1)}, u32[]{:S(2)}, u32[]{:S(2)}) collective-permute-start(bf16[16,3712]{1,0:T(8,128)(2,1)S(1)} %get-tuple-element.44), channel_id=1, source_target_pairs={{0,10},{1,11},{2,8},{3,9},{4,2},{5,3},{6,0},{7,1},{8,14},{9,15},{1... | collective-permute-start | bytes 356360 | tf_op jit(solution)/shard_map/ppermute | solution.py:306
  22.1 4.1 %collective-permute-done.3.refs_4_ = bf16[16,3712]{1,0:T(8,128)(2,1)S(1)} collective-permute-done((bf16[16,3712]{1,0:T(8,128)(2,1)S(1)}, bf16[16,3712]{1,0:T(8,128)(2,1)S(1)}, u32[]{:S(2)}, u32[]{:S(2)}) %collective-permute-start.3) | collective-permute-done | bytes 118816 | tf_op jit(solution)/shard_map/ppermute | solution.py:306
  26.2 1.2 %collective-permute-done.6.refs_7_ = bf16[16,3712]{1,0:T(8,128)(2,1)S(1)} collective-permute-done((bf16[16,3712]{1,0:T(8,128)(2,1)S(1)}, bf16[16,3712]{1,0:T(8,128)(2,1)S(1)}, u32[]{:S(2)}, u32[]{:S(2)}) %collective-permute-start.6) | collective-permute-done | bytes 118816 | tf_op jit(solution)/shard_map/ppermute | solution.py:306
  27.3 1.8 %near_pass.1 = (bf16[128,3712]{1,0:T(8,128)(2,1)S(1)}, f32[128,3584]{1,0:T(8,128)S(1)}) custom-call(bf16[16,3712]{1,0:T(8,128)(2,1)S(1)} %get-tuple-element.32.refs_0_, bf16[16,3712]{1,0:T(8,128)(2,1)S(1)} %collective-permute-done.refs_1_, bf16[16,3712]{1,0:T(8,128)(2,1)S(1)} %get-tuple-element.37.refs_2_, ...), custom_call_target="tpu_custom_call" | custom-call | bytes 11010048 | tf_op jit(solution)/shard_map/near_pass/pallas_call | solution.py:84
  29.1 1.7 %far_pass.1 = (bf16[16,3712]{1,0:T(8,128)(2,1)S(1)}, bf16[16,3712]{1,0:T(8,128)(2,1)S(1)}, bf16[16,3712]{1,0:T(8,128)(2,1)S(1)}, bf16[16,3712]{1,0:T(8,128)(2,1)...) custom-call(bf16[128,3712]{1,0:T(8,128)(2,1)S(1)} %get-tuple-element, ...), custom_call_target="tpu_custom_call" | custom-call | bytes 11010048 | tf_op jit(solution)/shard_map/far_pass/pallas_call | solution.py:84
  31.9 2.9 %collective-permute-start.11 = (bf16[16,3712]{1,0:T(8,128)(2,1)S(1)}, bf16[16,3712]{1,0:T(8,128)(2,1)S(1)}, u32[]{:S(2)}, u32[]{:S(2)}) collective-permute-start(bf16[16,3712]{1,0:T(8,128)(2,1)S(1)} %get-tuple-element.49), channel_id=1, source_target_pairs={{0,6},{1,7},{2,4},{3,5},{4,14},{5,15},{6,12},{7,13},{8,2},{9,3},{1... | collective-permute-start | bytes 356360 | tf_op jit(solution)/shard_map/ppermute | solution.py:306
  35.3 2.4 %collective-permute-done.10.refs_1_ = bf16[16,3712]{1,0:T(8,128)(2,1)S(1)} collective-permute-done((bf16[16,3712]{1,0:T(8,128)(2,1)S(1)}, bf16[16,3712]{1,0:T(8,128)(2,1)S(1)}, u32[]{:S(2)}, u32[]{:S(2)}) %collective-permute-start.10) | collective-permute-done | bytes 118816 | tf_op jit(solution)/shard_map/ppermute | solution.py:306
  37.7 2.0 %collective-permute-done.11.refs_2_ = bf16[16,3712]{1,0:T(8,128)(2,1)S(1)} collective-permute-done((bf16[16,3712]{1,0:T(8,128)(2,1)S(1)}, bf16[16,3712]{1,0:T(8,128)(2,1)S(1)}, u32[]{:S(2)}, u32[]{:S(2)}) %collective-permute-start.11) | collective-permute-done | bytes 118816 | tf_op jit(solution)/shard_map/ppermute | solution.py:306
  39.7 1.3 %collective-permute-done.9.refs_0_ = bf16[16,3712]{1,0:T(8,128)(2,1)S(1)} collective-permute-done((bf16[16,3712]{1,0:T(8,128)(2,1)S(1)}, bf16[16,3712]{1,0:T(8,128)(2,1)S(1)}, u32[]{:S(2)}, u32[]{:S(2)}) %collective-permute-start.9) | collective-permute-done | bytes 118816 | tf_op jit(solution)/shard_map/ppermute | solution.py:306
  41.6 1.3 %collective-permute-start.13 = (bf16[16,3712]{1,0:T(8,128)(2,1)S(1)}, bf16[16,3712]{1,0:T(8,128)(2,1)S(1)}, u32[]{:S(2)}, u32[]{:S(2)}) collective-permute-start(bf16[16,3712]{1,0:T(8,128)(2,1)S(1)} %get-tuple-element.51), channel_id=1, source_target_pairs={{0,2},{1,3},{2,0},{3,1},{4,6},{5,7},{6,4},{7,5},{8,10},{9,11},{10,... | collective-permute-start | bytes 356360 | tf_op jit(solution)/shard_map/ppermute | solution.py:306
  42.9 1.5 %collective-permute-start.14 = (bf16[16,3712]{1,0:T(8,128)(2,1)S(1)}, bf16[16,3712]{1,0:T(8,128)(2,1)S(1)}, u32[]{:S(2)}, u32[]{:S(2)}) collective-permute-start(bf16[16,3712]{1,0:T(8,128)(2,1)S(1)} %get-tuple-element.52), channel_id=1, source_target_pairs={{0,16},{1,17},{2,18},{3,19},{4,20},{5,21},{6,22},{7,23},{8,24},{9,... | collective-permute-start | bytes 356360 | tf_op jit(solution)/shard_map/ppermute | solution.py:306
  45.1 2.6 %collective-permute-done.13.refs_0_ = bf16[16,3712]{1,0:T(8,128)(2,1)S(1)} collective-permute-done((bf16[16,3712]{1,0:T(8,128)(2,1)S(1)}, bf16[16,3712]{1,0:T(8,128)(2,1)S(1)}, u32[]{:S(2)}, u32[]{:S(2)}) %collective-permute-start.13) | collective-permute-done | bytes 118816 | tf_op jit(solution)/shard_map/ppermute | solution.py:306
  47.8 2.3 %collective-permute-done.15.refs_1_ = bf16[16,3712]{1,0:T(8,128)(2,1)S(1)} collective-permute-done((bf16[16,3712]{1,0:T(8,128)(2,1)S(1)}, bf16[16,3712]{1,0:T(8,128)(2,1)S(1)}, u32[]{:S(2)}, u32[]{:S(2)}) %collective-permute-start.15) | collective-permute-done | bytes 118816 | tf_op jit(solution)/shard_map/ppermute | solution.py:306
  50.5 2.0 %collective-permute-start.16 = (bf16[32,3584]{1,0:T(8,128)(2,1)S(1)}, bf16[32,3584]{1,0:T(8,128)(2,1)S(1)}, u32[]{:S(2)}, u32[]{:S(2)}) collective-permute-start(bf16[32,3584]{1,0:T(8,128)(2,1)S(1)} %combine.4), channel_id=1, source_target_pairs={{0,20},{1,21},{2,22},{3,23},{4,28},{5,29},{6,30},{7,31},{8,16},{9,... | collective-permute-start | bytes 688136 | tf_op jit(solution)/shard_map/ppermute | solution.py:306
  52.5 5.9 %collective-permute-done.16.refs_2_ = bf16[32,3584]{1,0:T(8,128)(2,1)S(1)} collective-permute-done((bf16[32,3584]{1,0:T(8,128)(2,1)S(1)}, bf16[32,3584]{1,0:T(8,128)(2,1)S(1)}, u32[]{:S(2)}, u32[]{:S(2)}) %collective-permute-start.16) | collective-permute-done | bytes 229408 | tf_op jit(solution)/shard_map/ppermute | solution.py:306
  58.4 1.1 %combine.5 = bf16[32,3584]{1,0:T(8,128)(2,1)} custom-call(bf16[16,3712]{1,0:T(8,128)(2,1)S(1)} %collective-permute-done.14.refs_0_, bf16[16,3712]{1,0:T(8,128)(2,1)S(1)} %collective-permute-done.15.refs_1_, bf16[32,3584]{1,0:T(8,128)(2,1)S(1)} %collective-permute-done.16.refs_2_), custom_call_target="tpu_custom_call" | custom-call | tf_op jit(solution)/shard_map/combine/pallas_call | solution.py:84
  (24 shorter events, 6.9 us)
Async XLA Ops:
  0.0 29.1 %collective-permute-start.7 = (bf16[3584,1024]{1,0:T(8,128)(2,1)}, bf16[3584,1024]{1,0:T(8,128)(2,1)S(1)}, u32[]{:S(2)}, u32[]{:S(2)}) collective-permute-start(bf16[3584,1024]{1,0:T(8,128)(2,1)} %bitcast.10), channel_id=1, source_target_pairs={{0,1},{1,0},{2,3},{3,2},{4,5},{5,4},{6,7},{7,6},{8,9},{9,8},{10,11... | collective-permute-start | bytes 22020104 | tf_op jit(solution)/shard_map/ppermute | solution.py:324
  0.5 28.6 %collective-permute-start.8 = (bf16[512,3584]{1,0:T(8,128)(2,1)}, bf16[512,3584]{1,0:T(8,128)(2,1)S(1)}, u32[]{:S(2)}, u32[]{:S(2)}) collective-permute-start(bf16[512,3584]{1,0:T(8,128)(2,1)} %bitcast.12), channel_id=1, source_target_pairs={{0,1},{1,0},{2,3},{3,2},{4,5},{5,4},{6,7},{7,6},{8,9},{9,8},{10,11... | collective-permute-start | bytes 11010056 | tf_op jit(solution)/shard_map/ppermute | solution.py:323
  1.5 10.5 %collective-permute-start.1 = (bf16[32,3712]{1,0:T(8,128)(2,1)S(1)}, bf16[32,3712]{1,0:T(8,128)(2,1)S(1)}, u32[]{:S(2)}, u32[]{:S(2)}) collective-permute-start(bf16[32,3712]{1,0:T(8,128)(2,1)S(1)} %prepare.1.block), channel_id=1, source_target_pairs={{0,4},{1,5},{2,6},{3,7},{4,12},{5,13},{6,14},{7,15},{8,0},{9,1},{1... | collective-permute-start | bytes 712712 | tf_op jit(solution)/shard_map/ppermute | solution.py:306
  5.0 7.0 %collective-permute-start = (bf16[16,3712]{1,0:T(8,128)(2,1)S(1)}, bf16[16,3712]{1,0:T(8,128)(2,1)S(1)}, u32[]{:S(2)}, u32[]{:S(2)}) collective-permute-start(bf16[16,3712]{1,0:T(8,128)(2,1)S(1)} %get-tuple-element.33), channel_id=1, source_target_pairs={{0,2},{1,3},{2,0},{3,1},{4,6},{5,7},{6,4},{7,5},{8,10},{9,11},{10,... | collective-permute-start | bytes 356360 | tf_op jit(solution)/shard_map/ppermute | solution.py:306
  6.6 3.1 %copy-start = (bf16[1,3584,1024]{2,1,0:T(8,128)(2,1)S(1)}, bf16[1,3584,1024]{2,1,0:T(8,128)(2,1)}, u32[]{:S(2)}) copy-start(bf16[1,3584,1024]{2,1,0:T(8,128)(2,1)} %param.8) | copy-start | bytes 22020100
  9.7 2.0 %copy-start.1 = (bf16[1,512,3584]{2,1,0:T(8,128)(2,1)S(1)}, bf16[1,512,3584]{2,1,0:T(8,128)(2,1)}, u32[]{:S(2)}) copy-start(bf16[1,512,3584]{2,1,0:T(8,128)(2,1)} %param.9) | copy-start | bytes 11010052
  12.4 5.3 %collective-permute-start.4 = (bf16[16,3712]{1,0:T(8,128)(2,1)S(1)}, bf16[16,3712]{1,0:T(8,128)(2,1)S(1)}, u32[]{:S(2)}, u32[]{:S(2)}) collective-permute-start(bf16[16,3712]{1,0:T(8,128)(2,1)S(1)} %get-tuple-element.40), channel_id=1, source_target_pairs={{0,2},{1,3},{2,0},{3,1},{4,6},{5,7},{6,4},{7,5},{8,10},{9,11},{10,... | collective-permute-start | bytes 356360 | tf_op jit(solution)/shard_map/ppermute | solution.py:306
  13.6 6.3 %collective-permute-start.2 = (bf16[16,3712]{1,0:T(8,128)(2,1)S(1)}, bf16[16,3712]{1,0:T(8,128)(2,1)S(1)}, u32[]{:S(2)}, u32[]{:S(2)}) collective-permute-start(bf16[16,3712]{1,0:T(8,128)(2,1)S(1)} %get-tuple-element.38), channel_id=1, source_target_pairs={{0,4},{1,5},{2,6},{3,7},{4,12},{5,13},{6,14},{7,15},{8,0},{9,1},{1... | collective-permute-start | bytes 356360 | tf_op jit(solution)/shard_map/ppermute | solution.py:306
  15.6 10.6 %collective-permute-start.3 = (bf16[16,3712]{1,0:T(8,128)(2,1)S(1)}, bf16[16,3712]{1,0:T(8,128)(2,1)S(1)}, u32[]{:S(2)}, u32[]{:S(2)}) collective-permute-start(bf16[16,3712]{1,0:T(8,128)(2,1)S(1)} %get-tuple-element.39), channel_id=1, source_target_pairs={{0,6},{1,7},{2,4},{3,5},{4,14},{5,15},{6,12},{7,13},{8,2},{9,3},{1... | collective-permute-start | bytes 356360 | tf_op jit(solution)/shard_map/ppermute | solution.py:306
  17.7 8.4 %collective-permute-start.5 = (bf16[16,3712]{1,0:T(8,128)(2,1)S(1)}, bf16[16,3712]{1,0:T(8,128)(2,1)S(1)}, u32[]{:S(2)}, u32[]{:S(2)}) collective-permute-start(bf16[16,3712]{1,0:T(8,128)(2,1)S(1)} %get-tuple-element.43), channel_id=1, source_target_pairs={{0,8},{1,9},{2,10},{3,11},{4,0},{5,1},{6,2},{7,3},{8,12},{9,13},{1... | collective-permute-start | bytes 356360 | tf_op jit(solution)/shard_map/ppermute | solution.py:306
  19.9 7.5 %collective-permute-start.6 = (bf16[16,3712]{1,0:T(8,128)(2,1)S(1)}, bf16[16,3712]{1,0:T(8,128)(2,1)S(1)}, u32[]{:S(2)}, u32[]{:S(2)}) collective-permute-start(bf16[16,3712]{1,0:T(8,128)(2,1)S(1)} %get-tuple-element.44), channel_id=1, source_target_pairs={{0,10},{1,11},{2,8},{3,9},{4,2},{5,3},{6,0},{7,1},{8,14},{9,15},{1... | collective-permute-start | bytes 356360 | tf_op jit(solution)/shard_map/ppermute | solution.py:306
  30.9 6.8 %collective-permute-start.10 = (bf16[16,3712]{1,0:T(8,128)(2,1)S(1)}, bf16[16,3712]{1,0:T(8,128)(2,1)S(1)}, u32[]{:S(2)}, u32[]{:S(2)}) collective-permute-start(bf16[16,3712]{1,0:T(8,128)(2,1)S(1)} %get-tuple-element.48), channel_id=1, source_target_pairs={{0,4},{1,5},{2,6},{3,7},{4,12},{5,13},{6,14},{7,15},{8,0},{9,1},{1... | collective-permute-start | bytes 356360 | tf_op jit(solution)/shard_map/ppermute | solution.py:306
  31.9 7.8 %collective-permute-start.11 = (bf16[16,3712]{1,0:T(8,128)(2,1)S(1)}, bf16[16,3712]{1,0:T(8,128)(2,1)S(1)}, u32[]{:S(2)}, u32[]{:S(2)}) collective-permute-start(bf16[16,3712]{1,0:T(8,128)(2,1)S(1)} %get-tuple-element.49), channel_id=1, source_target_pairs={{0,6},{1,7},{2,4},{3,5},{4,14},{5,15},{6,12},{7,13},{8,2},{9,3},{1... | collective-permute-start | bytes 356360 | tf_op jit(solution)/shard_map/ppermute | solution.py:306
  34.8 6.1 %collective-permute-start.9 = (bf16[16,3712]{1,0:T(8,128)(2,1)S(1)}, bf16[16,3712]{1,0:T(8,128)(2,1)S(1)}, u32[]{:S(2)}, u32[]{:S(2)}) collective-permute-start(bf16[16,3712]{1,0:T(8,128)(2,1)S(1)} %get-tuple-element.47), channel_id=1, source_target_pairs={{0,2},{1,3},{2,0},{3,1},{4,6},{5,7},{6,4},{7,5},{8,10},{9,11},{10,... | collective-permute-start | bytes 356360 | tf_op jit(solution)/shard_map/ppermute | solution.py:306
  41.4 8.7 %collective-permute-start.12 = (bf16[32,3584]{1,0:T(8,128)(2,1)S(1)}, bf16[32,3584]{1,0:T(8,128)(2,1)S(1)}, u32[]{:S(2)}, u32[]{:S(2)}) collective-permute-start(bf16[32,3584]{1,0:T(8,128)(2,1)S(1)} %combine.3), channel_id=1, source_target_pairs={{0,4},{1,5},{2,6},{3,7},{4,12},{5,13},{6,14},{7,15},{8,0},{9,1},{1... | collective-permute-start | bytes 688136 | tf_op jit(solution)/shard_map/ppermute | solution.py:306
  41.6 6.1 %collective-permute-start.13 = (bf16[16,3712]{1,0:T(8,128)(2,1)S(1)}, bf16[16,3712]{1,0:T(8,128)(2,1)S(1)}, u32[]{:S(2)}, u32[]{:S(2)}) collective-permute-start(bf16[16,3712]{1,0:T(8,128)(2,1)S(1)} %get-tuple-element.51), channel_id=1, source_target_pairs={{0,2},{1,3},{2,0},{3,1},{4,6},{5,7},{6,4},{7,5},{8,10},{9,11},{10,... | collective-permute-start | bytes 356360 | tf_op jit(solution)/shard_map/ppermute | solution.py:306
  42.9 4.9 %collective-permute-start.14 = (bf16[16,3712]{1,0:T(8,128)(2,1)S(1)}, bf16[16,3712]{1,0:T(8,128)(2,1)S(1)}, u32[]{:S(2)}, u32[]{:S(2)}) collective-permute-start(bf16[16,3712]{1,0:T(8,128)(2,1)S(1)} %get-tuple-element.52), channel_id=1, source_target_pairs={{0,16},{1,17},{2,18},{3,19},{4,20},{5,21},{6,22},{7,23},{8,24},{9,... | collective-permute-start | bytes 356360 | tf_op jit(solution)/shard_map/ppermute | solution.py:306
  44.4 5.7 %collective-permute-start.15 = (bf16[16,3712]{1,0:T(8,128)(2,1)S(1)}, bf16[16,3712]{1,0:T(8,128)(2,1)S(1)}, u32[]{:S(2)}, u32[]{:S(2)}) collective-permute-start(bf16[16,3712]{1,0:T(8,128)(2,1)S(1)} %get-tuple-element.53), channel_id=1, source_target_pairs={{0,18},{1,19},{2,16},{3,17},{4,22},{5,23},{6,20},{7,21},{8,26},{9,... | collective-permute-start | bytes 356360 | tf_op jit(solution)/shard_map/ppermute | solution.py:306
  50.5 7.9 %collective-permute-start.16 = (bf16[32,3584]{1,0:T(8,128)(2,1)S(1)}, bf16[32,3584]{1,0:T(8,128)(2,1)S(1)}, u32[]{:S(2)}, u32[]{:S(2)}) collective-permute-start(bf16[32,3584]{1,0:T(8,128)(2,1)S(1)} %combine.4), channel_id=1, source_target_pairs={{0,20},{1,21},{2,22},{3,23},{4,28},{5,29},{6,30},{7,31},{8,16},{9,... | collective-permute-start | bytes 688136 | tf_op jit(solution)/shard_map/ppermute | solution.py:306

commit v16 on v13

--- a/solution.py
+++ b/solution.py
@@ -340,17 +340,16 @@
     slots, total = near_pass(pieces, near)
     pieces = far_pass(slots, total, (far_in, far_out), capacity)
     piece = dict(zip(places, pieces))
-    straight = {at: sent(piece[at, 0], sections, 1, -at, 0) for at in range(2)}
     first = [
-        straight[1],
+        sent(piece[0, 0], sections, 1, 0, 0),
         sent(piece[2, 1], sections, 0, 1, 1),
         sent(piece[3, 1], sections, 0, 0, 1),
         sent(piece[2, 0], sections, 0, 1, 0),
-        straight[0],
     ]
-    one, *merged, zero = lax.optimization_barrier(first)
+    zero, *merged = lax.optimization_barrier(first)
     merged.append(piece[3, 0])
-    straight = [one, zero] + [sent(piece[at, 1], sections, 1, -at, 1) for at in range(2)]
+    straight = [zero, sent(piece[0, 1], sections, 1, 0, 1)]
+    straight += [sent(piece[1, flip], sections, 1, -1, flip) for flip in range(2)]
     merged = sent(combine(merged, tok_count), sections, 1, 1, 0)
     return combine(straight, tok_count, merged)[None]
 

time: 57.7 us -> 57.5 us (level)
  transfers between devices with their start and end apart: 17 -> 17, of which waited for: 9 -> 8; matrix products, arithmetic and copies ran while one was open for 0% -> 0% of each run, Pallas kernels for 8% -> 8%
where the time goes in v16:
time: 57.5 us; the launch traced here: 57.3 us
  starting transfers between devices  26.7 us (46%)
  waiting for transfers between devices  18.3 us (32%)
  Pallas kernels  7.61 us (13%)
  local copies, waits for them, and re-layouts  4.62 us (8%)
    ppermute x15, starting transfers between devices, sent(): return lax.ppermute(shard, ('section', 'expert'), pairs)  26.2 us
    ppermute x15, waiting for transfers between devices, sent(): return lax.ppermute(shard, ('section', 'expert'), pairs)  18.3 us
    pallas_call x9, Pallas kernels, local_call(): pl.pallas_call(kernel, out_shape=out_shape, in_specs=[vmem if spec is Non...  7.61 us
    unnamed x4, local copies, waits for them, and re-layouts  4.62 us
  transfers between devices with their start and end apart: 17, of which 8 were waited for; matrix products, arithmetic and copies ran while one was open for 0% of the time, Pallas kernels for 8%

profile of v16, /device:TPU:0, one launch (start us, length us, event | category | flops | bytes accessed | tf_op | source)
XLA Modules:
  0.0 57.3 jit_solution(13183247015375578185)
XLA Ops:
  0.5 1.0 %prepare.1.block = bf16[32,3712]{1,0:T(8,128)(2,1)S(1)} custom-call(s32[2,32]{1,0:T(2,128)} %bitcast.15, f32[2,32]{1,0:T(2,128)} %bitcast.16, bf16[32,3584]{1,0:T(8,128)(2,1)} %bitcast.14), custom_call_target="tpu_custom_call" | custom-call | tf_op jit(solution)/shard_map/prepare/pallas_call | solution.py:84
  1.5 3.1 %collective-permute-start.1 = (bf16[32,3712]{1,0:T(8,128)(2,1)S(1)}, bf16[32,3712]{1,0:T(8,128)(2,1)S(1)}, u32[]{:S(2)}, u32[]{:S(2)}) collective-permute-start(bf16[32,3712]{1,0:T(8,128)(2,1)S(1)} %prepare.1.block), channel_id=1, source_target_pairs={{0,4},{1,5},{2,6},{3,7},{4,12},{5,13},{6,14},{7,15},{8,0},{9,1},{1... | collective-permute-start | bytes 712712 | tf_op jit(solution)/shard_map/ppermute | solution.py:306
  5.0 1.6 %collective-permute-start = (bf16[16,3712]{1,0:T(8,128)(2,1)S(1)}, bf16[16,3712]{1,0:T(8,128)(2,1)S(1)}, u32[]{:S(2)}, u32[]{:S(2)}) collective-permute-start(bf16[16,3712]{1,0:T(8,128)(2,1)S(1)} %get-tuple-element.33), channel_id=1, source_target_pairs={{0,2},{1,3},{2,0},{3,1},{4,6},{5,7},{6,4},{7,5},{8,10},{9,11},{10,... | collective-permute-start | bytes 356360 | tf_op jit(solution)/shard_map/ppermute | solution.py:306
  6.6 3.1 %copy-done = bf16[1,3584,1024]{2,1,0:T(8,128)(2,1)S(1)} copy-done((bf16[1,3584,1024]{2,1,0:T(8,128)(2,1)S(1)}, bf16[1,3584,1024]{2,1,0:T(8,128)(2,1)}, u32[]{:S(2)}) %copy-start) | copy-done | bytes 7340056
  10.2 1.5 %copy-done.1 = bf16[1,512,3584]{2,1,0:T(8,128)(2,1)S(1)} copy-done((bf16[1,512,3584]{2,1,0:T(8,128)(2,1)S(1)}, bf16[1,512,3584]{2,1,0:T(8,128)(2,1)}, u32[]{:S(2)}) %copy-start.1) | copy-done | bytes 3670040
  12.4 1.2 %collective-permute-start.4 = (bf16[16,3712]{1,0:T(8,128)(2,1)S(1)}, bf16[16,3712]{1,0:T(8,128)(2,1)S(1)}, u32[]{:S(2)}, u32[]{:S(2)}) collective-permute-start(bf16[16,3712]{1,0:T(8,128)(2,1)S(1)} %get-tuple-element.40), channel_id=1, source_target_pairs={{0,2},{1,3},{2,0},{3,1},{4,6},{5,7},{6,4},{7,5},{8,10},{9,11},{10,... | collective-permute-start | bytes 356360 | tf_op jit(solution)/shard_map/ppermute | solution.py:306
  13.6 2.0 %collective-permute-start.2 = (bf16[16,3712]{1,0:T(8,128)(2,1)S(1)}, bf16[16,3712]{1,0:T(8,128)(2,1)S(1)}, u32[]{:S(2)}, u32[]{:S(2)}) collective-permute-start(bf16[16,3712]{1,0:T(8,128)(2,1)S(1)} %get-tuple-element.38), channel_id=1, source_target_pairs={{0,4},{1,5},{2,6},{3,7},{4,12},{5,13},{6,14},{7,15},{8,0},{9,1},{1... | collective-permute-start | bytes 356360 | tf_op jit(solution)/shard_map/ppermute | solution.py:306
  15.6 2.1 %collective-permute-start.3 = (bf16[16,3712]{1,0:T(8,128)(2,1)S(1)}, bf16[16,3712]{1,0:T(8,128)(2,1)S(1)}, u32[]{:S(2)}, u32[]{:S(2)}) collective-permute-start(bf16[16,3712]{1,0:T(8,128)(2,1)S(1)} %get-tuple-element.39), channel_id=1, source_target_pairs={{0,6},{1,7},{2,4},{3,5},{4,14},{5,15},{6,12},{7,13},{8,2},{9,3},{1... | collective-permute-start | bytes 356360 | tf_op jit(solution)/shard_map/ppermute | solution.py:306
  17.7 1.7 %collective-permute-start.5 = (bf16[16,3712]{1,0:T(8,128)(2,1)S(1)}, bf16[16,3712]{1,0:T(8,128)(2,1)S(1)}, u32[]{:S(2)}, u32[]{:S(2)}) collective-permute-start(bf16[16,3712]{1,0:T(8,128)(2,1)S(1)} %get-tuple-element.43), channel_id=1, source_target_pairs={{0,8},{1,9},{2,10},{3,11},{4,0},{5,1},{6,2},{7,3},{8,12},{9,13},{1... | collective-permute-start | bytes 356360 | tf_op jit(solution)/shard_map/ppermute | solution.py:306
  19.9 2.2 %collective-permute-start.6 = (bf16[16,3712]{1,0:T(8,128)(2,1)S(1)}, bf16[16,3712]{1,0:T(8,128)(2,1)S(1)}, u32[]{:S(2)}, u32[]{:S(2)}) collective-permute-start(bf16[16,3712]{1,0:T(8,128)(2,1)S(1)} %get-tuple-element.44), channel_id=1, source_target_pairs={{0,10},{1,11},{2,8},{3,9},{4,2},{5,3},{6,0},{7,1},{8,14},{9,15},{1... | collective-permute-start | bytes 356360 | tf_op jit(solution)/shard_map/ppermute | solution.py:306
  22.1 4.1 %collective-permute-done.3.refs_4_ = bf16[16,3712]{1,0:T(8,128)(2,1)S(1)} collective-permute-done((bf16[16,3712]{1,0:T(8,128)(2,1)S(1)}, bf16[16,3712]{1,0:T(8,128)(2,1)S(1)}, u32[]{:S(2)}, u32[]{:S(2)}) %collective-permute-start.3) | collective-permute-done | bytes 118816 | tf_op jit(solution)/shard_map/ppermute | solution.py:306
  26.2 1.2 %collective-permute-done.6.refs_7_ = bf16[16,3712]{1,0:T(8,128)(2,1)S(1)} collective-permute-done((bf16[16,3712]{1,0:T(8,128)(2,1)S(1)}, bf16[16,3712]{1,0:T(8,128)(2,1)S(1)}, u32[]{:S(2)}, u32[]{:S(2)}) %collective-permute-start.6) | collective-permute-done | bytes 118816 | tf_op jit(solution)/shard_map/ppermute | solution.py:306
  27.3 1.8 %near_pass.1 = (bf16[128,3712]{1,0:T(8,128)(2,1)S(1)}, f32[128,3584]{1,0:T(8,128)S(1)}) custom-call(bf16[16,3712]{1,0:T(8,128)(2,1)S(1)} %get-tuple-element.32.refs_0_, bf16[16,3712]{1,0:T(8,128)(2,1)S(1)} %collective-permute-done.refs_1_, bf16[16,3712]{1,0:T(8,128)(2,1)S(1)} %get-tuple-element.37.refs_2_, ...), custom_call_target="tpu_custom_call" | custom-call | bytes 11010048 | tf_op jit(solution)/shard_map/near_pass/pallas_call | solution.py:84
  29.1 1.7 %far_pass.1 = (bf16[16,3712]{1,0:T(8,128)(2,1)S(1)}, bf16[16,3712]{1,0:T(8,128)(2,1)S(1)}, bf16[16,3712]{1,0:T(8,128)(2,1)S(1)}, bf16[16,3712]{1,0:T(8,128)(2,1)...) custom-call(bf16[128,3712]{1,0:T(8,128)(2,1)S(1)} %get-tuple-element, ...), custom_call_target="tpu_custom_call" | custom-call | bytes 11010048 | tf_op jit(solution)/shard_map/far_pass/pallas_call | solution.py:84
  30.9 2.0 %collective-permute-start.10 = (bf16[16,3712]{1,0:T(8,128)(2,1)S(1)}, bf16[16,3712]{1,0:T(8,128)(2,1)S(1)}, u32[]{:S(2)}, u32[]{:S(2)}) collective-permute-start(bf16[16,3712]{1,0:T(8,128)(2,1)S(1)} %get-tuple-element.48), channel_id=1, source_target_pairs={{0,6},{1,7},{2,4},{3,5},{4,14},{5,15},{6,12},{7,13},{8,2},{9,3},{1... | collective-permute-start | bytes 356360 | tf_op jit(solution)/shard_map/ppermute | solution.py:306
  33.4 2.0 %collective-permute-start.12 = (bf16[16,3712]{1,0:T(8,128)(2,1)S(1)}, bf16[16,3712]{1,0:T(8,128)(2,1)S(1)}, u32[]{:S(2)}, u32[]{:S(2)}) collective-permute-start(bf16[16,3712]{1,0:T(8,128)(2,1)S(1)} %get-tuple-element.50), channel_id=1, source_target_pairs={{0,4},{1,5},{2,6},{3,7},{4,12},{5,13},{6,14},{7,15},{8,0},{9,1},{1... | collective-permute-start | bytes 356360 | tf_op jit(solution)/shard_map/ppermute | solution.py:306
  35.3 1.5 %collective-permute-start.9 = (bf16[16,3712]{1,0:T(8,128)(2,1)S(1)}, bf16[16,3712]{1,0:T(8,128)(2,1)S(1)}, u32[]{:S(2)}, u32[]{:S(2)}) collective-permute-start(bf16[16,3712]{1,0:T(8,128)(2,1)S(1)} %get-tuple-element.47), channel_id=1, source_target_pairs={{0,16},{1,17},{2,18},{3,19},{4,20},{5,21},{6,22},{7,23},{8,24},{9,... | collective-permute-start | bytes 356360 | tf_op jit(solution)/shard_map/ppermute | solution.py:306
  36.8 1.9 %collective-permute-done.10.refs_0_ = bf16[16,3712]{1,0:T(8,128)(2,1)S(1)} collective-permute-done((bf16[16,3712]{1,0:T(8,128)(2,1)S(1)}, bf16[16,3712]{1,0:T(8,128)(2,1)S(1)}, u32[]{:S(2)}, u32[]{:S(2)}) %collective-permute-start.10) | collective-permute-done | bytes 118816 | tf_op jit(solution)/shard_map/ppermute | solution.py:306
  38.9 0.7 %collective-permute-done.12.refs_2_ = bf16[16,3712]{1,0:T(8,128)(2,1)S(1)} collective-permute-done((bf16[16,3712]{1,0:T(8,128)(2,1)S(1)}, bf16[16,3712]{1,0:T(8,128)(2,1)S(1)}, u32[]{:S(2)}, u32[]{:S(2)}) %collective-permute-start.12) | collective-permute-done | bytes 118816 | tf_op jit(solution)/shard_map/ppermute | solution.py:306
  40.6 2.4 %collective-permute-start.16 = (bf16[32,3584]{1,0:T(8,128)(2,1)S(1)}, bf16[32,3584]{1,0:T(8,128)(2,1)S(1)}, u32[]{:S(2)}, u32[]{:S(2)}) collective-permute-start(bf16[32,3584]{1,0:T(8,128)(2,1)S(1)} %combine.2), channel_id=1, source_target_pairs={{0,20},{1,21},{2,22},{3,23},{4,28},{5,29},{6,30},{7,31},{8,16},{9,... | collective-permute-start | bytes 688136 | tf_op jit(solution)/shard_map/ppermute | solution.py:306
  43.0 0.6 %collective-permute-start.13 = (bf16[16,3712]{1,0:T(8,128)(2,1)S(1)}, bf16[16,3712]{1,0:T(8,128)(2,1)S(1)}, u32[]{:S(2)}, u32[]{:S(2)}) collective-permute-start(bf16[16,3712]{1,0:T(8,128)(2,1)S(1)} %get-tuple-element.52), channel_id=1, source_target_pairs={{0,18},{1,19},{2,16},{3,17},{4,22},{5,23},{6,20},{7,21},{8,26},{9,... | collective-permute-start | bytes 356360 | tf_op jit(solution)/shard_map/ppermute | solution.py:306
  43.6 3.4 %collective-permute-start.14 = (bf16[16,3712]{1,0:T(8,128)(2,1)S(1)}, bf16[16,3712]{1,0:T(8,128)(2,1)S(1)}, u32[]{:S(2)}, u32[]{:S(2)}) collective-permute-start(bf16[16,3712]{1,0:T(8,128)(2,1)S(1)} %get-tuple-element.53), channel_id=1, source_target_pairs={{0,24},{1,25},{2,26},{3,27},{4,16},{5,17},{6,18},{7,19},{8,28},{9,... | collective-permute-start | bytes 356360 | tf_op jit(solution)/shard_map/ppermute | solution.py:306
  46.9 9.3 %collective-permute-done.13.refs_1_ = bf16[16,3712]{1,0:T(8,128)(2,1)S(1)} collective-permute-done((bf16[16,3712]{1,0:T(8,128)(2,1)S(1)}, bf16[16,3712]{1,0:T(8,128)(2,1)S(1)}, u32[]{:S(2)}, u32[]{:S(2)}) %collective-permute-start.13) | collective-permute-done | bytes 118816 | tf_op jit(solution)/shard_map/ppermute | solution.py:306
  56.2 1.1 %combine.3 = bf16[32,3584]{1,0:T(8,128)(2,1)} custom-call(bf16[16,3712]{1,0:T(8,128)(2,1)S(1)} %collective-permute-done.9.refs_0_, bf16[16,3712]{1,0:T(8,128)(2,1)S(1)} %collective-permute-done.13.refs_1_, bf16[16,3712]{1,0:T(8,128)(2,1)S(1)} %collective-permute-done.14.refs_2_, bf16[16,3712]{1,0:T(8,128)(2,1)S(1)} %collective-permute-done.15.refs_3_, ...), custom_call_target="tpu_custom_call" | custom-call | tf_op jit(solution)/shard_map/combine/pallas_call | solution.py:84
  (23 shorter events, 4.2 us)
Async XLA Ops:
  0.0 29.1 %collective-permute-start.7 = (bf16[3584,1024]{1,0:T(8,128)(2,1)}, bf16[3584,1024]{1,0:T(8,128)(2,1)S(1)}, u32[]{:S(2)}, u32[]{:S(2)}) collective-permute-start(bf16[3584,1024]{1,0:T(8,128)(2,1)} %bitcast.10), channel_id=1, source_target_pairs={{0,1},{1,0},{2,3},{3,2},{4,5},{5,4},{6,7},{7,6},{8,9},{9,8},{10,11... | collective-permute-start | bytes 22020104 | tf_op jit(solution)/shard_map/ppermute | solution.py:324
  0.5 28.6 %collective-permute-start.8 = (bf16[512,3584]{1,0:T(8,128)(2,1)}, bf16[512,3584]{1,0:T(8,128)(2,1)S(1)}, u32[]{:S(2)}, u32[]{:S(2)}) collective-permute-start(bf16[512,3584]{1,0:T(8,128)(2,1)} %bitcast.12), channel_id=1, source_target_pairs={{0,1},{1,0},{2,3},{3,2},{4,5},{5,4},{6,7},{7,6},{8,9},{9,8},{10,11... | collective-permute-start | bytes 11010056 | tf_op jit(solution)/shard_map/ppermute | solution.py:323
  1.5 10.5 %collective-permute-start.1 = (bf16[32,3712]{1,0:T(8,128)(2,1)S(1)}, bf16[32,3712]{1,0:T(8,128)(2,1)S(1)}, u32[]{:S(2)}, u32[]{:S(2)}) collective-permute-start(bf16[32,3712]{1,0:T(8,128)(2,1)S(1)} %prepare.1.block), channel_id=1, source_target_pairs={{0,4},{1,5},{2,6},{3,7},{4,12},{5,13},{6,14},{7,15},{8,0},{9,1},{1... | collective-permute-start | bytes 712712 | tf_op jit(solution)/shard_map/ppermute | solution.py:306
  5.0 7.0 %collective-permute-start = (bf16[16,3712]{1,0:T(8,128)(2,1)S(1)}, bf16[16,3712]{1,0:T(8,128)(2,1)S(1)}, u32[]{:S(2)}, u32[]{:S(2)}) collective-permute-start(bf16[16,3712]{1,0:T(8,128)(2,1)S(1)} %get-tuple-element.33), channel_id=1, source_target_pairs={{0,2},{1,3},{2,0},{3,1},{4,6},{5,7},{6,4},{7,5},{8,10},{9,11},{10,... | collective-permute-start | bytes 356360 | tf_op jit(solution)/shard_map/ppermute | solution.py:306
  6.6 3.1 %copy-start = (bf16[1,3584,1024]{2,1,0:T(8,128)(2,1)S(1)}, bf16[1,3584,1024]{2,1,0:T(8,128)(2,1)}, u32[]{:S(2)}) copy-start(bf16[1,3584,1024]{2,1,0:T(8,128)(2,1)} %param.8) | copy-start | bytes 22020100
  9.7 2.0 %copy-start.1 = (bf16[1,512,3584]{2,1,0:T(8,128)(2,1)S(1)}, bf16[1,512,3584]{2,1,0:T(8,128)(2,1)}, u32[]{:S(2)}) copy-start(bf16[1,512,3584]{2,1,0:T(8,128)(2,1)} %param.9) | copy-start | bytes 11010052
  12.4 5.3 %collective-permute-start.4 = (bf16[16,3712]{1,0:T(8,128)(2,1)S(1)}, bf16[16,3712]{1,0:T(8,128)(2,1)S(1)}, u32[]{:S(2)}, u32[]{:S(2)}) collective-permute-start(bf16[16,3712]{1,0:T(8,128)(2,1)S(1)} %get-tuple-element.40), channel_id=1, source_target_pairs={{0,2},{1,3},{2,0},{3,1},{4,6},{5,7},{6,4},{7,5},{8,10},{9,11},{10,... | collective-permute-start | bytes 356360 | tf_op jit(solution)/shard_map/ppermute | solution.py:306
  13.6 6.3 %collective-permute-start.2 = (bf16[16,3712]{1,0:T(8,128)(2,1)S(1)}, bf16[16,3712]{1,0:T(8,128)(2,1)S(1)}, u32[]{:S(2)}, u32[]{:S(2)}) collective-permute-start(bf16[16,3712]{1,0:T(8,128)(2,1)S(1)} %get-tuple-element.38), channel_id=1, source_target_pairs={{0,4},{1,5},{2,6},{3,7},{4,12},{5,13},{6,14},{7,15},{8,0},{9,1},{1... | collective-permute-start | bytes 356360 | tf_op jit(solution)/shard_map/ppermute | solution.py:306
  15.6 10.6 %collective-permute-start.3 = (bf16[16,3712]{1,0:T(8,128)(2,1)S(1)}, bf16[16,3712]{1,0:T(8,128)(2,1)S(1)}, u32[]{:S(2)}, u32[]{:S(2)}) collective-permute-start(bf16[16,3712]{1,0:T(8,128)(2,1)S(1)} %get-tuple-element.39), channel_id=1, source_target_pairs={{0,6},{1,7},{2,4},{3,5},{4,14},{5,15},{6,12},{7,13},{8,2},{9,3},{1... | collective-permute-start | bytes 356360 | tf_op jit(solution)/shard_map/ppermute | solution.py:306
  17.7 8.4 %collective-permute-start.5 = (bf16[16,3712]{1,0:T(8,128)(2,1)S(1)}, bf16[16,3712]{1,0:T(8,128)(2,1)S(1)}, u32[]{:S(2)}, u32[]{:S(2)}) collective-permute-start(bf16[16,3712]{1,0:T(8,128)(2,1)S(1)} %get-tuple-element.43), channel_id=1, source_target_pairs={{0,8},{1,9},{2,10},{3,11},{4,0},{5,1},{6,2},{7,3},{8,12},{9,13},{1... | collective-permute-start | bytes 356360 | tf_op jit(solution)/shard_map/ppermute | solution.py:306
  19.9 7.5 %collective-permute-start.6 = (bf16[16,3712]{1,0:T(8,128)(2,1)S(1)}, bf16[16,3712]{1,0:T(8,128)(2,1)S(1)}, u32[]{:S(2)}, u32[]{:S(2)}) collective-permute-start(bf16[16,3712]{1,0:T(8,128)(2,1)S(1)} %get-tuple-element.44), channel_id=1, source_target_pairs={{0,10},{1,11},{2,8},{3,9},{4,2},{5,3},{6,0},{7,1},{8,14},{9,15},{1... | collective-permute-start | bytes 356360 | tf_op jit(solution)/shard_map/ppermute | solution.py:306
  30.9 7.8 %collective-permute-start.10 = (bf16[16,3712]{1,0:T(8,128)(2,1)S(1)}, bf16[16,3712]{1,0:T(8,128)(2,1)S(1)}, u32[]{:S(2)}, u32[]{:S(2)}) collective-permute-start(bf16[16,3712]{1,0:T(8,128)(2,1)S(1)} %get-tuple-element.48), channel_id=1, source_target_pairs={{0,6},{1,7},{2,4},{3,5},{4,14},{5,15},{6,12},{7,13},{8,2},{9,3},{1... | collective-permute-start | bytes 356360 | tf_op jit(solution)/shard_map/ppermute | solution.py:306
  32.8 6.1 %collective-permute-start.11 = (bf16[16,3712]{1,0:T(8,128)(2,1)S(1)}, bf16[16,3712]{1,0:T(8,128)(2,1)S(1)}, u32[]{:S(2)}, u32[]{:S(2)}) collective-permute-start(bf16[16,3712]{1,0:T(8,128)(2,1)S(1)} %get-tuple-element.49), channel_id=1, source_target_pairs={{0,2},{1,3},{2,0},{3,1},{4,6},{5,7},{6,4},{7,5},{8,10},{9,11},{10,... | collective-permute-start | bytes 356360 | tf_op jit(solution)/shard_map/ppermute | solution.py:306
  33.4 6.2 %collective-permute-start.12 = (bf16[16,3712]{1,0:T(8,128)(2,1)S(1)}, bf16[16,3712]{1,0:T(8,128)(2,1)S(1)}, u32[]{:S(2)}, u32[]{:S(2)}) collective-permute-start(bf16[16,3712]{1,0:T(8,128)(2,1)S(1)} %get-tuple-element.50), channel_id=1, source_target_pairs={{0,4},{1,5},{2,6},{3,7},{4,12},{5,13},{6,14},{7,15},{8,0},{9,1},{1... | collective-permute-start | bytes 356360 | tf_op jit(solution)/shard_map/ppermute | solution.py:306
  35.3 4.8 %collective-permute-start.9 = (bf16[16,3712]{1,0:T(8,128)(2,1)S(1)}, bf16[16,3712]{1,0:T(8,128)(2,1)S(1)}, u32[]{:S(2)}, u32[]{:S(2)}) collective-permute-start(bf16[16,3712]{1,0:T(8,128)(2,1)S(1)} %get-tuple-element.47), channel_id=1, source_target_pairs={{0,16},{1,17},{2,18},{3,19},{4,20},{5,21},{6,22},{7,23},{8,24},{9,... | collective-permute-start | bytes 356360 | tf_op jit(solution)/shard_map/ppermute | solution.py:306
  40.6 15.6 %collective-permute-start.16 = (bf16[32,3584]{1,0:T(8,128)(2,1)S(1)}, bf16[32,3584]{1,0:T(8,128)(2,1)S(1)}, u32[]{:S(2)}, u32[]{:S(2)}) collective-permute-start(bf16[32,3584]{1,0:T(8,128)(2,1)S(1)} %combine.2), channel_id=1, source_target_pairs={{0,20},{1,21},{2,22},{3,23},{4,28},{5,29},{6,30},{7,31},{8,16},{9,... | collective-permute-start | bytes 688136 | tf_op jit(solution)/shard_map/ppermute | solution.py:306
  43.0 13.2 %collective-permute-start.13 = (bf16[16,3712]{1,0:T(8,128)(2,1)S(1)}, bf16[16,3712]{1,0:T(8,128)(2,1)S(1)}, u32[]{:S(2)}, u32[]{:S(2)}) collective-permute-start(bf16[16,3712]{1,0:T(8,128)(2,1)S(1)} %get-tuple-element.52), channel_id=1, source_target_pairs={{0,18},{1,19},{2,16},{3,17},{4,22},{5,23},{6,20},{7,21},{8,26},{9,... | collective-permute-start | bytes 356360 | tf_op jit(solution)/shard_map/ppermute | solution.py:306
  43.6 12.7 %collective-permute-start.14 = (bf16[16,3712]{1,0:T(8,128)(2,1)S(1)}, bf16[16,3712]{1,0:T(8,128)(2,1)S(1)}, u32[]{:S(2)}, u32[]{:S(2)}) collective-permute-start(bf16[16,3712]{1,0:T(8,128)(2,1)S(1)} %get-tuple-element.53), channel_id=1, source_target_pairs={{0,24},{1,25},{2,26},{3,27},{4,16},{5,17},{6,18},{7,19},{8,28},{9,... | collective-permute-start | bytes 356360 | tf_op jit(solution)/shard_map/ppermute | solution.py:306
  46.9 9.3 %collective-permute-start.15 = (bf16[16,3712]{1,0:T(8,128)(2,1)S(1)}, bf16[16,3712]{1,0:T(8,128)(2,1)S(1)}, u32[]{:S(2)}, u32[]{:S(2)}) collective-permute-start(bf16[16,3712]{1,0:T(8,128)(2,1)S(1)} %get-tuple-element.54), channel_id=1, source_target_pairs={{0,26},{1,27},{2,24},{3,25},{4,18},{5,19},{6,16},{7,17},{8,30},{9,... | collective-permute-start | bytes 356360 | tf_op jit(solution)/shard_map/ppermute | solution.py:306

commit v17 on v16

--- a/solution.py
+++ b/solution.py
@@ -332,23 +332,24 @@
     other1 = sent(other, sections, 0, 0, 1)
     own2 = sent(on0, sections, 0, 1, 0)
     other2 = sent(on1, sections, 0, 1, 1)
-    back0, back1 = after((back0, back1), other1)
+    back1, back0 = after((back1, back0), other1)
+    other3 = sent(back1, sections, 0, 3, 1)
     own3 = sent(back0, sections, 0, 3, 0)
-    other3 = sent(back1, sections, 0, 3, 1)
-    pieces = (own0, other0, own1, own2, other2, other1, own3, other3)
-    places = ((0, 0), (0, 1), (1, 0), (2, 0), (2, 1), (1, 1), (3, 0), (3, 1))
+    pieces = (own0, other0, own1, own2, other2, other1, other3, own3)
+    places = ((0, 0), (0, 1), (1, 0), (2, 0), (2, 1), (1, 1), (3, 1), (3, 0))
     slots, total = near_pass(pieces, near)
     pieces = far_pass(slots, total, (far_in, far_out), capacity)
     piece = dict(zip(places, pieces))
     first = [
-        sent(piece[0, 0], sections, 1, 0, 0),
+        sent(piece[0, 1], sections, 1, 0, 1),
         sent(piece[2, 1], sections, 0, 1, 1),
         sent(piece[3, 1], sections, 0, 0, 1),
         sent(piece[2, 0], sections, 0, 1, 0),
+        sent(piece[0, 0], sections, 1, 0, 0),
     ]
-    zero, *merged = lax.optimization_barrier(first)
+    one, *merged, zero = lax.optimization_barrier(first)
     merged.append(piece[3, 0])
-    straight = [zero, sent(piece[0, 1], sections, 1, 0, 1)]
+    straight = [zero, one]
     straight += [sent(piece[1, flip], sections, 1, -1, flip) for flip in range(2)]
     merged = sent(combine(merged, tok_count), sections, 1, 1, 0)
     return combine(straight, tok_count, merged)[None]

time: 57.5 us -> 56.7 us (0.986)
  waiting for transfers between devices: 18.3 us -> 16.8 us
  starting transfers between devices: 26.7 us -> 27.3 us
    ppermute x15, waiting for transfers between devices: 18.3 us -> 16.8 us  [sent(): return lax.ppermute(shard, ('section', 'expert'), pairs)]
    ppermute x15, starting transfers between devices: 26.2 us -> 26.8 us  [sent(): return lax.ppermute(shard, ('section', 'expert'), pairs)]
  transfers between devices with their start and end apart: 17 -> 17, of which waited for: 8 -> 9; matrix products, arithmetic and copies ran while one was open for 0% -> 0% of each run, Pallas kernels for 8% -> 8%
where the time goes in v17:
time: 56.7 us; the launch traced here: 56.5 us
  starting transfers between devices  27.3 us (48%)
  waiting for transfers between devices  16.8 us (30%)
  Pallas kernels  7.6 us (13%)
  local copies, waits for them, and re-layouts  4.62 us (8%)
    ppermute x15, starting transfers between devices, sent(): return lax.ppermute(shard, ('section', 'expert'), pairs)  26.8 us
    ppermute x15, waiting for transfers between devices, sent(): return lax.ppermute(shard, ('section', 'expert'), pairs)  16.8 us
    pallas_call x9, Pallas kernels, local_call(): pl.pallas_call(kernel, out_shape=out_shape, in_specs=[vmem if spec is Non...  7.6 us
    unnamed x4, local copies, waits for them, and re-layouts  4.62 us
  transfers between devices with their start and end apart: 17, of which 9 were waited for; matrix products, arithmetic and copies ran while one was open for 0% of the time, Pallas kernels for 8%

profile of v17, /device:TPU:0, one launch (start us, length us, event | category | flops | bytes accessed | tf_op | source)
XLA Modules:
  0.0 56.5 jit_solution(17316314146839141597)
XLA Ops:
  0.5 1.0 %prepare.1.block = bf16[32,3712]{1,0:T(8,128)(2,1)S(1)} custom-call(s32[2,32]{1,0:T(2,128)} %bitcast.15, f32[2,32]{1,0:T(2,128)} %bitcast.16, bf16[32,3584]{1,0:T(8,128)(2,1)} %bitcast.14), custom_call_target="tpu_custom_call" | custom-call | tf_op jit(solution)/shard_map/prepare/pallas_call | solution.py:84
  1.5 3.1 %collective-permute-start.1 = (bf16[32,3712]{1,0:T(8,128)(2,1)S(1)}, bf16[32,3712]{1,0:T(8,128)(2,1)S(1)}, u32[]{:S(2)}, u32[]{:S(2)}) collective-permute-start(bf16[32,3712]{1,0:T(8,128)(2,1)S(1)} %prepare.1.block), channel_id=1, source_target_pairs={{0,4},{1,5},{2,6},{3,7},{4,12},{5,13},{6,14},{7,15},{8,0},{9,1},{1... | collective-permute-start | bytes 712712 | tf_op jit(solution)/shard_map/ppermute | solution.py:306
  5.0 1.6 %collective-permute-start = (bf16[16,3712]{1,0:T(8,128)(2,1)S(1)}, bf16[16,3712]{1,0:T(8,128)(2,1)S(1)}, u32[]{:S(2)}, u32[]{:S(2)}) collective-permute-start(bf16[16,3712]{1,0:T(8,128)(2,1)S(1)} %get-tuple-element.34), channel_id=1, source_target_pairs={{0,2},{1,3},{2,0},{3,1},{4,6},{5,7},{6,4},{7,5},{8,10},{9,11},{10,... | collective-permute-start | bytes 356360 | tf_op jit(solution)/shard_map/ppermute | solution.py:306
  6.6 3.1 %copy-done = bf16[1,3584,1024]{2,1,0:T(8,128)(2,1)S(1)} copy-done((bf16[1,3584,1024]{2,1,0:T(8,128)(2,1)S(1)}, bf16[1,3584,1024]{2,1,0:T(8,128)(2,1)}, u32[]{:S(2)}) %copy-start) | copy-done | bytes 7340056
  10.2 1.5 %copy-done.1 = bf16[1,512,3584]{2,1,0:T(8,128)(2,1)S(1)} copy-done((bf16[1,512,3584]{2,1,0:T(8,128)(2,1)S(1)}, bf16[1,512,3584]{2,1,0:T(8,128)(2,1)}, u32[]{:S(2)}) %copy-start.1) | copy-done | bytes 3670040
  12.4 1.2 %collective-permute-start.4 = (bf16[16,3712]{1,0:T(8,128)(2,1)S(1)}, bf16[16,3712]{1,0:T(8,128)(2,1)S(1)}, u32[]{:S(2)}, u32[]{:S(2)}) collective-permute-start(bf16[16,3712]{1,0:T(8,128)(2,1)S(1)} %get-tuple-element.41), channel_id=1, source_target_pairs={{0,2},{1,3},{2,0},{3,1},{4,6},{5,7},{6,4},{7,5},{8,10},{9,11},{10,... | collective-permute-start | bytes 356360 | tf_op jit(solution)/shard_map/ppermute | solution.py:306
  13.6 2.0 %collective-permute-start.2 = (bf16[16,3712]{1,0:T(8,128)(2,1)S(1)}, bf16[16,3712]{1,0:T(8,128)(2,1)S(1)}, u32[]{:S(2)}, u32[]{:S(2)}) collective-permute-start(bf16[16,3712]{1,0:T(8,128)(2,1)S(1)} %get-tuple-element.39), channel_id=1, source_target_pairs={{0,4},{1,5},{2,6},{3,7},{4,12},{5,13},{6,14},{7,15},{8,0},{9,1},{1... | collective-permute-start | bytes 356360 | tf_op jit(solution)/shard_map/ppermute | solution.py:306
  15.6 2.1 %collective-permute-start.3 = (bf16[16,3712]{1,0:T(8,128)(2,1)S(1)}, bf16[16,3712]{1,0:T(8,128)(2,1)S(1)}, u32[]{:S(2)}, u32[]{:S(2)}) collective-permute-start(bf16[16,3712]{1,0:T(8,128)(2,1)S(1)} %get-tuple-element.40), channel_id=1, source_target_pairs={{0,6},{1,7},{2,4},{3,5},{4,14},{5,15},{6,12},{7,13},{8,2},{9,3},{1... | collective-permute-start | bytes 356360 | tf_op jit(solution)/shard_map/ppermute | solution.py:306
  17.7 1.9 %collective-permute-start.5 = (bf16[16,3712]{1,0:T(8,128)(2,1)S(1)}, bf16[16,3712]{1,0:T(8,128)(2,1)S(1)}, u32[]{:S(2)}, u32[]{:S(2)}) collective-permute-start(bf16[16,3712]{1,0:T(8,128)(2,1)S(1)} %get-tuple-element.44), channel_id=1, source_target_pairs={{0,10},{1,11},{2,8},{3,9},{4,2},{5,3},{6,0},{7,1},{8,14},{9,15},{1... | collective-permute-start | bytes 356360 | tf_op jit(solution)/shard_map/ppermute | solution.py:306
  19.8 2.2 %collective-permute-start.6 = (bf16[16,3712]{1,0:T(8,128)(2,1)S(1)}, bf16[16,3712]{1,0:T(8,128)(2,1)S(1)}, u32[]{:S(2)}, u32[]{:S(2)}) collective-permute-start(bf16[16,3712]{1,0:T(8,128)(2,1)S(1)} %get-tuple-element.45), channel_id=1, source_target_pairs={{0,8},{1,9},{2,10},{3,11},{4,0},{5,1},{6,2},{7,3},{8,12},{9,13},{1... | collective-permute-start | bytes 356360 | tf_op jit(solution)/shard_map/ppermute | solution.py:306
  22.1 4.1 %collective-permute-done.3.refs_4_ = bf16[16,3712]{1,0:T(8,128)(2,1)S(1)} collective-permute-done((bf16[16,3712]{1,0:T(8,128)(2,1)S(1)}, bf16[16,3712]{1,0:T(8,128)(2,1)S(1)}, u32[]{:S(2)}, u32[]{:S(2)}) %collective-permute-start.3) | collective-permute-done | bytes 118816 | tf_op jit(solution)/shard_map/ppermute | solution.py:306
  26.8 1.7 %near_pass.1 = (bf16[128,3712]{1,0:T(8,128)(2,1)S(1)}, f32[128,3584]{1,0:T(8,128)S(1)}) custom-call(bf16[16,3712]{1,0:T(8,128)(2,1)S(1)} %get-tuple-element.33.refs_0_, bf16[16,3712]{1,0:T(8,128)(2,1)S(1)} %collective-permute-done.refs_1_, bf16[16,3712]{1,0:T(8,128)(2,1)S(1)} %get-tuple-element.38.refs_2_, ...), custom_call_target="tpu_custom_call" | custom-call | bytes 11010048 | tf_op jit(solution)/shard_map/near_pass/pallas_call | solution.py:84
  28.6 1.7 %far_pass.1 = (bf16[16,3712]{1,0:T(8,128)(2,1)S(1)}, bf16[16,3712]{1,0:T(8,128)(2,1)S(1)}, bf16[16,3712]{1,0:T(8,128)(2,1)S(1)}, bf16[16,3712]{1,0:T(8,128)(2,1)...) custom-call(bf16[128,3712]{1,0:T(8,128)(2,1)S(1)} %get-tuple-element, ...), custom_call_target="tpu_custom_call" | custom-call | bytes 11010048 | tf_op jit(solution)/shard_map/far_pass/pallas_call | solution.py:84
  30.3 1.6 %collective-permute-start.10 = (bf16[16,3712]{1,0:T(8,128)(2,1)S(1)}, bf16[16,3712]{1,0:T(8,128)(2,1)S(1)}, u32[]{:S(2)}, u32[]{:S(2)}) collective-permute-start(bf16[16,3712]{1,0:T(8,128)(2,1)S(1)} %get-tuple-element.49), channel_id=1, source_target_pairs={{0,6},{1,7},{2,4},{3,5},{4,14},{5,15},{6,12},{7,13},{8,2},{9,3},{1... | collective-permute-start | bytes 356360 | tf_op jit(solution)/shard_map/ppermute | solution.py:306
  32.8 2.5 %collective-permute-start.12 = (bf16[16,3712]{1,0:T(8,128)(2,1)S(1)}, bf16[16,3712]{1,0:T(8,128)(2,1)S(1)}, u32[]{:S(2)}, u32[]{:S(2)}) collective-permute-start(bf16[16,3712]{1,0:T(8,128)(2,1)S(1)} %get-tuple-element.51), channel_id=1, source_target_pairs={{0,4},{1,5},{2,6},{3,7},{4,12},{5,13},{6,14},{7,15},{8,0},{9,1},{1... | collective-permute-start | bytes 356360 | tf_op jit(solution)/shard_map/ppermute | solution.py:306
  35.3 1.5 %collective-permute-start.13 = (bf16[16,3712]{1,0:T(8,128)(2,1)S(1)}, bf16[16,3712]{1,0:T(8,128)(2,1)S(1)}, u32[]{:S(2)}, u32[]{:S(2)}) collective-permute-start(bf16[16,3712]{1,0:T(8,128)(2,1)S(1)} %get-tuple-element.52), channel_id=1, source_target_pairs={{0,16},{1,17},{2,18},{3,19},{4,20},{5,21},{6,22},{7,23},{8,24},{9,... | collective-permute-start | bytes 356360 | tf_op jit(solution)/shard_map/ppermute | solution.py:306
  36.8 1.5 %collective-permute-start.9 = (bf16[16,3712]{1,0:T(8,128)(2,1)S(1)}, bf16[16,3712]{1,0:T(8,128)(2,1)S(1)}, u32[]{:S(2)}, u32[]{:S(2)}) collective-permute-start(bf16[16,3712]{1,0:T(8,128)(2,1)S(1)} %get-tuple-element.48), channel_id=1, source_target_pairs={{0,18},{1,19},{2,16},{3,17},{4,22},{5,23},{6,20},{7,21},{8,26},{9,... | collective-permute-start | bytes 356360 | tf_op jit(solution)/shard_map/ppermute | solution.py:306
  38.3 1.2 %collective-permute-done.12.refs_2_ = bf16[16,3712]{1,0:T(8,128)(2,1)S(1)} collective-permute-done((bf16[16,3712]{1,0:T(8,128)(2,1)S(1)}, bf16[16,3712]{1,0:T(8,128)(2,1)S(1)}, u32[]{:S(2)}, u32[]{:S(2)}) %collective-permute-start.12) | collective-permute-done | bytes 118816 | tf_op jit(solution)/shard_map/ppermute | solution.py:306
  40.4 2.2 %collective-permute-done.9.refs_1_ = bf16[16,3712]{1,0:T(8,128)(2,1)S(1)} collective-permute-done((bf16[16,3712]{1,0:T(8,128)(2,1)S(1)}, bf16[16,3712]{1,0:T(8,128)(2,1)S(1)}, u32[]{:S(2)}, u32[]{:S(2)}) %collective-permute-start.9) | collective-permute-done | bytes 118816 | tf_op jit(solution)/shard_map/ppermute | solution.py:306
  43.0 1.3 %collective-permute-start.16 = (bf16[32,3584]{1,0:T(8,128)(2,1)S(1)}, bf16[32,3584]{1,0:T(8,128)(2,1)S(1)}, u32[]{:S(2)}, u32[]{:S(2)}) collective-permute-start(bf16[32,3584]{1,0:T(8,128)(2,1)S(1)} %combine.2), channel_id=1, source_target_pairs={{0,20},{1,21},{2,22},{3,23},{4,28},{5,29},{6,30},{7,31},{8,16},{9,... | collective-permute-start | bytes 688136 | tf_op jit(solution)/shard_map/ppermute | solution.py:306
  44.2 2.6 %collective-permute-start.14 = (bf16[16,3712]{1,0:T(8,128)(2,1)S(1)}, bf16[16,3712]{1,0:T(8,128)(2,1)S(1)}, u32[]{:S(2)}, u32[]{:S(2)}) collective-permute-start(bf16[16,3712]{1,0:T(8,128)(2,1)S(1)} %get-tuple-element.55), channel_id=1, source_target_pairs={{0,24},{1,25},{2,26},{3,27},{4,16},{5,17},{6,18},{7,19},{8,28},{9,... | collective-permute-start | bytes 356360 | tf_op jit(solution)/shard_map/ppermute | solution.py:306
  47.8 4.8 %collective-permute-done.14.refs_2_ = bf16[16,3712]{1,0:T(8,128)(2,1)S(1)} collective-permute-done((bf16[16,3712]{1,0:T(8,128)(2,1)S(1)}, bf16[16,3712]{1,0:T(8,128)(2,1)S(1)}, u32[]{:S(2)}, u32[]{:S(2)}) %collective-permute-start.14) | collective-permute-done | bytes 118816 | tf_op jit(solution)/shard_map/ppermute | solution.py:306
  52.6 2.0 %collective-permute-done.15.refs_3_ = bf16[16,3712]{1,0:T(8,128)(2,1)S(1)} collective-permute-done((bf16[16,3712]{1,0:T(8,128)(2,1)S(1)}, bf16[16,3712]{1,0:T(8,128)(2,1)S(1)}, u32[]{:S(2)}, u32[]{:S(2)}) %collective-permute-start.15) | collective-permute-done | bytes 118816 | tf_op jit(solution)/shard_map/ppermute | solution.py:306
  55.3 1.1 %combine.3 = bf16[32,3584]{1,0:T(8,128)(2,1)} custom-call(bf16[16,3712]{1,0:T(8,128)(2,1)S(1)} %collective-permute-done.13.refs_0_, bf16[16,3712]{1,0:T(8,128)(2,1)S(1)} %collective-permute-done.9.refs_1_, bf16[16,3712]{1,0:T(8,128)(2,1)S(1)} %collective-permute-done.14.refs_2_, bf16[16,3712]{1,0:T(8,128)(2,1)S(1)} %collective-permute-done.15.refs_3_, ...), custom_call_target="tpu_custom_call" | custom-call | tf_op jit(solution)/shard_map/combine/pallas_call | solution.py:84
  (23 shorter events, 6.9 us)
Async XLA Ops:
  0.0 28.6 %collective-permute-start.7 = (bf16[3584,1024]{1,0:T(8,128)(2,1)}, bf16[3584,1024]{1,0:T(8,128)(2,1)S(1)}, u32[]{:S(2)}, u32[]{:S(2)}) collective-permute-start(bf16[3584,1024]{1,0:T(8,128)(2,1)} %bitcast.10), channel_id=1, source_target_pairs={{0,1},{1,0},{2,3},{3,2},{4,5},{5,4},{6,7},{7,6},{8,9},{9,8},{10,11... | collective-permute-start | bytes 22020104 | tf_op jit(solution)/shard_map/ppermute | solution.py:324
  0.5 28.1 %collective-permute-start.8 = (bf16[512,3584]{1,0:T(8,128)(2,1)}, bf16[512,3584]{1,0:T(8,128)(2,1)S(1)}, u32[]{:S(2)}, u32[]{:S(2)}) collective-permute-start(bf16[512,3584]{1,0:T(8,128)(2,1)} %bitcast.12), channel_id=1, source_target_pairs={{0,1},{1,0},{2,3},{3,2},{4,5},{5,4},{6,7},{7,6},{8,9},{9,8},{10,11... | collective-permute-start | bytes 11010056 | tf_op jit(solution)/shard_map/ppermute | solution.py:323
  1.5 10.5 %collective-permute-start.1 = (bf16[32,3712]{1,0:T(8,128)(2,1)S(1)}, bf16[32,3712]{1,0:T(8,128)(2,1)S(1)}, u32[]{:S(2)}, u32[]{:S(2)}) collective-permute-start(bf16[32,3712]{1,0:T(8,128)(2,1)S(1)} %prepare.1.block), channel_id=1, source_target_pairs={{0,4},{1,5},{2,6},{3,7},{4,12},{5,13},{6,14},{7,15},{8,0},{9,1},{1... | collective-permute-start | bytes 712712 | tf_op jit(solution)/shard_map/ppermute | solution.py:306
  5.0 7.0 %collective-permute-start = (bf16[16,3712]{1,0:T(8,128)(2,1)S(1)}, bf16[16,3712]{1,0:T(8,128)(2,1)S(1)}, u32[]{:S(2)}, u32[]{:S(2)}) collective-permute-start(bf16[16,3712]{1,0:T(8,128)(2,1)S(1)} %get-tuple-element.34), channel_id=1, source_target_pairs={{0,2},{1,3},{2,0},{3,1},{4,6},{5,7},{6,4},{7,5},{8,10},{9,11},{10,... | collective-permute-start | bytes 356360 | tf_op jit(solution)/shard_map/ppermute | solution.py:306
  6.6 3.1 %copy-start = (bf16[1,3584,1024]{2,1,0:T(8,128)(2,1)S(1)}, bf16[1,3584,1024]{2,1,0:T(8,128)(2,1)}, u32[]{:S(2)}) copy-start(bf16[1,3584,1024]{2,1,0:T(8,128)(2,1)} %param.8) | copy-start | bytes 22020100
  9.7 2.0 %copy-start.1 = (bf16[1,512,3584]{2,1,0:T(8,128)(2,1)S(1)}, bf16[1,512,3584]{2,1,0:T(8,128)(2,1)}, u32[]{:S(2)}) copy-start(bf16[1,512,3584]{2,1,0:T(8,128)(2,1)} %param.9) | copy-start | bytes 11010052
  12.4 5.3 %collective-permute-start.4 = (bf16[16,3712]{1,0:T(8,128)(2,1)S(1)}, bf16[16,3712]{1,0:T(8,128)(2,1)S(1)}, u32[]{:S(2)}, u32[]{:S(2)}) collective-permute-start(bf16[16,3712]{1,0:T(8,128)(2,1)S(1)} %get-tuple-element.41), channel_id=1, source_target_pairs={{0,2},{1,3},{2,0},{3,1},{4,6},{5,7},{6,4},{7,5},{8,10},{9,11},{10,... | collective-permute-start | bytes 356360 | tf_op jit(solution)/shard_map/ppermute | solution.py:306
  13.6 6.2 %collective-permute-start.2 = (bf16[16,3712]{1,0:T(8,128)(2,1)S(1)}, bf16[16,3712]{1,0:T(8,128)(2,1)S(1)}, u32[]{:S(2)}, u32[]{:S(2)}) collective-permute-start(bf16[16,3712]{1,0:T(8,128)(2,1)S(1)} %get-tuple-element.39), channel_id=1, source_target_pairs={{0,4},{1,5},{2,6},{3,7},{4,12},{5,13},{6,14},{7,15},{8,0},{9,1},{1... | collective-permute-start | bytes 356360 | tf_op jit(solution)/shard_map/ppermute | solution.py:306
  15.6 10.6 %collective-permute-start.3 = (bf16[16,3712]{1,0:T(8,128)(2,1)S(1)}, bf16[16,3712]{1,0:T(8,128)(2,1)S(1)}, u32[]{:S(2)}, u32[]{:S(2)}) collective-permute-start(bf16[16,3712]{1,0:T(8,128)(2,1)S(1)} %get-tuple-element.40), channel_id=1, source_target_pairs={{0,6},{1,7},{2,4},{3,5},{4,14},{5,15},{6,12},{7,13},{8,2},{9,3},{1... | collective-permute-start | bytes 356360 | tf_op jit(solution)/shard_map/ppermute | solution.py:306
  17.7 8.5 %collective-permute-start.5 = (bf16[16,3712]{1,0:T(8,128)(2,1)S(1)}, bf16[16,3712]{1,0:T(8,128)(2,1)S(1)}, u32[]{:S(2)}, u32[]{:S(2)}) collective-permute-start(bf16[16,3712]{1,0:T(8,128)(2,1)S(1)} %get-tuple-element.44), channel_id=1, source_target_pairs={{0,10},{1,11},{2,8},{3,9},{4,2},{5,3},{6,0},{7,1},{8,14},{9,15},{1... | collective-permute-start | bytes 356360 | tf_op jit(solution)/shard_map/ppermute | solution.py:306
  19.8 7.0 %collective-permute-start.6 = (bf16[16,3712]{1,0:T(8,128)(2,1)S(1)}, bf16[16,3712]{1,0:T(8,128)(2,1)S(1)}, u32[]{:S(2)}, u32[]{:S(2)}) collective-permute-start(bf16[16,3712]{1,0:T(8,128)(2,1)S(1)} %get-tuple-element.45), channel_id=1, source_target_pairs={{0,8},{1,9},{2,10},{3,11},{4,0},{5,1},{6,2},{7,3},{8,12},{9,13},{1... | collective-permute-start | bytes 356360 | tf_op jit(solution)/shard_map/ppermute | solution.py:306
  30.3 7.9 %collective-permute-start.10 = (bf16[16,3712]{1,0:T(8,128)(2,1)S(1)}, bf16[16,3712]{1,0:T(8,128)(2,1)S(1)}, u32[]{:S(2)}, u32[]{:S(2)}) collective-permute-start(bf16[16,3712]{1,0:T(8,128)(2,1)S(1)} %get-tuple-element.49), channel_id=1, source_target_pairs={{0,6},{1,7},{2,4},{3,5},{4,14},{5,15},{6,12},{7,13},{8,2},{9,3},{1... | collective-permute-start | bytes 356360 | tf_op jit(solution)/shard_map/ppermute | solution.py:306
  31.9 6.3 %collective-permute-start.11 = (bf16[16,3712]{1,0:T(8,128)(2,1)S(1)}, bf16[16,3712]{1,0:T(8,128)(2,1)S(1)}, u32[]{:S(2)}, u32[]{:S(2)}) collective-permute-start(bf16[16,3712]{1,0:T(8,128)(2,1)S(1)} %get-tuple-element.50), channel_id=1, source_target_pairs={{0,2},{1,3},{2,0},{3,1},{4,6},{5,7},{6,4},{7,5},{8,10},{9,11},{10,... | collective-permute-start | bytes 356360 | tf_op jit(solution)/shard_map/ppermute | solution.py:306
  32.8 6.7 %collective-permute-start.12 = (bf16[16,3712]{1,0:T(8,128)(2,1)S(1)}, bf16[16,3712]{1,0:T(8,128)(2,1)S(1)}, u32[]{:S(2)}, u32[]{:S(2)}) collective-permute-start(bf16[16,3712]{1,0:T(8,128)(2,1)S(1)} %get-tuple-element.51), channel_id=1, source_target_pairs={{0,4},{1,5},{2,6},{3,7},{4,12},{5,13},{6,14},{7,15},{8,0},{9,1},{1... | collective-permute-start | bytes 356360 | tf_op jit(solution)/shard_map/ppermute | solution.py:306
  35.3 5.0 %collective-permute-start.13 = (bf16[16,3712]{1,0:T(8,128)(2,1)S(1)}, bf16[16,3712]{1,0:T(8,128)(2,1)S(1)}, u32[]{:S(2)}, u32[]{:S(2)}) collective-permute-start(bf16[16,3712]{1,0:T(8,128)(2,1)S(1)} %get-tuple-element.52), channel_id=1, source_target_pairs={{0,16},{1,17},{2,18},{3,19},{4,20},{5,21},{6,22},{7,23},{8,24},{9,... | collective-permute-start | bytes 356360 | tf_op jit(solution)/shard_map/ppermute | solution.py:306
  36.8 5.7 %collective-permute-start.9 = (bf16[16,3712]{1,0:T(8,128)(2,1)S(1)}, bf16[16,3712]{1,0:T(8,128)(2,1)S(1)}, u32[]{:S(2)}, u32[]{:S(2)}) collective-permute-start(bf16[16,3712]{1,0:T(8,128)(2,1)S(1)} %get-tuple-element.48), channel_id=1, source_target_pairs={{0,18},{1,19},{2,16},{3,17},{4,22},{5,23},{6,20},{7,21},{8,26},{9,... | collective-permute-start | bytes 356360 | tf_op jit(solution)/shard_map/ppermute | solution.py:306
  43.0 12.4 %collective-permute-start.16 = (bf16[32,3584]{1,0:T(8,128)(2,1)S(1)}, bf16[32,3584]{1,0:T(8,128)(2,1)S(1)}, u32[]{:S(2)}, u32[]{:S(2)}) collective-permute-start(bf16[32,3584]{1,0:T(8,128)(2,1)S(1)} %combine.2), channel_id=1, source_target_pairs={{0,20},{1,21},{2,22},{3,23},{4,28},{5,29},{6,30},{7,31},{8,16},{9,... | collective-permute-start | bytes 688136 | tf_op jit(solution)/shard_map/ppermute | solution.py:306
  44.2 8.3 %collective-permute-start.14 = (bf16[16,3712]{1,0:T(8,128)(2,1)S(1)}, bf16[16,3712]{1,0:T(8,128)(2,1)S(1)}, u32[]{:S(2)}, u32[]{:S(2)}) collective-permute-start(bf16[16,3712]{1,0:T(8,128)(2,1)S(1)} %get-tuple-element.55), channel_id=1, source_target_pairs={{0,24},{1,25},{2,26},{3,27},{4,16},{5,17},{6,18},{7,19},{8,28},{9,... | collective-permute-start | bytes 356360 | tf_op jit(solution)/shard_map/ppermute | solution.py:306
  46.9 7.7 %collective-permute-start.15 = (bf16[16,3712]{1,0:T(8,128)(2,1)S(1)}, bf16[16,3712]{1,0:T(8,128)(2,1)S(1)}, u32[]{:S(2)}, u32[]{:S(2)}) collective-permute-start(bf16[16,3712]{1,0:T(8,128)(2,1)S(1)} %get-tuple-element.56), channel_id=1, source_target_pairs={{0,26},{1,27},{2,24},{3,25},{4,18},{5,19},{6,16},{7,17},{8,30},{9,... | collective-permute-start | bytes 356360 | tf_op jit(solution)/shard_map/ppermute | solution.py:306

commit v18 on v17

--- a/solution.py
+++ b/solution.py
@@ -341,14 +341,14 @@
     pieces = far_pass(slots, total, (far_in, far_out), capacity)
     piece = dict(zip(places, pieces))
     first = [
-        sent(piece[0, 1], sections, 1, 0, 1),
+        sent(piece[0, 0], sections, 1, 0, 0),
         sent(piece[2, 1], sections, 0, 1, 1),
         sent(piece[3, 1], sections, 0, 0, 1),
+        sent(piece[0, 1], sections, 1, 0, 1),
         sent(piece[2, 0], sections, 0, 1, 0),
-        sent(piece[0, 0], sections, 1, 0, 0),
     ]
-    one, *merged, zero = lax.optimization_barrier(first)
-    merged.append(piece[3, 0])
+    zero, two, three, one, four = lax.optimization_barrier(first)
+    merged = [piece[3, 0], two, three, four]
     straight = [zero, one]
     straight += [sent(piece[1, flip], sections, 1, -1, flip) for flip in range(2)]
     merged = sent(combine(merged, tok_count), sections, 1, 1, 0)

time: 56.7 us -> 57.1 us (level)
  waiting for transfers between devices: 16.8 us -> 17.8 us
    ppermute x15, waiting for transfers between devices: 16.8 us -> 17.8 us  [sent(): return lax.ppermute(shard, ('section', 'expert'), pairs)]
where the time goes in v18:
time: 57.1 us; the launch traced here: 56.9 us
  starting transfers between devices  26.8 us (47%)
  waiting for transfers between devices  17.8 us (31%)
  Pallas kernels  7.59 us (13%)
  local copies, waits for them, and re-layouts  4.62 us (8%)
    ppermute x15, starting transfers between devices, sent(): return lax.ppermute(shard, ('section', 'expert'), pairs)  26.3 us
    ppermute x15, waiting for transfers between devices, sent(): return lax.ppermute(shard, ('section', 'expert'), pairs)  17.8 us
    pallas_call x9, Pallas kernels, local_call(): pl.pallas_call(kernel, out_shape=out_shape, in_specs=[vmem if spec is Non...  7.59 us
    unnamed x4, local copies, waits for them, and re-layouts  4.62 us
  transfers between devices with their start and end apart: 17, of which 9 were waited for; matrix products, arithmetic and copies ran while one was open for 0% of the time, Pallas kernels for 8%

profile of v18, /device:TPU:0, one launch (start us, length us, event | category | flops | bytes accessed | tf_op | source)
XLA Modules:
  0.0 56.9 jit_solution(6417263664193492765)
XLA Ops:
  0.5 1.0 %prepare.1.block = bf16[32,3712]{1,0:T(8,128)(2,1)S(1)} custom-call(s32[2,32]{1,0:T(2,128)} %bitcast.15, f32[2,32]{1,0:T(2,128)} %bitcast.16, bf16[32,3584]{1,0:T(8,128)(2,1)} %bitcast.14), custom_call_target="tpu_custom_call" | custom-call | tf_op jit(solution)/shard_map/prepare/pallas_call | solution.py:84
  1.5 3.1 %collective-permute-start.1 = (bf16[32,3712]{1,0:T(8,128)(2,1)S(1)}, bf16[32,3712]{1,0:T(8,128)(2,1)S(1)}, u32[]{:S(2)}, u32[]{:S(2)}) collective-permute-start(bf16[32,3712]{1,0:T(8,128)(2,1)S(1)} %prepare.1.block), channel_id=1, source_target_pairs={{0,4},{1,5},{2,6},{3,7},{4,12},{5,13},{6,14},{7,15},{8,0},{9,1},{1... | collective-permute-start | bytes 712712 | tf_op jit(solution)/shard_map/ppermute | solution.py:306
  5.0 1.6 %collective-permute-start = (bf16[16,3712]{1,0:T(8,128)(2,1)S(1)}, bf16[16,3712]{1,0:T(8,128)(2,1)S(1)}, u32[]{:S(2)}, u32[]{:S(2)}) collective-permute-start(bf16[16,3712]{1,0:T(8,128)(2,1)S(1)} %get-tuple-element.34), channel_id=1, source_target_pairs={{0,2},{1,3},{2,0},{3,1},{4,6},{5,7},{6,4},{7,5},{8,10},{9,11},{10,... | collective-permute-start | bytes 356360 | tf_op jit(solution)/shard_map/ppermute | solution.py:306
  6.6 3.1 %copy-done = bf16[1,3584,1024]{2,1,0:T(8,128)(2,1)S(1)} copy-done((bf16[1,3584,1024]{2,1,0:T(8,128)(2,1)S(1)}, bf16[1,3584,1024]{2,1,0:T(8,128)(2,1)}, u32[]{:S(2)}) %copy-start) | copy-done | bytes 7340056
  10.2 1.5 %copy-done.1 = bf16[1,512,3584]{2,1,0:T(8,128)(2,1)S(1)} copy-done((bf16[1,512,3584]{2,1,0:T(8,128)(2,1)S(1)}, bf16[1,512,3584]{2,1,0:T(8,128)(2,1)}, u32[]{:S(2)}) %copy-start.1) | copy-done | bytes 3670040
  12.4 1.2 %collective-permute-start.4 = (bf16[16,3712]{1,0:T(8,128)(2,1)S(1)}, bf16[16,3712]{1,0:T(8,128)(2,1)S(1)}, u32[]{:S(2)}, u32[]{:S(2)}) collective-permute-start(bf16[16,3712]{1,0:T(8,128)(2,1)S(1)} %get-tuple-element.41), channel_id=1, source_target_pairs={{0,2},{1,3},{2,0},{3,1},{4,6},{5,7},{6,4},{7,5},{8,10},{9,11},{10,... | collective-permute-start | bytes 356360 | tf_op jit(solution)/shard_map/ppermute | solution.py:306
  13.6 2.0 %collective-permute-start.2 = (bf16[16,3712]{1,0:T(8,128)(2,1)S(1)}, bf16[16,3712]{1,0:T(8,128)(2,1)S(1)}, u32[]{:S(2)}, u32[]{:S(2)}) collective-permute-start(bf16[16,3712]{1,0:T(8,128)(2,1)S(1)} %get-tuple-element.39), channel_id=1, source_target_pairs={{0,4},{1,5},{2,6},{3,7},{4,12},{5,13},{6,14},{7,15},{8,0},{9,1},{1... | collective-permute-start | bytes 356360 | tf_op jit(solution)/shard_map/ppermute | solution.py:306
  15.6 2.1 %collective-permute-start.3 = (bf16[16,3712]{1,0:T(8,128)(2,1)S(1)}, bf16[16,3712]{1,0:T(8,128)(2,1)S(1)}, u32[]{:S(2)}, u32[]{:S(2)}) collective-permute-start(bf16[16,3712]{1,0:T(8,128)(2,1)S(1)} %get-tuple-element.40), channel_id=1, source_target_pairs={{0,6},{1,7},{2,4},{3,5},{4,14},{5,15},{6,12},{7,13},{8,2},{9,3},{1... | collective-permute-start | bytes 356360 | tf_op jit(solution)/shard_map/ppermute | solution.py:306
  17.7 1.9 %collective-permute-start.5 = (bf16[16,3712]{1,0:T(8,128)(2,1)S(1)}, bf16[16,3712]{1,0:T(8,128)(2,1)S(1)}, u32[]{:S(2)}, u32[]{:S(2)}) collective-permute-start(bf16[16,3712]{1,0:T(8,128)(2,1)S(1)} %get-tuple-element.44), channel_id=1, source_target_pairs={{0,10},{1,11},{2,8},{3,9},{4,2},{5,3},{6,0},{7,1},{8,14},{9,15},{1... | collective-permute-start | bytes 356360 | tf_op jit(solution)/shard_map/ppermute | solution.py:306
  19.8 2.2 %collective-permute-start.6 = (bf16[16,3712]{1,0:T(8,128)(2,1)S(1)}, bf16[16,3712]{1,0:T(8,128)(2,1)S(1)}, u32[]{:S(2)}, u32[]{:S(2)}) collective-permute-start(bf16[16,3712]{1,0:T(8,128)(2,1)S(1)} %get-tuple-element.45), channel_id=1, source_target_pairs={{0,8},{1,9},{2,10},{3,11},{4,0},{5,1},{6,2},{7,3},{8,12},{9,13},{1... | collective-permute-start | bytes 356360 | tf_op jit(solution)/shard_map/ppermute | solution.py:306
  22.1 4.1 %collective-permute-done.3.refs_4_ = bf16[16,3712]{1,0:T(8,128)(2,1)S(1)} collective-permute-done((bf16[16,3712]{1,0:T(8,128)(2,1)S(1)}, bf16[16,3712]{1,0:T(8,128)(2,1)S(1)}, u32[]{:S(2)}, u32[]{:S(2)}) %collective-permute-start.3) | collective-permute-done | bytes 118816 | tf_op jit(solution)/shard_map/ppermute | solution.py:306
  26.8 1.7 %near_pass.1 = (bf16[128,3712]{1,0:T(8,128)(2,1)S(1)}, f32[128,3584]{1,0:T(8,128)S(1)}) custom-call(bf16[16,3712]{1,0:T(8,128)(2,1)S(1)} %get-tuple-element.33.refs_0_, bf16[16,3712]{1,0:T(8,128)(2,1)S(1)} %collective-permute-done.refs_1_, bf16[16,3712]{1,0:T(8,128)(2,1)S(1)} %get-tuple-element.38.refs_2_, ...), custom_call_target="tpu_custom_call" | custom-call | bytes 11010048 | tf_op jit(solution)/shard_map/near_pass/pallas_call | solution.py:84
  28.6 1.7 %far_pass.1 = (bf16[16,3712]{1,0:T(8,128)(2,1)S(1)}, bf16[16,3712]{1,0:T(8,128)(2,1)S(1)}, bf16[16,3712]{1,0:T(8,128)(2,1)S(1)}, bf16[16,3712]{1,0:T(8,128)(2,1)...) custom-call(bf16[128,3712]{1,0:T(8,128)(2,1)S(1)} %get-tuple-element, ...), custom_call_target="tpu_custom_call" | custom-call | bytes 11010048 | tf_op jit(solution)/shard_map/far_pass/pallas_call | solution.py:84
  30.3 1.6 %collective-permute-start.10 = (bf16[16,3712]{1,0:T(8,128)(2,1)S(1)}, bf16[16,3712]{1,0:T(8,128)(2,1)S(1)}, u32[]{:S(2)}, u32[]{:S(2)}) collective-permute-start(bf16[16,3712]{1,0:T(8,128)(2,1)S(1)} %get-tuple-element.49), channel_id=1, source_target_pairs={{0,6},{1,7},{2,4},{3,5},{4,14},{5,15},{6,12},{7,13},{8,2},{9,3},{1... | collective-permute-start | bytes 356360 | tf_op jit(solution)/shard_map/ppermute | solution.py:306
  31.9 0.9 %collective-permute-start.11 = (bf16[16,3712]{1,0:T(8,128)(2,1)S(1)}, bf16[16,3712]{1,0:T(8,128)(2,1)S(1)}, u32[]{:S(2)}, u32[]{:S(2)}) collective-permute-start(bf16[16,3712]{1,0:T(8,128)(2,1)S(1)} %get-tuple-element.50), channel_id=1, source_target_pairs={{0,2},{1,3},{2,0},{3,1},{4,6},{5,7},{6,4},{7,5},{8,10},{9,11},{10,... | collective-permute-start | bytes 356360 | tf_op jit(solution)/shard_map/ppermute | solution.py:306
  32.8 2.1 %collective-permute-start.12 = (bf16[16,3712]{1,0:T(8,128)(2,1)S(1)}, bf16[16,3712]{1,0:T(8,128)(2,1)S(1)}, u32[]{:S(2)}, u32[]{:S(2)}) collective-permute-start(bf16[16,3712]{1,0:T(8,128)(2,1)S(1)} %get-tuple-element.51), channel_id=1, source_target_pairs={{0,18},{1,19},{2,16},{3,17},{4,22},{5,23},{6,20},{7,21},{8,26},{9,... | collective-permute-start | bytes 356360 | tf_op jit(solution)/shard_map/ppermute | solution.py:306
  34.9 2.8 %collective-permute-start.13 = (bf16[16,3712]{1,0:T(8,128)(2,1)S(1)}, bf16[16,3712]{1,0:T(8,128)(2,1)S(1)}, u32[]{:S(2)}, u32[]{:S(2)}) collective-permute-start(bf16[16,3712]{1,0:T(8,128)(2,1)S(1)} %get-tuple-element.52), channel_id=1, source_target_pairs={{0,4},{1,5},{2,6},{3,7},{4,12},{5,13},{6,14},{7,15},{8,0},{9,1},{1... | collective-permute-start | bytes 356360 | tf_op jit(solution)/shard_map/ppermute | solution.py:306
  38.3 2.1 %collective-permute-done.11.refs_2_ = bf16[16,3712]{1,0:T(8,128)(2,1)S(1)} collective-permute-done((bf16[16,3712]{1,0:T(8,128)(2,1)S(1)}, bf16[16,3712]{1,0:T(8,128)(2,1)S(1)}, u32[]{:S(2)}, u32[]{:S(2)}) %collective-permute-start.11) | collective-permute-done | bytes 118816 | tf_op jit(solution)/shard_map/ppermute | solution.py:306
  40.6 1.9 %collective-permute-done.9.refs_0_ = bf16[16,3712]{1,0:T(8,128)(2,1)S(1)} collective-permute-done((bf16[16,3712]{1,0:T(8,128)(2,1)S(1)}, bf16[16,3712]{1,0:T(8,128)(2,1)S(1)}, u32[]{:S(2)}, u32[]{:S(2)}) %collective-permute-start.9) | collective-permute-done | bytes 118816 | tf_op jit(solution)/shard_map/ppermute | solution.py:306
  43.8 3.1 %collective-permute-start.14 = (bf16[16,3712]{1,0:T(8,128)(2,1)S(1)}, bf16[16,3712]{1,0:T(8,128)(2,1)S(1)}, u32[]{:S(2)}, u32[]{:S(2)}) collective-permute-start(bf16[16,3712]{1,0:T(8,128)(2,1)S(1)} %get-tuple-element.55), channel_id=1, source_target_pairs={{0,24},{1,25},{2,26},{3,27},{4,16},{5,17},{6,18},{7,19},{8,28},{9,... | collective-permute-start | bytes 356360 | tf_op jit(solution)/shard_map/ppermute | solution.py:306
  47.3 5.4 %collective-permute-done.14.refs_2_ = bf16[16,3712]{1,0:T(8,128)(2,1)S(1)} collective-permute-done((bf16[16,3712]{1,0:T(8,128)(2,1)S(1)}, bf16[16,3712]{1,0:T(8,128)(2,1)S(1)}, u32[]{:S(2)}, u32[]{:S(2)}) %collective-permute-start.14) | collective-permute-done | bytes 118816 | tf_op jit(solution)/shard_map/ppermute | solution.py:306
  52.7 1.9 %collective-permute-done.15.refs_3_ = bf16[16,3712]{1,0:T(8,128)(2,1)S(1)} collective-permute-done((bf16[16,3712]{1,0:T(8,128)(2,1)S(1)}, bf16[16,3712]{1,0:T(8,128)(2,1)S(1)}, u32[]{:S(2)}, u32[]{:S(2)}) %collective-permute-start.15) | collective-permute-done | bytes 118816 | tf_op jit(solution)/shard_map/ppermute | solution.py:306
  54.6 1.2 %collective-permute-done.16.refs_4_ = bf16[32,3584]{1,0:T(8,128)(2,1)S(1)} collective-permute-done((bf16[32,3584]{1,0:T(8,128)(2,1)S(1)}, bf16[32,3584]{1,0:T(8,128)(2,1)S(1)}, u32[]{:S(2)}, u32[]{:S(2)}) %collective-permute-start.16) | collective-permute-done | bytes 229408 | tf_op jit(solution)/shard_map/ppermute | solution.py:306
  55.8 1.1 %combine.3 = bf16[32,3584]{1,0:T(8,128)(2,1)} custom-call(bf16[16,3712]{1,0:T(8,128)(2,1)S(1)} %collective-permute-done.9.refs_0_, bf16[16,3712]{1,0:T(8,128)(2,1)S(1)} %collective-permute-done.12.refs_1_, bf16[16,3712]{1,0:T(8,128)(2,1)S(1)} %collective-permute-done.14.refs_2_, bf16[16,3712]{1,0:T(8,128)(2,1)S(1)} %collective-permute-done.15.refs_3_, ...), custom_call_target="tpu_custom_call" | custom-call | tf_op jit(solution)/shard_map/combine/pallas_call | solution.py:84
  (23 shorter events, 5.4 us)
Async XLA Ops:
  0.0 28.6 %collective-permute-start.7 = (bf16[3584,1024]{1,0:T(8,128)(2,1)}, bf16[3584,1024]{1,0:T(8,128)(2,1)S(1)}, u32[]{:S(2)}, u32[]{:S(2)}) collective-permute-start(bf16[3584,1024]{1,0:T(8,128)(2,1)} %bitcast.10), channel_id=1, source_target_pairs={{0,1},{1,0},{2,3},{3,2},{4,5},{5,4},{6,7},{7,6},{8,9},{9,8},{10,11... | collective-permute-start | bytes 22020104 | tf_op jit(solution)/shard_map/ppermute | solution.py:324
  0.5 28.1 %collective-permute-start.8 = (bf16[512,3584]{1,0:T(8,128)(2,1)}, bf16[512,3584]{1,0:T(8,128)(2,1)S(1)}, u32[]{:S(2)}, u32[]{:S(2)}) collective-permute-start(bf16[512,3584]{1,0:T(8,128)(2,1)} %bitcast.12), channel_id=1, source_target_pairs={{0,1},{1,0},{2,3},{3,2},{4,5},{5,4},{6,7},{7,6},{8,9},{9,8},{10,11... | collective-permute-start | bytes 11010056 | tf_op jit(solution)/shard_map/ppermute | solution.py:323
  1.5 10.5 %collective-permute-start.1 = (bf16[32,3712]{1,0:T(8,128)(2,1)S(1)}, bf16[32,3712]{1,0:T(8,128)(2,1)S(1)}, u32[]{:S(2)}, u32[]{:S(2)}) collective-permute-start(bf16[32,3712]{1,0:T(8,128)(2,1)S(1)} %prepare.1.block), channel_id=1, source_target_pairs={{0,4},{1,5},{2,6},{3,7},{4,12},{5,13},{6,14},{7,15},{8,0},{9,1},{1... | collective-permute-start | bytes 712712 | tf_op jit(solution)/shard_map/ppermute | solution.py:306
  5.0 7.0 %collective-permute-start = (bf16[16,3712]{1,0:T(8,128)(2,1)S(1)}, bf16[16,3712]{1,0:T(8,128)(2,1)S(1)}, u32[]{:S(2)}, u32[]{:S(2)}) collective-permute-start(bf16[16,3712]{1,0:T(8,128)(2,1)S(1)} %get-tuple-element.34), channel_id=1, source_target_pairs={{0,2},{1,3},{2,0},{3,1},{4,6},{5,7},{6,4},{7,5},{8,10},{9,11},{10,... | collective-permute-start | bytes 356360 | tf_op jit(solution)/shard_map/ppermute | solution.py:306
  6.6 3.1 %copy-start = (bf16[1,3584,1024]{2,1,0:T(8,128)(2,1)S(1)}, bf16[1,3584,1024]{2,1,0:T(8,128)(2,1)}, u32[]{:S(2)}) copy-start(bf16[1,3584,1024]{2,1,0:T(8,128)(2,1)} %param.8) | copy-start | bytes 22020100
  9.7 2.0 %copy-start.1 = (bf16[1,512,3584]{2,1,0:T(8,128)(2,1)S(1)}, bf16[1,512,3584]{2,1,0:T(8,128)(2,1)}, u32[]{:S(2)}) copy-start(bf16[1,512,3584]{2,1,0:T(8,128)(2,1)} %param.9) | copy-start | bytes 11010052
  12.4 5.3 %collective-permute-start.4 = (bf16[16,3712]{1,0:T(8,128)(2,1)S(1)}, bf16[16,3712]{1,0:T(8,128)(2,1)S(1)}, u32[]{:S(2)}, u32[]{:S(2)}) collective-permute-start(bf16[16,3712]{1,0:T(8,128)(2,1)S(1)} %get-tuple-element.41), channel_id=1, source_target_pairs={{0,2},{1,3},{2,0},{3,1},{4,6},{5,7},{6,4},{7,5},{8,10},{9,11},{10,... | collective-permute-start | bytes 356360 | tf_op jit(solution)/shard_map/ppermute | solution.py:306
  13.6 6.2 %collective-permute-start.2 = (bf16[16,3712]{1,0:T(8,128)(2,1)S(1)}, bf16[16,3712]{1,0:T(8,128)(2,1)S(1)}, u32[]{:S(2)}, u32[]{:S(2)}) collective-permute-start(bf16[16,3712]{1,0:T(8,128)(2,1)S(1)} %get-tuple-element.39), channel_id=1, source_target_pairs={{0,4},{1,5},{2,6},{3,7},{4,12},{5,13},{6,14},{7,15},{8,0},{9,1},{1... | collective-permute-start | bytes 356360 | tf_op jit(solution)/shard_map/ppermute | solution.py:306
  15.6 10.6 %collective-permute-start.3 = (bf16[16,3712]{1,0:T(8,128)(2,1)S(1)}, bf16[16,3712]{1,0:T(8,128)(2,1)S(1)}, u32[]{:S(2)}, u32[]{:S(2)}) collective-permute-start(bf16[16,3712]{1,0:T(8,128)(2,1)S(1)} %get-tuple-element.40), channel_id=1, source_target_pairs={{0,6},{1,7},{2,4},{3,5},{4,14},{5,15},{6,12},{7,13},{8,2},{9,3},{1... | collective-permute-start | bytes 356360 | tf_op jit(solution)/shard_map/ppermute | solution.py:306
  17.7 8.5 %collective-permute-start.5 = (bf16[16,3712]{1,0:T(8,128)(2,1)S(1)}, bf16[16,3712]{1,0:T(8,128)(2,1)S(1)}, u32[]{:S(2)}, u32[]{:S(2)}) collective-permute-start(bf16[16,3712]{1,0:T(8,128)(2,1)S(1)} %get-tuple-element.44), channel_id=1, source_target_pairs={{0,10},{1,11},{2,8},{3,9},{4,2},{5,3},{6,0},{7,1},{8,14},{9,15},{1... | collective-permute-start | bytes 356360 | tf_op jit(solution)/shard_map/ppermute | solution.py:306
  19.8 7.0 %collective-permute-start.6 = (bf16[16,3712]{1,0:T(8,128)(2,1)S(1)}, bf16[16,3712]{1,0:T(8,128)(2,1)S(1)}, u32[]{:S(2)}, u32[]{:S(2)}) collective-permute-start(bf16[16,3712]{1,0:T(8,128)(2,1)S(1)} %get-tuple-element.45), channel_id=1, source_target_pairs={{0,8},{1,9},{2,10},{3,11},{4,0},{5,1},{6,2},{7,3},{8,12},{9,13},{1... | collective-permute-start | bytes 356360 | tf_op jit(solution)/shard_map/ppermute | solution.py:306
  30.3 7.9 %collective-permute-start.10 = (bf16[16,3712]{1,0:T(8,128)(2,1)S(1)}, bf16[16,3712]{1,0:T(8,128)(2,1)S(1)}, u32[]{:S(2)}, u32[]{:S(2)}) collective-permute-start(bf16[16,3712]{1,0:T(8,128)(2,1)S(1)} %get-tuple-element.49), channel_id=1, source_target_pairs={{0,6},{1,7},{2,4},{3,5},{4,14},{5,15},{6,12},{7,13},{8,2},{9,3},{1... | collective-permute-start | bytes 356360 | tf_op jit(solution)/shard_map/ppermute | solution.py:306
  31.9 8.5 %collective-permute-start.11 = (bf16[16,3712]{1,0:T(8,128)(2,1)S(1)}, bf16[16,3712]{1,0:T(8,128)(2,1)S(1)}, u32[]{:S(2)}, u32[]{:S(2)}) collective-permute-start(bf16[16,3712]{1,0:T(8,128)(2,1)S(1)} %get-tuple-element.50), channel_id=1, source_target_pairs={{0,2},{1,3},{2,0},{3,1},{4,6},{5,7},{6,4},{7,5},{8,10},{9,11},{10,... | collective-permute-start | bytes 356360 | tf_op jit(solution)/shard_map/ppermute | solution.py:306
  32.8 7.6 %collective-permute-start.12 = (bf16[16,3712]{1,0:T(8,128)(2,1)S(1)}, bf16[16,3712]{1,0:T(8,128)(2,1)S(1)}, u32[]{:S(2)}, u32[]{:S(2)}) collective-permute-start(bf16[16,3712]{1,0:T(8,128)(2,1)S(1)} %get-tuple-element.51), channel_id=1, source_target_pairs={{0,18},{1,19},{2,16},{3,17},{4,22},{5,23},{6,20},{7,21},{8,26},{9,... | collective-permute-start | bytes 356360 | tf_op jit(solution)/shard_map/ppermute | solution.py:306
  34.9 5.7 %collective-permute-start.13 = (bf16[16,3712]{1,0:T(8,128)(2,1)S(1)}, bf16[16,3712]{1,0:T(8,128)(2,1)S(1)}, u32[]{:S(2)}, u32[]{:S(2)}) collective-permute-start(bf16[16,3712]{1,0:T(8,128)(2,1)S(1)} %get-tuple-element.52), channel_id=1, source_target_pairs={{0,4},{1,5},{2,6},{3,7},{4,12},{5,13},{6,14},{7,15},{8,0},{9,1},{1... | collective-permute-start | bytes 356360 | tf_op jit(solution)/shard_map/ppermute | solution.py:306
  37.7 4.8 %collective-permute-start.9 = (bf16[16,3712]{1,0:T(8,128)(2,1)S(1)}, bf16[16,3712]{1,0:T(8,128)(2,1)S(1)}, u32[]{:S(2)}, u32[]{:S(2)}) collective-permute-start(bf16[16,3712]{1,0:T(8,128)(2,1)S(1)} %get-tuple-element.48), channel_id=1, source_target_pairs={{0,16},{1,17},{2,18},{3,19},{4,20},{5,21},{6,22},{7,23},{8,24},{9,... | collective-permute-start | bytes 356360 | tf_op jit(solution)/shard_map/ppermute | solution.py:306
  43.0 12.8 %collective-permute-start.16 = (bf16[32,3584]{1,0:T(8,128)(2,1)S(1)}, bf16[32,3584]{1,0:T(8,128)(2,1)S(1)}, u32[]{:S(2)}, u32[]{:S(2)}) collective-permute-start(bf16[32,3584]{1,0:T(8,128)(2,1)S(1)} %combine.2), channel_id=1, source_target_pairs={{0,20},{1,21},{2,22},{3,23},{4,28},{5,29},{6,30},{7,31},{8,16},{9,... | collective-permute-start | bytes 688136 | tf_op jit(solution)/shard_map/ppermute | solution.py:306
  43.8 8.9 %collective-permute-start.14 = (bf16[16,3712]{1,0:T(8,128)(2,1)S(1)}, bf16[16,3712]{1,0:T(8,128)(2,1)S(1)}, u32[]{:S(2)}, u32[]{:S(2)}) collective-permute-start(bf16[16,3712]{1,0:T(8,128)(2,1)S(1)} %get-tuple-element.55), channel_id=1, source_target_pairs={{0,24},{1,25},{2,26},{3,27},{4,16},{5,17},{6,18},{7,19},{8,28},{9,... | collective-permute-start | bytes 356360 | tf_op jit(solution)/shard_map/ppermute | solution.py:306
  46.9 7.7 %collective-permute-start.15 = (bf16[16,3712]{1,0:T(8,128)(2,1)S(1)}, bf16[16,3712]{1,0:T(8,128)(2,1)S(1)}, u32[]{:S(2)}, u32[]{:S(2)}) collective-permute-start(bf16[16,3712]{1,0:T(8,128)(2,1)S(1)} %get-tuple-element.56), channel_id=1, source_target_pairs={{0,26},{1,27},{2,24},{3,25},{4,18},{5,19},{6,16},{7,17},{8,30},{9,... | collective-permute-start | bytes 356360 | tf_op jit(solution)/shard_map/ppermute | solution.py:306

commit v19 on v18

--- a/solution.py
+++ b/solution.py
@@ -198,22 +198,6 @@
     return (gate / (1.0 + jnp.exp(-gate)) * both[:, hidden:]).astype(jnp.bfloat16)
 
 
-def write_pieces(slots, total, outs):
-    chip = lax.axis_index("expert") >> 1
-    width = total.shape[1]
-    experts = 2 * len(RING)
-    notes = slots[:, width:].astype(jnp.float32)
-    lane = iota(notes.shape, 1)
-    mine = (lane >= experts) & (lane < 4 * experts) & ((lane & (experts - 1)) == chip)
-    scale = jnp.sum(jnp.where(mine, notes, 0.0), axis=1, keepdims=True)
-    start = 0
-    for out in outs:
-        stop = start + out.shape[0]
-        out[:, :width] = (total[start:stop] * scale[start:stop]).astype(jnp.bfloat16)
-        out[:, width:] = slots[start:stop, width:]
-        start = stop
-
-
 def near_kernel(*refs):
     pieces, (first, second, slots, total) = refs[:-4], refs[-4:]
     start = 0
@@ -241,21 +225,33 @@
     )
 
 
-def far_kernel(slots, before, first, second, *refs):
+def far_kernel(picks, slots, before, first, second, *refs):
     outs, total = refs[:-1], refs[-1]
+    device = lax.axis_index("expert")
+    chip, odd = device >> 1, device & 1
     width = total.shape[1]
+    experts = 2 * len(RING)
     both = jnp.dot(slots[:, :width], first[...], preferred_element_type=jnp.float32)
     term = jnp.dot(gated(both), second[...], preferred_element_type=jnp.float32)
-    total[...] = before[...] + term
-    write_pieces(slots, total, outs)
-
-
-def far_pass(slots, total, weights, capacity):
-    count, full = slots.shape
-    return local_call(
-        far_kernel,
+    notes = slots[:, width:].astype(jnp.float32)
+    lane = iota(notes.shape, 1)
+    mine = (lane >= experts) & (lane < 4 * experts) & ((lane & (experts - 1)) == chip)
+    scale = jnp.sum(jnp.where(mine, notes, 0.0), axis=1, keepdims=True)
+    total[...] = (before[...] + term) * scale
+    for out, (even_at, odd_at) in zip(outs, picks):
+        capacity = out.shape[0]
+        at = (even_at + odd * (odd_at - even_at)) * capacity
+        rows = pl.ds(pl.multiple_of(at, capacity), capacity)
+        out[:, :width] = total[rows, :].astype(jnp.bfloat16)
+        out[:, width:] = slots[rows, width:]
+
+
+def far_pass(slots, total, weights, capacity, picks):
+    full = slots.shape[1]
+    return local_call(
+        functools.partial(far_kernel, picks),
         "far_pass",
-        [jax.ShapeDtypeStruct((capacity, full), jnp.bfloat16)] * (count // capacity),
+        [jax.ShapeDtypeStruct((capacity, full), jnp.bfloat16) for _ in picks],
         [None] * 4,
         (slots, total, *weights),
         [pltpu.VMEM(total.shape, jnp.float32)],
@@ -264,13 +260,18 @@
     )
 
 
-def combine_kernel(count, *refs):
+def combine_kernel(picks, count, *refs):
     blocks, more, (out, slots) = refs[:count], refs[count:-2], refs[-2:]
     tok_count, width = out.shape
-    start = 0
-    for block in blocks:
-        slots[start : start + block.shape[0]] = block[...]
-        start += block.shape[0]
+    capacity = blocks[0].shape[0]
+    odd = lax.axis_index("expert") & 1
+    for side in range(2):
+
+        @pl.when(odd == side)
+        def _():
+            for at, pick in enumerate(picks):
+                slots[at * capacity : (at + 1) * capacity] = blocks[pick[side]][...]
+
     token = slots[:, width:]
     part = width // 7
     for at in range(7):
@@ -281,29 +282,33 @@
         out[:, place] = mixed.astype(out.dtype)
 
 
-def combine(blocks, tok_count, *more):
+def combine(blocks, picks, tok_count, *more):
     capacity, full = blocks[0].shape
     return local_call(
-        functools.partial(combine_kernel, len(blocks)),
+        functools.partial(combine_kernel, picks, len(blocks)),
         "combine",
         jax.ShapeDtypeStruct((tok_count, full - LANES), jnp.bfloat16),
         [None] * (len(blocks) + len(more)),
         (*blocks, *more),
-        [pltpu.VMEM((capacity * len(blocks), full), jnp.bfloat16)],
-    )
-
-
-def sent(shard, sections, section_step, ring_step, flip):
+        [pltpu.VMEM((capacity * len(picks), full), jnp.bfloat16)],
+    )
+
+
+def sent_by_core(shard, sections, moves):
     planes = len(RING)
     pairs = []
     for s in range(sections):
         for z in range(planes):
             for y in range(2):
-                for core in range(2):
+                for core, (section_step, ring_step, flip) in enumerate(moves):
                     plane = RING[(RING.index(z) + ring_step) % planes]
                     target = (((s + section_step) % sections) * planes + plane) * 2 + (y ^ flip)
                     pairs.append((((s * planes + z) * 2 + y) * 2 + core, target * 2 + core))
     return lax.ppermute(shard, ("section", "expert"), pairs)
+
+
+def sent(shard, sections, section_step, ring_step, flip):
+    return sent_by_core(shard, sections, [(section_step, ring_step, flip)] * 2)
 
 
 def after(value, other):
@@ -338,21 +343,21 @@
     pieces = (own0, other0, own1, own2, other2, other1, other3, own3)
     places = ((0, 0), (0, 1), (1, 0), (2, 0), (2, 1), (1, 1), (3, 1), (3, 0))
     slots, total = near_pass(pieces, near)
-    pieces = far_pass(slots, total, (far_in, far_out), capacity)
-    piece = dict(zip(places, pieces))
-    first = [
-        sent(piece[0, 0], sections, 1, 0, 0),
-        sent(piece[2, 1], sections, 0, 1, 1),
-        sent(piece[3, 1], sections, 0, 0, 1),
-        sent(piece[0, 1], sections, 1, 0, 1),
-        sent(piece[2, 0], sections, 0, 1, 0),
+    moves = {(2, 1): (0, 1, 1), (3, 1): (0, 0, 1), (2, 0): (0, 1, 0), (0, 0): (1, 0, 0), (0, 1): (1, 0, 1)}
+    even = ((2, 1), (3, 1), (2, 0), (0, 0), (0, 1))
+    odd = ((0, 0), (0, 1), (2, 1), (3, 1), (2, 0))
+    picks = [(places.index(a), places.index(b)) for a, b in zip(even, odd)]
+    picks += [(places.index(at),) * 2 for at in ((3, 0), (1, 0), (1, 1))]
+    *pieces, stays, near1, other1 = far_pass(slots, total, (far_in, far_out), capacity, picks)
+    stage = [
+        sent_by_core(piece, sections, (moves[a], moves[b])) for piece, a, b in zip(pieces, even, odd)
     ]
-    zero, two, three, one, four = lax.optimization_barrier(first)
-    merged = [piece[3, 0], two, three, four]
-    straight = [zero, one]
-    straight += [sent(piece[1, flip], sections, 1, -1, flip) for flip in range(2)]
-    merged = sent(combine(merged, tok_count), sections, 1, 1, 0)
-    return combine(straight, tok_count, merged)[None]
+    stage = lax.optimization_barrier(stage)
+    merged = combine([stays, *stage], ((0, 0), (1, 3), (2, 4), (3, 5)), tok_count)
+    merged = sent(merged, sections, 1, 1, 0)
+    last = [sent(near1, sections, 1, -1, 0), sent(other1, sections, 1, -1, 1)]
+    picks = ((0, 0), (1, 1), (5, 2), (6, 3))
+    return combine([*last, *stage], picks, tok_count, merged)[None]
 
 
 def per_device(rows, route_ids, route_weights, w_gate_up, w_down):

time: 57.1 us -> 57.7 us (1.011)
  transfers between devices with their start and end apart: 17 -> 17, of which waited for: 9 -> 7; matrix products, arithmetic and copies ran while one was open for 0% -> 0% of each run, Pallas kernels for 8% -> 8%
where the time goes in v19:
time: 57.7 us; the launch traced here: 57.5 us
  starting transfers between devices  27.3 us (47%)
  waiting for transfers between devices  17.6 us (31%)
  Pallas kernels  7.92 us (14%)
  local copies, waits for them, and re-layouts  4.62 us (8%)
    ppermute x15, starting transfers between devices, sent_by_core(): return lax.ppermute(shard, ('section', 'expert'), pairs)  26.8 us
    ppermute x15, waiting for transfers between devices, sent_by_core(): return lax.ppermute(shard, ('section', 'expert'), pairs)  17.6 us
    pallas_call x9, Pallas kernels, local_call(): pl.pallas_call(kernel, out_shape=out_shape, in_specs=[vmem if spec is Non...  7.92 us
    unnamed x4, local copies, waits for them, and re-layouts  4.62 us
  transfers between devices with their start and end apart: 17, of which 7 were waited for; matrix products, arithmetic and copies ran while one was open for 0% of the time, Pallas kernels for 8%

profile of v19, /device:TPU:0, one launch (start us, length us, event | category | flops | bytes accessed | tf_op | source)
XLA Modules:
  0.0 57.5 jit_solution(10738454960569443888)
XLA Ops:
  0.5 1.0 %prepare.1.block = bf16[32,3712]{1,0:T(8,128)(2,1)S(1)} custom-call(s32[2,32]{1,0:T(2,128)} %bitcast.15, f32[2,32]{1,0:T(2,128)} %bitcast.16, bf16[32,3584]{1,0:T(8,128)(2,1)} %bitcast.14), custom_call_target="tpu_custom_call" | custom-call | tf_op jit(solution)/shard_map/prepare/pallas_call | solution.py:84
  1.5 3.1 %collective-permute-start.1 = (bf16[32,3712]{1,0:T(8,128)(2,1)S(1)}, bf16[32,3712]{1,0:T(8,128)(2,1)S(1)}, u32[]{:S(2)}, u32[]{:S(2)}) collective-permute-start(bf16[32,3712]{1,0:T(8,128)(2,1)S(1)} %prepare.1.block), channel_id=1, source_target_pairs={{0,4},{1,5},{2,6},{3,7},{4,12},{5,13},{6,14},{7,15},{8,0},{9,1},{1... | collective-permute-start | bytes 712712 | tf_op jit(solution)/shard_map/ppermute | solution.py:307
  5.0 1.6 %collective-permute-start = (bf16[16,3712]{1,0:T(8,128)(2,1)S(1)}, bf16[16,3712]{1,0:T(8,128)(2,1)S(1)}, u32[]{:S(2)}, u32[]{:S(2)}) collective-permute-start(bf16[16,3712]{1,0:T(8,128)(2,1)S(1)} %get-tuple-element.34), channel_id=1, source_target_pairs={{0,2},{1,3},{2,0},{3,1},{4,6},{5,7},{6,4},{7,5},{8,10},{9,11},{10,... | collective-permute-start | bytes 356360 | tf_op jit(solution)/shard_map/ppermute | solution.py:307
  6.6 3.1 %copy-done = bf16[1,3584,1024]{2,1,0:T(8,128)(2,1)S(1)} copy-done((bf16[1,3584,1024]{2,1,0:T(8,128)(2,1)S(1)}, bf16[1,3584,1024]{2,1,0:T(8,128)(2,1)}, u32[]{:S(2)}) %copy-start) | copy-done | bytes 7340056
  10.2 1.5 %copy-done.1 = bf16[1,512,3584]{2,1,0:T(8,128)(2,1)S(1)} copy-done((bf16[1,512,3584]{2,1,0:T(8,128)(2,1)S(1)}, bf16[1,512,3584]{2,1,0:T(8,128)(2,1)}, u32[]{:S(2)}) %copy-start.1) | copy-done | bytes 3670040
  12.4 1.2 %collective-permute-start.4 = (bf16[16,3712]{1,0:T(8,128)(2,1)S(1)}, bf16[16,3712]{1,0:T(8,128)(2,1)S(1)}, u32[]{:S(2)}, u32[]{:S(2)}) collective-permute-start(bf16[16,3712]{1,0:T(8,128)(2,1)S(1)} %get-tuple-element.41), channel_id=1, source_target_pairs={{0,2},{1,3},{2,0},{3,1},{4,6},{5,7},{6,4},{7,5},{8,10},{9,11},{10,... | collective-permute-start | bytes 356360 | tf_op jit(solution)/shard_map/ppermute | solution.py:307
  13.6 2.0 %collective-permute-start.2 = (bf16[16,3712]{1,0:T(8,128)(2,1)S(1)}, bf16[16,3712]{1,0:T(8,128)(2,1)S(1)}, u32[]{:S(2)}, u32[]{:S(2)}) collective-permute-start(bf16[16,3712]{1,0:T(8,128)(2,1)S(1)} %get-tuple-element.39), channel_id=1, source_target_pairs={{0,4},{1,5},{2,6},{3,7},{4,12},{5,13},{6,14},{7,15},{8,0},{9,1},{1... | collective-permute-start | bytes 356360 | tf_op jit(solution)/shard_map/ppermute | solution.py:307
  15.6 2.1 %collective-permute-start.3 = (bf16[16,3712]{1,0:T(8,128)(2,1)S(1)}, bf16[16,3712]{1,0:T(8,128)(2,1)S(1)}, u32[]{:S(2)}, u32[]{:S(2)}) collective-permute-start(bf16[16,3712]{1,0:T(8,128)(2,1)S(1)} %get-tuple-element.40), channel_id=1, source_target_pairs={{0,6},{1,7},{2,4},{3,5},{4,14},{5,15},{6,12},{7,13},{8,2},{9,3},{1... | collective-permute-start | bytes 356360 | tf_op jit(solution)/shard_map/ppermute | solution.py:307
  17.7 1.9 %collective-permute-start.5 = (bf16[16,3712]{1,0:T(8,128)(2,1)S(1)}, bf16[16,3712]{1,0:T(8,128)(2,1)S(1)}, u32[]{:S(2)}, u32[]{:S(2)}) collective-permute-start(bf16[16,3712]{1,0:T(8,128)(2,1)S(1)} %get-tuple-element.44), channel_id=1, source_target_pairs={{0,10},{1,11},{2,8},{3,9},{4,2},{5,3},{6,0},{7,1},{8,14},{9,15},{1... | collective-permute-start | bytes 356360 | tf_op jit(solution)/shard_map/ppermute | solution.py:307
  19.8 2.2 %collective-permute-start.6 = (bf16[16,3712]{1,0:T(8,128)(2,1)S(1)}, bf16[16,3712]{1,0:T(8,128)(2,1)S(1)}, u32[]{:S(2)}, u32[]{:S(2)}) collective-permute-start(bf16[16,3712]{1,0:T(8,128)(2,1)S(1)} %get-tuple-element.45), channel_id=1, source_target_pairs={{0,8},{1,9},{2,10},{3,11},{4,0},{5,1},{6,2},{7,3},{8,12},{9,13},{1... | collective-permute-start | bytes 356360 | tf_op jit(solution)/shard_map/ppermute | solution.py:307
  22.1 4.1 %collective-permute-done.3.refs_4_ = bf16[16,3712]{1,0:T(8,128)(2,1)S(1)} collective-permute-done((bf16[16,3712]{1,0:T(8,128)(2,1)S(1)}, bf16[16,3712]{1,0:T(8,128)(2,1)S(1)}, u32[]{:S(2)}, u32[]{:S(2)}) %collective-permute-start.3) | collective-permute-done | bytes 118816 | tf_op jit(solution)/shard_map/ppermute | solution.py:307
  26.8 1.7 %near_pass.1 = (bf16[128,3712]{1,0:T(8,128)(2,1)S(1)}, f32[128,3584]{1,0:T(8,128)S(1)}) custom-call(bf16[16,3712]{1,0:T(8,128)(2,1)S(1)} %get-tuple-element.33.refs_0_, bf16[16,3712]{1,0:T(8,128)(2,1)S(1)} %collective-permute-done.refs_1_, bf16[16,3712]{1,0:T(8,128)(2,1)S(1)} %get-tuple-element.38.refs_2_, ...), custom_call_target="tpu_custom_call" | custom-call | bytes 11010048 | tf_op jit(solution)/shard_map/near_pass/pallas_call | solution.py:84
  28.6 2.0 %far_pass.1 = (bf16[16,3712]{1,0:T(8,128)(2,1)S(1)}, bf16[16,3712]{1,0:T(8,128)(2,1)S(1)}, bf16[16,3712]{1,0:T(8,128)(2,1)S(1)}, bf16[16,3712]{1,0:T(8,128)(2,1)...) custom-call(bf16[128,3712]{1,0:T(8,128)(2,1)S(1)} %get-tuple-element, ...), custom_call_target="tpu_custom_call" | custom-call | bytes 11010048 | tf_op jit(solution)/shard_map/far_pass/pallas_call | solution.py:84
  30.6 1.6 %collective-permute-start.11 = (bf16[16,3712]{1,0:T(8,128)(2,1)S(1)}, bf16[16,3712]{1,0:T(8,128)(2,1)S(1)}, u32[]{:S(2)}, u32[]{:S(2)}) collective-permute-start(bf16[16,3712]{1,0:T(8,128)(2,1)S(1)} %get-tuple-element.50), channel_id=1, source_target_pairs={{0,6},{1,17},{2,4},{3,19},{4,14},{5,21},{6,12},{7,23},{8,2},{9,25}... | collective-permute-start | bytes 356360 | tf_op jit(solution)/shard_map/ppermute | solution.py:307
  33.1 2.5 %collective-permute-start.13 = (bf16[16,3712]{1,0:T(8,128)(2,1)S(1)}, bf16[16,3712]{1,0:T(8,128)(2,1)S(1)}, u32[]{:S(2)}, u32[]{:S(2)}) collective-permute-start(bf16[16,3712]{1,0:T(8,128)(2,1)S(1)} %get-tuple-element.52), channel_id=1, source_target_pairs={{0,4},{1,7},{2,6},{3,5},{4,12},{5,15},{6,14},{7,13},{8,0},{9,3},{1... | collective-permute-start | bytes 356360 | tf_op jit(solution)/shard_map/ppermute | solution.py:307
  35.6 1.5 %collective-permute-start.14 = (bf16[16,3712]{1,0:T(8,128)(2,1)S(1)}, bf16[16,3712]{1,0:T(8,128)(2,1)S(1)}, u32[]{:S(2)}, u32[]{:S(2)}) collective-permute-start(bf16[16,3712]{1,0:T(8,128)(2,1)S(1)} %get-tuple-element.53), channel_id=1, source_target_pairs={{0,16},{1,3},{2,18},{3,1},{4,20},{5,7},{6,22},{7,5},{8,24},{9,11},... | collective-permute-start | bytes 356360 | tf_op jit(solution)/shard_map/ppermute | solution.py:307
  37.1 1.5 %collective-permute-start.15 = (bf16[16,3712]{1,0:T(8,128)(2,1)S(1)}, bf16[16,3712]{1,0:T(8,128)(2,1)S(1)}, u32[]{:S(2)}, u32[]{:S(2)}) collective-permute-start(bf16[16,3712]{1,0:T(8,128)(2,1)S(1)} %get-tuple-element.54), channel_id=1, source_target_pairs={{0,18},{1,5},{2,16},{3,7},{4,22},{5,13},{6,20},{7,15},{8,26},{9,1}... | collective-permute-start | bytes 356360 | tf_op jit(solution)/shard_map/ppermute | solution.py:307
  38.6 2.8 %collective-permute-done.12.refs_2_.refs_3_ = bf16[16,3712]{1,0:T(8,128)(2,1)S(1)} collective-permute-done((bf16[16,3712]{1,0:T(8,128)(2,1)S(1)}, bf16[16,3712]{1,0:T(8,128)(2,1)S(1)}, u32[]{:S(2)}, u32[]{:S(2)}) %collective-permute-start.12) | collective-permute-done | bytes 118816 | tf_op jit(solution)/shard_map/ppermute | solution.py:307
  41.4 1.4 %collective-permute-done.15.refs_5_.refs_6_ = bf16[16,3712]{1,0:T(8,128)(2,1)S(1)} collective-permute-done((bf16[16,3712]{1,0:T(8,128)(2,1)S(1)}, bf16[16,3712]{1,0:T(8,128)(2,1)S(1)}, u32[]{:S(2)}, u32[]{:S(2)}) %collective-permute-start.15) | collective-permute-done | bytes 118816 | tf_op jit(solution)/shard_map/ppermute | solution.py:307
  43.3 1.3 %collective-permute-start.16 = (bf16[32,3584]{1,0:T(8,128)(2,1)S(1)}, bf16[32,3584]{1,0:T(8,128)(2,1)S(1)}, u32[]{:S(2)}, u32[]{:S(2)}) collective-permute-start(bf16[32,3584]{1,0:T(8,128)(2,1)S(1)} %combine.2), channel_id=1, source_target_pairs={{0,20},{1,21},{2,22},{3,23},{4,28},{5,29},{6,30},{7,31},{8,16},{9,... | collective-permute-start | bytes 688136 | tf_op jit(solution)/shard_map/ppermute | solution.py:307
  44.6 3.5 %collective-permute-start.10 = (bf16[16,3712]{1,0:T(8,128)(2,1)S(1)}, bf16[16,3712]{1,0:T(8,128)(2,1)S(1)}, u32[]{:S(2)}, u32[]{:S(2)}) collective-permute-start(bf16[16,3712]{1,0:T(8,128)(2,1)S(1)} %get-tuple-element.49), channel_id=1, source_target_pairs={{0,26},{1,27},{2,24},{3,25},{4,18},{5,19},{6,16},{7,17},{8,30},{9,... | collective-permute-start | bytes 356360 | tf_op jit(solution)/shard_map/ppermute | solution.py:307
  48.1 6.7 %collective-permute-done.10.refs_1_ = bf16[16,3712]{1,0:T(8,128)(2,1)S(1)} collective-permute-done((bf16[16,3712]{1,0:T(8,128)(2,1)S(1)}, bf16[16,3712]{1,0:T(8,128)(2,1)S(1)}, u32[]{:S(2)}, u32[]{:S(2)}) %collective-permute-start.10) | collective-permute-done | bytes 118816 | tf_op jit(solution)/shard_map/ppermute | solution.py:307
  54.8 1.6 %collective-permute-done.9.refs_0_ = bf16[16,3712]{1,0:T(8,128)(2,1)S(1)} collective-permute-done((bf16[16,3712]{1,0:T(8,128)(2,1)S(1)}, bf16[16,3712]{1,0:T(8,128)(2,1)S(1)}, u32[]{:S(2)}, u32[]{:S(2)}) %collective-permute-start.9) | collective-permute-done | bytes 118816 | tf_op jit(solution)/shard_map/ppermute | solution.py:307
  56.4 1.1 %combine.3 = bf16[32,3584]{1,0:T(8,128)(2,1)} custom-call(bf16[16,3712]{1,0:T(8,128)(2,1)S(1)} %collective-permute-done.9.refs_0_, bf16[16,3712]{1,0:T(8,128)(2,1)S(1)} %collective-permute-done.10.refs_1_, bf16[16,3712]{1,0:T(8,128)(2,1)S(1)} %collective-permute-done.11.refs_1_.refs_2_, bf16[16,3712]{1,0:T(8,128)(2,1)S(1)} %collective-permute-done.12.refs_2_.refs_3_, ...), custom_call_target="tpu_custom_call" | custom-call | tf_op jit(solution)/shard_map/combine/pallas_call | solution.py:84
  (23 shorter events, 4.3 us)
Async XLA Ops:
  0.0 28.6 %collective-permute-start.7 = (bf16[3584,1024]{1,0:T(8,128)(2,1)}, bf16[3584,1024]{1,0:T(8,128)(2,1)S(1)}, u32[]{:S(2)}, u32[]{:S(2)}) collective-permute-start(bf16[3584,1024]{1,0:T(8,128)(2,1)} %bitcast.10), channel_id=1, source_target_pairs={{0,1},{1,0},{2,3},{3,2},{4,5},{5,4},{6,7},{7,6},{8,9},{9,8},{10,11... | collective-permute-start | bytes 22020104 | tf_op jit(solution)/shard_map/ppermute | solution.py:329
  0.5 28.1 %collective-permute-start.8 = (bf16[512,3584]{1,0:T(8,128)(2,1)}, bf16[512,3584]{1,0:T(8,128)(2,1)S(1)}, u32[]{:S(2)}, u32[]{:S(2)}) collective-permute-start(bf16[512,3584]{1,0:T(8,128)(2,1)} %bitcast.12), channel_id=1, source_target_pairs={{0,1},{1,0},{2,3},{3,2},{4,5},{5,4},{6,7},{7,6},{8,9},{9,8},{10,11... | collective-permute-start | bytes 11010056 | tf_op jit(solution)/shard_map/ppermute | solution.py:328
  1.5 10.5 %collective-permute-start.1 = (bf16[32,3712]{1,0:T(8,128)(2,1)S(1)}, bf16[32,3712]{1,0:T(8,128)(2,1)S(1)}, u32[]{:S(2)}, u32[]{:S(2)}) collective-permute-start(bf16[32,3712]{1,0:T(8,128)(2,1)S(1)} %prepare.1.block), channel_id=1, source_target_pairs={{0,4},{1,5},{2,6},{3,7},{4,12},{5,13},{6,14},{7,15},{8,0},{9,1},{1... | collective-permute-start | bytes 712712 | tf_op jit(solution)/shard_map/ppermute | solution.py:307
  5.0 7.0 %collective-permute-start = (bf16[16,3712]{1,0:T(8,128)(2,1)S(1)}, bf16[16,3712]{1,0:T(8,128)(2,1)S(1)}, u32[]{:S(2)}, u32[]{:S(2)}) collective-permute-start(bf16[16,3712]{1,0:T(8,128)(2,1)S(1)} %get-tuple-element.34), channel_id=1, source_target_pairs={{0,2},{1,3},{2,0},{3,1},{4,6},{5,7},{6,4},{7,5},{8,10},{9,11},{10,... | collective-permute-start | bytes 356360 | tf_op jit(solution)/shard_map/ppermute | solution.py:307
  6.6 3.1 %copy-start = (bf16[1,3584,1024]{2,1,0:T(8,128)(2,1)S(1)}, bf16[1,3584,1024]{2,1,0:T(8,128)(2,1)}, u32[]{:S(2)}) copy-start(bf16[1,3584,1024]{2,1,0:T(8,128)(2,1)} %param.8) | copy-start | bytes 22020100
  9.7 2.0 %copy-start.1 = (bf16[1,512,3584]{2,1,0:T(8,128)(2,1)S(1)}, bf16[1,512,3584]{2,1,0:T(8,128)(2,1)}, u32[]{:S(2)}) copy-start(bf16[1,512,3584]{2,1,0:T(8,128)(2,1)} %param.9) | copy-start | bytes 11010052
  12.4 5.3 %collective-permute-start.4 = (bf16[16,3712]{1,0:T(8,128)(2,1)S(1)}, bf16[16,3712]{1,0:T(8,128)(2,1)S(1)}, u32[]{:S(2)}, u32[]{:S(2)}) collective-permute-start(bf16[16,3712]{1,0:T(8,128)(2,1)S(1)} %get-tuple-element.41), channel_id=1, source_target_pairs={{0,2},{1,3},{2,0},{3,1},{4,6},{5,7},{6,4},{7,5},{8,10},{9,11},{10,... | collective-permute-start | bytes 356360 | tf_op jit(solution)/shard_map/ppermute | solution.py:307
  13.6 6.2 %collective-permute-start.2 = (bf16[16,3712]{1,0:T(8,128)(2,1)S(1)}, bf16[16,3712]{1,0:T(8,128)(2,1)S(1)}, u32[]{:S(2)}, u32[]{:S(2)}) collective-permute-start(bf16[16,3712]{1,0:T(8,128)(2,1)S(1)} %get-tuple-element.39), channel_id=1, source_target_pairs={{0,4},{1,5},{2,6},{3,7},{4,12},{5,13},{6,14},{7,15},{8,0},{9,1},{1... | collective-permute-start | bytes 356360 | tf_op jit(solution)/shard_map/ppermute | solution.py:307
  15.6 10.6 %collective-permute-start.3 = (bf16[16,3712]{1,0:T(8,128)(2,1)S(1)}, bf16[16,3712]{1,0:T(8,128)(2,1)S(1)}, u32[]{:S(2)}, u32[]{:S(2)}) collective-permute-start(bf16[16,3712]{1,0:T(8,128)(2,1)S(1)} %get-tuple-element.40), channel_id=1, source_target_pairs={{0,6},{1,7},{2,4},{3,5},{4,14},{5,15},{6,12},{7,13},{8,2},{9,3},{1... | collective-permute-start | bytes 356360 | tf_op jit(solution)/shard_map/ppermute | solution.py:307
  17.7 8.5 %collective-permute-start.5 = (bf16[16,3712]{1,0:T(8,128)(2,1)S(1)}, bf16[16,3712]{1,0:T(8,128)(2,1)S(1)}, u32[]{:S(2)}, u32[]{:S(2)}) collective-permute-start(bf16[16,3712]{1,0:T(8,128)(2,1)S(1)} %get-tuple-element.44), channel_id=1, source_target_pairs={{0,10},{1,11},{2,8},{3,9},{4,2},{5,3},{6,0},{7,1},{8,14},{9,15},{1... | collective-permute-start | bytes 356360 | tf_op jit(solution)/shard_map/ppermute | solution.py:307
  19.8 7.0 %collective-permute-start.6 = (bf16[16,3712]{1,0:T(8,128)(2,1)S(1)}, bf16[16,3712]{1,0:T(8,128)(2,1)S(1)}, u32[]{:S(2)}, u32[]{:S(2)}) collective-permute-start(bf16[16,3712]{1,0:T(8,128)(2,1)S(1)} %get-tuple-element.45), channel_id=1, source_target_pairs={{0,8},{1,9},{2,10},{3,11},{4,0},{5,1},{6,2},{7,3},{8,12},{9,13},{1... | collective-permute-start | bytes 356360 | tf_op jit(solution)/shard_map/ppermute | solution.py:307
  30.6 7.9 %collective-permute-start.11 = (bf16[16,3712]{1,0:T(8,128)(2,1)S(1)}, bf16[16,3712]{1,0:T(8,128)(2,1)S(1)}, u32[]{:S(2)}, u32[]{:S(2)}) collective-permute-start(bf16[16,3712]{1,0:T(8,128)(2,1)S(1)} %get-tuple-element.50), channel_id=1, source_target_pairs={{0,6},{1,17},{2,4},{3,19},{4,14},{5,21},{6,12},{7,23},{8,2},{9,25}... | collective-permute-start | bytes 356360 | tf_op jit(solution)/shard_map/ppermute | solution.py:307
  32.2 9.2 %collective-permute-start.12 = (bf16[16,3712]{1,0:T(8,128)(2,1)S(1)}, bf16[16,3712]{1,0:T(8,128)(2,1)S(1)}, u32[]{:S(2)}, u32[]{:S(2)}) collective-permute-start(bf16[16,3712]{1,0:T(8,128)(2,1)S(1)} %get-tuple-element.51), channel_id=1, source_target_pairs={{0,2},{1,19},{2,0},{3,17},{4,6},{5,23},{6,4},{7,21},{8,10},{9,27},... | collective-permute-start | bytes 356360 | tf_op jit(solution)/shard_map/ppermute | solution.py:307
  33.1 8.3 %collective-permute-start.13 = (bf16[16,3712]{1,0:T(8,128)(2,1)S(1)}, bf16[16,3712]{1,0:T(8,128)(2,1)S(1)}, u32[]{:S(2)}, u32[]{:S(2)}) collective-permute-start(bf16[16,3712]{1,0:T(8,128)(2,1)S(1)} %get-tuple-element.52), channel_id=1, source_target_pairs={{0,4},{1,7},{2,6},{3,5},{4,12},{5,15},{6,14},{7,13},{8,0},{9,3},{1... | collective-permute-start | bytes 356360 | tf_op jit(solution)/shard_map/ppermute | solution.py:307
  35.6 5.8 %collective-permute-start.14 = (bf16[16,3712]{1,0:T(8,128)(2,1)S(1)}, bf16[16,3712]{1,0:T(8,128)(2,1)S(1)}, u32[]{:S(2)}, u32[]{:S(2)}) collective-permute-start(bf16[16,3712]{1,0:T(8,128)(2,1)S(1)} %get-tuple-element.53), channel_id=1, source_target_pairs={{0,16},{1,3},{2,18},{3,1},{4,20},{5,7},{6,22},{7,5},{8,24},{9,11},... | collective-permute-start | bytes 356360 | tf_op jit(solution)/shard_map/ppermute | solution.py:307
  37.1 5.7 %collective-permute-start.15 = (bf16[16,3712]{1,0:T(8,128)(2,1)S(1)}, bf16[16,3712]{1,0:T(8,128)(2,1)S(1)}, u32[]{:S(2)}, u32[]{:S(2)}) collective-permute-start(bf16[16,3712]{1,0:T(8,128)(2,1)S(1)} %get-tuple-element.54), channel_id=1, source_target_pairs={{0,18},{1,5},{2,16},{3,7},{4,22},{5,13},{6,20},{7,15},{8,26},{9,1}... | collective-permute-start | bytes 356360 | tf_op jit(solution)/shard_map/ppermute | solution.py:307
  43.3 13.1 %collective-permute-start.16 = (bf16[32,3584]{1,0:T(8,128)(2,1)S(1)}, bf16[32,3584]{1,0:T(8,128)(2,1)S(1)}, u32[]{:S(2)}, u32[]{:S(2)}) collective-permute-start(bf16[32,3584]{1,0:T(8,128)(2,1)S(1)} %combine.2), channel_id=1, source_target_pairs={{0,20},{1,21},{2,22},{3,23},{4,28},{5,29},{6,30},{7,31},{8,16},{9,... | collective-permute-start | bytes 688136 | tf_op jit(solution)/shard_map/ppermute | solution.py:307
  44.6 10.2 %collective-permute-start.10 = (bf16[16,3712]{1,0:T(8,128)(2,1)S(1)}, bf16[16,3712]{1,0:T(8,128)(2,1)S(1)}, u32[]{:S(2)}, u32[]{:S(2)}) collective-permute-start(bf16[16,3712]{1,0:T(8,128)(2,1)S(1)} %get-tuple-element.49), channel_id=1, source_target_pairs={{0,26},{1,27},{2,24},{3,25},{4,18},{5,19},{6,16},{7,17},{8,30},{9,... | collective-permute-start | bytes 356360 | tf_op jit(solution)/shard_map/ppermute | solution.py:307
  48.1 8.3 %collective-permute-start.9 = (bf16[16,3712]{1,0:T(8,128)(2,1)S(1)}, bf16[16,3712]{1,0:T(8,128)(2,1)S(1)}, u32[]{:S(2)}, u32[]{:S(2)}) collective-permute-start(bf16[16,3712]{1,0:T(8,128)(2,1)S(1)} %get-tuple-element.48), channel_id=1, source_target_pairs={{0,24},{1,25},{2,26},{3,27},{4,16},{5,17},{6,18},{7,19},{8,28},{9,... | collective-permute-start | bytes 356360 | tf_op jit(solution)/shard_map/ppermute | solution.py:307

commit v20 on v10

--- a/solution.py
+++ b/solution.py
@@ -332,9 +332,8 @@
     other1 = sent(other, sections, 0, 0, 1)
     own2 = sent(on0, sections, 0, 1, 0)
     other2 = sent(on1, sections, 0, 1, 1)
-    back0, back1 = after((back0, back1), other1)
-    own3 = sent(back0, sections, 0, 3, 0)
-    other3 = sent(back1, sections, 0, 3, 1)
+    other3 = sent(after(back1, (near, other0)), sections, 0, 3, 1)
+    own3 = sent(after(back0, (other1, other3)), sections, 0, 3, 0)
     pieces = (own0, other0, own1, own2, other2, other1, own3, other3)
     places = ((0, 0), (0, 1), (1, 0), (2, 0), (2, 1), (1, 1), (3, 0), (3, 1))
     slots, total = near_pass(pieces, near)

time: 56.6 us -> 54.9 us (0.970)
  starting transfers between devices: 26.7 us -> 25.8 us
  waiting for transfers between devices: 17.3 us -> 16.6 us
    ppermute x15, starting transfers between devices: 26.2 us -> 25.3 us  [sent(): return lax.ppermute(shard, ('section', 'expert'), pairs)]
    ppermute x15, waiting for transfers between devices: 17.3 us -> 16.6 us  [sent(): return lax.ppermute(shard, ('section', 'expert'), pairs)]
  transfers between devices with their start and end apart: 17 -> 17, of which waited for: 9 -> 10; matrix products, arithmetic and copies ran while one was open for 0% -> 0% of each run, Pallas kernels for 8% -> 8%
where the time goes in v20:
time: 54.9 us; the launch traced here: 54.7 us
  starting transfers between devices  25.8 us (47%)
  waiting for transfers between devices  16.6 us (30%)
  Pallas kernels  7.58 us (14%)
  local copies, waits for them, and re-layouts  4.62 us (8%)
    ppermute x15, starting transfers between devices, sent(): return lax.ppermute(shard, ('section', 'expert'), pairs)  25.3 us
    ppermute x15, waiting for transfers between devices, sent(): return lax.ppermute(shard, ('section', 'expert'), pairs)  16.6 us
    pallas_call x9, Pallas kernels, local_call(): pl.pallas_call(kernel, out_shape=out_shape, in_specs=[vmem if spec is Non...  7.58 us
    unnamed x4, local copies, waits for them, and re-layouts  4.62 us
  transfers between devices with their start and end apart: 17, of which 10 were waited for; matrix products, arithmetic and copies ran while one was open for 0% of the time, Pallas kernels for 8%

profile of v20, /device:TPU:0, one launch (start us, length us, event | category | flops | bytes accessed | tf_op | source)
XLA Modules:
  0.0 54.7 jit_solution(16457342192095628820)
XLA Ops:
  0.5 1.0 %prepare.1.block = bf16[32,3712]{1,0:T(8,128)(2,1)S(1)} custom-call(s32[2,32]{1,0:T(2,128)} %bitcast.15, f32[2,32]{1,0:T(2,128)} %bitcast.16, bf16[32,3584]{1,0:T(8,128)(2,1)} %bitcast.14), custom_call_target="tpu_custom_call" | custom-call | tf_op jit(solution)/shard_map/prepare/pallas_call | solution.py:84
  1.5 3.1 %collective-permute-start.1 = (bf16[32,3712]{1,0:T(8,128)(2,1)S(1)}, bf16[32,3712]{1,0:T(8,128)(2,1)S(1)}, u32[]{:S(2)}, u32[]{:S(2)}) collective-permute-start(bf16[32,3712]{1,0:T(8,128)(2,1)S(1)} %prepare.1.block), channel_id=1, source_target_pairs={{0,4},{1,5},{2,6},{3,7},{4,12},{5,13},{6,14},{7,15},{8,0},{9,1},{1... | collective-permute-start | bytes 712712 | tf_op jit(solution)/shard_map/ppermute | solution.py:306
  5.0 1.6 %collective-permute-start = (bf16[16,3712]{1,0:T(8,128)(2,1)S(1)}, bf16[16,3712]{1,0:T(8,128)(2,1)S(1)}, u32[]{:S(2)}, u32[]{:S(2)}) collective-permute-start(bf16[16,3712]{1,0:T(8,128)(2,1)S(1)} %get-tuple-element.35), channel_id=1, source_target_pairs={{0,2},{1,3},{2,0},{3,1},{4,6},{5,7},{6,4},{7,5},{8,10},{9,11},{10,... | collective-permute-start | bytes 356360 | tf_op jit(solution)/shard_map/ppermute | solution.py:306
  6.6 3.1 %copy-done = bf16[1,3584,1024]{2,1,0:T(8,128)(2,1)S(1)} copy-done((bf16[1,3584,1024]{2,1,0:T(8,128)(2,1)S(1)}, bf16[1,3584,1024]{2,1,0:T(8,128)(2,1)}, u32[]{:S(2)}) %copy-start) | copy-done | bytes 7340056
  10.2 1.5 %copy-done.1 = bf16[1,512,3584]{2,1,0:T(8,128)(2,1)S(1)} copy-done((bf16[1,512,3584]{2,1,0:T(8,128)(2,1)S(1)}, bf16[1,512,3584]{2,1,0:T(8,128)(2,1)}, u32[]{:S(2)}) %copy-start.1) | copy-done | bytes 3670040
  12.0 1.0 %collective-permute-start.5 = (bf16[16,3712]{1,0:T(8,128)(2,1)S(1)}, bf16[16,3712]{1,0:T(8,128)(2,1)S(1)}, u32[]{:S(2)}, u32[]{:S(2)}) collective-permute-start(bf16[16,3712]{1,0:T(8,128)(2,1)S(1)} %get-tuple-element.45), channel_id=1, source_target_pairs={{0,10},{1,11},{2,8},{3,9},{4,2},{5,3},{6,0},{7,1},{8,14},{9,15},{1... | collective-permute-start | bytes 356360 | tf_op jit(solution)/shard_map/ppermute | solution.py:306
  13.5 1.9 %collective-permute-start.4 = (bf16[16,3712]{1,0:T(8,128)(2,1)S(1)}, bf16[16,3712]{1,0:T(8,128)(2,1)S(1)}, u32[]{:S(2)}, u32[]{:S(2)}) collective-permute-start(bf16[16,3712]{1,0:T(8,128)(2,1)S(1)} %get-tuple-element.42), channel_id=1, source_target_pairs={{0,2},{1,3},{2,0},{3,1},{4,6},{5,7},{6,4},{7,5},{8,10},{9,11},{10,... | collective-permute-start | bytes 356360 | tf_op jit(solution)/shard_map/ppermute | solution.py:306
  16.0 2.2 %collective-permute-done.5.refs_7_ = bf16[16,3712]{1,0:T(8,128)(2,1)S(1)} collective-permute-done((bf16[16,3712]{1,0:T(8,128)(2,1)S(1)}, bf16[16,3712]{1,0:T(8,128)(2,1)S(1)}, u32[]{:S(2)}, u32[]{:S(2)}) %collective-permute-start.5) | collective-permute-done | bytes 118816 | tf_op jit(solution)/shard_map/ppermute | solution.py:306
  18.2 4.1 %collective-permute-start.3 = (bf16[16,3712]{1,0:T(8,128)(2,1)S(1)}, bf16[16,3712]{1,0:T(8,128)(2,1)S(1)}, u32[]{:S(2)}, u32[]{:S(2)}) collective-permute-start(bf16[16,3712]{1,0:T(8,128)(2,1)S(1)} %get-tuple-element.41), channel_id=1, source_target_pairs={{0,6},{1,7},{2,4},{3,5},{4,14},{5,15},{6,12},{7,13},{8,2},{9,3},{1... | collective-permute-start | bytes 356360 | tf_op jit(solution)/shard_map/ppermute | solution.py:306
  23.0 3.6 %collective-permute-done.3.refs_4_ = bf16[16,3712]{1,0:T(8,128)(2,1)S(1)} collective-permute-done((bf16[16,3712]{1,0:T(8,128)(2,1)S(1)}, bf16[16,3712]{1,0:T(8,128)(2,1)S(1)}, u32[]{:S(2)}, u32[]{:S(2)}) %collective-permute-start.3) | collective-permute-done | bytes 118816 | tf_op jit(solution)/shard_map/ppermute | solution.py:306
  27.1 1.7 %near_pass.1 = (bf16[128,3712]{1,0:T(8,128)(2,1)S(1)}, f32[128,3584]{1,0:T(8,128)S(1)}) custom-call(bf16[16,3712]{1,0:T(8,128)(2,1)S(1)} %get-tuple-element.34.refs_0_, bf16[16,3712]{1,0:T(8,128)(2,1)S(1)} %collective-permute-done.refs_1_, bf16[16,3712]{1,0:T(8,128)(2,1)S(1)} %get-tuple-element.39.refs_2_, ...), custom_call_target="tpu_custom_call" | custom-call | bytes 11010048 | tf_op jit(solution)/shard_map/near_pass/pallas_call | solution.py:84
  28.9 1.7 %far_pass.1 = (bf16[16,3712]{1,0:T(8,128)(2,1)S(1)}, bf16[16,3712]{1,0:T(8,128)(2,1)S(1)}, bf16[16,3712]{1,0:T(8,128)(2,1)S(1)}, bf16[16,3712]{1,0:T(8,128)(2,1)...) custom-call(bf16[128,3712]{1,0:T(8,128)(2,1)S(1)} %get-tuple-element, ...), custom_call_target="tpu_custom_call" | custom-call | bytes 11010048 | tf_op jit(solution)/shard_map/far_pass/pallas_call | solution.py:84
  30.6 1.6 %collective-permute-start.10 = (bf16[16,3712]{1,0:T(8,128)(2,1)S(1)}, bf16[16,3712]{1,0:T(8,128)(2,1)S(1)}, u32[]{:S(2)}, u32[]{:S(2)}) collective-permute-start(bf16[16,3712]{1,0:T(8,128)(2,1)S(1)} %get-tuple-element.51), channel_id=1, source_target_pairs={{0,6},{1,7},{2,4},{3,5},{4,14},{5,15},{6,12},{7,13},{8,2},{9,3},{1... | collective-permute-start | bytes 356360 | tf_op jit(solution)/shard_map/ppermute | solution.py:306
  32.3 1.1 %collective-permute-start.11 = (bf16[16,3712]{1,0:T(8,128)(2,1)S(1)}, bf16[16,3712]{1,0:T(8,128)(2,1)S(1)}, u32[]{:S(2)}, u32[]{:S(2)}) collective-permute-start(bf16[16,3712]{1,0:T(8,128)(2,1)S(1)} %get-tuple-element.52), channel_id=1, source_target_pairs={{0,2},{1,3},{2,0},{3,1},{4,6},{5,7},{6,4},{7,5},{8,10},{9,11},{10,... | collective-permute-start | bytes 356360 | tf_op jit(solution)/shard_map/ppermute | solution.py:306
  33.4 1.5 %collective-permute-start.12 = (bf16[16,3712]{1,0:T(8,128)(2,1)S(1)}, bf16[16,3712]{1,0:T(8,128)(2,1)S(1)}, u32[]{:S(2)}, u32[]{:S(2)}) collective-permute-start(bf16[16,3712]{1,0:T(8,128)(2,1)S(1)} %get-tuple-element.53), channel_id=1, source_target_pairs={{0,16},{1,17},{2,18},{3,19},{4,20},{5,21},{6,22},{7,23},{8,24},{9,... | collective-permute-start | bytes 356360 | tf_op jit(solution)/shard_map/ppermute | solution.py:306
  35.7 1.9 %collective-permute-start.9 = (bf16[16,3712]{1,0:T(8,128)(2,1)S(1)}, bf16[16,3712]{1,0:T(8,128)(2,1)S(1)}, u32[]{:S(2)}, u32[]{:S(2)}) collective-permute-start(bf16[16,3712]{1,0:T(8,128)(2,1)S(1)} %get-tuple-element.50), channel_id=1, source_target_pairs={{0,4},{1,5},{2,6},{3,7},{4,12},{5,13},{6,14},{7,15},{8,0},{9,1},{1... | collective-permute-start | bytes 356360 | tf_op jit(solution)/shard_map/ppermute | solution.py:306
  38.0 1.4 %collective-permute-done.11.refs_3_ = bf16[16,3712]{1,0:T(8,128)(2,1)S(1)} collective-permute-done((bf16[16,3712]{1,0:T(8,128)(2,1)S(1)}, bf16[16,3712]{1,0:T(8,128)(2,1)S(1)}, u32[]{:S(2)}, u32[]{:S(2)}) %collective-permute-start.11) | collective-permute-done | bytes 118816 | tf_op jit(solution)/shard_map/ppermute | solution.py:306
  39.4 1.2 %collective-permute-done.13.refs_1_ = bf16[16,3712]{1,0:T(8,128)(2,1)S(1)} collective-permute-done((bf16[16,3712]{1,0:T(8,128)(2,1)S(1)}, bf16[16,3712]{1,0:T(8,128)(2,1)S(1)}, u32[]{:S(2)}, u32[]{:S(2)}) %collective-permute-start.13) | collective-permute-done | bytes 118816 | tf_op jit(solution)/shard_map/ppermute | solution.py:306
  41.9 2.1 %collective-permute-start.16 = (bf16[32,3584]{1,0:T(8,128)(2,1)S(1)}, bf16[32,3584]{1,0:T(8,128)(2,1)S(1)}, u32[]{:S(2)}, u32[]{:S(2)}) collective-permute-start(bf16[32,3584]{1,0:T(8,128)(2,1)S(1)} %combine.2), channel_id=1, source_target_pairs={{0,20},{1,21},{2,22},{3,23},{4,28},{5,29},{6,30},{7,31},{8,16},{9,... | collective-permute-start | bytes 688136 | tf_op jit(solution)/shard_map/ppermute | solution.py:306
  44.1 1.7 %collective-permute-start.14 = (bf16[16,3712]{1,0:T(8,128)(2,1)S(1)}, bf16[16,3712]{1,0:T(8,128)(2,1)S(1)}, u32[]{:S(2)}, u32[]{:S(2)}) collective-permute-start(bf16[16,3712]{1,0:T(8,128)(2,1)S(1)} %get-tuple-element.57), channel_id=1, source_target_pairs={{0,24},{1,25},{2,26},{3,27},{4,16},{5,17},{6,18},{7,19},{8,28},{9,... | collective-permute-start | bytes 356360 | tf_op jit(solution)/shard_map/ppermute | solution.py:306
  45.8 1.7 %collective-permute-start.15 = (bf16[16,3712]{1,0:T(8,128)(2,1)S(1)}, bf16[16,3712]{1,0:T(8,128)(2,1)S(1)}, u32[]{:S(2)}, u32[]{:S(2)}) collective-permute-start(bf16[16,3712]{1,0:T(8,128)(2,1)S(1)} %get-tuple-element.58), channel_id=1, source_target_pairs={{0,26},{1,27},{2,24},{3,25},{4,18},{5,19},{6,16},{7,17},{8,30},{9,... | collective-permute-start | bytes 356360 | tf_op jit(solution)/shard_map/ppermute | solution.py:306
  47.5 4.5 %collective-permute-done.14.refs_2_ = bf16[16,3712]{1,0:T(8,128)(2,1)S(1)} collective-permute-done((bf16[16,3712]{1,0:T(8,128)(2,1)S(1)}, bf16[16,3712]{1,0:T(8,128)(2,1)S(1)}, u32[]{:S(2)}, u32[]{:S(2)}) %collective-permute-start.14) | collective-permute-done | bytes 118816 | tf_op jit(solution)/shard_map/ppermute | solution.py:306
  52.1 1.5 %collective-permute-done.15.refs_3_ = bf16[16,3712]{1,0:T(8,128)(2,1)S(1)} collective-permute-done((bf16[16,3712]{1,0:T(8,128)(2,1)S(1)}, bf16[16,3712]{1,0:T(8,128)(2,1)S(1)}, u32[]{:S(2)}, u32[]{:S(2)}) %collective-permute-start.15) | collective-permute-done | bytes 118816 | tf_op jit(solution)/shard_map/ppermute | solution.py:306
  53.6 1.1 %combine.3 = bf16[32,3584]{1,0:T(8,128)(2,1)} custom-call(bf16[16,3712]{1,0:T(8,128)(2,1)S(1)} %collective-permute-done.12.refs_0_, bf16[16,3712]{1,0:T(8,128)(2,1)S(1)} %collective-permute-done.13.refs_1_, bf16[16,3712]{1,0:T(8,128)(2,1)S(1)} %collective-permute-done.14.refs_2_, bf16[16,3712]{1,0:T(8,128)(2,1)S(1)} %collective-permute-done.15.refs_3_, ...), custom_call_target="tpu_custom_call" | custom-call | tf_op jit(solution)/shard_map/combine/pallas_call | solution.py:84
  (23 shorter events, 6.6 us)
Async XLA Ops:
  0.0 28.9 %collective-permute-start.7 = (bf16[3584,1024]{1,0:T(8,128)(2,1)}, bf16[3584,1024]{1,0:T(8,128)(2,1)S(1)}, u32[]{:S(2)}, u32[]{:S(2)}) collective-permute-start(bf16[3584,1024]{1,0:T(8,128)(2,1)} %bitcast.10), channel_id=1, source_target_pairs={{0,1},{1,0},{2,3},{3,2},{4,5},{5,4},{6,7},{7,6},{8,9},{9,8},{10,11... | collective-permute-start | bytes 22020104 | tf_op jit(solution)/shard_map/ppermute | solution.py:324
  0.5 28.4 %collective-permute-start.8 = (bf16[512,3584]{1,0:T(8,128)(2,1)}, bf16[512,3584]{1,0:T(8,128)(2,1)S(1)}, u32[]{:S(2)}, u32[]{:S(2)}) collective-permute-start(bf16[512,3584]{1,0:T(8,128)(2,1)} %bitcast.12), channel_id=1, source_target_pairs={{0,1},{1,0},{2,3},{3,2},{4,5},{5,4},{6,7},{7,6},{8,9},{9,8},{10,11... | collective-permute-start | bytes 11010056 | tf_op jit(solution)/shard_map/ppermute | solution.py:323
  1.5 11.5 %collective-permute-start.1 = (bf16[32,3712]{1,0:T(8,128)(2,1)S(1)}, bf16[32,3712]{1,0:T(8,128)(2,1)S(1)}, u32[]{:S(2)}, u32[]{:S(2)}) collective-permute-start(bf16[32,3712]{1,0:T(8,128)(2,1)S(1)} %prepare.1.block), channel_id=1, source_target_pairs={{0,4},{1,5},{2,6},{3,7},{4,12},{5,13},{6,14},{7,15},{8,0},{9,1},{1... | collective-permute-start | bytes 712712 | tf_op jit(solution)/shard_map/ppermute | solution.py:306
  5.0 7.0 %collective-permute-start = (bf16[16,3712]{1,0:T(8,128)(2,1)S(1)}, bf16[16,3712]{1,0:T(8,128)(2,1)S(1)}, u32[]{:S(2)}, u32[]{:S(2)}) collective-permute-start(bf16[16,3712]{1,0:T(8,128)(2,1)S(1)} %get-tuple-element.35), channel_id=1, source_target_pairs={{0,2},{1,3},{2,0},{3,1},{4,6},{5,7},{6,4},{7,5},{8,10},{9,11},{10,... | collective-permute-start | bytes 356360 | tf_op jit(solution)/shard_map/ppermute | solution.py:306
  6.6 3.1 %copy-start = (bf16[1,3584,1024]{2,1,0:T(8,128)(2,1)S(1)}, bf16[1,3584,1024]{2,1,0:T(8,128)(2,1)}, u32[]{:S(2)}) copy-start(bf16[1,3584,1024]{2,1,0:T(8,128)(2,1)} %param.8) | copy-start | bytes 22020100
  9.7 2.0 %copy-start.1 = (bf16[1,512,3584]{2,1,0:T(8,128)(2,1)S(1)}, bf16[1,512,3584]{2,1,0:T(8,128)(2,1)}, u32[]{:S(2)}) copy-start(bf16[1,512,3584]{2,1,0:T(8,128)(2,1)} %param.9) | copy-start | bytes 11010052
  12.0 6.2 %collective-permute-start.5 = (bf16[16,3712]{1,0:T(8,128)(2,1)S(1)}, bf16[16,3712]{1,0:T(8,128)(2,1)S(1)}, u32[]{:S(2)}, u32[]{:S(2)}) collective-permute-start(bf16[16,3712]{1,0:T(8,128)(2,1)S(1)} %get-tuple-element.45), channel_id=1, source_target_pairs={{0,10},{1,11},{2,8},{3,9},{4,2},{5,3},{6,0},{7,1},{8,14},{9,15},{1... | collective-permute-start | bytes 356360 | tf_op jit(solution)/shard_map/ppermute | solution.py:306
  13.5 8.9 %collective-permute-start.4 = (bf16[16,3712]{1,0:T(8,128)(2,1)S(1)}, bf16[16,3712]{1,0:T(8,128)(2,1)S(1)}, u32[]{:S(2)}, u32[]{:S(2)}) collective-permute-start(bf16[16,3712]{1,0:T(8,128)(2,1)S(1)} %get-tuple-element.42), channel_id=1, source_target_pairs={{0,2},{1,3},{2,0},{3,1},{4,6},{5,7},{6,4},{7,5},{8,10},{9,11},{10,... | collective-permute-start | bytes 356360 | tf_op jit(solution)/shard_map/ppermute | solution.py:306
  15.4 7.6 %collective-permute-start.2 = (bf16[16,3712]{1,0:T(8,128)(2,1)S(1)}, bf16[16,3712]{1,0:T(8,128)(2,1)S(1)}, u32[]{:S(2)}, u32[]{:S(2)}) collective-permute-start(bf16[16,3712]{1,0:T(8,128)(2,1)S(1)} %get-tuple-element.40), channel_id=1, source_target_pairs={{0,4},{1,5},{2,6},{3,7},{4,12},{5,13},{6,14},{7,15},{8,0},{9,1},{1... | collective-permute-start | bytes 356360 | tf_op jit(solution)/shard_map/ppermute | solution.py:306
  18.2 8.4 %collective-permute-start.3 = (bf16[16,3712]{1,0:T(8,128)(2,1)S(1)}, bf16[16,3712]{1,0:T(8,128)(2,1)S(1)}, u32[]{:S(2)}, u32[]{:S(2)}) collective-permute-start(bf16[16,3712]{1,0:T(8,128)(2,1)S(1)} %get-tuple-element.41), channel_id=1, source_target_pairs={{0,6},{1,7},{2,4},{3,5},{4,14},{5,15},{6,12},{7,13},{8,2},{9,3},{1... | collective-permute-start | bytes 356360 | tf_op jit(solution)/shard_map/ppermute | solution.py:306
  22.3 4.8 %collective-permute-start.6 = (bf16[16,3712]{1,0:T(8,128)(2,1)S(1)}, bf16[16,3712]{1,0:T(8,128)(2,1)S(1)}, u32[]{:S(2)}, u32[]{:S(2)}) collective-permute-start(bf16[16,3712]{1,0:T(8,128)(2,1)S(1)} %get-tuple-element.46), channel_id=1, source_target_pairs={{0,8},{1,9},{2,10},{3,11},{4,0},{5,1},{6,2},{7,3},{8,12},{9,13},{1... | collective-permute-start | bytes 356360 | tf_op jit(solution)/shard_map/ppermute | solution.py:306
  30.6 7.4 %collective-permute-start.10 = (bf16[16,3712]{1,0:T(8,128)(2,1)S(1)}, bf16[16,3712]{1,0:T(8,128)(2,1)S(1)}, u32[]{:S(2)}, u32[]{:S(2)}) collective-permute-start(bf16[16,3712]{1,0:T(8,128)(2,1)S(1)} %get-tuple-element.51), channel_id=1, source_target_pairs={{0,6},{1,7},{2,4},{3,5},{4,14},{5,15},{6,12},{7,13},{8,2},{9,3},{1... | collective-permute-start | bytes 356360 | tf_op jit(solution)/shard_map/ppermute | solution.py:306
  32.3 7.1 %collective-permute-start.11 = (bf16[16,3712]{1,0:T(8,128)(2,1)S(1)}, bf16[16,3712]{1,0:T(8,128)(2,1)S(1)}, u32[]{:S(2)}, u32[]{:S(2)}) collective-permute-start(bf16[16,3712]{1,0:T(8,128)(2,1)S(1)} %get-tuple-element.52), channel_id=1, source_target_pairs={{0,2},{1,3},{2,0},{3,1},{4,6},{5,7},{6,4},{7,5},{8,10},{9,11},{10,... | collective-permute-start | bytes 356360 | tf_op jit(solution)/shard_map/ppermute | solution.py:306
  33.4 6.0 %collective-permute-start.12 = (bf16[16,3712]{1,0:T(8,128)(2,1)S(1)}, bf16[16,3712]{1,0:T(8,128)(2,1)S(1)}, u32[]{:S(2)}, u32[]{:S(2)}) collective-permute-start(bf16[16,3712]{1,0:T(8,128)(2,1)S(1)} %get-tuple-element.53), channel_id=1, source_target_pairs={{0,16},{1,17},{2,18},{3,19},{4,20},{5,21},{6,22},{7,23},{8,24},{9,... | collective-permute-start | bytes 356360 | tf_op jit(solution)/shard_map/ppermute | solution.py:306
  34.9 5.7 %collective-permute-start.13 = (bf16[16,3712]{1,0:T(8,128)(2,1)S(1)}, bf16[16,3712]{1,0:T(8,128)(2,1)S(1)}, u32[]{:S(2)}, u32[]{:S(2)}) collective-permute-start(bf16[16,3712]{1,0:T(8,128)(2,1)S(1)} %get-tuple-element.54), channel_id=1, source_target_pairs={{0,18},{1,19},{2,16},{3,17},{4,22},{5,23},{6,20},{7,21},{8,26},{9,... | collective-permute-start | bytes 356360 | tf_op jit(solution)/shard_map/ppermute | solution.py:306
  35.7 5.7 %collective-permute-start.9 = (bf16[16,3712]{1,0:T(8,128)(2,1)S(1)}, bf16[16,3712]{1,0:T(8,128)(2,1)S(1)}, u32[]{:S(2)}, u32[]{:S(2)}) collective-permute-start(bf16[16,3712]{1,0:T(8,128)(2,1)S(1)} %get-tuple-element.50), channel_id=1, source_target_pairs={{0,4},{1,5},{2,6},{3,7},{4,12},{5,13},{6,14},{7,15},{8,0},{9,1},{1... | collective-permute-start | bytes 356360 | tf_op jit(solution)/shard_map/ppermute | solution.py:306
  41.9 11.7 %collective-permute-start.16 = (bf16[32,3584]{1,0:T(8,128)(2,1)S(1)}, bf16[32,3584]{1,0:T(8,128)(2,1)S(1)}, u32[]{:S(2)}, u32[]{:S(2)}) collective-permute-start(bf16[32,3584]{1,0:T(8,128)(2,1)S(1)} %combine.2), channel_id=1, source_target_pairs={{0,20},{1,21},{2,22},{3,23},{4,28},{5,29},{6,30},{7,31},{8,16},{9,... | collective-permute-start | bytes 688136 | tf_op jit(solution)/shard_map/ppermute | solution.py:306
  44.1 8.0 %collective-permute-start.14 = (bf16[16,3712]{1,0:T(8,128)(2,1)S(1)}, bf16[16,3712]{1,0:T(8,128)(2,1)S(1)}, u32[]{:S(2)}, u32[]{:S(2)}) collective-permute-start(bf16[16,3712]{1,0:T(8,128)(2,1)S(1)} %get-tuple-element.57), channel_id=1, source_target_pairs={{0,24},{1,25},{2,26},{3,27},{4,16},{5,17},{6,18},{7,19},{8,28},{9,... | collective-permute-start | bytes 356360 | tf_op jit(solution)/shard_map/ppermute | solution.py:306
  45.8 7.8 %collective-permute-start.15 = (bf16[16,3712]{1,0:T(8,128)(2,1)S(1)}, bf16[16,3712]{1,0:T(8,128)(2,1)S(1)}, u32[]{:S(2)}, u32[]{:S(2)}) collective-permute-start(bf16[16,3712]{1,0:T(8,128)(2,1)S(1)} %get-tuple-element.58), channel_id=1, source_target_pairs={{0,26},{1,27},{2,24},{3,25},{4,18},{5,19},{6,16},{7,17},{8,30},{9,... | collective-permute-start | bytes 356360 | tf_op jit(solution)/shard_map/ppermute | solution.py:306

commit v21 on v20

--- a/solution.py
+++ b/solution.py
@@ -329,11 +329,11 @@
     near = (loaded(after(w_in, own0)), loaded(after(w_out, own0)))
     block1 = after(block1, (near, other0))
     own1, other, on0, on1 = choose(block1, capacity, ((0, 0), (0, 1), (1, 0), (1, 1)))
-    other1 = sent(other, sections, 0, 0, 1)
     own2 = sent(on0, sections, 0, 1, 0)
     other2 = sent(on1, sections, 0, 1, 1)
     other3 = sent(after(back1, (near, other0)), sections, 0, 3, 1)
-    own3 = sent(after(back0, (other1, other3)), sections, 0, 3, 0)
+    other1 = sent(after(other, (other3, own2)), sections, 0, 0, 1)
+    own3 = sent(after(back0, (other3, own2)), sections, 0, 3, 0)
     pieces = (own0, other0, own1, own2, other2, other1, own3, other3)
     places = ((0, 0), (0, 1), (1, 0), (2, 0), (2, 1), (1, 1), (3, 0), (3, 1))
     slots, total = near_pass(pieces, near)

time: 54.9 us -> 56.2 us (1.024)
  starting transfers between devices: 25.8 us -> 27.4 us
    ppermute x15, starting transfers between devices: 25.3 us -> 26.9 us  [sent(): return lax.ppermute(shard, ('section', 'expert'), pairs)]
  transfers between devices with their start and end apart: 17 -> 17, of which waited for: 10 -> 9; matrix products, arithmetic and copies ran while one was open for 0% -> 0% of each run, Pallas kernels for 8% -> 8%
where the time goes in v21:
time: 56.2 us; the launch traced here: 56 us
  starting transfers between devices  27.4 us (49%)
  waiting for transfers between devices  16.3 us (29%)
  Pallas kernels  7.57 us (13%)
  local copies, waits for them, and re-layouts  4.62 us (8%)
    ppermute x15, starting transfers between devices, sent(): return lax.ppermute(shard, ('section', 'expert'), pairs)  26.9 us
    ppermute x15, waiting for transfers between devices, sent(): return lax.ppermute(shard, ('section', 'expert'), pairs)  16.3 us
    pallas_call x9, Pallas kernels, local_call(): pl.pallas_call(kernel, out_shape=out_shape, in_specs=[vmem if spec is Non...  7.57 us
    unnamed x4, local copies, waits for them, and re-layouts  4.62 us
  transfers between devices with their start and end apart: 17, of which 9 were waited for; matrix products, arithmetic and copies ran while one was open for 0% of the time, Pallas kernels for 8%

profile of v21, /device:TPU:0, one launch (start us, length us, event | category | flops | bytes accessed | tf_op | source)
XLA Modules:
  0.0 56.0 jit_solution(18344383752727012840)
XLA Ops:
  1.5 3.1 %collective-permute-start.1 = (bf16[32,3712]{1,0:T(8,128)(2,1)S(1)}, bf16[32,3712]{1,0:T(8,128)(2,1)S(1)}, u32[]{:S(2)}, u32[]{:S(2)}) collective-permute-start(bf16[32,3712]{1,0:T(8,128)(2,1)S(1)} %prepare.1.block), channel_id=1, source_target_pairs={{0,4},{1,5},{2,6},{3,7},{4,12},{5,13},{6,14},{7,15},{8,0},{9,1},{1... | collective-permute-start | bytes 712712 | tf_op jit(solution)/shard_map/ppermute | solution.py:306
  5.0 1.6 %collective-permute-start = (bf16[16,3712]{1,0:T(8,128)(2,1)S(1)}, bf16[16,3712]{1,0:T(8,128)(2,1)S(1)}, u32[]{:S(2)}, u32[]{:S(2)}) collective-permute-start(bf16[16,3712]{1,0:T(8,128)(2,1)S(1)} %get-tuple-element.36), channel_id=1, source_target_pairs={{0,2},{1,3},{2,0},{3,1},{4,6},{5,7},{6,4},{7,5},{8,10},{9,11},{10,... | collective-permute-start | bytes 356360 | tf_op jit(solution)/shard_map/ppermute | solution.py:306
  6.6 3.1 %copy-done = bf16[1,3584,1024]{2,1,0:T(8,128)(2,1)S(1)} copy-done((bf16[1,3584,1024]{2,1,0:T(8,128)(2,1)S(1)}, bf16[1,3584,1024]{2,1,0:T(8,128)(2,1)}, u32[]{:S(2)}) %copy-start) | copy-done | bytes 7340056
  10.2 1.5 %copy-done.1 = bf16[1,512,3584]{2,1,0:T(8,128)(2,1)S(1)} copy-done((bf16[1,512,3584]{2,1,0:T(8,128)(2,1)S(1)}, bf16[1,512,3584]{2,1,0:T(8,128)(2,1)}, u32[]{:S(2)}) %copy-start.1) | copy-done | bytes 3670040
  13.5 1.7 %collective-permute-start.2 = (bf16[16,3712]{1,0:T(8,128)(2,1)S(1)}, bf16[16,3712]{1,0:T(8,128)(2,1)S(1)}, u32[]{:S(2)}, u32[]{:S(2)}) collective-permute-start(bf16[16,3712]{1,0:T(8,128)(2,1)S(1)} %get-tuple-element.41), channel_id=1, source_target_pairs={{0,4},{1,5},{2,6},{3,7},{4,12},{5,13},{6,14},{7,15},{8,0},{9,1},{1... | collective-permute-start | bytes 356360 | tf_op jit(solution)/shard_map/ppermute | solution.py:306
  15.1 3.8 %collective-permute-start.3 = (bf16[16,3712]{1,0:T(8,128)(2,1)S(1)}, bf16[16,3712]{1,0:T(8,128)(2,1)S(1)}, u32[]{:S(2)}, u32[]{:S(2)}) collective-permute-start(bf16[16,3712]{1,0:T(8,128)(2,1)S(1)} %get-tuple-element.42), channel_id=1, source_target_pairs={{0,6},{1,7},{2,4},{3,5},{4,14},{5,15},{6,12},{7,13},{8,2},{9,3},{1... | collective-permute-start | bytes 356360 | tf_op jit(solution)/shard_map/ppermute | solution.py:306
  18.9 3.3 %collective-permute-done.2.refs_3_ = bf16[16,3712]{1,0:T(8,128)(2,1)S(1)} collective-permute-done((bf16[16,3712]{1,0:T(8,128)(2,1)S(1)}, bf16[16,3712]{1,0:T(8,128)(2,1)S(1)}, u32[]{:S(2)}, u32[]{:S(2)}) %collective-permute-start.2) | collective-permute-done | bytes 118816 | tf_op jit(solution)/shard_map/ppermute | solution.py:306
  22.2 1.5 %collective-permute-start.5 = (bf16[16,3712]{1,0:T(8,128)(2,1)S(1)}, bf16[16,3712]{1,0:T(8,128)(2,1)S(1)}, u32[]{:S(2)}, u32[]{:S(2)}) collective-permute-start(bf16[16,3712]{1,0:T(8,128)(2,1)S(1)} %get-tuple-element.46), channel_id=1, source_target_pairs={{0,2},{1,3},{2,0},{3,1},{4,6},{5,7},{6,4},{7,5},{8,10},{9,11},{10,... | collective-permute-start | bytes 356360 | tf_op jit(solution)/shard_map/ppermute | solution.py:306
  23.7 2.0 %collective-permute-start.6 = (bf16[16,3712]{1,0:T(8,128)(2,1)S(1)}, bf16[16,3712]{1,0:T(8,128)(2,1)S(1)}, u32[]{:S(2)}, u32[]{:S(2)}) collective-permute-start(bf16[16,3712]{1,0:T(8,128)(2,1)S(1)} %get-tuple-element.48), channel_id=1, source_target_pairs={{0,8},{1,9},{2,10},{3,11},{4,0},{5,1},{6,2},{7,3},{8,12},{9,13},{1... | collective-permute-start | bytes 356360 | tf_op jit(solution)/shard_map/ppermute | solution.py:306
  26.1 1.5 %collective-permute-done.5.refs_5_ = bf16[16,3712]{1,0:T(8,128)(2,1)S(1)} collective-permute-done((bf16[16,3712]{1,0:T(8,128)(2,1)S(1)}, bf16[16,3712]{1,0:T(8,128)(2,1)S(1)}, u32[]{:S(2)}, u32[]{:S(2)}) %collective-permute-start.5) | collective-permute-done | bytes 118816 | tf_op jit(solution)/shard_map/ppermute | solution.py:306
  28.6 1.7 %near_pass.1 = (bf16[128,3712]{1,0:T(8,128)(2,1)S(1)}, f32[128,3584]{1,0:T(8,128)S(1)}) custom-call(bf16[16,3712]{1,0:T(8,128)(2,1)S(1)} %get-tuple-element.35.refs_0_, bf16[16,3712]{1,0:T(8,128)(2,1)S(1)} %collective-permute-done.refs_1_, bf16[16,3712]{1,0:T(8,128)(2,1)S(1)} %get-tuple-element.40.refs_2_, ...), custom_call_target="tpu_custom_call" | custom-call | bytes 11010048 | tf_op jit(solution)/shard_map/near_pass/pallas_call | solution.py:84
  30.3 1.7 %far_pass.1 = (bf16[16,3712]{1,0:T(8,128)(2,1)S(1)}, bf16[16,3712]{1,0:T(8,128)(2,1)S(1)}, bf16[16,3712]{1,0:T(8,128)(2,1)S(1)}, bf16[16,3712]{1,0:T(8,128)(2,1)...) custom-call(bf16[128,3712]{1,0:T(8,128)(2,1)S(1)} %get-tuple-element, ...), custom_call_target="tpu_custom_call" | custom-call | bytes 11010048 | tf_op jit(solution)/shard_map/far_pass/pallas_call | solution.py:84
  32.1 1.4 %collective-permute-start.10 = (bf16[16,3712]{1,0:T(8,128)(2,1)S(1)}, bf16[16,3712]{1,0:T(8,128)(2,1)S(1)}, u32[]{:S(2)}, u32[]{:S(2)}) collective-permute-start(bf16[16,3712]{1,0:T(8,128)(2,1)S(1)} %get-tuple-element.53), channel_id=1, source_target_pairs={{0,6},{1,7},{2,4},{3,5},{4,14},{5,15},{6,12},{7,13},{8,2},{9,3},{1... | collective-permute-start | bytes 356360 | tf_op jit(solution)/shard_map/ppermute | solution.py:306
  34.5 1.4 %collective-permute-start.12 = (bf16[16,3712]{1,0:T(8,128)(2,1)S(1)}, bf16[16,3712]{1,0:T(8,128)(2,1)S(1)}, u32[]{:S(2)}, u32[]{:S(2)}) collective-permute-start(bf16[16,3712]{1,0:T(8,128)(2,1)S(1)} %get-tuple-element.55), channel_id=1, source_target_pairs={{0,16},{1,17},{2,18},{3,19},{4,20},{5,21},{6,22},{7,23},{8,24},{9,... | collective-permute-start | bytes 356360 | tf_op jit(solution)/shard_map/ppermute | solution.py:306
  35.9 1.1 %collective-permute-start.13 = (bf16[16,3712]{1,0:T(8,128)(2,1)S(1)}, bf16[16,3712]{1,0:T(8,128)(2,1)S(1)}, u32[]{:S(2)}, u32[]{:S(2)}) collective-permute-start(bf16[16,3712]{1,0:T(8,128)(2,1)S(1)} %get-tuple-element.56), channel_id=1, source_target_pairs={{0,18},{1,19},{2,16},{3,17},{4,22},{5,23},{6,20},{7,21},{8,26},{9,... | collective-permute-start | bytes 356360 | tf_op jit(solution)/shard_map/ppermute | solution.py:306
  38.0 1.9 %collective-permute-done.10.refs_2_ = bf16[16,3712]{1,0:T(8,128)(2,1)S(1)} collective-permute-done((bf16[16,3712]{1,0:T(8,128)(2,1)S(1)}, bf16[16,3712]{1,0:T(8,128)(2,1)S(1)}, u32[]{:S(2)}, u32[]{:S(2)}) %collective-permute-start.10) | collective-permute-done | bytes 118816 | tf_op jit(solution)/shard_map/ppermute | solution.py:306
  39.9 1.7 %collective-permute-done.13.refs_1_ = bf16[16,3712]{1,0:T(8,128)(2,1)S(1)} collective-permute-done((bf16[16,3712]{1,0:T(8,128)(2,1)S(1)}, bf16[16,3712]{1,0:T(8,128)(2,1)S(1)}, u32[]{:S(2)}, u32[]{:S(2)}) %collective-permute-start.13) | collective-permute-done | bytes 118816 | tf_op jit(solution)/shard_map/ppermute | solution.py:306
  41.6 1.1 %collective-permute-done.9.refs_1_ = bf16[16,3712]{1,0:T(8,128)(2,1)S(1)} collective-permute-done((bf16[16,3712]{1,0:T(8,128)(2,1)S(1)}, bf16[16,3712]{1,0:T(8,128)(2,1)S(1)}, u32[]{:S(2)}, u32[]{:S(2)}) %collective-permute-start.9) | collective-permute-done | bytes 118816 | tf_op jit(solution)/shard_map/ppermute | solution.py:306
  43.2 2.1 %collective-permute-start.16 = (bf16[32,3584]{1,0:T(8,128)(2,1)S(1)}, bf16[32,3584]{1,0:T(8,128)(2,1)S(1)}, u32[]{:S(2)}, u32[]{:S(2)}) collective-permute-start(bf16[32,3584]{1,0:T(8,128)(2,1)S(1)} %combine.2), channel_id=1, source_target_pairs={{0,20},{1,21},{2,22},{3,23},{4,28},{5,29},{6,30},{7,31},{8,16},{9,... | collective-permute-start | bytes 688136 | tf_op jit(solution)/shard_map/ppermute | solution.py:306
  45.2 1.8 %collective-permute-start.14 = (bf16[16,3712]{1,0:T(8,128)(2,1)S(1)}, bf16[16,3712]{1,0:T(8,128)(2,1)S(1)}, u32[]{:S(2)}, u32[]{:S(2)}) collective-permute-start(bf16[16,3712]{1,0:T(8,128)(2,1)S(1)} %get-tuple-element.59), channel_id=1, source_target_pairs={{0,24},{1,25},{2,26},{3,27},{4,16},{5,17},{6,18},{7,19},{8,28},{9,... | collective-permute-start | bytes 356360 | tf_op jit(solution)/shard_map/ppermute | solution.py:306
  47.0 2.4 %collective-permute-start.15 = (bf16[16,3712]{1,0:T(8,128)(2,1)S(1)}, bf16[16,3712]{1,0:T(8,128)(2,1)S(1)}, u32[]{:S(2)}, u32[]{:S(2)}) collective-permute-start(bf16[16,3712]{1,0:T(8,128)(2,1)S(1)} %get-tuple-element.60), channel_id=1, source_target_pairs={{0,26},{1,27},{2,24},{3,25},{4,18},{5,19},{6,16},{7,17},{8,30},{9,... | collective-permute-start | bytes 356360 | tf_op jit(solution)/shard_map/ppermute | solution.py:306
  49.5 3.4 %collective-permute-done.14.refs_2_ = bf16[16,3712]{1,0:T(8,128)(2,1)S(1)} collective-permute-done((bf16[16,3712]{1,0:T(8,128)(2,1)S(1)}, bf16[16,3712]{1,0:T(8,128)(2,1)S(1)}, u32[]{:S(2)}, u32[]{:S(2)}) %collective-permute-start.14) | collective-permute-done | bytes 118816 | tf_op jit(solution)/shard_map/ppermute | solution.py:306
  52.9 2.0 %collective-permute-done.15.refs_3_ = bf16[16,3712]{1,0:T(8,128)(2,1)S(1)} collective-permute-done((bf16[16,3712]{1,0:T(8,128)(2,1)S(1)}, bf16[16,3712]{1,0:T(8,128)(2,1)S(1)}, u32[]{:S(2)}, u32[]{:S(2)}) %collective-permute-start.15) | collective-permute-done | bytes 118816 | tf_op jit(solution)/shard_map/ppermute | solution.py:306
  54.9 1.1 %combine.3 = bf16[32,3584]{1,0:T(8,128)(2,1)} custom-call(bf16[16,3712]{1,0:T(8,128)(2,1)S(1)} %collective-permute-done.12.refs_0_, bf16[16,3712]{1,0:T(8,128)(2,1)S(1)} %collective-permute-done.13.refs_1_, bf16[16,3712]{1,0:T(8,128)(2,1)S(1)} %collective-permute-done.14.refs_2_, bf16[16,3712]{1,0:T(8,128)(2,1)S(1)} %collective-permute-done.15.refs_3_, ...), custom_call_target="tpu_custom_call" | custom-call | tf_op jit(solution)/shard_map/combine/pallas_call | solution.py:84
  (23 shorter events, 7.8 us)
Async XLA Ops:
  0.0 30.3 %collective-permute-start.7 = (bf16[3584,1024]{1,0:T(8,128)(2,1)}, bf16[3584,1024]{1,0:T(8,128)(2,1)S(1)}, u32[]{:S(2)}, u32[]{:S(2)}) collective-permute-start(bf16[3584,1024]{1,0:T(8,128)(2,1)} %bitcast.10), channel_id=1, source_target_pairs={{0,1},{1,0},{2,3},{3,2},{4,5},{5,4},{6,7},{7,6},{8,9},{9,8},{10,11... | collective-permute-start | bytes 22020104 | tf_op jit(solution)/shard_map/ppermute | solution.py:324
  0.5 29.9 %collective-permute-start.8 = (bf16[512,3584]{1,0:T(8,128)(2,1)}, bf16[512,3584]{1,0:T(8,128)(2,1)S(1)}, u32[]{:S(2)}, u32[]{:S(2)}) collective-permute-start(bf16[512,3584]{1,0:T(8,128)(2,1)} %bitcast.12), channel_id=1, source_target_pairs={{0,1},{1,0},{2,3},{3,2},{4,5},{5,4},{6,7},{7,6},{8,9},{9,8},{10,11... | collective-permute-start | bytes 11010056 | tf_op jit(solution)/shard_map/ppermute | solution.py:323
  1.5 11.5 %collective-permute-start.1 = (bf16[32,3712]{1,0:T(8,128)(2,1)S(1)}, bf16[32,3712]{1,0:T(8,128)(2,1)S(1)}, u32[]{:S(2)}, u32[]{:S(2)}) collective-permute-start(bf16[32,3712]{1,0:T(8,128)(2,1)S(1)} %prepare.1.block), channel_id=1, source_target_pairs={{0,4},{1,5},{2,6},{3,7},{4,12},{5,13},{6,14},{7,15},{8,0},{9,1},{1... | collective-permute-start | bytes 712712 | tf_op jit(solution)/shard_map/ppermute | solution.py:306
  5.0 7.0 %collective-permute-start = (bf16[16,3712]{1,0:T(8,128)(2,1)S(1)}, bf16[16,3712]{1,0:T(8,128)(2,1)S(1)}, u32[]{:S(2)}, u32[]{:S(2)}) collective-permute-start(bf16[16,3712]{1,0:T(8,128)(2,1)S(1)} %get-tuple-element.36), channel_id=1, source_target_pairs={{0,2},{1,3},{2,0},{3,1},{4,6},{5,7},{6,4},{7,5},{8,10},{9,11},{10,... | collective-permute-start | bytes 356360 | tf_op jit(solution)/shard_map/ppermute | solution.py:306
  6.6 3.1 %copy-start = (bf16[1,3584,1024]{2,1,0:T(8,128)(2,1)S(1)}, bf16[1,3584,1024]{2,1,0:T(8,128)(2,1)}, u32[]{:S(2)}) copy-start(bf16[1,3584,1024]{2,1,0:T(8,128)(2,1)} %param.8) | copy-start | bytes 22020100
  9.7 2.0 %copy-start.1 = (bf16[1,512,3584]{2,1,0:T(8,128)(2,1)S(1)}, bf16[1,512,3584]{2,1,0:T(8,128)(2,1)}, u32[]{:S(2)}) copy-start(bf16[1,512,3584]{2,1,0:T(8,128)(2,1)} %param.9) | copy-start | bytes 11010052
  12.0 6.9 %collective-permute-start.4 = (bf16[16,3712]{1,0:T(8,128)(2,1)S(1)}, bf16[16,3712]{1,0:T(8,128)(2,1)S(1)}, u32[]{:S(2)}, u32[]{:S(2)}) collective-permute-start(bf16[16,3712]{1,0:T(8,128)(2,1)S(1)} %get-tuple-element.45), channel_id=1, source_target_pairs={{0,10},{1,11},{2,8},{3,9},{4,2},{5,3},{6,0},{7,1},{8,14},{9,15},{1... | collective-permute-start | bytes 356360 | tf_op jit(solution)/shard_map/ppermute | solution.py:306
  13.5 8.8 %collective-permute-start.2 = (bf16[16,3712]{1,0:T(8,128)(2,1)S(1)}, bf16[16,3712]{1,0:T(8,128)(2,1)S(1)}, u32[]{:S(2)}, u32[]{:S(2)}) collective-permute-start(bf16[16,3712]{1,0:T(8,128)(2,1)S(1)} %get-tuple-element.41), channel_id=1, source_target_pairs={{0,4},{1,5},{2,6},{3,7},{4,12},{5,13},{6,14},{7,15},{8,0},{9,1},{1... | collective-permute-start | bytes 356360 | tf_op jit(solution)/shard_map/ppermute | solution.py:306
  15.1 10.9 %collective-permute-start.3 = (bf16[16,3712]{1,0:T(8,128)(2,1)S(1)}, bf16[16,3712]{1,0:T(8,128)(2,1)S(1)}, u32[]{:S(2)}, u32[]{:S(2)}) collective-permute-start(bf16[16,3712]{1,0:T(8,128)(2,1)S(1)} %get-tuple-element.42), channel_id=1, source_target_pairs={{0,6},{1,7},{2,4},{3,5},{4,14},{5,15},{6,12},{7,13},{8,2},{9,3},{1... | collective-permute-start | bytes 356360 | tf_op jit(solution)/shard_map/ppermute | solution.py:306
  22.2 5.4 %collective-permute-start.5 = (bf16[16,3712]{1,0:T(8,128)(2,1)S(1)}, bf16[16,3712]{1,0:T(8,128)(2,1)S(1)}, u32[]{:S(2)}, u32[]{:S(2)}) collective-permute-start(bf16[16,3712]{1,0:T(8,128)(2,1)S(1)} %get-tuple-element.46), channel_id=1, source_target_pairs={{0,2},{1,3},{2,0},{3,1},{4,6},{5,7},{6,4},{7,5},{8,10},{9,11},{10,... | collective-permute-start | bytes 356360 | tf_op jit(solution)/shard_map/ppermute | solution.py:306
  23.7 4.8 %collective-permute-start.6 = (bf16[16,3712]{1,0:T(8,128)(2,1)S(1)}, bf16[16,3712]{1,0:T(8,128)(2,1)S(1)}, u32[]{:S(2)}, u32[]{:S(2)}) collective-permute-start(bf16[16,3712]{1,0:T(8,128)(2,1)S(1)} %get-tuple-element.48), channel_id=1, source_target_pairs={{0,8},{1,9},{2,10},{3,11},{4,0},{5,1},{6,2},{7,3},{8,12},{9,13},{1... | collective-permute-start | bytes 356360 | tf_op jit(solution)/shard_map/ppermute | solution.py:306
  32.1 7.9 %collective-permute-start.10 = (bf16[16,3712]{1,0:T(8,128)(2,1)S(1)}, bf16[16,3712]{1,0:T(8,128)(2,1)S(1)}, u32[]{:S(2)}, u32[]{:S(2)}) collective-permute-start(bf16[16,3712]{1,0:T(8,128)(2,1)S(1)} %get-tuple-element.53), channel_id=1, source_target_pairs={{0,6},{1,7},{2,4},{3,5},{4,14},{5,15},{6,12},{7,13},{8,2},{9,3},{1... | collective-permute-start | bytes 356360 | tf_op jit(solution)/shard_map/ppermute | solution.py:306
  33.5 6.4 %collective-permute-start.11 = (bf16[16,3712]{1,0:T(8,128)(2,1)S(1)}, bf16[16,3712]{1,0:T(8,128)(2,1)S(1)}, u32[]{:S(2)}, u32[]{:S(2)}) collective-permute-start(bf16[16,3712]{1,0:T(8,128)(2,1)S(1)} %get-tuple-element.54), channel_id=1, source_target_pairs={{0,2},{1,3},{2,0},{3,1},{4,6},{5,7},{6,4},{7,5},{8,10},{9,11},{10,... | collective-permute-start | bytes 356360 | tf_op jit(solution)/shard_map/ppermute | solution.py:306
  34.5 5.5 %collective-permute-start.12 = (bf16[16,3712]{1,0:T(8,128)(2,1)S(1)}, bf16[16,3712]{1,0:T(8,128)(2,1)S(1)}, u32[]{:S(2)}, u32[]{:S(2)}) collective-permute-start(bf16[16,3712]{1,0:T(8,128)(2,1)S(1)} %get-tuple-element.55), channel_id=1, source_target_pairs={{0,16},{1,17},{2,18},{3,19},{4,20},{5,21},{6,22},{7,23},{8,24},{9,... | collective-permute-start | bytes 356360 | tf_op jit(solution)/shard_map/ppermute | solution.py:306
  35.9 5.7 %collective-permute-start.13 = (bf16[16,3712]{1,0:T(8,128)(2,1)S(1)}, bf16[16,3712]{1,0:T(8,128)(2,1)S(1)}, u32[]{:S(2)}, u32[]{:S(2)}) collective-permute-start(bf16[16,3712]{1,0:T(8,128)(2,1)S(1)} %get-tuple-element.56), channel_id=1, source_target_pairs={{0,18},{1,19},{2,16},{3,17},{4,22},{5,23},{6,20},{7,21},{8,26},{9,... | collective-permute-start | bytes 356360 | tf_op jit(solution)/shard_map/ppermute | solution.py:306
  37.0 5.7 %collective-permute-start.9 = (bf16[16,3712]{1,0:T(8,128)(2,1)S(1)}, bf16[16,3712]{1,0:T(8,128)(2,1)S(1)}, u32[]{:S(2)}, u32[]{:S(2)}) collective-permute-start(bf16[16,3712]{1,0:T(8,128)(2,1)S(1)} %get-tuple-element.52), channel_id=1, source_target_pairs={{0,4},{1,5},{2,6},{3,7},{4,12},{5,13},{6,14},{7,15},{8,0},{9,1},{1... | collective-permute-start | bytes 356360 | tf_op jit(solution)/shard_map/ppermute | solution.py:306
  43.2 11.7 %collective-permute-start.16 = (bf16[32,3584]{1,0:T(8,128)(2,1)S(1)}, bf16[32,3584]{1,0:T(8,128)(2,1)S(1)}, u32[]{:S(2)}, u32[]{:S(2)}) collective-permute-start(bf16[32,3584]{1,0:T(8,128)(2,1)S(1)} %combine.2), channel_id=1, source_target_pairs={{0,20},{1,21},{2,22},{3,23},{4,28},{5,29},{6,30},{7,31},{8,16},{9,... | collective-permute-start | bytes 688136 | tf_op jit(solution)/shard_map/ppermute | solution.py:306
  45.2 7.7 %collective-permute-start.14 = (bf16[16,3712]{1,0:T(8,128)(2,1)S(1)}, bf16[16,3712]{1,0:T(8,128)(2,1)S(1)}, u32[]{:S(2)}, u32[]{:S(2)}) collective-permute-start(bf16[16,3712]{1,0:T(8,128)(2,1)S(1)} %get-tuple-element.59), channel_id=1, source_target_pairs={{0,24},{1,25},{2,26},{3,27},{4,16},{5,17},{6,18},{7,19},{8,28},{9,... | collective-permute-start | bytes 356360 | tf_op jit(solution)/shard_map/ppermute | solution.py:306
  47.0 7.8 %collective-permute-start.15 = (bf16[16,3712]{1,0:T(8,128)(2,1)S(1)}, bf16[16,3712]{1,0:T(8,128)(2,1)S(1)}, u32[]{:S(2)}, u32[]{:S(2)}) collective-permute-start(bf16[16,3712]{1,0:T(8,128)(2,1)S(1)} %get-tuple-element.60), channel_id=1, source_target_pairs={{0,26},{1,27},{2,24},{3,25},{4,18},{5,19},{6,16},{7,17},{8,30},{9,... | collective-permute-start | bytes 356360 | tf_op jit(solution)/shard_map/ppermute | solution.py:306

commit v22 on v20

--- a/solution.py
+++ b/solution.py
@@ -347,7 +347,8 @@
     ]
     straight = [sent(piece[0, flip], sections, 1, 0, flip) for flip in range(2)]
     merged, straight = lax.optimization_barrier((merged, straight))
-    straight += [sent(piece[1, flip], sections, 1, -1, flip) for flip in range(2)]
+    straight.append(sent(piece[1, 0], sections, 1, -1, 0))
+    straight.append(sent(after(piece[1, 1], straight[-1]), sections, 1, -1, 1))
     merged = sent(combine(merged, tok_count), sections, 1, 1, 0)
     return combine(straight, tok_count, merged)[None]
 

time: 54.9 us -> 54.9 us (level)
  waiting for transfers between devices: 16.6 us -> 14 us
  starting transfers between devices: 25.8 us -> 28.4 us
    ppermute x15, waiting for transfers between devices: 16.6 us -> 14 us  [sent(): return lax.ppermute(shard, ('section', 'expert'), pairs)]
    ppermute x15, starting transfers between devices: 25.3 us -> 27.9 us  [sent(): return lax.ppermute(shard, ('section', 'expert'), pairs)]
  transfers between devices with their start and end apart: 17 -> 17, of which waited for: 10 -> 9; matrix products, arithmetic and copies ran while one was open for 0% -> 0% of each run, Pallas kernels for 8% -> 9%
where the time goes in v22:
time: 54.9 us; the launch traced here: 54.6 us
  starting transfers between devices  28.4 us (52%)
  waiting for transfers between devices  14 us (26%)
  Pallas kernels  7.58 us (14%)
  local copies, waits for them, and re-layouts  4.62 us (8%)
    ppermute x15, starting transfers between devices, sent(): return lax.ppermute(shard, ('section', 'expert'), pairs)  27.9 us
    ppermute x15, waiting for transfers between devices, sent(): return lax.ppermute(shard, ('section', 'expert'), pairs)  14 us
    pallas_call x9, Pallas kernels, local_call(): pl.pallas_call(kernel, out_shape=out_shape, in_specs=[vmem if spec is Non...  7.58 us
    unnamed x4, local copies, waits for them, and re-layouts  4.62 us
  transfers between devices with their start and end apart: 17, of which 9 were waited for; matrix products, arithmetic and copies ran while one was open for 0% of the time, Pallas kernels for 9%

profile of v22, /device:TPU:0, one launch (start us, length us, event | category | flops | bytes accessed | tf_op | source)
XLA Modules:
  0.0 54.6 jit_solution(12567546804084887780)
XLA Ops:
  0.5 1.0 %prepare.1.block = bf16[32,3712]{1,0:T(8,128)(2,1)S(1)} custom-call(s32[2,32]{1,0:T(2,128)} %bitcast.15, f32[2,32]{1,0:T(2,128)} %bitcast.16, bf16[32,3584]{1,0:T(8,128)(2,1)} %bitcast.14), custom_call_target="tpu_custom_call" | custom-call | tf_op jit(solution)/shard_map/prepare/pallas_call | solution.py:84
  1.5 3.1 %collective-permute-start.1 = (bf16[32,3712]{1,0:T(8,128)(2,1)S(1)}, bf16[32,3712]{1,0:T(8,128)(2,1)S(1)}, u32[]{:S(2)}, u32[]{:S(2)}) collective-permute-start(bf16[32,3712]{1,0:T(8,128)(2,1)S(1)} %prepare.1.block), channel_id=1, source_target_pairs={{0,4},{1,5},{2,6},{3,7},{4,12},{5,13},{6,14},{7,15},{8,0},{9,1},{1... | collective-permute-start | bytes 712712 | tf_op jit(solution)/shard_map/ppermute | solution.py:306
  5.0 1.6 %collective-permute-start = (bf16[16,3712]{1,0:T(8,128)(2,1)S(1)}, bf16[16,3712]{1,0:T(8,128)(2,1)S(1)}, u32[]{:S(2)}, u32[]{:S(2)}) collective-permute-start(bf16[16,3712]{1,0:T(8,128)(2,1)S(1)} %get-tuple-element.36), channel_id=1, source_target_pairs={{0,2},{1,3},{2,0},{3,1},{4,6},{5,7},{6,4},{7,5},{8,10},{9,11},{10,... | collective-permute-start | bytes 356360 | tf_op jit(solution)/shard_map/ppermute | solution.py:306
  6.6 3.1 %copy-done = bf16[1,3584,1024]{2,1,0:T(8,128)(2,1)S(1)} copy-done((bf16[1,3584,1024]{2,1,0:T(8,128)(2,1)S(1)}, bf16[1,3584,1024]{2,1,0:T(8,128)(2,1)}, u32[]{:S(2)}) %copy-start) | copy-done | bytes 7340056
  10.2 1.5 %copy-done.1 = bf16[1,512,3584]{2,1,0:T(8,128)(2,1)S(1)} copy-done((bf16[1,512,3584]{2,1,0:T(8,128)(2,1)S(1)}, bf16[1,512,3584]{2,1,0:T(8,128)(2,1)}, u32[]{:S(2)}) %copy-start.1) | copy-done | bytes 3670040
  12.0 1.0 %collective-permute-start.5 = (bf16[16,3712]{1,0:T(8,128)(2,1)S(1)}, bf16[16,3712]{1,0:T(8,128)(2,1)S(1)}, u32[]{:S(2)}, u32[]{:S(2)}) collective-permute-start(bf16[16,3712]{1,0:T(8,128)(2,1)S(1)} %get-tuple-element.46), channel_id=1, source_target_pairs={{0,10},{1,11},{2,8},{3,9},{4,2},{5,3},{6,0},{7,1},{8,14},{9,15},{1... | collective-permute-start | bytes 356360 | tf_op jit(solution)/shard_map/ppermute | solution.py:306
  13.5 1.9 %collective-permute-start.4 = (bf16[16,3712]{1,0:T(8,128)(2,1)S(1)}, bf16[16,3712]{1,0:T(8,128)(2,1)S(1)}, u32[]{:S(2)}, u32[]{:S(2)}) collective-permute-start(bf16[16,3712]{1,0:T(8,128)(2,1)S(1)} %get-tuple-element.43), channel_id=1, source_target_pairs={{0,2},{1,3},{2,0},{3,1},{4,6},{5,7},{6,4},{7,5},{8,10},{9,11},{10,... | collective-permute-start | bytes 356360 | tf_op jit(solution)/shard_map/ppermute | solution.py:306
  16.0 2.2 %collective-permute-done.5.refs_7_ = bf16[16,3712]{1,0:T(8,128)(2,1)S(1)} collective-permute-done((bf16[16,3712]{1,0:T(8,128)(2,1)S(1)}, bf16[16,3712]{1,0:T(8,128)(2,1)S(1)}, u32[]{:S(2)}, u32[]{:S(2)}) %collective-permute-start.5) | collective-permute-done | bytes 118816 | tf_op jit(solution)/shard_map/ppermute | solution.py:306
  18.2 4.1 %collective-permute-start.3 = (bf16[16,3712]{1,0:T(8,128)(2,1)S(1)}, bf16[16,3712]{1,0:T(8,128)(2,1)S(1)}, u32[]{:S(2)}, u32[]{:S(2)}) collective-permute-start(bf16[16,3712]{1,0:T(8,128)(2,1)S(1)} %get-tuple-element.42), channel_id=1, source_target_pairs={{0,6},{1,7},{2,4},{3,5},{4,14},{5,15},{6,12},{7,13},{8,2},{9,3},{1... | collective-permute-start | bytes 356360 | tf_op jit(solution)/shard_map/ppermute | solution.py:306
  23.0 3.6 %collective-permute-done.3.refs_4_ = bf16[16,3712]{1,0:T(8,128)(2,1)S(1)} collective-permute-done((bf16[16,3712]{1,0:T(8,128)(2,1)S(1)}, bf16[16,3712]{1,0:T(8,128)(2,1)S(1)}, u32[]{:S(2)}, u32[]{:S(2)}) %collective-permute-start.3) | collective-permute-done | bytes 118816 | tf_op jit(solution)/shard_map/ppermute | solution.py:306
  27.1 1.7 %near_pass.1 = (bf16[128,3712]{1,0:T(8,128)(2,1)S(1)}, f32[128,3584]{1,0:T(8,128)S(1)}) custom-call(bf16[16,3712]{1,0:T(8,128)(2,1)S(1)} %get-tuple-element.35.refs_0_, bf16[16,3712]{1,0:T(8,128)(2,1)S(1)} %collective-permute-done.refs_1_, bf16[16,3712]{1,0:T(8,128)(2,1)S(1)} %get-tuple-element.40.refs_2_, ...), custom_call_target="tpu_custom_call" | custom-call | bytes 11010048 | tf_op jit(solution)/shard_map/near_pass/pallas_call | solution.py:84
  28.9 1.7 %far_pass.1 = (bf16[16,3712]{1,0:T(8,128)(2,1)S(1)}, bf16[16,3712]{1,0:T(8,128)(2,1)S(1)}, bf16[16,3712]{1,0:T(8,128)(2,1)S(1)}, bf16[16,3712]{1,0:T(8,128)(2,1)...) custom-call(bf16[128,3712]{1,0:T(8,128)(2,1)S(1)} %get-tuple-element, ...), custom_call_target="tpu_custom_call" | custom-call | bytes 11010048 | tf_op jit(solution)/shard_map/far_pass/pallas_call | solution.py:84
  30.6 1.6 %collective-permute-start.10 = (bf16[16,3712]{1,0:T(8,128)(2,1)S(1)}, bf16[16,3712]{1,0:T(8,128)(2,1)S(1)}, u32[]{:S(2)}, u32[]{:S(2)}) collective-permute-start(bf16[16,3712]{1,0:T(8,128)(2,1)S(1)} %get-tuple-element.52), channel_id=1, source_target_pairs={{0,6},{1,7},{2,4},{3,5},{4,14},{5,15},{6,12},{7,13},{8,2},{9,3},{1... | collective-permute-start | bytes 356360 | tf_op jit(solution)/shard_map/ppermute | solution.py:306
  32.3 1.1 %collective-permute-start.11 = (bf16[16,3712]{1,0:T(8,128)(2,1)S(1)}, bf16[16,3712]{1,0:T(8,128)(2,1)S(1)}, u32[]{:S(2)}, u32[]{:S(2)}) collective-permute-start(bf16[16,3712]{1,0:T(8,128)(2,1)S(1)} %get-tuple-element.53), channel_id=1, source_target_pairs={{0,2},{1,3},{2,0},{3,1},{4,6},{5,7},{6,4},{7,5},{8,10},{9,11},{10,... | collective-permute-start | bytes 356360 | tf_op jit(solution)/shard_map/ppermute | solution.py:306
  33.4 1.5 %collective-permute-start.12 = (bf16[16,3712]{1,0:T(8,128)(2,1)S(1)}, bf16[16,3712]{1,0:T(8,128)(2,1)S(1)}, u32[]{:S(2)}, u32[]{:S(2)}) collective-permute-start(bf16[16,3712]{1,0:T(8,128)(2,1)S(1)} %get-tuple-element.54), channel_id=1, source_target_pairs={{0,16},{1,17},{2,18},{3,19},{4,20},{5,21},{6,22},{7,23},{8,24},{9,... | collective-permute-start | bytes 356360 | tf_op jit(solution)/shard_map/ppermute | solution.py:306
  34.9 0.9 %collective-permute-start.13 = (bf16[16,3712]{1,0:T(8,128)(2,1)S(1)}, bf16[16,3712]{1,0:T(8,128)(2,1)S(1)}, u32[]{:S(2)}, u32[]{:S(2)}) collective-permute-start(bf16[16,3712]{1,0:T(8,128)(2,1)S(1)} %get-tuple-element.55), channel_id=1, source_target_pairs={{0,18},{1,19},{2,16},{3,17},{4,22},{5,23},{6,20},{7,21},{8,26},{9,... | collective-permute-start | bytes 356360 | tf_op jit(solution)/shard_map/ppermute | solution.py:306
  35.7 1.9 %collective-permute-start.9 = (bf16[16,3712]{1,0:T(8,128)(2,1)S(1)}, bf16[16,3712]{1,0:T(8,128)(2,1)S(1)}, u32[]{:S(2)}, u32[]{:S(2)}) collective-permute-start(bf16[16,3712]{1,0:T(8,128)(2,1)S(1)} %get-tuple-element.51), channel_id=1, source_target_pairs={{0,4},{1,5},{2,6},{3,7},{4,12},{5,13},{6,14},{7,15},{8,0},{9,1},{1... | collective-permute-start | bytes 356360 | tf_op jit(solution)/shard_map/ppermute | solution.py:306
  38.0 3.1 %collective-permute-start.14 = (bf16[16,3712]{1,0:T(8,128)(2,1)S(1)}, bf16[16,3712]{1,0:T(8,128)(2,1)S(1)}, u32[]{:S(2)}, u32[]{:S(2)}) collective-permute-start(bf16[16,3712]{1,0:T(8,128)(2,1)S(1)} %get-tuple-element.58), channel_id=1, source_target_pairs={{0,24},{1,25},{2,26},{3,27},{4,16},{5,17},{6,18},{7,19},{8,28},{9,... | collective-permute-start | bytes 356360 | tf_op jit(solution)/shard_map/ppermute | solution.py:306
  41.1 0.7 %collective-permute-done.13.refs_1_ = bf16[16,3712]{1,0:T(8,128)(2,1)S(1)} collective-permute-done((bf16[16,3712]{1,0:T(8,128)(2,1)S(1)}, bf16[16,3712]{1,0:T(8,128)(2,1)S(1)}, u32[]{:S(2)}, u32[]{:S(2)}) %collective-permute-start.13) | collective-permute-done | bytes 118816 | tf_op jit(solution)/shard_map/ppermute | solution.py:306
  42.6 1.9 %collective-permute-start.16 = (bf16[32,3584]{1,0:T(8,128)(2,1)S(1)}, bf16[32,3584]{1,0:T(8,128)(2,1)S(1)}, u32[]{:S(2)}, u32[]{:S(2)}) collective-permute-start(bf16[32,3584]{1,0:T(8,128)(2,1)S(1)} %combine.2), channel_id=1, source_target_pairs={{0,20},{1,21},{2,22},{3,23},{4,28},{5,29},{6,30},{7,31},{8,16},{9,... | collective-permute-start | bytes 688136 | tf_op jit(solution)/shard_map/ppermute | solution.py:306
  44.5 2.4 %collective-permute-done.14.refs_2_ = bf16[16,3712]{1,0:T(8,128)(2,1)S(1)} collective-permute-done((bf16[16,3712]{1,0:T(8,128)(2,1)S(1)}, bf16[16,3712]{1,0:T(8,128)(2,1)S(1)}, u32[]{:S(2)}, u32[]{:S(2)}) %collective-permute-start.14) | collective-permute-done | bytes 118816 | tf_op jit(solution)/shard_map/ppermute | solution.py:306
  46.9 3.2 %collective-permute-start.15 = (bf16[16,3712]{1,0:T(8,128)(2,1)S(1)}, bf16[16,3712]{1,0:T(8,128)(2,1)S(1)}, u32[]{:S(2)}, u32[]{:S(2)}) collective-permute-start(bf16[16,3712]{1,0:T(8,128)(2,1)S(1)} %get-tuple-element.60), channel_id=1, source_target_pairs={{0,26},{1,27},{2,24},{3,25},{4,18},{5,19},{6,16},{7,17},{8,30},{9,... | collective-permute-start | bytes 356360 | tf_op jit(solution)/shard_map/ppermute | solution.py:306
  50.1 3.4 %collective-permute-done.15.refs_3_ = bf16[16,3712]{1,0:T(8,128)(2,1)S(1)} collective-permute-done((bf16[16,3712]{1,0:T(8,128)(2,1)S(1)}, bf16[16,3712]{1,0:T(8,128)(2,1)S(1)}, u32[]{:S(2)}, u32[]{:S(2)}) %collective-permute-start.15) | collective-permute-done | bytes 118816 | tf_op jit(solution)/shard_map/ppermute | solution.py:306
  53.5 1.1 %combine.3 = bf16[32,3584]{1,0:T(8,128)(2,1)} custom-call(bf16[16,3712]{1,0:T(8,128)(2,1)S(1)} %collective-permute-done.12.refs_0_, bf16[16,3712]{1,0:T(8,128)(2,1)S(1)} %collective-permute-done.13.refs_1_, bf16[16,3712]{1,0:T(8,128)(2,1)S(1)} %collective-permute-done.14.refs_2_, bf16[16,3712]{1,0:T(8,128)(2,1)S(1)} %collective-permute-done.15.refs_3_, ...), custom_call_target="tpu_custom_call" | custom-call | tf_op jit(solution)/shard_map/combine/pallas_call | solution.py:84
  (23 shorter events, 5.1 us)
Async XLA Ops:
  0.0 28.9 %collective-permute-start.7 = (bf16[3584,1024]{1,0:T(8,128)(2,1)}, bf16[3584,1024]{1,0:T(8,128)(2,1)S(1)}, u32[]{:S(2)}, u32[]{:S(2)}) collective-permute-start(bf16[3584,1024]{1,0:T(8,128)(2,1)} %bitcast.10), channel_id=1, source_target_pairs={{0,1},{1,0},{2,3},{3,2},{4,5},{5,4},{6,7},{7,6},{8,9},{9,8},{10,11... | collective-permute-start | bytes 22020104 | tf_op jit(solution)/shard_map/ppermute | solution.py:324
  0.5 28.4 %collective-permute-start.8 = (bf16[512,3584]{1,0:T(8,128)(2,1)}, bf16[512,3584]{1,0:T(8,128)(2,1)S(1)}, u32[]{:S(2)}, u32[]{:S(2)}) collective-permute-start(bf16[512,3584]{1,0:T(8,128)(2,1)} %bitcast.12), channel_id=1, source_target_pairs={{0,1},{1,0},{2,3},{3,2},{4,5},{5,4},{6,7},{7,6},{8,9},{9,8},{10,11... | collective-permute-start | bytes 11010056 | tf_op jit(solution)/shard_map/ppermute | solution.py:323
  1.5 11.5 %collective-permute-start.1 = (bf16[32,3712]{1,0:T(8,128)(2,1)S(1)}, bf16[32,3712]{1,0:T(8,128)(2,1)S(1)}, u32[]{:S(2)}, u32[]{:S(2)}) collective-permute-start(bf16[32,3712]{1,0:T(8,128)(2,1)S(1)} %prepare.1.block), channel_id=1, source_target_pairs={{0,4},{1,5},{2,6},{3,7},{4,12},{5,13},{6,14},{7,15},{8,0},{9,1},{1... | collective-permute-start | bytes 712712 | tf_op jit(solution)/shard_map/ppermute | solution.py:306
  5.0 7.0 %collective-permute-start = (bf16[16,3712]{1,0:T(8,128)(2,1)S(1)}, bf16[16,3712]{1,0:T(8,128)(2,1)S(1)}, u32[]{:S(2)}, u32[]{:S(2)}) collective-permute-start(bf16[16,3712]{1,0:T(8,128)(2,1)S(1)} %get-tuple-element.36), channel_id=1, source_target_pairs={{0,2},{1,3},{2,0},{3,1},{4,6},{5,7},{6,4},{7,5},{8,10},{9,11},{10,... | collective-permute-start | bytes 356360 | tf_op jit(solution)/shard_map/ppermute | solution.py:306
  6.6 3.1 %copy-start = (bf16[1,3584,1024]{2,1,0:T(8,128)(2,1)S(1)}, bf16[1,3584,1024]{2,1,0:T(8,128)(2,1)}, u32[]{:S(2)}) copy-start(bf16[1,3584,1024]{2,1,0:T(8,128)(2,1)} %param.8) | copy-start | bytes 22020100
  9.7 2.0 %copy-start.1 = (bf16[1,512,3584]{2,1,0:T(8,128)(2,1)S(1)}, bf16[1,512,3584]{2,1,0:T(8,128)(2,1)}, u32[]{:S(2)}) copy-start(bf16[1,512,3584]{2,1,0:T(8,128)(2,1)} %param.9) | copy-start | bytes 11010052
  12.0 6.2 %collective-permute-start.5 = (bf16[16,3712]{1,0:T(8,128)(2,1)S(1)}, bf16[16,3712]{1,0:T(8,128)(2,1)S(1)}, u32[]{:S(2)}, u32[]{:S(2)}) collective-permute-start(bf16[16,3712]{1,0:T(8,128)(2,1)S(1)} %get-tuple-element.46), channel_id=1, source_target_pairs={{0,10},{1,11},{2,8},{3,9},{4,2},{5,3},{6,0},{7,1},{8,14},{9,15},{1... | collective-permute-start | bytes 356360 | tf_op jit(solution)/shard_map/ppermute | solution.py:306
  13.5 8.9 %collective-permute-start.4 = (bf16[16,3712]{1,0:T(8,128)(2,1)S(1)}, bf16[16,3712]{1,0:T(8,128)(2,1)S(1)}, u32[]{:S(2)}, u32[]{:S(2)}) collective-permute-start(bf16[16,3712]{1,0:T(8,128)(2,1)S(1)} %get-tuple-element.43), channel_id=1, source_target_pairs={{0,2},{1,3},{2,0},{3,1},{4,6},{5,7},{6,4},{7,5},{8,10},{9,11},{10,... | collective-permute-start | bytes 356360 | tf_op jit(solution)/shard_map/ppermute | solution.py:306
  15.4 7.6 %collective-permute-start.2 = (bf16[16,3712]{1,0:T(8,128)(2,1)S(1)}, bf16[16,3712]{1,0:T(8,128)(2,1)S(1)}, u32[]{:S(2)}, u32[]{:S(2)}) collective-permute-start(bf16[16,3712]{1,0:T(8,128)(2,1)S(1)} %get-tuple-element.41), channel_id=1, source_target_pairs={{0,4},{1,5},{2,6},{3,7},{4,12},{5,13},{6,14},{7,15},{8,0},{9,1},{1... | collective-permute-start | bytes 356360 | tf_op jit(solution)/shard_map/ppermute | solution.py:306
  18.2 8.4 %collective-permute-start.3 = (bf16[16,3712]{1,0:T(8,128)(2,1)S(1)}, bf16[16,3712]{1,0:T(8,128)(2,1)S(1)}, u32[]{:S(2)}, u32[]{:S(2)}) collective-permute-start(bf16[16,3712]{1,0:T(8,128)(2,1)S(1)} %get-tuple-element.42), channel_id=1, source_target_pairs={{0,6},{1,7},{2,4},{3,5},{4,14},{5,15},{6,12},{7,13},{8,2},{9,3},{1... | collective-permute-start | bytes 356360 | tf_op jit(solution)/shard_map/ppermute | solution.py:306
  22.3 4.8 %collective-permute-start.6 = (bf16[16,3712]{1,0:T(8,128)(2,1)S(1)}, bf16[16,3712]{1,0:T(8,128)(2,1)S(1)}, u32[]{:S(2)}, u32[]{:S(2)}) collective-permute-start(bf16[16,3712]{1,0:T(8,128)(2,1)S(1)} %get-tuple-element.47), channel_id=1, source_target_pairs={{0,8},{1,9},{2,10},{3,11},{4,0},{5,1},{6,2},{7,3},{8,12},{9,13},{1... | collective-permute-start | bytes 356360 | tf_op jit(solution)/shard_map/ppermute | solution.py:306
  30.6 7.4 %collective-permute-start.10 = (bf16[16,3712]{1,0:T(8,128)(2,1)S(1)}, bf16[16,3712]{1,0:T(8,128)(2,1)S(1)}, u32[]{:S(2)}, u32[]{:S(2)}) collective-permute-start(bf16[16,3712]{1,0:T(8,128)(2,1)S(1)} %get-tuple-element.52), channel_id=1, source_target_pairs={{0,6},{1,7},{2,4},{3,5},{4,14},{5,15},{6,12},{7,13},{8,2},{9,3},{1... | collective-permute-start | bytes 356360 | tf_op jit(solution)/shard_map/ppermute | solution.py:306
  32.3 8.9 %collective-permute-start.11 = (bf16[16,3712]{1,0:T(8,128)(2,1)S(1)}, bf16[16,3712]{1,0:T(8,128)(2,1)S(1)}, u32[]{:S(2)}, u32[]{:S(2)}) collective-permute-start(bf16[16,3712]{1,0:T(8,128)(2,1)S(1)} %get-tuple-element.53), channel_id=1, source_target_pairs={{0,2},{1,3},{2,0},{3,1},{4,6},{5,7},{6,4},{7,5},{8,10},{9,11},{10,... | collective-permute-start | bytes 356360 | tf_op jit(solution)/shard_map/ppermute | solution.py:306
  33.4 7.7 %collective-permute-start.12 = (bf16[16,3712]{1,0:T(8,128)(2,1)S(1)}, bf16[16,3712]{1,0:T(8,128)(2,1)S(1)}, u32[]{:S(2)}, u32[]{:S(2)}) collective-permute-start(bf16[16,3712]{1,0:T(8,128)(2,1)S(1)} %get-tuple-element.54), channel_id=1, source_target_pairs={{0,16},{1,17},{2,18},{3,19},{4,20},{5,21},{6,22},{7,23},{8,24},{9,... | collective-permute-start | bytes 356360 | tf_op jit(solution)/shard_map/ppermute | solution.py:306
  34.9 7.0 %collective-permute-start.13 = (bf16[16,3712]{1,0:T(8,128)(2,1)S(1)}, bf16[16,3712]{1,0:T(8,128)(2,1)S(1)}, u32[]{:S(2)}, u32[]{:S(2)}) collective-permute-start(bf16[16,3712]{1,0:T(8,128)(2,1)S(1)} %get-tuple-element.55), channel_id=1, source_target_pairs={{0,18},{1,19},{2,16},{3,17},{4,22},{5,23},{6,20},{7,21},{8,26},{9,... | collective-permute-start | bytes 356360 | tf_op jit(solution)/shard_map/ppermute | solution.py:306
  35.7 6.4 %collective-permute-start.9 = (bf16[16,3712]{1,0:T(8,128)(2,1)S(1)}, bf16[16,3712]{1,0:T(8,128)(2,1)S(1)}, u32[]{:S(2)}, u32[]{:S(2)}) collective-permute-start(bf16[16,3712]{1,0:T(8,128)(2,1)S(1)} %get-tuple-element.51), channel_id=1, source_target_pairs={{0,4},{1,5},{2,6},{3,7},{4,12},{5,13},{6,14},{7,15},{8,0},{9,1},{1... | collective-permute-start | bytes 356360 | tf_op jit(solution)/shard_map/ppermute | solution.py:306
  38.0 8.9 %collective-permute-start.14 = (bf16[16,3712]{1,0:T(8,128)(2,1)S(1)}, bf16[16,3712]{1,0:T(8,128)(2,1)S(1)}, u32[]{:S(2)}, u32[]{:S(2)}) collective-permute-start(bf16[16,3712]{1,0:T(8,128)(2,1)S(1)} %get-tuple-element.58), channel_id=1, source_target_pairs={{0,24},{1,25},{2,26},{3,27},{4,16},{5,17},{6,18},{7,19},{8,28},{9,... | collective-permute-start | bytes 356360 | tf_op jit(solution)/shard_map/ppermute | solution.py:306
  42.6 10.9 %collective-permute-start.16 = (bf16[32,3584]{1,0:T(8,128)(2,1)S(1)}, bf16[32,3584]{1,0:T(8,128)(2,1)S(1)}, u32[]{:S(2)}, u32[]{:S(2)}) collective-permute-start(bf16[32,3584]{1,0:T(8,128)(2,1)S(1)} %combine.2), channel_id=1, source_target_pairs={{0,20},{1,21},{2,22},{3,23},{4,28},{5,29},{6,30},{7,31},{8,16},{9,... | collective-permute-start | bytes 688136 | tf_op jit(solution)/shard_map/ppermute | solution.py:306
  46.9 6.6 %collective-permute-start.15 = (bf16[16,3712]{1,0:T(8,128)(2,1)S(1)}, bf16[16,3712]{1,0:T(8,128)(2,1)S(1)}, u32[]{:S(2)}, u32[]{:S(2)}) collective-permute-start(bf16[16,3712]{1,0:T(8,128)(2,1)S(1)} %get-tuple-element.60), channel_id=1, source_target_pairs={{0,26},{1,27},{2,24},{3,25},{4,18},{5,19},{6,16},{7,17},{8,30},{9,... | collective-permute-start | bytes 356360 | tf_op jit(solution)/shard_map/ppermute | solution.py:306

commit v23 on v20

--- a/solution.py
+++ b/solution.py
@@ -339,15 +339,18 @@
     slots, total = near_pass(pieces, near)
     pieces = far_pass(slots, total, (far_in, far_out), capacity)
     piece = dict(zip(places, pieces))
+    straight = [
+        sent(piece[0, 0], sections, 1, 0, 0),
+        sent(piece[0, 1], sections, 1, 0, 1),
+        sent(piece[1, 0], sections, 1, -1, 0),
+    ]
     merged = [
         piece[3, 0],
-        sent(piece[2, 0], sections, 0, 1, 0),
         sent(piece[2, 1], sections, 0, 1, 1),
         sent(piece[3, 1], sections, 0, 0, 1),
+        sent(piece[2, 0], sections, 0, 1, 0),
     ]
-    straight = [sent(piece[0, flip], sections, 1, 0, flip) for flip in range(2)]
-    merged, straight = lax.optimization_barrier((merged, straight))
-    straight += [sent(piece[1, flip], sections, 1, -1, flip) for flip in range(2)]
+    straight.append(sent(after(piece[1, 1], straight), sections, 1, -1, 1))
     merged = sent(combine(merged, tok_count), sections, 1, 1, 0)
     return combine(straight, tok_count, merged)[None]
 

time: 54.9 us -> 57.9 us (1.055)
  waiting for transfers between devices: 16.6 us -> 20.3 us
  starting transfers between devices: 25.8 us -> 25.1 us
    ppermute x15, waiting for transfers between devices: 16.6 us -> 20.3 us  [sent(): return lax.ppermute(shard, ('section', 'expert'), pairs)]
    ppermute x15, starting transfers between devices: 25.3 us -> 24.6 us  [sent(): return lax.ppermute(shard, ('section', 'expert'), pairs)]
  transfers between devices with their start and end apart: 17 -> 17, of which waited for: 10 -> 9; matrix products, arithmetic and copies ran while one was open for 0% -> 0% of each run, Pallas kernels for 8% -> 8%
where the time goes in v23:
time: 57.9 us; the launch traced here: 57.7 us
  starting transfers between devices  25.1 us (43%)
  waiting for transfers between devices  20.3 us (35%)
  Pallas kernels  7.58 us (13%)
  local copies, waits for them, and re-layouts  4.62 us (8%)
    ppermute x15, starting transfers between devices, sent(): return lax.ppermute(shard, ('section', 'expert'), pairs)  24.6 us
    ppermute x15, waiting for transfers between devices, sent(): return lax.ppermute(shard, ('section', 'expert'), pairs)  20.3 us
    pallas_call x9, Pallas kernels, local_call(): pl.pallas_call(kernel, out_shape=out_shape, in_specs=[vmem if spec is Non...  7.58 us
    unnamed x4, local copies, waits for them, and re-layouts  4.62 us
  transfers between devices with their start and end apart: 17, of which 9 were waited for; matrix products, arithmetic and copies ran while one was open for 0% of the time, Pallas kernels for 8%

profile of v23, /device:TPU:0, one launch (start us, length us, event | category | flops | bytes accessed | tf_op | source)
XLA Modules:
  0.0 57.7 jit_solution(1514937982761268498)
XLA Ops:
  0.5 1.0 %prepare.1.block = bf16[32,3712]{1,0:T(8,128)(2,1)S(1)} custom-call(s32[2,32]{1,0:T(2,128)} %bitcast.15, f32[2,32]{1,0:T(2,128)} %bitcast.16, bf16[32,3584]{1,0:T(8,128)(2,1)} %bitcast.14), custom_call_target="tpu_custom_call" | custom-call | tf_op jit(solution)/shard_map/prepare/pallas_call | solution.py:84
  1.5 3.1 %collective-permute-start.1 = (bf16[32,3712]{1,0:T(8,128)(2,1)S(1)}, bf16[32,3712]{1,0:T(8,128)(2,1)S(1)}, u32[]{:S(2)}, u32[]{:S(2)}) collective-permute-start(bf16[32,3712]{1,0:T(8,128)(2,1)S(1)} %prepare.1.block), channel_id=1, source_target_pairs={{0,4},{1,5},{2,6},{3,7},{4,12},{5,13},{6,14},{7,15},{8,0},{9,1},{1... | collective-permute-start | bytes 712712 | tf_op jit(solution)/shard_map/ppermute | solution.py:306
  5.0 1.6 %collective-permute-start = (bf16[16,3712]{1,0:T(8,128)(2,1)S(1)}, bf16[16,3712]{1,0:T(8,128)(2,1)S(1)}, u32[]{:S(2)}, u32[]{:S(2)}) collective-permute-start(bf16[16,3712]{1,0:T(8,128)(2,1)S(1)} %get-tuple-element.30), channel_id=1, source_target_pairs={{0,2},{1,3},{2,0},{3,1},{4,6},{5,7},{6,4},{7,5},{8,10},{9,11},{10,... | collective-permute-start | bytes 356360 | tf_op jit(solution)/shard_map/ppermute | solution.py:306
  6.6 3.1 %copy-done = bf16[1,3584,1024]{2,1,0:T(8,128)(2,1)S(1)} copy-done((bf16[1,3584,1024]{2,1,0:T(8,128)(2,1)S(1)}, bf16[1,3584,1024]{2,1,0:T(8,128)(2,1)}, u32[]{:S(2)}) %copy-start) | copy-done | bytes 7340056
  10.2 1.5 %copy-done.1 = bf16[1,512,3584]{2,1,0:T(8,128)(2,1)S(1)} copy-done((bf16[1,512,3584]{2,1,0:T(8,128)(2,1)S(1)}, bf16[1,512,3584]{2,1,0:T(8,128)(2,1)}, u32[]{:S(2)}) %copy-start.1) | copy-done | bytes 3670040
  12.0 1.0 %collective-permute-start.5 = (bf16[16,3712]{1,0:T(8,128)(2,1)S(1)}, bf16[16,3712]{1,0:T(8,128)(2,1)S(1)}, u32[]{:S(2)}, u32[]{:S(2)}) collective-permute-start(bf16[16,3712]{1,0:T(8,128)(2,1)S(1)} %get-tuple-element.40), channel_id=1, source_target_pairs={{0,10},{1,11},{2,8},{3,9},{4,2},{5,3},{6,0},{7,1},{8,14},{9,15},{1... | collective-permute-start | bytes 356360 | tf_op jit(solution)/shard_map/ppermute | solution.py:306
  13.5 1.9 %collective-permute-start.4 = (bf16[16,3712]{1,0:T(8,128)(2,1)S(1)}, bf16[16,3712]{1,0:T(8,128)(2,1)S(1)}, u32[]{:S(2)}, u32[]{:S(2)}) collective-permute-start(bf16[16,3712]{1,0:T(8,128)(2,1)S(1)} %get-tuple-element.37), channel_id=1, source_target_pairs={{0,2},{1,3},{2,0},{3,1},{4,6},{5,7},{6,4},{7,5},{8,10},{9,11},{10,... | collective-permute-start | bytes 356360 | tf_op jit(solution)/shard_map/ppermute | solution.py:306
  15.4 0.7 %collective-permute-start.2 = (bf16[16,3712]{1,0:T(8,128)(2,1)S(1)}, bf16[16,3712]{1,0:T(8,128)(2,1)S(1)}, u32[]{:S(2)}, u32[]{:S(2)}) collective-permute-start(bf16[16,3712]{1,0:T(8,128)(2,1)S(1)} %get-tuple-element.35), channel_id=1, source_target_pairs={{0,4},{1,5},{2,6},{3,7},{4,12},{5,13},{6,14},{7,15},{8,0},{9,1},{1... | collective-permute-start | bytes 356360 | tf_op jit(solution)/shard_map/ppermute | solution.py:306
  16.0 2.2 %collective-permute-done.5.refs_7_ = bf16[16,3712]{1,0:T(8,128)(2,1)S(1)} collective-permute-done((bf16[16,3712]{1,0:T(8,128)(2,1)S(1)}, bf16[16,3712]{1,0:T(8,128)(2,1)S(1)}, u32[]{:S(2)}, u32[]{:S(2)}) %collective-permute-start.5) | collective-permute-done | bytes 118816 | tf_op jit(solution)/shard_map/ppermute | solution.py:306
  18.2 4.1 %collective-permute-start.3 = (bf16[16,3712]{1,0:T(8,128)(2,1)S(1)}, bf16[16,3712]{1,0:T(8,128)(2,1)S(1)}, u32[]{:S(2)}, u32[]{:S(2)}) collective-permute-start(bf16[16,3712]{1,0:T(8,128)(2,1)S(1)} %get-tuple-element.36), channel_id=1, source_target_pairs={{0,6},{1,7},{2,4},{3,5},{4,14},{5,15},{6,12},{7,13},{8,2},{9,3},{1... | collective-permute-start | bytes 356360 | tf_op jit(solution)/shard_map/ppermute | solution.py:306
  23.0 3.6 %collective-permute-done.3.refs_4_ = bf16[16,3712]{1,0:T(8,128)(2,1)S(1)} collective-permute-done((bf16[16,3712]{1,0:T(8,128)(2,1)S(1)}, bf16[16,3712]{1,0:T(8,128)(2,1)S(1)}, u32[]{:S(2)}, u32[]{:S(2)}) %collective-permute-start.3) | collective-permute-done | bytes 118816 | tf_op jit(solution)/shard_map/ppermute | solution.py:306
  27.1 1.7 %near_pass.1 = (bf16[128,3712]{1,0:T(8,128)(2,1)S(1)}, f32[128,3584]{1,0:T(8,128)S(1)}) custom-call(bf16[16,3712]{1,0:T(8,128)(2,1)S(1)} %get-tuple-element.29.refs_0_, bf16[16,3712]{1,0:T(8,128)(2,1)S(1)} %collective-permute-done.refs_1_, bf16[16,3712]{1,0:T(8,128)(2,1)S(1)} %get-tuple-element.34.refs_2_, ...), custom_call_target="tpu_custom_call" | custom-call | bytes 11010048 | tf_op jit(solution)/shard_map/near_pass/pallas_call | solution.py:84
  28.9 1.7 %far_pass.1 = (bf16[16,3712]{1,0:T(8,128)(2,1)S(1)}, bf16[16,3712]{1,0:T(8,128)(2,1)S(1)}, bf16[16,3712]{1,0:T(8,128)(2,1)S(1)}, bf16[16,3712]{1,0:T(8,128)(2,1)...) custom-call(bf16[128,3712]{1,0:T(8,128)(2,1)S(1)} %get-tuple-element, ...), custom_call_target="tpu_custom_call" | custom-call | bytes 11010048 | tf_op jit(solution)/shard_map/far_pass/pallas_call | solution.py:84
  30.6 1.6 %collective-permute-start.13 = (bf16[16,3712]{1,0:T(8,128)(2,1)S(1)}, bf16[16,3712]{1,0:T(8,128)(2,1)S(1)}, u32[]{:S(2)}, u32[]{:S(2)}) collective-permute-start(bf16[16,3712]{1,0:T(8,128)(2,1)S(1)} %get-tuple-element.50), channel_id=1, source_target_pairs={{0,6},{1,7},{2,4},{3,5},{4,14},{5,15},{6,12},{7,13},{8,2},{9,3},{1... | collective-permute-start | bytes 356360 | tf_op jit(solution)/shard_map/ppermute | solution.py:306
  32.3 1.1 %collective-permute-start.14 = (bf16[16,3712]{1,0:T(8,128)(2,1)S(1)}, bf16[16,3712]{1,0:T(8,128)(2,1)S(1)}, u32[]{:S(2)}, u32[]{:S(2)}) collective-permute-start(bf16[16,3712]{1,0:T(8,128)(2,1)S(1)} %get-tuple-element.51), channel_id=1, source_target_pairs={{0,2},{1,3},{2,0},{3,1},{4,6},{5,7},{6,4},{7,5},{8,10},{9,11},{10,... | collective-permute-start | bytes 356360 | tf_op jit(solution)/shard_map/ppermute | solution.py:306
  33.4 1.6 %collective-permute-start.15 = (bf16[16,3712]{1,0:T(8,128)(2,1)S(1)}, bf16[16,3712]{1,0:T(8,128)(2,1)S(1)}, u32[]{:S(2)}, u32[]{:S(2)}) collective-permute-start(bf16[16,3712]{1,0:T(8,128)(2,1)S(1)} %get-tuple-element.52), channel_id=1, source_target_pairs={{0,4},{1,5},{2,6},{3,7},{4,12},{5,13},{6,14},{7,15},{8,0},{9,1},{1... | collective-permute-start | bytes 356360 | tf_op jit(solution)/shard_map/ppermute | solution.py:306
  34.9 2.2 %collective-permute-start.10 = (bf16[16,3712]{1,0:T(8,128)(2,1)S(1)}, bf16[16,3712]{1,0:T(8,128)(2,1)S(1)}, u32[]{:S(2)}, u32[]{:S(2)}) collective-permute-start(bf16[16,3712]{1,0:T(8,128)(2,1)S(1)} %get-tuple-element.45), channel_id=1, source_target_pairs={{0,18},{1,19},{2,16},{3,17},{4,22},{5,23},{6,20},{7,21},{8,26},{9,... | collective-permute-start | bytes 356360 | tf_op jit(solution)/shard_map/ppermute | solution.py:306
  37.1 1.0 %collective-permute-start.11 = (bf16[16,3712]{1,0:T(8,128)(2,1)S(1)}, bf16[16,3712]{1,0:T(8,128)(2,1)S(1)}, u32[]{:S(2)}, u32[]{:S(2)}) collective-permute-start(bf16[16,3712]{1,0:T(8,128)(2,1)S(1)} %get-tuple-element.46), channel_id=1, source_target_pairs={{0,24},{1,25},{2,26},{3,27},{4,16},{5,17},{6,18},{7,19},{8,28},{9,... | collective-permute-start | bytes 356360 | tf_op jit(solution)/shard_map/ppermute | solution.py:306
  38.2 1.5 %collective-permute-start.9 = (bf16[16,3712]{1,0:T(8,128)(2,1)S(1)}, bf16[16,3712]{1,0:T(8,128)(2,1)S(1)}, u32[]{:S(2)}, u32[]{:S(2)}) collective-permute-start(bf16[16,3712]{1,0:T(8,128)(2,1)S(1)} %get-tuple-element.44), channel_id=1, source_target_pairs={{0,16},{1,17},{2,18},{3,19},{4,20},{5,21},{6,22},{7,23},{8,24},{9,... | collective-permute-start | bytes 356360 | tf_op jit(solution)/shard_map/ppermute | solution.py:306
  40.6 1.6 %collective-permute-start.16 = (bf16[32,3584]{1,0:T(8,128)(2,1)S(1)}, bf16[32,3584]{1,0:T(8,128)(2,1)S(1)}, u32[]{:S(2)}, u32[]{:S(2)}) collective-permute-start(bf16[32,3584]{1,0:T(8,128)(2,1)S(1)} %combine.2), channel_id=1, source_target_pairs={{0,20},{1,21},{2,22},{3,23},{4,28},{5,29},{6,30},{7,31},{8,16},{9,... | collective-permute-start | bytes 688136 | tf_op jit(solution)/shard_map/ppermute | solution.py:306
  42.2 7.3 %collective-permute-done.10.refs_1_ = bf16[16,3712]{1,0:T(8,128)(2,1)S(1)} collective-permute-done((bf16[16,3712]{1,0:T(8,128)(2,1)S(1)}, bf16[16,3712]{1,0:T(8,128)(2,1)S(1)}, u32[]{:S(2)}, u32[]{:S(2)}) %collective-permute-start.10) | collective-permute-done | bytes 118816 | tf_op jit(solution)/shard_map/ppermute | solution.py:306
  50.0 1.4 %collective-permute-start.12 = (bf16[16,3712]{1,0:T(8,128)(2,1)S(1)}, bf16[16,3712]{1,0:T(8,128)(2,1)S(1)}, u32[]{:S(2)}, u32[]{:S(2)}) collective-permute-start(bf16[16,3712]{1,0:T(8,128)(2,1)S(1)} %get-tuple-element.48), channel_id=1, source_target_pairs={{0,26},{1,27},{2,24},{3,25},{4,18},{5,19},{6,16},{7,17},{8,30},{9,... | collective-permute-start | bytes 356360 | tf_op jit(solution)/shard_map/ppermute | solution.py:306
  51.4 5.2 %collective-permute-done.12.refs_3_ = bf16[16,3712]{1,0:T(8,128)(2,1)S(1)} collective-permute-done((bf16[16,3712]{1,0:T(8,128)(2,1)S(1)}, bf16[16,3712]{1,0:T(8,128)(2,1)S(1)}, u32[]{:S(2)}, u32[]{:S(2)}) %collective-permute-start.12) | collective-permute-done | bytes 118816 | tf_op jit(solution)/shard_map/ppermute | solution.py:306
  56.6 1.1 %combine.3 = bf16[32,3584]{1,0:T(8,128)(2,1)} custom-call(bf16[16,3712]{1,0:T(8,128)(2,1)S(1)} %collective-permute-done.9.refs_0_, bf16[16,3712]{1,0:T(8,128)(2,1)S(1)} %collective-permute-done.10.refs_1_, bf16[16,3712]{1,0:T(8,128)(2,1)S(1)} %collective-permute-done.11.refs_2_, bf16[16,3712]{1,0:T(8,128)(2,1)S(1)} %collective-permute-done.12.refs_3_, ...), custom_call_target="tpu_custom_call" | custom-call | tf_op jit(solution)/shard_map/combine/pallas_call | solution.py:84
  (23 shorter events, 4.8 us)
Async XLA Ops:
  0.0 28.9 %collective-permute-start.7 = (bf16[3584,1024]{1,0:T(8,128)(2,1)}, bf16[3584,1024]{1,0:T(8,128)(2,1)S(1)}, u32[]{:S(2)}, u32[]{:S(2)}) collective-permute-start(bf16[3584,1024]{1,0:T(8,128)(2,1)} %bitcast.10), channel_id=1, source_target_pairs={{0,1},{1,0},{2,3},{3,2},{4,5},{5,4},{6,7},{7,6},{8,9},{9,8},{10,11... | collective-permute-start | bytes 22020104 | tf_op jit(solution)/shard_map/ppermute | solution.py:324
  0.5 28.4 %collective-permute-start.8 = (bf16[512,3584]{1,0:T(8,128)(2,1)}, bf16[512,3584]{1,0:T(8,128)(2,1)S(1)}, u32[]{:S(2)}, u32[]{:S(2)}) collective-permute-start(bf16[512,3584]{1,0:T(8,128)(2,1)} %bitcast.12), channel_id=1, source_target_pairs={{0,1},{1,0},{2,3},{3,2},{4,5},{5,4},{6,7},{7,6},{8,9},{9,8},{10,11... | collective-permute-start | bytes 11010056 | tf_op jit(solution)/shard_map/ppermute | solution.py:323
  1.5 11.5 %collective-permute-start.1 = (bf16[32,3712]{1,0:T(8,128)(2,1)S(1)}, bf16[32,3712]{1,0:T(8,128)(2,1)S(1)}, u32[]{:S(2)}, u32[]{:S(2)}) collective-permute-start(bf16[32,3712]{1,0:T(8,128)(2,1)S(1)} %prepare.1.block), channel_id=1, source_target_pairs={{0,4},{1,5},{2,6},{3,7},{4,12},{5,13},{6,14},{7,15},{8,0},{9,1},{1... | collective-permute-start | bytes 712712 | tf_op jit(solution)/shard_map/ppermute | solution.py:306
  5.0 7.0 %collective-permute-start = (bf16[16,3712]{1,0:T(8,128)(2,1)S(1)}, bf16[16,3712]{1,0:T(8,128)(2,1)S(1)}, u32[]{:S(2)}, u32[]{:S(2)}) collective-permute-start(bf16[16,3712]{1,0:T(8,128)(2,1)S(1)} %get-tuple-element.30), channel_id=1, source_target_pairs={{0,2},{1,3},{2,0},{3,1},{4,6},{5,7},{6,4},{7,5},{8,10},{9,11},{10,... | collective-permute-start | bytes 356360 | tf_op jit(solution)/shard_map/ppermute | solution.py:306
  6.6 3.1 %copy-start = (bf16[1,3584,1024]{2,1,0:T(8,128)(2,1)S(1)}, bf16[1,3584,1024]{2,1,0:T(8,128)(2,1)}, u32[]{:S(2)}) copy-start(bf16[1,3584,1024]{2,1,0:T(8,128)(2,1)} %param.8) | copy-start | bytes 22020100
  9.7 2.0 %copy-start.1 = (bf16[1,512,3584]{2,1,0:T(8,128)(2,1)S(1)}, bf16[1,512,3584]{2,1,0:T(8,128)(2,1)}, u32[]{:S(2)}) copy-start(bf16[1,512,3584]{2,1,0:T(8,128)(2,1)} %param.9) | copy-start | bytes 11010052
  12.0 6.2 %collective-permute-start.5 = (bf16[16,3712]{1,0:T(8,128)(2,1)S(1)}, bf16[16,3712]{1,0:T(8,128)(2,1)S(1)}, u32[]{:S(2)}, u32[]{:S(2)}) collective-permute-start(bf16[16,3712]{1,0:T(8,128)(2,1)S(1)} %get-tuple-element.40), channel_id=1, source_target_pairs={{0,10},{1,11},{2,8},{3,9},{4,2},{5,3},{6,0},{7,1},{8,14},{9,15},{1... | collective-permute-start | bytes 356360 | tf_op jit(solution)/shard_map/ppermute | solution.py:306
  13.5 8.9 %collective-permute-start.4 = (bf16[16,3712]{1,0:T(8,128)(2,1)S(1)}, bf16[16,3712]{1,0:T(8,128)(2,1)S(1)}, u32[]{:S(2)}, u32[]{:S(2)}) collective-permute-start(bf16[16,3712]{1,0:T(8,128)(2,1)S(1)} %get-tuple-element.37), channel_id=1, source_target_pairs={{0,2},{1,3},{2,0},{3,1},{4,6},{5,7},{6,4},{7,5},{8,10},{9,11},{10,... | collective-permute-start | bytes 356360 | tf_op jit(solution)/shard_map/ppermute | solution.py:306
  15.4 7.6 %collective-permute-start.2 = (bf16[16,3712]{1,0:T(8,128)(2,1)S(1)}, bf16[16,3712]{1,0:T(8,128)(2,1)S(1)}, u32[]{:S(2)}, u32[]{:S(2)}) collective-permute-start(bf16[16,3712]{1,0:T(8,128)(2,1)S(1)} %get-tuple-element.35), channel_id=1, source_target_pairs={{0,4},{1,5},{2,6},{3,7},{4,12},{5,13},{6,14},{7,15},{8,0},{9,1},{1... | collective-permute-start | bytes 356360 | tf_op jit(solution)/shard_map/ppermute | solution.py:306
  18.2 8.4 %collective-permute-start.3 = (bf16[16,3712]{1,0:T(8,128)(2,1)S(1)}, bf16[16,3712]{1,0:T(8,128)(2,1)S(1)}, u32[]{:S(2)}, u32[]{:S(2)}) collective-permute-start(bf16[16,3712]{1,0:T(8,128)(2,1)S(1)} %get-tuple-element.36), channel_id=1, source_target_pairs={{0,6},{1,7},{2,4},{3,5},{4,14},{5,15},{6,12},{7,13},{8,2},{9,3},{1... | collective-permute-start | bytes 356360 | tf_op jit(solution)/shard_map/ppermute | solution.py:306
  22.3 4.8 %collective-permute-start.6 = (bf16[16,3712]{1,0:T(8,128)(2,1)S(1)}, bf16[16,3712]{1,0:T(8,128)(2,1)S(1)}, u32[]{:S(2)}, u32[]{:S(2)}) collective-permute-start(bf16[16,3712]{1,0:T(8,128)(2,1)S(1)} %get-tuple-element.41), channel_id=1, source_target_pairs={{0,8},{1,9},{2,10},{3,11},{4,0},{5,1},{6,2},{7,3},{8,12},{9,13},{1... | collective-permute-start | bytes 356360 | tf_op jit(solution)/shard_map/ppermute | solution.py:306
  30.6 7.6 %collective-permute-start.13 = (bf16[16,3712]{1,0:T(8,128)(2,1)S(1)}, bf16[16,3712]{1,0:T(8,128)(2,1)S(1)}, u32[]{:S(2)}, u32[]{:S(2)}) collective-permute-start(bf16[16,3712]{1,0:T(8,128)(2,1)S(1)} %get-tuple-element.50), channel_id=1, source_target_pairs={{0,6},{1,7},{2,4},{3,5},{4,14},{5,15},{6,12},{7,13},{8,2},{9,3},{1... | collective-permute-start | bytes 356360 | tf_op jit(solution)/shard_map/ppermute | solution.py:306
  32.3 7.5 %collective-permute-start.14 = (bf16[16,3712]{1,0:T(8,128)(2,1)S(1)}, bf16[16,3712]{1,0:T(8,128)(2,1)S(1)}, u32[]{:S(2)}, u32[]{:S(2)}) collective-permute-start(bf16[16,3712]{1,0:T(8,128)(2,1)S(1)} %get-tuple-element.51), channel_id=1, source_target_pairs={{0,2},{1,3},{2,0},{3,1},{4,6},{5,7},{6,4},{7,5},{8,10},{9,11},{10,... | collective-permute-start | bytes 356360 | tf_op jit(solution)/shard_map/ppermute | solution.py:306
  33.4 6.8 %collective-permute-start.15 = (bf16[16,3712]{1,0:T(8,128)(2,1)S(1)}, bf16[16,3712]{1,0:T(8,128)(2,1)S(1)}, u32[]{:S(2)}, u32[]{:S(2)}) collective-permute-start(bf16[16,3712]{1,0:T(8,128)(2,1)S(1)} %get-tuple-element.52), channel_id=1, source_target_pairs={{0,4},{1,5},{2,6},{3,7},{4,12},{5,13},{6,14},{7,15},{8,0},{9,1},{1... | collective-permute-start | bytes 356360 | tf_op jit(solution)/shard_map/ppermute | solution.py:306
  34.9 14.6 %collective-permute-start.10 = (bf16[16,3712]{1,0:T(8,128)(2,1)S(1)}, bf16[16,3712]{1,0:T(8,128)(2,1)S(1)}, u32[]{:S(2)}, u32[]{:S(2)}) collective-permute-start(bf16[16,3712]{1,0:T(8,128)(2,1)S(1)} %get-tuple-element.45), channel_id=1, source_target_pairs={{0,18},{1,19},{2,16},{3,17},{4,22},{5,23},{6,20},{7,21},{8,26},{9,... | collective-permute-start | bytes 356360 | tf_op jit(solution)/shard_map/ppermute | solution.py:306
  37.1 12.4 %collective-permute-start.11 = (bf16[16,3712]{1,0:T(8,128)(2,1)S(1)}, bf16[16,3712]{1,0:T(8,128)(2,1)S(1)}, u32[]{:S(2)}, u32[]{:S(2)}) collective-permute-start(bf16[16,3712]{1,0:T(8,128)(2,1)S(1)} %get-tuple-element.46), channel_id=1, source_target_pairs={{0,24},{1,25},{2,26},{3,27},{4,16},{5,17},{6,18},{7,19},{8,28},{9,... | collective-permute-start | bytes 356360 | tf_op jit(solution)/shard_map/ppermute | solution.py:306
  38.2 11.7 %collective-permute-start.9 = (bf16[16,3712]{1,0:T(8,128)(2,1)S(1)}, bf16[16,3712]{1,0:T(8,128)(2,1)S(1)}, u32[]{:S(2)}, u32[]{:S(2)}) collective-permute-start(bf16[16,3712]{1,0:T(8,128)(2,1)S(1)} %get-tuple-element.44), channel_id=1, source_target_pairs={{0,16},{1,17},{2,18},{3,19},{4,20},{5,21},{6,22},{7,23},{8,24},{9,... | collective-permute-start | bytes 356360 | tf_op jit(solution)/shard_map/ppermute | solution.py:306
  40.6 16.0 %collective-permute-start.16 = (bf16[32,3584]{1,0:T(8,128)(2,1)S(1)}, bf16[32,3584]{1,0:T(8,128)(2,1)S(1)}, u32[]{:S(2)}, u32[]{:S(2)}) collective-permute-start(bf16[32,3584]{1,0:T(8,128)(2,1)S(1)} %combine.2), channel_id=1, source_target_pairs={{0,20},{1,21},{2,22},{3,23},{4,28},{5,29},{6,30},{7,31},{8,16},{9,... | collective-permute-start | bytes 688136 | tf_op jit(solution)/shard_map/ppermute | solution.py:306
  50.0 6.6 %collective-permute-start.12 = (bf16[16,3712]{1,0:T(8,128)(2,1)S(1)}, bf16[16,3712]{1,0:T(8,128)(2,1)S(1)}, u32[]{:S(2)}, u32[]{:S(2)}) collective-permute-start(bf16[16,3712]{1,0:T(8,128)(2,1)S(1)} %get-tuple-element.48), channel_id=1, source_target_pairs={{0,26},{1,27},{2,24},{3,25},{4,18},{5,19},{6,16},{7,17},{8,30},{9,... | collective-permute-start | bytes 356360 | tf_op jit(solution)/shard_map/ppermute | solution.py:306

commit v24 on v20

--- a/solution.py
+++ b/solution.py
@@ -339,15 +339,16 @@
     slots, total = near_pass(pieces, near)
     pieces = far_pass(slots, total, (far_in, far_out), capacity)
     piece = dict(zip(places, pieces))
-    merged = [
-        piece[3, 0],
+    first = [
         sent(piece[2, 0], sections, 0, 1, 0),
         sent(piece[2, 1], sections, 0, 1, 1),
         sent(piece[3, 1], sections, 0, 0, 1),
+        sent(piece[0, 1], sections, 1, 0, 1),
+        sent(piece[1, 0], sections, 1, -1, 0),
     ]
-    straight = [sent(piece[0, flip], sections, 1, 0, flip) for flip in range(2)]
-    merged, straight = lax.optimization_barrier((merged, straight))
-    straight += [sent(piece[1, flip], sections, 1, -1, flip) for flip in range(2)]
+    *merged, zero, one = lax.optimization_barrier(first)
+    merged.append(piece[3, 0])
+    straight = [zero, one, sent(piece[1, 1], sections, 1, -1, 1), sent(piece[0, 0], sections, 1, 0, 0)]
     merged = sent(combine(merged, tok_count), sections, 1, 1, 0)
     return combine(straight, tok_count, merged)[None]
 

time: 54.9 us -> 56.5 us (1.029)
  waiting for transfers between devices: 16.6 us -> 18.2 us
    ppermute x15, waiting for transfers between devices: 16.6 us -> 18.2 us  [sent(): return lax.ppermute(shard, ('section', 'expert'), pairs)]
where the time goes in v24:
time: 56.5 us; the launch traced here: 56.3 us
  starting transfers between devices  25.8 us (46%)
  waiting for transfers between devices  18.2 us (32%)
  Pallas kernels  7.58 us (13%)
  local copies, waits for them, and re-layouts  4.62 us (8%)
    ppermute x15, starting transfers between devices, sent(): return lax.ppermute(shard, ('section', 'expert'), pairs)  25.3 us
    ppermute x15, waiting for transfers between devices, sent(): return lax.ppermute(shard, ('section', 'expert'), pairs)  18.2 us
    pallas_call x9, Pallas kernels, local_call(): pl.pallas_call(kernel, out_shape=out_shape, in_specs=[vmem if spec is Non...  7.58 us
    unnamed x4, local copies, waits for them, and re-layouts  4.62 us
  transfers between devices with their start and end apart: 17, of which 10 were waited for; matrix products, arithmetic and copies ran while one was open for 0% of the time, Pallas kernels for 8%

profile of v24, /device:TPU:0, one launch (start us, length us, event | category | flops | bytes accessed | tf_op | source)
XLA Modules:
  0.0 56.3 jit_solution(7539923073001937074)
XLA Ops:
  1.5 3.1 %collective-permute-start.1 = (bf16[32,3712]{1,0:T(8,128)(2,1)S(1)}, bf16[32,3712]{1,0:T(8,128)(2,1)S(1)}, u32[]{:S(2)}, u32[]{:S(2)}) collective-permute-start(bf16[32,3712]{1,0:T(8,128)(2,1)S(1)} %prepare.1.block), channel_id=1, source_target_pairs={{0,4},{1,5},{2,6},{3,7},{4,12},{5,13},{6,14},{7,15},{8,0},{9,1},{1... | collective-permute-start | bytes 712712 | tf_op jit(solution)/shard_map/ppermute | solution.py:306
  5.0 1.6 %collective-permute-start = (bf16[16,3712]{1,0:T(8,128)(2,1)S(1)}, bf16[16,3712]{1,0:T(8,128)(2,1)S(1)}, u32[]{:S(2)}, u32[]{:S(2)}) collective-permute-start(bf16[16,3712]{1,0:T(8,128)(2,1)S(1)} %get-tuple-element.34), channel_id=1, source_target_pairs={{0,2},{1,3},{2,0},{3,1},{4,6},{5,7},{6,4},{7,5},{8,10},{9,11},{10,... | collective-permute-start | bytes 356360 | tf_op jit(solution)/shard_map/ppermute | solution.py:306
  6.6 3.1 %copy-done = bf16[1,3584,1024]{2,1,0:T(8,128)(2,1)S(1)} copy-done((bf16[1,3584,1024]{2,1,0:T(8,128)(2,1)S(1)}, bf16[1,3584,1024]{2,1,0:T(8,128)(2,1)}, u32[]{:S(2)}) %copy-start) | copy-done | bytes 7340056
  10.2 1.5 %copy-done.1 = bf16[1,512,3584]{2,1,0:T(8,128)(2,1)S(1)} copy-done((bf16[1,512,3584]{2,1,0:T(8,128)(2,1)S(1)}, bf16[1,512,3584]{2,1,0:T(8,128)(2,1)}, u32[]{:S(2)}) %copy-start.1) | copy-done | bytes 3670040
  12.0 1.0 %collective-permute-start.5 = (bf16[16,3712]{1,0:T(8,128)(2,1)S(1)}, bf16[16,3712]{1,0:T(8,128)(2,1)S(1)}, u32[]{:S(2)}, u32[]{:S(2)}) collective-permute-start(bf16[16,3712]{1,0:T(8,128)(2,1)S(1)} %get-tuple-element.44), channel_id=1, source_target_pairs={{0,10},{1,11},{2,8},{3,9},{4,2},{5,3},{6,0},{7,1},{8,14},{9,15},{1... | collective-permute-start | bytes 356360 | tf_op jit(solution)/shard_map/ppermute | solution.py:306
  13.5 1.9 %collective-permute-start.4 = (bf16[16,3712]{1,0:T(8,128)(2,1)S(1)}, bf16[16,3712]{1,0:T(8,128)(2,1)S(1)}, u32[]{:S(2)}, u32[]{:S(2)}) collective-permute-start(bf16[16,3712]{1,0:T(8,128)(2,1)S(1)} %get-tuple-element.41), channel_id=1, source_target_pairs={{0,2},{1,3},{2,0},{3,1},{4,6},{5,7},{6,4},{7,5},{8,10},{9,11},{10,... | collective-permute-start | bytes 356360 | tf_op jit(solution)/shard_map/ppermute | solution.py:306
  16.0 2.2 %collective-permute-done.5.refs_7_ = bf16[16,3712]{1,0:T(8,128)(2,1)S(1)} collective-permute-done((bf16[16,3712]{1,0:T(8,128)(2,1)S(1)}, bf16[16,3712]{1,0:T(8,128)(2,1)S(1)}, u32[]{:S(2)}, u32[]{:S(2)}) %collective-permute-start.5) | collective-permute-done | bytes 118816 | tf_op jit(solution)/shard_map/ppermute | solution.py:306
  18.2 4.1 %collective-permute-start.3 = (bf16[16,3712]{1,0:T(8,128)(2,1)S(1)}, bf16[16,3712]{1,0:T(8,128)(2,1)S(1)}, u32[]{:S(2)}, u32[]{:S(2)}) collective-permute-start(bf16[16,3712]{1,0:T(8,128)(2,1)S(1)} %get-tuple-element.40), channel_id=1, source_target_pairs={{0,6},{1,7},{2,4},{3,5},{4,14},{5,15},{6,12},{7,13},{8,2},{9,3},{1... | collective-permute-start | bytes 356360 | tf_op jit(solution)/shard_map/ppermute | solution.py:306
  23.0 3.6 %collective-permute-done.3.refs_4_ = bf16[16,3712]{1,0:T(8,128)(2,1)S(1)} collective-permute-done((bf16[16,3712]{1,0:T(8,128)(2,1)S(1)}, bf16[16,3712]{1,0:T(8,128)(2,1)S(1)}, u32[]{:S(2)}, u32[]{:S(2)}) %collective-permute-start.3) | collective-permute-done | bytes 118816 | tf_op jit(solution)/shard_map/ppermute | solution.py:306
  27.1 1.7 %near_pass.1 = (bf16[128,3712]{1,0:T(8,128)(2,1)S(1)}, f32[128,3584]{1,0:T(8,128)S(1)}) custom-call(bf16[16,3712]{1,0:T(8,128)(2,1)S(1)} %get-tuple-element.33.refs_0_, bf16[16,3712]{1,0:T(8,128)(2,1)S(1)} %collective-permute-done.refs_1_, bf16[16,3712]{1,0:T(8,128)(2,1)S(1)} %get-tuple-element.38.refs_2_, ...), custom_call_target="tpu_custom_call" | custom-call | bytes 11010048 | tf_op jit(solution)/shard_map/near_pass/pallas_call | solution.py:84
  28.9 1.7 %far_pass.1 = (bf16[16,3712]{1,0:T(8,128)(2,1)S(1)}, bf16[16,3712]{1,0:T(8,128)(2,1)S(1)}, bf16[16,3712]{1,0:T(8,128)(2,1)S(1)}, bf16[16,3712]{1,0:T(8,128)(2,1)...) custom-call(bf16[128,3712]{1,0:T(8,128)(2,1)S(1)} %get-tuple-element, ...), custom_call_target="tpu_custom_call" | custom-call | bytes 11010048 | tf_op jit(solution)/shard_map/far_pass/pallas_call | solution.py:84
  30.6 1.6 %collective-permute-start.10 = (bf16[16,3712]{1,0:T(8,128)(2,1)S(1)}, bf16[16,3712]{1,0:T(8,128)(2,1)S(1)}, u32[]{:S(2)}, u32[]{:S(2)}) collective-permute-start(bf16[16,3712]{1,0:T(8,128)(2,1)S(1)} %get-tuple-element.49), channel_id=1, source_target_pairs={{0,6},{1,7},{2,4},{3,5},{4,14},{5,15},{6,12},{7,13},{8,2},{9,3},{1... | collective-permute-start | bytes 356360 | tf_op jit(solution)/shard_map/ppermute | solution.py:306
  32.3 1.1 %collective-permute-start.11 = (bf16[16,3712]{1,0:T(8,128)(2,1)S(1)}, bf16[16,3712]{1,0:T(8,128)(2,1)S(1)}, u32[]{:S(2)}, u32[]{:S(2)}) collective-permute-start(bf16[16,3712]{1,0:T(8,128)(2,1)S(1)} %get-tuple-element.50), channel_id=1, source_target_pairs={{0,2},{1,3},{2,0},{3,1},{4,6},{5,7},{6,4},{7,5},{8,10},{9,11},{10,... | collective-permute-start | bytes 356360 | tf_op jit(solution)/shard_map/ppermute | solution.py:306
  33.4 1.8 %collective-permute-start.12 = (bf16[16,3712]{1,0:T(8,128)(2,1)S(1)}, bf16[16,3712]{1,0:T(8,128)(2,1)S(1)}, u32[]{:S(2)}, u32[]{:S(2)}) collective-permute-start(bf16[16,3712]{1,0:T(8,128)(2,1)S(1)} %get-tuple-element.51), channel_id=1, source_target_pairs={{0,18},{1,19},{2,16},{3,17},{4,22},{5,23},{6,20},{7,21},{8,26},{9,... | collective-permute-start | bytes 356360 | tf_op jit(solution)/shard_map/ppermute | solution.py:306
  35.2 2.6 %collective-permute-start.13 = (bf16[16,3712]{1,0:T(8,128)(2,1)S(1)}, bf16[16,3712]{1,0:T(8,128)(2,1)S(1)}, u32[]{:S(2)}, u32[]{:S(2)}) collective-permute-start(bf16[16,3712]{1,0:T(8,128)(2,1)S(1)} %get-tuple-element.52), channel_id=1, source_target_pairs={{0,24},{1,25},{2,26},{3,27},{4,16},{5,17},{6,18},{7,19},{8,28},{9,... | collective-permute-start | bytes 356360 | tf_op jit(solution)/shard_map/ppermute | solution.py:306
  37.9 2.7 %collective-permute-done.11.refs_2_ = bf16[16,3712]{1,0:T(8,128)(2,1)S(1)} collective-permute-done((bf16[16,3712]{1,0:T(8,128)(2,1)S(1)}, bf16[16,3712]{1,0:T(8,128)(2,1)S(1)}, u32[]{:S(2)}, u32[]{:S(2)}) %collective-permute-start.11) | collective-permute-done | bytes 118816 | tf_op jit(solution)/shard_map/ppermute | solution.py:306
  40.5 1.9 %collective-permute-done.13.refs_1_ = bf16[16,3712]{1,0:T(8,128)(2,1)S(1)} collective-permute-done((bf16[16,3712]{1,0:T(8,128)(2,1)S(1)}, bf16[16,3712]{1,0:T(8,128)(2,1)S(1)}, u32[]{:S(2)}, u32[]{:S(2)}) %collective-permute-start.13) | collective-permute-done | bytes 118816 | tf_op jit(solution)/shard_map/ppermute | solution.py:306
  42.4 1.2 %collective-permute-done.9.refs_0_ = bf16[16,3712]{1,0:T(8,128)(2,1)S(1)} collective-permute-done((bf16[16,3712]{1,0:T(8,128)(2,1)S(1)}, bf16[16,3712]{1,0:T(8,128)(2,1)S(1)}, u32[]{:S(2)}, u32[]{:S(2)}) %collective-permute-start.9) | collective-permute-done | bytes 118816 | tf_op jit(solution)/shard_map/ppermute | solution.py:306
  44.0 1.4 %collective-permute-start.16 = (bf16[32,3584]{1,0:T(8,128)(2,1)S(1)}, bf16[32,3584]{1,0:T(8,128)(2,1)S(1)}, u32[]{:S(2)}, u32[]{:S(2)}) collective-permute-start(bf16[32,3584]{1,0:T(8,128)(2,1)S(1)} %combine.2), channel_id=1, source_target_pairs={{0,20},{1,21},{2,22},{3,23},{4,28},{5,29},{6,30},{7,31},{8,16},{9,... | collective-permute-start | bytes 688136 | tf_op jit(solution)/shard_map/ppermute | solution.py:306
  45.4 2.6 %collective-permute-start.14 = (bf16[16,3712]{1,0:T(8,128)(2,1)S(1)}, bf16[16,3712]{1,0:T(8,128)(2,1)S(1)}, u32[]{:S(2)}, u32[]{:S(2)}) collective-permute-start(bf16[16,3712]{1,0:T(8,128)(2,1)S(1)} %get-tuple-element.55), channel_id=1, source_target_pairs={{0,26},{1,27},{2,24},{3,25},{4,18},{5,19},{6,16},{7,17},{8,30},{9,... | collective-permute-start | bytes 356360 | tf_op jit(solution)/shard_map/ppermute | solution.py:306
  48.0 1.5 %collective-permute-start.15 = (bf16[16,3712]{1,0:T(8,128)(2,1)S(1)}, bf16[16,3712]{1,0:T(8,128)(2,1)S(1)}, u32[]{:S(2)}, u32[]{:S(2)}) collective-permute-start(bf16[16,3712]{1,0:T(8,128)(2,1)S(1)} %get-tuple-element.56), channel_id=1, source_target_pairs={{0,16},{1,17},{2,18},{3,19},{4,20},{5,21},{6,22},{7,23},{8,24},{9,... | collective-permute-start | bytes 356360 | tf_op jit(solution)/shard_map/ppermute | solution.py:306
  49.5 4.3 %collective-permute-done.14.refs_2_ = bf16[16,3712]{1,0:T(8,128)(2,1)S(1)} collective-permute-done((bf16[16,3712]{1,0:T(8,128)(2,1)S(1)}, bf16[16,3712]{1,0:T(8,128)(2,1)S(1)}, u32[]{:S(2)}, u32[]{:S(2)}) %collective-permute-start.14) | collective-permute-done | bytes 118816 | tf_op jit(solution)/shard_map/ppermute | solution.py:306
  53.9 1.3 %collective-permute-done.15.refs_3_ = bf16[16,3712]{1,0:T(8,128)(2,1)S(1)} collective-permute-done((bf16[16,3712]{1,0:T(8,128)(2,1)S(1)}, bf16[16,3712]{1,0:T(8,128)(2,1)S(1)}, u32[]{:S(2)}, u32[]{:S(2)}) %collective-permute-start.15) | collective-permute-done | bytes 118816 | tf_op jit(solution)/shard_map/ppermute | solution.py:306
  55.2 1.1 %combine.3 = bf16[32,3584]{1,0:T(8,128)(2,1)} custom-call(bf16[16,3712]{1,0:T(8,128)(2,1)S(1)} %collective-permute-done.12.refs_0_, bf16[16,3712]{1,0:T(8,128)(2,1)S(1)} %collective-permute-done.13.refs_1_, bf16[16,3712]{1,0:T(8,128)(2,1)S(1)} %collective-permute-done.14.refs_2_, bf16[16,3712]{1,0:T(8,128)(2,1)S(1)} %collective-permute-done.15.refs_3_, ...), custom_call_target="tpu_custom_call" | custom-call | tf_op jit(solution)/shard_map/combine/pallas_call | solution.py:84
  (23 shorter events, 5.6 us)
Async XLA Ops:
  0.0 28.9 %collective-permute-start.7 = (bf16[3584,1024]{1,0:T(8,128)(2,1)}, bf16[3584,1024]{1,0:T(8,128)(2,1)S(1)}, u32[]{:S(2)}, u32[]{:S(2)}) collective-permute-start(bf16[3584,1024]{1,0:T(8,128)(2,1)} %bitcast.10), channel_id=1, source_target_pairs={{0,1},{1,0},{2,3},{3,2},{4,5},{5,4},{6,7},{7,6},{8,9},{9,8},{10,11... | collective-permute-start | bytes 22020104 | tf_op jit(solution)/shard_map/ppermute | solution.py:324
  0.5 28.4 %collective-permute-start.8 = (bf16[512,3584]{1,0:T(8,128)(2,1)}, bf16[512,3584]{1,0:T(8,128)(2,1)S(1)}, u32[]{:S(2)}, u32[]{:S(2)}) collective-permute-start(bf16[512,3584]{1,0:T(8,128)(2,1)} %bitcast.12), channel_id=1, source_target_pairs={{0,1},{1,0},{2,3},{3,2},{4,5},{5,4},{6,7},{7,6},{8,9},{9,8},{10,11... | collective-permute-start | bytes 11010056 | tf_op jit(solution)/shard_map/ppermute | solution.py:323
  1.5 11.5 %collective-permute-start.1 = (bf16[32,3712]{1,0:T(8,128)(2,1)S(1)}, bf16[32,3712]{1,0:T(8,128)(2,1)S(1)}, u32[]{:S(2)}, u32[]{:S(2)}) collective-permute-start(bf16[32,3712]{1,0:T(8,128)(2,1)S(1)} %prepare.1.block), channel_id=1, source_target_pairs={{0,4},{1,5},{2,6},{3,7},{4,12},{5,13},{6,14},{7,15},{8,0},{9,1},{1... | collective-permute-start | bytes 712712 | tf_op jit(solution)/shard_map/ppermute | solution.py:306
  5.0 7.0 %collective-permute-start = (bf16[16,3712]{1,0:T(8,128)(2,1)S(1)}, bf16[16,3712]{1,0:T(8,128)(2,1)S(1)}, u32[]{:S(2)}, u32[]{:S(2)}) collective-permute-start(bf16[16,3712]{1,0:T(8,128)(2,1)S(1)} %get-tuple-element.34), channel_id=1, source_target_pairs={{0,2},{1,3},{2,0},{3,1},{4,6},{5,7},{6,4},{7,5},{8,10},{9,11},{10,... | collective-permute-start | bytes 356360 | tf_op jit(solution)/shard_map/ppermute | solution.py:306
  6.6 3.1 %copy-start = (bf16[1,3584,1024]{2,1,0:T(8,128)(2,1)S(1)}, bf16[1,3584,1024]{2,1,0:T(8,128)(2,1)}, u32[]{:S(2)}) copy-start(bf16[1,3584,1024]{2,1,0:T(8,128)(2,1)} %param.8) | copy-start | bytes 22020100
  9.7 2.0 %copy-start.1 = (bf16[1,512,3584]{2,1,0:T(8,128)(2,1)S(1)}, bf16[1,512,3584]{2,1,0:T(8,128)(2,1)}, u32[]{:S(2)}) copy-start(bf16[1,512,3584]{2,1,0:T(8,128)(2,1)} %param.9) | copy-start | bytes 11010052
  12.0 6.2 %collective-permute-start.5 = (bf16[16,3712]{1,0:T(8,128)(2,1)S(1)}, bf16[16,3712]{1,0:T(8,128)(2,1)S(1)}, u32[]{:S(2)}, u32[]{:S(2)}) collective-permute-start(bf16[16,3712]{1,0:T(8,128)(2,1)S(1)} %get-tuple-element.44), channel_id=1, source_target_pairs={{0,10},{1,11},{2,8},{3,9},{4,2},{5,3},{6,0},{7,1},{8,14},{9,15},{1... | collective-permute-start | bytes 356360 | tf_op jit(solution)/shard_map/ppermute | solution.py:306
  13.5 8.9 %collective-permute-start.4 = (bf16[16,3712]{1,0:T(8,128)(2,1)S(1)}, bf16[16,3712]{1,0:T(8,128)(2,1)S(1)}, u32[]{:S(2)}, u32[]{:S(2)}) collective-permute-start(bf16[16,3712]{1,0:T(8,128)(2,1)S(1)} %get-tuple-element.41), channel_id=1, source_target_pairs={{0,2},{1,3},{2,0},{3,1},{4,6},{5,7},{6,4},{7,5},{8,10},{9,11},{10,... | collective-permute-start | bytes 356360 | tf_op jit(solution)/shard_map/ppermute | solution.py:306
  15.4 7.6 %collective-permute-start.2 = (bf16[16,3712]{1,0:T(8,128)(2,1)S(1)}, bf16[16,3712]{1,0:T(8,128)(2,1)S(1)}, u32[]{:S(2)}, u32[]{:S(2)}) collective-permute-start(bf16[16,3712]{1,0:T(8,128)(2,1)S(1)} %get-tuple-element.39), channel_id=1, source_target_pairs={{0,4},{1,5},{2,6},{3,7},{4,12},{5,13},{6,14},{7,15},{8,0},{9,1},{1... | collective-permute-start | bytes 356360 | tf_op jit(solution)/shard_map/ppermute | solution.py:306
  18.2 8.4 %collective-permute-start.3 = (bf16[16,3712]{1,0:T(8,128)(2,1)S(1)}, bf16[16,3712]{1,0:T(8,128)(2,1)S(1)}, u32[]{:S(2)}, u32[]{:S(2)}) collective-permute-start(bf16[16,3712]{1,0:T(8,128)(2,1)S(1)} %get-tuple-element.40), channel_id=1, source_target_pairs={{0,6},{1,7},{2,4},{3,5},{4,14},{5,15},{6,12},{7,13},{8,2},{9,3},{1... | collective-permute-start | bytes 356360 | tf_op jit(solution)/shard_map/ppermute | solution.py:306
  22.3 4.8 %collective-permute-start.6 = (bf16[16,3712]{1,0:T(8,128)(2,1)S(1)}, bf16[16,3712]{1,0:T(8,128)(2,1)S(1)}, u32[]{:S(2)}, u32[]{:S(2)}) collective-permute-start(bf16[16,3712]{1,0:T(8,128)(2,1)S(1)} %get-tuple-element.45), channel_id=1, source_target_pairs={{0,8},{1,9},{2,10},{3,11},{4,0},{5,1},{6,2},{7,3},{8,12},{9,13},{1... | collective-permute-start | bytes 356360 | tf_op jit(solution)/shard_map/ppermute | solution.py:306
  30.6 7.2 %collective-permute-start.10 = (bf16[16,3712]{1,0:T(8,128)(2,1)S(1)}, bf16[16,3712]{1,0:T(8,128)(2,1)S(1)}, u32[]{:S(2)}, u32[]{:S(2)}) collective-permute-start(bf16[16,3712]{1,0:T(8,128)(2,1)S(1)} %get-tuple-element.49), channel_id=1, source_target_pairs={{0,6},{1,7},{2,4},{3,5},{4,14},{5,15},{6,12},{7,13},{8,2},{9,3},{1... | collective-permute-start | bytes 356360 | tf_op jit(solution)/shard_map/ppermute | solution.py:306
  32.3 8.3 %collective-permute-start.11 = (bf16[16,3712]{1,0:T(8,128)(2,1)S(1)}, bf16[16,3712]{1,0:T(8,128)(2,1)S(1)}, u32[]{:S(2)}, u32[]{:S(2)}) collective-permute-start(bf16[16,3712]{1,0:T(8,128)(2,1)S(1)} %get-tuple-element.50), channel_id=1, source_target_pairs={{0,2},{1,3},{2,0},{3,1},{4,6},{5,7},{6,4},{7,5},{8,10},{9,11},{10,... | collective-permute-start | bytes 356360 | tf_op jit(solution)/shard_map/ppermute | solution.py:306
  33.4 7.2 %collective-permute-start.12 = (bf16[16,3712]{1,0:T(8,128)(2,1)S(1)}, bf16[16,3712]{1,0:T(8,128)(2,1)S(1)}, u32[]{:S(2)}, u32[]{:S(2)}) collective-permute-start(bf16[16,3712]{1,0:T(8,128)(2,1)S(1)} %get-tuple-element.51), channel_id=1, source_target_pairs={{0,18},{1,19},{2,16},{3,17},{4,22},{5,23},{6,20},{7,21},{8,26},{9,... | collective-permute-start | bytes 356360 | tf_op jit(solution)/shard_map/ppermute | solution.py:306
  35.2 7.2 %collective-permute-start.13 = (bf16[16,3712]{1,0:T(8,128)(2,1)S(1)}, bf16[16,3712]{1,0:T(8,128)(2,1)S(1)}, u32[]{:S(2)}, u32[]{:S(2)}) collective-permute-start(bf16[16,3712]{1,0:T(8,128)(2,1)S(1)} %get-tuple-element.52), channel_id=1, source_target_pairs={{0,24},{1,25},{2,26},{3,27},{4,16},{5,17},{6,18},{7,19},{8,28},{9,... | collective-permute-start | bytes 356360 | tf_op jit(solution)/shard_map/ppermute | solution.py:306
  37.8 5.8 %collective-permute-start.9 = (bf16[16,3712]{1,0:T(8,128)(2,1)S(1)}, bf16[16,3712]{1,0:T(8,128)(2,1)S(1)}, u32[]{:S(2)}, u32[]{:S(2)}) collective-permute-start(bf16[16,3712]{1,0:T(8,128)(2,1)S(1)} %get-tuple-element.48), channel_id=1, source_target_pairs={{0,4},{1,5},{2,6},{3,7},{4,12},{5,13},{6,14},{7,15},{8,0},{9,1},{1... | collective-permute-start | bytes 356360 | tf_op jit(solution)/shard_map/ppermute | solution.py:306
  44.0 11.2 %collective-permute-start.16 = (bf16[32,3584]{1,0:T(8,128)(2,1)S(1)}, bf16[32,3584]{1,0:T(8,128)(2,1)S(1)}, u32[]{:S(2)}, u32[]{:S(2)}) collective-permute-start(bf16[32,3584]{1,0:T(8,128)(2,1)S(1)} %combine.2), channel_id=1, source_target_pairs={{0,20},{1,21},{2,22},{3,23},{4,28},{5,29},{6,30},{7,31},{8,16},{9,... | collective-permute-start | bytes 688136 | tf_op jit(solution)/shard_map/ppermute | solution.py:306
  45.4 8.5 %collective-permute-start.14 = (bf16[16,3712]{1,0:T(8,128)(2,1)S(1)}, bf16[16,3712]{1,0:T(8,128)(2,1)S(1)}, u32[]{:S(2)}, u32[]{:S(2)}) collective-permute-start(bf16[16,3712]{1,0:T(8,128)(2,1)S(1)} %get-tuple-element.55), channel_id=1, source_target_pairs={{0,26},{1,27},{2,24},{3,25},{4,18},{5,19},{6,16},{7,17},{8,30},{9,... | collective-permute-start | bytes 356360 | tf_op jit(solution)/shard_map/ppermute | solution.py:306
  48.0 7.2 %collective-permute-start.15 = (bf16[16,3712]{1,0:T(8,128)(2,1)S(1)}, bf16[16,3712]{1,0:T(8,128)(2,1)S(1)}, u32[]{:S(2)}, u32[]{:S(2)}) collective-permute-start(bf16[16,3712]{1,0:T(8,128)(2,1)S(1)} %get-tuple-element.56), channel_id=1, source_target_pairs={{0,16},{1,17},{2,18},{3,19},{4,20},{5,21},{6,22},{7,23},{8,24},{9,... | collective-permute-start | bytes 356360 | tf_op jit(solution)/shard_map/ppermute | solution.py:306

commit v25 on v20

--- a/solution.py
+++ b/solution.py
@@ -328,14 +328,14 @@
     other0 = sent(other, sections, 0, 0, 1)
     near = (loaded(after(w_in, own0)), loaded(after(w_out, own0)))
     block1 = after(block1, (near, other0))
-    own1, other, on0, on1 = choose(block1, capacity, ((0, 0), (0, 1), (1, 0), (1, 1)))
+    own1, other, on1, on0 = choose(block1, capacity, ((0, 0), (0, 1), (1, 1), (1, 0)))
     other1 = sent(other, sections, 0, 0, 1)
+    other2 = sent(on1, sections, 0, 1, 1)
     own2 = sent(on0, sections, 0, 1, 0)
-    other2 = sent(on1, sections, 0, 1, 1)
     other3 = sent(after(back1, (near, other0)), sections, 0, 3, 1)
     own3 = sent(after(back0, (other1, other3)), sections, 0, 3, 0)
-    pieces = (own0, other0, own1, own2, other2, other1, own3, other3)
-    places = ((0, 0), (0, 1), (1, 0), (2, 0), (2, 1), (1, 1), (3, 0), (3, 1))
+    pieces = (own0, other0, own1, other2, own2, other1, own3, other3)
+    places = ((0, 0), (0, 1), (1, 0), (2, 1), (2, 0), (1, 1), (3, 0), (3, 1))
     slots, total = near_pass(pieces, near)
     pieces = far_pass(slots, total, (far_in, far_out), capacity)
     piece = dict(zip(places, pieces))

time: 54.9 us -> 57.2 us (1.042)
  starting transfers between devices: 25.8 us -> 27.2 us
  waiting for transfers between devices: 16.6 us -> 17.5 us
    ppermute x15, starting transfers between devices: 25.3 us -> 26.7 us  [sent(): return lax.ppermute(shard, ('section', 'expert'), pairs)]
    ppermute x15, waiting for transfers between devices: 16.6 us -> 17.5 us  [sent(): return lax.ppermute(shard, ('section', 'expert'), pairs)]
where the time goes in v25:
time: 57.2 us; the launch traced here: 57 us
  starting transfers between devices  27.2 us (48%)
  waiting for transfers between devices  17.5 us (31%)
  Pallas kernels  7.58 us (13%)
  local copies, waits for them, and re-layouts  4.62 us (8%)
    ppermute x15, starting transfers between devices, sent(): return lax.ppermute(shard, ('section', 'expert'), pairs)  26.7 us
    ppermute x15, waiting for transfers between devices, sent(): return lax.ppermute(shard, ('section', 'expert'), pairs)  17.5 us
    pallas_call x9, Pallas kernels, local_call(): pl.pallas_call(kernel, out_shape=out_shape, in_specs=[vmem if spec is Non...  7.58 us
    unnamed x4, local copies, waits for them, and re-layouts  4.62 us
  transfers between devices with their start and end apart: 17, of which 10 were waited for; matrix products, arithmetic and copies ran while one was open for 0% of the time, Pallas kernels for 8%

profile of v25, /device:TPU:0, one launch (start us, length us, event | category | flops | bytes accessed | tf_op | source)
XLA Modules:
  0.0 57.0 jit_solution(10055292843356975727)
XLA Ops:
  1.5 3.1 %collective-permute-start.1 = (bf16[32,3712]{1,0:T(8,128)(2,1)S(1)}, bf16[32,3712]{1,0:T(8,128)(2,1)S(1)}, u32[]{:S(2)}, u32[]{:S(2)}) collective-permute-start(bf16[32,3712]{1,0:T(8,128)(2,1)S(1)} %prepare.1.block), channel_id=1, source_target_pairs={{0,4},{1,5},{2,6},{3,7},{4,12},{5,13},{6,14},{7,15},{8,0},{9,1},{1... | collective-permute-start | bytes 712712 | tf_op jit(solution)/shard_map/ppermute | solution.py:306
  5.0 1.6 %collective-permute-start = (bf16[16,3712]{1,0:T(8,128)(2,1)S(1)}, bf16[16,3712]{1,0:T(8,128)(2,1)S(1)}, u32[]{:S(2)}, u32[]{:S(2)}) collective-permute-start(bf16[16,3712]{1,0:T(8,128)(2,1)S(1)} %get-tuple-element.35), channel_id=1, source_target_pairs={{0,2},{1,3},{2,0},{3,1},{4,6},{5,7},{6,4},{7,5},{8,10},{9,11},{10,... | collective-permute-start | bytes 356360 | tf_op jit(solution)/shard_map/ppermute | solution.py:306
  6.6 3.1 %copy-done = bf16[1,3584,1024]{2,1,0:T(8,128)(2,1)S(1)} copy-done((bf16[1,3584,1024]{2,1,0:T(8,128)(2,1)S(1)}, bf16[1,3584,1024]{2,1,0:T(8,128)(2,1)}, u32[]{:S(2)}) %copy-start) | copy-done | bytes 7340056
  10.2 1.5 %copy-done.1 = bf16[1,512,3584]{2,1,0:T(8,128)(2,1)S(1)} copy-done((bf16[1,512,3584]{2,1,0:T(8,128)(2,1)S(1)}, bf16[1,512,3584]{2,1,0:T(8,128)(2,1)}, u32[]{:S(2)}) %copy-start.1) | copy-done | bytes 3670040
  13.5 1.9 %collective-permute-start.4 = (bf16[16,3712]{1,0:T(8,128)(2,1)S(1)}, bf16[16,3712]{1,0:T(8,128)(2,1)S(1)}, u32[]{:S(2)}, u32[]{:S(2)}) collective-permute-start(bf16[16,3712]{1,0:T(8,128)(2,1)S(1)} %get-tuple-element.42), channel_id=1, source_target_pairs={{0,2},{1,3},{2,0},{3,1},{4,6},{5,7},{6,4},{7,5},{8,10},{9,11},{10,... | collective-permute-start | bytes 356360 | tf_op jit(solution)/shard_map/ppermute | solution.py:306
  15.4 1.3 %collective-permute-start.2 = (bf16[16,3712]{1,0:T(8,128)(2,1)S(1)}, bf16[16,3712]{1,0:T(8,128)(2,1)S(1)}, u32[]{:S(2)}, u32[]{:S(2)}) collective-permute-start(bf16[16,3712]{1,0:T(8,128)(2,1)S(1)} %get-tuple-element.40), channel_id=1, source_target_pairs={{0,6},{1,7},{2,4},{3,5},{4,14},{5,15},{6,12},{7,13},{8,2},{9,3},{1... | collective-permute-start | bytes 356360 | tf_op jit(solution)/shard_map/ppermute | solution.py:306
  16.6 1.2 %collective-permute-done.5.refs_7_ = bf16[16,3712]{1,0:T(8,128)(2,1)S(1)} collective-permute-done((bf16[16,3712]{1,0:T(8,128)(2,1)S(1)}, bf16[16,3712]{1,0:T(8,128)(2,1)S(1)}, u32[]{:S(2)}, u32[]{:S(2)}) %collective-permute-start.5) | collective-permute-done | bytes 118816 | tf_op jit(solution)/shard_map/ppermute | solution.py:306
  17.9 5.7 %collective-permute-start.3 = (bf16[16,3712]{1,0:T(8,128)(2,1)S(1)}, bf16[16,3712]{1,0:T(8,128)(2,1)S(1)}, u32[]{:S(2)}, u32[]{:S(2)}) collective-permute-start(bf16[16,3712]{1,0:T(8,128)(2,1)S(1)} %get-tuple-element.41), channel_id=1, source_target_pairs={{0,4},{1,5},{2,6},{3,7},{4,12},{5,13},{6,14},{7,15},{8,0},{9,1},{1... | collective-permute-start | bytes 356360 | tf_op jit(solution)/shard_map/ppermute | solution.py:306
  23.5 1.1 %collective-permute-start.6 = (bf16[16,3712]{1,0:T(8,128)(2,1)S(1)}, bf16[16,3712]{1,0:T(8,128)(2,1)S(1)}, u32[]{:S(2)}, u32[]{:S(2)}) collective-permute-start(bf16[16,3712]{1,0:T(8,128)(2,1)S(1)} %get-tuple-element.46), channel_id=1, source_target_pairs={{0,8},{1,9},{2,10},{3,11},{4,0},{5,1},{6,2},{7,3},{8,12},{9,13},{1... | collective-permute-start | bytes 356360 | tf_op jit(solution)/shard_map/ppermute | solution.py:306
  24.6 2.2 %collective-permute-done.3.refs_4_ = bf16[16,3712]{1,0:T(8,128)(2,1)S(1)} collective-permute-done((bf16[16,3712]{1,0:T(8,128)(2,1)S(1)}, bf16[16,3712]{1,0:T(8,128)(2,1)S(1)}, u32[]{:S(2)}, u32[]{:S(2)}) %collective-permute-start.3) | collective-permute-done | bytes 118816 | tf_op jit(solution)/shard_map/ppermute | solution.py:306
  26.8 1.6 %collective-permute-done.6.refs_6_ = bf16[16,3712]{1,0:T(8,128)(2,1)S(1)} collective-permute-done((bf16[16,3712]{1,0:T(8,128)(2,1)S(1)}, bf16[16,3712]{1,0:T(8,128)(2,1)S(1)}, u32[]{:S(2)}, u32[]{:S(2)}) %collective-permute-start.6) | collective-permute-done | bytes 118816 | tf_op jit(solution)/shard_map/ppermute | solution.py:306
  28.4 1.7 %near_pass.1 = (bf16[128,3712]{1,0:T(8,128)(2,1)S(1)}, f32[128,3584]{1,0:T(8,128)S(1)}) custom-call(bf16[16,3712]{1,0:T(8,128)(2,1)S(1)} %get-tuple-element.34.refs_0_, bf16[16,3712]{1,0:T(8,128)(2,1)S(1)} %collective-permute-done.refs_1_, bf16[16,3712]{1,0:T(8,128)(2,1)S(1)} %get-tuple-element.39.refs_2_, ...), custom_call_target="tpu_custom_call" | custom-call | bytes 11010048 | tf_op jit(solution)/shard_map/near_pass/pallas_call | solution.py:84
  30.1 1.7 %far_pass.1 = (bf16[16,3712]{1,0:T(8,128)(2,1)S(1)}, bf16[16,3712]{1,0:T(8,128)(2,1)S(1)}, bf16[16,3712]{1,0:T(8,128)(2,1)S(1)}, bf16[16,3712]{1,0:T(8,128)(2,1)...) custom-call(bf16[128,3712]{1,0:T(8,128)(2,1)S(1)} %get-tuple-element, ...), custom_call_target="tpu_custom_call" | custom-call | bytes 11010048 | tf_op jit(solution)/shard_map/far_pass/pallas_call | solution.py:84
  31.9 2.3 %collective-permute-start.10 = (bf16[16,3712]{1,0:T(8,128)(2,1)S(1)}, bf16[16,3712]{1,0:T(8,128)(2,1)S(1)}, u32[]{:S(2)}, u32[]{:S(2)}) collective-permute-start(bf16[16,3712]{1,0:T(8,128)(2,1)S(1)} %get-tuple-element.51), channel_id=1, source_target_pairs={{0,6},{1,7},{2,4},{3,5},{4,14},{5,15},{6,12},{7,13},{8,2},{9,3},{1... | collective-permute-start | bytes 356360 | tf_op jit(solution)/shard_map/ppermute | solution.py:306
  34.2 1.4 %collective-permute-start.11 = (bf16[16,3712]{1,0:T(8,128)(2,1)S(1)}, bf16[16,3712]{1,0:T(8,128)(2,1)S(1)}, u32[]{:S(2)}, u32[]{:S(2)}) collective-permute-start(bf16[16,3712]{1,0:T(8,128)(2,1)S(1)} %get-tuple-element.52), channel_id=1, source_target_pairs={{0,2},{1,3},{2,0},{3,1},{4,6},{5,7},{6,4},{7,5},{8,10},{9,11},{10,... | collective-permute-start | bytes 356360 | tf_op jit(solution)/shard_map/ppermute | solution.py:306
  35.6 1.5 %collective-permute-start.12 = (bf16[16,3712]{1,0:T(8,128)(2,1)S(1)}, bf16[16,3712]{1,0:T(8,128)(2,1)S(1)}, u32[]{:S(2)}, u32[]{:S(2)}) collective-permute-start(bf16[16,3712]{1,0:T(8,128)(2,1)S(1)} %get-tuple-element.53), channel_id=1, source_target_pairs={{0,16},{1,17},{2,18},{3,19},{4,20},{5,21},{6,22},{7,23},{8,24},{9,... | collective-permute-start | bytes 356360 | tf_op jit(solution)/shard_map/ppermute | solution.py:306
  37.7 2.1 %collective-permute-done.10.refs_2_ = bf16[16,3712]{1,0:T(8,128)(2,1)S(1)} collective-permute-done((bf16[16,3712]{1,0:T(8,128)(2,1)S(1)}, bf16[16,3712]{1,0:T(8,128)(2,1)S(1)}, u32[]{:S(2)}, u32[]{:S(2)}) %collective-permute-start.10) | collective-permute-done | bytes 118816 | tf_op jit(solution)/shard_map/ppermute | solution.py:306
  39.8 1.2 %collective-permute-done.11.refs_3_ = bf16[16,3712]{1,0:T(8,128)(2,1)S(1)} collective-permute-done((bf16[16,3712]{1,0:T(8,128)(2,1)S(1)}, bf16[16,3712]{1,0:T(8,128)(2,1)S(1)}, u32[]{:S(2)}, u32[]{:S(2)}) %collective-permute-start.11) | collective-permute-done | bytes 118816 | tf_op jit(solution)/shard_map/ppermute | solution.py:306
  41.0 1.8 %collective-permute-done.13.refs_1_ = bf16[16,3712]{1,0:T(8,128)(2,1)S(1)} collective-permute-done((bf16[16,3712]{1,0:T(8,128)(2,1)S(1)}, bf16[16,3712]{1,0:T(8,128)(2,1)S(1)}, u32[]{:S(2)}, u32[]{:S(2)}) %collective-permute-start.13) | collective-permute-done | bytes 118816 | tf_op jit(solution)/shard_map/ppermute | solution.py:306
  44.6 3.1 %collective-permute-start.14 = (bf16[16,3712]{1,0:T(8,128)(2,1)S(1)}, bf16[16,3712]{1,0:T(8,128)(2,1)S(1)}, u32[]{:S(2)}, u32[]{:S(2)}) collective-permute-start(bf16[16,3712]{1,0:T(8,128)(2,1)S(1)} %get-tuple-element.57), channel_id=1, source_target_pairs={{0,24},{1,25},{2,26},{3,27},{4,16},{5,17},{6,18},{7,19},{8,28},{9,... | collective-permute-start | bytes 356360 | tf_op jit(solution)/shard_map/ppermute | solution.py:306
  47.7 1.3 %collective-permute-start.15 = (bf16[16,3712]{1,0:T(8,128)(2,1)S(1)}, bf16[16,3712]{1,0:T(8,128)(2,1)S(1)}, u32[]{:S(2)}, u32[]{:S(2)}) collective-permute-start(bf16[16,3712]{1,0:T(8,128)(2,1)S(1)} %get-tuple-element.58), channel_id=1, source_target_pairs={{0,26},{1,27},{2,24},{3,25},{4,18},{5,19},{6,16},{7,17},{8,30},{9,... | collective-permute-start | bytes 356360 | tf_op jit(solution)/shard_map/ppermute | solution.py:306
  49.0 4.7 %collective-permute-done.14.refs_2_ = bf16[16,3712]{1,0:T(8,128)(2,1)S(1)} collective-permute-done((bf16[16,3712]{1,0:T(8,128)(2,1)S(1)}, bf16[16,3712]{1,0:T(8,128)(2,1)S(1)}, u32[]{:S(2)}, u32[]{:S(2)}) %collective-permute-start.14) | collective-permute-done | bytes 118816 | tf_op jit(solution)/shard_map/ppermute | solution.py:306
  53.7 1.4 %collective-permute-done.15.refs_3_ = bf16[16,3712]{1,0:T(8,128)(2,1)S(1)} collective-permute-done((bf16[16,3712]{1,0:T(8,128)(2,1)S(1)}, bf16[16,3712]{1,0:T(8,128)(2,1)S(1)}, u32[]{:S(2)}, u32[]{:S(2)}) %collective-permute-start.15) | collective-permute-done | bytes 118816 | tf_op jit(solution)/shard_map/ppermute | solution.py:306
  55.8 1.1 %combine.3 = bf16[32,3584]{1,0:T(8,128)(2,1)} custom-call(bf16[16,3712]{1,0:T(8,128)(2,1)S(1)} %collective-permute-done.12.refs_0_, bf16[16,3712]{1,0:T(8,128)(2,1)S(1)} %collective-permute-done.13.refs_1_, bf16[16,3712]{1,0:T(8,128)(2,1)S(1)} %collective-permute-done.14.refs_2_, bf16[16,3712]{1,0:T(8,128)(2,1)S(1)} %collective-permute-done.15.refs_3_, ...), custom_call_target="tpu_custom_call" | custom-call | tf_op jit(solution)/shard_map/combine/pallas_call | solution.py:84
  (23 shorter events, 7.3 us)
Async XLA Ops:
  0.0 30.1 %collective-permute-start.7 = (bf16[3584,1024]{1,0:T(8,128)(2,1)}, bf16[3584,1024]{1,0:T(8,128)(2,1)S(1)}, u32[]{:S(2)}, u32[]{:S(2)}) collective-permute-start(bf16[3584,1024]{1,0:T(8,128)(2,1)} %bitcast.10), channel_id=1, source_target_pairs={{0,1},{1,0},{2,3},{3,2},{4,5},{5,4},{6,7},{7,6},{8,9},{9,8},{10,11... | collective-permute-start | bytes 22020104 | tf_op jit(solution)/shard_map/ppermute | solution.py:324
  0.5 29.7 %collective-permute-start.8 = (bf16[512,3584]{1,0:T(8,128)(2,1)}, bf16[512,3584]{1,0:T(8,128)(2,1)S(1)}, u32[]{:S(2)}, u32[]{:S(2)}) collective-permute-start(bf16[512,3584]{1,0:T(8,128)(2,1)} %bitcast.12), channel_id=1, source_target_pairs={{0,1},{1,0},{2,3},{3,2},{4,5},{5,4},{6,7},{7,6},{8,9},{9,8},{10,11... | collective-permute-start | bytes 11010056 | tf_op jit(solution)/shard_map/ppermute | solution.py:323
  1.5 11.5 %collective-permute-start.1 = (bf16[32,3712]{1,0:T(8,128)(2,1)S(1)}, bf16[32,3712]{1,0:T(8,128)(2,1)S(1)}, u32[]{:S(2)}, u32[]{:S(2)}) collective-permute-start(bf16[32,3712]{1,0:T(8,128)(2,1)S(1)} %prepare.1.block), channel_id=1, source_target_pairs={{0,4},{1,5},{2,6},{3,7},{4,12},{5,13},{6,14},{7,15},{8,0},{9,1},{1... | collective-permute-start | bytes 712712 | tf_op jit(solution)/shard_map/ppermute | solution.py:306
  5.0 7.0 %collective-permute-start = (bf16[16,3712]{1,0:T(8,128)(2,1)S(1)}, bf16[16,3712]{1,0:T(8,128)(2,1)S(1)}, u32[]{:S(2)}, u32[]{:S(2)}) collective-permute-start(bf16[16,3712]{1,0:T(8,128)(2,1)S(1)} %get-tuple-element.35), channel_id=1, source_target_pairs={{0,2},{1,3},{2,0},{3,1},{4,6},{5,7},{6,4},{7,5},{8,10},{9,11},{10,... | collective-permute-start | bytes 356360 | tf_op jit(solution)/shard_map/ppermute | solution.py:306
  6.6 3.1 %copy-start = (bf16[1,3584,1024]{2,1,0:T(8,128)(2,1)S(1)}, bf16[1,3584,1024]{2,1,0:T(8,128)(2,1)}, u32[]{:S(2)}) copy-start(bf16[1,3584,1024]{2,1,0:T(8,128)(2,1)} %param.8) | copy-start | bytes 22020100
  9.7 2.0 %copy-start.1 = (bf16[1,512,3584]{2,1,0:T(8,128)(2,1)S(1)}, bf16[1,512,3584]{2,1,0:T(8,128)(2,1)}, u32[]{:S(2)}) copy-start(bf16[1,512,3584]{2,1,0:T(8,128)(2,1)} %param.9) | copy-start | bytes 11010052
  12.0 5.8 %collective-permute-start.5 = (bf16[16,3712]{1,0:T(8,128)(2,1)S(1)}, bf16[16,3712]{1,0:T(8,128)(2,1)S(1)}, u32[]{:S(2)}, u32[]{:S(2)}) collective-permute-start(bf16[16,3712]{1,0:T(8,128)(2,1)S(1)} %get-tuple-element.45), channel_id=1, source_target_pairs={{0,10},{1,11},{2,8},{3,9},{4,2},{5,3},{6,0},{7,1},{8,14},{9,15},{1... | collective-permute-start | bytes 356360 | tf_op jit(solution)/shard_map/ppermute | solution.py:306
  13.5 10.1 %collective-permute-start.4 = (bf16[16,3712]{1,0:T(8,128)(2,1)S(1)}, bf16[16,3712]{1,0:T(8,128)(2,1)S(1)}, u32[]{:S(2)}, u32[]{:S(2)}) collective-permute-start(bf16[16,3712]{1,0:T(8,128)(2,1)S(1)} %get-tuple-element.42), channel_id=1, source_target_pairs={{0,2},{1,3},{2,0},{3,1},{4,6},{5,7},{6,4},{7,5},{8,10},{9,11},{10,... | collective-permute-start | bytes 356360 | tf_op jit(solution)/shard_map/ppermute | solution.py:306
  15.4 9.2 %collective-permute-start.2 = (bf16[16,3712]{1,0:T(8,128)(2,1)S(1)}, bf16[16,3712]{1,0:T(8,128)(2,1)S(1)}, u32[]{:S(2)}, u32[]{:S(2)}) collective-permute-start(bf16[16,3712]{1,0:T(8,128)(2,1)S(1)} %get-tuple-element.40), channel_id=1, source_target_pairs={{0,6},{1,7},{2,4},{3,5},{4,14},{5,15},{6,12},{7,13},{8,2},{9,3},{1... | collective-permute-start | bytes 356360 | tf_op jit(solution)/shard_map/ppermute | solution.py:306
  17.9 8.9 %collective-permute-start.3 = (bf16[16,3712]{1,0:T(8,128)(2,1)S(1)}, bf16[16,3712]{1,0:T(8,128)(2,1)S(1)}, u32[]{:S(2)}, u32[]{:S(2)}) collective-permute-start(bf16[16,3712]{1,0:T(8,128)(2,1)S(1)} %get-tuple-element.41), channel_id=1, source_target_pairs={{0,4},{1,5},{2,6},{3,7},{4,12},{5,13},{6,14},{7,15},{8,0},{9,1},{1... | collective-permute-start | bytes 356360 | tf_op jit(solution)/shard_map/ppermute | solution.py:306
  23.5 4.8 %collective-permute-start.6 = (bf16[16,3712]{1,0:T(8,128)(2,1)S(1)}, bf16[16,3712]{1,0:T(8,128)(2,1)S(1)}, u32[]{:S(2)}, u32[]{:S(2)}) collective-permute-start(bf16[16,3712]{1,0:T(8,128)(2,1)S(1)} %get-tuple-element.46), channel_id=1, source_target_pairs={{0,8},{1,9},{2,10},{3,11},{4,0},{5,1},{6,2},{7,3},{8,12},{9,13},{1... | collective-permute-start | bytes 356360 | tf_op jit(solution)/shard_map/ppermute | solution.py:306
  31.9 7.9 %collective-permute-start.10 = (bf16[16,3712]{1,0:T(8,128)(2,1)S(1)}, bf16[16,3712]{1,0:T(8,128)(2,1)S(1)}, u32[]{:S(2)}, u32[]{:S(2)}) collective-permute-start(bf16[16,3712]{1,0:T(8,128)(2,1)S(1)} %get-tuple-element.51), channel_id=1, source_target_pairs={{0,6},{1,7},{2,4},{3,5},{4,14},{5,15},{6,12},{7,13},{8,2},{9,3},{1... | collective-permute-start | bytes 356360 | tf_op jit(solution)/shard_map/ppermute | solution.py:306
  34.2 6.8 %collective-permute-start.11 = (bf16[16,3712]{1,0:T(8,128)(2,1)S(1)}, bf16[16,3712]{1,0:T(8,128)(2,1)S(1)}, u32[]{:S(2)}, u32[]{:S(2)}) collective-permute-start(bf16[16,3712]{1,0:T(8,128)(2,1)S(1)} %get-tuple-element.52), channel_id=1, source_target_pairs={{0,2},{1,3},{2,0},{3,1},{4,6},{5,7},{6,4},{7,5},{8,10},{9,11},{10,... | collective-permute-start | bytes 356360 | tf_op jit(solution)/shard_map/ppermute | solution.py:306
  35.6 5.4 %collective-permute-start.12 = (bf16[16,3712]{1,0:T(8,128)(2,1)S(1)}, bf16[16,3712]{1,0:T(8,128)(2,1)S(1)}, u32[]{:S(2)}, u32[]{:S(2)}) collective-permute-start(bf16[16,3712]{1,0:T(8,128)(2,1)S(1)} %get-tuple-element.53), channel_id=1, source_target_pairs={{0,16},{1,17},{2,18},{3,19},{4,20},{5,21},{6,22},{7,23},{8,24},{9,... | collective-permute-start | bytes 356360 | tf_op jit(solution)/shard_map/ppermute | solution.py:306
  37.1 5.7 %collective-permute-start.13 = (bf16[16,3712]{1,0:T(8,128)(2,1)S(1)}, bf16[16,3712]{1,0:T(8,128)(2,1)S(1)}, u32[]{:S(2)}, u32[]{:S(2)}) collective-permute-start(bf16[16,3712]{1,0:T(8,128)(2,1)S(1)} %get-tuple-element.54), channel_id=1, source_target_pairs={{0,18},{1,19},{2,16},{3,17},{4,22},{5,23},{6,20},{7,21},{8,26},{9,... | collective-permute-start | bytes 356360 | tf_op jit(solution)/shard_map/ppermute | solution.py:306
  37.6 5.7 %collective-permute-start.9 = (bf16[16,3712]{1,0:T(8,128)(2,1)S(1)}, bf16[16,3712]{1,0:T(8,128)(2,1)S(1)}, u32[]{:S(2)}, u32[]{:S(2)}) collective-permute-start(bf16[16,3712]{1,0:T(8,128)(2,1)S(1)} %get-tuple-element.50), channel_id=1, source_target_pairs={{0,4},{1,5},{2,6},{3,7},{4,12},{5,13},{6,14},{7,15},{8,0},{9,1},{1... | collective-permute-start | bytes 356360 | tf_op jit(solution)/shard_map/ppermute | solution.py:306
  43.8 12.0 %collective-permute-start.16 = (bf16[32,3584]{1,0:T(8,128)(2,1)S(1)}, bf16[32,3584]{1,0:T(8,128)(2,1)S(1)}, u32[]{:S(2)}, u32[]{:S(2)}) collective-permute-start(bf16[32,3584]{1,0:T(8,128)(2,1)S(1)} %combine.2), channel_id=1, source_target_pairs={{0,20},{1,21},{2,22},{3,23},{4,28},{5,29},{6,30},{7,31},{8,16},{9,... | collective-permute-start | bytes 688136 | tf_op jit(solution)/shard_map/ppermute | solution.py:306
  44.6 9.1 %collective-permute-start.14 = (bf16[16,3712]{1,0:T(8,128)(2,1)S(1)}, bf16[16,3712]{1,0:T(8,128)(2,1)S(1)}, u32[]{:S(2)}, u32[]{:S(2)}) collective-permute-start(bf16[16,3712]{1,0:T(8,128)(2,1)S(1)} %get-tuple-element.57), channel_id=1, source_target_pairs={{0,24},{1,25},{2,26},{3,27},{4,16},{5,17},{6,18},{7,19},{8,28},{9,... | collective-permute-start | bytes 356360 | tf_op jit(solution)/shard_map/ppermute | solution.py:306
  47.7 7.4 %collective-permute-start.15 = (bf16[16,3712]{1,0:T(8,128)(2,1)S(1)}, bf16[16,3712]{1,0:T(8,128)(2,1)S(1)}, u32[]{:S(2)}, u32[]{:S(2)}) collective-permute-start(bf16[16,3712]{1,0:T(8,128)(2,1)S(1)} %get-tuple-element.58), channel_id=1, source_target_pairs={{0,26},{1,27},{2,24},{3,25},{4,18},{5,19},{6,16},{7,17},{8,30},{9,... | collective-permute-start | bytes 356360 | tf_op jit(solution)/shard_map/ppermute | solution.py:306

commit v26 on v24

--- a/solution.py
+++ b/solution.py
@@ -93,14 +93,13 @@
     )(*operands)
 
 
-def prepare_kernel(ids_in, weights_in, rows_in, block, ids, weights, sems):
-    tok_count, width = rows_in.shape
+def prepare_kernel(ids_in, weights_in, out, ids, weights, sems):
+    tok_count = out.shape[0]
     top_count = ids.shape[0]
     experts = 2 * len(RING)
     copies = [
         pltpu.make_async_copy(ids_in, ids, sems.at[0]),
         pltpu.make_async_copy(weights_in, weights, sems.at[1]),
-        pltpu.make_async_copy(rows_in, block.at[:, pl.ds(0, width)], sems.at[2]),
     ]
     for copy in copies:
         copy.start()
@@ -124,31 +123,31 @@
         scale = scale - piece
         notes.append(piece)
     notes = across(jnp.concatenate(notes, axis=0).astype(jnp.bfloat16), unit)
-    block[:, width:] = notes.astype(jnp.bfloat16) + token
-    copies[2].wait()
-
-
-def prepare(ids, weights, tokens):
-    tok_count, width = tokens.shape
+    out[...] = notes.astype(jnp.bfloat16) + token
+
+
+def prepare(ids, weights):
+    tok_count = ids.shape[1]
     return local_call(
         prepare_kernel,
         "prepare",
-        pltpu.VMEM((tok_count, width + LANES), jnp.bfloat16),
-        [pl.ANY] * 3,
-        tuple(pltpu.with_memory_space_constraint(x, pltpu.HBM) for x in (ids, weights, tokens)),
+        pltpu.VMEM((tok_count, LANES), jnp.bfloat16),
+        [pl.ANY] * 2,
+        tuple(pltpu.with_memory_space_constraint(x, pltpu.HBM) for x in (ids, weights)),
         [
             pltpu.VMEM(ids.shape, ids.dtype),
             pltpu.VMEM(weights.shape, weights.dtype),
-            pltpu.SemaphoreType.DMA((3,)),
+            pltpu.SemaphoreType.DMA((2,)),
         ],
         limit=8,
     )
 
 
-def choose_kernel(places, capacity, block, *refs):
+def choose_kernel(places, capacity, block, marks, *refs):
     chip = lax.axis_index("expert") >> 1
     tok_count = block.shape[0]
-    notes = block[:, -LANES:].astype(jnp.float32)
+    notes = marks[...].astype(jnp.float32)
+    width = block.shape[1]
     lane = iota(notes.shape, 1)
     slot = iota((tok_count, len(places) * capacity), 1)
     code = jnp.zeros(slot.shape, jnp.float32)
@@ -158,18 +157,22 @@
         column = jnp.sum(jnp.where(lane == wanted, notes, 0.0), axis=1, keepdims=True)
         code = jnp.where(slot >= at * capacity, column, code)
         order = jnp.where(slot >= at * capacity, slot + 1 - at * capacity, order)
-    rows = across(ones_where(code == order.astype(jnp.float32)), block[...]).astype(jnp.bfloat16)
+    pick = ones_where(code == order.astype(jnp.float32))
+    rows = across(pick, block[...]).astype(jnp.bfloat16)
+    marked = across(pick, marks[...]).astype(jnp.bfloat16)
     for at in range(len(places)):
-        refs[at][...] = rows[at * capacity : (at + 1) * capacity]
-
-
-def choose(block, capacity, places):
+        place = slice(at * capacity, (at + 1) * capacity)
+        refs[at][:, :width] = rows[place]
+        refs[at][:, width:] = marked[place]
+
+
+def choose(block, marks, capacity, places):
     return local_call(
         functools.partial(choose_kernel, places, capacity),
         "choose",
-        [jax.ShapeDtypeStruct((capacity, block.shape[1]), jnp.bfloat16) for _ in places],
-        [None],
-        (block,),
+        [jax.ShapeDtypeStruct((capacity, block.shape[1] + LANES), jnp.bfloat16) for _ in places],
+        [None] * 2,
+        (block, marks),
     )
 
 
@@ -322,13 +325,14 @@
     w_in, w_out = w_gate_up[0], w_down[0]
     far_out = lax.ppermute(w_out, "expert", swap)
     far_in = lax.ppermute(w_in, "expert", swap)
-    block = prepare(route_ids[0].T, route_weights[0].T, tokens)
-    block1 = sent(block, sections, 0, 1, 0)
-    own0, other, back0, back1 = choose(block, capacity, ((0, 0), (0, 1), (3, 0), (3, 1)))
+    block1 = sent(tokens, sections, 0, 1, 0)
+    marks = prepare(route_ids[0].T, route_weights[0].T)
+    marks1 = sent(marks, sections, 0, 1, 0)
+    own0, other, back0, back1 = choose(tokens, marks, capacity, ((0, 0), (0, 1), (3, 0), (3, 1)))
     other0 = sent(other, sections, 0, 0, 1)
     near = (loaded(after(w_in, own0)), loaded(after(w_out, own0)))
     block1 = after(block1, (near, other0))
-    own1, other, on0, on1 = choose(block1, capacity, ((0, 0), (0, 1), (1, 0), (1, 1)))
+    own1, other, on0, on1 = choose(block1, marks1, capacity, ((0, 0), (0, 1), (1, 0), (1, 1)))
     other1 = sent(other, sections, 0, 0, 1)
     own2 = sent(on0, sections, 0, 1, 0)
     other2 = sent(on1, sections, 0, 1, 1)
@@ -340,15 +344,15 @@
     pieces = far_pass(slots, total, (far_in, far_out), capacity)
     piece = dict(zip(places, pieces))
     first = [
-        sent(piece[2, 0], sections, 0, 1, 0),
         sent(piece[2, 1], sections, 0, 1, 1),
         sent(piece[3, 1], sections, 0, 0, 1),
+        sent(piece[0, 0], sections, 1, 0, 0),
         sent(piece[0, 1], sections, 1, 0, 1),
-        sent(piece[1, 0], sections, 1, -1, 0),
+        sent(piece[2, 0], sections, 0, 1, 0),
     ]
-    *merged, zero, one = lax.optimization_barrier(first)
-    merged.append(piece[3, 0])
-    straight = [zero, one, sent(piece[1, 1], sections, 1, -1, 1), sent(piece[0, 0], sections, 1, 0, 0)]
+    two, three, *straight, four = lax.optimization_barrier(first)
+    merged = [piece[3, 0], two, three, four]
+    straight += [sent(piece[1, flip], sections, 1, -1, flip) for flip in range(2)]
     merged = sent(combine(merged, tok_count), sections, 1, 1, 0)
     return combine(straight, tok_count, merged)[None]
 

time: 56.5 us -> 57.5 us (1.018)
  local copies, waits for them, and re-layouts: 4.62 us -> 5.55 us
    unnamed x4 -> x6, local copies, waits for them, and re-layouts: 4.62 us -> 5.55 us
    ppermute x15 -> x16, starting transfers between devices: 25.3 us -> 25.5 us  [sent(): return lax.ppermute(shard, ('section', 'expert'), pairs)]
    ppermute x15 -> x16, waiting for transfers between devices: 18.2 us -> 18.1 us  [sent(): return lax.ppermute(shard, ('section', 'expert'), pairs)]
  transfers between devices with their start and end apart: 17 -> 18, of which waited for: 10 -> 8; matrix products, arithmetic and copies ran while one was open for 0% -> 0% of each run, Pallas kernels for 8% -> 8%
where the time goes in v26:
time: 57.5 us; the launch traced here: 57.3 us
  starting transfers between devices  26 us (45%)
  waiting for transfers between devices  18.1 us (31%)
  Pallas kernels  7.57 us (13%)
  local copies, waits for them, and re-layouts  5.55 us (10%)
    ppermute x16, starting transfers between devices, sent(): return lax.ppermute(shard, ('section', 'expert'), pairs)  25.5 us
    ppermute x16, waiting for transfers between devices, sent(): return lax.ppermute(shard, ('section', 'expert'), pairs)  18.1 us
    pallas_call x9, Pallas kernels, local_call(): pl.pallas_call(kernel, out_shape=out_shape, in_specs=[vmem if spec is Non...  7.57 us
    unnamed x6, local copies, waits for them, and re-layouts  5.55 us
  transfers between devices with their start and end apart: 18, of which 8 were waited for; matrix products, arithmetic and copies ran while one was open for 0% of the time, Pallas kernels for 8%

profile of v26, /device:TPU:0, one launch (start us, length us, event | category | flops | bytes accessed | tf_op | source)
XLA Modules:
  0.0 57.3 jit_solution(316440924955621775)
XLA Ops:
  0.5 3.0 %collective-permute-start.1 = (bf16[32,3584]{1,0:T(8,128)(2,1)}, bf16[32,3584]{1,0:T(8,128)(2,1)S(1)}, u32[]{:S(2)}, u32[]{:S(2)}) collective-permute-start(bf16[32,3584]{1,0:T(8,128)(2,1)} %bitcast.14), channel_id=1, source_target_pairs={{0,4},{1,5},{2,6},{3,7},{4,12},{5,13},{6,14},{7,15},{8,0},{9,1},{1... | collective-permute-start | bytes 688136 | tf_op jit(solution)/shard_map/ppermute | solution.py:309
  3.5 1.0 %prepare.1.marks = bf16[32,128]{1,0:T(8,128)(2,1)S(1)} custom-call(s32[2,32]{1,0:T(2,128)} %bitcast.16, f32[2,32]{1,0:T(2,128)} %bitcast.17), custom_call_target="tpu_custom_call" | custom-call | tf_op jit(solution)/shard_map/prepare/pallas_call | solution.py:84
  5.9 1.6 %collective-permute-start = (bf16[16,3712]{1,0:T(8,128)(2,1)S(1)}, bf16[16,3712]{1,0:T(8,128)(2,1)S(1)}, u32[]{:S(2)}, u32[]{:S(2)}) collective-permute-start(bf16[16,3712]{1,0:T(8,128)(2,1)S(1)} %get-tuple-element.34), channel_id=1, source_target_pairs={{0,2},{1,3},{2,0},{3,1},{4,6},{5,7},{6,4},{7,5},{8,10},{9,11},{10,... | collective-permute-start | bytes 356360 | tf_op jit(solution)/shard_map/ppermute | solution.py:309
  7.5 2.6 %collective-permute-start.2 = (bf16[32,128]{1,0:T(8,128)(2,1)S(1)}, bf16[32,128]{1,0:T(8,128)(2,1)S(1)}, u32[]{:S(2)}, u32[]{:S(2)}) collective-permute-start(bf16[32,128]{1,0:T(8,128)(2,1)S(1)} %prepare.1.marks), channel_id=1, source_target_pairs={{0,4},{1,5},{2,6},{3,7},{4,12},{5,13},{6,14},{7,15},{8,0},{9,1},{1... | collective-permute-start | bytes 24584 | tf_op jit(solution)/shard_map/ppermute | solution.py:309
  10.1 3.1 %copy-done = bf16[1,3584,1024]{2,1,0:T(8,128)(2,1)S(1)} copy-done((bf16[1,3584,1024]{2,1,0:T(8,128)(2,1)S(1)}, bf16[1,3584,1024]{2,1,0:T(8,128)(2,1)}, u32[]{:S(2)}) %copy-start) | copy-done | bytes 7340056
  13.7 1.5 %copy-done.1 = bf16[1,512,3584]{2,1,0:T(8,128)(2,1)S(1)} copy-done((bf16[1,512,3584]{2,1,0:T(8,128)(2,1)S(1)}, bf16[1,512,3584]{2,1,0:T(8,128)(2,1)}, u32[]{:S(2)}) %copy-start.1) | copy-done | bytes 3670040
  16.2 1.6 %collective-permute-start.5 = (bf16[16,3712]{1,0:T(8,128)(2,1)S(1)}, bf16[16,3712]{1,0:T(8,128)(2,1)S(1)}, u32[]{:S(2)}, u32[]{:S(2)}) collective-permute-start(bf16[16,3712]{1,0:T(8,128)(2,1)S(1)} %get-tuple-element.41), channel_id=1, source_target_pairs={{0,2},{1,3},{2,0},{3,1},{4,6},{5,7},{6,4},{7,5},{8,10},{9,11},{10,... | collective-permute-start | bytes 356360 | tf_op jit(solution)/shard_map/ppermute | solution.py:309
  17.8 1.7 %collective-permute-start.3 = (bf16[16,3712]{1,0:T(8,128)(2,1)S(1)}, bf16[16,3712]{1,0:T(8,128)(2,1)S(1)}, u32[]{:S(2)}, u32[]{:S(2)}) collective-permute-start(bf16[16,3712]{1,0:T(8,128)(2,1)S(1)} %get-tuple-element.39), channel_id=1, source_target_pairs={{0,4},{1,5},{2,6},{3,7},{4,12},{5,13},{6,14},{7,15},{8,0},{9,1},{1... | collective-permute-start | bytes 356360 | tf_op jit(solution)/shard_map/ppermute | solution.py:309
  19.5 3.1 %collective-permute-done.6.refs_7_ = bf16[16,3712]{1,0:T(8,128)(2,1)S(1)} collective-permute-done((bf16[16,3712]{1,0:T(8,128)(2,1)S(1)}, bf16[16,3712]{1,0:T(8,128)(2,1)S(1)}, u32[]{:S(2)}, u32[]{:S(2)}) %collective-permute-start.6) | collective-permute-done | bytes 118816 | tf_op jit(solution)/shard_map/ppermute | solution.py:309
  22.6 1.3 %collective-permute-start.4 = (bf16[16,3712]{1,0:T(8,128)(2,1)S(1)}, bf16[16,3712]{1,0:T(8,128)(2,1)S(1)}, u32[]{:S(2)}, u32[]{:S(2)}) collective-permute-start(bf16[16,3712]{1,0:T(8,128)(2,1)S(1)} %get-tuple-element.40), channel_id=1, source_target_pairs={{0,6},{1,7},{2,4},{3,5},{4,14},{5,15},{6,12},{7,13},{8,2},{9,3},{1... | collective-permute-start | bytes 356360 | tf_op jit(solution)/shard_map/ppermute | solution.py:309
  24.6 5.9 %collective-permute-done.4.refs_4_ = bf16[16,3712]{1,0:T(8,128)(2,1)S(1)} collective-permute-done((bf16[16,3712]{1,0:T(8,128)(2,1)S(1)}, bf16[16,3712]{1,0:T(8,128)(2,1)S(1)}, u32[]{:S(2)}, u32[]{:S(2)}) %collective-permute-start.4) | collective-permute-done | bytes 118816 | tf_op jit(solution)/shard_map/ppermute | solution.py:309
  30.5 1.7 %near_pass.1 = (bf16[128,3712]{1,0:T(8,128)(2,1)S(1)}, f32[128,3584]{1,0:T(8,128)S(1)}) custom-call(bf16[16,3712]{1,0:T(8,128)(2,1)S(1)} %get-tuple-element.33.refs_0_, bf16[16,3712]{1,0:T(8,128)(2,1)S(1)} %collective-permute-done.refs_1_, bf16[16,3712]{1,0:T(8,128)(2,1)S(1)} %get-tuple-element.38.refs_2_, ...), custom_call_target="tpu_custom_call" | custom-call | bytes 11010048 | tf_op jit(solution)/shard_map/near_pass/pallas_call | solution.py:84
  32.3 1.7 %far_pass.1 = (bf16[16,3712]{1,0:T(8,128)(2,1)S(1)}, bf16[16,3712]{1,0:T(8,128)(2,1)S(1)}, bf16[16,3712]{1,0:T(8,128)(2,1)S(1)}, bf16[16,3712]{1,0:T(8,128)(2,1)...) custom-call(bf16[128,3712]{1,0:T(8,128)(2,1)S(1)} %get-tuple-element, ...), custom_call_target="tpu_custom_call" | custom-call | bytes 11010048 | tf_op jit(solution)/shard_map/far_pass/pallas_call | solution.py:84
  34.4 2.2 %collective-permute-start.11 = (bf16[16,3712]{1,0:T(8,128)(2,1)S(1)}, bf16[16,3712]{1,0:T(8,128)(2,1)S(1)}, u32[]{:S(2)}, u32[]{:S(2)}) collective-permute-start(bf16[16,3712]{1,0:T(8,128)(2,1)S(1)} %get-tuple-element.49), channel_id=1, source_target_pairs={{0,2},{1,3},{2,0},{3,1},{4,6},{5,7},{6,4},{7,5},{8,10},{9,11},{10,... | collective-permute-start | bytes 356360 | tf_op jit(solution)/shard_map/ppermute | solution.py:309
  36.6 1.5 %collective-permute-start.12 = (bf16[16,3712]{1,0:T(8,128)(2,1)S(1)}, bf16[16,3712]{1,0:T(8,128)(2,1)S(1)}, u32[]{:S(2)}, u32[]{:S(2)}) collective-permute-start(bf16[16,3712]{1,0:T(8,128)(2,1)S(1)} %get-tuple-element.50), channel_id=1, source_target_pairs={{0,16},{1,17},{2,18},{3,19},{4,20},{5,21},{6,22},{7,23},{8,24},{9,... | collective-permute-start | bytes 356360 | tf_op jit(solution)/shard_map/ppermute | solution.py:309
  38.1 1.1 %collective-permute-start.14 = (bf16[16,3712]{1,0:T(8,128)(2,1)S(1)}, bf16[16,3712]{1,0:T(8,128)(2,1)S(1)}, u32[]{:S(2)}, u32[]{:S(2)}) collective-permute-start(bf16[16,3712]{1,0:T(8,128)(2,1)S(1)} %get-tuple-element.52), channel_id=1, source_target_pairs={{0,4},{1,5},{2,6},{3,7},{4,12},{5,13},{6,14},{7,15},{8,0},{9,1},{1... | collective-permute-start | bytes 356360 | tf_op jit(solution)/shard_map/ppermute | solution.py:309
  39.2 2.5 %collective-permute-done.10.refs_1_ = bf16[16,3712]{1,0:T(8,128)(2,1)S(1)} collective-permute-done((bf16[16,3712]{1,0:T(8,128)(2,1)S(1)}, bf16[16,3712]{1,0:T(8,128)(2,1)S(1)}, u32[]{:S(2)}, u32[]{:S(2)}) %collective-permute-start.10) | collective-permute-done | bytes 118816 | tf_op jit(solution)/shard_map/ppermute | solution.py:309
  41.8 2.0 %collective-permute-done.13.refs_1_ = bf16[16,3712]{1,0:T(8,128)(2,1)S(1)} collective-permute-done((bf16[16,3712]{1,0:T(8,128)(2,1)S(1)}, bf16[16,3712]{1,0:T(8,128)(2,1)S(1)}, u32[]{:S(2)}, u32[]{:S(2)}) %collective-permute-start.13) | collective-permute-done | bytes 118816 | tf_op jit(solution)/shard_map/ppermute | solution.py:309
  44.2 1.7 %collective-permute-start.17 = (bf16[32,3584]{1,0:T(8,128)(2,1)S(1)}, bf16[32,3584]{1,0:T(8,128)(2,1)S(1)}, u32[]{:S(2)}, u32[]{:S(2)}) collective-permute-start(bf16[32,3584]{1,0:T(8,128)(2,1)S(1)} %combine.2), channel_id=1, source_target_pairs={{0,20},{1,21},{2,22},{3,23},{4,28},{5,29},{6,30},{7,31},{8,16},{9,... | collective-permute-start | bytes 688136 | tf_op jit(solution)/shard_map/ppermute | solution.py:309
  45.9 2.2 %collective-permute-start.15 = (bf16[16,3712]{1,0:T(8,128)(2,1)S(1)}, bf16[16,3712]{1,0:T(8,128)(2,1)S(1)}, u32[]{:S(2)}, u32[]{:S(2)}) collective-permute-start(bf16[16,3712]{1,0:T(8,128)(2,1)S(1)} %get-tuple-element.55), channel_id=1, source_target_pairs={{0,24},{1,25},{2,26},{3,27},{4,16},{5,17},{6,18},{7,19},{8,28},{9,... | collective-permute-start | bytes 356360 | tf_op jit(solution)/shard_map/ppermute | solution.py:309
  48.1 3.7 %collective-permute-start.16 = (bf16[16,3712]{1,0:T(8,128)(2,1)S(1)}, bf16[16,3712]{1,0:T(8,128)(2,1)S(1)}, u32[]{:S(2)}, u32[]{:S(2)}) collective-permute-start(bf16[16,3712]{1,0:T(8,128)(2,1)S(1)} %get-tuple-element.56), channel_id=1, source_target_pairs={{0,26},{1,27},{2,24},{3,25},{4,18},{5,19},{6,16},{7,17},{8,30},{9,... | collective-permute-start | bytes 356360 | tf_op jit(solution)/shard_map/ppermute | solution.py:309
  51.8 2.1 %collective-permute-done.15.refs_2_ = bf16[16,3712]{1,0:T(8,128)(2,1)S(1)} collective-permute-done((bf16[16,3712]{1,0:T(8,128)(2,1)S(1)}, bf16[16,3712]{1,0:T(8,128)(2,1)S(1)}, u32[]{:S(2)}, u32[]{:S(2)}) %collective-permute-start.15) | collective-permute-done | bytes 118816 | tf_op jit(solution)/shard_map/ppermute | solution.py:309
  53.9 2.3 %collective-permute-done.16.refs_3_ = bf16[16,3712]{1,0:T(8,128)(2,1)S(1)} collective-permute-done((bf16[16,3712]{1,0:T(8,128)(2,1)S(1)}, bf16[16,3712]{1,0:T(8,128)(2,1)S(1)}, u32[]{:S(2)}, u32[]{:S(2)}) %collective-permute-start.16) | collective-permute-done | bytes 118816 | tf_op jit(solution)/shard_map/ppermute | solution.py:309
  56.2 1.1 %combine.3 = bf16[32,3584]{1,0:T(8,128)(2,1)} custom-call(bf16[16,3712]{1,0:T(8,128)(2,1)S(1)} %collective-permute-done.12.refs_0_, bf16[16,3712]{1,0:T(8,128)(2,1)S(1)} %collective-permute-done.13.refs_1_, bf16[16,3712]{1,0:T(8,128)(2,1)S(1)} %collective-permute-done.15.refs_2_, bf16[16,3712]{1,0:T(8,128)(2,1)S(1)} %collective-permute-done.16.refs_3_, ...), custom_call_target="tpu_custom_call" | custom-call | tf_op jit(solution)/shard_map/combine/pallas_call | solution.py:84
  (27 shorter events, 5.1 us)
Async XLA Ops:
  0.0 32.3 %collective-permute-start.8 = (bf16[3584,1024]{1,0:T(8,128)(2,1)}, bf16[3584,1024]{1,0:T(8,128)(2,1)S(1)}, u32[]{:S(2)}, u32[]{:S(2)}) collective-permute-start(bf16[3584,1024]{1,0:T(8,128)(2,1)} %bitcast.10), channel_id=1, source_target_pairs={{0,1},{1,0},{2,3},{3,2},{4,5},{5,4},{6,7},{7,6},{8,9},{9,8},{10,11... | collective-permute-start | bytes 22020104 | tf_op jit(solution)/shard_map/ppermute | solution.py:327
  0.5 31.8 %collective-permute-start.9 = (bf16[512,3584]{1,0:T(8,128)(2,1)}, bf16[512,3584]{1,0:T(8,128)(2,1)S(1)}, u32[]{:S(2)}, u32[]{:S(2)}) collective-permute-start(bf16[512,3584]{1,0:T(8,128)(2,1)} %bitcast.12), channel_id=1, source_target_pairs={{0,1},{1,0},{2,3},{3,2},{4,5},{5,4},{6,7},{7,6},{8,9},{9,8},{10,11... | collective-permute-start | bytes 11010056 | tf_op jit(solution)/shard_map/ppermute | solution.py:326
  0.5 15.3 %collective-permute-start.1 = (bf16[32,3584]{1,0:T(8,128)(2,1)}, bf16[32,3584]{1,0:T(8,128)(2,1)S(1)}, u32[]{:S(2)}, u32[]{:S(2)}) collective-permute-start(bf16[32,3584]{1,0:T(8,128)(2,1)} %bitcast.14), channel_id=1, source_target_pairs={{0,4},{1,5},{2,6},{3,7},{4,12},{5,13},{6,14},{7,15},{8,0},{9,1},{1... | collective-permute-start | bytes 688136 | tf_op jit(solution)/shard_map/ppermute | solution.py:309
  4.5 0.9 %copy-start.2 = (bf16[1,32,3584]{2,1,0:T(8,128)(2,1)S(1)}, bf16[1,32,3584]{2,1,0:T(8,128)(2,1)}, u32[]{:S(2)}) copy-start(bf16[1,32,3584]{2,1,0:T(8,128)(2,1)} %param.5) | copy-start | bytes 688132
  5.9 9.6 %collective-permute-start = (bf16[16,3712]{1,0:T(8,128)(2,1)S(1)}, bf16[16,3712]{1,0:T(8,128)(2,1)S(1)}, u32[]{:S(2)}, u32[]{:S(2)}) collective-permute-start(bf16[16,3712]{1,0:T(8,128)(2,1)S(1)} %get-tuple-element.34), channel_id=1, source_target_pairs={{0,2},{1,3},{2,0},{3,1},{4,6},{5,7},{6,4},{7,5},{8,10},{9,11},{10,... | collective-permute-start | bytes 356360 | tf_op jit(solution)/shard_map/ppermute | solution.py:309
  7.5 8.3 %collective-permute-start.2 = (bf16[32,128]{1,0:T(8,128)(2,1)S(1)}, bf16[32,128]{1,0:T(8,128)(2,1)S(1)}, u32[]{:S(2)}, u32[]{:S(2)}) collective-permute-start(bf16[32,128]{1,0:T(8,128)(2,1)S(1)} %prepare.1.marks), channel_id=1, source_target_pairs={{0,4},{1,5},{2,6},{3,7},{4,12},{5,13},{6,14},{7,15},{8,0},{9,1},{1... | collective-permute-start | bytes 24584 | tf_op jit(solution)/shard_map/ppermute | solution.py:309
  10.1 3.1 %copy-start = (bf16[1,3584,1024]{2,1,0:T(8,128)(2,1)S(1)}, bf16[1,3584,1024]{2,1,0:T(8,128)(2,1)}, u32[]{:S(2)}) copy-start(bf16[1,3584,1024]{2,1,0:T(8,128)(2,1)} %param.8) | copy-start | bytes 22020100
  13.2 2.0 %copy-start.1 = (bf16[1,512,3584]{2,1,0:T(8,128)(2,1)S(1)}, bf16[1,512,3584]{2,1,0:T(8,128)(2,1)}, u32[]{:S(2)}) copy-start(bf16[1,512,3584]{2,1,0:T(8,128)(2,1)} %param.9) | copy-start | bytes 11010052
  15.5 7.1 %collective-permute-start.6 = (bf16[16,3712]{1,0:T(8,128)(2,1)S(1)}, bf16[16,3712]{1,0:T(8,128)(2,1)S(1)}, u32[]{:S(2)}, u32[]{:S(2)}) collective-permute-start(bf16[16,3712]{1,0:T(8,128)(2,1)S(1)} %get-tuple-element.44), channel_id=1, source_target_pairs={{0,10},{1,11},{2,8},{3,9},{4,2},{5,3},{6,0},{7,1},{8,14},{9,15},{1... | collective-permute-start | bytes 356360 | tf_op jit(solution)/shard_map/ppermute | solution.py:309
  16.2 7.6 %collective-permute-start.5 = (bf16[16,3712]{1,0:T(8,128)(2,1)S(1)}, bf16[16,3712]{1,0:T(8,128)(2,1)S(1)}, u32[]{:S(2)}, u32[]{:S(2)}) collective-permute-start(bf16[16,3712]{1,0:T(8,128)(2,1)S(1)} %get-tuple-element.41), channel_id=1, source_target_pairs={{0,2},{1,3},{2,0},{3,1},{4,6},{5,7},{6,4},{7,5},{8,10},{9,11},{10,... | collective-permute-start | bytes 356360 | tf_op jit(solution)/shard_map/ppermute | solution.py:309
  17.8 6.8 %collective-permute-start.3 = (bf16[16,3712]{1,0:T(8,128)(2,1)S(1)}, bf16[16,3712]{1,0:T(8,128)(2,1)S(1)}, u32[]{:S(2)}, u32[]{:S(2)}) collective-permute-start(bf16[16,3712]{1,0:T(8,128)(2,1)S(1)} %get-tuple-element.39), channel_id=1, source_target_pairs={{0,4},{1,5},{2,6},{3,7},{4,12},{5,13},{6,14},{7,15},{8,0},{9,1},{1... | collective-permute-start | bytes 356360 | tf_op jit(solution)/shard_map/ppermute | solution.py:309
  22.6 7.9 %collective-permute-start.4 = (bf16[16,3712]{1,0:T(8,128)(2,1)S(1)}, bf16[16,3712]{1,0:T(8,128)(2,1)S(1)}, u32[]{:S(2)}, u32[]{:S(2)}) collective-permute-start(bf16[16,3712]{1,0:T(8,128)(2,1)S(1)} %get-tuple-element.40), channel_id=1, source_target_pairs={{0,6},{1,7},{2,4},{3,5},{4,14},{5,15},{6,12},{7,13},{8,2},{9,3},{1... | collective-permute-start | bytes 356360 | tf_op jit(solution)/shard_map/ppermute | solution.py:309
  23.9 6.7 %collective-permute-start.7 = (bf16[16,3712]{1,0:T(8,128)(2,1)S(1)}, bf16[16,3712]{1,0:T(8,128)(2,1)S(1)}, u32[]{:S(2)}, u32[]{:S(2)}) collective-permute-start(bf16[16,3712]{1,0:T(8,128)(2,1)S(1)} %get-tuple-element.45), channel_id=1, source_target_pairs={{0,8},{1,9},{2,10},{3,11},{4,0},{5,1},{6,2},{7,3},{8,12},{9,13},{1... | collective-permute-start | bytes 356360 | tf_op jit(solution)/shard_map/ppermute | solution.py:309
  34.0 7.7 %collective-permute-start.10 = (bf16[16,3712]{1,0:T(8,128)(2,1)S(1)}, bf16[16,3712]{1,0:T(8,128)(2,1)S(1)}, u32[]{:S(2)}, u32[]{:S(2)}) collective-permute-start(bf16[16,3712]{1,0:T(8,128)(2,1)S(1)} %get-tuple-element.48), channel_id=1, source_target_pairs={{0,6},{1,7},{2,4},{3,5},{4,14},{5,15},{6,12},{7,13},{8,2},{9,3},{1... | collective-permute-start | bytes 356360 | tf_op jit(solution)/shard_map/ppermute | solution.py:309
  34.4 7.3 %collective-permute-start.11 = (bf16[16,3712]{1,0:T(8,128)(2,1)S(1)}, bf16[16,3712]{1,0:T(8,128)(2,1)S(1)}, u32[]{:S(2)}, u32[]{:S(2)}) collective-permute-start(bf16[16,3712]{1,0:T(8,128)(2,1)S(1)} %get-tuple-element.49), channel_id=1, source_target_pairs={{0,2},{1,3},{2,0},{3,1},{4,6},{5,7},{6,4},{7,5},{8,10},{9,11},{10,... | collective-permute-start | bytes 356360 | tf_op jit(solution)/shard_map/ppermute | solution.py:309
  36.6 5.2 %collective-permute-start.12 = (bf16[16,3712]{1,0:T(8,128)(2,1)S(1)}, bf16[16,3712]{1,0:T(8,128)(2,1)S(1)}, u32[]{:S(2)}, u32[]{:S(2)}) collective-permute-start(bf16[16,3712]{1,0:T(8,128)(2,1)S(1)} %get-tuple-element.50), channel_id=1, source_target_pairs={{0,16},{1,17},{2,18},{3,19},{4,20},{5,21},{6,22},{7,23},{8,24},{9,... | collective-permute-start | bytes 356360 | tf_op jit(solution)/shard_map/ppermute | solution.py:309
  38.1 5.7 %collective-permute-start.13 = (bf16[16,3712]{1,0:T(8,128)(2,1)S(1)}, bf16[16,3712]{1,0:T(8,128)(2,1)S(1)}, u32[]{:S(2)}, u32[]{:S(2)}) collective-permute-start(bf16[16,3712]{1,0:T(8,128)(2,1)S(1)} %get-tuple-element.51), channel_id=1, source_target_pairs={{0,18},{1,19},{2,16},{3,17},{4,22},{5,23},{6,20},{7,21},{8,26},{9,... | collective-permute-start | bytes 356360 | tf_op jit(solution)/shard_map/ppermute | solution.py:309
  38.1 5.7 %collective-permute-start.14 = (bf16[16,3712]{1,0:T(8,128)(2,1)S(1)}, bf16[16,3712]{1,0:T(8,128)(2,1)S(1)}, u32[]{:S(2)}, u32[]{:S(2)}) collective-permute-start(bf16[16,3712]{1,0:T(8,128)(2,1)S(1)} %get-tuple-element.52), channel_id=1, source_target_pairs={{0,4},{1,5},{2,6},{3,7},{4,12},{5,13},{6,14},{7,15},{8,0},{9,1},{1... | collective-permute-start | bytes 356360 | tf_op jit(solution)/shard_map/ppermute | solution.py:309
  44.2 11.9 %collective-permute-start.17 = (bf16[32,3584]{1,0:T(8,128)(2,1)S(1)}, bf16[32,3584]{1,0:T(8,128)(2,1)S(1)}, u32[]{:S(2)}, u32[]{:S(2)}) collective-permute-start(bf16[32,3584]{1,0:T(8,128)(2,1)S(1)} %combine.2), channel_id=1, source_target_pairs={{0,20},{1,21},{2,22},{3,23},{4,28},{5,29},{6,30},{7,31},{8,16},{9,... | collective-permute-start | bytes 688136 | tf_op jit(solution)/shard_map/ppermute | solution.py:309
  45.9 8.0 %collective-permute-start.15 = (bf16[16,3712]{1,0:T(8,128)(2,1)S(1)}, bf16[16,3712]{1,0:T(8,128)(2,1)S(1)}, u32[]{:S(2)}, u32[]{:S(2)}) collective-permute-start(bf16[16,3712]{1,0:T(8,128)(2,1)S(1)} %get-tuple-element.55), channel_id=1, source_target_pairs={{0,24},{1,25},{2,26},{3,27},{4,16},{5,17},{6,18},{7,19},{8,28},{9,... | collective-permute-start | bytes 356360 | tf_op jit(solution)/shard_map/ppermute | solution.py:309
  48.1 8.1 %collective-permute-start.16 = (bf16[16,3712]{1,0:T(8,128)(2,1)S(1)}, bf16[16,3712]{1,0:T(8,128)(2,1)S(1)}, u32[]{:S(2)}, u32[]{:S(2)}) collective-permute-start(bf16[16,3712]{1,0:T(8,128)(2,1)S(1)} %get-tuple-element.56), channel_id=1, source_target_pairs={{0,26},{1,27},{2,24},{3,25},{4,18},{5,19},{6,16},{7,17},{8,30},{9,... | collective-permute-start | bytes 356360 | tf_op jit(solution)/shard_map/ppermute | solution.py:309

commit v27 on v26

--- a/solution.py
+++ b/solution.py
@@ -330,14 +330,15 @@
     marks1 = sent(marks, sections, 0, 1, 0)
     own0, other, back0, back1 = choose(tokens, marks, capacity, ((0, 0), (0, 1), (3, 0), (3, 1)))
     other0 = sent(other, sections, 0, 0, 1)
-    near = (loaded(after(w_in, own0)), loaded(after(w_out, own0)))
-    block1 = after(block1, (near, other0))
+    block1 = after(block1, other0)
     own1, other, on0, on1 = choose(block1, marks1, capacity, ((0, 0), (0, 1), (1, 0), (1, 1)))
     other1 = sent(other, sections, 0, 0, 1)
     own2 = sent(on0, sections, 0, 1, 0)
     other2 = sent(on1, sections, 0, 1, 1)
-    other3 = sent(after(back1, (near, other0)), sections, 0, 3, 1)
-    own3 = sent(after(back0, (other1, other3)), sections, 0, 3, 0)
+    other3 = sent(after(back1, other0), sections, 0, 3, 1)
+    back0 = after(back0, (other1, other3))
+    own3 = sent(back0, sections, 0, 3, 0)
+    near = (loaded(after(w_in, back0)), loaded(after(w_out, back0)))
     pieces = (own0, other0, own1, own2, other2, other1, own3, other3)
     places = ((0, 0), (0, 1), (1, 0), (2, 0), (2, 1), (1, 1), (3, 0), (3, 1))
     slots, total = near_pass(pieces, near)

time: 57.5 us -> 54.9 us (0.955)
  waiting for transfers between devices: 18.1 us -> 16.1 us
  starting transfers between devices: 26 us -> 25.4 us
    ppermute x16, waiting for transfers between devices: 18.1 us -> 16.1 us  [sent(): return lax.ppermute(shard, ('section', 'expert'), pairs)]
    ppermute x16, starting transfers between devices: 25.5 us -> 24.9 us  [sent(): return lax.ppermute(shard, ('section', 'expert'), pairs)]
  transfers between devices with their start and end apart: 18 -> 18, of which waited for: 8 -> 10; matrix products, arithmetic and copies ran while one was open for 0% -> 0% of each run, Pallas kernels for 8% -> 8%
where the time goes in v27:
time: 54.9 us; the launch traced here: 54.7 us
  starting transfers between devices  25.4 us (46%)
  waiting for transfers between devices  16.1 us (29%)
  Pallas kernels  7.56 us (14%)
  local copies, waits for them, and re-layouts  5.55 us (10%)
    ppermute x16, starting transfers between devices, sent(): return lax.ppermute(shard, ('section', 'expert'), pairs)  24.9 us
    ppermute x16, waiting for transfers between devices, sent(): return lax.ppermute(shard, ('section', 'expert'), pairs)  16.1 us
    pallas_call x9, Pallas kernels, local_call(): pl.pallas_call(kernel, out_shape=out_shape, in_specs=[vmem if spec is Non...  7.56 us
    unnamed x6, local copies, waits for them, and re-layouts  5.55 us
  transfers between devices with their start and end apart: 18, of which 10 were waited for; matrix products, arithmetic and copies ran while one was open for 0% of the time, Pallas kernels for 8%

profile of v27, /device:TPU:0, one launch (start us, length us, event | category | flops | bytes accessed | tf_op | source)
XLA Modules:
  0.0 54.7 jit_solution(8800749016458467063)
XLA Ops:
  0.5 3.0 %collective-permute-start.1 = (bf16[32,3584]{1,0:T(8,128)(2,1)}, bf16[32,3584]{1,0:T(8,128)(2,1)S(1)}, u32[]{:S(2)}, u32[]{:S(2)}) collective-permute-start(bf16[32,3584]{1,0:T(8,128)(2,1)} %bitcast.14), channel_id=1, source_target_pairs={{0,4},{1,5},{2,6},{3,7},{4,12},{5,13},{6,14},{7,15},{8,0},{9,1},{1... | collective-permute-start | bytes 688136 | tf_op jit(solution)/shard_map/ppermute | solution.py:309
  3.5 1.0 %prepare.1.marks = bf16[32,128]{1,0:T(8,128)(2,1)S(1)} custom-call(s32[2,32]{1,0:T(2,128)} %bitcast.16, f32[2,32]{1,0:T(2,128)} %bitcast.17), custom_call_target="tpu_custom_call" | custom-call | tf_op jit(solution)/shard_map/prepare/pallas_call | solution.py:84
  4.6 0.9 %copy-done.2 = bf16[1,32,3584]{2,1,0:T(8,128)(2,1)S(1)} copy-done((bf16[1,32,3584]{2,1,0:T(8,128)(2,1)S(1)}, bf16[1,32,3584]{2,1,0:T(8,128)(2,1)}, u32[]{:S(2)}) %copy-start.2) | copy-done | bytes 229400
  5.9 1.6 %collective-permute-start = (bf16[16,3712]{1,0:T(8,128)(2,1)S(1)}, bf16[16,3712]{1,0:T(8,128)(2,1)S(1)}, u32[]{:S(2)}, u32[]{:S(2)}) collective-permute-start(bf16[16,3712]{1,0:T(8,128)(2,1)S(1)} %get-tuple-element.34), channel_id=1, source_target_pairs={{0,2},{1,3},{2,0},{3,1},{4,6},{5,7},{6,4},{7,5},{8,10},{9,11},{10,... | collective-permute-start | bytes 356360 | tf_op jit(solution)/shard_map/ppermute | solution.py:309
  7.5 2.6 %collective-permute-start.2 = (bf16[32,128]{1,0:T(8,128)(2,1)S(1)}, bf16[32,128]{1,0:T(8,128)(2,1)S(1)}, u32[]{:S(2)}, u32[]{:S(2)}) collective-permute-start(bf16[32,128]{1,0:T(8,128)(2,1)S(1)} %prepare.1.marks), channel_id=1, source_target_pairs={{0,4},{1,5},{2,6},{3,7},{4,12},{5,13},{6,14},{7,15},{8,0},{9,1},{1... | collective-permute-start | bytes 24584 | tf_op jit(solution)/shard_map/ppermute | solution.py:309
  10.8 2.3 %collective-permute-start.6 = (bf16[16,3712]{1,0:T(8,128)(2,1)S(1)}, bf16[16,3712]{1,0:T(8,128)(2,1)S(1)}, u32[]{:S(2)}, u32[]{:S(2)}) collective-permute-start(bf16[16,3712]{1,0:T(8,128)(2,1)S(1)} %get-tuple-element.42), channel_id=1, source_target_pairs={{0,10},{1,11},{2,8},{3,9},{4,2},{5,3},{6,0},{7,1},{8,14},{9,15},{1... | collective-permute-start | bytes 356360 | tf_op jit(solution)/shard_map/ppermute | solution.py:309
  14.1 1.4 %collective-permute-start.3 = (bf16[16,3712]{1,0:T(8,128)(2,1)S(1)}, bf16[16,3712]{1,0:T(8,128)(2,1)S(1)}, u32[]{:S(2)}, u32[]{:S(2)}) collective-permute-start(bf16[16,3712]{1,0:T(8,128)(2,1)S(1)} %get-tuple-element.37), channel_id=1, source_target_pairs={{0,4},{1,5},{2,6},{3,7},{4,12},{5,13},{6,14},{7,15},{8,0},{9,1},{1... | collective-permute-start | bytes 356360 | tf_op jit(solution)/shard_map/ppermute | solution.py:309
  15.4 3.0 %collective-permute-done.6.refs_7_ = bf16[16,3712]{1,0:T(8,128)(2,1)S(1)} collective-permute-done((bf16[16,3712]{1,0:T(8,128)(2,1)S(1)}, bf16[16,3712]{1,0:T(8,128)(2,1)S(1)}, u32[]{:S(2)}, u32[]{:S(2)}) %collective-permute-start.6) | collective-permute-done | bytes 118816 | tf_op jit(solution)/shard_map/ppermute | solution.py:309
  18.4 2.8 %collective-permute-start.4 = (bf16[16,3712]{1,0:T(8,128)(2,1)S(1)}, bf16[16,3712]{1,0:T(8,128)(2,1)S(1)}, u32[]{:S(2)}, u32[]{:S(2)}) collective-permute-start(bf16[16,3712]{1,0:T(8,128)(2,1)S(1)} %get-tuple-element.38), channel_id=1, source_target_pairs={{0,6},{1,7},{2,4},{3,5},{4,14},{5,15},{6,12},{7,13},{8,2},{9,3},{1... | collective-permute-start | bytes 356360 | tf_op jit(solution)/shard_map/ppermute | solution.py:309
  21.2 3.1 %copy-done = bf16[1,3584,1024]{2,1,0:T(8,128)(2,1)S(1)} copy-done((bf16[1,3584,1024]{2,1,0:T(8,128)(2,1)S(1)}, bf16[1,3584,1024]{2,1,0:T(8,128)(2,1)}, u32[]{:S(2)}) %copy-start) | copy-done | bytes 7340056
  24.8 1.5 %copy-done.1 = bf16[1,512,3584]{2,1,0:T(8,128)(2,1)S(1)} copy-done((bf16[1,512,3584]{2,1,0:T(8,128)(2,1)S(1)}, bf16[1,512,3584]{2,1,0:T(8,128)(2,1)}, u32[]{:S(2)}) %copy-start.1) | copy-done | bytes 3670040
  26.7 1.7 %near_pass.1 = (bf16[128,3712]{1,0:T(8,128)(2,1)S(1)}, f32[128,3584]{1,0:T(8,128)S(1)}) custom-call(bf16[16,3712]{1,0:T(8,128)(2,1)S(1)} %get-tuple-element.33.refs_0_, bf16[16,3712]{1,0:T(8,128)(2,1)S(1)} %collective-permute-done.refs_1_, bf16[16,3712]{1,0:T(8,128)(2,1)S(1)} %get-tuple-element.36.refs_2_, ...), custom_call_target="tpu_custom_call" | custom-call | bytes 11010048 | tf_op jit(solution)/shard_map/near_pass/pallas_call | solution.py:84
  28.4 1.7 %far_pass.1 = (bf16[16,3712]{1,0:T(8,128)(2,1)S(1)}, bf16[16,3712]{1,0:T(8,128)(2,1)S(1)}, bf16[16,3712]{1,0:T(8,128)(2,1)S(1)}, bf16[16,3712]{1,0:T(8,128)(2,1)...) custom-call(bf16[128,3712]{1,0:T(8,128)(2,1)S(1)} %get-tuple-element, ...), custom_call_target="tpu_custom_call" | custom-call | bytes 11010048 | tf_op jit(solution)/shard_map/far_pass/pallas_call | solution.py:84
  30.1 2.7 %collective-permute-start.10 = (bf16[16,3712]{1,0:T(8,128)(2,1)S(1)}, bf16[16,3712]{1,0:T(8,128)(2,1)S(1)}, u32[]{:S(2)}, u32[]{:S(2)}) collective-permute-start(bf16[16,3712]{1,0:T(8,128)(2,1)S(1)} %get-tuple-element.48), channel_id=1, source_target_pairs={{0,6},{1,7},{2,4},{3,5},{4,14},{5,15},{6,12},{7,13},{8,2},{9,3},{1... | collective-permute-start | bytes 356360 | tf_op jit(solution)/shard_map/ppermute | solution.py:309
  33.7 1.5 %collective-permute-start.12 = (bf16[16,3712]{1,0:T(8,128)(2,1)S(1)}, bf16[16,3712]{1,0:T(8,128)(2,1)S(1)}, u32[]{:S(2)}, u32[]{:S(2)}) collective-permute-start(bf16[16,3712]{1,0:T(8,128)(2,1)S(1)} %get-tuple-element.50), channel_id=1, source_target_pairs={{0,16},{1,17},{2,18},{3,19},{4,20},{5,21},{6,22},{7,23},{8,24},{9,... | collective-permute-start | bytes 356360 | tf_op jit(solution)/shard_map/ppermute | solution.py:309
  35.2 1.1 %collective-permute-start.13 = (bf16[16,3712]{1,0:T(8,128)(2,1)S(1)}, bf16[16,3712]{1,0:T(8,128)(2,1)S(1)}, u32[]{:S(2)}, u32[]{:S(2)}) collective-permute-start(bf16[16,3712]{1,0:T(8,128)(2,1)S(1)} %get-tuple-element.51), channel_id=1, source_target_pairs={{0,18},{1,19},{2,16},{3,17},{4,22},{5,23},{6,20},{7,21},{8,26},{9,... | collective-permute-start | bytes 356360 | tf_op jit(solution)/shard_map/ppermute | solution.py:309
  36.6 1.3 %collective-permute-done.10.refs_1_ = bf16[16,3712]{1,0:T(8,128)(2,1)S(1)} collective-permute-done((bf16[16,3712]{1,0:T(8,128)(2,1)S(1)}, bf16[16,3712]{1,0:T(8,128)(2,1)S(1)}, u32[]{:S(2)}, u32[]{:S(2)}) %collective-permute-start.10) | collective-permute-done | bytes 118816 | tf_op jit(solution)/shard_map/ppermute | solution.py:309
  38.5 2.4 %collective-permute-done.13.refs_1_ = bf16[16,3712]{1,0:T(8,128)(2,1)S(1)} collective-permute-done((bf16[16,3712]{1,0:T(8,128)(2,1)S(1)}, bf16[16,3712]{1,0:T(8,128)(2,1)S(1)}, u32[]{:S(2)}, u32[]{:S(2)}) %collective-permute-start.13) | collective-permute-done | bytes 118816 | tf_op jit(solution)/shard_map/ppermute | solution.py:309
  40.9 1.5 %collective-permute-done.14.refs_3_ = bf16[16,3712]{1,0:T(8,128)(2,1)S(1)} collective-permute-done((bf16[16,3712]{1,0:T(8,128)(2,1)S(1)}, bf16[16,3712]{1,0:T(8,128)(2,1)S(1)}, u32[]{:S(2)}, u32[]{:S(2)}) %collective-permute-start.14) | collective-permute-done | bytes 118816 | tf_op jit(solution)/shard_map/ppermute | solution.py:309
  42.9 1.3 %collective-permute-start.17 = (bf16[32,3584]{1,0:T(8,128)(2,1)S(1)}, bf16[32,3584]{1,0:T(8,128)(2,1)S(1)}, u32[]{:S(2)}, u32[]{:S(2)}) collective-permute-start(bf16[32,3584]{1,0:T(8,128)(2,1)S(1)} %combine.2), channel_id=1, source_target_pairs={{0,20},{1,21},{2,22},{3,23},{4,28},{5,29},{6,30},{7,31},{8,16},{9,... | collective-permute-start | bytes 688136 | tf_op jit(solution)/shard_map/ppermute | solution.py:309
  44.2 2.6 %collective-permute-start.15 = (bf16[16,3712]{1,0:T(8,128)(2,1)S(1)}, bf16[16,3712]{1,0:T(8,128)(2,1)S(1)}, u32[]{:S(2)}, u32[]{:S(2)}) collective-permute-start(bf16[16,3712]{1,0:T(8,128)(2,1)S(1)} %get-tuple-element.55), channel_id=1, source_target_pairs={{0,24},{1,25},{2,26},{3,27},{4,16},{5,17},{6,18},{7,19},{8,28},{9,... | collective-permute-start | bytes 356360 | tf_op jit(solution)/shard_map/ppermute | solution.py:309
  47.1 4.6 %collective-permute-done.15.refs_2_ = bf16[16,3712]{1,0:T(8,128)(2,1)S(1)} collective-permute-done((bf16[16,3712]{1,0:T(8,128)(2,1)S(1)}, bf16[16,3712]{1,0:T(8,128)(2,1)S(1)}, u32[]{:S(2)}, u32[]{:S(2)}) %collective-permute-start.15) | collective-permute-done | bytes 118816 | tf_op jit(solution)/shard_map/ppermute | solution.py:309
  51.7 1.7 %collective-permute-done.16.refs_3_ = bf16[16,3712]{1,0:T(8,128)(2,1)S(1)} collective-permute-done((bf16[16,3712]{1,0:T(8,128)(2,1)S(1)}, bf16[16,3712]{1,0:T(8,128)(2,1)S(1)}, u32[]{:S(2)}, u32[]{:S(2)}) %collective-permute-start.16) | collective-permute-done | bytes 118816 | tf_op jit(solution)/shard_map/ppermute | solution.py:309
  53.6 1.1 %combine.3 = bf16[32,3584]{1,0:T(8,128)(2,1)} custom-call(bf16[16,3712]{1,0:T(8,128)(2,1)S(1)} %collective-permute-done.12.refs_0_, bf16[16,3712]{1,0:T(8,128)(2,1)S(1)} %collective-permute-done.13.refs_1_, bf16[16,3712]{1,0:T(8,128)(2,1)S(1)} %collective-permute-done.15.refs_2_, bf16[16,3712]{1,0:T(8,128)(2,1)S(1)} %collective-permute-done.16.refs_3_, ...), custom_call_target="tpu_custom_call" | custom-call | tf_op jit(solution)/shard_map/combine/pallas_call | solution.py:84
  (27 shorter events, 6.2 us)
Async XLA Ops:
  0.0 28.4 %collective-permute-start.8 = (bf16[3584,1024]{1,0:T(8,128)(2,1)}, bf16[3584,1024]{1,0:T(8,128)(2,1)S(1)}, u32[]{:S(2)}, u32[]{:S(2)}) collective-permute-start(bf16[3584,1024]{1,0:T(8,128)(2,1)} %bitcast.10), channel_id=1, source_target_pairs={{0,1},{1,0},{2,3},{3,2},{4,5},{5,4},{6,7},{7,6},{8,9},{9,8},{10,11... | collective-permute-start | bytes 22020104 | tf_op jit(solution)/shard_map/ppermute | solution.py:327
  0.5 27.9 %collective-permute-start.9 = (bf16[512,3584]{1,0:T(8,128)(2,1)}, bf16[512,3584]{1,0:T(8,128)(2,1)S(1)}, u32[]{:S(2)}, u32[]{:S(2)}) collective-permute-start(bf16[512,3584]{1,0:T(8,128)(2,1)} %bitcast.12), channel_id=1, source_target_pairs={{0,1},{1,0},{2,3},{3,2},{4,5},{5,4},{6,7},{7,6},{8,9},{9,8},{10,11... | collective-permute-start | bytes 11010056 | tf_op jit(solution)/shard_map/ppermute | solution.py:326
  0.5 12.6 %collective-permute-start.1 = (bf16[32,3584]{1,0:T(8,128)(2,1)}, bf16[32,3584]{1,0:T(8,128)(2,1)S(1)}, u32[]{:S(2)}, u32[]{:S(2)}) collective-permute-start(bf16[32,3584]{1,0:T(8,128)(2,1)} %bitcast.14), channel_id=1, source_target_pairs={{0,4},{1,5},{2,6},{3,7},{4,12},{5,13},{6,14},{7,15},{8,0},{9,1},{1... | collective-permute-start | bytes 688136 | tf_op jit(solution)/shard_map/ppermute | solution.py:309
  4.5 0.9 %copy-start.2 = (bf16[1,32,3584]{2,1,0:T(8,128)(2,1)S(1)}, bf16[1,32,3584]{2,1,0:T(8,128)(2,1)}, u32[]{:S(2)}) copy-start(bf16[1,32,3584]{2,1,0:T(8,128)(2,1)} %param.5) | copy-start | bytes 688132
  5.9 4.9 %collective-permute-start = (bf16[16,3712]{1,0:T(8,128)(2,1)S(1)}, bf16[16,3712]{1,0:T(8,128)(2,1)S(1)}, u32[]{:S(2)}, u32[]{:S(2)}) collective-permute-start(bf16[16,3712]{1,0:T(8,128)(2,1)S(1)} %get-tuple-element.34), channel_id=1, source_target_pairs={{0,2},{1,3},{2,0},{3,1},{4,6},{5,7},{6,4},{7,5},{8,10},{9,11},{10,... | collective-permute-start | bytes 356360 | tf_op jit(solution)/shard_map/ppermute | solution.py:309
  7.5 5.7 %collective-permute-start.2 = (bf16[32,128]{1,0:T(8,128)(2,1)S(1)}, bf16[32,128]{1,0:T(8,128)(2,1)S(1)}, u32[]{:S(2)}, u32[]{:S(2)}) collective-permute-start(bf16[32,128]{1,0:T(8,128)(2,1)S(1)} %prepare.1.marks), channel_id=1, source_target_pairs={{0,4},{1,5},{2,6},{3,7},{4,12},{5,13},{6,14},{7,15},{8,0},{9,1},{1... | collective-permute-start | bytes 24584 | tf_op jit(solution)/shard_map/ppermute | solution.py:309
  10.8 7.6 %collective-permute-start.6 = (bf16[16,3712]{1,0:T(8,128)(2,1)S(1)}, bf16[16,3712]{1,0:T(8,128)(2,1)S(1)}, u32[]{:S(2)}, u32[]{:S(2)}) collective-permute-start(bf16[16,3712]{1,0:T(8,128)(2,1)S(1)} %get-tuple-element.42), channel_id=1, source_target_pairs={{0,10},{1,11},{2,8},{3,9},{4,2},{5,3},{6,0},{7,1},{8,14},{9,15},{1... | collective-permute-start | bytes 356360 | tf_op jit(solution)/shard_map/ppermute | solution.py:309
  13.6 7.7 %collective-permute-start.5 = (bf16[16,3712]{1,0:T(8,128)(2,1)S(1)}, bf16[16,3712]{1,0:T(8,128)(2,1)S(1)}, u32[]{:S(2)}, u32[]{:S(2)}) collective-permute-start(bf16[16,3712]{1,0:T(8,128)(2,1)S(1)} %get-tuple-element.39), channel_id=1, source_target_pairs={{0,2},{1,3},{2,0},{3,1},{4,6},{5,7},{6,4},{7,5},{8,10},{9,11},{10,... | collective-permute-start | bytes 356360 | tf_op jit(solution)/shard_map/ppermute | solution.py:309
  14.1 12.6 %collective-permute-start.3 = (bf16[16,3712]{1,0:T(8,128)(2,1)S(1)}, bf16[16,3712]{1,0:T(8,128)(2,1)S(1)}, u32[]{:S(2)}, u32[]{:S(2)}) collective-permute-start(bf16[16,3712]{1,0:T(8,128)(2,1)S(1)} %get-tuple-element.37), channel_id=1, source_target_pairs={{0,4},{1,5},{2,6},{3,7},{4,12},{5,13},{6,14},{7,15},{8,0},{9,1},{1... | collective-permute-start | bytes 356360 | tf_op jit(solution)/shard_map/ppermute | solution.py:309
  18.4 8.2 %collective-permute-start.4 = (bf16[16,3712]{1,0:T(8,128)(2,1)S(1)}, bf16[16,3712]{1,0:T(8,128)(2,1)S(1)}, u32[]{:S(2)}, u32[]{:S(2)}) collective-permute-start(bf16[16,3712]{1,0:T(8,128)(2,1)S(1)} %get-tuple-element.38), channel_id=1, source_target_pairs={{0,6},{1,7},{2,4},{3,5},{4,14},{5,15},{6,12},{7,13},{8,2},{9,3},{1... | collective-permute-start | bytes 356360 | tf_op jit(solution)/shard_map/ppermute | solution.py:309
  21.2 5.4 %collective-permute-start.7 = (bf16[16,3712]{1,0:T(8,128)(2,1)S(1)}, bf16[16,3712]{1,0:T(8,128)(2,1)S(1)}, u32[]{:S(2)}, u32[]{:S(2)}) collective-permute-start(bf16[16,3712]{1,0:T(8,128)(2,1)S(1)} %get-tuple-element.43), channel_id=1, source_target_pairs={{0,8},{1,9},{2,10},{3,11},{4,0},{5,1},{6,2},{7,3},{8,12},{9,13},{1... | collective-permute-start | bytes 356360 | tf_op jit(solution)/shard_map/ppermute | solution.py:309
  21.2 3.1 %copy-start = (bf16[1,3584,1024]{2,1,0:T(8,128)(2,1)S(1)}, bf16[1,3584,1024]{2,1,0:T(8,128)(2,1)}, u32[]{:S(2)}) copy-start(bf16[1,3584,1024]{2,1,0:T(8,128)(2,1)} %param.8) | copy-start | bytes 22020100
  24.3 2.0 %copy-start.1 = (bf16[1,512,3584]{2,1,0:T(8,128)(2,1)S(1)}, bf16[1,512,3584]{2,1,0:T(8,128)(2,1)}, u32[]{:S(2)}) copy-start(bf16[1,512,3584]{2,1,0:T(8,128)(2,1)} %param.9) | copy-start | bytes 11010052
  30.1 7.8 %collective-permute-start.10 = (bf16[16,3712]{1,0:T(8,128)(2,1)S(1)}, bf16[16,3712]{1,0:T(8,128)(2,1)S(1)}, u32[]{:S(2)}, u32[]{:S(2)}) collective-permute-start(bf16[16,3712]{1,0:T(8,128)(2,1)S(1)} %get-tuple-element.48), channel_id=1, source_target_pairs={{0,6},{1,7},{2,4},{3,5},{4,14},{5,15},{6,12},{7,13},{8,2},{9,3},{1... | collective-permute-start | bytes 356360 | tf_op jit(solution)/shard_map/ppermute | solution.py:309
  32.8 5.6 %collective-permute-start.11 = (bf16[16,3712]{1,0:T(8,128)(2,1)S(1)}, bf16[16,3712]{1,0:T(8,128)(2,1)S(1)}, u32[]{:S(2)}, u32[]{:S(2)}) collective-permute-start(bf16[16,3712]{1,0:T(8,128)(2,1)S(1)} %get-tuple-element.49), channel_id=1, source_target_pairs={{0,2},{1,3},{2,0},{3,1},{4,6},{5,7},{6,4},{7,5},{8,10},{9,11},{10,... | collective-permute-start | bytes 356360 | tf_op jit(solution)/shard_map/ppermute | solution.py:309
  33.7 4.8 %collective-permute-start.12 = (bf16[16,3712]{1,0:T(8,128)(2,1)S(1)}, bf16[16,3712]{1,0:T(8,128)(2,1)S(1)}, u32[]{:S(2)}, u32[]{:S(2)}) collective-permute-start(bf16[16,3712]{1,0:T(8,128)(2,1)S(1)} %get-tuple-element.50), channel_id=1, source_target_pairs={{0,16},{1,17},{2,18},{3,19},{4,20},{5,21},{6,22},{7,23},{8,24},{9,... | collective-permute-start | bytes 356360 | tf_op jit(solution)/shard_map/ppermute | solution.py:309
  35.2 5.7 %collective-permute-start.13 = (bf16[16,3712]{1,0:T(8,128)(2,1)S(1)}, bf16[16,3712]{1,0:T(8,128)(2,1)S(1)}, u32[]{:S(2)}, u32[]{:S(2)}) collective-permute-start(bf16[16,3712]{1,0:T(8,128)(2,1)S(1)} %get-tuple-element.51), channel_id=1, source_target_pairs={{0,18},{1,19},{2,16},{3,17},{4,22},{5,23},{6,20},{7,21},{8,26},{9,... | collective-permute-start | bytes 356360 | tf_op jit(solution)/shard_map/ppermute | solution.py:309
  36.3 6.2 %collective-permute-start.14 = (bf16[16,3712]{1,0:T(8,128)(2,1)S(1)}, bf16[16,3712]{1,0:T(8,128)(2,1)S(1)}, u32[]{:S(2)}, u32[]{:S(2)}) collective-permute-start(bf16[16,3712]{1,0:T(8,128)(2,1)S(1)} %get-tuple-element.52), channel_id=1, source_target_pairs={{0,4},{1,5},{2,6},{3,7},{4,12},{5,13},{6,14},{7,15},{8,0},{9,1},{1... | collective-permute-start | bytes 356360 | tf_op jit(solution)/shard_map/ppermute | solution.py:309
  42.9 10.7 %collective-permute-start.17 = (bf16[32,3584]{1,0:T(8,128)(2,1)S(1)}, bf16[32,3584]{1,0:T(8,128)(2,1)S(1)}, u32[]{:S(2)}, u32[]{:S(2)}) collective-permute-start(bf16[32,3584]{1,0:T(8,128)(2,1)S(1)} %combine.2), channel_id=1, source_target_pairs={{0,20},{1,21},{2,22},{3,23},{4,28},{5,29},{6,30},{7,31},{8,16},{9,... | collective-permute-start | bytes 688136 | tf_op jit(solution)/shard_map/ppermute | solution.py:309
  44.2 7.5 %collective-permute-start.15 = (bf16[16,3712]{1,0:T(8,128)(2,1)S(1)}, bf16[16,3712]{1,0:T(8,128)(2,1)S(1)}, u32[]{:S(2)}, u32[]{:S(2)}) collective-permute-start(bf16[16,3712]{1,0:T(8,128)(2,1)S(1)} %get-tuple-element.55), channel_id=1, source_target_pairs={{0,24},{1,25},{2,26},{3,27},{4,16},{5,17},{6,18},{7,19},{8,28},{9,... | collective-permute-start | bytes 356360 | tf_op jit(solution)/shard_map/ppermute | solution.py:309
  46.8 6.6 %collective-permute-start.16 = (bf16[16,3712]{1,0:T(8,128)(2,1)S(1)}, bf16[16,3712]{1,0:T(8,128)(2,1)S(1)}, u32[]{:S(2)}, u32[]{:S(2)}) collective-permute-start(bf16[16,3712]{1,0:T(8,128)(2,1)S(1)} %get-tuple-element.56), channel_id=1, source_target_pairs={{0,26},{1,27},{2,24},{3,25},{4,18},{5,19},{6,16},{7,17},{8,30},{9,... | collective-permute-start | bytes 356360 | tf_op jit(solution)/shard_map/ppermute | solution.py:309

commit v28 on v27

--- a/solution.py
+++ b/solution.py
@@ -330,7 +330,8 @@
     marks1 = sent(marks, sections, 0, 1, 0)
     own0, other, back0, back1 = choose(tokens, marks, capacity, ((0, 0), (0, 1), (3, 0), (3, 1)))
     other0 = sent(other, sections, 0, 0, 1)
-    block1 = after(block1, other0)
+    near_in = loaded(after(w_in, own0))
+    block1 = after(block1, (near_in, other0))
     own1, other, on0, on1 = choose(block1, marks1, capacity, ((0, 0), (0, 1), (1, 0), (1, 1)))
     other1 = sent(other, sections, 0, 0, 1)
     own2 = sent(on0, sections, 0, 1, 0)
@@ -338,7 +339,7 @@
     other3 = sent(after(back1, other0), sections, 0, 3, 1)
     back0 = after(back0, (other1, other3))
     own3 = sent(back0, sections, 0, 3, 0)
-    near = (loaded(after(w_in, back0)), loaded(after(w_out, back0)))
+    near = (near_in, loaded(after(w_out, back0)))
     pieces = (own0, other0, own1, own2, other2, other1, own3, other3)
     places = ((0, 0), (0, 1), (1, 0), (2, 0), (2, 1), (1, 1), (3, 0), (3, 1))
     slots, total = near_pass(pieces, near)

time: 54.9 us -> 55.7 us (1.015)
  local copies, waits for them, and re-layouts: 5.55 us -> 4.02 us
  waiting for transfers between devices: 16.1 us -> 17.6 us
  starting transfers between devices: 25.4 us -> 26.2 us
    ppermute x16, waiting for transfers between devices: 16.1 us -> 17.6 us  [sent(): return lax.ppermute(shard, ('section', 'expert'), pairs)]
    unnamed x6, local copies, waits for them, and re-layouts: 5.55 us -> 4.02 us
    ppermute x16, starting transfers between devices: 24.9 us -> 25.7 us  [sent(): return lax.ppermute(shard, ('section', 'expert'), pairs)]
  transfers between devices with their start and end apart: 18 -> 18, of which waited for: 10 -> 7; matrix products, arithmetic and copies ran while one was open for 0% -> 0% of each run, Pallas kernels for 8% -> 8%
where the time goes in v28:
time: 55.7 us; the launch traced here: 55.5 us
  starting transfers between devices  26.2 us (47%)
  waiting for transfers between devices  17.6 us (32%)
  Pallas kernels  7.57 us (14%)
  local copies, waits for them, and re-layouts  4.02 us (7%)
    ppermute x16, starting transfers between devices, sent(): return lax.ppermute(shard, ('section', 'expert'), pairs)  25.7 us
    ppermute x16, waiting for transfers between devices, sent(): return lax.ppermute(shard, ('section', 'expert'), pairs)  17.6 us
    pallas_call x9, Pallas kernels, local_call(): pl.pallas_call(kernel, out_shape=out_shape, in_specs=[vmem if spec is Non...  7.57 us
    unnamed x6, local copies, waits for them, and re-layouts  4.02 us
  transfers between devices with their start and end apart: 18, of which 7 were waited for; matrix products, arithmetic and copies ran while one was open for 0% of the time, Pallas kernels for 8%

profile of v28, /device:TPU:0, one launch (start us, length us, event | category | flops | bytes accessed | tf_op | source)
XLA Modules:
  0.0 55.5 jit_solution(4199484742784774535)
XLA Ops:
  0.5 3.0 %collective-permute-start.1 = (bf16[32,3584]{1,0:T(8,128)(2,1)}, bf16[32,3584]{1,0:T(8,128)(2,1)S(1)}, u32[]{:S(2)}, u32[]{:S(2)}) collective-permute-start(bf16[32,3584]{1,0:T(8,128)(2,1)} %bitcast.14), channel_id=1, source_target_pairs={{0,4},{1,5},{2,6},{3,7},{4,12},{5,13},{6,14},{7,15},{8,0},{9,1},{1... | collective-permute-start | bytes 688136 | tf_op jit(solution)/shard_map/ppermute | solution.py:309
  3.5 1.0 %prepare.1.marks = bf16[32,128]{1,0:T(8,128)(2,1)S(1)} custom-call(s32[2,32]{1,0:T(2,128)} %bitcast.16, f32[2,32]{1,0:T(2,128)} %bitcast.17), custom_call_target="tpu_custom_call" | custom-call | tf_op jit(solution)/shard_map/prepare/pallas_call | solution.py:84
  4.6 0.9 %copy-done.2 = bf16[1,32,3584]{2,1,0:T(8,128)(2,1)S(1)} copy-done((bf16[1,32,3584]{2,1,0:T(8,128)(2,1)S(1)}, bf16[1,32,3584]{2,1,0:T(8,128)(2,1)}, u32[]{:S(2)}) %copy-start.2) | copy-done | bytes 229400
  5.9 1.6 %collective-permute-start = (bf16[16,3712]{1,0:T(8,128)(2,1)S(1)}, bf16[16,3712]{1,0:T(8,128)(2,1)S(1)}, u32[]{:S(2)}, u32[]{:S(2)}) collective-permute-start(bf16[16,3712]{1,0:T(8,128)(2,1)S(1)} %get-tuple-element.34), channel_id=1, source_target_pairs={{0,2},{1,3},{2,0},{3,1},{4,6},{5,7},{6,4},{7,5},{8,10},{9,11},{10,... | collective-permute-start | bytes 356360 | tf_op jit(solution)/shard_map/ppermute | solution.py:309
  7.5 2.6 %collective-permute-start.2 = (bf16[32,128]{1,0:T(8,128)(2,1)S(1)}, bf16[32,128]{1,0:T(8,128)(2,1)S(1)}, u32[]{:S(2)}, u32[]{:S(2)}) collective-permute-start(bf16[32,128]{1,0:T(8,128)(2,1)S(1)} %prepare.1.marks), channel_id=1, source_target_pairs={{0,4},{1,5},{2,6},{3,7},{4,12},{5,13},{6,14},{7,15},{8,0},{9,1},{1... | collective-permute-start | bytes 24584 | tf_op jit(solution)/shard_map/ppermute | solution.py:309
  10.1 3.1 %copy-done = bf16[1,3584,1024]{2,1,0:T(8,128)(2,1)S(1)} copy-done((bf16[1,3584,1024]{2,1,0:T(8,128)(2,1)S(1)}, bf16[1,3584,1024]{2,1,0:T(8,128)(2,1)}, u32[]{:S(2)}) %copy-start) | copy-done | bytes 7340056
  14.4 1.6 %collective-permute-start.5 = (bf16[16,3712]{1,0:T(8,128)(2,1)S(1)}, bf16[16,3712]{1,0:T(8,128)(2,1)S(1)}, u32[]{:S(2)}, u32[]{:S(2)}) collective-permute-start(bf16[16,3712]{1,0:T(8,128)(2,1)S(1)} %get-tuple-element.40), channel_id=1, source_target_pairs={{0,2},{1,3},{2,0},{3,1},{4,6},{5,7},{6,4},{7,5},{8,10},{9,11},{10,... | collective-permute-start | bytes 356360 | tf_op jit(solution)/shard_map/ppermute | solution.py:309
  16.0 1.7 %collective-permute-start.3 = (bf16[16,3712]{1,0:T(8,128)(2,1)S(1)}, bf16[16,3712]{1,0:T(8,128)(2,1)S(1)}, u32[]{:S(2)}, u32[]{:S(2)}) collective-permute-start(bf16[16,3712]{1,0:T(8,128)(2,1)S(1)} %get-tuple-element.38), channel_id=1, source_target_pairs={{0,4},{1,5},{2,6},{3,7},{4,12},{5,13},{6,14},{7,15},{8,0},{9,1},{1... | collective-permute-start | bytes 356360 | tf_op jit(solution)/shard_map/ppermute | solution.py:309
  17.7 3.1 %collective-permute-done.6.refs_7_ = bf16[16,3712]{1,0:T(8,128)(2,1)S(1)} collective-permute-done((bf16[16,3712]{1,0:T(8,128)(2,1)S(1)}, bf16[16,3712]{1,0:T(8,128)(2,1)S(1)}, u32[]{:S(2)}, u32[]{:S(2)}) %collective-permute-start.6) | collective-permute-done | bytes 118816 | tf_op jit(solution)/shard_map/ppermute | solution.py:309
  20.8 1.3 %collective-permute-start.4 = (bf16[16,3712]{1,0:T(8,128)(2,1)S(1)}, bf16[16,3712]{1,0:T(8,128)(2,1)S(1)}, u32[]{:S(2)}, u32[]{:S(2)}) collective-permute-start(bf16[16,3712]{1,0:T(8,128)(2,1)S(1)} %get-tuple-element.39), channel_id=1, source_target_pairs={{0,6},{1,7},{2,4},{3,5},{4,14},{5,15},{6,12},{7,13},{8,2},{9,3},{1... | collective-permute-start | bytes 356360 | tf_op jit(solution)/shard_map/ppermute | solution.py:309
  23.2 5.5 %collective-permute-done.4.refs_4_ = bf16[16,3712]{1,0:T(8,128)(2,1)S(1)} collective-permute-done((bf16[16,3712]{1,0:T(8,128)(2,1)S(1)}, bf16[16,3712]{1,0:T(8,128)(2,1)S(1)}, u32[]{:S(2)}, u32[]{:S(2)}) %collective-permute-start.4) | collective-permute-done | bytes 118816 | tf_op jit(solution)/shard_map/ppermute | solution.py:309
  28.7 1.7 %near_pass.1 = (bf16[128,3712]{1,0:T(8,128)(2,1)S(1)}, f32[128,3584]{1,0:T(8,128)S(1)}) custom-call(bf16[16,3712]{1,0:T(8,128)(2,1)S(1)} %get-tuple-element.33.refs_0_, bf16[16,3712]{1,0:T(8,128)(2,1)S(1)} %collective-permute-done.refs_1_, bf16[16,3712]{1,0:T(8,128)(2,1)S(1)} %get-tuple-element.37.refs_2_, ...), custom_call_target="tpu_custom_call" | custom-call | bytes 11010048 | tf_op jit(solution)/shard_map/near_pass/pallas_call | solution.py:84
  30.5 1.7 %far_pass.1 = (bf16[16,3712]{1,0:T(8,128)(2,1)S(1)}, bf16[16,3712]{1,0:T(8,128)(2,1)S(1)}, bf16[16,3712]{1,0:T(8,128)(2,1)S(1)}, bf16[16,3712]{1,0:T(8,128)(2,1)...) custom-call(bf16[128,3712]{1,0:T(8,128)(2,1)S(1)} %get-tuple-element, ...), custom_call_target="tpu_custom_call" | custom-call | bytes 11010048 | tf_op jit(solution)/shard_map/far_pass/pallas_call | solution.py:84
  32.6 2.2 %collective-permute-start.11 = (bf16[16,3712]{1,0:T(8,128)(2,1)S(1)}, bf16[16,3712]{1,0:T(8,128)(2,1)S(1)}, u32[]{:S(2)}, u32[]{:S(2)}) collective-permute-start(bf16[16,3712]{1,0:T(8,128)(2,1)S(1)} %get-tuple-element.49), channel_id=1, source_target_pairs={{0,2},{1,3},{2,0},{3,1},{4,6},{5,7},{6,4},{7,5},{8,10},{9,11},{10,... | collective-permute-start | bytes 356360 | tf_op jit(solution)/shard_map/ppermute | solution.py:309
  34.8 1.5 %collective-permute-start.12 = (bf16[16,3712]{1,0:T(8,128)(2,1)S(1)}, bf16[16,3712]{1,0:T(8,128)(2,1)S(1)}, u32[]{:S(2)}, u32[]{:S(2)}) collective-permute-start(bf16[16,3712]{1,0:T(8,128)(2,1)S(1)} %get-tuple-element.50), channel_id=1, source_target_pairs={{0,16},{1,17},{2,18},{3,19},{4,20},{5,21},{6,22},{7,23},{8,24},{9,... | collective-permute-start | bytes 356360 | tf_op jit(solution)/shard_map/ppermute | solution.py:309
  36.3 1.1 %collective-permute-start.14 = (bf16[16,3712]{1,0:T(8,128)(2,1)S(1)}, bf16[16,3712]{1,0:T(8,128)(2,1)S(1)}, u32[]{:S(2)}, u32[]{:S(2)}) collective-permute-start(bf16[16,3712]{1,0:T(8,128)(2,1)S(1)} %get-tuple-element.52), channel_id=1, source_target_pairs={{0,4},{1,5},{2,6},{3,7},{4,12},{5,13},{6,14},{7,15},{8,0},{9,1},{1... | collective-permute-start | bytes 356360 | tf_op jit(solution)/shard_map/ppermute | solution.py:309
  37.4 2.5 %collective-permute-done.10.refs_1_ = bf16[16,3712]{1,0:T(8,128)(2,1)S(1)} collective-permute-done((bf16[16,3712]{1,0:T(8,128)(2,1)S(1)}, bf16[16,3712]{1,0:T(8,128)(2,1)S(1)}, u32[]{:S(2)}, u32[]{:S(2)}) %collective-permute-start.10) | collective-permute-done | bytes 118816 | tf_op jit(solution)/shard_map/ppermute | solution.py:309
  40.0 2.0 %collective-permute-done.13.refs_1_ = bf16[16,3712]{1,0:T(8,128)(2,1)S(1)} collective-permute-done((bf16[16,3712]{1,0:T(8,128)(2,1)S(1)}, bf16[16,3712]{1,0:T(8,128)(2,1)S(1)}, u32[]{:S(2)}, u32[]{:S(2)}) %collective-permute-start.13) | collective-permute-done | bytes 118816 | tf_op jit(solution)/shard_map/ppermute | solution.py:309
  42.5 1.7 %collective-permute-start.17 = (bf16[32,3584]{1,0:T(8,128)(2,1)S(1)}, bf16[32,3584]{1,0:T(8,128)(2,1)S(1)}, u32[]{:S(2)}, u32[]{:S(2)}) collective-permute-start(bf16[32,3584]{1,0:T(8,128)(2,1)S(1)} %combine.2), channel_id=1, source_target_pairs={{0,20},{1,21},{2,22},{3,23},{4,28},{5,29},{6,30},{7,31},{8,16},{9,... | collective-permute-start | bytes 688136 | tf_op jit(solution)/shard_map/ppermute | solution.py:309
  44.2 2.2 %collective-permute-start.15 = (bf16[16,3712]{1,0:T(8,128)(2,1)S(1)}, bf16[16,3712]{1,0:T(8,128)(2,1)S(1)}, u32[]{:S(2)}, u32[]{:S(2)}) collective-permute-start(bf16[16,3712]{1,0:T(8,128)(2,1)S(1)} %get-tuple-element.55), channel_id=1, source_target_pairs={{0,24},{1,25},{2,26},{3,27},{4,16},{5,17},{6,18},{7,19},{8,28},{9,... | collective-permute-start | bytes 356360 | tf_op jit(solution)/shard_map/ppermute | solution.py:309
  46.3 3.7 %collective-permute-start.16 = (bf16[16,3712]{1,0:T(8,128)(2,1)S(1)}, bf16[16,3712]{1,0:T(8,128)(2,1)S(1)}, u32[]{:S(2)}, u32[]{:S(2)}) collective-permute-start(bf16[16,3712]{1,0:T(8,128)(2,1)S(1)} %get-tuple-element.56), channel_id=1, source_target_pairs={{0,26},{1,27},{2,24},{3,25},{4,18},{5,19},{6,16},{7,17},{8,30},{9,... | collective-permute-start | bytes 356360 | tf_op jit(solution)/shard_map/ppermute | solution.py:309
  50.0 2.1 %collective-permute-done.15.refs_2_ = bf16[16,3712]{1,0:T(8,128)(2,1)S(1)} collective-permute-done((bf16[16,3712]{1,0:T(8,128)(2,1)S(1)}, bf16[16,3712]{1,0:T(8,128)(2,1)S(1)}, u32[]{:S(2)}, u32[]{:S(2)}) %collective-permute-start.15) | collective-permute-done | bytes 118816 | tf_op jit(solution)/shard_map/ppermute | solution.py:309
  52.1 2.3 %collective-permute-done.16.refs_3_ = bf16[16,3712]{1,0:T(8,128)(2,1)S(1)} collective-permute-done((bf16[16,3712]{1,0:T(8,128)(2,1)S(1)}, bf16[16,3712]{1,0:T(8,128)(2,1)S(1)}, u32[]{:S(2)}, u32[]{:S(2)}) %collective-permute-start.16) | collective-permute-done | bytes 118816 | tf_op jit(solution)/shard_map/ppermute | solution.py:309
  54.4 1.1 %combine.3 = bf16[32,3584]{1,0:T(8,128)(2,1)} custom-call(bf16[16,3712]{1,0:T(8,128)(2,1)S(1)} %collective-permute-done.12.refs_0_, bf16[16,3712]{1,0:T(8,128)(2,1)S(1)} %collective-permute-done.13.refs_1_, bf16[16,3712]{1,0:T(8,128)(2,1)S(1)} %collective-permute-done.15.refs_2_, bf16[16,3712]{1,0:T(8,128)(2,1)S(1)} %collective-permute-done.16.refs_3_, ...), custom_call_target="tpu_custom_call" | custom-call | tf_op jit(solution)/shard_map/combine/pallas_call | solution.py:84
  (27 shorter events, 4.2 us)
Async XLA Ops:
  0.0 30.5 %collective-permute-start.8 = (bf16[3584,1024]{1,0:T(8,128)(2,1)}, bf16[3584,1024]{1,0:T(8,128)(2,1)S(1)}, u32[]{:S(2)}, u32[]{:S(2)}) collective-permute-start(bf16[3584,1024]{1,0:T(8,128)(2,1)} %bitcast.10), channel_id=1, source_target_pairs={{0,1},{1,0},{2,3},{3,2},{4,5},{5,4},{6,7},{7,6},{8,9},{9,8},{10,11... | collective-permute-start | bytes 22020104 | tf_op jit(solution)/shard_map/ppermute | solution.py:327
  0.5 30.0 %collective-permute-start.9 = (bf16[512,3584]{1,0:T(8,128)(2,1)}, bf16[512,3584]{1,0:T(8,128)(2,1)S(1)}, u32[]{:S(2)}, u32[]{:S(2)}) collective-permute-start(bf16[512,3584]{1,0:T(8,128)(2,1)} %bitcast.12), channel_id=1, source_target_pairs={{0,1},{1,0},{2,3},{3,2},{4,5},{5,4},{6,7},{7,6},{8,9},{9,8},{10,11... | collective-permute-start | bytes 11010056 | tf_op jit(solution)/shard_map/ppermute | solution.py:326
  0.5 13.5 %collective-permute-start.1 = (bf16[32,3584]{1,0:T(8,128)(2,1)}, bf16[32,3584]{1,0:T(8,128)(2,1)S(1)}, u32[]{:S(2)}, u32[]{:S(2)}) collective-permute-start(bf16[32,3584]{1,0:T(8,128)(2,1)} %bitcast.14), channel_id=1, source_target_pairs={{0,4},{1,5},{2,6},{3,7},{4,12},{5,13},{6,14},{7,15},{8,0},{9,1},{1... | collective-permute-start | bytes 688136 | tf_op jit(solution)/shard_map/ppermute | solution.py:309
  4.5 0.9 %copy-start.2 = (bf16[1,32,3584]{2,1,0:T(8,128)(2,1)S(1)}, bf16[1,32,3584]{2,1,0:T(8,128)(2,1)}, u32[]{:S(2)}) copy-start(bf16[1,32,3584]{2,1,0:T(8,128)(2,1)} %param.5) | copy-start | bytes 688132
  5.9 7.8 %collective-permute-start = (bf16[16,3712]{1,0:T(8,128)(2,1)S(1)}, bf16[16,3712]{1,0:T(8,128)(2,1)S(1)}, u32[]{:S(2)}, u32[]{:S(2)}) collective-permute-start(bf16[16,3712]{1,0:T(8,128)(2,1)S(1)} %get-tuple-element.34), channel_id=1, source_target_pairs={{0,2},{1,3},{2,0},{3,1},{4,6},{5,7},{6,4},{7,5},{8,10},{9,11},{10,... | collective-permute-start | bytes 356360 | tf_op jit(solution)/shard_map/ppermute | solution.py:309
  7.5 6.5 %collective-permute-start.2 = (bf16[32,128]{1,0:T(8,128)(2,1)S(1)}, bf16[32,128]{1,0:T(8,128)(2,1)S(1)}, u32[]{:S(2)}, u32[]{:S(2)}) collective-permute-start(bf16[32,128]{1,0:T(8,128)(2,1)S(1)} %prepare.1.marks), channel_id=1, source_target_pairs={{0,4},{1,5},{2,6},{3,7},{4,12},{5,13},{6,14},{7,15},{8,0},{9,1},{1... | collective-permute-start | bytes 24584 | tf_op jit(solution)/shard_map/ppermute | solution.py:309
  10.1 3.1 %copy-start = (bf16[1,3584,1024]{2,1,0:T(8,128)(2,1)S(1)}, bf16[1,3584,1024]{2,1,0:T(8,128)(2,1)}, u32[]{:S(2)}) copy-start(bf16[1,3584,1024]{2,1,0:T(8,128)(2,1)} %param.8) | copy-start | bytes 22020100
  13.2 9.7 %copy-start.1 = (bf16[1,512,3584]{2,1,0:T(8,128)(2,1)S(1)}, bf16[1,512,3584]{2,1,0:T(8,128)(2,1)}, u32[]{:S(2)}) copy-start(bf16[1,512,3584]{2,1,0:T(8,128)(2,1)} %param.9) | copy-start | bytes 11010052
  13.7 7.1 %collective-permute-start.6 = (bf16[16,3712]{1,0:T(8,128)(2,1)S(1)}, bf16[16,3712]{1,0:T(8,128)(2,1)S(1)}, u32[]{:S(2)}, u32[]{:S(2)}) collective-permute-start(bf16[16,3712]{1,0:T(8,128)(2,1)S(1)} %get-tuple-element.43), channel_id=1, source_target_pairs={{0,10},{1,11},{2,8},{3,9},{4,2},{5,3},{6,0},{7,1},{8,14},{9,15},{1... | collective-permute-start | bytes 356360 | tf_op jit(solution)/shard_map/ppermute | solution.py:309
  14.4 7.7 %collective-permute-start.5 = (bf16[16,3712]{1,0:T(8,128)(2,1)S(1)}, bf16[16,3712]{1,0:T(8,128)(2,1)S(1)}, u32[]{:S(2)}, u32[]{:S(2)}) collective-permute-start(bf16[16,3712]{1,0:T(8,128)(2,1)S(1)} %get-tuple-element.40), channel_id=1, source_target_pairs={{0,2},{1,3},{2,0},{3,1},{4,6},{5,7},{6,4},{7,5},{8,10},{9,11},{10,... | collective-permute-start | bytes 356360 | tf_op jit(solution)/shard_map/ppermute | solution.py:309
  16.0 7.1 %collective-permute-start.3 = (bf16[16,3712]{1,0:T(8,128)(2,1)S(1)}, bf16[16,3712]{1,0:T(8,128)(2,1)S(1)}, u32[]{:S(2)}, u32[]{:S(2)}) collective-permute-start(bf16[16,3712]{1,0:T(8,128)(2,1)S(1)} %get-tuple-element.38), channel_id=1, source_target_pairs={{0,4},{1,5},{2,6},{3,7},{4,12},{5,13},{6,14},{7,15},{8,0},{9,1},{1... | collective-permute-start | bytes 356360 | tf_op jit(solution)/shard_map/ppermute | solution.py:309
  20.8 7.9 %collective-permute-start.4 = (bf16[16,3712]{1,0:T(8,128)(2,1)S(1)}, bf16[16,3712]{1,0:T(8,128)(2,1)S(1)}, u32[]{:S(2)}, u32[]{:S(2)}) collective-permute-start(bf16[16,3712]{1,0:T(8,128)(2,1)S(1)} %get-tuple-element.39), channel_id=1, source_target_pairs={{0,6},{1,7},{2,4},{3,5},{4,14},{5,15},{6,12},{7,13},{8,2},{9,3},{1... | collective-permute-start | bytes 356360 | tf_op jit(solution)/shard_map/ppermute | solution.py:309
  22.1 6.6 %collective-permute-start.7 = (bf16[16,3712]{1,0:T(8,128)(2,1)S(1)}, bf16[16,3712]{1,0:T(8,128)(2,1)S(1)}, u32[]{:S(2)}, u32[]{:S(2)}) collective-permute-start(bf16[16,3712]{1,0:T(8,128)(2,1)S(1)} %get-tuple-element.44), channel_id=1, source_target_pairs={{0,8},{1,9},{2,10},{3,11},{4,0},{5,1},{6,2},{7,3},{8,12},{9,13},{1... | collective-permute-start | bytes 356360 | tf_op jit(solution)/shard_map/ppermute | solution.py:309
  32.2 7.7 %collective-permute-start.10 = (bf16[16,3712]{1,0:T(8,128)(2,1)S(1)}, bf16[16,3712]{1,0:T(8,128)(2,1)S(1)}, u32[]{:S(2)}, u32[]{:S(2)}) collective-permute-start(bf16[16,3712]{1,0:T(8,128)(2,1)S(1)} %get-tuple-element.48), channel_id=1, source_target_pairs={{0,6},{1,7},{2,4},{3,5},{4,14},{5,15},{6,12},{7,13},{8,2},{9,3},{1... | collective-permute-start | bytes 356360 | tf_op jit(solution)/shard_map/ppermute | solution.py:309
  32.6 7.3 %collective-permute-start.11 = (bf16[16,3712]{1,0:T(8,128)(2,1)S(1)}, bf16[16,3712]{1,0:T(8,128)(2,1)S(1)}, u32[]{:S(2)}, u32[]{:S(2)}) collective-permute-start(bf16[16,3712]{1,0:T(8,128)(2,1)S(1)} %get-tuple-element.49), channel_id=1, source_target_pairs={{0,2},{1,3},{2,0},{3,1},{4,6},{5,7},{6,4},{7,5},{8,10},{9,11},{10,... | collective-permute-start | bytes 356360 | tf_op jit(solution)/shard_map/ppermute | solution.py:309
  34.8 5.2 %collective-permute-start.12 = (bf16[16,3712]{1,0:T(8,128)(2,1)S(1)}, bf16[16,3712]{1,0:T(8,128)(2,1)S(1)}, u32[]{:S(2)}, u32[]{:S(2)}) collective-permute-start(bf16[16,3712]{1,0:T(8,128)(2,1)S(1)} %get-tuple-element.50), channel_id=1, source_target_pairs={{0,16},{1,17},{2,18},{3,19},{4,20},{5,21},{6,22},{7,23},{8,24},{9,... | collective-permute-start | bytes 356360 | tf_op jit(solution)/shard_map/ppermute | solution.py:309
  36.3 5.7 %collective-permute-start.13 = (bf16[16,3712]{1,0:T(8,128)(2,1)S(1)}, bf16[16,3712]{1,0:T(8,128)(2,1)S(1)}, u32[]{:S(2)}, u32[]{:S(2)}) collective-permute-start(bf16[16,3712]{1,0:T(8,128)(2,1)S(1)} %get-tuple-element.51), channel_id=1, source_target_pairs={{0,18},{1,19},{2,16},{3,17},{4,22},{5,23},{6,20},{7,21},{8,26},{9,... | collective-permute-start | bytes 356360 | tf_op jit(solution)/shard_map/ppermute | solution.py:309
  36.3 5.7 %collective-permute-start.14 = (bf16[16,3712]{1,0:T(8,128)(2,1)S(1)}, bf16[16,3712]{1,0:T(8,128)(2,1)S(1)}, u32[]{:S(2)}, u32[]{:S(2)}) collective-permute-start(bf16[16,3712]{1,0:T(8,128)(2,1)S(1)} %get-tuple-element.52), channel_id=1, source_target_pairs={{0,4},{1,5},{2,6},{3,7},{4,12},{5,13},{6,14},{7,15},{8,0},{9,1},{1... | collective-permute-start | bytes 356360 | tf_op jit(solution)/shard_map/ppermute | solution.py:309
  42.5 11.9 %collective-permute-start.17 = (bf16[32,3584]{1,0:T(8,128)(2,1)S(1)}, bf16[32,3584]{1,0:T(8,128)(2,1)S(1)}, u32[]{:S(2)}, u32[]{:S(2)}) collective-permute-start(bf16[32,3584]{1,0:T(8,128)(2,1)S(1)} %combine.2), channel_id=1, source_target_pairs={{0,20},{1,21},{2,22},{3,23},{4,28},{5,29},{6,30},{7,31},{8,16},{9,... | collective-permute-start | bytes 688136 | tf_op jit(solution)/shard_map/ppermute | solution.py:309
  44.2 7.9 %collective-permute-start.15 = (bf16[16,3712]{1,0:T(8,128)(2,1)S(1)}, bf16[16,3712]{1,0:T(8,128)(2,1)S(1)}, u32[]{:S(2)}, u32[]{:S(2)}) collective-permute-start(bf16[16,3712]{1,0:T(8,128)(2,1)S(1)} %get-tuple-element.55), channel_id=1, source_target_pairs={{0,24},{1,25},{2,26},{3,27},{4,16},{5,17},{6,18},{7,19},{8,28},{9,... | collective-permute-start | bytes 356360 | tf_op jit(solution)/shard_map/ppermute | solution.py:309
  46.3 8.1 %collective-permute-start.16 = (bf16[16,3712]{1,0:T(8,128)(2,1)S(1)}, bf16[16,3712]{1,0:T(8,128)(2,1)S(1)}, u32[]{:S(2)}, u32[]{:S(2)}) collective-permute-start(bf16[16,3712]{1,0:T(8,128)(2,1)S(1)} %get-tuple-element.56), channel_id=1, source_target_pairs={{0,26},{1,27},{2,24},{3,25},{4,18},{5,19},{6,16},{7,17},{8,30},{9,... | collective-permute-start | bytes 356360 | tf_op jit(solution)/shard_map/ppermute | solution.py:309

commit v29 on v27

--- a/solution.py
+++ b/solution.py
@@ -330,7 +330,8 @@
     marks1 = sent(marks, sections, 0, 1, 0)
     own0, other, back0, back1 = choose(tokens, marks, capacity, ((0, 0), (0, 1), (3, 0), (3, 1)))
     other0 = sent(other, sections, 0, 0, 1)
-    block1 = after(block1, other0)
+    near_out = loaded(after(w_out, own0))
+    block1 = after(block1, (near_out, other0))
     own1, other, on0, on1 = choose(block1, marks1, capacity, ((0, 0), (0, 1), (1, 0), (1, 1)))
     other1 = sent(other, sections, 0, 0, 1)
     own2 = sent(on0, sections, 0, 1, 0)
@@ -338,7 +339,7 @@
     other3 = sent(after(back1, other0), sections, 0, 3, 1)
     back0 = after(back0, (other1, other3))
     own3 = sent(back0, sections, 0, 3, 0)
-    near = (loaded(after(w_in, back0)), loaded(after(w_out, back0)))
+    near = (loaded(after(w_in, back0)), near_out)
     pieces = (own0, other0, own1, own2, other2, other1, own3, other3)
     places = ((0, 0), (0, 1), (1, 0), (2, 0), (2, 1), (1, 1), (3, 0), (3, 1))
     slots, total = near_pass(pieces, near)

time: 54.9 us -> 54.8 us (level)
  local copies, waits for them, and re-layouts: 5.55 us -> 2.98 us
  waiting for transfers between devices: 16.1 us -> 18 us
    unnamed x6, local copies, waits for them, and re-layouts: 5.55 us -> 2.98 us
    ppermute x16, waiting for transfers between devices: 16.1 us -> 18 us  [sent(): return lax.ppermute(shard, ('section', 'expert'), pairs)]
    ppermute x16, starting transfers between devices: 24.9 us -> 25.4 us  [sent(): return lax.ppermute(shard, ('section', 'expert'), pairs)]
  transfers between devices with their start and end apart: 18 -> 18, of which waited for: 10 -> 8; matrix products, arithmetic and copies ran while one was open for 0% -> 0% of each run, Pallas kernels for 8% -> 8%
where the time goes in v29:
time: 54.8 us; the launch traced here: 54.6 us
  starting transfers between devices  25.9 us (47%)
  waiting for transfers between devices  18 us (33%)
  Pallas kernels  7.57 us (14%)
  local copies, waits for them, and re-layouts  2.98 us (5%)
    ppermute x16, starting transfers between devices, sent(): return lax.ppermute(shard, ('section', 'expert'), pairs)  25.4 us
    ppermute x16, waiting for transfers between devices, sent(): return lax.ppermute(shard, ('section', 'expert'), pairs)  18 us
    pallas_call x9, Pallas kernels, local_call(): pl.pallas_call(kernel, out_shape=out_shape, in_specs=[vmem if spec is Non...  7.57 us
    unnamed x6, local copies, waits for them, and re-layouts  2.98 us
  transfers between devices with their start and end apart: 18, of which 8 were waited for; matrix products, arithmetic and copies ran while one was open for 0% of the time, Pallas kernels for 8%

profile of v29, /device:TPU:0, one launch (start us, length us, event | category | flops | bytes accessed | tf_op | source)
XLA Modules:
  0.0 54.6 jit_solution(5956877128496216546)
XLA Ops:
  0.5 3.0 %collective-permute-start.1 = (bf16[32,3584]{1,0:T(8,128)(2,1)}, bf16[32,3584]{1,0:T(8,128)(2,1)S(1)}, u32[]{:S(2)}, u32[]{:S(2)}) collective-permute-start(bf16[32,3584]{1,0:T(8,128)(2,1)} %bitcast.14), channel_id=1, source_target_pairs={{0,4},{1,5},{2,6},{3,7},{4,12},{5,13},{6,14},{7,15},{8,0},{9,1},{1... | collective-permute-start | bytes 688136 | tf_op jit(solution)/shard_map/ppermute | solution.py:309
  3.5 1.0 %prepare.1.marks = bf16[32,128]{1,0:T(8,128)(2,1)S(1)} custom-call(s32[2,32]{1,0:T(2,128)} %bitcast.16, f32[2,32]{1,0:T(2,128)} %bitcast.17), custom_call_target="tpu_custom_call" | custom-call | tf_op jit(solution)/shard_map/prepare/pallas_call | solution.py:84
  5.9 1.6 %collective-permute-start = (bf16[16,3712]{1,0:T(8,128)(2,1)S(1)}, bf16[16,3712]{1,0:T(8,128)(2,1)S(1)}, u32[]{:S(2)}, u32[]{:S(2)}) collective-permute-start(bf16[16,3712]{1,0:T(8,128)(2,1)S(1)} %get-tuple-element.34), channel_id=1, source_target_pairs={{0,2},{1,3},{2,0},{3,1},{4,6},{5,7},{6,4},{7,5},{8,10},{9,11},{10,... | collective-permute-start | bytes 356360 | tf_op jit(solution)/shard_map/ppermute | solution.py:309
  7.5 2.6 %collective-permute-start.2 = (bf16[32,128]{1,0:T(8,128)(2,1)S(1)}, bf16[32,128]{1,0:T(8,128)(2,1)S(1)}, u32[]{:S(2)}, u32[]{:S(2)}) collective-permute-start(bf16[32,128]{1,0:T(8,128)(2,1)S(1)} %prepare.1.marks), channel_id=1, source_target_pairs={{0,4},{1,5},{2,6},{3,7},{4,12},{5,13},{6,14},{7,15},{8,0},{9,1},{1... | collective-permute-start | bytes 24584 | tf_op jit(solution)/shard_map/ppermute | solution.py:309
  10.1 2.0 %copy-done.1 = bf16[1,512,3584]{2,1,0:T(8,128)(2,1)S(1)} copy-done((bf16[1,512,3584]{2,1,0:T(8,128)(2,1)S(1)}, bf16[1,512,3584]{2,1,0:T(8,128)(2,1)}, u32[]{:S(2)}) %copy-start.1) | copy-done | bytes 3670040
  13.6 1.2 %collective-permute-start.5 = (bf16[16,3712]{1,0:T(8,128)(2,1)S(1)}, bf16[16,3712]{1,0:T(8,128)(2,1)S(1)}, u32[]{:S(2)}, u32[]{:S(2)}) collective-permute-start(bf16[16,3712]{1,0:T(8,128)(2,1)S(1)} %get-tuple-element.40), channel_id=1, source_target_pairs={{0,2},{1,3},{2,0},{3,1},{4,6},{5,7},{6,4},{7,5},{8,10},{9,11},{10,... | collective-permute-start | bytes 356360 | tf_op jit(solution)/shard_map/ppermute | solution.py:309
  14.7 1.7 %collective-permute-start.3 = (bf16[16,3712]{1,0:T(8,128)(2,1)S(1)}, bf16[16,3712]{1,0:T(8,128)(2,1)S(1)}, u32[]{:S(2)}, u32[]{:S(2)}) collective-permute-start(bf16[16,3712]{1,0:T(8,128)(2,1)S(1)} %get-tuple-element.38), channel_id=1, source_target_pairs={{0,4},{1,5},{2,6},{3,7},{4,12},{5,13},{6,14},{7,15},{8,0},{9,1},{1... | collective-permute-start | bytes 356360 | tf_op jit(solution)/shard_map/ppermute | solution.py:309
  16.4 3.1 %collective-permute-done.6.refs_7_ = bf16[16,3712]{1,0:T(8,128)(2,1)S(1)} collective-permute-done((bf16[16,3712]{1,0:T(8,128)(2,1)S(1)}, bf16[16,3712]{1,0:T(8,128)(2,1)S(1)}, u32[]{:S(2)}, u32[]{:S(2)}) %collective-permute-start.6) | collective-permute-done | bytes 118816 | tf_op jit(solution)/shard_map/ppermute | solution.py:309
  19.5 1.8 %collective-permute-start.4 = (bf16[16,3712]{1,0:T(8,128)(2,1)S(1)}, bf16[16,3712]{1,0:T(8,128)(2,1)S(1)}, u32[]{:S(2)}, u32[]{:S(2)}) collective-permute-start(bf16[16,3712]{1,0:T(8,128)(2,1)S(1)} %get-tuple-element.39), channel_id=1, source_target_pairs={{0,6},{1,7},{2,4},{3,5},{4,14},{5,15},{6,12},{7,13},{8,2},{9,3},{1... | collective-permute-start | bytes 356360 | tf_op jit(solution)/shard_map/ppermute | solution.py:309
  21.3 1.2 %collective-permute-start.7 = (bf16[16,3712]{1,0:T(8,128)(2,1)S(1)}, bf16[16,3712]{1,0:T(8,128)(2,1)S(1)}, u32[]{:S(2)}, u32[]{:S(2)}) collective-permute-start(bf16[16,3712]{1,0:T(8,128)(2,1)S(1)} %get-tuple-element.44), channel_id=1, source_target_pairs={{0,8},{1,9},{2,10},{3,11},{4,0},{5,1},{6,2},{7,3},{8,12},{9,13},{1... | collective-permute-start | bytes 356360 | tf_op jit(solution)/shard_map/ppermute | solution.py:309
  23.0 4.3 %collective-permute-done.4.refs_4_ = bf16[16,3712]{1,0:T(8,128)(2,1)S(1)} collective-permute-done((bf16[16,3712]{1,0:T(8,128)(2,1)S(1)}, bf16[16,3712]{1,0:T(8,128)(2,1)S(1)}, u32[]{:S(2)}, u32[]{:S(2)}) %collective-permute-start.4) | collective-permute-done | bytes 118816 | tf_op jit(solution)/shard_map/ppermute | solution.py:309
  27.3 1.7 %near_pass.1 = (bf16[128,3712]{1,0:T(8,128)(2,1)S(1)}, f32[128,3584]{1,0:T(8,128)S(1)}) custom-call(bf16[16,3712]{1,0:T(8,128)(2,1)S(1)} %get-tuple-element.33.refs_0_, bf16[16,3712]{1,0:T(8,128)(2,1)S(1)} %collective-permute-done.refs_1_, bf16[16,3712]{1,0:T(8,128)(2,1)S(1)} %get-tuple-element.37.refs_2_, ...), custom_call_target="tpu_custom_call" | custom-call | bytes 11010048 | tf_op jit(solution)/shard_map/near_pass/pallas_call | solution.py:84
  29.0 1.7 %far_pass.1 = (bf16[16,3712]{1,0:T(8,128)(2,1)S(1)}, bf16[16,3712]{1,0:T(8,128)(2,1)S(1)}, bf16[16,3712]{1,0:T(8,128)(2,1)S(1)}, bf16[16,3712]{1,0:T(8,128)(2,1)...) custom-call(bf16[128,3712]{1,0:T(8,128)(2,1)S(1)} %get-tuple-element, ...), custom_call_target="tpu_custom_call" | custom-call | bytes 11010048 | tf_op jit(solution)/shard_map/far_pass/pallas_call | solution.py:84
  30.8 2.2 %collective-permute-start.10 = (bf16[16,3712]{1,0:T(8,128)(2,1)S(1)}, bf16[16,3712]{1,0:T(8,128)(2,1)S(1)}, u32[]{:S(2)}, u32[]{:S(2)}) collective-permute-start(bf16[16,3712]{1,0:T(8,128)(2,1)S(1)} %get-tuple-element.48), channel_id=1, source_target_pairs={{0,6},{1,7},{2,4},{3,5},{4,14},{5,15},{6,12},{7,13},{8,2},{9,3},{1... | collective-permute-start | bytes 356360 | tf_op jit(solution)/shard_map/ppermute | solution.py:309
  33.5 1.5 %collective-permute-start.12 = (bf16[16,3712]{1,0:T(8,128)(2,1)S(1)}, bf16[16,3712]{1,0:T(8,128)(2,1)S(1)}, u32[]{:S(2)}, u32[]{:S(2)}) collective-permute-start(bf16[16,3712]{1,0:T(8,128)(2,1)S(1)} %get-tuple-element.50), channel_id=1, source_target_pairs={{0,16},{1,17},{2,18},{3,19},{4,20},{5,21},{6,22},{7,23},{8,24},{9,... | collective-permute-start | bytes 356360 | tf_op jit(solution)/shard_map/ppermute | solution.py:309
  35.0 1.5 %collective-permute-start.13 = (bf16[16,3712]{1,0:T(8,128)(2,1)S(1)}, bf16[16,3712]{1,0:T(8,128)(2,1)S(1)}, u32[]{:S(2)}, u32[]{:S(2)}) collective-permute-start(bf16[16,3712]{1,0:T(8,128)(2,1)S(1)} %get-tuple-element.51), channel_id=1, source_target_pairs={{0,18},{1,19},{2,16},{3,17},{4,22},{5,23},{6,20},{7,21},{8,26},{9,... | collective-permute-start | bytes 356360 | tf_op jit(solution)/shard_map/ppermute | solution.py:309
  36.5 2.0 %collective-permute-done.10.refs_1_ = bf16[16,3712]{1,0:T(8,128)(2,1)S(1)} collective-permute-done((bf16[16,3712]{1,0:T(8,128)(2,1)S(1)}, bf16[16,3712]{1,0:T(8,128)(2,1)S(1)}, u32[]{:S(2)}, u32[]{:S(2)}) %collective-permute-start.10) | collective-permute-done | bytes 118816 | tf_op jit(solution)/shard_map/ppermute | solution.py:309
  39.4 1.3 %collective-permute-done.13.refs_1_ = bf16[16,3712]{1,0:T(8,128)(2,1)S(1)} collective-permute-done((bf16[16,3712]{1,0:T(8,128)(2,1)S(1)}, bf16[16,3712]{1,0:T(8,128)(2,1)S(1)}, u32[]{:S(2)}, u32[]{:S(2)}) %collective-permute-start.13) | collective-permute-done | bytes 118816 | tf_op jit(solution)/shard_map/ppermute | solution.py:309
  40.7 1.5 %collective-permute-done.14.refs_3_ = bf16[16,3712]{1,0:T(8,128)(2,1)S(1)} collective-permute-done((bf16[16,3712]{1,0:T(8,128)(2,1)S(1)}, bf16[16,3712]{1,0:T(8,128)(2,1)S(1)}, u32[]{:S(2)}, u32[]{:S(2)}) %collective-permute-start.14) | collective-permute-done | bytes 118816 | tf_op jit(solution)/shard_map/ppermute | solution.py:309
  42.7 3.8 %collective-permute-start.15 = (bf16[16,3712]{1,0:T(8,128)(2,1)S(1)}, bf16[16,3712]{1,0:T(8,128)(2,1)S(1)}, u32[]{:S(2)}, u32[]{:S(2)}) collective-permute-start(bf16[16,3712]{1,0:T(8,128)(2,1)S(1)} %get-tuple-element.55), channel_id=1, source_target_pairs={{0,24},{1,25},{2,26},{3,27},{4,16},{5,17},{6,18},{7,19},{8,28},{9,... | collective-permute-start | bytes 356360 | tf_op jit(solution)/shard_map/ppermute | solution.py:309
  46.5 2.1 %collective-permute-start.16 = (bf16[16,3712]{1,0:T(8,128)(2,1)S(1)}, bf16[16,3712]{1,0:T(8,128)(2,1)S(1)}, u32[]{:S(2)}, u32[]{:S(2)}) collective-permute-start(bf16[16,3712]{1,0:T(8,128)(2,1)S(1)} %get-tuple-element.56), channel_id=1, source_target_pairs={{0,26},{1,27},{2,24},{3,25},{4,18},{5,19},{6,16},{7,17},{8,30},{9,... | collective-permute-start | bytes 356360 | tf_op jit(solution)/shard_map/ppermute | solution.py:309
  48.6 3.3 %collective-permute-done.15.refs_2_ = bf16[16,3712]{1,0:T(8,128)(2,1)S(1)} collective-permute-done((bf16[16,3712]{1,0:T(8,128)(2,1)S(1)}, bf16[16,3712]{1,0:T(8,128)(2,1)S(1)}, u32[]{:S(2)}, u32[]{:S(2)}) %collective-permute-start.15) | collective-permute-done | bytes 118816 | tf_op jit(solution)/shard_map/ppermute | solution.py:309
  51.9 1.6 %collective-permute-done.16.refs_3_ = bf16[16,3712]{1,0:T(8,128)(2,1)S(1)} collective-permute-done((bf16[16,3712]{1,0:T(8,128)(2,1)S(1)}, bf16[16,3712]{1,0:T(8,128)(2,1)S(1)}, u32[]{:S(2)}, u32[]{:S(2)}) %collective-permute-start.16) | collective-permute-done | bytes 118816 | tf_op jit(solution)/shard_map/ppermute | solution.py:309
  53.5 1.1 %combine.3 = bf16[32,3584]{1,0:T(8,128)(2,1)} custom-call(bf16[16,3712]{1,0:T(8,128)(2,1)S(1)} %collective-permute-done.12.refs_0_, bf16[16,3712]{1,0:T(8,128)(2,1)S(1)} %collective-permute-done.13.refs_1_, bf16[16,3712]{1,0:T(8,128)(2,1)S(1)} %collective-permute-done.15.refs_2_, bf16[16,3712]{1,0:T(8,128)(2,1)S(1)} %collective-permute-done.16.refs_3_, ...), custom_call_target="tpu_custom_call" | custom-call | tf_op jit(solution)/shard_map/combine/pallas_call | solution.py:84
  (27 shorter events, 5.8 us)
Async XLA Ops:
  0.0 29.0 %collective-permute-start.8 = (bf16[3584,1024]{1,0:T(8,128)(2,1)}, bf16[3584,1024]{1,0:T(8,128)(2,1)S(1)}, u32[]{:S(2)}, u32[]{:S(2)}) collective-permute-start(bf16[3584,1024]{1,0:T(8,128)(2,1)} %bitcast.10), channel_id=1, source_target_pairs={{0,1},{1,0},{2,3},{3,2},{4,5},{5,4},{6,7},{7,6},{8,9},{9,8},{10,11... | collective-permute-start | bytes 22020104 | tf_op jit(solution)/shard_map/ppermute | solution.py:327
  0.5 28.6 %collective-permute-start.9 = (bf16[512,3584]{1,0:T(8,128)(2,1)}, bf16[512,3584]{1,0:T(8,128)(2,1)S(1)}, u32[]{:S(2)}, u32[]{:S(2)}) collective-permute-start(bf16[512,3584]{1,0:T(8,128)(2,1)} %bitcast.12), channel_id=1, source_target_pairs={{0,1},{1,0},{2,3},{3,2},{4,5},{5,4},{6,7},{7,6},{8,9},{9,8},{10,11... | collective-permute-start | bytes 11010056 | tf_op jit(solution)/shard_map/ppermute | solution.py:326
  0.5 12.6 %collective-permute-start.1 = (bf16[32,3584]{1,0:T(8,128)(2,1)}, bf16[32,3584]{1,0:T(8,128)(2,1)S(1)}, u32[]{:S(2)}, u32[]{:S(2)}) collective-permute-start(bf16[32,3584]{1,0:T(8,128)(2,1)} %bitcast.14), channel_id=1, source_target_pairs={{0,4},{1,5},{2,6},{3,7},{4,12},{5,13},{6,14},{7,15},{8,0},{9,1},{1... | collective-permute-start | bytes 688136 | tf_op jit(solution)/shard_map/ppermute | solution.py:309
  4.5 0.9 %copy-start.2 = (bf16[1,32,3584]{2,1,0:T(8,128)(2,1)S(1)}, bf16[1,32,3584]{2,1,0:T(8,128)(2,1)}, u32[]{:S(2)}) copy-start(bf16[1,32,3584]{2,1,0:T(8,128)(2,1)} %param.5) | copy-start | bytes 688132
  5.9 6.5 %collective-permute-start = (bf16[16,3712]{1,0:T(8,128)(2,1)S(1)}, bf16[16,3712]{1,0:T(8,128)(2,1)S(1)}, u32[]{:S(2)}, u32[]{:S(2)}) collective-permute-start(bf16[16,3712]{1,0:T(8,128)(2,1)S(1)} %get-tuple-element.34), channel_id=1, source_target_pairs={{0,2},{1,3},{2,0},{3,1},{4,6},{5,7},{6,4},{7,5},{8,10},{9,11},{10,... | collective-permute-start | bytes 356360 | tf_op jit(solution)/shard_map/ppermute | solution.py:309
  7.5 5.7 %collective-permute-start.2 = (bf16[32,128]{1,0:T(8,128)(2,1)S(1)}, bf16[32,128]{1,0:T(8,128)(2,1)S(1)}, u32[]{:S(2)}, u32[]{:S(2)}) collective-permute-start(bf16[32,128]{1,0:T(8,128)(2,1)S(1)} %prepare.1.marks), channel_id=1, source_target_pairs={{0,4},{1,5},{2,6},{3,7},{4,12},{5,13},{6,14},{7,15},{8,0},{9,1},{1... | collective-permute-start | bytes 24584 | tf_op jit(solution)/shard_map/ppermute | solution.py:309
  10.1 2.0 %copy-start.1 = (bf16[1,512,3584]{2,1,0:T(8,128)(2,1)S(1)}, bf16[1,512,3584]{2,1,0:T(8,128)(2,1)}, u32[]{:S(2)}) copy-start(bf16[1,512,3584]{2,1,0:T(8,128)(2,1)} %param.9) | copy-start | bytes 11010052
  12.1 10.3 %copy-start = (bf16[1,3584,1024]{2,1,0:T(8,128)(2,1)S(1)}, bf16[1,3584,1024]{2,1,0:T(8,128)(2,1)}, u32[]{:S(2)}) copy-start(bf16[1,3584,1024]{2,1,0:T(8,128)(2,1)} %param.8) | copy-start | bytes 22020100
  12.4 7.1 %collective-permute-start.6 = (bf16[16,3712]{1,0:T(8,128)(2,1)S(1)}, bf16[16,3712]{1,0:T(8,128)(2,1)S(1)}, u32[]{:S(2)}, u32[]{:S(2)}) collective-permute-start(bf16[16,3712]{1,0:T(8,128)(2,1)S(1)} %get-tuple-element.43), channel_id=1, source_target_pairs={{0,10},{1,11},{2,8},{3,9},{4,2},{5,3},{6,0},{7,1},{8,14},{9,15},{1... | collective-permute-start | bytes 356360 | tf_op jit(solution)/shard_map/ppermute | solution.py:309
  13.6 7.7 %collective-permute-start.5 = (bf16[16,3712]{1,0:T(8,128)(2,1)S(1)}, bf16[16,3712]{1,0:T(8,128)(2,1)S(1)}, u32[]{:S(2)}, u32[]{:S(2)}) collective-permute-start(bf16[16,3712]{1,0:T(8,128)(2,1)S(1)} %get-tuple-element.40), channel_id=1, source_target_pairs={{0,2},{1,3},{2,0},{3,1},{4,6},{5,7},{6,4},{7,5},{8,10},{9,11},{10,... | collective-permute-start | bytes 356360 | tf_op jit(solution)/shard_map/ppermute | solution.py:309
  14.7 8.2 %collective-permute-start.3 = (bf16[16,3712]{1,0:T(8,128)(2,1)S(1)}, bf16[16,3712]{1,0:T(8,128)(2,1)S(1)}, u32[]{:S(2)}, u32[]{:S(2)}) collective-permute-start(bf16[16,3712]{1,0:T(8,128)(2,1)S(1)} %get-tuple-element.38), channel_id=1, source_target_pairs={{0,4},{1,5},{2,6},{3,7},{4,12},{5,13},{6,14},{7,15},{8,0},{9,1},{1... | collective-permute-start | bytes 356360 | tf_op jit(solution)/shard_map/ppermute | solution.py:309
  19.5 7.8 %collective-permute-start.4 = (bf16[16,3712]{1,0:T(8,128)(2,1)S(1)}, bf16[16,3712]{1,0:T(8,128)(2,1)S(1)}, u32[]{:S(2)}, u32[]{:S(2)}) collective-permute-start(bf16[16,3712]{1,0:T(8,128)(2,1)S(1)} %get-tuple-element.39), channel_id=1, source_target_pairs={{0,6},{1,7},{2,4},{3,5},{4,14},{5,15},{6,12},{7,13},{8,2},{9,3},{1... | collective-permute-start | bytes 356360 | tf_op jit(solution)/shard_map/ppermute | solution.py:309
  21.3 6.0 %collective-permute-start.7 = (bf16[16,3712]{1,0:T(8,128)(2,1)S(1)}, bf16[16,3712]{1,0:T(8,128)(2,1)S(1)}, u32[]{:S(2)}, u32[]{:S(2)}) collective-permute-start(bf16[16,3712]{1,0:T(8,128)(2,1)S(1)} %get-tuple-element.44), channel_id=1, source_target_pairs={{0,8},{1,9},{2,10},{3,11},{4,0},{5,1},{6,2},{7,3},{8,12},{9,13},{1... | collective-permute-start | bytes 356360 | tf_op jit(solution)/shard_map/ppermute | solution.py:309
  30.8 7.7 %collective-permute-start.10 = (bf16[16,3712]{1,0:T(8,128)(2,1)S(1)}, bf16[16,3712]{1,0:T(8,128)(2,1)S(1)}, u32[]{:S(2)}, u32[]{:S(2)}) collective-permute-start(bf16[16,3712]{1,0:T(8,128)(2,1)S(1)} %get-tuple-element.48), channel_id=1, source_target_pairs={{0,6},{1,7},{2,4},{3,5},{4,14},{5,15},{6,12},{7,13},{8,2},{9,3},{1... | collective-permute-start | bytes 356360 | tf_op jit(solution)/shard_map/ppermute | solution.py:309
  33.0 6.5 %collective-permute-start.11 = (bf16[16,3712]{1,0:T(8,128)(2,1)S(1)}, bf16[16,3712]{1,0:T(8,128)(2,1)S(1)}, u32[]{:S(2)}, u32[]{:S(2)}) collective-permute-start(bf16[16,3712]{1,0:T(8,128)(2,1)S(1)} %get-tuple-element.49), channel_id=1, source_target_pairs={{0,2},{1,3},{2,0},{3,1},{4,6},{5,7},{6,4},{7,5},{8,10},{9,11},{10,... | collective-permute-start | bytes 356360 | tf_op jit(solution)/shard_map/ppermute | solution.py:309
  33.5 6.0 %collective-permute-start.12 = (bf16[16,3712]{1,0:T(8,128)(2,1)S(1)}, bf16[16,3712]{1,0:T(8,128)(2,1)S(1)}, u32[]{:S(2)}, u32[]{:S(2)}) collective-permute-start(bf16[16,3712]{1,0:T(8,128)(2,1)S(1)} %get-tuple-element.50), channel_id=1, source_target_pairs={{0,16},{1,17},{2,18},{3,19},{4,20},{5,21},{6,22},{7,23},{8,24},{9,... | collective-permute-start | bytes 356360 | tf_op jit(solution)/shard_map/ppermute | solution.py:309
  35.0 5.7 %collective-permute-start.13 = (bf16[16,3712]{1,0:T(8,128)(2,1)S(1)}, bf16[16,3712]{1,0:T(8,128)(2,1)S(1)}, u32[]{:S(2)}, u32[]{:S(2)}) collective-permute-start(bf16[16,3712]{1,0:T(8,128)(2,1)S(1)} %get-tuple-element.51), channel_id=1, source_target_pairs={{0,18},{1,19},{2,16},{3,17},{4,22},{5,23},{6,20},{7,21},{8,26},{9,... | collective-permute-start | bytes 356360 | tf_op jit(solution)/shard_map/ppermute | solution.py:309
  36.5 5.7 %collective-permute-start.14 = (bf16[16,3712]{1,0:T(8,128)(2,1)S(1)}, bf16[16,3712]{1,0:T(8,128)(2,1)S(1)}, u32[]{:S(2)}, u32[]{:S(2)}) collective-permute-start(bf16[16,3712]{1,0:T(8,128)(2,1)S(1)} %get-tuple-element.52), channel_id=1, source_target_pairs={{0,4},{1,5},{2,6},{3,7},{4,12},{5,13},{6,14},{7,15},{8,0},{9,1},{1... | collective-permute-start | bytes 356360 | tf_op jit(solution)/shard_map/ppermute | solution.py:309
  42.6 10.9 %collective-permute-start.17 = (bf16[32,3584]{1,0:T(8,128)(2,1)S(1)}, bf16[32,3584]{1,0:T(8,128)(2,1)S(1)}, u32[]{:S(2)}, u32[]{:S(2)}) collective-permute-start(bf16[32,3584]{1,0:T(8,128)(2,1)S(1)} %combine.2), channel_id=1, source_target_pairs={{0,20},{1,21},{2,22},{3,23},{4,28},{5,29},{6,30},{7,31},{8,16},{9,... | collective-permute-start | bytes 688136 | tf_op jit(solution)/shard_map/ppermute | solution.py:309
  42.7 9.1 %collective-permute-start.15 = (bf16[16,3712]{1,0:T(8,128)(2,1)S(1)}, bf16[16,3712]{1,0:T(8,128)(2,1)S(1)}, u32[]{:S(2)}, u32[]{:S(2)}) collective-permute-start(bf16[16,3712]{1,0:T(8,128)(2,1)S(1)} %get-tuple-element.55), channel_id=1, source_target_pairs={{0,24},{1,25},{2,26},{3,27},{4,16},{5,17},{6,18},{7,19},{8,28},{9,... | collective-permute-start | bytes 356360 | tf_op jit(solution)/shard_map/ppermute | solution.py:309
  46.5 7.0 %collective-permute-start.16 = (bf16[16,3712]{1,0:T(8,128)(2,1)S(1)}, bf16[16,3712]{1,0:T(8,128)(2,1)S(1)}, u32[]{:S(2)}, u32[]{:S(2)}) collective-permute-start(bf16[16,3712]{1,0:T(8,128)(2,1)S(1)} %get-tuple-element.56), channel_id=1, source_target_pairs={{0,26},{1,27},{2,24},{3,25},{4,18},{5,19},{6,16},{7,17},{8,30},{9,... | collective-permute-start | bytes 356360 | tf_op jit(solution)/shard_map/ppermute | solution.py:309

commit v30 on v29

--- a/solution.py
+++ b/solution.py
@@ -284,16 +284,25 @@
         out[:, place] = mixed.astype(out.dtype)
 
 
-def combine(blocks, tok_count, *more):
+def combine(blocks, tok_count, dtype=jnp.bfloat16):
     capacity, full = blocks[0].shape
     return local_call(
         functools.partial(combine_kernel, len(blocks)),
         "combine",
-        jax.ShapeDtypeStruct((tok_count, full - LANES), jnp.bfloat16),
-        [None] * (len(blocks) + len(more)),
-        (*blocks, *more),
+        jax.ShapeDtypeStruct((tok_count, full - LANES), dtype),
+        [None] * len(blocks),
+        tuple(blocks),
         [pltpu.VMEM((capacity * len(blocks), full), jnp.bfloat16)],
     )
+
+
+def add_kernel(left, right, out):
+    out[...] = (left[...] + right[...].astype(jnp.float32)).astype(out.dtype)
+
+
+def added(left, right):
+    out_shape = jax.ShapeDtypeStruct(right.shape, right.dtype)
+    return local_call(add_kernel, "added", out_shape, [None] * 2, (left, right))
 
 
 def sent(shard, sections, section_step, ring_step, flip):
@@ -356,7 +365,7 @@
     merged = [piece[3, 0], two, three, four]
     straight += [sent(piece[1, flip], sections, 1, -1, flip) for flip in range(2)]
     merged = sent(combine(merged, tok_count), sections, 1, 1, 0)
-    return combine(straight, tok_count, merged)[None]
+    return added(combine(straight, tok_count, jnp.float32), merged)[None]
 
 
 def per_device(rows, route_ids, route_weights, w_gate_up, w_down):

time: 54.8 us -> 54.8 us (level)
    pallas_call x9 -> x10, Pallas kernels: 7.57 us -> 7.61 us  [local_call(): pl.pallas_call(kernel, out_shape=out_shape, in_specs=[vmem if spec is Non...]
  transfers between devices with their start and end apart: 18 -> 18, of which waited for: 8 -> 8; matrix products, arithmetic and copies ran while one was open for 0% -> 0% of each run, Pallas kernels for 8% -> 9%
where the time goes in v30:
time: 54.8 us; the launch traced here: 54.7 us
  starting transfers between devices  25.9 us (47%)
  waiting for transfers between devices  18 us (33%)
  Pallas kernels  7.61 us (14%)
  local copies, waits for them, and re-layouts  2.98 us (5%)
    ppermute x16, starting transfers between devices, sent(): return lax.ppermute(shard, ('section', 'expert'), pairs)  25.4 us
    ppermute x16, waiting for transfers between devices, sent(): return lax.ppermute(shard, ('section', 'expert'), pairs)  18 us
    pallas_call x10, Pallas kernels, local_call(): pl.pallas_call(kernel, out_shape=out_shape, in_specs=[vmem if spec is Non...  7.61 us
    unnamed x6, local copies, waits for them, and re-layouts  2.98 us
  transfers between devices with their start and end apart: 18, of which 8 were waited for; matrix products, arithmetic and copies ran while one was open for 0% of the time, Pallas kernels for 9%

profile of v30, /device:TPU:0, one launch (start us, length us, event | category | flops | bytes accessed | tf_op | source)
XLA Modules:
  0.0 54.7 jit_solution(12798950213723485946)
XLA Ops:
  0.5 3.0 %collective-permute-start.1 = (bf16[32,3584]{1,0:T(8,128)(2,1)}, bf16[32,3584]{1,0:T(8,128)(2,1)S(1)}, u32[]{:S(2)}, u32[]{:S(2)}) collective-permute-start(bf16[32,3584]{1,0:T(8,128)(2,1)} %bitcast.14), channel_id=1, source_target_pairs={{0,4},{1,5},{2,6},{3,7},{4,12},{5,13},{6,14},{7,15},{8,0},{9,1},{1... | collective-permute-start | bytes 688136 | tf_op jit(solution)/shard_map/ppermute | solution.py:318
  3.5 1.0 %prepare.1.marks = bf16[32,128]{1,0:T(8,128)(2,1)S(1)} custom-call(s32[2,32]{1,0:T(2,128)} %bitcast.16, f32[2,32]{1,0:T(2,128)} %bitcast.17), custom_call_target="tpu_custom_call" | custom-call | tf_op jit(solution)/shard_map/prepare/pallas_call | solution.py:84
  5.9 1.6 %collective-permute-start = (bf16[16,3712]{1,0:T(8,128)(2,1)S(1)}, bf16[16,3712]{1,0:T(8,128)(2,1)S(1)}, u32[]{:S(2)}, u32[]{:S(2)}) collective-permute-start(bf16[16,3712]{1,0:T(8,128)(2,1)S(1)} %get-tuple-element.34), channel_id=1, source_target_pairs={{0,2},{1,3},{2,0},{3,1},{4,6},{5,7},{6,4},{7,5},{8,10},{9,11},{10,... | collective-permute-start | bytes 356360 | tf_op jit(solution)/shard_map/ppermute | solution.py:318
  7.5 2.6 %collective-permute-start.2 = (bf16[32,128]{1,0:T(8,128)(2,1)S(1)}, bf16[32,128]{1,0:T(8,128)(2,1)S(1)}, u32[]{:S(2)}, u32[]{:S(2)}) collective-permute-start(bf16[32,128]{1,0:T(8,128)(2,1)S(1)} %prepare.1.marks), channel_id=1, source_target_pairs={{0,4},{1,5},{2,6},{3,7},{4,12},{5,13},{6,14},{7,15},{8,0},{9,1},{1... | collective-permute-start | bytes 24584 | tf_op jit(solution)/shard_map/ppermute | solution.py:318
  10.1 2.0 %copy-done.1 = bf16[1,512,3584]{2,1,0:T(8,128)(2,1)S(1)} copy-done((bf16[1,512,3584]{2,1,0:T(8,128)(2,1)S(1)}, bf16[1,512,3584]{2,1,0:T(8,128)(2,1)}, u32[]{:S(2)}) %copy-start.1) | copy-done | bytes 3670040
  13.6 1.2 %collective-permute-start.5 = (bf16[16,3712]{1,0:T(8,128)(2,1)S(1)}, bf16[16,3712]{1,0:T(8,128)(2,1)S(1)}, u32[]{:S(2)}, u32[]{:S(2)}) collective-permute-start(bf16[16,3712]{1,0:T(8,128)(2,1)S(1)} %get-tuple-element.40), channel_id=1, source_target_pairs={{0,2},{1,3},{2,0},{3,1},{4,6},{5,7},{6,4},{7,5},{8,10},{9,11},{10,... | collective-permute-start | bytes 356360 | tf_op jit(solution)/shard_map/ppermute | solution.py:318
  14.7 1.7 %collective-permute-start.3 = (bf16[16,3712]{1,0:T(8,128)(2,1)S(1)}, bf16[16,3712]{1,0:T(8,128)(2,1)S(1)}, u32[]{:S(2)}, u32[]{:S(2)}) collective-permute-start(bf16[16,3712]{1,0:T(8,128)(2,1)S(1)} %get-tuple-element.38), channel_id=1, source_target_pairs={{0,4},{1,5},{2,6},{3,7},{4,12},{5,13},{6,14},{7,15},{8,0},{9,1},{1... | collective-permute-start | bytes 356360 | tf_op jit(solution)/shard_map/ppermute | solution.py:318
  16.4 3.1 %collective-permute-done.6.refs_7_ = bf16[16,3712]{1,0:T(8,128)(2,1)S(1)} collective-permute-done((bf16[16,3712]{1,0:T(8,128)(2,1)S(1)}, bf16[16,3712]{1,0:T(8,128)(2,1)S(1)}, u32[]{:S(2)}, u32[]{:S(2)}) %collective-permute-start.6) | collective-permute-done | bytes 118816 | tf_op jit(solution)/shard_map/ppermute | solution.py:318
  19.5 1.8 %collective-permute-start.4 = (bf16[16,3712]{1,0:T(8,128)(2,1)S(1)}, bf16[16,3712]{1,0:T(8,128)(2,1)S(1)}, u32[]{:S(2)}, u32[]{:S(2)}) collective-permute-start(bf16[16,3712]{1,0:T(8,128)(2,1)S(1)} %get-tuple-element.39), channel_id=1, source_target_pairs={{0,6},{1,7},{2,4},{3,5},{4,14},{5,15},{6,12},{7,13},{8,2},{9,3},{1... | collective-permute-start | bytes 356360 | tf_op jit(solution)/shard_map/ppermute | solution.py:318
  21.3 1.2 %collective-permute-start.7 = (bf16[16,3712]{1,0:T(8,128)(2,1)S(1)}, bf16[16,3712]{1,0:T(8,128)(2,1)S(1)}, u32[]{:S(2)}, u32[]{:S(2)}) collective-permute-start(bf16[16,3712]{1,0:T(8,128)(2,1)S(1)} %get-tuple-element.44), channel_id=1, source_target_pairs={{0,8},{1,9},{2,10},{3,11},{4,0},{5,1},{6,2},{7,3},{8,12},{9,13},{1... | collective-permute-start | bytes 356360 | tf_op jit(solution)/shard_map/ppermute | solution.py:318
  23.0 4.3 %collective-permute-done.4.refs_4_ = bf16[16,3712]{1,0:T(8,128)(2,1)S(1)} collective-permute-done((bf16[16,3712]{1,0:T(8,128)(2,1)S(1)}, bf16[16,3712]{1,0:T(8,128)(2,1)S(1)}, u32[]{:S(2)}, u32[]{:S(2)}) %collective-permute-start.4) | collective-permute-done | bytes 118816 | tf_op jit(solution)/shard_map/ppermute | solution.py:318
  27.3 1.7 %near_pass.1 = (bf16[128,3712]{1,0:T(8,128)(2,1)S(1)}, f32[128,3584]{1,0:T(8,128)S(1)}) custom-call(bf16[16,3712]{1,0:T(8,128)(2,1)S(1)} %get-tuple-element.33.refs_0_, bf16[16,3712]{1,0:T(8,128)(2,1)S(1)} %collective-permute-done.refs_1_, bf16[16,3712]{1,0:T(8,128)(2,1)S(1)} %get-tuple-element.37.refs_2_, ...), custom_call_target="tpu_custom_call" | custom-call | bytes 11010048 | tf_op jit(solution)/shard_map/near_pass/pallas_call | solution.py:84
  29.0 1.7 %far_pass.1 = (bf16[16,3712]{1,0:T(8,128)(2,1)S(1)}, bf16[16,3712]{1,0:T(8,128)(2,1)S(1)}, bf16[16,3712]{1,0:T(8,128)(2,1)S(1)}, bf16[16,3712]{1,0:T(8,128)(2,1)...) custom-call(bf16[128,3712]{1,0:T(8,128)(2,1)S(1)} %get-tuple-element, ...), custom_call_target="tpu_custom_call" | custom-call | bytes 11010048 | tf_op jit(solution)/shard_map/far_pass/pallas_call | solution.py:84
  30.8 2.2 %collective-permute-start.10 = (bf16[16,3712]{1,0:T(8,128)(2,1)S(1)}, bf16[16,3712]{1,0:T(8,128)(2,1)S(1)}, u32[]{:S(2)}, u32[]{:S(2)}) collective-permute-start(bf16[16,3712]{1,0:T(8,128)(2,1)S(1)} %get-tuple-element.48), channel_id=1, source_target_pairs={{0,6},{1,7},{2,4},{3,5},{4,14},{5,15},{6,12},{7,13},{8,2},{9,3},{1... | collective-permute-start | bytes 356360 | tf_op jit(solution)/shard_map/ppermute | solution.py:318
  33.5 1.5 %collective-permute-start.12 = (bf16[16,3712]{1,0:T(8,128)(2,1)S(1)}, bf16[16,3712]{1,0:T(8,128)(2,1)S(1)}, u32[]{:S(2)}, u32[]{:S(2)}) collective-permute-start(bf16[16,3712]{1,0:T(8,128)(2,1)S(1)} %get-tuple-element.50), channel_id=1, source_target_pairs={{0,16},{1,17},{2,18},{3,19},{4,20},{5,21},{6,22},{7,23},{8,24},{9,... | collective-permute-start | bytes 356360 | tf_op jit(solution)/shard_map/ppermute | solution.py:318
  35.0 1.5 %collective-permute-start.13 = (bf16[16,3712]{1,0:T(8,128)(2,1)S(1)}, bf16[16,3712]{1,0:T(8,128)(2,1)S(1)}, u32[]{:S(2)}, u32[]{:S(2)}) collective-permute-start(bf16[16,3712]{1,0:T(8,128)(2,1)S(1)} %get-tuple-element.51), channel_id=1, source_target_pairs={{0,18},{1,19},{2,16},{3,17},{4,22},{5,23},{6,20},{7,21},{8,26},{9,... | collective-permute-start | bytes 356360 | tf_op jit(solution)/shard_map/ppermute | solution.py:318
  36.5 2.0 %collective-permute-done.10.refs_1_ = bf16[16,3712]{1,0:T(8,128)(2,1)S(1)} collective-permute-done((bf16[16,3712]{1,0:T(8,128)(2,1)S(1)}, bf16[16,3712]{1,0:T(8,128)(2,1)S(1)}, u32[]{:S(2)}, u32[]{:S(2)}) %collective-permute-start.10) | collective-permute-done | bytes 118816 | tf_op jit(solution)/shard_map/ppermute | solution.py:318
  38.5 1.0 %collective-permute-done.11.refs_2_ = bf16[16,3712]{1,0:T(8,128)(2,1)S(1)} collective-permute-done((bf16[16,3712]{1,0:T(8,128)(2,1)S(1)}, bf16[16,3712]{1,0:T(8,128)(2,1)S(1)}, u32[]{:S(2)}, u32[]{:S(2)}) %collective-permute-start.11) | collective-permute-done | bytes 118816 | tf_op jit(solution)/shard_map/ppermute | solution.py:318
  39.4 1.3 %collective-permute-done.13.refs_1_ = bf16[16,3712]{1,0:T(8,128)(2,1)S(1)} collective-permute-done((bf16[16,3712]{1,0:T(8,128)(2,1)S(1)}, bf16[16,3712]{1,0:T(8,128)(2,1)S(1)}, u32[]{:S(2)}, u32[]{:S(2)}) %collective-permute-start.13) | collective-permute-done | bytes 118816 | tf_op jit(solution)/shard_map/ppermute | solution.py:318
  40.7 1.5 %collective-permute-done.14.refs_3_ = bf16[16,3712]{1,0:T(8,128)(2,1)S(1)} collective-permute-done((bf16[16,3712]{1,0:T(8,128)(2,1)S(1)}, bf16[16,3712]{1,0:T(8,128)(2,1)S(1)}, u32[]{:S(2)}, u32[]{:S(2)}) %collective-permute-start.14) | collective-permute-done | bytes 118816 | tf_op jit(solution)/shard_map/ppermute | solution.py:318
  42.7 3.8 %collective-permute-start.15 = (bf16[16,3712]{1,0:T(8,128)(2,1)S(1)}, bf16[16,3712]{1,0:T(8,128)(2,1)S(1)}, u32[]{:S(2)}, u32[]{:S(2)}) collective-permute-start(bf16[16,3712]{1,0:T(8,128)(2,1)S(1)} %get-tuple-element.55), channel_id=1, source_target_pairs={{0,24},{1,25},{2,26},{3,27},{4,16},{5,17},{6,18},{7,19},{8,28},{9,... | collective-permute-start | bytes 356360 | tf_op jit(solution)/shard_map/ppermute | solution.py:318
  46.5 2.1 %collective-permute-start.16 = (bf16[16,3712]{1,0:T(8,128)(2,1)S(1)}, bf16[16,3712]{1,0:T(8,128)(2,1)S(1)}, u32[]{:S(2)}, u32[]{:S(2)}) collective-permute-start(bf16[16,3712]{1,0:T(8,128)(2,1)S(1)} %get-tuple-element.56), channel_id=1, source_target_pairs={{0,26},{1,27},{2,24},{3,25},{4,18},{5,19},{6,16},{7,17},{8,30},{9,... | collective-permute-start | bytes 356360 | tf_op jit(solution)/shard_map/ppermute | solution.py:318
  48.6 3.3 %collective-permute-done.15.refs_2_ = bf16[16,3712]{1,0:T(8,128)(2,1)S(1)} collective-permute-done((bf16[16,3712]{1,0:T(8,128)(2,1)S(1)}, bf16[16,3712]{1,0:T(8,128)(2,1)S(1)}, u32[]{:S(2)}, u32[]{:S(2)}) %collective-permute-start.15) | collective-permute-done | bytes 118816 | tf_op jit(solution)/shard_map/ppermute | solution.py:318
  51.9 1.6 %collective-permute-done.16.refs_3_ = bf16[16,3712]{1,0:T(8,128)(2,1)S(1)} collective-permute-done((bf16[16,3712]{1,0:T(8,128)(2,1)S(1)}, bf16[16,3712]{1,0:T(8,128)(2,1)S(1)}, u32[]{:S(2)}, u32[]{:S(2)}) %collective-permute-start.16) | collective-permute-done | bytes 118816 | tf_op jit(solution)/shard_map/ppermute | solution.py:318
  (28 shorter events, 6.0 us)
Async XLA Ops:
  0.0 29.0 %collective-permute-start.8 = (bf16[3584,1024]{1,0:T(8,128)(2,1)}, bf16[3584,1024]{1,0:T(8,128)(2,1)S(1)}, u32[]{:S(2)}, u32[]{:S(2)}) collective-permute-start(bf16[3584,1024]{1,0:T(8,128)(2,1)} %bitcast.10), channel_id=1, source_target_pairs={{0,1},{1,0},{2,3},{3,2},{4,5},{5,4},{6,7},{7,6},{8,9},{9,8},{10,11... | collective-permute-start | bytes 22020104 | tf_op jit(solution)/shard_map/ppermute | solution.py:336
  0.5 28.6 %collective-permute-start.9 = (bf16[512,3584]{1,0:T(8,128)(2,1)}, bf16[512,3584]{1,0:T(8,128)(2,1)S(1)}, u32[]{:S(2)}, u32[]{:S(2)}) collective-permute-start(bf16[512,3584]{1,0:T(8,128)(2,1)} %bitcast.12), channel_id=1, source_target_pairs={{0,1},{1,0},{2,3},{3,2},{4,5},{5,4},{6,7},{7,6},{8,9},{9,8},{10,11... | collective-permute-start | bytes 11010056 | tf_op jit(solution)/shard_map/ppermute | solution.py:335
  0.5 12.6 %collective-permute-start.1 = (bf16[32,3584]{1,0:T(8,128)(2,1)}, bf16[32,3584]{1,0:T(8,128)(2,1)S(1)}, u32[]{:S(2)}, u32[]{:S(2)}) collective-permute-start(bf16[32,3584]{1,0:T(8,128)(2,1)} %bitcast.14), channel_id=1, source_target_pairs={{0,4},{1,5},{2,6},{3,7},{4,12},{5,13},{6,14},{7,15},{8,0},{9,1},{1... | collective-permute-start | bytes 688136 | tf_op jit(solution)/shard_map/ppermute | solution.py:318
  4.5 0.9 %copy-start.2 = (bf16[1,32,3584]{2,1,0:T(8,128)(2,1)S(1)}, bf16[1,32,3584]{2,1,0:T(8,128)(2,1)}, u32[]{:S(2)}) copy-start(bf16[1,32,3584]{2,1,0:T(8,128)(2,1)} %param.5) | copy-start | bytes 688132
  5.9 6.5 %collective-permute-start = (bf16[16,3712]{1,0:T(8,128)(2,1)S(1)}, bf16[16,3712]{1,0:T(8,128)(2,1)S(1)}, u32[]{:S(2)}, u32[]{:S(2)}) collective-permute-start(bf16[16,3712]{1,0:T(8,128)(2,1)S(1)} %get-tuple-element.34), channel_id=1, source_target_pairs={{0,2},{1,3},{2,0},{3,1},{4,6},{5,7},{6,4},{7,5},{8,10},{9,11},{10,... | collective-permute-start | bytes 356360 | tf_op jit(solution)/shard_map/ppermute | solution.py:318
  7.5 5.7 %collective-permute-start.2 = (bf16[32,128]{1,0:T(8,128)(2,1)S(1)}, bf16[32,128]{1,0:T(8,128)(2,1)S(1)}, u32[]{:S(2)}, u32[]{:S(2)}) collective-permute-start(bf16[32,128]{1,0:T(8,128)(2,1)S(1)} %prepare.1.marks), channel_id=1, source_target_pairs={{0,4},{1,5},{2,6},{3,7},{4,12},{5,13},{6,14},{7,15},{8,0},{9,1},{1... | collective-permute-start | bytes 24584 | tf_op jit(solution)/shard_map/ppermute | solution.py:318
  10.1 2.0 %copy-start.1 = (bf16[1,512,3584]{2,1,0:T(8,128)(2,1)S(1)}, bf16[1,512,3584]{2,1,0:T(8,128)(2,1)}, u32[]{:S(2)}) copy-start(bf16[1,512,3584]{2,1,0:T(8,128)(2,1)} %param.9) | copy-start | bytes 11010052
  12.1 10.3 %copy-start = (bf16[1,3584,1024]{2,1,0:T(8,128)(2,1)S(1)}, bf16[1,3584,1024]{2,1,0:T(8,128)(2,1)}, u32[]{:S(2)}) copy-start(bf16[1,3584,1024]{2,1,0:T(8,128)(2,1)} %param.8) | copy-start | bytes 22020100
  12.4 7.1 %collective-permute-start.6 = (bf16[16,3712]{1,0:T(8,128)(2,1)S(1)}, bf16[16,3712]{1,0:T(8,128)(2,1)S(1)}, u32[]{:S(2)}, u32[]{:S(2)}) collective-permute-start(bf16[16,3712]{1,0:T(8,128)(2,1)S(1)} %get-tuple-element.43), channel_id=1, source_target_pairs={{0,10},{1,11},{2,8},{3,9},{4,2},{5,3},{6,0},{7,1},{8,14},{9,15},{1... | collective-permute-start | bytes 356360 | tf_op jit(solution)/shard_map/ppermute | solution.py:318
  13.6 7.7 %collective-permute-start.5 = (bf16[16,3712]{1,0:T(8,128)(2,1)S(1)}, bf16[16,3712]{1,0:T(8,128)(2,1)S(1)}, u32[]{:S(2)}, u32[]{:S(2)}) collective-permute-start(bf16[16,3712]{1,0:T(8,128)(2,1)S(1)} %get-tuple-element.40), channel_id=1, source_target_pairs={{0,2},{1,3},{2,0},{3,1},{4,6},{5,7},{6,4},{7,5},{8,10},{9,11},{10,... | collective-permute-start | bytes 356360 | tf_op jit(solution)/shard_map/ppermute | solution.py:318
  14.7 8.2 %collective-permute-start.3 = (bf16[16,3712]{1,0:T(8,128)(2,1)S(1)}, bf16[16,3712]{1,0:T(8,128)(2,1)S(1)}, u32[]{:S(2)}, u32[]{:S(2)}) collective-permute-start(bf16[16,3712]{1,0:T(8,128)(2,1)S(1)} %get-tuple-element.38), channel_id=1, source_target_pairs={{0,4},{1,5},{2,6},{3,7},{4,12},{5,13},{6,14},{7,15},{8,0},{9,1},{1... | collective-permute-start | bytes 356360 | tf_op jit(solution)/shard_map/ppermute | solution.py:318
  19.5 7.8 %collective-permute-start.4 = (bf16[16,3712]{1,0:T(8,128)(2,1)S(1)}, bf16[16,3712]{1,0:T(8,128)(2,1)S(1)}, u32[]{:S(2)}, u32[]{:S(2)}) collective-permute-start(bf16[16,3712]{1,0:T(8,128)(2,1)S(1)} %get-tuple-element.39), channel_id=1, source_target_pairs={{0,6},{1,7},{2,4},{3,5},{4,14},{5,15},{6,12},{7,13},{8,2},{9,3},{1... | collective-permute-start | bytes 356360 | tf_op jit(solution)/shard_map/ppermute | solution.py:318
  21.3 6.0 %collective-permute-start.7 = (bf16[16,3712]{1,0:T(8,128)(2,1)S(1)}, bf16[16,3712]{1,0:T(8,128)(2,1)S(1)}, u32[]{:S(2)}, u32[]{:S(2)}) collective-permute-start(bf16[16,3712]{1,0:T(8,128)(2,1)S(1)} %get-tuple-element.44), channel_id=1, source_target_pairs={{0,8},{1,9},{2,10},{3,11},{4,0},{5,1},{6,2},{7,3},{8,12},{9,13},{1... | collective-permute-start | bytes 356360 | tf_op jit(solution)/shard_map/ppermute | solution.py:318
  30.8 7.7 %collective-permute-start.10 = (bf16[16,3712]{1,0:T(8,128)(2,1)S(1)}, bf16[16,3712]{1,0:T(8,128)(2,1)S(1)}, u32[]{:S(2)}, u32[]{:S(2)}) collective-permute-start(bf16[16,3712]{1,0:T(8,128)(2,1)S(1)} %get-tuple-element.48), channel_id=1, source_target_pairs={{0,6},{1,7},{2,4},{3,5},{4,14},{5,15},{6,12},{7,13},{8,2},{9,3},{1... | collective-permute-start | bytes 356360 | tf_op jit(solution)/shard_map/ppermute | solution.py:318
  33.0 6.5 %collective-permute-start.11 = (bf16[16,3712]{1,0:T(8,128)(2,1)S(1)}, bf16[16,3712]{1,0:T(8,128)(2,1)S(1)}, u32[]{:S(2)}, u32[]{:S(2)}) collective-permute-start(bf16[16,3712]{1,0:T(8,128)(2,1)S(1)} %get-tuple-element.49), channel_id=1, source_target_pairs={{0,2},{1,3},{2,0},{3,1},{4,6},{5,7},{6,4},{7,5},{8,10},{9,11},{10,... | collective-permute-start | bytes 356360 | tf_op jit(solution)/shard_map/ppermute | solution.py:318
  33.5 6.0 %collective-permute-start.12 = (bf16[16,3712]{1,0:T(8,128)(2,1)S(1)}, bf16[16,3712]{1,0:T(8,128)(2,1)S(1)}, u32[]{:S(2)}, u32[]{:S(2)}) collective-permute-start(bf16[16,3712]{1,0:T(8,128)(2,1)S(1)} %get-tuple-element.50), channel_id=1, source_target_pairs={{0,16},{1,17},{2,18},{3,19},{4,20},{5,21},{6,22},{7,23},{8,24},{9,... | collective-permute-start | bytes 356360 | tf_op jit(solution)/shard_map/ppermute | solution.py:318
  35.0 5.7 %collective-permute-start.13 = (bf16[16,3712]{1,0:T(8,128)(2,1)S(1)}, bf16[16,3712]{1,0:T(8,128)(2,1)S(1)}, u32[]{:S(2)}, u32[]{:S(2)}) collective-permute-start(bf16[16,3712]{1,0:T(8,128)(2,1)S(1)} %get-tuple-element.51), channel_id=1, source_target_pairs={{0,18},{1,19},{2,16},{3,17},{4,22},{5,23},{6,20},{7,21},{8,26},{9,... | collective-permute-start | bytes 356360 | tf_op jit(solution)/shard_map/ppermute | solution.py:318
  36.5 5.7 %collective-permute-start.14 = (bf16[16,3712]{1,0:T(8,128)(2,1)S(1)}, bf16[16,3712]{1,0:T(8,128)(2,1)S(1)}, u32[]{:S(2)}, u32[]{:S(2)}) collective-permute-start(bf16[16,3712]{1,0:T(8,128)(2,1)S(1)} %get-tuple-element.52), channel_id=1, source_target_pairs={{0,4},{1,5},{2,6},{3,7},{4,12},{5,13},{6,14},{7,15},{8,0},{9,1},{1... | collective-permute-start | bytes 356360 | tf_op jit(solution)/shard_map/ppermute | solution.py:318
  42.6 11.3 %collective-permute-start.17 = (bf16[32,3584]{1,0:T(8,128)(2,1)S(1)}, bf16[32,3584]{1,0:T(8,128)(2,1)S(1)}, u32[]{:S(2)}, u32[]{:S(2)}) collective-permute-start(bf16[32,3584]{1,0:T(8,128)(2,1)S(1)} %combine.3), channel_id=1, source_target_pairs={{0,20},{1,21},{2,22},{3,23},{4,28},{5,29},{6,30},{7,31},{8,16},{9,... | collective-permute-start | bytes 688136 | tf_op jit(solution)/shard_map/ppermute | solution.py:318
  42.7 9.1 %collective-permute-start.15 = (bf16[16,3712]{1,0:T(8,128)(2,1)S(1)}, bf16[16,3712]{1,0:T(8,128)(2,1)S(1)}, u32[]{:S(2)}, u32[]{:S(2)}) collective-permute-start(bf16[16,3712]{1,0:T(8,128)(2,1)S(1)} %get-tuple-element.55), channel_id=1, source_target_pairs={{0,24},{1,25},{2,26},{3,27},{4,16},{5,17},{6,18},{7,19},{8,28},{9,... | collective-permute-start | bytes 356360 | tf_op jit(solution)/shard_map/ppermute | solution.py:318
  46.5 7.0 %collective-permute-start.16 = (bf16[16,3712]{1,0:T(8,128)(2,1)S(1)}, bf16[16,3712]{1,0:T(8,128)(2,1)S(1)}, u32[]{:S(2)}, u32[]{:S(2)}) collective-permute-start(bf16[16,3712]{1,0:T(8,128)(2,1)S(1)} %get-tuple-element.56), channel_id=1, source_target_pairs={{0,26},{1,27},{2,24},{3,25},{4,18},{5,19},{6,16},{7,17},{8,30},{9,... | collective-permute-start | bytes 356360 | tf_op jit(solution)/shard_map/ppermute | solution.py:318

commit v31 on v29

--- a/solution.py
+++ b/solution.py
@@ -354,7 +354,8 @@
     ]
     two, three, *straight, four = lax.optimization_barrier(first)
     merged = [piece[3, 0], two, three, four]
-    straight += [sent(piece[1, flip], sections, 1, -1, flip) for flip in range(2)]
+    straight.append(sent(piece[1, 0], sections, 1, -1, 0))
+    straight.append(sent(after(piece[1, 1], straight[-1]), sections, 1, -1, 1))
     merged = sent(combine(merged, tok_count), sections, 1, 1, 0)
     return combine(straight, tok_count, merged)[None]
 

time: 54.8 us -> 53.9 us (0.984)
  waiting for transfers between devices: 18 us -> 16.8 us
    ppermute x16, waiting for transfers between devices: 18 us -> 16.8 us  [sent(): return lax.ppermute(shard, ('section', 'expert'), pairs)]
  transfers between devices with their start and end apart: 18 -> 18, of which waited for: 8 -> 7; matrix products, arithmetic and copies ran while one was open for 0% -> 0% of each run, Pallas kernels for 8% -> 9%
where the time goes in v31:
time: 53.9 us; the launch traced here: 53.7 us
  starting transfers between devices  26.2 us (49%)
  waiting for transfers between devices  16.8 us (31%)
  Pallas kernels  7.57 us (14%)
  local copies, waits for them, and re-layouts  2.98 us (6%)
    ppermute x16, starting transfers between devices, sent(): return lax.ppermute(shard, ('section', 'expert'), pairs)  25.7 us
    ppermute x16, waiting for transfers between devices, sent(): return lax.ppermute(shard, ('section', 'expert'), pairs)  16.8 us
    pallas_call x9, Pallas kernels, local_call(): pl.pallas_call(kernel, out_shape=out_shape, in_specs=[vmem if spec is Non...  7.57 us
    unnamed x6, local copies, waits for them, and re-layouts  2.98 us
  transfers between devices with their start and end apart: 18, of which 7 were waited for; matrix products, arithmetic and copies ran while one was open for 0% of the time, Pallas kernels for 9%

profile of v31, /device:TPU:0, one launch (start us, length us, event | category | flops | bytes accessed | tf_op | source)
XLA Modules:
  0.0 53.7 jit_solution(12976239833390306688)
XLA Ops:
  0.5 3.0 %collective-permute-start.1 = (bf16[32,3584]{1,0:T(8,128)(2,1)}, bf16[32,3584]{1,0:T(8,128)(2,1)S(1)}, u32[]{:S(2)}, u32[]{:S(2)}) collective-permute-start(bf16[32,3584]{1,0:T(8,128)(2,1)} %bitcast.14), channel_id=1, source_target_pairs={{0,4},{1,5},{2,6},{3,7},{4,12},{5,13},{6,14},{7,15},{8,0},{9,1},{1... | collective-permute-start | bytes 688136 | tf_op jit(solution)/shard_map/ppermute | solution.py:309
  3.5 1.0 %prepare.1.marks = bf16[32,128]{1,0:T(8,128)(2,1)S(1)} custom-call(s32[2,32]{1,0:T(2,128)} %bitcast.16, f32[2,32]{1,0:T(2,128)} %bitcast.17), custom_call_target="tpu_custom_call" | custom-call | tf_op jit(solution)/shard_map/prepare/pallas_call | solution.py:84
  4.6 0.9 %copy-done.2 = bf16[1,32,3584]{2,1,0:T(8,128)(2,1)S(1)} copy-done((bf16[1,32,3584]{2,1,0:T(8,128)(2,1)S(1)}, bf16[1,32,3584]{2,1,0:T(8,128)(2,1)}, u32[]{:S(2)}) %copy-start.2) | copy-done | bytes 229400
  5.9 1.6 %collective-permute-start = (bf16[16,3712]{1,0:T(8,128)(2,1)S(1)}, bf16[16,3712]{1,0:T(8,128)(2,1)S(1)}, u32[]{:S(2)}, u32[]{:S(2)}) collective-permute-start(bf16[16,3712]{1,0:T(8,128)(2,1)S(1)} %get-tuple-element.35), channel_id=1, source_target_pairs={{0,2},{1,3},{2,0},{3,1},{4,6},{5,7},{6,4},{7,5},{8,10},{9,11},{10,... | collective-permute-start | bytes 356360 | tf_op jit(solution)/shard_map/ppermute | solution.py:309
  7.5 2.6 %collective-permute-start.2 = (bf16[32,128]{1,0:T(8,128)(2,1)S(1)}, bf16[32,128]{1,0:T(8,128)(2,1)S(1)}, u32[]{:S(2)}, u32[]{:S(2)}) collective-permute-start(bf16[32,128]{1,0:T(8,128)(2,1)S(1)} %prepare.1.marks), channel_id=1, source_target_pairs={{0,4},{1,5},{2,6},{3,7},{4,12},{5,13},{6,14},{7,15},{8,0},{9,1},{1... | collective-permute-start | bytes 24584 | tf_op jit(solution)/shard_map/ppermute | solution.py:309
  10.1 2.0 %copy-done.1 = bf16[1,512,3584]{2,1,0:T(8,128)(2,1)S(1)} copy-done((bf16[1,512,3584]{2,1,0:T(8,128)(2,1)S(1)}, bf16[1,512,3584]{2,1,0:T(8,128)(2,1)}, u32[]{:S(2)}) %copy-start.1) | copy-done | bytes 3670040
  13.6 1.2 %collective-permute-start.5 = (bf16[16,3712]{1,0:T(8,128)(2,1)S(1)}, bf16[16,3712]{1,0:T(8,128)(2,1)S(1)}, u32[]{:S(2)}, u32[]{:S(2)}) collective-permute-start(bf16[16,3712]{1,0:T(8,128)(2,1)S(1)} %get-tuple-element.41), channel_id=1, source_target_pairs={{0,2},{1,3},{2,0},{3,1},{4,6},{5,7},{6,4},{7,5},{8,10},{9,11},{10,... | collective-permute-start | bytes 356360 | tf_op jit(solution)/shard_map/ppermute | solution.py:309
  14.7 1.7 %collective-permute-start.3 = (bf16[16,3712]{1,0:T(8,128)(2,1)S(1)}, bf16[16,3712]{1,0:T(8,128)(2,1)S(1)}, u32[]{:S(2)}, u32[]{:S(2)}) collective-permute-start(bf16[16,3712]{1,0:T(8,128)(2,1)S(1)} %get-tuple-element.39), channel_id=1, source_target_pairs={{0,4},{1,5},{2,6},{3,7},{4,12},{5,13},{6,14},{7,15},{8,0},{9,1},{1... | collective-permute-start | bytes 356360 | tf_op jit(solution)/shard_map/ppermute | solution.py:309
  16.4 3.1 %collective-permute-done.6.refs_7_ = bf16[16,3712]{1,0:T(8,128)(2,1)S(1)} collective-permute-done((bf16[16,3712]{1,0:T(8,128)(2,1)S(1)}, bf16[16,3712]{1,0:T(8,128)(2,1)S(1)}, u32[]{:S(2)}, u32[]{:S(2)}) %collective-permute-start.6) | collective-permute-done | bytes 118816 | tf_op jit(solution)/shard_map/ppermute | solution.py:309
  19.5 1.8 %collective-permute-start.4 = (bf16[16,3712]{1,0:T(8,128)(2,1)S(1)}, bf16[16,3712]{1,0:T(8,128)(2,1)S(1)}, u32[]{:S(2)}, u32[]{:S(2)}) collective-permute-start(bf16[16,3712]{1,0:T(8,128)(2,1)S(1)} %get-tuple-element.40), channel_id=1, source_target_pairs={{0,6},{1,7},{2,4},{3,5},{4,14},{5,15},{6,12},{7,13},{8,2},{9,3},{1... | collective-permute-start | bytes 356360 | tf_op jit(solution)/shard_map/ppermute | solution.py:309
  21.3 1.2 %collective-permute-start.7 = (bf16[16,3712]{1,0:T(8,128)(2,1)S(1)}, bf16[16,3712]{1,0:T(8,128)(2,1)S(1)}, u32[]{:S(2)}, u32[]{:S(2)}) collective-permute-start(bf16[16,3712]{1,0:T(8,128)(2,1)S(1)} %get-tuple-element.45), channel_id=1, source_target_pairs={{0,8},{1,9},{2,10},{3,11},{4,0},{5,1},{6,2},{7,3},{8,12},{9,13},{1... | collective-permute-start | bytes 356360 | tf_op jit(solution)/shard_map/ppermute | solution.py:309
  23.0 4.3 %collective-permute-done.4.refs_4_ = bf16[16,3712]{1,0:T(8,128)(2,1)S(1)} collective-permute-done((bf16[16,3712]{1,0:T(8,128)(2,1)S(1)}, bf16[16,3712]{1,0:T(8,128)(2,1)S(1)}, u32[]{:S(2)}, u32[]{:S(2)}) %collective-permute-start.4) | collective-permute-done | bytes 118816 | tf_op jit(solution)/shard_map/ppermute | solution.py:309
  27.3 1.7 %near_pass.1 = (bf16[128,3712]{1,0:T(8,128)(2,1)S(1)}, f32[128,3584]{1,0:T(8,128)S(1)}) custom-call(bf16[16,3712]{1,0:T(8,128)(2,1)S(1)} %get-tuple-element.34.refs_0_, bf16[16,3712]{1,0:T(8,128)(2,1)S(1)} %collective-permute-done.refs_1_, bf16[16,3712]{1,0:T(8,128)(2,1)S(1)} %get-tuple-element.38.refs_2_, ...), custom_call_target="tpu_custom_call" | custom-call | bytes 11010048 | tf_op jit(solution)/shard_map/near_pass/pallas_call | solution.py:84
  29.0 1.7 %far_pass.1 = (bf16[16,3712]{1,0:T(8,128)(2,1)S(1)}, bf16[16,3712]{1,0:T(8,128)(2,1)S(1)}, bf16[16,3712]{1,0:T(8,128)(2,1)S(1)}, bf16[16,3712]{1,0:T(8,128)(2,1)...) custom-call(bf16[128,3712]{1,0:T(8,128)(2,1)S(1)} %get-tuple-element, ...), custom_call_target="tpu_custom_call" | custom-call | bytes 11010048 | tf_op jit(solution)/shard_map/far_pass/pallas_call | solution.py:84
  30.8 2.2 %collective-permute-start.10 = (bf16[16,3712]{1,0:T(8,128)(2,1)S(1)}, bf16[16,3712]{1,0:T(8,128)(2,1)S(1)}, u32[]{:S(2)}, u32[]{:S(2)}) collective-permute-start(bf16[16,3712]{1,0:T(8,128)(2,1)S(1)} %get-tuple-element.49), channel_id=1, source_target_pairs={{0,6},{1,7},{2,4},{3,5},{4,14},{5,15},{6,12},{7,13},{8,2},{9,3},{1... | collective-permute-start | bytes 356360 | tf_op jit(solution)/shard_map/ppermute | solution.py:309
  33.5 1.5 %collective-permute-start.12 = (bf16[16,3712]{1,0:T(8,128)(2,1)S(1)}, bf16[16,3712]{1,0:T(8,128)(2,1)S(1)}, u32[]{:S(2)}, u32[]{:S(2)}) collective-permute-start(bf16[16,3712]{1,0:T(8,128)(2,1)S(1)} %get-tuple-element.51), channel_id=1, source_target_pairs={{0,16},{1,17},{2,18},{3,19},{4,20},{5,21},{6,22},{7,23},{8,24},{9,... | collective-permute-start | bytes 356360 | tf_op jit(solution)/shard_map/ppermute | solution.py:309
  35.0 1.5 %collective-permute-start.13 = (bf16[16,3712]{1,0:T(8,128)(2,1)S(1)}, bf16[16,3712]{1,0:T(8,128)(2,1)S(1)}, u32[]{:S(2)}, u32[]{:S(2)}) collective-permute-start(bf16[16,3712]{1,0:T(8,128)(2,1)S(1)} %get-tuple-element.52), channel_id=1, source_target_pairs={{0,18},{1,19},{2,16},{3,17},{4,22},{5,23},{6,20},{7,21},{8,26},{9,... | collective-permute-start | bytes 356360 | tf_op jit(solution)/shard_map/ppermute | solution.py:309
  36.5 2.1 %collective-permute-done.10.refs_1_ = bf16[16,3712]{1,0:T(8,128)(2,1)S(1)} collective-permute-done((bf16[16,3712]{1,0:T(8,128)(2,1)S(1)}, bf16[16,3712]{1,0:T(8,128)(2,1)S(1)}, u32[]{:S(2)}, u32[]{:S(2)}) %collective-permute-start.10) | collective-permute-done | bytes 118816 | tf_op jit(solution)/shard_map/ppermute | solution.py:309
  38.6 1.7 %collective-permute-start.15 = (bf16[16,3712]{1,0:T(8,128)(2,1)S(1)}, bf16[16,3712]{1,0:T(8,128)(2,1)S(1)}, u32[]{:S(2)}, u32[]{:S(2)}) collective-permute-start(bf16[16,3712]{1,0:T(8,128)(2,1)S(1)} %get-tuple-element.56), channel_id=1, source_target_pairs={{0,24},{1,25},{2,26},{3,27},{4,16},{5,17},{6,18},{7,19},{8,28},{9,... | collective-permute-start | bytes 356360 | tf_op jit(solution)/shard_map/ppermute | solution.py:309
  40.3 1.6 %collective-permute-done.13.refs_1_ = bf16[16,3712]{1,0:T(8,128)(2,1)S(1)} collective-permute-done((bf16[16,3712]{1,0:T(8,128)(2,1)S(1)}, bf16[16,3712]{1,0:T(8,128)(2,1)S(1)}, u32[]{:S(2)}, u32[]{:S(2)}) %collective-permute-start.13) | collective-permute-done | bytes 118816 | tf_op jit(solution)/shard_map/ppermute | solution.py:309
  43.1 1.3 %collective-permute-done.15.refs_2_ = bf16[16,3712]{1,0:T(8,128)(2,1)S(1)} collective-permute-done((bf16[16,3712]{1,0:T(8,128)(2,1)S(1)}, bf16[16,3712]{1,0:T(8,128)(2,1)S(1)}, u32[]{:S(2)}, u32[]{:S(2)}) %collective-permute-start.15) | collective-permute-done | bytes 118816 | tf_op jit(solution)/shard_map/ppermute | solution.py:309
  44.4 4.0 %collective-permute-start.16 = (bf16[16,3712]{1,0:T(8,128)(2,1)S(1)}, bf16[16,3712]{1,0:T(8,128)(2,1)S(1)}, u32[]{:S(2)}, u32[]{:S(2)}) collective-permute-start(bf16[16,3712]{1,0:T(8,128)(2,1)S(1)} %get-tuple-element.58), channel_id=1, source_target_pairs={{0,26},{1,27},{2,24},{3,25},{4,18},{5,19},{6,16},{7,17},{8,30},{9,... | collective-permute-start | bytes 356360 | tf_op jit(solution)/shard_map/ppermute | solution.py:309
  48.3 4.2 %collective-permute-done.16.refs_3_ = bf16[16,3712]{1,0:T(8,128)(2,1)S(1)} collective-permute-done((bf16[16,3712]{1,0:T(8,128)(2,1)S(1)}, bf16[16,3712]{1,0:T(8,128)(2,1)S(1)}, u32[]{:S(2)}, u32[]{:S(2)}) %collective-permute-start.16) | collective-permute-done | bytes 118816 | tf_op jit(solution)/shard_map/ppermute | solution.py:309
  52.6 1.1 %combine.3 = bf16[32,3584]{1,0:T(8,128)(2,1)} custom-call(bf16[16,3712]{1,0:T(8,128)(2,1)S(1)} %collective-permute-done.12.refs_0_, bf16[16,3712]{1,0:T(8,128)(2,1)S(1)} %collective-permute-done.13.refs_1_, bf16[16,3712]{1,0:T(8,128)(2,1)S(1)} %collective-permute-done.15.refs_2_, bf16[16,3712]{1,0:T(8,128)(2,1)S(1)} %collective-permute-done.16.refs_3_, ...), custom_call_target="tpu_custom_call" | custom-call | tf_op jit(solution)/shard_map/combine/pallas_call | solution.py:84
  (27 shorter events, 4.6 us)
Async XLA Ops:
  0.0 29.0 %collective-permute-start.8 = (bf16[3584,1024]{1,0:T(8,128)(2,1)}, bf16[3584,1024]{1,0:T(8,128)(2,1)S(1)}, u32[]{:S(2)}, u32[]{:S(2)}) collective-permute-start(bf16[3584,1024]{1,0:T(8,128)(2,1)} %bitcast.10), channel_id=1, source_target_pairs={{0,1},{1,0},{2,3},{3,2},{4,5},{5,4},{6,7},{7,6},{8,9},{9,8},{10,11... | collective-permute-start | bytes 22020104 | tf_op jit(solution)/shard_map/ppermute | solution.py:327
  0.5 28.6 %collective-permute-start.9 = (bf16[512,3584]{1,0:T(8,128)(2,1)}, bf16[512,3584]{1,0:T(8,128)(2,1)S(1)}, u32[]{:S(2)}, u32[]{:S(2)}) collective-permute-start(bf16[512,3584]{1,0:T(8,128)(2,1)} %bitcast.12), channel_id=1, source_target_pairs={{0,1},{1,0},{2,3},{3,2},{4,5},{5,4},{6,7},{7,6},{8,9},{9,8},{10,11... | collective-permute-start | bytes 11010056 | tf_op jit(solution)/shard_map/ppermute | solution.py:326
  0.5 12.6 %collective-permute-start.1 = (bf16[32,3584]{1,0:T(8,128)(2,1)}, bf16[32,3584]{1,0:T(8,128)(2,1)S(1)}, u32[]{:S(2)}, u32[]{:S(2)}) collective-permute-start(bf16[32,3584]{1,0:T(8,128)(2,1)} %bitcast.14), channel_id=1, source_target_pairs={{0,4},{1,5},{2,6},{3,7},{4,12},{5,13},{6,14},{7,15},{8,0},{9,1},{1... | collective-permute-start | bytes 688136 | tf_op jit(solution)/shard_map/ppermute | solution.py:309
  4.5 0.9 %copy-start.2 = (bf16[1,32,3584]{2,1,0:T(8,128)(2,1)S(1)}, bf16[1,32,3584]{2,1,0:T(8,128)(2,1)}, u32[]{:S(2)}) copy-start(bf16[1,32,3584]{2,1,0:T(8,128)(2,1)} %param.5) | copy-start | bytes 688132
  5.9 6.5 %collective-permute-start = (bf16[16,3712]{1,0:T(8,128)(2,1)S(1)}, bf16[16,3712]{1,0:T(8,128)(2,1)S(1)}, u32[]{:S(2)}, u32[]{:S(2)}) collective-permute-start(bf16[16,3712]{1,0:T(8,128)(2,1)S(1)} %get-tuple-element.35), channel_id=1, source_target_pairs={{0,2},{1,3},{2,0},{3,1},{4,6},{5,7},{6,4},{7,5},{8,10},{9,11},{10,... | collective-permute-start | bytes 356360 | tf_op jit(solution)/shard_map/ppermute | solution.py:309
  7.5 5.7 %collective-permute-start.2 = (bf16[32,128]{1,0:T(8,128)(2,1)S(1)}, bf16[32,128]{1,0:T(8,128)(2,1)S(1)}, u32[]{:S(2)}, u32[]{:S(2)}) collective-permute-start(bf16[32,128]{1,0:T(8,128)(2,1)S(1)} %prepare.1.marks), channel_id=1, source_target_pairs={{0,4},{1,5},{2,6},{3,7},{4,12},{5,13},{6,14},{7,15},{8,0},{9,1},{1... | collective-permute-start | bytes 24584 | tf_op jit(solution)/shard_map/ppermute | solution.py:309
  10.1 2.0 %copy-start.1 = (bf16[1,512,3584]{2,1,0:T(8,128)(2,1)S(1)}, bf16[1,512,3584]{2,1,0:T(8,128)(2,1)}, u32[]{:S(2)}) copy-start(bf16[1,512,3584]{2,1,0:T(8,128)(2,1)} %param.9) | copy-start | bytes 11010052
  12.1 10.3 %copy-start = (bf16[1,3584,1024]{2,1,0:T(8,128)(2,1)S(1)}, bf16[1,3584,1024]{2,1,0:T(8,128)(2,1)}, u32[]{:S(2)}) copy-start(bf16[1,3584,1024]{2,1,0:T(8,128)(2,1)} %param.8) | copy-start | bytes 22020100
  12.4 7.1 %collective-permute-start.6 = (bf16[16,3712]{1,0:T(8,128)(2,1)S(1)}, bf16[16,3712]{1,0:T(8,128)(2,1)S(1)}, u32[]{:S(2)}, u32[]{:S(2)}) collective-permute-start(bf16[16,3712]{1,0:T(8,128)(2,1)S(1)} %get-tuple-element.44), channel_id=1, source_target_pairs={{0,10},{1,11},{2,8},{3,9},{4,2},{5,3},{6,0},{7,1},{8,14},{9,15},{1... | collective-permute-start | bytes 356360 | tf_op jit(solution)/shard_map/ppermute | solution.py:309
  13.6 7.7 %collective-permute-start.5 = (bf16[16,3712]{1,0:T(8,128)(2,1)S(1)}, bf16[16,3712]{1,0:T(8,128)(2,1)S(1)}, u32[]{:S(2)}, u32[]{:S(2)}) collective-permute-start(bf16[16,3712]{1,0:T(8,128)(2,1)S(1)} %get-tuple-element.41), channel_id=1, source_target_pairs={{0,2},{1,3},{2,0},{3,1},{4,6},{5,7},{6,4},{7,5},{8,10},{9,11},{10,... | collective-permute-start | bytes 356360 | tf_op jit(solution)/shard_map/ppermute | solution.py:309
  14.7 8.2 %collective-permute-start.3 = (bf16[16,3712]{1,0:T(8,128)(2,1)S(1)}, bf16[16,3712]{1,0:T(8,128)(2,1)S(1)}, u32[]{:S(2)}, u32[]{:S(2)}) collective-permute-start(bf16[16,3712]{1,0:T(8,128)(2,1)S(1)} %get-tuple-element.39), channel_id=1, source_target_pairs={{0,4},{1,5},{2,6},{3,7},{4,12},{5,13},{6,14},{7,15},{8,0},{9,1},{1... | collective-permute-start | bytes 356360 | tf_op jit(solution)/shard_map/ppermute | solution.py:309
  19.5 7.8 %collective-permute-start.4 = (bf16[16,3712]{1,0:T(8,128)(2,1)S(1)}, bf16[16,3712]{1,0:T(8,128)(2,1)S(1)}, u32[]{:S(2)}, u32[]{:S(2)}) collective-permute-start(bf16[16,3712]{1,0:T(8,128)(2,1)S(1)} %get-tuple-element.40), channel_id=1, source_target_pairs={{0,6},{1,7},{2,4},{3,5},{4,14},{5,15},{6,12},{7,13},{8,2},{9,3},{1... | collective-permute-start | bytes 356360 | tf_op jit(solution)/shard_map/ppermute | solution.py:309
  21.3 6.0 %collective-permute-start.7 = (bf16[16,3712]{1,0:T(8,128)(2,1)S(1)}, bf16[16,3712]{1,0:T(8,128)(2,1)S(1)}, u32[]{:S(2)}, u32[]{:S(2)}) collective-permute-start(bf16[16,3712]{1,0:T(8,128)(2,1)S(1)} %get-tuple-element.45), channel_id=1, source_target_pairs={{0,8},{1,9},{2,10},{3,11},{4,0},{5,1},{6,2},{7,3},{8,12},{9,13},{1... | collective-permute-start | bytes 356360 | tf_op jit(solution)/shard_map/ppermute | solution.py:309
  30.8 7.8 %collective-permute-start.10 = (bf16[16,3712]{1,0:T(8,128)(2,1)S(1)}, bf16[16,3712]{1,0:T(8,128)(2,1)S(1)}, u32[]{:S(2)}, u32[]{:S(2)}) collective-permute-start(bf16[16,3712]{1,0:T(8,128)(2,1)S(1)} %get-tuple-element.49), channel_id=1, source_target_pairs={{0,6},{1,7},{2,4},{3,5},{4,14},{5,15},{6,12},{7,13},{8,2},{9,3},{1... | collective-permute-start | bytes 356360 | tf_op jit(solution)/shard_map/ppermute | solution.py:309
  33.0 7.3 %collective-permute-start.11 = (bf16[16,3712]{1,0:T(8,128)(2,1)S(1)}, bf16[16,3712]{1,0:T(8,128)(2,1)S(1)}, u32[]{:S(2)}, u32[]{:S(2)}) collective-permute-start(bf16[16,3712]{1,0:T(8,128)(2,1)S(1)} %get-tuple-element.50), channel_id=1, source_target_pairs={{0,2},{1,3},{2,0},{3,1},{4,6},{5,7},{6,4},{7,5},{8,10},{9,11},{10,... | collective-permute-start | bytes 356360 | tf_op jit(solution)/shard_map/ppermute | solution.py:309
  33.5 6.8 %collective-permute-start.12 = (bf16[16,3712]{1,0:T(8,128)(2,1)S(1)}, bf16[16,3712]{1,0:T(8,128)(2,1)S(1)}, u32[]{:S(2)}, u32[]{:S(2)}) collective-permute-start(bf16[16,3712]{1,0:T(8,128)(2,1)S(1)} %get-tuple-element.51), channel_id=1, source_target_pairs={{0,16},{1,17},{2,18},{3,19},{4,20},{5,21},{6,22},{7,23},{8,24},{9,... | collective-permute-start | bytes 356360 | tf_op jit(solution)/shard_map/ppermute | solution.py:309
  35.0 6.9 %collective-permute-start.13 = (bf16[16,3712]{1,0:T(8,128)(2,1)S(1)}, bf16[16,3712]{1,0:T(8,128)(2,1)S(1)}, u32[]{:S(2)}, u32[]{:S(2)}) collective-permute-start(bf16[16,3712]{1,0:T(8,128)(2,1)S(1)} %get-tuple-element.52), channel_id=1, source_target_pairs={{0,18},{1,19},{2,16},{3,17},{4,22},{5,23},{6,20},{7,21},{8,26},{9,... | collective-permute-start | bytes 356360 | tf_op jit(solution)/shard_map/ppermute | solution.py:309
  36.5 5.7 %collective-permute-start.14 = (bf16[16,3712]{1,0:T(8,128)(2,1)S(1)}, bf16[16,3712]{1,0:T(8,128)(2,1)S(1)}, u32[]{:S(2)}, u32[]{:S(2)}) collective-permute-start(bf16[16,3712]{1,0:T(8,128)(2,1)S(1)} %get-tuple-element.53), channel_id=1, source_target_pairs={{0,4},{1,5},{2,6},{3,7},{4,12},{5,13},{6,14},{7,15},{8,0},{9,1},{1... | collective-permute-start | bytes 356360 | tf_op jit(solution)/shard_map/ppermute | solution.py:309
  38.6 5.8 %collective-permute-start.15 = (bf16[16,3712]{1,0:T(8,128)(2,1)S(1)}, bf16[16,3712]{1,0:T(8,128)(2,1)S(1)}, u32[]{:S(2)}, u32[]{:S(2)}) collective-permute-start(bf16[16,3712]{1,0:T(8,128)(2,1)S(1)} %get-tuple-element.56), channel_id=1, source_target_pairs={{0,24},{1,25},{2,26},{3,27},{4,16},{5,17},{6,18},{7,19},{8,28},{9,... | collective-permute-start | bytes 356360 | tf_op jit(solution)/shard_map/ppermute | solution.py:309
  42.6 9.9 %collective-permute-start.17 = (bf16[32,3584]{1,0:T(8,128)(2,1)S(1)}, bf16[32,3584]{1,0:T(8,128)(2,1)S(1)}, u32[]{:S(2)}, u32[]{:S(2)}) collective-permute-start(bf16[32,3584]{1,0:T(8,128)(2,1)S(1)} %combine.2), channel_id=1, source_target_pairs={{0,20},{1,21},{2,22},{3,23},{4,28},{5,29},{6,30},{7,31},{8,16},{9,... | collective-permute-start | bytes 688136 | tf_op jit(solution)/shard_map/ppermute | solution.py:309
  44.4 8.2 %collective-permute-start.16 = (bf16[16,3712]{1,0:T(8,128)(2,1)S(1)}, bf16[16,3712]{1,0:T(8,128)(2,1)S(1)}, u32[]{:S(2)}, u32[]{:S(2)}) collective-permute-start(bf16[16,3712]{1,0:T(8,128)(2,1)S(1)} %get-tuple-element.58), channel_id=1, source_target_pairs={{0,26},{1,27},{2,24},{3,25},{4,18},{5,19},{6,16},{7,17},{8,30},{9,... | collective-permute-start | bytes 356360 | tf_op jit(solution)/shard_map/ppermute | solution.py:309
